TPU v7x, 32 devices: a whole 2x2x4 slice. The times are simulated.
32 devices in a mesh: tm: 8 (over z, core), depth: 4 (over y, x).
Axes of the slice: x: 2, y: 2, z: 4, core: 2. Of those that a mesh axis runs over, the one named last changes fastest.
Arguments:
- raw: bfloat16 [128, 32, 128], P('tm', 'depth'), may hold values from -6 to 6
- stream: bfloat16 [128, 32, 2048], P('tm', 'depth'), may hold values from -6 to 6
- conv_w: bfloat16 [3, 128, 2048], replicated, may hold values from -0.3125 to 0.3125
- gain: float32 [2048], replicated, may hold values from 0.1 to 1.9
- w_qkv: bfloat16 [2048, 3072], P('tm', 'depth'), may hold values from -4 to 4
- mask: int32 [4, 8, 5], P('depth', 'tm'), may hold values from 0 to 1, as said below
Outputs:
- context: bfloat16 [128, 32, 1024], P('tm', 'depth')
Inputs may be any that keep to these rules, and one draw needn't show every extreme that they name: mask[p, i, 2] = 1 for every block; mask[p, i, e] = 0 wherever i + e - 2 lies outside 0 to 7.
All inputs are finite; a program needn't handle non-finite values.
Results may differ from a plain program's by a relative error of at most 0.012.
The roundings to bfloat16 on the way count: a program that leaves them out, or rounds other values in their place, can miss the bound.
Values may be sent and summed in bfloat16 or wider, within the bound.
No kernel may reach another device: no remote copies, remote signals or barrier semaphores. Data moves between devices by JAX's collectives and lax.ppermute only.
A program may use at most 64 MiB of HBM per device.

v0:
```python
import math

import jax
import jax.numpy as jnp
from jax import lax
from jax.sharding import PartitionSpec as P

HEADS = 8
HD = 128
BT = 16
PP = 8
RD = 2


def padded_2(value, sides, width):
    for axis, dim in sides:
        devices, length = (lax.axis_size(axis), value.shape[dim])
        up = [(i, (i + 1) % devices) for i in range(devices - 1)]
        down = [(j, i) for i, j in up]
        last = lax.slice_in_dim(value, length - width, length, axis=dim)
        leading = lax.slice_in_dim(value, 0, width, axis=dim)
        before = lax.ppermute(last, axis, up)
        after = lax.ppermute(leading, axis, down)
        value = jnp.concatenate([before, value, after], axis=dim)
    return value


def from_behind(value, axis, by):
    devices = lax.axis_size(axis)
    pairs = [(i, i + by) for i in range(devices) if 0 <= i + by < devices]
    return lax.ppermute(value, axis, pairs)


def head_attend(query_head, key_head, value_head, allowed):
    inv_root = 1.0 / math.sqrt(HD)
    scores = (
        jnp.einsum("qd,kd->qk", query_head, key_head, preferred_element_type=jnp.float32) * inv_root
    )
    scores = jnp.where(allowed, scores, -1e30)
    row_max = jnp.max(scores, axis=-1, keepdims=True)
    powers = jnp.exp(scores - row_max)
    weights = (powers / jnp.sum(powers, axis=-1, keepdims=True)).astype(jnp.bfloat16)
    return jnp.dot(weights, value_head, preferred_element_type=jnp.float32).astype(jnp.bfloat16)


def per_device(raw, stream, conv_w, gain, w_qkv, mask):
    time_len, site_len, feat_len = raw.shape
    tok_rows = time_len * site_len
    padded = padded_2(raw, (("depth", 1),), 1)
    embedded = stream.reshape(tok_rows, stream.shape[2]).astype(jnp.float32)
    for offset in range(3):
        window = padded[:, offset : offset + site_len].reshape(tok_rows, feat_len)
        embedded = embedded + jnp.dot(window, conv_w[offset], preferred_element_type=jnp.float32)
    normed = (
        embedded * lax.rsqrt(jnp.mean(embedded * embedded, axis=-1, keepdims=True) + 1e-05) * gain
    ).astype(jnp.bfloat16)
    columns = lax.all_gather(w_qkv, "depth", axis=1, tiled=True)
    projected = jnp.dot(
        normed,
        lax.all_gather(columns, "tm", axis=0, tiled=True),
        preferred_element_type=jnp.float32,
    ).astype(jnp.bfloat16)
    head_cols = projected.shape[1] // 3
    queries = projected[:, :head_cols]
    keyvals = projected[:, head_cols:]
    earlier = []
    later = []
    moving_back = keyvals
    moving_ahead = keyvals
    for hop_index in range(RD):
        moving_back = from_behind(moving_back, "tm", 1)
        moving_ahead = from_behind(moving_ahead, "tm", -1)
        earlier.insert(0, moving_back)
        later.append(moving_ahead)
    gathered = jnp.concatenate(earlier + [keyvals] + later, axis=0)
    block_rows = BT * PP
    own_blocks = tok_rows // block_rows
    span_blocks = gathered.shape[0] // block_rows
    local_mask = mask[0]
    query_ids = jnp.arange(own_blocks, dtype=jnp.int32)[:, None]
    key_ids = jnp.arange(span_blocks, dtype=jnp.int32)[None, :]
    entry_ids = key_ids - query_ids
    picks = entry_ids[:, :, None] == jnp.arange(local_mask.shape[1], dtype=jnp.int32)[None, None, :]
    block_allowed = jnp.sum(jnp.where(picks, local_mask[:, None, :], 0), axis=-1) > 0
    allowed = jnp.repeat(jnp.repeat(block_allowed, block_rows, axis=0), block_rows, axis=1)
    query_heads = queries.reshape(tok_rows, HEADS, HD).transpose(1, 0, 2)
    key_heads = gathered[:, :head_cols].reshape(gathered.shape[0], HEADS, HD).transpose(1, 0, 2)
    value_heads = gathered[:, head_cols:].reshape(gathered.shape[0], HEADS, HD).transpose(1, 0, 2)
    context = lax.map(
        lambda operands: head_attend(operands[0], operands[1], operands[2], allowed),
        (query_heads, key_heads, value_heads),
    )
    return context.transpose(1, 0, 2).reshape(time_len, site_len, head_cols)


def solution(mesh):
    in_specs = (
        P("tm", "depth", None),
        P("tm", "depth", None),
        P(),
        P(),
        P("tm", "depth"),
        P("depth", "tm", None),
    )
    out_specs = P("tm", "depth", None)
    return jax.shard_map(
        per_device, mesh=mesh, in_specs=in_specs, out_specs=out_specs, check_vma=False
    )
```

profile of v0, /device:TPU:9, one launch (start us, length us, event | category | flops | bytes accessed | tf_op | source)
XLA Modules:
  0.0 205.5 jit_solution(16200699698925124070)
XLA Ops:
  6.5 0.7 all-gather.3.cloned.1.call-update
  7.3 34.1 %all-gather.3.cloned.1.call-done = bf16[256,3072]{1,0:T(8,128)(2,1)} async-done(((bf16[256,768]{1,0:T(8,128)(2,1)}), bf16[256,3072]{1,0:T(8,128)(2,1)}) %all-gather.3.cloned.1.call-update) | async-done | bytes 1572880 | tf_op jit(solution)/shard_map/all_gather | solution.py:57
  41.5 3.2 %collective-permute-start = (bf16[16,1,128]{2,1,0:T(2,128)(2,1)S(1)}, bf16[16,1,128]{2,1,0:T(2,128)(2,1)S(1)}, u32[]{:S(2)}, u32[]{:S(2)}) collective-permute-start(bf16[16,1,128]{2,1,0:T(2,128)(2,1)S(1)} %get-tuple-element.70), channel_id=1, source_target_pairs={{0,1},{1,2},{2,3},{4,5},{5,6},{6,7},{8,9},{9,10},{10,11},{12,13},{... | collective-permute-start | bytes 12296 | tf_op jit(solution)/shard_map/ppermute | solution.py:22
  44.7 1.3 collective-permute-start.1
  46.6 2.5 %collective-permute-done.1 = bf16[16,1,128]{2,1,0:T(2,128)(2,1)S(1)} collective-permute-done((bf16[16,1,128]{2,1,0:T(2,128)(2,1)S(1)}, bf16[16,1,128]{2,1,0:T(2,128)(2,1)S(1)}, u32[]{:S(2)}, u32[]{:S(2)}) %collective-permute-start.1) | collective-permute-done | bytes 4128 | tf_op jit(solution)/shard_map/ppermute | solution.py:23
  49.1 0.4 multiply_reduce_fusion
  49.4 107.8 %all-gather.5.cloned.1.call-done = bf16[2048,3072]{1,0:T(8,128)(2,1)} async-done(((bf16[256,3072]{1,0:T(8,128)(2,1)}), bf16[2048,3072]{1,0:T(8,128)(2,1)}) %all-gather.5.cloned.1.call-update) | async-done | bytes 12582928 | tf_op jit(solution)/shard_map/all_gather | solution.py:60
  157.2 6.5 %convolution_convert_fusion.1 = bf16[128,3072]{1,0:T(8,128)(2,1)S(1)} fusion(bf16[2048,3072]{1,0:T(8,128)(2,1)} %all-gather.5.cloned.1.call-done, f32[128,2048]{1,0:T(8,128)S(1)} %get-tuple-element.72, f32[2048]{0:T(1024)S(1)} %copy-done.4, f32[128]{0:T(128)S(1)} %add_rsqrt_fusion), kind=kOutput, calls=%fused_computation.19 | convolution fusion | flops 1611792384 | bytes 14426624 | tf_op jit(solution)/shard_map/dot_general | solution.py:58
  163.7 4.5 %collective-permute-start.2 = (bf16[128,2048]{1,0:T(8,128)(2,1)S(1)}, bf16[128,2048]{1,0:T(8,128)(2,1)S(1)}, u32[]{:S(2)}, u32[]{:S(2)}) collective-permute-start(bf16[128,2048]{1,0:T(8,128)(2,1)S(1)} %slice.47), channel_id=1, source_target_pairs={{0,4},{4,8},{8,12},{12,16},{16,20},{20,24},{24,28},{1,5},{5,9},{9,... | collective-permute-start | bytes 1572872 | tf_op jit(solution)/shard_map/ppermute | solution.py:31
  168.4 1.9 collective-permute-start.4
  170.4 4.0 %collective-permute-done.2 = bf16[128,2048]{1,0:T(8,128)(2,1)S(1)} collective-permute-done((bf16[128,2048]{1,0:T(8,128)(2,1)S(1)}, bf16[128,2048]{1,0:T(8,128)(2,1)S(1)}, u32[]{:S(2)}, u32[]{:S(2)}) %collective-permute-start.2) | collective-permute-done | bytes 524320 | tf_op jit(solution)/shard_map/ppermute | solution.py:31
  174.3 4.4 %collective-permute-start.3 = (bf16[128,2048]{1,0:T(8,128)(2,1)S(1)}, bf16[128,2048]{1,0:T(8,128)(2,1)S(1)}, u32[]{:S(2)}, u32[]{:S(2)}) collective-permute-start(bf16[128,2048]{1,0:T(8,128)(2,1)S(1)} %collective-permute-done.2), channel_id=1, source_target_pairs={{0,4},{4,8},{8,12},{12,16},{16,20},{20,24},{24,28},{1,5},{5,9},{9,... | collective-permute-start | bytes 1572872 | tf_op jit(solution)/shard_map/ppermute | solution.py:31
  178.9 1.9 collective-permute-start.5
  180.8 4.0 %collective-permute-done.3 = bf16[128,2048]{1,0:T(8,128)(2,1)S(1)} collective-permute-done((bf16[128,2048]{1,0:T(8,128)(2,1)S(1)}, bf16[128,2048]{1,0:T(8,128)(2,1)S(1)}, u32[]{:S(2)}, u32[]{:S(2)}) %collective-permute-start.3) | collective-permute-done | bytes 524320 | tf_op jit(solution)/shard_map/ppermute | solution.py:31
  185.0 4.4 %collective-permute-done.5 = bf16[128,2048]{1,0:T(8,128)(2,1)S(1)} collective-permute-done((bf16[128,2048]{1,0:T(8,128)(2,1)S(1)}, bf16[128,2048]{1,0:T(8,128)(2,1)S(1)}, u32[]{:S(2)}, u32[]{:S(2)}) %collective-permute-start.5) | collective-permute-done | bytes 524320 | tf_op jit(solution)/shard_map/ppermute | solution.py:31
  189.5 0.7 slice_bitcast_fusion
  190.2 0.6 bitcast_bitcast_fusion
  190.8 0.3 copy-done.3
  191.1 6.6 %while.11 = (s32[]{:T(128)}, bf16[8,128,128]{2,1,0:T(8,128)(2,1)S(1)}, bf16[8,128,128]{2,1,0:T(8,128)(2,1)S(1)}, bf16[8,640,128]{2,1,0:T(8,128)(2,1)S(1)}, bf16[...) while((s32[]{:T(128)}, bf16[8,128,128]{2,1,0:T(8,128)(2,1)S(1)}, ...), condition=%wide.region_5.6_spmd.clone, body=%wide.region_2.5_spmd.clone.sunk | while | flops 42614528 | bytes 1381973 | solution.py:89
  191.9 0.3 fusion.44
  192.8 0.3 fusion.44
  193.6 0.3 fusion.44
  194.4 0.3 fusion.44
  197.9 0.8 reshape.99
  (52 shorter events, 6.6 us)
Async XLA Ops:
  6.5 34.9 %copy-start.2 = (bf16[16,8,128]{2,1,0:T(8,128)(2,1)S(1)}, bf16[16,8,128]{2,1,0:T(8,128)(2,1)}, u32[]{:S(2)}) copy-start(bf16[16,8,128]{2,1,0:T(8,128)(2,1)} %param.8) | copy-start | bytes 98308
  6.5 39.4 %copy-start = (bf16[3,128,2048]{2,1,0:T(8,128)(2,1)S(1)}, bf16[3,128,2048]{2,1,0:T(8,128)(2,1)}, u32[]{:S(2)}) copy-start(bf16[3,128,2048]{2,1,0:T(8,128)(2,1)} %param.10) | copy-start | bytes 4718596
  6.5 34.9 %all-gather.3.cloned.1.call-start = ((), (), s32[]{:S(2)}) async-start(), calls=%async_computation | async-start | bytes 1966080 | tf_op jit(solution)/shard_map/all_gather | solution.py:57
  7.3 150.0 %all-gather.5.cloned.1.call-start = ((), (), s32[]{:S(2)}) async-start(), calls=%async_computation.1 | async-start | bytes 14155776 | tf_op jit(solution)/shard_map/all_gather | solution.py:60
  41.4 4.9 %copy-start.1 = (bf16[16,8,2048]{2,1,0:T(8,128)(2,1)S(1)}, bf16[16,8,2048]{2,1,0:T(8,128)(2,1)}, u32[]{:S(2)}) copy-start(bf16[16,8,2048]{2,1,0:T(8,128)(2,1)} %param.9) | copy-start | bytes 1572868
  41.5 4.8 %collective-permute-start = (bf16[16,1,128]{2,1,0:T(2,128)(2,1)S(1)}, bf16[16,1,128]{2,1,0:T(2,128)(2,1)S(1)}, u32[]{:S(2)}, u32[]{:S(2)}) collective-permute-start(bf16[16,1,128]{2,1,0:T(2,128)(2,1)S(1)} %get-tuple-element.70), channel_id=1, source_target_pairs={{0,1},{1,2},{2,3},{4,5},{5,6},{6,7},{8,9},{9,10},{10,11},{12,13},{... | collective-permute-start | bytes 12296 | tf_op jit(solution)/shard_map/ppermute | solution.py:22
  44.7 4.4 %collective-permute-start.1 = (bf16[16,1,128]{2,1,0:T(2,128)(2,1)S(1)}, bf16[16,1,128]{2,1,0:T(2,128)(2,1)S(1)}, u32[]{:S(2)}, u32[]{:S(2)}) collective-permute-start(bf16[16,1,128]{2,1,0:T(2,128)(2,1)S(1)} %get-tuple-element.69), channel_id=1, source_target_pairs={{1,0},{2,1},{3,2},{5,4},{6,5},{7,6},{9,8},{10,9},{11,10},{13,12},{... | collective-permute-start | bytes 12296 | tf_op jit(solution)/shard_map/ppermute | solution.py:23
  46.6 110.7 %copy-start.4 = (f32[2048]{0:T(1024)S(1)}, f32[2048]{0:T(1024)}, u32[]{:S(2)}) copy-start(f32[2048]{0:T(1024)} %param.11) | copy-start | bytes 24580
  157.2 11.0 %copy-start.5 = (s32[1,1,5]{2,1,0:T(1,128)S(1)}, s32[1,1,5]{2,1,0:T(1,128)}, u32[]{:S(2)}) copy-start(s32[1,1,5]{2,1,0:T(1,128)} %param.13) | copy-start | bytes 64
  163.7 10.6 %collective-permute-start.2 = (bf16[128,2048]{1,0:T(8,128)(2,1)S(1)}, bf16[128,2048]{1,0:T(8,128)(2,1)S(1)}, u32[]{:S(2)}, u32[]{:S(2)}) collective-permute-start(bf16[128,2048]{1,0:T(8,128)(2,1)S(1)} %slice.47), channel_id=1, source_target_pairs={{0,4},{4,8},{8,12},{12,16},{16,20},{20,24},{24,28},{1,5},{5,9},{9,... | collective-permute-start | bytes 1572872 | tf_op jit(solution)/shard_map/ppermute | solution.py:31
  168.4 10.5 %collective-permute-start.4 = (bf16[128,2048]{1,0:T(8,128)(2,1)S(1)}, bf16[128,2048]{1,0:T(8,128)(2,1)S(1)}, u32[]{:S(2)}, u32[]{:S(2)}) collective-permute-start(bf16[128,2048]{1,0:T(8,128)(2,1)S(1)} %slice.47), channel_id=1, source_target_pairs={{4,0},{8,4},{12,8},{16,12},{20,16},{24,20},{28,24},{5,1},{9,5},{13... | collective-permute-start | bytes 1572872 | tf_op jit(solution)/shard_map/ppermute | solution.py:31
  174.3 10.5 %collective-permute-start.3 = (bf16[128,2048]{1,0:T(8,128)(2,1)S(1)}, bf16[128,2048]{1,0:T(8,128)(2,1)S(1)}, u32[]{:S(2)}, u32[]{:S(2)}) collective-permute-start(bf16[128,2048]{1,0:T(8,128)(2,1)S(1)} %collective-permute-done.2), channel_id=1, source_target_pairs={{0,4},{4,8},{8,12},{12,16},{16,20},{20,24},{24,28},{1,5},{5,9},{9,... | collective-permute-start | bytes 1572872 | tf_op jit(solution)/shard_map/ppermute | solution.py:31
  178.9 10.5 %collective-permute-start.5 = (bf16[128,2048]{1,0:T(8,128)(2,1)S(1)}, bf16[128,2048]{1,0:T(8,128)(2,1)S(1)}, u32[]{:S(2)}, u32[]{:S(2)}) collective-permute-start(bf16[128,2048]{1,0:T(8,128)(2,1)S(1)} %collective-permute-done.4), channel_id=1, source_target_pairs={{4,0},{8,4},{12,8},{16,12},{20,16},{24,20},{28,24},{5,1},{9,5},{13... | collective-permute-start | bytes 1572872 | tf_op jit(solution)/shard_map/ppermute | solution.py:31
  190.1 1.0 copy-start.3
Sparse Core Ops, SparseCore 0:
  9.2 32.1 all-gather.2
  43.0 114.1 all-gather.4
where the time goes:
time: 207 us; the launch traced here: 206 us
  waiting for transfers between devices  157 us (76%)
  starting transfers between devices  17.2 us (8%)
  between operations  13.6 us (7%)
  matrix products  12.1 us (6%)
  local copies, waits for them, and re-layouts  2.99 us (1%)
    all_gather x1, waiting for transfers between devices, per_device(): lax.all_gather(columns, 'tm', axis=0, tiled=True)  108 us
    all_gather x1, waiting for transfers between devices, per_device(): columns = lax.all_gather(w_qkv, 'depth', axis=1, tiled=True)  34.1 us
    ppermute x4, starting transfers between devices, from_behind(): return lax.ppermute(value, axis, pairs)  12.7 us
    ppermute x4, waiting for transfers between devices, from_behind(): return lax.ppermute(value, axis, pairs)  12.4 us
    dot_general x1, matrix products, per_device(): jnp.dot(normed, lax.all_gather(columns, 'tm', axis=0, tiled=True), prefer...  6.45 us
  transfers between devices with their start and end apart: 8, of which 7 were waited for; matrix products, arithmetic and copies ran while one was open for 1% of the time, Pallas kernels for 0%

commit v1 on v0

--- a/solution.py
+++ b/solution.py
@@ -1,8 +1,11 @@
+import functools
 import math
 
 import jax
 import jax.numpy as jnp
 from jax import lax
+from jax.experimental import pallas as pl
+from jax.experimental.pallas import tpu as pltpu
 from jax.sharding import PartitionSpec as P
 
 HEADS = 8
@@ -10,6 +13,8 @@
 BT = 16
 PP = 8
 RD = 2
+VMEM = pltpu.VMEM
+SMEM = pltpu.SMEM
 
 
 def padded_2(value, sides, width):
@@ -25,25 +30,7 @@
     return value
 
 
-def from_behind(value, axis, by):
-    devices = lax.axis_size(axis)
-    pairs = [(i, i + by) for i in range(devices) if 0 <= i + by < devices]
-    return lax.ppermute(value, axis, pairs)
-
-
-def head_attend(query_head, key_head, value_head, allowed):
-    inv_root = 1.0 / math.sqrt(HD)
-    scores = (
-        jnp.einsum("qd,kd->qk", query_head, key_head, preferred_element_type=jnp.float32) * inv_root
-    )
-    scores = jnp.where(allowed, scores, -1e30)
-    row_max = jnp.max(scores, axis=-1, keepdims=True)
-    powers = jnp.exp(scores - row_max)
-    weights = (powers / jnp.sum(powers, axis=-1, keepdims=True)).astype(jnp.bfloat16)
-    return jnp.dot(weights, value_head, preferred_element_type=jnp.float32).astype(jnp.bfloat16)
-
-
-def per_device(raw, stream, conv_w, gain, w_qkv, mask):
+def normed_tokens(raw, stream, conv_w, gain):
     time_len, site_len, feat_len = raw.shape
     tok_rows = time_len * site_len
     padded = padded_2(raw, (("depth", 1),), 1)
@@ -51,9 +38,205 @@
     for offset in range(3):
         window = padded[:, offset : offset + site_len].reshape(tok_rows, feat_len)
         embedded = embedded + jnp.dot(window, conv_w[offset], preferred_element_type=jnp.float32)
-    normed = (
-        embedded * lax.rsqrt(jnp.mean(embedded * embedded, axis=-1, keepdims=True) + 1e-05) * gain
-    ).astype(jnp.bfloat16)
+    scale = lax.rsqrt(jnp.mean(embedded * embedded, axis=-1, keepdims=True) + 1e-05)
+    return (embedded * scale * gain).astype(jnp.bfloat16)
+
+
+def hop(value, fn, zs):
+    pairs = []
+    for z in range(zs):
+        for core in range(2):
+            for depth in range(4):
+                to = fn(z, core, depth)
+                if to is not None:
+                    pairs.append(((2 * z + core) * 4 + depth, (2 * to[0] + to[1]) * 4 + to[2]))
+    return lax.ppermute(value, ("tm", "depth"), pairs)
+
+
+def swap_core(value, zs):
+    return hop(value, lambda z, c, d: (z, 1 - c, d), zs)
+
+
+def swap_depth(value, bits, zs):
+    return hop(value, lambda z, c, d: (z, c, d ^ bits), zs)
+
+
+def move_z(value, by, zs, first=0, last=None):
+    last = zs if last is None else last
+    return hop(value, lambda z, c, d: (z + by, c, d) if 0 <= z + by < zs and first <= z < last else None, zs)
+
+
+def project_kernel(zs, place, *refs):
+    x_refs, shards = refs[:2], refs[2 : 2 + 2 * zs - 1]
+    q_ref, kv_ref, w_full = refs[2 + 2 * zs - 1 :]
+    z, core = place[0], place[1]
+    rows = shards[0].shape[0]
+    for r in range(-(zs - 1), zs):
+        source = z - r
+
+        @pl.when((source >= 0) & (source < zs))
+        def _():
+            at = pl.ds(pl.multiple_of(source * rows, rows), rows)
+            for part in range(3):
+                third = pl.multiple_of(place[2 + part] * HD, HD)
+                w_full[at, pl.ds(third, HD)] = shards[r + zs - 1][:, part * HD : (part + 1) * HD]
+
+    block = x_refs[0].shape[1]
+    for rel in range(2):
+        u = core ^ rel
+
+        def body(step, carry):
+            pair = x_refs[rel][pl.ds(2 * step, 2)].reshape(2 * block, x_refs[rel].shape[2])
+            out = jnp.dot(pair, w_full[...], preferred_element_type=jnp.float32)
+            out = out.astype(jnp.bfloat16).reshape(2, block, 3 * HD)
+            at = pl.ds(pl.multiple_of(u * block, block), block)
+            q_ref[pl.ds(2 * step, 2), at, :] = out[:, :, :HD]
+            kv_ref[pl.ds(2 * step, 2), at, :] = out[:, :, HD:]
+            return carry
+
+        lax.fori_loop(0, 2, body, 0)
+
+
+def attend_kernel(place, mask, q_ref, before, own, after, keep_ref, send_ref):
+    core = place[1]
+    block = q_ref.shape[1] // 2
+    inv_root = 1.0 / math.sqrt(HD)
+
+    def body(r, carry):
+        q = q_ref[r]
+        scores = []
+        for side, kv in enumerate((before, own, after)):
+            s = lax.dot_general(q, kv[r][:, :HD], (((1,), (1,)), ((), ())), preferred_element_type=jnp.float32)
+            s = (s * inv_root).reshape(2, block, 2, block)
+            rows = []
+            for u in range(2):
+                cols = []
+                for v in range(2):
+                    entry = 2 * side + v - u
+                    piece = s[u, :, v]
+                    if 0 <= entry <= 4:
+                        flag = mask[((u ^ core) * 4 + r) * 5 + entry]
+                        piece = jnp.where(flag > 0, piece, -1e30)
+                    else:
+                        piece = jnp.full_like(piece, -1e30)
+                    cols.append(piece)
+                rows.append(jnp.concatenate(cols, axis=1))
+            scores.append(jnp.concatenate(rows, axis=0))
+        top = functools.reduce(jnp.maximum, [jnp.max(s, axis=1, keepdims=True) for s in scores])
+        powers = [jnp.exp(s - top) for s in scores]
+        total = functools.reduce(jnp.add, [jnp.sum(p, axis=1, keepdims=True) for p in powers])
+        inverse = 1.0 / total
+        result = jnp.zeros((2 * block, HD), jnp.float32)
+        for p, kv in zip(powers, (before, own, after)):
+            w = (p * inverse).astype(jnp.bfloat16)
+            result += jnp.dot(w, kv[r][:, HD:], preferred_element_type=jnp.float32)
+        result = result.astype(jnp.bfloat16)
+        for u in range(2):
+
+            @pl.when(core == u)
+            def _():
+                keep_ref[r] = result[u * block : (u + 1) * block]
+                send_ref[r] = result[(1 - u) * block : (2 - u) * block]
+
+        return carry
+
+    lax.fori_loop(0, 4, body, 0)
+
+
+def gather_kernel(place, own, x, y, diagonal, out_ref):
+    core, depth = place[1], place[5]
+    for r, ref in enumerate((own, x, y, diagonal)):
+        for rel in range(2):
+            at = pl.multiple_of((2 * (depth ^ r) + (core ^ rel)) * HD, HD)
+            out_ref[:, pl.ds(at, HD)] = ref[:, rel * HD : (rel + 1) * HD]
+
+
+def vmem_call(kernel, outs, scratch=(), smem=1, total=1, limit=40):
+    return pl.pallas_call(
+        kernel,
+        out_shape=outs,
+        in_specs=[pl.BlockSpec(memory_space=SMEM)] * smem + [pl.BlockSpec(memory_space=VMEM)] * (total - smem),
+        out_specs=jax.tree.map(lambda _: pl.BlockSpec(memory_space=VMEM), outs),
+        scratch_shapes=list(scratch),
+        compiler_params=pltpu.CompilerParams(vmem_limit_bytes=limit * 2**20),
+    )
+
+
+def plane_device(raw, stream, conv_w, gain, w_qkv, mask):
+    zs = lax.axis_size("tm") // 2
+    tm, depth = lax.axis_index("tm"), lax.axis_index("depth")
+    z, core = tm // 2, tm % 2
+    time_len, site_len, _ = raw.shape
+    block = time_len * site_len
+    width = stream.shape[2]
+
+    rows = w_qkv.shape[0]
+    grouped = w_qkv.reshape(rows, 3, 2, HD)
+    keep = lax.dynamic_index_in_dim(grouped, core, 2, keepdims=False)
+    send = lax.dynamic_index_in_dim(grouped, 1 - core, 2, keepdims=False)
+    received = swap_core(send, zs)
+    first = core == 0
+    both = jnp.concatenate([jnp.where(first, keep, received), jnp.where(first, received, keep)], axis=0)
+    parts = [hop(both[:, k], lambda z, c, d, k=k: (z, c, (k - d) % 4), zs) for k in range(3)]
+    shard = jnp.concatenate(parts, axis=1)
+    thirds = [(3 * ((k - depth) % 4) + k) // 4 for k in range(3)]
+
+    normed = normed_tokens(raw, stream, conv_w, gain)
+
+    ahead, back = [shard], [shard]
+    for r in range(1, zs):
+        ahead.append(move_z(ahead[-1], 1, zs, first=r - 1))
+        back.append(move_z(back[-1], -1, zs, last=zs - r + 1))
+    shards = back[:0:-1] + ahead
+
+    own_tokens = jnp.stack([normed] + [swap_depth(normed, bits, zs) for bits in (1, 2, 3)])
+    other_tokens = swap_core(own_tokens, zs)
+
+    flags = mask.reshape(1, mask.shape[2])
+    flags = jnp.concatenate([flags] + [swap_depth(flags, bits, zs) for bits in (1, 2, 3)])
+    flags = jnp.concatenate([flags, swap_core(flags, zs)]).reshape(-1)
+
+    place = jnp.stack([z, core] + thirds + [depth]).astype(jnp.int32)
+    bf16 = jnp.bfloat16
+    q, kv = vmem_call(
+        functools.partial(project_kernel, zs),
+        (jax.ShapeDtypeStruct((4, 2 * block, HD), bf16), jax.ShapeDtypeStruct((4, 2 * block, 2 * HD), bf16)),
+        scratch=[VMEM((width, 3 * HD), bf16)],
+        total=3 + 2 * zs - 1,
+    )(place, own_tokens, other_tokens, *shards)
+
+    before = move_z(kv, 1, zs)
+    after = move_z(kv, -1, zs)
+    piece = jax.ShapeDtypeStruct((4, block, HD), bf16)
+    kept, sent = vmem_call(attend_kernel, (piece, piece), smem=2, total=6)(place, flags, q, before, kv, after)
+    pair = jnp.concatenate([kept, swap_core(sent, zs)], axis=2)
+    pieces = [pair[0]] + [swap_depth(pair[bits], bits, zs) for bits in (1, 2, 3)]
+    context = vmem_call(gather_kernel, jax.ShapeDtypeStruct((block, HEADS * HD), bf16), total=5)(place, *pieces)
+    return context.reshape(time_len, site_len, HEADS * HD)
+
+
+def from_behind(value, axis, by):
+    devices = lax.axis_size(axis)
+    pairs = [(i, i + by) for i in range(devices) if 0 <= i + by < devices]
+    return lax.ppermute(value, axis, pairs)
+
+
+def head_attend(query_head, key_head, value_head, allowed):
+    inv_root = 1.0 / math.sqrt(HD)
+    scores = (
+        jnp.einsum("qd,kd->qk", query_head, key_head, preferred_element_type=jnp.float32) * inv_root
+    )
+    scores = jnp.where(allowed, scores, -1e30)
+    row_max = jnp.max(scores, axis=-1, keepdims=True)
+    powers = jnp.exp(scores - row_max)
+    weights = (powers / jnp.sum(powers, axis=-1, keepdims=True)).astype(jnp.bfloat16)
+    return jnp.dot(weights, value_head, preferred_element_type=jnp.float32).astype(jnp.bfloat16)
+
+
+def per_device(raw, stream, conv_w, gain, w_qkv, mask):
+    time_len, site_len, _ = raw.shape
+    tok_rows = time_len * site_len
+    normed = normed_tokens(raw, stream, conv_w, gain)
     columns = lax.all_gather(w_qkv, "depth", axis=1, tiled=True)
     projected = jnp.dot(
         normed,
@@ -103,6 +286,7 @@
         P("depth", "tm", None),
     )
     out_specs = P("tm", "depth", None)
+    fits = mesh.shape["depth"] == 4 and mesh.shape["tm"] % 2 == 0
     return jax.shard_map(
-        per_device, mesh=mesh, in_specs=in_specs, out_specs=out_specs, check_vma=False
-    )
+        plane_device if fits else per_device, mesh=mesh, in_specs=in_specs, out_specs=out_specs, check_vma=False
+    )

time: 207 us -> 125 us (0.60)
  the two profiles are of different devices: /device:TPU:9 before, /device:TPU:0 now
where the time goes in v1:
time: 125 us
  waiting for transfers between devices  61.9 us (50%)
  starting transfers between devices  37.8 us (30%)
  Pallas kernels  12.1 us (10%)
  local copies, waits for them, and re-layouts  8.99 us (7%)
  matrix products  2.79 us (2%)
    ppermute x24, waiting for transfers between devices, hop(): return lax.ppermute(value, ('tm', 'depth'), pairs)  61 us
    ppermute x24, starting transfers between devices, hop(): return lax.ppermute(value, ('tm', 'depth'), pairs)  31.7 us
    pallas_call x1, Pallas kernels, plane_device(): vmem_call(attend_kernel, (piece, piece), smem=2, total=6)  5.8 us
    unnamed x26, local copies, waits for them, and re-layouts  5.27 us
    pallas_call x1, Pallas kernels, plane_device(): vmem_call(functools.partial(project_kernel, zs), (jax.ShapeDtypeStruct((4...  5.02 us
    ppermute x1, starting transfers between devices, padded_2(): before = lax.ppermute(last, axis, up)  4.83 us
    dot_general x3, matrix products, normed_tokens(): jnp.dot(window, conv_w[offset], preferred_element_type=jnp.float32)  2.79 us
  transfers between devices with their start and end apart: 26, of which 18 were waited for; matrix products, arithmetic and copies ran while one was open for 4% of the time, Pallas kernels for 0%

profile of v1, /device:TPU:0, one launch (start us, length us, event | category | flops | bytes accessed | tf_op | source)
XLA Modules:
  0.0 124.8 jit_solution(17840555614424188687)
XLA Ops:
  0.0 1.5 %fusion.22 = (bf16[16,1,128]{2,1,0:T(2,128)(2,1)}, bf16[16,1,128]{2,1,0:T(2,128)(2,1)}) fusion(bf16[16,8,128]{2,1,0:T(8,128)(2,1)} %param.6), kind=kLoop, calls=%fused_computation.49 | loop fusion | bytes 16384 | tf_op jit(solution)/shard_map/slice | solution.py:26
  1.5 4.8 %collective-permute-start.4 = (bf16[16,1,128]{2,1,0:T(2,128)(2,1)}, bf16[16,1,128]{2,1,0:T(2,128)(2,1)S(1)}, u32[]{:S(2)}, u32[]{:S(2)}) collective-permute-start(bf16[16,1,128]{2,1,0:T(2,128)(2,1)} %get-tuple-element.25), channel_id=1, source_target_pairs={{0,1},{1,2},{2,3},{4,5},{5,6},{6,7},{8,9},{9,10},{10,11},{12,13},{... | collective-permute-start | bytes 12296 | tf_op jit(solution)/shard_map/ppermute | solution.py:27
  7.7 1.3 %fusion.2 = f32[128,2048]{1,0:T(8,128)S(1)} fusion(bf16[3,128,2048]{2,1,0:T(8,128)(2,1)} %param.8, bf16[16,8,128]{2,1,0:T(8,128)(2,1)} %param.6), kind=kOutput, calls=%fused_computation.7 | convolution fusion | flops 67108864 | bytes 1605632 | tf_op jit(solution)/shard_map/dot_general | solution.py:40
  12.7 2.5 %collective-permute-start.6 = (bf16[128,2048]{1,0:T(8,128)(2,1)S(1)}, bf16[128,2048]{1,0:T(8,128)(2,1)S(1)}, u32[]{:S(2)}, u32[]{:S(2)}) collective-permute-start(bf16[128,2048]{1,0:T(8,128)(2,1)S(1)} %multiply_convert_fusion), channel_id=1, source_target_pairs={{0,1},{1,0},{2,3},{3,2},{4,5},{5,4},{6,7},{7,6},{8,9},{9,8},{10,11... | collective-permute-start | bytes 1572872 | tf_op jit(solution)/shard_map/ppermute | solution.py:53
  18.4 9.6 %collective-permute-done.6 = bf16[128,2048]{1,0:T(8,128)(2,1)S(1)} collective-permute-done((bf16[128,2048]{1,0:T(8,128)(2,1)S(1)}, bf16[128,2048]{1,0:T(8,128)(2,1)S(1)}, u32[]{:S(2)}, u32[]{:S(2)}) %collective-permute-start.6) | collective-permute-done | bytes 524320 | tf_op jit(solution)/shard_map/ppermute | solution.py:53
  28.0 10.0 %collective-permute-done.7 = bf16[128,2048]{1,0:T(8,128)(2,1)S(1)} collective-permute-done((bf16[128,2048]{1,0:T(8,128)(2,1)S(1)}, bf16[128,2048]{1,0:T(8,128)(2,1)S(1)}, u32[]{:S(2)}, u32[]{:S(2)}) %collective-permute-start.7) | collective-permute-done | bytes 524320 | tf_op jit(solution)/shard_map/ppermute | solution.py:53
  38.0 1.6 %collective-permute-done.8 = bf16[128,2048]{1,0:T(8,128)(2,1)S(1)} collective-permute-done((bf16[128,2048]{1,0:T(8,128)(2,1)S(1)}, bf16[128,2048]{1,0:T(8,128)(2,1)S(1)}, u32[]{:S(2)}, u32[]{:S(2)}) %collective-permute-start.8) | collective-permute-done | bytes 524320 | tf_op jit(solution)/shard_map/ppermute | solution.py:53
  40.7 3.6 %collective-permute-start.12 = (bf16[512,128]{1,0:T(8,128)(2,1)S(1)}, bf16[512,128]{1,0:T(8,128)(2,1)S(1)}, u32[]{:S(2)}, u32[]{:S(2)}) collective-permute-start(bf16[512,128]{1,0:T(8,128)(2,1)S(1)} %get-tuple-element.17), channel_id=1, source_target_pairs={{0,1},{1,0},{2,3},{3,2},{4,5},{5,4},{6,7},{7,6},{8,9},{9,8},{10,11... | collective-permute-start | bytes 393224 | tf_op jit(solution)/shard_map/ppermute | solution.py:53
  44.3 2.2 %collective-permute-start.13 = (bf16[512,128]{1,0:T(8,128)(2,1)S(1)}, bf16[512,128]{1,0:T(8,128)(2,1)S(1)}, u32[]{:S(2)}, u32[]{:S(2)}) collective-permute-start(bf16[512,128]{1,0:T(8,128)(2,1)S(1)} %get-tuple-element.15), channel_id=1, source_target_pairs={{0,2},{1,1},{2,0},{3,3},{4,6},{5,5},{6,4},{7,7},{8,10},{9,9},{10,8... | collective-permute-start | bytes 393224 | tf_op jit(solution)/shard_map/ppermute | solution.py:53
  46.6 1.6 %collective-permute-done.12 = bf16[512,128]{1,0:T(8,128)(2,1)S(1)} collective-permute-done((bf16[512,128]{1,0:T(8,128)(2,1)S(1)}, bf16[512,128]{1,0:T(8,128)(2,1)S(1)}, u32[]{:S(2)}, u32[]{:S(2)}) %collective-permute-start.12) | collective-permute-done | bytes 131104 | tf_op jit(solution)/shard_map/ppermute | solution.py:53
  48.2 3.3 %collective-permute-done.13 = bf16[512,128]{1,0:T(8,128)(2,1)S(1)} collective-permute-done((bf16[512,128]{1,0:T(8,128)(2,1)S(1)}, bf16[512,128]{1,0:T(8,128)(2,1)S(1)}, u32[]{:S(2)}, u32[]{:S(2)}) %collective-permute-start.13) | collective-permute-done | bytes 131104 | tf_op jit(solution)/shard_map/ppermute | solution.py:53
  52.8 4.6 %collective-permute-start.17 = (bf16[512,384]{1,0:T(8,128)(2,1)S(1)}, bf16[512,384]{1,0:T(8,128)(2,1)S(1)}, u32[]{:S(2)}, u32[]{:S(2)}) collective-permute-start(bf16[512,384]{1,0:T(8,128)(2,1)S(1)} %constant_dynamic-update-slice_fusion.refs_5_), channel_id=1, source_target_pairs={{0,8},{1,9},{2,10},{3,11},{4,12},{5,13},{6,14},{7,15},{8,16},{9,17... | collective-permute-start | bytes 1179656 | tf_op jit(solution)/shard_map/ppermute | solution.py:53
  57.4 6.1 %collective-permute-done.14.refs_4_ = bf16[512,384]{1,0:T(8,128)(2,1)S(1)} collective-permute-done((bf16[512,384]{1,0:T(8,128)(2,1)S(1)}, bf16[512,384]{1,0:T(8,128)(2,1)S(1)}, u32[]{:S(2)}, u32[]{:S(2)}) %collective-permute-start.14) | collective-permute-done | bytes 393248 | tf_op jit(solution)/shard_map/ppermute | solution.py:53
  64.8 1.4 %collective-permute-start.18 = (bf16[512,384]{1,0:T(8,128)(2,1)S(1)}, bf16[512,384]{1,0:T(8,128)(2,1)}, u32[]{:S(2)}, u32[]{:S(2)}) collective-permute-start(bf16[512,384]{1,0:T(8,128)(2,1)S(1)} %collective-permute-done.17.refs_6_), channel_id=1, source_target_pairs={{8,16},{9,17},{10,18},{11,19},{12,20},{13,21},{14,22},{15,23},{16,... | collective-permute-start | bytes 1179656 | tf_op jit(solution)/shard_map/ppermute | solution.py:53
  67.0 7.7 %collective-permute-done.15.refs_3_ = bf16[512,384]{1,0:T(8,128)(2,1)} collective-permute-done((bf16[512,384]{1,0:T(8,128)(2,1)S(1)}, bf16[512,384]{1,0:T(8,128)(2,1)}, u32[]{:S(2)}, u32[]{:S(2)}) %collective-permute-start.15) | collective-permute-done | bytes 393248 | tf_op jit(solution)/shard_map/ppermute | solution.py:53
  76.9 8.2 %collective-permute-done.16.refs_2_ = bf16[512,384]{1,0:T(8,128)(2,1)} collective-permute-done((bf16[512,384]{1,0:T(8,128)(2,1)}, bf16[512,384]{1,0:T(8,128)(2,1)}, u32[]{:S(2)}, u32[]{:S(2)}) %collective-permute-start.16) | collective-permute-done | bytes 393248 | tf_op jit(solution)/shard_map/ppermute | solution.py:53
  87.8 5.0 %shard_map.64 = (bf16[4,256,128]{2,1,0:T(8,128)(2,1)S(1)}, bf16[4,256,256]{2,1,0:T(8,128)(2,1)S(1)}) custom-call(s32[6]{0:T(128)S(1)} %stack.42.place, bf16[4,128,2048]{2,1,0:T(8,128)(2,1)S(1)} %pad_maximum_fusion.refs_0_, bf16[4,128,2048]{2,1,0:T(8,128)(2,1)} %collective-permute-done.9.refs_1_, bf16[512,384]{1,0:T(8,128)(2,1)} %collective-permute-done.16.refs_2_, ...), custom_call_target="tpu_custom_call" | custom-call | tf_op jit(solution)/shard_map/pallas_call | solution.py:201
  93.6 1.5 %collective-permute-start.20 = (bf16[4,256,256]{2,1,0:T(8,128)(2,1)S(1)}, bf16[4,256,256]{2,1,0:T(8,128)(2,1)S(1)}, u32[]{:S(2)}, u32[]{:S(2)}) collective-permute-start(bf16[4,256,256]{2,1,0:T(8,128)(2,1)S(1)} %get-tuple-element.10.own), channel_id=1, source_target_pairs={{0,8},{1,9},{2,10},{3,11},{4,12},{5,13},{6,14},{7,15},{8,16},{9,17... | collective-permute-start | bytes 1572872 | tf_op jit(solution)/shard_map/ppermute | solution.py:53
  96.9 3.0 %collective-permute-start.2 = (s32[1,5]{1,0:T(1,128)S(1)}, s32[1,5]{1,0:T(1,128)S(1)}, u32[]{:S(2)}, u32[]{:S(2)}) collective-permute-start(s32[1,5]{1,0:T(1,128)S(1)} %bitcast.67), channel_id=1, source_target_pairs={{0,3},{1,2},{2,1},{3,0},{4,7},{5,6},{6,5},{7,4},{8,11},{9,10},{10,... | collective-permute-start | bytes 68 | tf_op jit(solution)/shard_map/ppermute | solution.py:53
  100.1 1.4 %collective-permute-done.2 = s32[1,5]{1,0:T(1,128)S(1)} collective-permute-done((s32[1,5]{1,0:T(1,128)S(1)}, s32[1,5]{1,0:T(1,128)S(1)}, u32[]{:S(2)}, u32[]{:S(2)}) %collective-permute-start.2) | collective-permute-done | bytes 52 | tf_op jit(solution)/shard_map/ppermute | solution.py:53
  102.8 6.1 %collective-permute-done.21.after = bf16[4,256,256]{2,1,0:T(8,128)(2,1)S(1)} collective-permute-done((bf16[4,256,256]{2,1,0:T(8,128)(2,1)S(1)}, bf16[4,256,256]{2,1,0:T(8,128)(2,1)S(1)}, u32[]{:S(2)}, u32[]{:S(2)}) %collective-permute-start.21) | collective-permute-done | bytes 524320 | tf_op jit(solution)/shard_map/ppermute | solution.py:53
  109.8 5.8 %shard_map.65 = (bf16[4,128,128]{2,1,0:T(8,128)(2,1)S(1)}, bf16[4,128,128]{2,1,0:T(8,128)(2,1)S(1)}) custom-call(s32[6]{0:T(128)S(1)} %stack.42.place, s32[40]{0:T(128)S(1)} %reshape.34.mask, bf16[4,256,128]{2,1,0:T(8,128)(2,1)S(1)} %copy-done.5, bf16[4,256,256]{2,1,0:T(8,128)(2,1)S(1)} %collective-permute-done.20.before, ...), custom_call_target="tpu_custom_call" | custom-call | tf_op jit(solution)/shard_map/pallas_call | solution.py:211
  118.3 2.3 %collective-permute-start.25 = (bf16[128,256]{1,0:T(8,128)(2,1)S(1)}, bf16[128,256]{1,0:T(8,128)(2,1)S(1)}, u32[]{:S(2)}, u32[]{:S(2)}) collective-permute-start(bf16[128,256]{1,0:T(8,128)(2,1)S(1)} %get-tuple-element.20), channel_id=1, source_target_pairs={{0,3},{1,2},{2,1},{3,0},{4,7},{5,6},{6,5},{7,4},{8,11},{9,10},{10,... | collective-permute-start | bytes 196616 | tf_op jit(solution)/shard_map/ppermute | solution.py:53
  123.5 1.3 %shard_map.66 = bf16[128,1024]{1,0:T(8,128)(2,1)} custom-call(s32[6]{0:T(128)S(1)} %stack.42.place, bf16[128,256]{1,0:T(8,128)(2,1)S(1)} %get-tuple-element.23.own, bf16[128,256]{1,0:T(8,128)(2,1)S(1)} %collective-permute-done.23.x, bf16[128,256]{1,0:T(8,128)(2,1)S(1)} %collective-permute-done.24.y, bf16[128,256]{1,0:T(8,128)(2,1)S(1)} %collective-permute-done.25.diagonal), custom_call_target="tpu_custom_call" | custom-call | tf_op jit(solution)/shard_map/pallas_call | solution.py:214
  (76 shorter events, 27.8 us)
Async XLA Ops:
  1.5 8.6 %collective-permute-start.4 = (bf16[16,1,128]{2,1,0:T(2,128)(2,1)}, bf16[16,1,128]{2,1,0:T(2,128)(2,1)S(1)}, u32[]{:S(2)}, u32[]{:S(2)}) collective-permute-start(bf16[16,1,128]{2,1,0:T(2,128)(2,1)} %get-tuple-element.25), channel_id=1, source_target_pairs={{0,1},{1,2},{2,3},{4,5},{5,6},{6,7},{8,9},{9,10},{10,11},{12,13},{... | collective-permute-start | bytes 12296 | tf_op jit(solution)/shard_map/ppermute | solution.py:27
  6.4 5.8 %collective-permute-start.5 = (bf16[16,1,128]{2,1,0:T(2,128)(2,1)}, bf16[16,1,128]{2,1,0:T(2,128)(2,1)S(1)}, u32[]{:S(2)}, u32[]{:S(2)}) collective-permute-start(bf16[16,1,128]{2,1,0:T(2,128)(2,1)} %get-tuple-element.24), channel_id=1, source_target_pairs={{1,0},{2,1},{3,2},{5,4},{6,5},{7,6},{9,8},{10,9},{11,10},{13,12},{... | collective-permute-start | bytes 12296 | tf_op jit(solution)/shard_map/ppermute | solution.py:28
  12.7 15.3 %collective-permute-start.6 = (bf16[128,2048]{1,0:T(8,128)(2,1)S(1)}, bf16[128,2048]{1,0:T(8,128)(2,1)S(1)}, u32[]{:S(2)}, u32[]{:S(2)}) collective-permute-start(bf16[128,2048]{1,0:T(8,128)(2,1)S(1)} %multiply_convert_fusion), channel_id=1, source_target_pairs={{0,1},{1,0},{2,3},{3,2},{4,5},{5,4},{6,7},{7,6},{8,9},{9,8},{10,11... | collective-permute-start | bytes 1572872 | tf_op jit(solution)/shard_map/ppermute | solution.py:53
  15.2 22.8 %collective-permute-start.7 = (bf16[128,2048]{1,0:T(8,128)(2,1)S(1)}, bf16[128,2048]{1,0:T(8,128)(2,1)S(1)}, u32[]{:S(2)}, u32[]{:S(2)}) collective-permute-start(bf16[128,2048]{1,0:T(8,128)(2,1)S(1)} %multiply_convert_fusion), channel_id=1, source_target_pairs={{0,2},{1,3},{2,0},{3,1},{4,6},{5,7},{6,4},{7,5},{8,10},{9,11},{10,... | collective-permute-start | bytes 1572872 | tf_op jit(solution)/shard_map/ppermute | solution.py:53
  16.4 23.2 %collective-permute-start.8 = (bf16[128,2048]{1,0:T(8,128)(2,1)S(1)}, bf16[128,2048]{1,0:T(8,128)(2,1)S(1)}, u32[]{:S(2)}, u32[]{:S(2)}) collective-permute-start(bf16[128,2048]{1,0:T(8,128)(2,1)S(1)} %multiply_convert_fusion), channel_id=1, source_target_pairs={{0,3},{1,2},{2,1},{3,0},{4,7},{5,6},{6,5},{7,4},{8,11},{9,10},{10,... | collective-permute-start | bytes 1572872 | tf_op jit(solution)/shard_map/ppermute | solution.py:53
  18.1 21.8 %collective-permute-start.10 = (bf16[256,3,128]{2,0,1:T(8,128)(2,1)S(1)}, bf16[256,3,128]{2,0,1:T(8,128)(2,1)S(1)}, u32[]{:S(2)}, u32[]{:S(2)}) collective-permute-start(bf16[256,3,128]{2,0,1:T(8,128)(2,1)S(1)} %bitcast.64), channel_id=1, source_target_pairs={{0,4},{1,5},{2,6},{3,7},{4,0},{5,1},{6,2},{7,3},{8,12},{9,13},{10,... | collective-permute-start | bytes 589832 | tf_op jit(solution)/shard_map/ppermute | solution.py:53
  39.8 46.0 %collective-permute-start.9 = (bf16[4,128,2048]{2,1,0:T(8,128)(2,1)S(1)}, bf16[4,128,2048]{2,1,0:T(8,128)(2,1)}, u32[]{:S(2)}, u32[]{:S(2)}) collective-permute-start(bf16[4,128,2048]{2,1,0:T(8,128)(2,1)S(1)} %pad_maximum_fusion.refs_0_), channel_id=1, source_target_pairs={{0,4},{1,5},{2,6},{3,7},{4,0},{5,1},{6,2},{7,3},{8,12},{9,13},{10,... | collective-permute-start | bytes 6291464 | tf_op jit(solution)/shard_map/ppermute | solution.py:53
  40.0 6.5 %collective-permute-start.11 = (bf16[512,128]{1,0:T(8,128)(2,1)S(1)}, bf16[512,128]{1,0:T(8,128)(2,1)S(1)}, u32[]{:S(2)}, u32[]{:S(2)}) collective-permute-start(bf16[512,128]{1,0:T(8,128)(2,1)S(1)} %get-tuple-element.16), channel_id=1, source_target_pairs={{0,0},{1,3},{2,2},{3,1},{4,4},{5,7},{6,6},{7,5},{8,8},{9,11},{10,1... | collective-permute-start | bytes 393224 | tf_op jit(solution)/shard_map/ppermute | solution.py:53
  40.7 7.5 %collective-permute-start.12 = (bf16[512,128]{1,0:T(8,128)(2,1)S(1)}, bf16[512,128]{1,0:T(8,128)(2,1)S(1)}, u32[]{:S(2)}, u32[]{:S(2)}) collective-permute-start(bf16[512,128]{1,0:T(8,128)(2,1)S(1)} %get-tuple-element.17), channel_id=1, source_target_pairs={{0,1},{1,0},{2,3},{3,2},{4,5},{5,4},{6,7},{7,6},{8,9},{9,8},{10,11... | collective-permute-start | bytes 393224 | tf_op jit(solution)/shard_map/ppermute | solution.py:53
  44.3 7.2 %collective-permute-start.13 = (bf16[512,128]{1,0:T(8,128)(2,1)S(1)}, bf16[512,128]{1,0:T(8,128)(2,1)S(1)}, u32[]{:S(2)}, u32[]{:S(2)}) collective-permute-start(bf16[512,128]{1,0:T(8,128)(2,1)S(1)} %get-tuple-element.15), channel_id=1, source_target_pairs={{0,2},{1,1},{2,0},{3,3},{4,6},{5,5},{6,4},{7,7},{8,10},{9,9},{10,8... | collective-permute-start | bytes 393224 | tf_op jit(solution)/shard_map/ppermute | solution.py:53
  51.5 12.0 %collective-permute-start.14 = (bf16[512,384]{1,0:T(8,128)(2,1)S(1)}, bf16[512,384]{1,0:T(8,128)(2,1)S(1)}, u32[]{:S(2)}, u32[]{:S(2)}) collective-permute-start(bf16[512,384]{1,0:T(8,128)(2,1)S(1)} %constant_dynamic-update-slice_fusion.refs_5_), channel_id=1, source_target_pairs={{8,0},{9,1},{10,2},{11,3},{12,4},{13,5},{14,6},{15,7},{16,8},{17,9... | collective-permute-start | bytes 1179656 | tf_op jit(solution)/shard_map/ppermute | solution.py:53
  52.8 12.0 %collective-permute-start.17 = (bf16[512,384]{1,0:T(8,128)(2,1)S(1)}, bf16[512,384]{1,0:T(8,128)(2,1)S(1)}, u32[]{:S(2)}, u32[]{:S(2)}) collective-permute-start(bf16[512,384]{1,0:T(8,128)(2,1)S(1)} %constant_dynamic-update-slice_fusion.refs_5_), channel_id=1, source_target_pairs={{0,8},{1,9},{2,10},{3,11},{4,12},{5,13},{6,14},{7,15},{8,16},{9,17... | collective-permute-start | bytes 1179656 | tf_op jit(solution)/shard_map/ppermute | solution.py:53
  63.5 11.1 %collective-permute-start.15 = (bf16[512,384]{1,0:T(8,128)(2,1)S(1)}, bf16[512,384]{1,0:T(8,128)(2,1)}, u32[]{:S(2)}, u32[]{:S(2)}) collective-permute-start(bf16[512,384]{1,0:T(8,128)(2,1)S(1)} %collective-permute-done.14.refs_4_), channel_id=1, source_target_pairs={{8,0},{9,1},{10,2},{11,3},{12,4},{13,5},{14,6},{15,7},{16,8},{17,9... | collective-permute-start | bytes 1179656 | tf_op jit(solution)/shard_map/ppermute | solution.py:53
  64.8 11.1 %collective-permute-start.18 = (bf16[512,384]{1,0:T(8,128)(2,1)S(1)}, bf16[512,384]{1,0:T(8,128)(2,1)}, u32[]{:S(2)}, u32[]{:S(2)}) collective-permute-start(bf16[512,384]{1,0:T(8,128)(2,1)S(1)} %collective-permute-done.17.refs_6_), channel_id=1, source_target_pairs={{8,16},{9,17},{10,18},{11,19},{12,20},{13,21},{14,22},{15,23},{16,... | collective-permute-start | bytes 1179656 | tf_op jit(solution)/shard_map/ppermute | solution.py:53
  74.7 10.4 %collective-permute-start.16 = (bf16[512,384]{1,0:T(8,128)(2,1)}, bf16[512,384]{1,0:T(8,128)(2,1)}, u32[]{:S(2)}, u32[]{:S(2)}) collective-permute-start(bf16[512,384]{1,0:T(8,128)(2,1)} %collective-permute-done.15.refs_3_), channel_id=1, source_target_pairs={{8,0},{9,1},{10,2},{11,3},{12,4},{13,5},{14,6},{15,7}} | collective-permute-start | bytes 1179656 | tf_op jit(solution)/shard_map/ppermute | solution.py:53
  76.0 9.1 %collective-permute-start.19 = (bf16[512,384]{1,0:T(8,128)(2,1)}, bf16[512,384]{1,0:T(8,128)(2,1)S(1)}, u32[]{:S(2)}, u32[]{:S(2)}) collective-permute-start(bf16[512,384]{1,0:T(8,128)(2,1)} %collective-permute-done.18.refs_7_), channel_id=1, source_target_pairs={{16,24},{17,25},{18,26},{19,27},{20,28},{21,29},{22,30},{23,31}} | collective-permute-start | bytes 1179656 | tf_op jit(solution)/shard_map/ppermute | solution.py:53
  93.6 9.2 %collective-permute-start.20 = (bf16[4,256,256]{2,1,0:T(8,128)(2,1)S(1)}, bf16[4,256,256]{2,1,0:T(8,128)(2,1)S(1)}, u32[]{:S(2)}, u32[]{:S(2)}) collective-permute-start(bf16[4,256,256]{2,1,0:T(8,128)(2,1)S(1)} %get-tuple-element.10.own), channel_id=1, source_target_pairs={{0,8},{1,9},{2,10},{3,11},{4,12},{5,13},{6,14},{7,15},{8,16},{9,17... | collective-permute-start | bytes 1572872 | tf_op jit(solution)/shard_map/ppermute | solution.py:53
  95.1 13.8 %collective-permute-start.21 = (bf16[4,256,256]{2,1,0:T(8,128)(2,1)S(1)}, bf16[4,256,256]{2,1,0:T(8,128)(2,1)S(1)}, u32[]{:S(2)}, u32[]{:S(2)}) collective-permute-start(bf16[4,256,256]{2,1,0:T(8,128)(2,1)S(1)} %get-tuple-element.10.own), channel_id=1, source_target_pairs={{8,0},{9,1},{10,2},{11,3},{12,4},{13,5},{14,6},{15,7},{16,8},{17,9... | collective-permute-start | bytes 1572872 | tf_op jit(solution)/shard_map/ppermute | solution.py:53
  96.4 3.6 %collective-permute-start = (s32[1,5]{1,0:T(1,128)S(1)}, s32[1,5]{1,0:T(1,128)S(1)}, u32[]{:S(2)}, u32[]{:S(2)}) collective-permute-start(s32[1,5]{1,0:T(1,128)S(1)} %bitcast.65), channel_id=1, source_target_pairs={{0,1},{1,0},{2,3},{3,2},{4,5},{5,4},{6,7},{7,6},{8,9},{9,8},{10,11... | collective-permute-start | bytes 68 | tf_op jit(solution)/shard_map/ppermute | solution.py:53
  96.4 3.6 %collective-permute-start.1 = (s32[1,5]{1,0:T(1,128)S(1)}, s32[1,5]{1,0:T(1,128)S(1)}, u32[]{:S(2)}, u32[]{:S(2)}) collective-permute-start(s32[1,5]{1,0:T(1,128)S(1)} %bitcast.66), channel_id=1, source_target_pairs={{0,2},{1,3},{2,0},{3,1},{4,6},{5,7},{6,4},{7,5},{8,10},{9,11},{10,... | collective-permute-start | bytes 68 | tf_op jit(solution)/shard_map/ppermute | solution.py:53
  96.9 4.5 %collective-permute-start.2 = (s32[1,5]{1,0:T(1,128)S(1)}, s32[1,5]{1,0:T(1,128)S(1)}, u32[]{:S(2)}, u32[]{:S(2)}) collective-permute-start(s32[1,5]{1,0:T(1,128)S(1)} %bitcast.67), channel_id=1, source_target_pairs={{0,3},{1,2},{2,1},{3,0},{4,7},{5,6},{6,5},{7,4},{8,11},{9,10},{10,... | collective-permute-start | bytes 68 | tf_op jit(solution)/shard_map/ppermute | solution.py:53
  117.1 4.7 %collective-permute-start.23 = (bf16[128,256]{1,0:T(8,128)(2,1)S(1)}, bf16[128,256]{1,0:T(8,128)(2,1)S(1)}, u32[]{:S(2)}, u32[]{:S(2)}) collective-permute-start(bf16[128,256]{1,0:T(8,128)(2,1)S(1)} %get-tuple-element.22), channel_id=1, source_target_pairs={{0,1},{1,0},{2,3},{3,2},{4,5},{5,4},{6,7},{7,6},{8,9},{9,8},{10,11... | collective-permute-start | bytes 196616 | tf_op jit(solution)/shard_map/ppermute | solution.py:53
  117.2 5.0 %collective-permute-start.24 = (bf16[128,256]{1,0:T(8,128)(2,1)S(1)}, bf16[128,256]{1,0:T(8,128)(2,1)S(1)}, u32[]{:S(2)}, u32[]{:S(2)}) collective-permute-start(bf16[128,256]{1,0:T(8,128)(2,1)S(1)} %get-tuple-element.21), channel_id=1, source_target_pairs={{0,2},{1,3},{2,0},{3,1},{4,6},{5,7},{6,4},{7,5},{8,10},{9,11},{10,... | collective-permute-start | bytes 196616 | tf_op jit(solution)/shard_map/ppermute | solution.py:53
  118.3 5.2 %collective-permute-start.25 = (bf16[128,256]{1,0:T(8,128)(2,1)S(1)}, bf16[128,256]{1,0:T(8,128)(2,1)S(1)}, u32[]{:S(2)}, u32[]{:S(2)}) collective-permute-start(bf16[128,256]{1,0:T(8,128)(2,1)S(1)} %get-tuple-element.20), channel_id=1, source_target_pairs={{0,3},{1,2},{2,1},{3,0},{4,7},{5,6},{6,5},{7,4},{8,11},{9,10},{10,... | collective-permute-start | bytes 196616 | tf_op jit(solution)/shard_map/ppermute | solution.py:53
  (13 other events, 51.0 us)

commit v2 on v1

--- a/solution.py
+++ b/solution.py
@@ -66,85 +66,92 @@
     return hop(value, lambda z, c, d: (z + by, c, d) if 0 <= z + by < zs and first <= z < last else None, zs)
 
 
+def partial_kernel(zs, place, *refs):
+    near = 2 * (zs - 2) + 1
+    x_refs, shards, acc_ref = refs[:8], refs[8 : 8 + near], refs[8 + near]
+    z = place[0] >> 1
+    rows, block = shards[0].shape[0], x_refs[0].shape[0]
+
+    def add(source, shard, fresh):
+        at = pl.ds(pl.multiple_of(source * rows, rows), rows)
+        for rel in range(2):
+            x = jnp.concatenate([ref[:, at] for ref in x_refs[4 * rel : 4 * rel + 4]], axis=0)
+            value = jnp.dot(x, shard[...], preferred_element_type=jnp.float32)
+            here = slice(4 * rel * block, 4 * (rel + 1) * block)
+            acc_ref[here] = value if fresh else acc_ref[here] + value
+
+    add(z, shards[zs - 2], True)
+    for r in range(-(zs - 2), zs - 1):
+        if r:
+            pl.when((z - r >= 0) & (z - r < zs))(functools.partial(add, z - r, shards[r + zs - 2], False))
+
+
 def project_kernel(zs, place, *refs):
-    x_refs, shards = refs[:2], refs[2 : 2 + 2 * zs - 1]
-    q_ref, kv_ref, w_full = refs[2 + 2 * zs - 1 :]
-    z, core = place[0], place[1]
-    rows = shards[0].shape[0]
-    for r in range(-(zs - 1), zs):
-        source = z - r
-
-        @pl.when((source >= 0) & (source < zs))
-        def _():
-            at = pl.ds(pl.multiple_of(source * rows, rows), rows)
-            for part in range(3):
-                third = pl.multiple_of(place[2 + part] * HD, HD)
-                w_full[at, pl.ds(third, HD)] = shards[r + zs - 1][:, part * HD : (part + 1) * HD]
-
-    block = x_refs[0].shape[1]
+    x_refs, (from_last, from_first, acc_in, q_ref, kv_ref, acc_ref) = refs[:8], refs[8:]
+    z, core, depth = place[0] >> 1, place[0] & 1, place[1]
+    turn = jnp.where(depth == 3, 0, depth)
+    rows, block = from_last.shape[0], x_refs[0].shape[0]
     for rel in range(2):
         u = core ^ rel
-
-        def body(step, carry):
-            pair = x_refs[rel][pl.ds(2 * step, 2)].reshape(2 * block, x_refs[rel].shape[2])
-            out = jnp.dot(pair, w_full[...], preferred_element_type=jnp.float32)
-            out = out.astype(jnp.bfloat16).reshape(2, block, 3 * HD)
-            at = pl.ds(pl.multiple_of(u * block, block), block)
-            q_ref[pl.ds(2 * step, 2), at, :] = out[:, :, :HD]
-            kv_ref[pl.ds(2 * step, 2), at, :] = out[:, :, HD:]
-            return carry
-
-        lax.fori_loop(0, 2, body, 0)
+        here = slice(4 * rel * block, 4 * (rel + 1) * block)
+        acc_ref[here] = acc_in[here]
+        for edge, source, shard in ((0, zs - 1, from_last), (zs - 1, 0, from_first)):
+
+            @pl.when(z == edge)
+            def _(source=source, shard=shard):
+                x = jnp.concatenate(
+                    [ref[:, source * rows : (source + 1) * rows] for ref in x_refs[4 * rel : 4 * rel + 4]], axis=0
+                )
+                acc_ref[here] += jnp.dot(x, shard[...], preferred_element_type=jnp.float32)
+
+        at = pl.ds(pl.multiple_of(u * block, block), block)
+        for r in range(4):
+            mine = slice((4 * rel + r) * block, (4 * rel + r + 1) * block)
+            for third, (ref, column) in enumerate(((q_ref, 0), (kv_ref, 0), (kv_ref, HD))):
+                at_group = third + turn
+                at_group = jnp.where(at_group >= 3, at_group - 3, at_group)
+                lanes = pl.ds(pl.multiple_of(at_group * HD, HD), HD)
+                ref[r, at, column : column + HD] = acc_ref[mine, lanes].astype(jnp.bfloat16)
 
 
 def attend_kernel(place, mask, q_ref, before, own, after, keep_ref, send_ref):
-    core = place[1]
+    core = place[0] & 1
     block = q_ref.shape[1] // 2
     inv_root = 1.0 / math.sqrt(HD)
-
-    def body(r, carry):
-        q = q_ref[r]
-        scores = []
-        for side, kv in enumerate((before, own, after)):
-            s = lax.dot_general(q, kv[r][:, :HD], (((1,), (1,)), ((), ())), preferred_element_type=jnp.float32)
-            s = (s * inv_root).reshape(2, block, 2, block)
-            rows = []
-            for u in range(2):
-                cols = []
-                for v in range(2):
-                    entry = 2 * side + v - u
-                    piece = s[u, :, v]
-                    if 0 <= entry <= 4:
-                        flag = mask[((u ^ core) * 4 + r) * 5 + entry]
-                        piece = jnp.where(flag > 0, piece, -1e30)
-                    else:
-                        piece = jnp.full_like(piece, -1e30)
-                    cols.append(piece)
-                rows.append(jnp.concatenate(cols, axis=1))
-            scores.append(jnp.concatenate(rows, axis=0))
-        top = functools.reduce(jnp.maximum, [jnp.max(s, axis=1, keepdims=True) for s in scores])
-        powers = [jnp.exp(s - top) for s in scores]
-        total = functools.reduce(jnp.add, [jnp.sum(p, axis=1, keepdims=True) for p in powers])
-        inverse = 1.0 / total
-        result = jnp.zeros((2 * block, HD), jnp.float32)
-        for p, kv in zip(powers, (before, own, after)):
-            w = (p * inverse).astype(jnp.bfloat16)
-            result += jnp.dot(w, kv[r][:, HD:], preferred_element_type=jnp.float32)
-        result = result.astype(jnp.bfloat16)
+    for r in range(4):
         for u in range(2):
+            q = q_ref[r, u * block : (u + 1) * block]
+            spans = ((before, u, 2), (own, 0, 2), (after, 0, 1 + u))
+            scores, entry = [], 0
+            for ref, first, last in spans:
+                k = ref[r, first * block : last * block, :HD]
+                s = lax.dot_general(q, k, (((1,), (1,)), ((), ())), preferred_element_type=jnp.float32)
+                for v in range(last - first):
+                    flag = mask[((u ^ core) * 4 + r) * 5 + entry]
+                    scores.append(jnp.where(flag > 0, s[:, v * block : (v + 1) * block] * inv_root, -1e30))
+                    entry += 1
+            top = jnp.max(functools.reduce(jnp.maximum, scores), axis=1, keepdims=True)
+            powers = [jnp.exp(s - top) for s in scores]
+            inverse = 1.0 / jnp.sum(functools.reduce(jnp.add, powers), axis=1, keepdims=True)
+            weights = [(p * inverse).astype(jnp.bfloat16) for p in powers]
+            result, entry = jnp.zeros((block, HD), jnp.float32), 0
+            for ref, first, last in spans:
+                w = jnp.concatenate(weights[entry : entry + last - first], axis=1)
+                entry += last - first
+                result += jnp.dot(w, ref[r, first * block : last * block, HD:], preferred_element_type=jnp.float32)
+            result = result.astype(jnp.bfloat16)
 
             @pl.when(core == u)
             def _():
-                keep_ref[r] = result[u * block : (u + 1) * block]
-                send_ref[r] = result[(1 - u) * block : (2 - u) * block]
-
-        return carry
-
-    lax.fori_loop(0, 4, body, 0)
+                keep_ref[r] = result
+
+            @pl.when(core != u)
+            def _():
+                send_ref[r] = result
 
 
 def gather_kernel(place, own, x, y, diagonal, out_ref):
-    core, depth = place[1], place[5]
+    core, depth = place[0] & 1, place[1]
     for r, ref in enumerate((own, x, y, diagonal)):
         for rel in range(2):
             at = pl.multiple_of((2 * (depth ^ r) + (core ^ rel)) * HD, HD)
@@ -162,55 +169,63 @@
     )
 
 
+def after(value, *others):
+    return lax.optimization_barrier((value, *others))[0]
+
+
 def plane_device(raw, stream, conv_w, gain, w_qkv, mask):
     zs = lax.axis_size("tm") // 2
     tm, depth = lax.axis_index("tm"), lax.axis_index("depth")
-    z, core = tm // 2, tm % 2
+    core = tm & 1
     time_len, site_len, _ = raw.shape
     block = time_len * site_len
-    width = stream.shape[2]
-
-    rows = w_qkv.shape[0]
-    grouped = w_qkv.reshape(rows, 3, 2, HD)
-    keep = lax.dynamic_index_in_dim(grouped, core, 2, keepdims=False)
-    send = lax.dynamic_index_in_dim(grouped, 1 - core, 2, keepdims=False)
+    bf16, f32 = jnp.bfloat16, jnp.float32
+
+    pair = 2 * HD
+    low, mid, high = (w_qkv[:, k * pair : (k + 1) * pair] for k in range(3))
+    mid = lax.optimization_barrier(mid)
+    even = (depth & 1) == 0
+    from_y = swap_depth(jnp.where(even, high, low), 2, zs)
+    from_x = swap_depth(mid, 1, zs)
+    groups = [jnp.where(even, low, from_y), from_x, jnp.where(even, from_y, high)]
+    first = core == 0
+    keep = jnp.concatenate([jnp.where(first, g[:, :HD], g[:, HD:]) for g in groups], axis=1)
+    send = jnp.concatenate([jnp.where(first, g[:, HD:], g[:, :HD]) for g in groups], axis=1)
     received = swap_core(send, zs)
-    first = core == 0
-    both = jnp.concatenate([jnp.where(first, keep, received), jnp.where(first, received, keep)], axis=0)
-    parts = [hop(both[:, k], lambda z, c, d, k=k: (z, c, (k - d) % 4), zs) for k in range(3)]
-    shard = jnp.concatenate(parts, axis=1)
-    thirds = [(3 * ((k - depth) % 4) + k) // 4 for k in range(3)]
-
-    normed = normed_tokens(raw, stream, conv_w, gain)
+    shard = jnp.concatenate([jnp.where(first, keep, received), jnp.where(first, received, keep)], axis=0)
 
     ahead, back = [shard], [shard]
     for r in range(1, zs):
         ahead.append(move_z(ahead[-1], 1, zs, first=r - 1))
         back.append(move_z(back[-1], -1, zs, last=zs - r + 1))
-    shards = back[:0:-1] + ahead
-
-    own_tokens = jnp.stack([normed] + [swap_depth(normed, bits, zs) for bits in (1, 2, 3)])
-    other_tokens = swap_core(own_tokens, zs)
-
-    flags = mask.reshape(1, mask.shape[2])
+
+    normed = normed_tokens(raw, stream, conv_w, gain)
+    tokens = [normed] + [swap_depth(normed, bits, zs) for bits in (1, 2, 3)]
+    tokens += [swap_core(t, zs) for t in tokens]
+
+    flags = after(mask.reshape(1, mask.shape[2]), tokens[1])
     flags = jnp.concatenate([flags] + [swap_depth(flags, bits, zs) for bits in (1, 2, 3)])
     flags = jnp.concatenate([flags, swap_core(flags, zs)]).reshape(-1)
 
-    place = jnp.stack([z, core] + thirds + [depth]).astype(jnp.int32)
-    bf16 = jnp.bfloat16
+    place = jnp.stack([tm, depth]).astype(jnp.int32)
+    near = back[-2:0:-1] + ahead[:-1]
+    total = vmem_call(
+        functools.partial(partial_kernel, zs), jax.ShapeDtypeStruct((8 * block, 3 * HD), f32), total=9 + len(near)
+    )(place, *tokens, *near)
+    total = after(total, flags)
     q, kv = vmem_call(
         functools.partial(project_kernel, zs),
         (jax.ShapeDtypeStruct((4, 2 * block, HD), bf16), jax.ShapeDtypeStruct((4, 2 * block, 2 * HD), bf16)),
-        scratch=[VMEM((width, 3 * HD), bf16)],
-        total=3 + 2 * zs - 1,
-    )(place, own_tokens, other_tokens, *shards)
-
-    before = move_z(kv, 1, zs)
-    after = move_z(kv, -1, zs)
+        scratch=[VMEM((8 * block, 3 * HD), f32)],
+        total=12,
+    )(place, *tokens, back[-1], ahead[-1], total)
+
     piece = jax.ShapeDtypeStruct((4, block, HD), bf16)
-    kept, sent = vmem_call(attend_kernel, (piece, piece), smem=2, total=6)(place, flags, q, before, kv, after)
-    pair = jnp.concatenate([kept, swap_core(sent, zs)], axis=2)
-    pieces = [pair[0]] + [swap_depth(pair[bits], bits, zs) for bits in (1, 2, 3)]
+    kept, sent = vmem_call(attend_kernel, (piece, piece), smem=2, total=6)(
+        place, flags, q, move_z(kv, 1, zs), kv, move_z(kv, -1, zs)
+    )
+    pairs = jnp.concatenate([kept, swap_core(sent, zs)], axis=2)
+    pieces = [pairs[0]] + [swap_depth(pairs[bits], bits, zs) for bits in (1, 2, 3)]
     context = vmem_call(gather_kernel, jax.ShapeDtypeStruct((block, HEADS * HD), bf16), total=5)(place, *pieces)
     return context.reshape(time_len, site_len, HEADS * HD)
 

time: 125 us -> 120 us (0.960)
  the two profiles are of different devices: /device:TPU:0 before, /device:TPU:9 now
where the time goes in v2:
time: 120 us; the launch traced here: 118 us
  starting transfers between devices  51.4 us (43%)
  waiting for transfers between devices  43.9 us (37%)
  Pallas kernels  12.4 us (10%)
  local copies, waits for them, and re-layouts  5.46 us (5%)
  matrix products  3.04 us (3%)
  other arithmetic  1.57 us (1%)
    ppermute x26, starting transfers between devices, hop(): return lax.ppermute(value, ('tm', 'depth'), pairs)  47 us
    ppermute x26, waiting for transfers between devices, hop(): return lax.ppermute(value, ('tm', 'depth'), pairs)  43.5 us
    pallas_call x1, Pallas kernels, plane_device(): vmem_call(attend_kernel, (piece, piece), smem=2, total=6)  5.12 us
    pallas_call x1, Pallas kernels, plane_device(): vmem_call(functools.partial(partial_kernel, zs), jax.ShapeDtypeStruct((8...  4.31 us
    unnamed x25, local copies, waits for them, and re-layouts  3.78 us
    ppermute x1, starting transfers between devices, padded_2(): before = lax.ppermute(last, axis, up)  3.12 us
    dot_general x3, matrix products, normed_tokens(): jnp.dot(window, conv_w[offset], preferred_element_type=jnp.float32)  3.04 us
  transfers between devices with their start and end apart: 28, of which 14 were waited for; matrix products, arithmetic and copies ran while one was open for 4% of the time, Pallas kernels for 4%

profile of v2, /device:TPU:9, one launch (start us, length us, event | category | flops | bytes accessed | tf_op | source)
XLA Modules:
  0.0 118.0 jit_solution(2579035513875548526)
XLA Ops:
  3.3 3.1 %collective-permute-start = (bf16[16,1,128]{2,1,0:T(2,128)(2,1)S(1)}, bf16[16,1,128]{2,1,0:T(2,128)(2,1)S(1)}, u32[]{:S(2)}, u32[]{:S(2)}) collective-permute-start(bf16[16,1,128]{2,1,0:T(2,128)(2,1)S(1)} %get-tuple-element.33), channel_id=1, source_target_pairs={{0,1},{1,2},{2,3},{4,5},{5,6},{6,7},{8,9},{9,10},{10,11},{12,13},{... | collective-permute-start | bytes 12296 | tf_op jit(solution)/shard_map/ppermute | solution.py:27
  11.5 2.1 %collective-permute-start.14 = (bf16[256,256]{1,0:T(8,128)(2,1)S(1)}, bf16[256,256]{1,0:T(8,128)(2,1)S(1)}, u32[]{:S(2)}, u32[]{:S(2)}) collective-permute-start(bf16[256,256]{1,0:T(8,128)(2,1)S(1)} %get-tuple-element.21), channel_id=1, source_target_pairs={{0,1},{1,0},{2,3},{3,2},{4,5},{5,4},{6,7},{7,6},{8,9},{9,8},{10,11... | collective-permute-start | bytes 393224 | tf_op jit(solution)/shard_map/ppermute | solution.py:53
  13.6 2.3 %collective-permute-done.14 = bf16[256,256]{1,0:T(8,128)(2,1)S(1)} collective-permute-done((bf16[256,256]{1,0:T(8,128)(2,1)S(1)}, bf16[256,256]{1,0:T(8,128)(2,1)S(1)}, u32[]{:S(2)}, u32[]{:S(2)}) %collective-permute-start.14) | collective-permute-done | bytes 131104 | tf_op jit(solution)/shard_map/ppermute | solution.py:53
  16.0 2.8 %collective-permute-start.15 = (bf16[256,384]{1,0:T(8,128)(2,1)S(1)}, bf16[256,384]{1,0:T(8,128)(2,1)S(1)}, u32[]{:S(2)}, u32[]{:S(2)}) collective-permute-start(bf16[256,384]{1,0:T(8,128)(2,1)S(1)} %pad_maximum_fusion.2), channel_id=1, source_target_pairs={{0,4},{1,5},{2,6},{3,7},{4,0},{5,1},{6,2},{7,3},{8,12},{9,13},{10,... | collective-permute-start | bytes 589832 | tf_op jit(solution)/shard_map/ppermute | solution.py:53
  18.9 1.5 %collective-permute-start.2 = (bf16[128,2048]{1,0:T(8,128)(2,1)S(1)}, bf16[128,2048]{1,0:T(8,128)(2,1)S(1)}, u32[]{:S(2)}, u32[]{:S(2)}) collective-permute-start(bf16[128,2048]{1,0:T(8,128)(2,1)S(1)} %multiply_convert_fusion.refs_0_), channel_id=1, source_target_pairs={{0,1},{1,0},{2,3},{3,2},{4,5},{5,4},{6,7},{7,6},{8,9},{9,8},{10,11... | collective-permute-start | bytes 1572872 | tf_op jit(solution)/shard_map/ppermute | solution.py:53
  20.6 2.1 %collective-permute-start.16 = (bf16[512,384]{1,0:T(8,128)(2,1)S(1)}, bf16[512,384]{1,0:T(8,128)(2,1)S(1)}, u32[]{:S(2)}, u32[]{:S(2)}) collective-permute-start(bf16[512,384]{1,0:T(8,128)(2,1)S(1)} %pad_maximum_fusion.refs_10_), channel_id=1, source_target_pairs={{8,0},{9,1},{10,2},{11,3},{12,4},{13,5},{14,6},{15,7},{16,8},{17,9... | collective-permute-start | bytes 1179656 | tf_op jit(solution)/shard_map/ppermute | solution.py:53
  22.7 3.2 %collective-permute-start.19 = (bf16[512,384]{1,0:T(8,128)(2,1)S(1)}, bf16[512,384]{1,0:T(8,128)(2,1)S(1)}, u32[]{:S(2)}, u32[]{:S(2)}) collective-permute-start(bf16[512,384]{1,0:T(8,128)(2,1)S(1)} %pad_maximum_fusion.refs_10_), channel_id=1, source_target_pairs={{0,8},{1,9},{2,10},{3,11},{4,12},{5,13},{6,14},{7,15},{8,16},{9,17... | collective-permute-start | bytes 1179656 | tf_op jit(solution)/shard_map/ppermute | solution.py:53
  28.0 4.6 %collective-permute-done.2.refs_1_ = bf16[128,2048]{1,0:T(8,128)(2,1)S(1)} collective-permute-done((bf16[128,2048]{1,0:T(8,128)(2,1)S(1)}, bf16[128,2048]{1,0:T(8,128)(2,1)S(1)}, u32[]{:S(2)}, u32[]{:S(2)}) %collective-permute-start.2) | collective-permute-done | bytes 524320 | tf_op jit(solution)/shard_map/ppermute | solution.py:53
  34.0 9.8 %collective-permute-done.3 = s32[1,5]{1,0:T(1,128)S(1)} collective-permute-done((s32[1,5]{1,0:T(1,128)S(1)}, s32[1,5]{1,0:T(1,128)S(1)}, u32[]{:S(2)}, u32[]{:S(2)}) %collective-permute-start.3) | collective-permute-done | bytes 52 | tf_op jit(solution)/shard_map/ppermute | solution.py:53
  45.1 4.6 %collective-permute-done.4 = s32[1,5]{1,0:T(1,128)S(1)} collective-permute-done((s32[1,5]{1,0:T(1,128)S(1)}, s32[1,5]{1,0:T(1,128)S(1)}, u32[]{:S(2)}, u32[]{:S(2)}) %collective-permute-start.4) | collective-permute-done | bytes 52 | tf_op jit(solution)/shard_map/ppermute | solution.py:53
  50.8 2.2 %collective-permute-done.5 = s32[1,5]{1,0:T(1,128)S(1)} collective-permute-done((s32[1,5]{1,0:T(1,128)S(1)}, s32[1,5]{1,0:T(1,128)S(1)}, u32[]{:S(2)}, u32[]{:S(2)}) %collective-permute-start.5) | collective-permute-done | bytes 52 | tf_op jit(solution)/shard_map/ppermute | solution.py:53
  53.0 3.0 %collective-permute-start.9 = (bf16[128,2048]{1,0:T(8,128)(2,1)S(1)}, bf16[128,2048]{1,0:T(8,128)(2,1)S(1)}, u32[]{:S(2)}, u32[]{:S(2)}) collective-permute-start(bf16[128,2048]{1,0:T(8,128)(2,1)S(1)} %multiply_convert_fusion.refs_0_), channel_id=1, source_target_pairs={{0,4},{1,5},{2,6},{3,7},{4,0},{5,1},{6,2},{7,3},{8,12},{9,13},{10,... | collective-permute-start | bytes 1572872 | tf_op jit(solution)/shard_map/ppermute | solution.py:53
  56.0 2.1 %collective-permute-start.17 = (bf16[512,384]{1,0:T(8,128)(2,1)S(1)}, bf16[512,384]{1,0:T(8,128)(2,1)}, u32[]{:S(2)}, u32[]{:S(2)}) collective-permute-start(bf16[512,384]{1,0:T(8,128)(2,1)S(1)} %collective-permute-done.16.refs_9_), channel_id=1, source_target_pairs={{8,0},{9,1},{10,2},{11,3},{12,4},{13,5},{14,6},{15,7},{16,8},{17,9... | collective-permute-start | bytes 1179656 | tf_op jit(solution)/shard_map/ppermute | solution.py:53
  58.9 4.7 %collective-permute-start.20 = (bf16[512,384]{1,0:T(8,128)(2,1)S(1)}, bf16[512,384]{1,0:T(8,128)(2,1)}, u32[]{:S(2)}, u32[]{:S(2)}) collective-permute-start(bf16[512,384]{1,0:T(8,128)(2,1)S(1)} %collective-permute-done.19.refs_11_), channel_id=1, source_target_pairs={{8,16},{9,17},{10,18},{11,19},{12,20},{13,21},{14,22},{15,23},{16,... | collective-permute-start | bytes 1179656 | tf_op jit(solution)/shard_map/ppermute | solution.py:53
  66.9 1.9 %collective-permute-done.17.refs_8_ = bf16[512,384]{1,0:T(8,128)(2,1)} collective-permute-done((bf16[512,384]{1,0:T(8,128)(2,1)S(1)}, bf16[512,384]{1,0:T(8,128)(2,1)}, u32[]{:S(2)}, u32[]{:S(2)}) %collective-permute-start.17) | collective-permute-done | bytes 393248 | tf_op jit(solution)/shard_map/ppermute | solution.py:53
  68.8 2.8 %collective-permute-start.18 = (bf16[512,384]{1,0:T(8,128)(2,1)}, bf16[512,384]{1,0:T(8,128)(2,1)}, u32[]{:S(2)}, u32[]{:S(2)}) collective-permute-start(bf16[512,384]{1,0:T(8,128)(2,1)} %collective-permute-done.17.refs_8_), channel_id=1, source_target_pairs={{8,0},{9,1},{10,2},{11,3},{12,4},{13,5},{14,6},{15,7}} | collective-permute-start | bytes 1179656 | tf_op jit(solution)/shard_map/ppermute | solution.py:53
  75.9 4.3 %shard_map.64.refs_10_ = f32[1024,384]{1,0:T(8,128)S(1)} custom-call(s32[2]{0:T(128)S(1)} %pad_add_fusion.1.place, bf16[128,2048]{1,0:T(8,128)(2,1)S(1)} %multiply_convert_fusion.refs_0_, bf16[128,2048]{1,0:T(8,128)(2,1)S(1)} %collective-permute-done.2.refs_1_, bf16[128,2048]{1,0:T(8,128)(2,1)S(1)} %collective-permute-done.7.refs_2_, ...), custom_call_target="tpu_custom_call" | custom-call | tf_op jit(solution)/shard_map/pallas_call | solution.py:212
  80.2 1.7 %shard_map.65 = (bf16[4,256,128]{2,1,0:T(8,128)(2,1)S(1)}, bf16[4,256,256]{2,1,0:T(8,128)(2,1)S(1)}) custom-call(s32[2]{0:T(128)S(1)} %pad_add_fusion.1.place, bf16[128,2048]{1,0:T(8,128)(2,1)S(1)} %multiply_convert_fusion.refs_0_, bf16[128,2048]{1,0:T(8,128)(2,1)S(1)} %collective-permute-done.2.refs_1_, ...), custom_call_target="tpu_custom_call" | custom-call | tf_op jit(solution)/shard_map/pallas_call | solution.py:216
  81.9 5.2 %collective-permute-start.22 = (bf16[4,256,256]{2,1,0:T(8,128)(2,1)S(1)}, bf16[4,256,256]{2,1,0:T(8,128)(2,1)S(1)}, u32[]{:S(2)}, u32[]{:S(2)}) collective-permute-start(bf16[4,256,256]{2,1,0:T(8,128)(2,1)S(1)} %get-tuple-element.14.own), channel_id=1, source_target_pairs={{0,8},{1,9},{2,10},{3,11},{4,12},{5,13},{6,14},{7,15},{8,16},{9,17... | collective-permute-start | bytes 1572872 | tf_op jit(solution)/shard_map/ppermute | solution.py:53
  87.1 1.9 %collective-permute-start.23 = (bf16[4,256,256]{2,1,0:T(8,128)(2,1)S(1)}, bf16[4,256,256]{2,1,0:T(8,128)(2,1)S(1)}, u32[]{:S(2)}, u32[]{:S(2)}) collective-permute-start(bf16[4,256,256]{2,1,0:T(8,128)(2,1)S(1)} %get-tuple-element.14.own), channel_id=1, source_target_pairs={{8,0},{9,1},{10,2},{11,3},{12,4},{13,5},{14,6},{15,7},{16,8},{17,9... | collective-permute-start | bytes 1572872 | tf_op jit(solution)/shard_map/ppermute | solution.py:53
  89.0 7.6 %collective-permute-done.22.before = bf16[4,256,256]{2,1,0:T(8,128)(2,1)S(1)} collective-permute-done((bf16[4,256,256]{2,1,0:T(8,128)(2,1)S(1)}, bf16[4,256,256]{2,1,0:T(8,128)(2,1)S(1)}, u32[]{:S(2)}, u32[]{:S(2)}) %collective-permute-start.22) | collective-permute-done | bytes 524320 | tf_op jit(solution)/shard_map/ppermute | solution.py:53
  96.7 5.6 %collective-permute-done.23.after = bf16[4,256,256]{2,1,0:T(8,128)(2,1)S(1)} collective-permute-done((bf16[4,256,256]{2,1,0:T(8,128)(2,1)S(1)}, bf16[4,256,256]{2,1,0:T(8,128)(2,1)S(1)}, u32[]{:S(2)}, u32[]{:S(2)}) %collective-permute-start.23) | collective-permute-done | bytes 524320 | tf_op jit(solution)/shard_map/ppermute | solution.py:53
  102.3 5.1 %shard_map.66 = (bf16[4,128,128]{2,1,0:T(8,128)(2,1)S(1)}, bf16[4,128,128]{2,1,0:T(8,128)(2,1)S(1)}) custom-call(s32[2]{0:T(128)S(1)} %pad_add_fusion.1.place, s32[40]{0:T(128)S(1)} %reshape.34.mask, bf16[4,256,128]{2,1,0:T(8,128)(2,1)S(1)} %get-tuple-element.13.q_ref, bf16[4,256,256]{2,1,0:T(8,128)(2,1)S(1)} %collective-permute-done.22.before, ...), custom_call_target="tpu_custom_call" | custom-call | tf_op jit(solution)/shard_map/pallas_call | solution.py:224
  107.4 2.7 %collective-permute-start.24 = (bf16[4,128,128]{2,1,0:T(8,128)(2,1)S(1)}, bf16[4,128,128]{2,1,0:T(8,128)(2,1)S(1)}, u32[]{:S(2)}, u32[]{:S(2)}) collective-permute-start(bf16[4,128,128]{2,1,0:T(8,128)(2,1)S(1)} %get-tuple-element.16), channel_id=1, source_target_pairs={{0,4},{1,5},{2,6},{3,7},{4,0},{5,1},{6,2},{7,3},{8,12},{9,13},{10,... | collective-permute-start | bytes 393224 | tf_op jit(solution)/shard_map/ppermute | solution.py:53
  (80 shorter events, 30.8 us)
Async XLA Ops:
  1.1 10.1 %collective-permute-start.13 = (bf16[256,256]{1,0:T(8,128)(2,1)S(1)}, bf16[256,256]{1,0:T(8,128)(2,1)S(1)}, u32[]{:S(2)}, u32[]{:S(2)}) collective-permute-start(bf16[256,256]{1,0:T(8,128)(2,1)S(1)} %broadcast_select_fusion.4), channel_id=1, source_target_pairs={{0,2},{1,3},{2,0},{3,1},{4,6},{5,7},{6,4},{7,5},{8,10},{9,11},{10,... | collective-permute-start | bytes 393224 | tf_op jit(solution)/shard_map/ppermute | solution.py:53
  3.3 5.8 %collective-permute-start = (bf16[16,1,128]{2,1,0:T(2,128)(2,1)S(1)}, bf16[16,1,128]{2,1,0:T(2,128)(2,1)S(1)}, u32[]{:S(2)}, u32[]{:S(2)}) collective-permute-start(bf16[16,1,128]{2,1,0:T(2,128)(2,1)S(1)} %get-tuple-element.33), channel_id=1, source_target_pairs={{0,1},{1,2},{2,3},{4,5},{5,6},{6,7},{8,9},{9,10},{10,11},{12,13},{... | collective-permute-start | bytes 12296 | tf_op jit(solution)/shard_map/ppermute | solution.py:27
  6.4 4.4 %collective-permute-start.1 = (bf16[16,1,128]{2,1,0:T(2,128)(2,1)S(1)}, bf16[16,1,128]{2,1,0:T(2,128)(2,1)S(1)}, u32[]{:S(2)}, u32[]{:S(2)}) collective-permute-start(bf16[16,1,128]{2,1,0:T(2,128)(2,1)S(1)} %get-tuple-element.32), channel_id=1, source_target_pairs={{1,0},{2,1},{3,2},{5,4},{6,5},{7,6},{9,8},{10,9},{11,10},{13,12},{... | collective-permute-start | bytes 12296 | tf_op jit(solution)/shard_map/ppermute | solution.py:28
  11.5 4.5 %collective-permute-start.14 = (bf16[256,256]{1,0:T(8,128)(2,1)S(1)}, bf16[256,256]{1,0:T(8,128)(2,1)S(1)}, u32[]{:S(2)}, u32[]{:S(2)}) collective-permute-start(bf16[256,256]{1,0:T(8,128)(2,1)S(1)} %get-tuple-element.21), channel_id=1, source_target_pairs={{0,1},{1,0},{2,3},{3,2},{4,5},{5,4},{6,7},{7,6},{8,9},{9,8},{10,11... | collective-permute-start | bytes 393224 | tf_op jit(solution)/shard_map/ppermute | solution.py:53
  16.0 4.4 %collective-permute-start.15 = (bf16[256,384]{1,0:T(8,128)(2,1)S(1)}, bf16[256,384]{1,0:T(8,128)(2,1)S(1)}, u32[]{:S(2)}, u32[]{:S(2)}) collective-permute-start(bf16[256,384]{1,0:T(8,128)(2,1)S(1)} %pad_maximum_fusion.2), channel_id=1, source_target_pairs={{0,4},{1,5},{2,6},{3,7},{4,0},{5,1},{6,2},{7,3},{8,12},{9,13},{10,... | collective-permute-start | bytes 589832 | tf_op jit(solution)/shard_map/ppermute | solution.py:53
  18.9 13.6 %collective-permute-start.2 = (bf16[128,2048]{1,0:T(8,128)(2,1)S(1)}, bf16[128,2048]{1,0:T(8,128)(2,1)S(1)}, u32[]{:S(2)}, u32[]{:S(2)}) collective-permute-start(bf16[128,2048]{1,0:T(8,128)(2,1)S(1)} %multiply_convert_fusion.refs_0_), channel_id=1, source_target_pairs={{0,1},{1,0},{2,3},{3,2},{4,5},{5,4},{6,7},{7,6},{8,9},{9,8},{10,11... | collective-permute-start | bytes 1572872 | tf_op jit(solution)/shard_map/ppermute | solution.py:53
  20.6 35.5 %collective-permute-start.16 = (bf16[512,384]{1,0:T(8,128)(2,1)S(1)}, bf16[512,384]{1,0:T(8,128)(2,1)S(1)}, u32[]{:S(2)}, u32[]{:S(2)}) collective-permute-start(bf16[512,384]{1,0:T(8,128)(2,1)S(1)} %pad_maximum_fusion.refs_10_), channel_id=1, source_target_pairs={{8,0},{9,1},{10,2},{11,3},{12,4},{13,5},{14,6},{15,7},{16,8},{17,9... | collective-permute-start | bytes 1179656 | tf_op jit(solution)/shard_map/ppermute | solution.py:53
  22.7 36.2 %collective-permute-start.19 = (bf16[512,384]{1,0:T(8,128)(2,1)S(1)}, bf16[512,384]{1,0:T(8,128)(2,1)S(1)}, u32[]{:S(2)}, u32[]{:S(2)}) collective-permute-start(bf16[512,384]{1,0:T(8,128)(2,1)S(1)} %pad_maximum_fusion.refs_10_), channel_id=1, source_target_pairs={{0,8},{1,9},{2,10},{3,11},{4,12},{5,13},{6,14},{7,15},{8,16},{9,17... | collective-permute-start | bytes 1179656 | tf_op jit(solution)/shard_map/ppermute | solution.py:53
  25.9 38.5 %collective-permute-start.7 = (bf16[128,2048]{1,0:T(8,128)(2,1)S(1)}, bf16[128,2048]{1,0:T(8,128)(2,1)S(1)}, u32[]{:S(2)}, u32[]{:S(2)}) collective-permute-start(bf16[128,2048]{1,0:T(8,128)(2,1)S(1)} %multiply_convert_fusion.refs_0_), channel_id=1, source_target_pairs={{0,2},{1,3},{2,0},{3,1},{4,6},{5,7},{6,4},{7,5},{8,10},{9,11},{10,... | collective-permute-start | bytes 1572872 | tf_op jit(solution)/shard_map/ppermute | solution.py:53
  26.7 38.3 %collective-permute-start.8 = (bf16[128,2048]{1,0:T(8,128)(2,1)S(1)}, bf16[128,2048]{1,0:T(8,128)(2,1)S(1)}, u32[]{:S(2)}, u32[]{:S(2)}) collective-permute-start(bf16[128,2048]{1,0:T(8,128)(2,1)S(1)} %multiply_convert_fusion.refs_0_), channel_id=1, source_target_pairs={{0,3},{1,2},{2,1},{3,0},{4,7},{5,6},{6,5},{7,4},{8,11},{9,10},{10,... | collective-permute-start | bytes 1572872 | tf_op jit(solution)/shard_map/ppermute | solution.py:53
  32.5 11.3 %collective-permute-start.3 = (s32[1,5]{1,0:T(1,128)S(1)}, s32[1,5]{1,0:T(1,128)S(1)}, u32[]{:S(2)}, u32[]{:S(2)}) collective-permute-start(s32[1,5]{1,0:T(1,128)S(1)} %bitcast.37), channel_id=1, source_target_pairs={{0,1},{1,0},{2,3},{3,2},{4,5},{5,4},{6,7},{7,6},{8,9},{9,8},{10,11... | collective-permute-start | bytes 68 | tf_op jit(solution)/shard_map/ppermute | solution.py:53
  43.8 5.9 %collective-permute-start.4 = (s32[1,5]{1,0:T(1,128)S(1)}, s32[1,5]{1,0:T(1,128)S(1)}, u32[]{:S(2)}, u32[]{:S(2)}) collective-permute-start(s32[1,5]{1,0:T(1,128)S(1)} %bitcast.38), channel_id=1, source_target_pairs={{0,2},{1,3},{2,0},{3,1},{4,6},{5,7},{6,4},{7,5},{8,10},{9,11},{10,... | collective-permute-start | bytes 68 | tf_op jit(solution)/shard_map/ppermute | solution.py:53
  53.0 12.0 %collective-permute-start.9 = (bf16[128,2048]{1,0:T(8,128)(2,1)S(1)}, bf16[128,2048]{1,0:T(8,128)(2,1)S(1)}, u32[]{:S(2)}, u32[]{:S(2)}) collective-permute-start(bf16[128,2048]{1,0:T(8,128)(2,1)S(1)} %multiply_convert_fusion.refs_0_), channel_id=1, source_target_pairs={{0,4},{1,5},{2,6},{3,7},{4,0},{5,1},{6,2},{7,3},{8,12},{9,13},{10,... | collective-permute-start | bytes 1572872 | tf_op jit(solution)/shard_map/ppermute | solution.py:53
  56.0 12.7 %collective-permute-start.17 = (bf16[512,384]{1,0:T(8,128)(2,1)S(1)}, bf16[512,384]{1,0:T(8,128)(2,1)}, u32[]{:S(2)}, u32[]{:S(2)}) collective-permute-start(bf16[512,384]{1,0:T(8,128)(2,1)S(1)} %collective-permute-done.16.refs_9_), channel_id=1, source_target_pairs={{8,0},{9,1},{10,2},{11,3},{12,4},{13,5},{14,6},{15,7},{16,8},{17,9... | collective-permute-start | bytes 1179656 | tf_op jit(solution)/shard_map/ppermute | solution.py:53
  58.9 12.7 %collective-permute-start.20 = (bf16[512,384]{1,0:T(8,128)(2,1)S(1)}, bf16[512,384]{1,0:T(8,128)(2,1)}, u32[]{:S(2)}, u32[]{:S(2)}) collective-permute-start(bf16[512,384]{1,0:T(8,128)(2,1)S(1)} %collective-permute-done.19.refs_11_), channel_id=1, source_target_pairs={{8,16},{9,17},{10,18},{11,19},{12,20},{13,21},{14,22},{15,23},{16,... | collective-permute-start | bytes 1179656 | tf_op jit(solution)/shard_map/ppermute | solution.py:53
  64.3 9.5 %collective-permute-start.10 = (bf16[128,2048]{1,0:T(8,128)(2,1)S(1)}, bf16[128,2048]{1,0:T(8,128)(2,1)S(1)}, u32[]{:S(2)}, u32[]{:S(2)}) collective-permute-start(bf16[128,2048]{1,0:T(8,128)(2,1)S(1)} %collective-permute-done.2.refs_1_), channel_id=1, source_target_pairs={{0,4},{1,5},{2,6},{3,7},{4,0},{5,1},{6,2},{7,3},{8,12},{9,13},{10,... | collective-permute-start | bytes 1572872 | tf_op jit(solution)/shard_map/ppermute | solution.py:53
  65.1 8.8 %collective-permute-start.11 = (bf16[128,2048]{1,0:T(8,128)(2,1)S(1)}, bf16[128,2048]{1,0:T(8,128)(2,1)}, u32[]{:S(2)}, u32[]{:S(2)}) collective-permute-start(bf16[128,2048]{1,0:T(8,128)(2,1)S(1)} %collective-permute-done.7.refs_2_), channel_id=1, source_target_pairs={{0,4},{1,5},{2,6},{3,7},{4,0},{5,1},{6,2},{7,3},{8,12},{9,13},{10,... | collective-permute-start | bytes 1572872 | tf_op jit(solution)/shard_map/ppermute | solution.py:53
  66.5 7.4 %collective-permute-start.12 = (bf16[128,2048]{1,0:T(8,128)(2,1)S(1)}, bf16[128,2048]{1,0:T(8,128)(2,1)}, u32[]{:S(2)}, u32[]{:S(2)}) collective-permute-start(bf16[128,2048]{1,0:T(8,128)(2,1)S(1)} %collective-permute-done.8.refs_3_), channel_id=1, source_target_pairs={{0,4},{1,5},{2,6},{3,7},{4,0},{5,1},{6,2},{7,3},{8,12},{9,13},{10,... | collective-permute-start | bytes 1572872 | tf_op jit(solution)/shard_map/ppermute | solution.py:53
  68.8 11.5 %collective-permute-start.18 = (bf16[512,384]{1,0:T(8,128)(2,1)}, bf16[512,384]{1,0:T(8,128)(2,1)}, u32[]{:S(2)}, u32[]{:S(2)}) collective-permute-start(bf16[512,384]{1,0:T(8,128)(2,1)} %collective-permute-done.17.refs_8_), channel_id=1, source_target_pairs={{8,0},{9,1},{10,2},{11,3},{12,4},{13,5},{14,6},{15,7}} | collective-permute-start | bytes 1179656 | tf_op jit(solution)/shard_map/ppermute | solution.py:53
  71.6 8.6 %collective-permute-start.21 = (bf16[512,384]{1,0:T(8,128)(2,1)}, bf16[512,384]{1,0:T(8,128)(2,1)}, u32[]{:S(2)}, u32[]{:S(2)}) collective-permute-start(bf16[512,384]{1,0:T(8,128)(2,1)} %collective-permute-done.20.refs_12_), channel_id=1, source_target_pairs={{16,24},{17,25},{18,26},{19,27},{20,28},{21,29},{22,30},{23,31}} | collective-permute-start | bytes 1179656 | tf_op jit(solution)/shard_map/ppermute | solution.py:53
  81.9 14.8 %collective-permute-start.22 = (bf16[4,256,256]{2,1,0:T(8,128)(2,1)S(1)}, bf16[4,256,256]{2,1,0:T(8,128)(2,1)S(1)}, u32[]{:S(2)}, u32[]{:S(2)}) collective-permute-start(bf16[4,256,256]{2,1,0:T(8,128)(2,1)S(1)} %get-tuple-element.14.own), channel_id=1, source_target_pairs={{0,8},{1,9},{2,10},{3,11},{4,12},{5,13},{6,14},{7,15},{8,16},{9,17... | collective-permute-start | bytes 1572872 | tf_op jit(solution)/shard_map/ppermute | solution.py:53
  87.1 15.2 %collective-permute-start.23 = (bf16[4,256,256]{2,1,0:T(8,128)(2,1)S(1)}, bf16[4,256,256]{2,1,0:T(8,128)(2,1)S(1)}, u32[]{:S(2)}, u32[]{:S(2)}) collective-permute-start(bf16[4,256,256]{2,1,0:T(8,128)(2,1)S(1)} %get-tuple-element.14.own), channel_id=1, source_target_pairs={{8,0},{9,1},{10,2},{11,3},{12,4},{13,5},{14,6},{15,7},{16,8},{17,9... | collective-permute-start | bytes 1572872 | tf_op jit(solution)/shard_map/ppermute | solution.py:53
  107.4 3.6 %collective-permute-start.24 = (bf16[4,128,128]{2,1,0:T(8,128)(2,1)S(1)}, bf16[4,128,128]{2,1,0:T(8,128)(2,1)S(1)}, u32[]{:S(2)}, u32[]{:S(2)}) collective-permute-start(bf16[4,128,128]{2,1,0:T(8,128)(2,1)S(1)} %get-tuple-element.16), channel_id=1, source_target_pairs={{0,4},{1,5},{2,6},{3,7},{4,0},{5,1},{6,2},{7,3},{8,12},{9,13},{10,... | collective-permute-start | bytes 393224 | tf_op jit(solution)/shard_map/ppermute | solution.py:53
  112.6 4.1 %collective-permute-start.27 = (bf16[128,256]{1,0:T(8,128)(2,1)S(1)}, bf16[128,256]{1,0:T(8,128)(2,1)S(1)}, u32[]{:S(2)}, u32[]{:S(2)}) collective-permute-start(bf16[128,256]{1,0:T(8,128)(2,1)S(1)} %get-tuple-element.22), channel_id=1, source_target_pairs={{0,3},{1,2},{2,1},{3,0},{4,7},{5,6},{6,5},{7,4},{8,11},{9,10},{10,... | collective-permute-start | bytes 196616 | tf_op jit(solution)/shard_map/ppermute | solution.py:53
  (16 other events, 127.9 us)

commit v3 on v0

--- a/solution.py
+++ b/solution.py
@@ -1,8 +1,11 @@
+import functools
 import math
 
 import jax
 import jax.numpy as jnp
 from jax import lax
+from jax.experimental import pallas as pl
+from jax.experimental.pallas import tpu as pltpu
 from jax.sharding import PartitionSpec as P
 
 HEADS = 8
@@ -10,6 +13,8 @@
 BT = 16
 PP = 8
 RD = 2
+VMEM = pltpu.VMEM
+SMEM = pltpu.SMEM
 
 
 def padded_2(value, sides, width):
@@ -25,6 +30,248 @@
     return value
 
 
+def normed_tokens(padded, stream, conv_w, gain):
+    time_len, site_len, width = stream.shape
+    tok_rows = time_len * site_len
+    embedded = stream.reshape(tok_rows, width).astype(jnp.float32)
+    for offset in range(3):
+        window = padded[:, offset : offset + site_len].reshape(tok_rows, padded.shape[2])
+        embedded = embedded + jnp.dot(window, conv_w[offset], preferred_element_type=jnp.float32)
+    scale = lax.rsqrt(jnp.mean(embedded * embedded, axis=-1, keepdims=True) + 1e-05)
+    return (embedded * scale * gain).astype(jnp.bfloat16)
+
+
+def hop(value, fn):
+    pairs = []
+    for z in range(4):
+        for core in range(2):
+            for depth in range(4):
+                to = fn(z, core, depth)
+                if to is not None:
+                    pairs.append(((2 * z + core) * 4 + depth, (2 * to[0] + to[1]) * 4 + to[2]))
+    return lax.ppermute(value, ("tm", "depth"), pairs)
+
+
+def swap_core(value):
+    return hop(value, lambda z, c, d: (z, 1 - c, d))
+
+
+def swap_depth(value, bits):
+    return hop(value, lambda z, c, d: (z, c, d ^ bits))
+
+
+def after(value, *others):
+    return lax.optimization_barrier((value, *others))[0]
+
+
+def move_z(value, by, only=range(4)):
+    return hop(value, lambda z, c, d: (z + by, c, d) if z in only and 0 <= z + by < 4 else None)
+
+
+def split_kernel(place, w_ref, x_ref, y_ref, keep_ref):
+    pair = 2 * HD
+    even = (place[1] & 1) == 0
+    low, high = w_ref[:, :pair], w_ref[:, 2 * pair :]
+    x_ref[...] = w_ref[:, pair : 2 * pair]
+    y_ref[...] = jnp.where(even, high, low)
+    keep_ref[...] = jnp.where(even, low, high)
+
+
+def sort_kernel(place, kept, from_x, from_y, keep_ref, send_ref):
+    first, even = (place[0] & 1) == 0, (place[1] & 1) == 0
+    low = jnp.where(even, kept[...], from_y[...])
+    high = jnp.where(even, from_y[...], kept[...])
+    for k, group in enumerate((low, from_x[...], high)):
+        here = slice(k * HD, (k + 1) * HD)
+        keep_ref[:, here] = jnp.where(first, group[:, :HD], group[:, HD:])
+        send_ref[:, here] = jnp.where(first, group[:, HD:], group[:, :HD])
+
+
+def embed_kernel(place, raw, beside, across, stream, conv_w, gain, out_ref, acc_ref):
+    time_len, site_len, feat_len = raw.shape
+    depth = place[1]
+    even = (depth & 1) == 0
+    side, far = beside[:time_len].astype(jnp.float32), across[:time_len].astype(jnp.float32)
+    before = jnp.where(even, jnp.where(depth == 2, far, 0.0), side)
+    behind = jnp.where(even, side, jnp.where(depth == 1, far, 0.0))
+    sites = raw[...].astype(jnp.float32)
+    padded = jnp.concatenate([before[:, None], sites, behind[:, None]], axis=1)
+    tok_rows = time_len * site_len
+    windows = [padded[:, j : j + site_len].reshape(tok_rows, feat_len).astype(jnp.bfloat16) for j in range(3)]
+    total = jnp.zeros((tok_rows, 1), jnp.float32)
+    width, step = stream.shape[1], 512
+    for at in range(0, width, step):
+        here = slice(at, at + step)
+        part = stream[:, here].astype(jnp.float32)
+        for j in range(3):
+            part += jnp.dot(windows[j], conv_w[j, :, here], preferred_element_type=jnp.float32)
+        acc_ref[:, here] = part
+        total += jnp.sum(part * part, axis=1, keepdims=True)
+    scale = lax.rsqrt(total / width + 1e-05)
+    out_ref[...] = (acc_ref[...] * scale * gain[...]).astype(jnp.bfloat16)
+
+
+def columns(x_refs, source, rows):
+    at = pl.ds(pl.multiple_of(source * rows, rows), rows)
+    return jnp.concatenate([ref[:, at] for ref in x_refs], axis=0)
+
+
+def partial_kernel(place, *refs):
+    x_refs, (own, far, near, acc_ref) = refs[:-4], refs[-4:]
+    z = place[0] >> 1
+    rows = own.shape[0]
+    value = jnp.dot(columns(x_refs, z, rows), own[...], preferred_element_type=jnp.float32)
+    value += jnp.dot(columns(x_refs, z ^ 2, rows), far[...], preferred_element_type=jnp.float32)
+    value += jnp.dot(columns(x_refs, z ^ 1, rows), near[...], preferred_element_type=jnp.float32)
+    acc_ref[...] = value
+
+
+def project_kernel(place, *refs):
+    x_refs, (own, far, near, last, acc_in, q_ref, kv_ref, acc_ref, both_ref) = refs[:10], refs[10:]
+    z, core, depth = place[0] >> 1, place[0] & 1, place[1]
+    rows, block = own.shape[0], x_refs[0].shape[0]
+    turn = jnp.where(depth == 3, 0, depth)
+    half = x_refs[6].shape[1]
+    for i in range(4):
+        both_ref[(i // 2) * block : (i // 2 + 1) * block, (i % 2) * half : (i % 2 + 1) * half] = x_refs[6 + i][...]
+    diagonals = [both_ref]
+    value = jnp.dot(columns(diagonals, z, rows), own[...], preferred_element_type=jnp.float32)
+    value += jnp.dot(columns(diagonals, z ^ 2, rows), far[...], preferred_element_type=jnp.float32)
+    value += jnp.dot(columns(diagonals, z ^ 1, rows), near[...], preferred_element_type=jnp.float32)
+    value += jnp.dot(columns(diagonals, z ^ 3, rows), last[...], preferred_element_type=jnp.float32)
+    acc_ref[6 * block :] = value
+    x = columns(x_refs[:6], z ^ 3, rows)
+    value = jnp.dot(x, last[...], preferred_element_type=jnp.float32)
+    acc_ref[: 6 * block] = acc_in[...] + value
+    for rel in range(2):
+        at = pl.ds(pl.multiple_of((core ^ rel) * block, block), block)
+        for r in range(4):
+            row = 3 * rel + r if r < 3 else 6 + rel
+            mine = slice(row * block, (row + 1) * block)
+            for third, (ref, column) in enumerate(((q_ref, 0), (kv_ref, 0), (kv_ref, HD))):
+                group = third + turn
+                group = jnp.where(group >= 3, group - 3, group)
+                lanes = pl.ds(pl.multiple_of(group * HD, HD), HD)
+                ref[r, at, column : column + HD] = acc_ref[mine, lanes].astype(jnp.bfloat16)
+
+
+def attend_kernel(place, mask, q_ref, before, own, behind, keep_ref, send_ref):
+    core = place[0] & 1
+    block = q_ref.shape[1] // 2
+    inv_root = 1.0 / math.sqrt(HD)
+    for r in range(4):
+        results = []
+        for u in range(2):
+            q = q_ref[r, u * block : (u + 1) * block]
+            spans = ((before, u, 2), (own, 0, 2), (behind, 0, 1 + u))
+            scores, entry = [], 0
+            for ref, first, last in spans:
+                k = ref[r, first * block : last * block, :HD]
+                s = lax.dot_general(q, k, (((1,), (1,)), ((), ())), preferred_element_type=jnp.float32)
+                for v in range(last - first):
+                    flag = mask[((u ^ core) * 4 + r) * 5 + entry]
+                    scores.append(jnp.where(flag > 0, s[:, v * block : (v + 1) * block] * inv_root, -1e30))
+                    entry += 1
+            top = jnp.max(functools.reduce(jnp.maximum, scores), axis=1, keepdims=True)
+            powers = [jnp.exp(s - top) for s in scores]
+            inverse = 1.0 / jnp.sum(functools.reduce(jnp.add, powers), axis=1, keepdims=True)
+            weights = [(p * inverse).astype(jnp.bfloat16) for p in powers]
+            result, entry = jnp.zeros((block, HD), jnp.float32), 0
+            for ref, first, last in spans:
+                w = jnp.concatenate(weights[entry : entry + last - first], axis=1)
+                entry += last - first
+                result += jnp.dot(w, ref[r, first * block : last * block, HD:], preferred_element_type=jnp.float32)
+            results.append(result.astype(jnp.bfloat16))
+        keep_ref[r] = jnp.where(core == 0, results[0], results[1])
+        send_ref[r] = jnp.where(core == 0, results[1], results[0])
+
+
+def gather_kernel(place, own, x, y, diagonal, out_ref):
+    core, depth = place[0] & 1, place[1]
+    for r, ref in enumerate((own, x, y, diagonal)):
+        for rel in range(2):
+            at = pl.multiple_of((2 * (depth ^ r) + (core ^ rel)) * HD, HD)
+            out_ref[:, pl.ds(at, HD)] = ref[:, rel * HD : (rel + 1) * HD]
+
+
+def vmem_call(kernel, outs, scratch=(), smem=1, total=1, limit=40, macs=0):
+    return pl.pallas_call(
+        kernel,
+        out_shape=outs,
+        in_specs=[pl.BlockSpec(memory_space=SMEM)] * smem + [pl.BlockSpec(memory_space=VMEM)] * (total - smem),
+        out_specs=jax.tree.map(lambda _: pl.BlockSpec(memory_space=VMEM), outs),
+        scratch_shapes=list(scratch),
+        cost_estimate=pl.CostEstimate(flops=2 * macs, bytes_accessed=0, transcendentals=0),
+        compiler_params=pltpu.CompilerParams(vmem_limit_bytes=limit * 2**20),
+    )
+
+
+def plane_device(raw, stream, conv_w, gain, w_qkv, mask):
+    tm, depth = lax.axis_index("tm"), lax.axis_index("depth")
+    first = (tm & 1) == 0
+    time_len, site_len, feat_len = raw.shape
+    block = time_len * site_len
+    bf16, f32 = jnp.bfloat16, jnp.float32
+
+    place = jnp.stack([tm, depth]).astype(jnp.int32)
+    pair = jax.ShapeDtypeStruct((w_qkv.shape[0], 2 * HD), bf16)
+    triple = jax.ShapeDtypeStruct((w_qkv.shape[0], 3 * HD), bf16)
+
+    to_x, to_y, kept = vmem_call(split_kernel, (pair,) * 3, total=2)(place, w_qkv)
+    from_y, from_x = swap_depth(to_y, 2), swap_depth(to_x, 1)
+    keep, send = vmem_call(sort_kernel, (triple,) * 2, total=4)(place, kept, from_x, from_y)
+    received = swap_core(send)
+    shard = jnp.concatenate([jnp.where(first, keep, received), jnp.where(first, received, keep)], axis=0)
+    far = hop(shard, lambda z, c, d: (z ^ 2, c, d))
+    near = hop(shard, lambda z, c, d: (z ^ 1, c, d))
+    far, near = lax.optimization_barrier((far, near))
+    last = hop(far, lambda z, c, d: (z ^ 1, c, d))
+
+    flags = jnp.pad(mask.reshape(1, mask.shape[2]), ((0, 0), (0, feat_len - mask.shape[2]))).astype(bf16)
+    edges = [jnp.where(depth == at, raw[:, -1], raw[:, 0]) for at in (depth & 2, 1)]
+    beside = swap_depth(jnp.concatenate([edges[0], flags]), 1)
+    across = swap_depth(jnp.concatenate([edges[1], flags]), 3)
+    flags = jnp.concatenate([flags, beside[time_len:], swap_depth(flags, 2), across[time_len:]])
+    flags = jnp.concatenate([flags, swap_core(flags)])[:, : mask.shape[2]].astype(jnp.int32).reshape(-1)
+
+    width = stream.shape[2]
+    normed = vmem_call(
+        embed_kernel,
+        jax.ShapeDtypeStruct((block, width), bf16),
+        scratch=[VMEM((block, width), f32)],
+        total=7,
+        macs=block * 3 * feat_len * width,
+    )(place, raw, beside, across, stream.reshape(block, width), conv_w, gain.reshape(1, width))
+    normed = after(normed, flags)
+    from_x, from_y = swap_depth(normed, 1), swap_depth(normed, 2)
+    half = width // 2
+    left, right = swap_depth(from_x[:, :half], 2), swap_depth(from_y[:, half:], 1)
+
+    rows = shard.shape[0]
+    tokens = [normed, from_x, from_y]
+    other = [swap_core(after(t, far)) for t in tokens]
+    total = vmem_call(
+        partial_kernel, jax.ShapeDtypeStruct((6 * block, 3 * HD), f32), total=10, macs=6 * block * 3 * rows * 3 * HD
+    )(place, *tokens, *other, shard, far, near)
+    left, right = after(left, total), after(right, total)
+    q, kv = vmem_call(
+        project_kernel,
+        (jax.ShapeDtypeStruct((4, 2 * block, HD), bf16), jax.ShapeDtypeStruct((4, 2 * block, 2 * HD), bf16)),
+        scratch=[VMEM((8 * block, 3 * HD), f32), VMEM((2 * block, width), bf16)],
+        total=16,
+        macs=14 * block * rows * 3 * HD,
+    )(place, *tokens, *other, left, right, swap_core(left), swap_core(right), shard, far, near, last, total)
+
+    piece = jax.ShapeDtypeStruct((4, block, HD), bf16)
+    kept, sent = vmem_call(attend_kernel, (piece, piece), smem=2, total=6, macs=8 * block * 10 * block * HD)(
+        place, flags, q, move_z(kv, 1), kv, move_z(kv, -1)
+    )
+    pairs = jnp.concatenate([kept, swap_core(sent)], axis=2)
+    pieces = [pairs[0]] + [swap_depth(pairs[bits], bits) for bits in (1, 2, 3)]
+    context = vmem_call(gather_kernel, jax.ShapeDtypeStruct((block, HEADS * HD), bf16), total=5)(place, *pieces)
+    return context.reshape(time_len, site_len, HEADS * HD)
+
+
 def from_behind(value, axis, by):
     devices = lax.axis_size(axis)
     pairs = [(i, i + by) for i in range(devices) if 0 <= i + by < devices]
@@ -44,16 +291,9 @@
 
 
 def per_device(raw, stream, conv_w, gain, w_qkv, mask):
-    time_len, site_len, feat_len = raw.shape
+    time_len, site_len, _ = raw.shape
     tok_rows = time_len * site_len
-    padded = padded_2(raw, (("depth", 1),), 1)
-    embedded = stream.reshape(tok_rows, stream.shape[2]).astype(jnp.float32)
-    for offset in range(3):
-        window = padded[:, offset : offset + site_len].reshape(tok_rows, feat_len)
-        embedded = embedded + jnp.dot(window, conv_w[offset], preferred_element_type=jnp.float32)
-    normed = (
-        embedded * lax.rsqrt(jnp.mean(embedded * embedded, axis=-1, keepdims=True) + 1e-05) * gain
-    ).astype(jnp.bfloat16)
+    normed = normed_tokens(padded_2(raw, (("depth", 1),), 1), stream, conv_w, gain)
     columns = lax.all_gather(w_qkv, "depth", axis=1, tiled=True)
     projected = jnp.dot(
         normed,
@@ -103,6 +343,7 @@
         P("depth", "tm", None),
     )
     out_specs = P("tm", "depth", None)
+    fits = mesh.shape["depth"] == 4 and mesh.shape["tm"] == 8
     return jax.shard_map(
-        per_device, mesh=mesh, in_specs=in_specs, out_specs=out_specs, check_vma=False
-    )
+        plane_device if fits else per_device, mesh=mesh, in_specs=in_specs, out_specs=out_specs, check_vma=False
+    )

time: 207 us -> 86.4 us (0.42)
  waiting for transfers between devices: 157 us -> 40 us
  between operations: 13.6 us -> 0.19 us
  matrix products: 12.1 us -> 0 us
  Pallas kernels: 0 us -> 11.4 us
  starting transfers between devices: 17.2 us -> 27 us
  local copies, waits for them, and re-layouts: 2.99 us -> 5.98 us
    all_gather x2 -> x0, waiting for transfers between devices: 142 us -> none  [the longest x1 108 us: per_device(): lax.all_gather(columns, 'tm', axis=0, tiled=True)]
    ppermute x6 -> x25, waiting for transfers between devices: 14.9 us -> 40 us  [hop(): return lax.ppermute(value, ('tm', 'depth'), pairs)]
    dot_general x20 -> x0, matrix products: 12.1 us -> none  [the longest x1 6.45 us: per_device(): jnp.dot(normed, lax.all_gather(columns, 'tm', axis=0, tiled=True), prefer...]
    pallas_call x0 -> x7, Pallas kernels: none -> 11.4 us  [the longest x1 3.9 us: plane_device(): vmem_call(attend_kernel, (piece, piece), smem=2, total=6, macs=8 * block...]
    ppermute x6 -> x25, starting transfers between devices: 17.2 us -> 27 us  [hop(): return lax.ppermute(value, ('tm', 'depth'), pairs)]
    unnamed x17 -> x11, local copies, waits for them, and re-layouts: 1.18 us -> 4.92 us
  transfers between devices with their start and end apart: 8 -> 25, of which waited for: 7 -> 11; matrix products, arithmetic and copies ran while one was open for 1% -> 1% of each run, Pallas kernels for 0% -> 4%
where the time goes in v3:
time: 86.4 us; the launch traced here: 85.5 us
  waiting for transfers between devices  40 us (46%)
  starting transfers between devices  27 us (31%)
  Pallas kernels  11.4 us (13%)
  local copies, waits for them, and re-layouts  5.98 us (7%)
    ppermute x25, waiting for transfers between devices, hop(): return lax.ppermute(value, ('tm', 'depth'), pairs)  40 us
    ppermute x25, starting transfers between devices, hop(): return lax.ppermute(value, ('tm', 'depth'), pairs)  27 us
    unnamed x11, local copies, waits for them, and re-layouts  4.92 us
    pallas_call x1, Pallas kernels, plane_device(): vmem_call(attend_kernel, (piece, piece), smem=2, total=6, macs=8 * block...  3.9 us
    pallas_call x1, Pallas kernels, plane_device(): vmem_call(partial_kernel, jax.ShapeDtypeStruct((6 * block, 3 * HD), f32),...  1.92 us
    pallas_call x1, Pallas kernels, plane_device(): vmem_call(project_kernel, (jax.ShapeDtypeStruct((4, 2 * block, HD), bf16)...  1.82 us
  transfers between devices with their start and end apart: 25, of which 11 were waited for; matrix products, arithmetic and copies ran while one was open for 1% of the time, Pallas kernels for 4%

profile of v3, /device:TPU:9, one launch (start us, length us, event | category | flops | bytes accessed | tf_op | source)
XLA Modules:
  0.0 85.5 jit_solution(6462484800169303664)
XLA Ops:
  0.7 1.2 %collective-permute-start.1 = (bf16[1,128]{1,0:T(2,128)(2,1)S(1)}, bf16[1,128]{1,0:T(2,128)(2,1)S(1)}, u32[]{:S(2)}, u32[]{:S(2)}) collective-permute-start(bf16[1,128]{1,0:T(2,128)(2,1)S(1)} %pad.5), channel_id=1, source_target_pairs={{0,2},{1,3},{2,0},{3,1},{4,6},{5,7},{6,4},{7,5},{8,10},{9,11},{10,... | collective-permute-start | bytes 776 | tf_op jit(solution)/shard_map/ppermute | solution.py:52
  5.9 1.3 %collective-permute-start.6 = (bf16[256,256]{1,0:T(8,128)(2,1)S(1)}, bf16[256,256]{1,0:T(8,128)(2,1)S(1)}, u32[]{:S(2)}, u32[]{:S(2)}) collective-permute-start(bf16[256,256]{1,0:T(8,128)(2,1)S(1)} %get-tuple-element.24), channel_id=1, source_target_pairs={{0,1},{1,0},{2,3},{3,2},{4,5},{5,4},{6,7},{7,6},{8,9},{9,8},{10,11... | collective-permute-start | bytes 393224 | tf_op jit(solution)/shard_map/ppermute | solution.py:52
  7.2 1.2 %collective-permute-start.7 = (bf16[256,256]{1,0:T(8,128)(2,1)S(1)}, bf16[256,256]{1,0:T(8,128)(2,1)S(1)}, u32[]{:S(2)}, u32[]{:S(2)}) collective-permute-start(bf16[256,256]{1,0:T(8,128)(2,1)S(1)} %get-tuple-element.25), channel_id=1, source_target_pairs={{0,2},{1,3},{2,0},{3,1},{4,6},{5,7},{6,4},{7,5},{8,10},{9,11},{10,... | collective-permute-start | bytes 393224 | tf_op jit(solution)/shard_map/ppermute | solution.py:52
  8.5 2.1 %collective-permute-start.3 = (bf16[4,128]{1,0:T(4,128)(2,1)S(1)}, bf16[4,128]{1,0:T(4,128)(2,1)S(1)}, u32[]{:S(2)}, u32[]{:S(2)}) collective-permute-start(bf16[4,128]{1,0:T(4,128)(2,1)S(1)} %pad_maximum_fusion.3), channel_id=1, source_target_pairs={{0,4},{1,5},{2,6},{3,7},{4,0},{5,1},{6,2},{7,3},{8,12},{9,13},{10,... | collective-permute-start | bytes 3080 | tf_op jit(solution)/shard_map/ppermute | solution.py:52
  10.6 1.4 %copy-done = bf16[3,128,2048]{2,1,0:T(8,128)(2,1)S(1)} copy-done((bf16[3,128,2048]{2,1,0:T(8,128)(2,1)S(1)}, bf16[3,128,2048]{2,1,0:T(8,128)(2,1)}, u32[]{:S(2)}) %copy-start) | copy-done | bytes 1572888
  14.5 1.3 %shard_map.64.refs_0_ = bf16[128,2048]{1,0:T(8,128)(2,1)S(1)} custom-call(s32[2]{0:T(128)S(1)} %pad_add_fusion.place, bf16[16,8,128]{2,1,0:T(8,128)(2,1)S(1)} %copy-done.3, bf16[17,128]{1,0:T(8,128)(2,1)S(1)} %collective-permute-done.beside, bf16[17,128]{1,0:T(8,128)(2,1)S(1)} %collective-permute-done.2.across, bf16[128,2048]{1,0:T(8,128)(2,1)S(1)} %bitcast.19, ...), custom_call_target="tpu_custom_call" | custom-call | flops 201326592 | tf_op jit(solution)/shard_map/pallas_call | solution.py:238
  18.3 2.3 %collective-permute-start.9 = (bf16[512,384]{1,0:T(8,128)(2,1)S(1)}, bf16[512,384]{1,0:T(8,128)(2,1)S(1)}, u32[]{:S(2)}, u32[]{:S(2)}) collective-permute-start(bf16[512,384]{1,0:T(8,128)(2,1)S(1)} %pad_maximum_fusion.refs_6_.refs_10_), channel_id=1, source_target_pairs={{0,16},{1,17},{2,18},{3,19},{4,20},{5,21},{6,22},{7,23},{8,24},{9,... | collective-permute-start | bytes 1179656 | tf_op jit(solution)/shard_map/ppermute | solution.py:52
  20.6 14.4 %collective-permute-done.10.refs_8_.refs_12_ = bf16[512,384]{1,0:T(8,128)(2,1)S(1)} collective-permute-done((bf16[512,384]{1,0:T(8,128)(2,1)S(1)}, bf16[512,384]{1,0:T(8,128)(2,1)S(1)}, u32[]{:S(2)}, u32[]{:S(2)}) %collective-permute-start.10) | collective-permute-done | bytes 393248 | tf_op jit(solution)/shard_map/ppermute | solution.py:52
  35.0 3.1 %collective-permute-done.9.refs_7_.refs_11_ = bf16[512,384]{1,0:T(8,128)(2,1)S(1)} collective-permute-done((bf16[512,384]{1,0:T(8,128)(2,1)S(1)}, bf16[512,384]{1,0:T(8,128)(2,1)S(1)}, u32[]{:S(2)}, u32[]{:S(2)}) %collective-permute-start.9) | collective-permute-done | bytes 393248 | tf_op jit(solution)/shard_map/ppermute | solution.py:52
  40.2 1.3 %collective-permute-start.14 = (bf16[128,1024]{1,0:T(8,128)(2,1)S(1)}, bf16[128,1024]{1,0:T(8,128)(2,1)S(1)}, u32[]{:S(2)}, u32[]{:S(2)}) collective-permute-start(bf16[128,1024]{1,0:T(8,128)(2,1)S(1)} %slice.48), channel_id=1, source_target_pairs={{0,2},{1,3},{2,0},{3,1},{4,6},{5,7},{6,4},{7,5},{8,10},{9,11},{10,... | collective-permute-start | bytes 786440 | tf_op jit(solution)/shard_map/ppermute | solution.py:52
  41.5 1.3 %collective-permute-start.18 = (bf16[512,384]{1,0:T(8,128)(2,1)S(1)}, bf16[512,384]{1,0:T(8,128)(2,1)S(1)}, u32[]{:S(2)}, u32[]{:S(2)}) collective-permute-start(bf16[512,384]{1,0:T(8,128)(2,1)S(1)} %collective-permute-done.9.refs_7_.refs_11_), channel_id=1, source_target_pairs={{0,8},{1,9},{2,10},{3,11},{4,12},{5,13},{6,14},{7,15},{8,0},{9,1},... | collective-permute-start | bytes 1179656 | tf_op jit(solution)/shard_map/ppermute | solution.py:52
  42.8 1.9 %shard_map.67.refs_14_ = f32[768,384]{1,0:T(8,128)S(1)} custom-call(s32[2]{0:T(128)S(1)} %pad_add_fusion.place, bf16[128,2048]{1,0:T(8,128)(2,1)S(1)} %shard_map.64.refs_0_, bf16[128,2048]{1,0:T(8,128)(2,1)S(1)} %collective-permute-done.4.refs_1_, bf16[128,2048]{1,0:T(8,128)(2,1)S(1)} %collective-permute-done.5.refs_2_, ...), custom_call_target="tpu_custom_call" | custom-call | flops 905969664 | tf_op jit(solution)/shard_map/pallas_call | solution.py:253
  44.8 2.9 %collective-permute-done.15.refs_7_ = bf16[128,1024]{1,0:T(8,128)(2,1)S(1)} collective-permute-done((bf16[128,1024]{1,0:T(8,128)(2,1)S(1)}, bf16[128,1024]{1,0:T(8,128)(2,1)S(1)}, u32[]{:S(2)}, u32[]{:S(2)}) %collective-permute-start.15) | collective-permute-done | bytes 262176 | tf_op jit(solution)/shard_map/ppermute | solution.py:52
  49.0 2.5 %collective-permute-done.18.refs_13_ = bf16[512,384]{1,0:T(8,128)(2,1)S(1)} collective-permute-done((bf16[512,384]{1,0:T(8,128)(2,1)S(1)}, bf16[512,384]{1,0:T(8,128)(2,1)S(1)}, u32[]{:S(2)}, u32[]{:S(2)}) %collective-permute-start.18) | collective-permute-done | bytes 393248 | tf_op jit(solution)/shard_map/ppermute | solution.py:52
  51.6 1.8 %shard_map.68 = (bf16[4,256,128]{2,1,0:T(8,128)(2,1)S(1)}, bf16[4,256,256]{2,1,0:T(8,128)(2,1)S(1)}) custom-call(s32[2]{0:T(128)S(1)} %pad_add_fusion.place, bf16[128,2048]{1,0:T(8,128)(2,1)S(1)} %shard_map.64.refs_0_, bf16[128,2048]{1,0:T(8,128)(2,1)S(1)} %collective-permute-done.4.refs_1_, bf16[128,2048]{1,0:T(8,128)(2,1)S(1)} %collective-permute-done.5.refs_2_, ...), custom_call_target="tpu_custom_call" | custom-call | flops 704643072 | tf_op jit(solution)/shard_map/pallas_call | solution.py:257
  53.4 3.2 %collective-permute-start.20 = (bf16[4,256,256]{2,1,0:T(8,128)(2,1)S(1)}, bf16[4,256,256]{2,1,0:T(8,128)(2,1)S(1)}, u32[]{:S(2)}, u32[]{:S(2)}) collective-permute-start(bf16[4,256,256]{2,1,0:T(8,128)(2,1)S(1)} %get-tuple-element.36.own), channel_id=1, source_target_pairs={{8,0},{9,1},{10,2},{11,3},{12,4},{13,5},{14,6},{15,7},{16,8},{17,9... | collective-permute-start | bytes 1572872 | tf_op jit(solution)/shard_map/ppermute | solution.py:52
  56.6 2.1 %collective-permute-start.19 = (bf16[4,256,256]{2,1,0:T(8,128)(2,1)S(1)}, bf16[4,256,256]{2,1,0:T(8,128)(2,1)S(1)}, u32[]{:S(2)}, u32[]{:S(2)}) collective-permute-start(bf16[4,256,256]{2,1,0:T(8,128)(2,1)S(1)} %get-tuple-element.36.own), channel_id=1, source_target_pairs={{0,8},{1,9},{2,10},{3,11},{4,12},{5,13},{6,14},{7,15},{8,16},{9,17... | collective-permute-start | bytes 1572872 | tf_op jit(solution)/shard_map/ppermute | solution.py:52
  58.7 8.5 %collective-permute-done.20.behind = bf16[4,256,256]{2,1,0:T(8,128)(2,1)S(1)} collective-permute-done((bf16[4,256,256]{2,1,0:T(8,128)(2,1)S(1)}, bf16[4,256,256]{2,1,0:T(8,128)(2,1)S(1)}, u32[]{:S(2)}, u32[]{:S(2)}) %collective-permute-start.20) | collective-permute-done | bytes 524320 | tf_op jit(solution)/shard_map/ppermute | solution.py:52
  67.2 2.9 %collective-permute-done.19.before = bf16[4,256,256]{2,1,0:T(8,128)(2,1)S(1)} collective-permute-done((bf16[4,256,256]{2,1,0:T(8,128)(2,1)S(1)}, bf16[4,256,256]{2,1,0:T(8,128)(2,1)S(1)}, u32[]{:S(2)}, u32[]{:S(2)}) %collective-permute-start.19) | collective-permute-done | bytes 524320 | tf_op jit(solution)/shard_map/ppermute | solution.py:52
  70.1 3.9 %shard_map.69 = (bf16[4,128,128]{2,1,0:T(8,128)(2,1)S(1)}, bf16[4,128,128]{2,1,0:T(8,128)(2,1)S(1)}) custom-call(s32[2]{0:T(128)S(1)} %pad_add_fusion.place, s32[40]{0:T(128)S(1)} %reshape.29.mask, bf16[4,256,128]{2,1,0:T(8,128)(2,1)S(1)} %get-tuple-element.35.q_ref, bf16[4,256,256]{2,1,0:T(8,128)(2,1)S(1)} %collective-permute-done.19.before, ...), custom_call_target="tpu_custom_call" | custom-call | flops 335544320 | tf_op jit(solution)/shard_map/pallas_call | solution.py:266
  74.0 2.8 %collective-permute-start.21 = (bf16[4,128,128]{2,1,0:T(8,128)(2,1)S(1)}, bf16[4,128,128]{2,1,0:T(8,128)(2,1)S(1)}, u32[]{:S(2)}, u32[]{:S(2)}) collective-permute-start(bf16[4,128,128]{2,1,0:T(8,128)(2,1)S(1)} %get-tuple-element.38), channel_id=1, source_target_pairs={{0,4},{1,5},{2,6},{3,7},{4,0},{5,1},{6,2},{7,3},{8,12},{9,13},{10,... | collective-permute-start | bytes 393224 | tf_op jit(solution)/shard_map/ppermute | solution.py:52
  80.6 1.4 %collective-permute-done.24.diagonal = bf16[128,256]{1,0:T(8,128)(2,1)S(1)} collective-permute-done((bf16[128,256]{1,0:T(8,128)(2,1)S(1)}, bf16[128,256]{1,0:T(8,128)(2,1)S(1)}, u32[]{:S(2)}, u32[]{:S(2)}) %collective-permute-start.24) | collective-permute-done | bytes 65568 | tf_op jit(solution)/shard_map/ppermute | solution.py:52
  82.0 2.2 %collective-permute-done.23.y = bf16[128,256]{1,0:T(8,128)(2,1)S(1)} collective-permute-done((bf16[128,256]{1,0:T(8,128)(2,1)S(1)}, bf16[128,256]{1,0:T(8,128)(2,1)S(1)}, u32[]{:S(2)}, u32[]{:S(2)}) %collective-permute-start.23) | collective-permute-done | bytes 65568 | tf_op jit(solution)/shard_map/ppermute | solution.py:52
  84.2 1.3 %shard_map.70 = bf16[128,1024]{1,0:T(8,128)(2,1)} custom-call(s32[2]{0:T(128)S(1)} %pad_add_fusion.place, bf16[128,256]{1,0:T(8,128)(2,1)S(1)} %get-tuple-element.44.own, bf16[128,256]{1,0:T(8,128)(2,1)S(1)} %collective-permute-done.22.x, bf16[128,256]{1,0:T(8,128)(2,1)S(1)} %collective-permute-done.23.y, bf16[128,256]{1,0:T(8,128)(2,1)S(1)} %collective-permute-done.24.diagonal), custom_call_target="tpu_custom_call" | custom-call | tf_op jit(solution)/shard_map/pallas_call | solution.py:271
  (62 shorter events, 16.8 us)
Async XLA Ops:
  0.7 7.8 %collective-permute-start.1 = (bf16[1,128]{1,0:T(2,128)(2,1)S(1)}, bf16[1,128]{1,0:T(2,128)(2,1)S(1)}, u32[]{:S(2)}, u32[]{:S(2)}) collective-permute-start(bf16[1,128]{1,0:T(2,128)(2,1)S(1)} %pad.5), channel_id=1, source_target_pairs={{0,2},{1,3},{2,0},{3,1},{4,6},{5,7},{6,4},{7,5},{8,10},{9,11},{10,... | collective-permute-start | bytes 776 | tf_op jit(solution)/shard_map/ppermute | solution.py:52
  2.8 5.6 %collective-permute-start.2 = (bf16[17,128]{1,0:T(8,128)(2,1)S(1)}, bf16[17,128]{1,0:T(8,128)(2,1)S(1)}, u32[]{:S(2)}, u32[]{:S(2)}) collective-permute-start(bf16[17,128]{1,0:T(8,128)(2,1)S(1)} %get-tuple-element.49), channel_id=1, source_target_pairs={{0,3},{1,2},{2,1},{3,0},{4,7},{5,6},{6,5},{7,4},{8,11},{9,10},{10,... | collective-permute-start | bytes 13064 | tf_op jit(solution)/shard_map/ppermute | solution.py:52
  4.0 4.4 %collective-permute-start = (bf16[17,128]{1,0:T(8,128)(2,1)S(1)}, bf16[17,128]{1,0:T(8,128)(2,1)S(1)}, u32[]{:S(2)}, u32[]{:S(2)}) collective-permute-start(bf16[17,128]{1,0:T(8,128)(2,1)S(1)} %get-tuple-element.50), channel_id=1, source_target_pairs={{0,1},{1,0},{2,3},{3,2},{4,5},{5,4},{6,7},{7,6},{8,9},{9,8},{10,11... | collective-permute-start | bytes 13064 | tf_op jit(solution)/shard_map/ppermute | solution.py:52
  5.9 9.9 %collective-permute-start.6 = (bf16[256,256]{1,0:T(8,128)(2,1)S(1)}, bf16[256,256]{1,0:T(8,128)(2,1)S(1)}, u32[]{:S(2)}, u32[]{:S(2)}) collective-permute-start(bf16[256,256]{1,0:T(8,128)(2,1)S(1)} %get-tuple-element.24), channel_id=1, source_target_pairs={{0,1},{1,0},{2,3},{3,2},{4,5},{5,4},{6,7},{7,6},{8,9},{9,8},{10,11... | collective-permute-start | bytes 393224 | tf_op jit(solution)/shard_map/ppermute | solution.py:52
  7.2 8.7 %collective-permute-start.7 = (bf16[256,256]{1,0:T(8,128)(2,1)S(1)}, bf16[256,256]{1,0:T(8,128)(2,1)S(1)}, u32[]{:S(2)}, u32[]{:S(2)}) collective-permute-start(bf16[256,256]{1,0:T(8,128)(2,1)S(1)} %get-tuple-element.25), channel_id=1, source_target_pairs={{0,2},{1,3},{2,0},{3,1},{4,6},{5,7},{6,4},{7,5},{8,10},{9,11},{10,... | collective-permute-start | bytes 393224 | tf_op jit(solution)/shard_map/ppermute | solution.py:52
  8.5 7.3 %collective-permute-start.3 = (bf16[4,128]{1,0:T(4,128)(2,1)S(1)}, bf16[4,128]{1,0:T(4,128)(2,1)S(1)}, u32[]{:S(2)}, u32[]{:S(2)}) collective-permute-start(bf16[4,128]{1,0:T(4,128)(2,1)S(1)} %pad_maximum_fusion.3), channel_id=1, source_target_pairs={{0,4},{1,5},{2,6},{3,7},{4,0},{5,1},{6,2},{7,3},{8,12},{9,13},{10,... | collective-permute-start | bytes 3080 | tf_op jit(solution)/shard_map/ppermute | solution.py:52
  16.7 22.6 %collective-permute-start.5 = (bf16[128,2048]{1,0:T(8,128)(2,1)S(1)}, bf16[128,2048]{1,0:T(8,128)(2,1)S(1)}, u32[]{:S(2)}, u32[]{:S(2)}) collective-permute-start(bf16[128,2048]{1,0:T(8,128)(2,1)S(1)} %shard_map.64.refs_0_), channel_id=1, source_target_pairs={{0,2},{1,3},{2,0},{3,1},{4,6},{5,7},{6,4},{7,5},{8,10},{9,11},{10,... | collective-permute-start | bytes 1572872 | tf_op jit(solution)/shard_map/ppermute | solution.py:52
  16.9 22.3 %collective-permute-start.4 = (bf16[128,2048]{1,0:T(8,128)(2,1)S(1)}, bf16[128,2048]{1,0:T(8,128)(2,1)S(1)}, u32[]{:S(2)}, u32[]{:S(2)}) collective-permute-start(bf16[128,2048]{1,0:T(8,128)(2,1)S(1)} %shard_map.64.refs_0_), channel_id=1, source_target_pairs={{0,1},{1,0},{2,3},{3,2},{4,5},{5,4},{6,7},{7,6},{8,9},{9,8},{10,11... | collective-permute-start | bytes 1572872 | tf_op jit(solution)/shard_map/ppermute | solution.py:52
  18.1 16.9 %collective-permute-start.10 = (bf16[512,384]{1,0:T(8,128)(2,1)S(1)}, bf16[512,384]{1,0:T(8,128)(2,1)S(1)}, u32[]{:S(2)}, u32[]{:S(2)}) collective-permute-start(bf16[512,384]{1,0:T(8,128)(2,1)S(1)} %pad_maximum_fusion.refs_6_.refs_10_), channel_id=1, source_target_pairs={{0,8},{1,9},{2,10},{3,11},{4,12},{5,13},{6,14},{7,15},{8,0},{9,1},... | collective-permute-start | bytes 1179656 | tf_op jit(solution)/shard_map/ppermute | solution.py:52
  18.3 19.8 %collective-permute-start.9 = (bf16[512,384]{1,0:T(8,128)(2,1)S(1)}, bf16[512,384]{1,0:T(8,128)(2,1)S(1)}, u32[]{:S(2)}, u32[]{:S(2)}) collective-permute-start(bf16[512,384]{1,0:T(8,128)(2,1)S(1)} %pad_maximum_fusion.refs_6_.refs_10_), channel_id=1, source_target_pairs={{0,16},{1,17},{2,18},{3,19},{4,20},{5,21},{6,22},{7,23},{8,24},{9,... | collective-permute-start | bytes 1179656 | tf_op jit(solution)/shard_map/ppermute | solution.py:52
  38.2 3.4 %collective-permute-start.11 = (bf16[128,2048]{1,0:T(8,128)(2,1)S(1)}, bf16[128,2048]{1,0:T(8,128)(2,1)S(1)}, u32[]{:S(2)}, u32[]{:S(2)}) collective-permute-start(bf16[128,2048]{1,0:T(8,128)(2,1)S(1)} %shard_map.64.refs_0_), channel_id=1, source_target_pairs={{0,4},{1,5},{2,6},{3,7},{4,0},{5,1},{6,2},{7,3},{8,12},{9,13},{10,... | collective-permute-start | bytes 1572872 | tf_op jit(solution)/shard_map/ppermute | solution.py:52
  39.2 3.6 %collective-permute-start.13 = (bf16[128,2048]{1,0:T(8,128)(2,1)S(1)}, bf16[128,2048]{1,0:T(8,128)(2,1)S(1)}, u32[]{:S(2)}, u32[]{:S(2)}) collective-permute-start(bf16[128,2048]{1,0:T(8,128)(2,1)S(1)} %collective-permute-done.5.refs_2_), channel_id=1, source_target_pairs={{0,4},{1,5},{2,6},{3,7},{4,0},{5,1},{6,2},{7,3},{8,12},{9,13},{10,... | collective-permute-start | bytes 1572872 | tf_op jit(solution)/shard_map/ppermute | solution.py:52
  39.2 3.6 %collective-permute-start.12 = (bf16[128,2048]{1,0:T(8,128)(2,1)S(1)}, bf16[128,2048]{1,0:T(8,128)(2,1)S(1)}, u32[]{:S(2)}, u32[]{:S(2)}) collective-permute-start(bf16[128,2048]{1,0:T(8,128)(2,1)S(1)} %collective-permute-done.4.refs_1_), channel_id=1, source_target_pairs={{0,4},{1,5},{2,6},{3,7},{4,0},{5,1},{6,2},{7,3},{8,12},{9,13},{10,... | collective-permute-start | bytes 1572872 | tf_op jit(solution)/shard_map/ppermute | solution.py:52
  39.8 7.9 %collective-permute-start.15 = (bf16[128,1024]{1,0:T(8,128)(2,1)S(1)}, bf16[128,1024]{1,0:T(8,128)(2,1)S(1)}, u32[]{:S(2)}, u32[]{:S(2)}) collective-permute-start(bf16[128,1024]{1,0:T(8,128)(2,1)S(1)} %slice.49), channel_id=1, source_target_pairs={{0,1},{1,0},{2,3},{3,2},{4,5},{5,4},{6,7},{7,6},{8,9},{9,8},{10,11... | collective-permute-start | bytes 786440 | tf_op jit(solution)/shard_map/ppermute | solution.py:52
  40.2 7.6 %collective-permute-start.14 = (bf16[128,1024]{1,0:T(8,128)(2,1)S(1)}, bf16[128,1024]{1,0:T(8,128)(2,1)S(1)}, u32[]{:S(2)}, u32[]{:S(2)}) collective-permute-start(bf16[128,1024]{1,0:T(8,128)(2,1)S(1)} %slice.48), channel_id=1, source_target_pairs={{0,2},{1,3},{2,0},{3,1},{4,6},{5,7},{6,4},{7,5},{8,10},{9,11},{10,... | collective-permute-start | bytes 786440 | tf_op jit(solution)/shard_map/ppermute | solution.py:52
  41.5 10.0 %collective-permute-start.18 = (bf16[512,384]{1,0:T(8,128)(2,1)S(1)}, bf16[512,384]{1,0:T(8,128)(2,1)S(1)}, u32[]{:S(2)}, u32[]{:S(2)}) collective-permute-start(bf16[512,384]{1,0:T(8,128)(2,1)S(1)} %collective-permute-done.9.refs_7_.refs_11_), channel_id=1, source_target_pairs={{0,8},{1,9},{2,10},{3,11},{4,12},{5,13},{6,14},{7,15},{8,0},{9,1},... | collective-permute-start | bytes 1179656 | tf_op jit(solution)/shard_map/ppermute | solution.py:52
  47.8 3.7 %collective-permute-start.16 = (bf16[128,1024]{1,0:T(8,128)(2,1)S(1)}, bf16[128,1024]{1,0:T(8,128)(2,1)S(1)}, u32[]{:S(2)}, u32[]{:S(2)}) collective-permute-start(bf16[128,1024]{1,0:T(8,128)(2,1)S(1)} %collective-permute-done.14.refs_6_), channel_id=1, source_target_pairs={{0,4},{1,5},{2,6},{3,7},{4,0},{5,1},{6,2},{7,3},{8,12},{9,13},{10,... | collective-permute-start | bytes 786440 | tf_op jit(solution)/shard_map/ppermute | solution.py:52
  49.0 2.6 %collective-permute-start.17 = (bf16[128,1024]{1,0:T(8,128)(2,1)S(1)}, bf16[128,1024]{1,0:T(8,128)(2,1)S(1)}, u32[]{:S(2)}, u32[]{:S(2)}) collective-permute-start(bf16[128,1024]{1,0:T(8,128)(2,1)S(1)} %collective-permute-done.15.refs_7_), channel_id=1, source_target_pairs={{0,4},{1,5},{2,6},{3,7},{4,0},{5,1},{6,2},{7,3},{8,12},{9,13},{10,... | collective-permute-start | bytes 786440 | tf_op jit(solution)/shard_map/ppermute | solution.py:52
  53.4 13.8 %collective-permute-start.20 = (bf16[4,256,256]{2,1,0:T(8,128)(2,1)S(1)}, bf16[4,256,256]{2,1,0:T(8,128)(2,1)S(1)}, u32[]{:S(2)}, u32[]{:S(2)}) collective-permute-start(bf16[4,256,256]{2,1,0:T(8,128)(2,1)S(1)} %get-tuple-element.36.own), channel_id=1, source_target_pairs={{8,0},{9,1},{10,2},{11,3},{12,4},{13,5},{14,6},{15,7},{16,8},{17,9... | collective-permute-start | bytes 1572872 | tf_op jit(solution)/shard_map/ppermute | solution.py:52
  56.6 13.5 %collective-permute-start.19 = (bf16[4,256,256]{2,1,0:T(8,128)(2,1)S(1)}, bf16[4,256,256]{2,1,0:T(8,128)(2,1)S(1)}, u32[]{:S(2)}, u32[]{:S(2)}) collective-permute-start(bf16[4,256,256]{2,1,0:T(8,128)(2,1)S(1)} %get-tuple-element.36.own), channel_id=1, source_target_pairs={{0,8},{1,9},{2,10},{3,11},{4,12},{5,13},{6,14},{7,15},{8,16},{9,17... | collective-permute-start | bytes 1572872 | tf_op jit(solution)/shard_map/ppermute | solution.py:52
  74.0 3.7 %collective-permute-start.21 = (bf16[4,128,128]{2,1,0:T(8,128)(2,1)S(1)}, bf16[4,128,128]{2,1,0:T(8,128)(2,1)S(1)}, u32[]{:S(2)}, u32[]{:S(2)}) collective-permute-start(bf16[4,128,128]{2,1,0:T(8,128)(2,1)S(1)} %get-tuple-element.38), channel_id=1, source_target_pairs={{0,4},{1,5},{2,6},{3,7},{4,0},{5,1},{6,2},{7,3},{8,12},{9,13},{10,... | collective-permute-start | bytes 393224 | tf_op jit(solution)/shard_map/ppermute | solution.py:52
  77.9 4.1 %collective-permute-start.24 = (bf16[128,256]{1,0:T(8,128)(2,1)S(1)}, bf16[128,256]{1,0:T(8,128)(2,1)S(1)}, u32[]{:S(2)}, u32[]{:S(2)}) collective-permute-start(bf16[128,256]{1,0:T(8,128)(2,1)S(1)} %get-tuple-element.41), channel_id=1, source_target_pairs={{0,3},{1,2},{2,1},{3,0},{4,7},{5,6},{6,5},{7,4},{8,11},{9,10},{10,... | collective-permute-start | bytes 196616 | tf_op jit(solution)/shard_map/ppermute | solution.py:52
  79.0 5.2 %collective-permute-start.23 = (bf16[128,256]{1,0:T(8,128)(2,1)S(1)}, bf16[128,256]{1,0:T(8,128)(2,1)S(1)}, u32[]{:S(2)}, u32[]{:S(2)}) collective-permute-start(bf16[128,256]{1,0:T(8,128)(2,1)S(1)} %get-tuple-element.42), channel_id=1, source_target_pairs={{0,2},{1,3},{2,0},{3,1},{4,6},{5,7},{6,4},{7,5},{8,10},{9,11},{10,... | collective-permute-start | bytes 196616 | tf_op jit(solution)/shard_map/ppermute | solution.py:52
  79.4 4.8 %collective-permute-start.22 = (bf16[128,256]{1,0:T(8,128)(2,1)S(1)}, bf16[128,256]{1,0:T(8,128)(2,1)S(1)}, u32[]{:S(2)}, u32[]{:S(2)}) collective-permute-start(bf16[128,256]{1,0:T(8,128)(2,1)S(1)} %get-tuple-element.43), channel_id=1, source_target_pairs={{0,1},{1,0},{2,3},{3,2},{4,5},{5,4},{6,7},{7,6},{8,9},{9,8},{10,11... | collective-permute-start | bytes 196616 | tf_op jit(solution)/shard_map/ppermute | solution.py:52
  (6 other events, 6.4 us)

commit v4 on v0

--- a/solution.py
+++ b/solution.py
@@ -1,8 +1,11 @@
+import functools
 import math
 
 import jax
 import jax.numpy as jnp
 from jax import lax
+from jax.experimental import pallas as pl
+from jax.experimental.pallas import tpu as pltpu
 from jax.sharding import PartitionSpec as P
 
 HEADS = 8
@@ -10,6 +13,8 @@
 BT = 16
 PP = 8
 RD = 2
+VMEM = pltpu.VMEM
+SMEM = pltpu.SMEM
 
 
 def padded_2(value, sides, width):
@@ -25,6 +30,325 @@
     return value
 
 
+def normed_tokens(padded, stream, conv_w, gain):
+    time_len, site_len, width = stream.shape
+    tok_rows = time_len * site_len
+    embedded = stream.reshape(tok_rows, width).astype(jnp.float32)
+    for offset in range(3):
+        window = padded[:, offset : offset + site_len].reshape(tok_rows, padded.shape[2])
+        embedded = embedded + jnp.dot(window, conv_w[offset], preferred_element_type=jnp.float32)
+    scale = lax.rsqrt(jnp.mean(embedded * embedded, axis=-1, keepdims=True) + 1e-05)
+    return (embedded * scale * gain).astype(jnp.bfloat16)
+
+
+PAIR = 2 * HD
+EXTRA = 16
+
+
+def hop(value, fn):
+    pairs = []
+    for z in range(4):
+        for core in range(2):
+            for depth in range(4):
+                to = fn(z, core, depth)
+                if to is not None:
+                    pairs.append(((2 * z + core) * 4 + depth, (2 * to[0] + to[1]) * 4 + to[2]))
+    return lax.ppermute(value, ("tm", "depth"), pairs)
+
+
+def swap_core(value):
+    return hop(value, lambda z, c, d: (z, 1 - c, d))
+
+
+def swap_depth(value, bits):
+    return hop(value, lambda z, c, d: (z, c, d ^ bits))
+
+
+def swap_z(value, bits):
+    return hop(value, lambda z, c, d: (z ^ bits, c, d))
+
+
+def move_z(value, by):
+    return hop(value, lambda z, c, d: (z + by, c, d) if 0 <= z + by < 4 else None)
+
+
+def after(value, *others):
+    return lax.optimization_barrier((value, *others))[0]
+
+
+def where_am_i():
+    tm = lax.axis_index("tm")
+    return tm >> 1, tm & 1, lax.axis_index("depth")
+
+
+def split_kernel(mask, w, raw, to_x, to_y, to_across, keep, sites, sems):
+    _, _, depth = where_am_i()
+    odd = depth & 1
+    size = w.shape[0]
+    copies = [pltpu.make_async_copy(raw, sites, sems.at[3])]
+    for i, (at, ref) in enumerate(
+        ((PAIR, to_x.at[:size]), ((1 - odd) * 2 * PAIR, to_y.at[:size]), (odd * 2 * PAIR, keep))
+    ):
+        at = at if isinstance(at, int) else pl.multiple_of(at, PAIR)
+        copies.append(pltpu.make_async_copy(w.at[:, pl.ds(at, PAIR)], ref, sems.at[i]))
+    for copy in copies:
+        copy.start()
+    lane = lax.broadcasted_iota(jnp.int32, (EXTRA, HD), 1)
+    flags = jnp.zeros((EXTRA, HD), jnp.int32)
+    for entry in range(mask.shape[0]):
+        flags = jnp.where(lane == entry, mask[entry], flags)
+    flags = flags.astype(jnp.float32).astype(jnp.bfloat16)
+    copies[0].wait()
+    values = sites[...].astype(jnp.float32)
+    first, last = values[:, 0], values[:, values.shape[1] - 1]
+    for ref, use_last, at in ((to_x, odd == 0, size), (to_across, depth == 1, 0)):
+        ref[at : at + EXTRA, :HD] = jnp.where(use_last, last, first).astype(jnp.bfloat16)
+        ref[at : at + EXTRA, HD:] = flags
+    to_y[size:, :HD] = flags
+    to_y[size:, HD:] = flags
+    for copy in copies[1:]:
+        copy.wait()
+
+
+def sort_kernel(kept, from_x, from_y, across, to_y, keep_ref, send_ref, flags_ref):
+    _, core, depth = where_am_i()
+    first, even = core == 0, (depth & 1) == 0
+    size = kept.shape[0]
+    low = jnp.where(even, kept[...], from_y[:size])
+    high = jnp.where(even, from_y[:size], kept[...])
+    for k, group in enumerate((low, from_x[:size], high)):
+        here = slice(k * HD, (k + 1) * HD)
+        keep_ref[:, here] = jnp.where(first, group[:, :HD], group[:, HD:])
+        send_ref[:size, here] = jnp.where(first, group[:, HD:], group[:, :HD])
+    row = lax.broadcasted_iota(jnp.int32, (EXTRA, HD), 0)
+    flags = to_y[size:, :HD].astype(jnp.float32)
+    for r, value in ((1, from_x[size:, HD:]), (2, from_y[size:, :HD]), (3, across[:, HD:])):
+        flags = jnp.where(row == r, value.astype(jnp.float32), flags)
+    flags = flags.astype(jnp.bfloat16)
+    flags_ref[...] = flags
+    for k in range(3):
+        send_ref[size:, k * HD : (k + 1) * HD] = flags
+
+
+def embed_kernel(from_x, across, gain, raw, stream, conv_w, out_ref, acc, sites, tokens, weights, sems):
+    time_len, site_len, feat_len = raw.shape
+    _, _, depth = where_am_i()
+    even = (depth & 1) == 0
+    rows, width = stream.shape
+    parts = weights.shape[0]
+    step = width // parts
+    first = pltpu.make_async_copy(raw, sites, sems.at[2 * parts])
+    first.start()
+    copies = []
+    for i in range(parts):
+        here = pl.ds(i * step, step)
+        pair = (
+            pltpu.make_async_copy(conv_w.at[:, :, here], weights.at[i], sems.at[2 * i]),
+            pltpu.make_async_copy(stream.at[:, here], tokens.at[i], sems.at[2 * i + 1]),
+        )
+        for copy in pair:
+            copy.start()
+        copies.append(pair)
+    side = from_x[from_x.shape[0] - EXTRA :, :HD].astype(jnp.float32)
+    far = across[:, :HD].astype(jnp.float32)
+    before = jnp.where(even, jnp.where(depth == 2, far, 0.0), side)
+    behind = jnp.where(even, side, jnp.where(depth == 1, far, 0.0))
+    first.wait()
+    padded = jnp.concatenate([before[:, None], sites[...].astype(jnp.float32), behind[:, None]], axis=1)
+    windows = [padded[:, j : j + site_len].reshape(rows, feat_len).astype(jnp.bfloat16) for j in range(3)]
+    windows = jnp.concatenate(windows, axis=1)
+    total = jnp.zeros((rows, 1), jnp.float32)
+    for i, pair in enumerate(copies):
+        for copy in pair:
+            copy.wait()
+        part = jnp.dot(windows, weights[i].reshape(3 * feat_len, step), preferred_element_type=jnp.float32)
+        part += tokens[i].astype(jnp.float32)
+        acc[:, i * step : (i + 1) * step] = part
+        total += jnp.sum(part * part, axis=1, keepdims=True)
+    scale = lax.rsqrt(total / width + 1e-05)
+    out_ref[...] = (acc[...] * scale * gain[...]).astype(jnp.bfloat16)
+
+
+def take(refs, source, core, rows):
+    half = rows // 2
+    cuts = [pl.ds(pl.multiple_of(source * rows + c * half, half), half) for c in (core, 1 - core)]
+    return jnp.concatenate([jnp.concatenate([ref[:, at] for at in cuts], axis=1) for ref in refs], axis=0)
+
+
+def partial_kernel(*refs):
+    x_refs, (own, far, near, acc_ref) = refs[:4], refs[4:]
+    z, core, _ = where_am_i()
+    w = jnp.concatenate([own[...], far[...], near[...]], axis=0)
+    x = [take(x_refs, source, core, own.shape[0]) for source in (z, z ^ 2, z ^ 1)]
+    acc_ref[...] = jnp.dot(jnp.concatenate(x, axis=1), w, preferred_element_type=jnp.float32)
+
+
+def project_kernel(*refs):
+    early, late, (own, far, near, last, acc_in, q_ref, k_ref, v_ref, acc_ref, x_all) = refs[:4], refs[4:12], refs[12:]
+    z, core, depth = where_am_i()
+    rows, block, half = last.shape[0], late[0].shape[0], late[0].shape[1]
+    for i, ref in enumerate(late):
+        x_all[(i // 2) * block : (i // 2 + 1) * block, (i % 2) * half : (i % 2 + 1) * half] = ref[...]
+    w = jnp.concatenate([own[...], far[...], near[...], last[...]], axis=0)
+    x = [take([x_all], source, core, rows) for source in (z, z ^ 2, z ^ 1, z ^ 3)]
+    acc_ref[4 * block :] = jnp.dot(jnp.concatenate(x, axis=1), w, preferred_element_type=jnp.float32)
+    x = take(early, z ^ 3, core, rows)
+    acc_ref[: 4 * block] = acc_in[...] + jnp.dot(x, last[...], preferred_element_type=jnp.float32)
+    order = ((0, 1, 2, 6), (3, 4, 5, 7))
+    turn = jnp.where(depth == 3, 0, depth)
+    for rel in range(2):
+        at = pl.ds(pl.multiple_of((core ^ rel) * block, block), block)
+        for r in range(4):
+            row = order[rel][r]
+            mine = slice(row * block, (row + 1) * block)
+            for third, ref in enumerate((q_ref, k_ref, v_ref)):
+                group = third + turn
+                group = jnp.where(group >= 3, group - 3, group)
+                lanes = pl.ds(pl.multiple_of(group * HD, HD), HD)
+                ref[r, at, :] = acc_ref[mine, lanes].astype(jnp.bfloat16)
+
+
+def spans(u):
+    return ((0, u, 2), (1, 0, 2), (2, 0, 1 + u))
+
+
+def weigh_kernel(q_ref, before, own, behind, own_flags, other_flags, out_ref):
+    _, core, _ = where_am_i()
+    block = q_ref.shape[1] // 2
+    inv_root = 1.0 / math.sqrt(HD)
+    flags = [own_flags[...].astype(jnp.float32), other_flags[...].astype(jnp.float32)]
+    flags = [jnp.where(core == u, flags[0], flags[1]) for u in range(2)]
+    bias = [(f - 1.0) * 1e30 for f in flags]
+    keys = (before, own, behind)
+    for r in range(4):
+        for u in range(2):
+            q = q_ref[r, u * block : (u + 1) * block]
+            scores = []
+            for side, first, last in spans(u):
+                k = keys[side][r, first * block : last * block]
+                s = lax.dot_general(q, k, (((1,), (1,)), ((), ())), preferred_element_type=jnp.float32)
+                for v in range(last - first):
+                    entry = len(scores)
+                    shut = jnp.broadcast_to(bias[u][r : r + 1, entry : entry + 1], (block, block))
+                    scores.append(s[:, v * block : (v + 1) * block] * inv_root + shut)
+            top = jnp.max(functools.reduce(jnp.maximum, scores), axis=1, keepdims=True)
+            powers = [jnp.exp(s - top) for s in scores]
+            inverse = 1.0 / jnp.sum(functools.reduce(jnp.add, powers), axis=1, keepdims=True)
+            for entry, p in enumerate(powers):
+                here = slice(entry * block, (entry + 1) * block)
+                out_ref[r, u * block : (u + 1) * block, here] = (p * inverse).astype(jnp.bfloat16)
+
+
+def mix_kernel(r, weights, before, own, behind, out_ref):
+    block = weights.shape[1] // 2
+    values = (before, own, behind)
+    for u in range(2):
+        w = weights[r, u * block : (u + 1) * block]
+        v = [values[side][r, first * block : last * block] for side, first, last in spans(u)]
+        result = jnp.dot(w, jnp.concatenate(v, axis=0), preferred_element_type=jnp.float32)
+        out_ref[u * block : (u + 1) * block] = result.astype(jnp.bfloat16)
+
+
+def gather_kernel(*refs):
+    out_ref = refs[-1]
+    _, core, depth = where_am_i()
+    block = out_ref.shape[0]
+    mine = pl.ds(pl.multiple_of(core * block, block), block)
+    for i, ref in enumerate(refs[:-1]):
+        r, rel = i >> 1, i & 1
+        at = pl.multiple_of((2 * (depth ^ r) + (core ^ rel)) * HD, HD)
+        out_ref[:, pl.ds(at, HD)] = ref[mine, :]
+
+
+def call(kernel, outs, places, scratch=(), macs=0):
+    spaces = {"s": SMEM, "v": VMEM, "a": pl.ANY}
+    return pl.pallas_call(
+        kernel,
+        out_shape=outs,
+        in_specs=[pl.BlockSpec(memory_space=spaces[place]) for place in places],
+        out_specs=jax.tree.map(lambda _: pl.BlockSpec(memory_space=VMEM), outs),
+        scratch_shapes=list(scratch),
+        cost_estimate=pl.CostEstimate(flops=2 * macs, bytes_accessed=0, transcendentals=0),
+        compiler_params=pltpu.CompilerParams(vmem_limit_bytes=({2: 60, 3: 58}.get(places.count("a"), 40)) * 2**20),
+    )
+
+
+def plane_device(raw, stream, conv_w, gain, w_qkv, mask):
+    time_len, site_len, feat_len = raw.shape
+    block, width = time_len * site_len, stream.shape[2]
+    half, size = width // 2, w_qkv.shape[0]
+    bf16, f32 = jnp.bfloat16, jnp.float32
+
+    def array(*shape, kind=bf16):
+        return jax.ShapeDtypeStruct(shape, kind)
+
+    to_x, to_y, to_across, kept = call(
+        split_kernel,
+        (array(size + EXTRA, PAIR), array(size + EXTRA, PAIR), array(EXTRA, PAIR), array(size, PAIR)),
+        "saa",
+        scratch=[VMEM(raw.shape, bf16), pltpu.SemaphoreType.DMA((4,))],
+    )(mask.reshape(mask.shape[2]), w_qkv, raw)
+    from_x, from_y, across = swap_depth(to_x, 1), swap_depth(to_y, 2), swap_depth(to_across, 3)
+    keep, send, flags = call(
+        sort_kernel, (array(size, 3 * HD), array(size + EXTRA, 3 * HD), array(EXTRA, HD)), "v" * 5
+    )(kept, from_x, from_y, across, to_y)
+    received = swap_core(send)
+    other_flags = received[size:, :HD]
+    shard = jnp.concatenate([keep, received[:size]], axis=0)
+    far, near = swap_z(shard, 2), swap_z(shard, 1)
+
+    parts = 4
+    normed = call(
+        embed_kernel,
+        array(block, width),
+        "vvvaaa",
+        scratch=[
+            VMEM((block, width), f32),
+            VMEM(raw.shape, bf16),
+            VMEM((parts, block, width // parts), bf16),
+            VMEM((parts, 3, feat_len, width // parts), bf16),
+            pltpu.SemaphoreType.DMA((2 * parts + 1,)),
+        ],
+        macs=block * 3 * feat_len * width,
+    )(from_x, across, gain.reshape(1, width), raw, stream.reshape(block, width), conv_w)
+    normed = after(normed, received)
+    beside, above = swap_depth(normed, 1), swap_depth(normed, 2)
+    opposite = swap_core(normed)
+    far, near, opposite = lax.optimization_barrier((far, near, opposite))
+    last = swap_z(far, 1)
+    halves = [t[:, i * half : (i + 1) * half] for t in (after(beside, far), after(above, far)) for i in range(2)]
+    diagonal = [swap_depth(halves[0], 2), swap_depth(halves[3], 1)]
+    rows = 2 * size
+    early = (normed, beside, above, opposite)
+    total = call(partial_kernel, array(4 * block, 3 * HD, kind=f32), "v" * 7, macs=4 * block * 3 * rows * 3 * HD)(
+        *early, shard, far, near
+    )
+    diagonal = [after(t, total) for t in diagonal]
+    late = [swap_core(t) for t in halves] + diagonal + [swap_core(t) for t in diagonal]
+    one_head = array(4, 2 * block, HD)
+    q, k, v = call(
+        project_kernel,
+        (one_head,) * 3,
+        "v" * 17,
+        scratch=[VMEM((8 * block, 3 * HD), f32), VMEM((4 * block, width), bf16)],
+        macs=20 * block * rows * 3 * HD,
+    )(*early, *late, shard, far, near, last, total)
+
+    weights = call(weigh_kernel, array(4, 2 * block, 5 * block), "v" * 6, macs=8 * block * 5 * block * HD)(
+        q, move_z(k, 1), k, move_z(k, -1), flags, other_flags
+    )
+    values = (move_z(v, 1), v, move_z(v, -1))
+    pieces = {}
+    for r in (3, 1, 2, 0):
+        mixed = call(functools.partial(mix_kernel, r), array(2 * block, HD), "vvvv", macs=2 * block * 5 * block * HD)(
+            weights, *values
+        )
+        pieces[r] = swap_depth(mixed, r) if r else mixed
+    both = [t for r in range(4) for t in (pieces[r], swap_core(pieces[r]))]
+    context = call(gather_kernel, array(block, HEADS * HD), "v" * 8)(*both)
+    return context.reshape(time_len, site_len, HEADS * HD)
+
+
 def from_behind(value, axis, by):
     devices = lax.axis_size(axis)
     pairs = [(i, i + by) for i in range(devices) if 0 <= i + by < devices]
@@ -44,16 +368,9 @@
 
 
 def per_device(raw, stream, conv_w, gain, w_qkv, mask):
-    time_len, site_len, feat_len = raw.shape
+    time_len, site_len, _ = raw.shape
     tok_rows = time_len * site_len
-    padded = padded_2(raw, (("depth", 1),), 1)
-    embedded = stream.reshape(tok_rows, stream.shape[2]).astype(jnp.float32)
-    for offset in range(3):
-        window = padded[:, offset : offset + site_len].reshape(tok_rows, feat_len)
-        embedded = embedded + jnp.dot(window, conv_w[offset], preferred_element_type=jnp.float32)
-    normed = (
-        embedded * lax.rsqrt(jnp.mean(embedded * embedded, axis=-1, keepdims=True) + 1e-05) * gain
-    ).astype(jnp.bfloat16)
+    normed = normed_tokens(padded_2(raw, (("depth", 1),), 1), stream, conv_w, gain)
     columns = lax.all_gather(w_qkv, "depth", axis=1, tiled=True)
     projected = jnp.dot(
         normed,
@@ -103,6 +420,7 @@
         P("depth", "tm", None),
     )
     out_specs = P("tm", "depth", None)
+    fits = mesh.shape["depth"] == 4 and mesh.shape["tm"] == 8
     return jax.shard_map(
-        per_device, mesh=mesh, in_specs=in_specs, out_specs=out_specs, check_vma=False
-    )
+        plane_device if fits else per_device, mesh=mesh, in_specs=in_specs, out_specs=out_specs, check_vma=False
+    )

time: 207 us -> 82.9 us (0.40)
  waiting for transfers between devices: 157 us -> 30.4 us
  starting transfers between devices: 17.2 us -> 37.4 us
  between operations: 13.6 us -> 0.2 us
  Pallas kernels: 0 us -> 12.4 us
  matrix products: 12.1 us -> 0 us
    all_gather x2 -> x0, waiting for transfers between devices: 142 us -> none  [the longest x1 108 us: per_device(): lax.all_gather(columns, 'tm', axis=0, tiled=True)]
    ppermute x6 -> x29, starting transfers between devices: 17.2 us -> 37.4 us  [hop(): return lax.ppermute(value, ('tm', 'depth'), pairs)]
    ppermute x6 -> x29, waiting for transfers between devices: 14.9 us -> 30.4 us  [hop(): return lax.ppermute(value, ('tm', 'depth'), pairs)]
    pallas_call x0 -> x11, Pallas kernels: none -> 12.4 us  [the longest x1 4.16 us: plane_device(): call(embed_kernel, array(block, width), 'vvvaaa', scratch=[VMEM((block, w...]
    dot_general x20 -> x0, matrix products: 12.1 us -> none  [the longest x1 6.45 us: per_device(): jnp.dot(normed, lax.all_gather(columns, 'tm', axis=0, tiled=True), prefer...]
  transfers between devices with their start and end apart: 8 -> 29, of which waited for: 7 -> 10; matrix products, arithmetic and copies ran while one was open for 1% -> 0% of each run, Pallas kernels for 0% -> 9%
where the time goes in v4:
time: 82.9 us; the launch traced here: 82.4 us
  starting transfers between devices  37.4 us (45%)
  waiting for transfers between devices  30.4 us (37%)
  Pallas kernels  12.4 us (15%)
  local copies, waits for them, and re-layouts  1.95 us (2%)
    ppermute x29, starting transfers between devices, hop(): return lax.ppermute(value, ('tm', 'depth'), pairs)  37.4 us
    ppermute x29, waiting for transfers between devices, hop(): return lax.ppermute(value, ('tm', 'depth'), pairs)  30.4 us
    pallas_call x1, Pallas kernels, plane_device(): call(embed_kernel, array(block, width), 'vvvaaa', scratch=[VMEM((block, w...  4.16 us
    pallas_call x1, Pallas kernels, plane_device(): call(split_kernel, (array(size + EXTRA, PAIR), array(size + EXTRA, PAIR),...  2.5 us
    unnamed x10, local copies, waits for them, and re-layouts  1.86 us
    pallas_call x1, Pallas kernels, plane_device(): call(project_kernel, (one_head,) * 3, 'v' * 17, scratch=[VMEM((8 * block,...  1.74 us
  transfers between devices with their start and end apart: 29, of which 10 were waited for; matrix products, arithmetic and copies ran while one was open for 0% of the time, Pallas kernels for 9%

profile of v4, /device:TPU:9, one launch (start us, length us, event | category | flops | bytes accessed | tf_op | source)
XLA Modules:
  0.0 82.4 jit_solution(16351060003714820380)
XLA Ops:
  0.0 2.5 %shard_map.64 = (bf16[272,256]{1,0:T(8,128)(2,1)}, bf16[272,256]{1,0:T(8,128)(2,1)}, bf16[16,256]{1,0:T(8,128)(2,1)}, bf16[256,256]{1,0:T(8,128)(2,1)}) custom-call(s32[5]{0:T(128)} %bitcast.6, bf16[256,768]{1,0:T(8,128)(2,1)} %w.1, bf16[16,8,128]{2,1,0:T(8,128)(2,1)} %raw.3), custom_call_target="tpu_custom_call" | custom-call | tf_op jit(solution)/shard_map/pallas_call | solution.py:285
  2.5 1.3 %collective-permute-start = (bf16[272,256]{1,0:T(8,128)(2,1)}, bf16[272,256]{1,0:T(8,128)(2,1)S(1)}, u32[]{:S(2)}, u32[]{:S(2)}) collective-permute-start(bf16[272,256]{1,0:T(8,128)(2,1)} %get-tuple-element.23), channel_id=1, source_target_pairs={{0,1},{1,0},{2,3},{3,2},{4,5},{5,4},{6,7},{7,6},{8,9},{9,8},{10,11... | collective-permute-start | bytes 417800 | tf_op jit(solution)/shard_map/ppermute | solution.py:56
  3.8 1.2 %collective-permute-start.2 = (bf16[272,256]{1,0:T(8,128)(2,1)}, bf16[272,256]{1,0:T(8,128)(2,1)S(1)}, u32[]{:S(2)}, u32[]{:S(2)}) collective-permute-start(bf16[272,256]{1,0:T(8,128)(2,1)} %get-tuple-element.26.to_y), channel_id=1, source_target_pairs={{0,2},{1,3},{2,0},{3,1},{4,6},{5,7},{6,4},{7,5},{8,10},{9,11},{10,... | collective-permute-start | bytes 417800 | tf_op jit(solution)/shard_map/ppermute | solution.py:56
  5.2 3.5 %collective-permute-done.1.across = bf16[16,256]{1,0:T(8,128)(2,1)S(1)} collective-permute-done((bf16[16,256]{1,0:T(8,128)(2,1)}, bf16[16,256]{1,0:T(8,128)(2,1)S(1)}, u32[]{:S(2)}, u32[]{:S(2)}) %collective-permute-start.1) | collective-permute-done | bytes 8224 | tf_op jit(solution)/shard_map/ppermute | solution.py:56
  10.7 2.3 %collective-permute-start.3 = (bf16[272,384]{1,0:T(8,128)(2,1)S(1)}, bf16[272,384]{1,0:T(8,128)(2,1)S(1)}, u32[]{:S(2)}, u32[]{:S(2)}) collective-permute-start(bf16[272,384]{1,0:T(8,128)(2,1)S(1)} %get-tuple-element.27), channel_id=1, source_target_pairs={{0,4},{1,5},{2,6},{3,7},{4,0},{5,1},{6,2},{7,3},{8,12},{9,13},{10,... | collective-permute-start | bytes 626696 | tf_op jit(solution)/shard_map/ppermute | solution.py:56
  13.0 4.2 %shard_map.65.refs_0_ = bf16[128,2048]{1,0:T(8,128)(2,1)} custom-call(bf16[272,256]{1,0:T(8,128)(2,1)} %copy-done.1, bf16[16,256]{1,0:T(8,128)(2,1)} %copy-done.4, f32[1,2048]{1,0:T(1,128)} %bitcast.5, bf16[16,8,128]{2,1,0:T(8,128)(2,1)} %raw.3, bf16[128,2048]{1,0:T(8,128)(2,1)} %bitcast.4, bf16[3,128,2048]{2,1,0:T(8,128)(2,1)} %conv_w.1), custom_call_target="tpu_custom_call" | custom-call | flops 201326592 | tf_op jit(solution)/shard_map/pallas_call | solution.py:301
  18.1 2.3 %collective-permute-start.6 = (bf16[512,384]{1,0:T(8,128)(2,1)S(1)}, bf16[512,384]{1,0:T(8,128)(2,1)S(1)}, u32[]{:S(2)}, u32[]{:S(2)}) collective-permute-start(bf16[512,384]{1,0:T(8,128)(2,1)S(1)} %pad_maximum_fusion.refs_4_.refs_12_), channel_id=1, source_target_pairs={{0,16},{1,17},{2,18},{3,19},{4,20},{5,21},{6,22},{7,23},{8,24},{9,... | collective-permute-start | bytes 1179656 | tf_op jit(solution)/shard_map/ppermute | solution.py:56
  20.7 13.5 %collective-permute-done.7.refs_6_.refs_14_ = bf16[512,384]{1,0:T(8,128)(2,1)S(1)} collective-permute-done((bf16[512,384]{1,0:T(8,128)(2,1)S(1)}, bf16[512,384]{1,0:T(8,128)(2,1)S(1)}, u32[]{:S(2)}, u32[]{:S(2)}) %collective-permute-start.7) | collective-permute-done | bytes 393248 | tf_op jit(solution)/shard_map/ppermute | solution.py:56
  34.2 3.2 %collective-permute-done.6.refs_5_.refs_13_ = bf16[512,384]{1,0:T(8,128)(2,1)S(1)} collective-permute-done((bf16[512,384]{1,0:T(8,128)(2,1)S(1)}, bf16[512,384]{1,0:T(8,128)(2,1)S(1)}, u32[]{:S(2)}, u32[]{:S(2)}) %collective-permute-start.6) | collective-permute-done | bytes 393248 | tf_op jit(solution)/shard_map/ppermute | solution.py:56
  38.9 2.2 %collective-permute-start.11 = (bf16[128,1024]{1,0:T(8,128)(2,1)S(1)}, bf16[128,1024]{1,0:T(8,128)(2,1)S(1)}, u32[]{:S(2)}, u32[]{:S(2)}) collective-permute-start(bf16[128,1024]{1,0:T(8,128)(2,1)S(1)} %get-tuple-element.42), channel_id=1, source_target_pairs={{0,4},{1,5},{2,6},{3,7},{4,0},{5,1},{6,2},{7,3},{8,12},{9,13},{10,... | collective-permute-start | bytes 786440 | tf_op jit(solution)/shard_map/ppermute | solution.py:56
  41.1 1.3 %collective-permute-start.17 = (bf16[512,384]{1,0:T(8,128)(2,1)S(1)}, bf16[512,384]{1,0:T(8,128)(2,1)S(1)}, u32[]{:S(2)}, u32[]{:S(2)}) collective-permute-start(bf16[512,384]{1,0:T(8,128)(2,1)S(1)} %collective-permute-done.6.refs_5_.refs_13_), channel_id=1, source_target_pairs={{0,8},{1,9},{2,10},{3,11},{4,12},{5,13},{6,14},{7,15},{8,0},{9,1},... | collective-permute-start | bytes 1179656 | tf_op jit(solution)/shard_map/ppermute | solution.py:56
  43.6 2.6 %collective-permute-start.9 = (bf16[128,1024]{1,0:T(8,128)(2,1)S(1)}, bf16[128,1024]{1,0:T(8,128)(2,1)S(1)}, u32[]{:S(2)}, u32[]{:S(2)}) collective-permute-start(bf16[128,1024]{1,0:T(8,128)(2,1)S(1)} %get-tuple-element.44), channel_id=1, source_target_pairs={{0,4},{1,5},{2,6},{3,7},{4,0},{5,1},{6,2},{7,3},{8,12},{9,13},{10,... | collective-permute-start | bytes 786440 | tf_op jit(solution)/shard_map/ppermute | solution.py:56
  47.7 3.5 %collective-permute-done.17.refs_15_ = bf16[512,384]{1,0:T(8,128)(2,1)S(1)} collective-permute-done((bf16[512,384]{1,0:T(8,128)(2,1)S(1)}, bf16[512,384]{1,0:T(8,128)(2,1)S(1)}, u32[]{:S(2)}, u32[]{:S(2)}) %collective-permute-start.17) | collective-permute-done | bytes 393248 | tf_op jit(solution)/shard_map/ppermute | solution.py:56
  51.3 1.7 %shard_map.68 = (bf16[4,256,128]{2,1,0:T(8,128)(2,1)S(1)}, bf16[4,256,128]{2,1,0:T(8,128)(2,1)S(1)}, bf16[4,256,128]{2,1,0:T(8,128)(2,1)S(1)}) custom-call(bf16[128,2048]{1,0:T(8,128)(2,1)S(1)} %copy-done, bf16[128,2048]{1,0:T(8,128)(2,1)S(1)} %collective-permute-done.4.refs_1_, bf16[128,2048]{1,0:T(8,128)(2,1)S(1)} %collective-permute-done.5.refs_2_, ...), custom_call_target="tpu_custom_call" | custom-call | flops 1006632960 | tf_op jit(solution)/shard_map/pallas_call | solution.py:329
  53.0 3.2 %collective-permute-start.19 = (bf16[4,256,128]{2,1,0:T(8,128)(2,1)S(1)}, bf16[4,256,128]{2,1,0:T(8,128)(2,1)S(1)}, u32[]{:S(2)}, u32[]{:S(2)}) collective-permute-start(bf16[4,256,128]{2,1,0:T(8,128)(2,1)S(1)} %get-tuple-element.38.own), channel_id=1, source_target_pairs={{8,0},{9,1},{10,2},{11,3},{12,4},{13,5},{14,6},{15,7},{16,8},{17,9... | collective-permute-start | bytes 786440 | tf_op jit(solution)/shard_map/ppermute | solution.py:56
  56.2 2.1 %collective-permute-start.18 = (bf16[4,256,128]{2,1,0:T(8,128)(2,1)S(1)}, bf16[4,256,128]{2,1,0:T(8,128)(2,1)S(1)}, u32[]{:S(2)}, u32[]{:S(2)}) collective-permute-start(bf16[4,256,128]{2,1,0:T(8,128)(2,1)S(1)} %get-tuple-element.38.own), channel_id=1, source_target_pairs={{0,8},{1,9},{2,10},{3,11},{4,12},{5,13},{6,14},{7,15},{8,16},{9,17... | collective-permute-start | bytes 786440 | tf_op jit(solution)/shard_map/ppermute | solution.py:56
  58.3 3.2 %collective-permute-start.21 = (bf16[4,256,128]{2,1,0:T(8,128)(2,1)S(1)}, bf16[4,256,128]{2,1,0:T(8,128)(2,1)S(1)}, u32[]{:S(2)}, u32[]{:S(2)}) collective-permute-start(bf16[4,256,128]{2,1,0:T(8,128)(2,1)S(1)} %get-tuple-element.40.own), channel_id=1, source_target_pairs={{8,0},{9,1},{10,2},{11,3},{12,4},{13,5},{14,6},{15,7},{16,8},{17,9... | collective-permute-start | bytes 786440 | tf_op jit(solution)/shard_map/ppermute | solution.py:56
  61.5 2.1 %collective-permute-start.20 = (bf16[4,256,128]{2,1,0:T(8,128)(2,1)S(1)}, bf16[4,256,128]{2,1,0:T(8,128)(2,1)S(1)}, u32[]{:S(2)}, u32[]{:S(2)}) collective-permute-start(bf16[4,256,128]{2,1,0:T(8,128)(2,1)S(1)} %get-tuple-element.40.own), channel_id=1, source_target_pairs={{0,8},{1,9},{2,10},{3,11},{4,12},{5,13},{6,14},{7,15},{8,16},{9,17... | collective-permute-start | bytes 786440 | tf_op jit(solution)/shard_map/ppermute | solution.py:56
  65.5 1.3 %collective-permute-done.21.behind = bf16[4,256,128]{2,1,0:T(8,128)(2,1)S(1)} collective-permute-done((bf16[4,256,128]{2,1,0:T(8,128)(2,1)S(1)}, bf16[4,256,128]{2,1,0:T(8,128)(2,1)S(1)}, u32[]{:S(2)}, u32[]{:S(2)}) %collective-permute-start.21) | collective-permute-done | bytes 262176 | tf_op jit(solution)/shard_map/ppermute | solution.py:56
  66.7 2.9 %collective-permute-done.20.before = bf16[4,256,128]{2,1,0:T(8,128)(2,1)S(1)} collective-permute-done((bf16[4,256,128]{2,1,0:T(8,128)(2,1)S(1)}, bf16[4,256,128]{2,1,0:T(8,128)(2,1)S(1)}, u32[]{:S(2)}, u32[]{:S(2)}) %collective-permute-start.20) | collective-permute-done | bytes 262176 | tf_op jit(solution)/shard_map/ppermute | solution.py:56
  69.9 1.3 %collective-permute-start.23 = (bf16[256,128]{1,0:T(8,128)(2,1)S(1)}, bf16[256,128]{1,0:T(8,128)(2,1)S(1)}, u32[]{:S(2)}, u32[]{:S(2)}) collective-permute-start(bf16[256,128]{1,0:T(8,128)(2,1)S(1)} %shard_map.71), channel_id=1, source_target_pairs={{0,1},{1,0},{2,3},{3,2},{4,5},{5,4},{6,7},{7,6},{8,9},{9,8},{10,11... | collective-permute-start | bytes 196616 | tf_op jit(solution)/shard_map/ppermute | solution.py:56
  73.5 3.7 %collective-permute-start.22 = (bf16[256,128]{1,0:T(8,128)(2,1)S(1)}, bf16[256,128]{1,0:T(8,128)(2,1)S(1)}, u32[]{:S(2)}, u32[]{:S(2)}) collective-permute-start(bf16[256,128]{1,0:T(8,128)(2,1)S(1)} %shard_map.70.refs_0_), channel_id=1, source_target_pairs={{0,4},{1,5},{2,6},{3,7},{4,0},{5,1},{6,2},{7,3},{8,12},{9,13},{10,... | collective-permute-start | bytes 196616 | tf_op jit(solution)/shard_map/ppermute | solution.py:56
  77.5 1.4 %collective-permute-start.26 = (bf16[256,128]{1,0:T(8,128)(2,1)S(1)}, bf16[256,128]{1,0:T(8,128)(2,1)S(1)}, u32[]{:S(2)}, u32[]{:S(2)}) collective-permute-start(bf16[256,128]{1,0:T(8,128)(2,1)S(1)} %collective-permute-done.25.refs_4_), channel_id=1, source_target_pairs={{0,4},{1,5},{2,6},{3,7},{4,0},{5,1},{6,2},{7,3},{8,12},{9,13},{10,... | collective-permute-start | bytes 196616 | tf_op jit(solution)/shard_map/ppermute | solution.py:56
  78.8 1.9 %collective-permute-start.28 = (bf16[256,128]{1,0:T(8,128)(2,1)S(1)}, bf16[256,128]{1,0:T(8,128)(2,1)S(1)}, u32[]{:S(2)}, u32[]{:S(2)}) collective-permute-start(bf16[256,128]{1,0:T(8,128)(2,1)S(1)} %collective-permute-done.27.refs_6_), channel_id=1, source_target_pairs={{0,4},{1,5},{2,6},{3,7},{4,0},{5,1},{6,2},{7,3},{8,12},{9,13},{10,... | collective-permute-start | bytes 196616 | tf_op jit(solution)/shard_map/ppermute | solution.py:56
  (60 shorter events, 13.8 us)
Async XLA Ops:
  2.5 6.3 %collective-permute-start = (bf16[272,256]{1,0:T(8,128)(2,1)}, bf16[272,256]{1,0:T(8,128)(2,1)S(1)}, u32[]{:S(2)}, u32[]{:S(2)}) collective-permute-start(bf16[272,256]{1,0:T(8,128)(2,1)} %get-tuple-element.23), channel_id=1, source_target_pairs={{0,1},{1,0},{2,3},{3,2},{4,5},{5,4},{6,7},{7,6},{8,9},{9,8},{10,11... | collective-permute-start | bytes 417800 | tf_op jit(solution)/shard_map/ppermute | solution.py:56
  3.8 5.0 %collective-permute-start.2 = (bf16[272,256]{1,0:T(8,128)(2,1)}, bf16[272,256]{1,0:T(8,128)(2,1)S(1)}, u32[]{:S(2)}, u32[]{:S(2)}) collective-permute-start(bf16[272,256]{1,0:T(8,128)(2,1)} %get-tuple-element.26.to_y), channel_id=1, source_target_pairs={{0,2},{1,3},{2,0},{3,1},{4,6},{5,7},{6,4},{7,5},{8,10},{9,11},{10,... | collective-permute-start | bytes 417800 | tf_op jit(solution)/shard_map/ppermute | solution.py:56
  10.7 6.5 %collective-permute-start.3 = (bf16[272,384]{1,0:T(8,128)(2,1)S(1)}, bf16[272,384]{1,0:T(8,128)(2,1)S(1)}, u32[]{:S(2)}, u32[]{:S(2)}) collective-permute-start(bf16[272,384]{1,0:T(8,128)(2,1)S(1)} %get-tuple-element.27), channel_id=1, source_target_pairs={{0,4},{1,5},{2,6},{3,7},{4,0},{5,1},{6,2},{7,3},{8,12},{9,13},{10,... | collective-permute-start | bytes 626696 | tf_op jit(solution)/shard_map/ppermute | solution.py:56
  17.2 20.1 %collective-permute-start.8 = (bf16[128,2048]{1,0:T(8,128)(2,1)}, bf16[128,2048]{1,0:T(8,128)(2,1)S(1)}, u32[]{:S(2)}, u32[]{:S(2)}) collective-permute-start(bf16[128,2048]{1,0:T(8,128)(2,1)} %shard_map.65.refs_0_), channel_id=1, source_target_pairs={{0,4},{1,5},{2,6},{3,7},{4,0},{5,1},{6,2},{7,3},{8,12},{9,13},{10,... | collective-permute-start | bytes 1572872 | tf_op jit(solution)/shard_map/ppermute | solution.py:56
  17.3 20.0 %collective-permute-start.5 = (bf16[128,2048]{1,0:T(8,128)(2,1)}, bf16[128,2048]{1,0:T(8,128)(2,1)S(1)}, u32[]{:S(2)}, u32[]{:S(2)}) collective-permute-start(bf16[128,2048]{1,0:T(8,128)(2,1)} %shard_map.65.refs_0_), channel_id=1, source_target_pairs={{0,2},{1,3},{2,0},{3,1},{4,6},{5,7},{6,4},{7,5},{8,10},{9,11},{10,... | collective-permute-start | bytes 1572872 | tf_op jit(solution)/shard_map/ppermute | solution.py:56
  17.9 16.3 %collective-permute-start.7 = (bf16[512,384]{1,0:T(8,128)(2,1)S(1)}, bf16[512,384]{1,0:T(8,128)(2,1)S(1)}, u32[]{:S(2)}, u32[]{:S(2)}) collective-permute-start(bf16[512,384]{1,0:T(8,128)(2,1)S(1)} %pad_maximum_fusion.refs_4_.refs_12_), channel_id=1, source_target_pairs={{0,8},{1,9},{2,10},{3,11},{4,12},{5,13},{6,14},{7,15},{8,0},{9,1},... | collective-permute-start | bytes 1179656 | tf_op jit(solution)/shard_map/ppermute | solution.py:56
  18.1 19.3 %collective-permute-start.6 = (bf16[512,384]{1,0:T(8,128)(2,1)S(1)}, bf16[512,384]{1,0:T(8,128)(2,1)S(1)}, u32[]{:S(2)}, u32[]{:S(2)}) collective-permute-start(bf16[512,384]{1,0:T(8,128)(2,1)S(1)} %pad_maximum_fusion.refs_4_.refs_12_), channel_id=1, source_target_pairs={{0,16},{1,17},{2,18},{3,19},{4,20},{5,21},{6,22},{7,23},{8,24},{9,... | collective-permute-start | bytes 1179656 | tf_op jit(solution)/shard_map/ppermute | solution.py:56
  20.4 17.3 %collective-permute-start.4 = (bf16[128,2048]{1,0:T(8,128)(2,1)}, bf16[128,2048]{1,0:T(8,128)(2,1)S(1)}, u32[]{:S(2)}, u32[]{:S(2)}) collective-permute-start(bf16[128,2048]{1,0:T(8,128)(2,1)} %shard_map.65.refs_0_), channel_id=1, source_target_pairs={{0,1},{1,0},{2,3},{3,2},{4,5},{5,4},{6,7},{7,6},{8,9},{9,8},{10,11... | collective-permute-start | bytes 1572872 | tf_op jit(solution)/shard_map/ppermute | solution.py:56
  37.4 6.2 %collective-permute-start.14 = (bf16[128,1024]{1,0:T(8,128)(2,1)S(1)}, bf16[128,1024]{1,0:T(8,128)(2,1)S(1)}, u32[]{:S(2)}, u32[]{:S(2)}) collective-permute-start(bf16[128,1024]{1,0:T(8,128)(2,1)S(1)} %get-tuple-element.41), channel_id=1, source_target_pairs={{0,1},{1,0},{2,3},{3,2},{4,5},{5,4},{6,7},{7,6},{8,9},{9,8},{10,11... | collective-permute-start | bytes 786440 | tf_op jit(solution)/shard_map/ppermute | solution.py:56
  37.8 8.4 %collective-permute-start.13 = (bf16[128,1024]{1,0:T(8,128)(2,1)S(1)}, bf16[128,1024]{1,0:T(8,128)(2,1)S(1)}, u32[]{:S(2)}, u32[]{:S(2)}) collective-permute-start(bf16[128,1024]{1,0:T(8,128)(2,1)S(1)} %get-tuple-element.44), channel_id=1, source_target_pairs={{0,2},{1,3},{2,0},{3,1},{4,6},{5,7},{6,4},{7,5},{8,10},{9,11},{10,... | collective-permute-start | bytes 786440 | tf_op jit(solution)/shard_map/ppermute | solution.py:56
  38.9 7.7 %collective-permute-start.11 = (bf16[128,1024]{1,0:T(8,128)(2,1)S(1)}, bf16[128,1024]{1,0:T(8,128)(2,1)S(1)}, u32[]{:S(2)}, u32[]{:S(2)}) collective-permute-start(bf16[128,1024]{1,0:T(8,128)(2,1)S(1)} %get-tuple-element.42), channel_id=1, source_target_pairs={{0,4},{1,5},{2,6},{3,7},{4,0},{5,1},{6,2},{7,3},{8,12},{9,13},{10,... | collective-permute-start | bytes 786440 | tf_op jit(solution)/shard_map/ppermute | solution.py:56
  41.1 5.6 %collective-permute-start.12 = (bf16[128,1024]{1,0:T(8,128)(2,1)S(1)}, bf16[128,1024]{1,0:T(8,128)(2,1)S(1)}, u32[]{:S(2)}, u32[]{:S(2)}) collective-permute-start(bf16[128,1024]{1,0:T(8,128)(2,1)S(1)} %get-tuple-element.41), channel_id=1, source_target_pairs={{0,4},{1,5},{2,6},{3,7},{4,0},{5,1},{6,2},{7,3},{8,12},{9,13},{10,... | collective-permute-start | bytes 786440 | tf_op jit(solution)/shard_map/ppermute | solution.py:56
  41.1 10.2 %collective-permute-start.17 = (bf16[512,384]{1,0:T(8,128)(2,1)S(1)}, bf16[512,384]{1,0:T(8,128)(2,1)S(1)}, u32[]{:S(2)}, u32[]{:S(2)}) collective-permute-start(bf16[512,384]{1,0:T(8,128)(2,1)S(1)} %collective-permute-done.6.refs_5_.refs_13_), channel_id=1, source_target_pairs={{0,8},{1,9},{2,10},{3,11},{4,12},{5,13},{6,14},{7,15},{8,0},{9,1},... | collective-permute-start | bytes 1179656 | tf_op jit(solution)/shard_map/ppermute | solution.py:56
  43.6 4.1 %collective-permute-start.9 = (bf16[128,1024]{1,0:T(8,128)(2,1)S(1)}, bf16[128,1024]{1,0:T(8,128)(2,1)S(1)}, u32[]{:S(2)}, u32[]{:S(2)}) collective-permute-start(bf16[128,1024]{1,0:T(8,128)(2,1)S(1)} %get-tuple-element.44), channel_id=1, source_target_pairs={{0,4},{1,5},{2,6},{3,7},{4,0},{5,1},{6,2},{7,3},{8,12},{9,13},{10,... | collective-permute-start | bytes 786440 | tf_op jit(solution)/shard_map/ppermute | solution.py:56
  46.6 4.7 %collective-permute-start.15 = (bf16[128,1024]{1,0:T(8,128)(2,1)S(1)}, bf16[128,1024]{1,0:T(8,128)(2,1)S(1)}, u32[]{:S(2)}, u32[]{:S(2)}) collective-permute-start(bf16[128,1024]{1,0:T(8,128)(2,1)S(1)} %collective-permute-done.13.refs_8_), channel_id=1, source_target_pairs={{0,4},{1,5},{2,6},{3,7},{4,0},{5,1},{6,2},{7,3},{8,12},{9,13},{10,... | collective-permute-start | bytes 786440 | tf_op jit(solution)/shard_map/ppermute | solution.py:56
  46.7 4.6 %collective-permute-start.16 = (bf16[128,1024]{1,0:T(8,128)(2,1)S(1)}, bf16[128,1024]{1,0:T(8,128)(2,1)S(1)}, u32[]{:S(2)}, u32[]{:S(2)}) collective-permute-start(bf16[128,1024]{1,0:T(8,128)(2,1)S(1)} %collective-permute-done.14.refs_9_), channel_id=1, source_target_pairs={{0,4},{1,5},{2,6},{3,7},{4,0},{5,1},{6,2},{7,3},{8,12},{9,13},{10,... | collective-permute-start | bytes 786440 | tf_op jit(solution)/shard_map/ppermute | solution.py:56
  53.0 10.6 %collective-permute-start.19 = (bf16[4,256,128]{2,1,0:T(8,128)(2,1)S(1)}, bf16[4,256,128]{2,1,0:T(8,128)(2,1)S(1)}, u32[]{:S(2)}, u32[]{:S(2)}) collective-permute-start(bf16[4,256,128]{2,1,0:T(8,128)(2,1)S(1)} %get-tuple-element.38.own), channel_id=1, source_target_pairs={{8,0},{9,1},{10,2},{11,3},{12,4},{13,5},{14,6},{15,7},{16,8},{17,9... | collective-permute-start | bytes 786440 | tf_op jit(solution)/shard_map/ppermute | solution.py:56
  56.2 8.1 %collective-permute-start.18 = (bf16[4,256,128]{2,1,0:T(8,128)(2,1)S(1)}, bf16[4,256,128]{2,1,0:T(8,128)(2,1)S(1)}, u32[]{:S(2)}, u32[]{:S(2)}) collective-permute-start(bf16[4,256,128]{2,1,0:T(8,128)(2,1)S(1)} %get-tuple-element.38.own), channel_id=1, source_target_pairs={{0,8},{1,9},{2,10},{3,11},{4,12},{5,13},{6,14},{7,15},{8,16},{9,17... | collective-permute-start | bytes 786440 | tf_op jit(solution)/shard_map/ppermute | solution.py:56
  58.3 8.4 %collective-permute-start.21 = (bf16[4,256,128]{2,1,0:T(8,128)(2,1)S(1)}, bf16[4,256,128]{2,1,0:T(8,128)(2,1)S(1)}, u32[]{:S(2)}, u32[]{:S(2)}) collective-permute-start(bf16[4,256,128]{2,1,0:T(8,128)(2,1)S(1)} %get-tuple-element.40.own), channel_id=1, source_target_pairs={{8,0},{9,1},{10,2},{11,3},{12,4},{13,5},{14,6},{15,7},{16,8},{17,9... | collective-permute-start | bytes 786440 | tf_op jit(solution)/shard_map/ppermute | solution.py:56
  61.5 8.1 %collective-permute-start.20 = (bf16[4,256,128]{2,1,0:T(8,128)(2,1)S(1)}, bf16[4,256,128]{2,1,0:T(8,128)(2,1)S(1)}, u32[]{:S(2)}, u32[]{:S(2)}) collective-permute-start(bf16[4,256,128]{2,1,0:T(8,128)(2,1)S(1)} %get-tuple-element.40.own), channel_id=1, source_target_pairs={{0,8},{1,9},{2,10},{3,11},{4,12},{5,13},{6,14},{7,15},{8,16},{9,17... | collective-permute-start | bytes 786440 | tf_op jit(solution)/shard_map/ppermute | solution.py:56
  69.9 7.3 %collective-permute-start.23 = (bf16[256,128]{1,0:T(8,128)(2,1)S(1)}, bf16[256,128]{1,0:T(8,128)(2,1)S(1)}, u32[]{:S(2)}, u32[]{:S(2)}) collective-permute-start(bf16[256,128]{1,0:T(8,128)(2,1)S(1)} %shard_map.71), channel_id=1, source_target_pairs={{0,1},{1,0},{2,3},{3,2},{4,5},{5,4},{6,7},{7,6},{8,9},{9,8},{10,11... | collective-permute-start | bytes 196616 | tf_op jit(solution)/shard_map/ppermute | solution.py:56
  71.4 6.1 %collective-permute-start.25 = (bf16[256,128]{1,0:T(8,128)(2,1)S(1)}, bf16[256,128]{1,0:T(8,128)(2,1)S(1)}, u32[]{:S(2)}, u32[]{:S(2)}) collective-permute-start(bf16[256,128]{1,0:T(8,128)(2,1)S(1)} %shard_map.72), channel_id=1, source_target_pairs={{0,2},{1,3},{2,0},{3,1},{4,6},{5,7},{6,4},{7,5},{8,10},{9,11},{10,... | collective-permute-start | bytes 196616 | tf_op jit(solution)/shard_map/ppermute | solution.py:56
  72.1 6.7 %collective-permute-start.27 = (bf16[256,128]{1,0:T(8,128)(2,1)S(1)}, bf16[256,128]{1,0:T(8,128)(2,1)S(1)}, u32[]{:S(2)}, u32[]{:S(2)}) collective-permute-start(bf16[256,128]{1,0:T(8,128)(2,1)S(1)} %shard_map.73), channel_id=1, source_target_pairs={{0,3},{1,2},{2,1},{3,0},{4,7},{5,6},{6,5},{7,4},{8,11},{9,10},{10,... | collective-permute-start | bytes 196616 | tf_op jit(solution)/shard_map/ppermute | solution.py:56
  73.5 7.3 %collective-permute-start.22 = (bf16[256,128]{1,0:T(8,128)(2,1)S(1)}, bf16[256,128]{1,0:T(8,128)(2,1)S(1)}, u32[]{:S(2)}, u32[]{:S(2)}) collective-permute-start(bf16[256,128]{1,0:T(8,128)(2,1)S(1)} %shard_map.70.refs_0_), channel_id=1, source_target_pairs={{0,4},{1,5},{2,6},{3,7},{4,0},{5,1},{6,2},{7,3},{8,12},{9,13},{10,... | collective-permute-start | bytes 196616 | tf_op jit(solution)/shard_map/ppermute | solution.py:56
  (10 other events, 50.5 us)

commit v5 on v4

--- a/solution.py
+++ b/solution.py
@@ -42,6 +42,7 @@
 
 
 PAIR = 2 * HD
+V_ORDER = (3, 1, 2, 0)
 EXTRA = 16
 
 
@@ -68,8 +69,8 @@
     return hop(value, lambda z, c, d: (z ^ bits, c, d))
 
 
-def move_z(value, by):
-    return hop(value, lambda z, c, d: (z + by, c, d) if 0 <= z + by < 4 else None)
+def swap_middle(value):
+    return hop(value, lambda z, c, d: (z ^ 3, c, d) if z in (1, 2) else None)
 
 
 def after(value, *others):
@@ -130,40 +131,33 @@
         send_ref[size:, k * HD : (k + 1) * HD] = flags
 
 
-def embed_kernel(from_x, across, gain, raw, stream, conv_w, out_ref, acc, sites, tokens, weights, sems):
+def load_kernel(*refs):
+    count = (len(refs) - 1) // 2
+    copies = [pltpu.make_async_copy(refs[i], refs[count + i], refs[-1].at[i]) for i in range(count)]
+    for copy in copies:
+        copy.start()
+    for copy in copies:
+        copy.wait()
+
+
+def embed_kernel(from_x, across, gain, raw, stream, conv_w, out_ref, acc):
     time_len, site_len, feat_len = raw.shape
     _, _, depth = where_am_i()
     even = (depth & 1) == 0
     rows, width = stream.shape
-    parts = weights.shape[0]
-    step = width // parts
-    first = pltpu.make_async_copy(raw, sites, sems.at[2 * parts])
-    first.start()
-    copies = []
-    for i in range(parts):
-        here = pl.ds(i * step, step)
-        pair = (
-            pltpu.make_async_copy(conv_w.at[:, :, here], weights.at[i], sems.at[2 * i]),
-            pltpu.make_async_copy(stream.at[:, here], tokens.at[i], sems.at[2 * i + 1]),
-        )
-        for copy in pair:
-            copy.start()
-        copies.append(pair)
     side = from_x[from_x.shape[0] - EXTRA :, :HD].astype(jnp.float32)
     far = across[:, :HD].astype(jnp.float32)
     before = jnp.where(even, jnp.where(depth == 2, far, 0.0), side)
     behind = jnp.where(even, side, jnp.where(depth == 1, far, 0.0))
-    first.wait()
-    padded = jnp.concatenate([before[:, None], sites[...].astype(jnp.float32), behind[:, None]], axis=1)
+    padded = jnp.concatenate([before[:, None], raw[...].astype(jnp.float32), behind[:, None]], axis=1)
     windows = [padded[:, j : j + site_len].reshape(rows, feat_len).astype(jnp.bfloat16) for j in range(3)]
     windows = jnp.concatenate(windows, axis=1)
-    total = jnp.zeros((rows, 1), jnp.float32)
-    for i, pair in enumerate(copies):
-        for copy in pair:
-            copy.wait()
-        part = jnp.dot(windows, weights[i].reshape(3 * feat_len, step), preferred_element_type=jnp.float32)
-        part += tokens[i].astype(jnp.float32)
-        acc[:, i * step : (i + 1) * step] = part
+    total, step = jnp.zeros((rows, 1), jnp.float32), width // 4
+    for at in range(0, width, step):
+        here = slice(at, at + step)
+        part = jnp.dot(windows, conv_w[:, here], preferred_element_type=jnp.float32)
+        part += stream[:, here].astype(jnp.float32)
+        acc[:, here] = part
         total += jnp.sum(part * part, axis=1, keepdims=True)
     scale = lax.rsqrt(total / width + 1e-05)
     out_ref[...] = (acc[...] * scale * gain[...]).astype(jnp.bfloat16)
@@ -176,24 +170,25 @@
 
 
 def partial_kernel(*refs):
-    x_refs, (own, far, near, acc_ref) = refs[:4], refs[4:]
+    x_refs, (own, far, near, acc_ref) = refs[:6], refs[6:]
     z, core, _ = where_am_i()
-    w = jnp.concatenate([own[...], far[...], near[...]], axis=0)
+    w = jnp.concatenate([ref[...] for ref in (own, far, near)], axis=0)
     x = [take(x_refs, source, core, own.shape[0]) for source in (z, z ^ 2, z ^ 1)]
     acc_ref[...] = jnp.dot(jnp.concatenate(x, axis=1), w, preferred_element_type=jnp.float32)
 
 
 def project_kernel(*refs):
-    early, late, (own, far, near, last, acc_in, q_ref, k_ref, v_ref, acc_ref, x_all) = refs[:4], refs[4:12], refs[12:]
+    early, late, (own, far, near, last, acc_in) = refs[:6], refs[6:10], refs[10:15]
+    q_ref, k_ref, v_first, v_second, acc_ref, x_all = refs[15:]
     z, core, depth = where_am_i()
-    rows, block, half = last.shape[0], late[0].shape[0], late[0].shape[1]
+    rows, block, half = own.shape[0], late[0].shape[0], late[0].shape[1]
     for i, ref in enumerate(late):
         x_all[(i // 2) * block : (i // 2 + 1) * block, (i % 2) * half : (i % 2 + 1) * half] = ref[...]
-    w = jnp.concatenate([own[...], far[...], near[...], last[...]], axis=0)
+    w = jnp.concatenate([ref[...] for ref in (own, far, near, last)], axis=0)
     x = [take([x_all], source, core, rows) for source in (z, z ^ 2, z ^ 1, z ^ 3)]
-    acc_ref[4 * block :] = jnp.dot(jnp.concatenate(x, axis=1), w, preferred_element_type=jnp.float32)
+    acc_ref[6 * block :] = jnp.dot(jnp.concatenate(x, axis=1), w, preferred_element_type=jnp.float32)
     x = take(early, z ^ 3, core, rows)
-    acc_ref[: 4 * block] = acc_in[...] + jnp.dot(x, last[...], preferred_element_type=jnp.float32)
+    acc_ref[: 6 * block] = acc_in[...] + jnp.dot(x, last[...], preferred_element_type=jnp.float32)
     order = ((0, 1, 2, 6), (3, 4, 5, 7))
     turn = jnp.where(depth == 3, 0, depth)
     for rel in range(2):
@@ -201,31 +196,40 @@
         for r in range(4):
             row = order[rel][r]
             mine = slice(row * block, (row + 1) * block)
-            for third, ref in enumerate((q_ref, k_ref, v_ref)):
+            v_at = V_ORDER.index(r)
+            targets = (q_ref.at[r], k_ref.at[r], (v_first, v_second)[v_at // 2].at[v_at % 2])
+            for third, ref in enumerate(targets):
                 group = third + turn
                 group = jnp.where(group >= 3, group - 3, group)
                 lanes = pl.ds(pl.multiple_of(group * HD, HD), HD)
-                ref[r, at, :] = acc_ref[mine, lanes].astype(jnp.bfloat16)
+                ref[at, :] = acc_ref[mine, lanes].astype(jnp.bfloat16)
 
 
 def spans(u):
     return ((0, u, 2), (1, 0, 2), (2, 0, 1 + u))
 
 
-def weigh_kernel(q_ref, before, own, behind, own_flags, other_flags, out_ref):
+def neighbours(outer, own, middle, index):
+    z, _, _ = where_am_i()
+    odd = (z & 1) == 1
+    outer, middle = outer[index], middle[index]
+    return jnp.where(odd, outer, middle), own[index], jnp.where(odd, middle, outer)
+
+
+def weigh_kernel(q_ref, outer, own, middle, own_flags, other_flags, out_ref):
     _, core, _ = where_am_i()
     block = q_ref.shape[1] // 2
     inv_root = 1.0 / math.sqrt(HD)
     flags = [own_flags[...].astype(jnp.float32), other_flags[...].astype(jnp.float32)]
     flags = [jnp.where(core == u, flags[0], flags[1]) for u in range(2)]
     bias = [(f - 1.0) * 1e30 for f in flags]
-    keys = (before, own, behind)
     for r in range(4):
+        keys = neighbours(outer, own, middle, r)
         for u in range(2):
             q = q_ref[r, u * block : (u + 1) * block]
             scores = []
             for side, first, last in spans(u):
-                k = keys[side][r, first * block : last * block]
+                k = keys[side][first * block : last * block]
                 s = lax.dot_general(q, k, (((1,), (1,)), ((), ())), preferred_element_type=jnp.float32)
                 for v in range(last - first):
                     entry = len(scores)
@@ -239,12 +243,12 @@
                 out_ref[r, u * block : (u + 1) * block, here] = (p * inverse).astype(jnp.bfloat16)
 
 
-def mix_kernel(r, weights, before, own, behind, out_ref):
+def mix_kernel(r, weights, outer, own, middle, out_ref):
     block = weights.shape[1] // 2
-    values = (before, own, behind)
+    values = neighbours(outer, own, middle, V_ORDER.index(r) % 2)
     for u in range(2):
         w = weights[r, u * block : (u + 1) * block]
-        v = [values[side][r, first * block : last * block] for side, first, last in spans(u)]
+        v = [values[side][first * block : last * block] for side, first, last in spans(u)]
         result = jnp.dot(w, jnp.concatenate(v, axis=0), preferred_element_type=jnp.float32)
         out_ref[u * block : (u + 1) * block] = result.astype(jnp.bfloat16)
 
@@ -261,7 +265,7 @@
 
 
 def call(kernel, outs, places, scratch=(), macs=0):
-    spaces = {"s": SMEM, "v": VMEM, "a": pl.ANY}
+    spaces = {"s": SMEM, "v": VMEM, "h": pltpu.HBM}
     return pl.pallas_call(
         kernel,
         out_shape=outs,
@@ -269,7 +273,7 @@
         out_specs=jax.tree.map(lambda _: pl.BlockSpec(memory_space=VMEM), outs),
         scratch_shapes=list(scratch),
         cost_estimate=pl.CostEstimate(flops=2 * macs, bytes_accessed=0, transcendentals=0),
-        compiler_params=pltpu.CompilerParams(vmem_limit_bytes=({2: 60, 3: 58}.get(places.count("a"), 40)) * 2**20),
+        compiler_params=pltpu.CompilerParams(vmem_limit_bytes=32 * 2**20),
     )
 
 
@@ -285,10 +289,15 @@
     to_x, to_y, to_across, kept = call(
         split_kernel,
         (array(size + EXTRA, PAIR), array(size + EXTRA, PAIR), array(EXTRA, PAIR), array(size, PAIR)),
-        "saa",
+        "shh",
         scratch=[VMEM(raw.shape, bf16), pltpu.SemaphoreType.DMA((4,))],
     )(mask.reshape(mask.shape[2]), w_qkv, raw)
     from_x, from_y, across = swap_depth(to_x, 1), swap_depth(to_y, 2), swap_depth(to_across, 3)
+    operands = (after(raw, to_x), stream.reshape(block, width), conv_w.reshape(3 * feat_len, width))
+    operands = call(
+        load_kernel, tuple(array(*t.shape) for t in operands), "hhh", scratch=[pltpu.SemaphoreType.DMA((3,))]
+    )(*operands)
+    kept, *operands = lax.optimization_barrier((kept, *operands))
     keep, send, flags = call(
         sort_kernel, (array(size, 3 * HD), array(size + EXTRA, 3 * HD), array(EXTRA, HD)), "v" * 5
     )(kept, from_x, from_y, across, to_y)
@@ -297,51 +306,43 @@
     shard = jnp.concatenate([keep, received[:size]], axis=0)
     far, near = swap_z(shard, 2), swap_z(shard, 1)
 
-    parts = 4
     normed = call(
         embed_kernel,
         array(block, width),
-        "vvvaaa",
-        scratch=[
-            VMEM((block, width), f32),
-            VMEM(raw.shape, bf16),
-            VMEM((parts, block, width // parts), bf16),
-            VMEM((parts, 3, feat_len, width // parts), bf16),
-            pltpu.SemaphoreType.DMA((2 * parts + 1,)),
-        ],
+        "v" * 6,
+        scratch=[VMEM((block, width), f32)],
         macs=block * 3 * feat_len * width,
-    )(from_x, across, gain.reshape(1, width), raw, stream.reshape(block, width), conv_w)
+    )(from_x, across, gain.reshape(1, width), *operands)
     normed = after(normed, received)
     beside, above = swap_depth(normed, 1), swap_depth(normed, 2)
     opposite = swap_core(normed)
-    far, near, opposite = lax.optimization_barrier((far, near, opposite))
+    far, near, opposite, beside, above = lax.optimization_barrier((far, near, opposite, beside, above))
+    early = (normed, beside, above, opposite, swap_core(beside), swap_core(above))
     last = swap_z(far, 1)
-    halves = [t[:, i * half : (i + 1) * half] for t in (after(beside, far), after(above, far)) for i in range(2)]
-    diagonal = [swap_depth(halves[0], 2), swap_depth(halves[3], 1)]
+    diagonal = [swap_depth(early[1][:, :half], 2), swap_depth(early[2][:, half:], 1)]
     rows = 2 * size
-    early = (normed, beside, above, opposite)
-    total = call(partial_kernel, array(4 * block, 3 * HD, kind=f32), "v" * 7, macs=4 * block * 3 * rows * 3 * HD)(
+    total = call(partial_kernel, array(6 * block, 3 * HD, kind=f32), "v" * 9, macs=6 * block * 3 * rows * 3 * HD)(
         *early, shard, far, near
     )
-    diagonal = [after(t, total) for t in diagonal]
-    late = [swap_core(t) for t in halves] + diagonal + [swap_core(t) for t in diagonal]
-    one_head = array(4, 2 * block, HD)
-    q, k, v = call(
+    last, total, *diagonal = lax.optimization_barrier((last, total, *diagonal))
+    late = diagonal + [swap_core(t) for t in diagonal]
+    one_head, half_head = array(4, 2 * block, HD), array(2, 2 * block, HD)
+    q, k, *v = call(
         project_kernel,
-        (one_head,) * 3,
-        "v" * 17,
-        scratch=[VMEM((8 * block, 3 * HD), f32), VMEM((4 * block, width), bf16)],
-        macs=20 * block * rows * 3 * HD,
+        (one_head, one_head, half_head, half_head),
+        "v" * 15,
+        scratch=[VMEM((8 * block, 3 * HD), f32), VMEM((2 * block, width), bf16)],
+        macs=14 * block * rows * 3 * HD,
     )(*early, *late, shard, far, near, last, total)
 
     weights = call(weigh_kernel, array(4, 2 * block, 5 * block), "v" * 6, macs=8 * block * 5 * block * HD)(
-        q, move_z(k, 1), k, move_z(k, -1), flags, other_flags
-    )
-    values = (move_z(v, 1), v, move_z(v, -1))
+        q, swap_z(k, 1), k, swap_middle(k), flags, other_flags
+    )
+    values = [(swap_z(t, 1), t, swap_middle(t)) for t in v]
     pieces = {}
-    for r in (3, 1, 2, 0):
+    for r in V_ORDER:
         mixed = call(functools.partial(mix_kernel, r), array(2 * block, HD), "vvvv", macs=2 * block * 5 * block * HD)(
-            weights, *values
+            weights, *values[V_ORDER.index(r) // 2]
         )
         pieces[r] = swap_depth(mixed, r) if r else mixed
     both = [t for r in range(4) for t in (pieces[r], swap_core(pieces[r]))]

time: 82.9 us -> 76.8 us (0.926)
  starting transfers between devices: 37.4 us -> 31.5 us
  Pallas kernels: 12.4 us -> 7.16 us
  local copies, waits for them, and re-layouts: 1.95 us -> 5.68 us
    ppermute x29, starting transfers between devices: 37.4 us -> 31.5 us  [hop(): return lax.ppermute(value, ('tm', 'depth'), pairs)]
    unnamed x10 -> x14, local copies, waits for them, and re-layouts: 1.86 us -> 5.62 us
    pallas_call x3 -> x4, Pallas kernels: 6.88 us -> 3.44 us  [the longest x1 1.38 us: plane_device(): call(partial_kernel, array(6 * block, 3 * HD, kind=f32), 'v' * 9, macs=6...]
    pallas_call x1, Pallas kernels: 2.5 us -> 0.7 us  [plane_device(): call(split_kernel, (array(size + EXTRA, PAIR), array(size + EXTRA, PAIR),...]
  transfers between devices with their start and end apart: 29 -> 29, of which waited for: 10 -> 13; matrix products, arithmetic and copies ran while one was open for 0% -> 0% of each run, Pallas kernels for 9% -> 6%
where the time goes in v5:
time: 76.8 us; the launch traced here: 75.7 us
  starting transfers between devices  31.5 us (41%)
  waiting for transfers between devices  31.2 us (41%)
  Pallas kernels  7.16 us (9%)
  local copies, waits for them, and re-layouts  5.68 us (7%)
    ppermute x29, starting transfers between devices, hop(): return lax.ppermute(value, ('tm', 'depth'), pairs)  31.5 us
    ppermute x29, waiting for transfers between devices, hop(): return lax.ppermute(value, ('tm', 'depth'), pairs)  31.2 us
    unnamed x14, local copies, waits for them, and re-layouts  5.62 us
  transfers between devices with their start and end apart: 29, of which 13 were waited for; matrix products, arithmetic and copies ran while one was open for 0% of the time, Pallas kernels for 6%

profile of v5, /device:TPU:9, one launch (start us, length us, event | category | flops | bytes accessed | tf_op | source)
XLA Modules:
  0.0 75.7 jit_solution(10010479096999331397)
XLA Ops:
  0.0 1.0 %copy-done.2 = bf16[256,768]{1,0:T(8,128)(2,1)S(1)} copy-done((bf16[256,768]{1,0:T(8,128)(2,1)S(1)}, bf16[256,768]{1,0:T(8,128)(2,1)}, u32[]{:S(2)}) %copy-start.2) | copy-done | bytes 393240
  3.1 1.3 %collective-permute-start = (bf16[272,256]{1,0:T(8,128)(2,1)S(1)}, bf16[272,256]{1,0:T(8,128)(2,1)S(1)}, u32[]{:S(2)}, u32[]{:S(2)}) collective-permute-start(bf16[272,256]{1,0:T(8,128)(2,1)S(1)} %get-tuple-element.34), channel_id=1, source_target_pairs={{0,1},{1,0},{2,3},{3,2},{4,5},{5,4},{6,7},{7,6},{8,9},{9,8},{10,11... | collective-permute-start | bytes 417800 | tf_op jit(solution)/shard_map/ppermute | solution.py:57
  4.4 1.2 %collective-permute-start.2 = (bf16[272,256]{1,0:T(8,128)(2,1)S(1)}, bf16[272,256]{1,0:T(8,128)(2,1)S(1)}, u32[]{:S(2)}, u32[]{:S(2)}) collective-permute-start(bf16[272,256]{1,0:T(8,128)(2,1)S(1)} %get-tuple-element.45.to_y), channel_id=1, source_target_pairs={{0,2},{1,3},{2,0},{3,1},{4,6},{5,7},{6,4},{7,5},{8,10},{9,11},{10,... | collective-permute-start | bytes 417800 | tf_op jit(solution)/shard_map/ppermute | solution.py:57
  5.8 1.4 %copy-done = bf16[3,128,2048]{2,1,0:T(8,128)(2,1)S(1)} copy-done((bf16[3,128,2048]{2,1,0:T(8,128)(2,1)S(1)}, bf16[3,128,2048]{2,1,0:T(8,128)(2,1)}, u32[]{:S(2)}) %copy-start) | copy-done | bytes 1572888
  7.2 1.0 %copy-done.1 = bf16[16,8,2048]{2,1,0:T(8,128)(2,1)S(1)} copy-done((bf16[16,8,2048]{2,1,0:T(8,128)(2,1)S(1)}, bf16[16,8,2048]{2,1,0:T(8,128)(2,1)}, u32[]{:S(2)}) %copy-start.1) | copy-done | bytes 524312
  9.4 2.2 %collective-permute-start.3 = (bf16[272,384]{1,0:T(8,128)(2,1)S(1)}, bf16[272,384]{1,0:T(8,128)(2,1)S(1)}, u32[]{:S(2)}, u32[]{:S(2)}) collective-permute-start(bf16[272,384]{1,0:T(8,128)(2,1)S(1)} %get-tuple-element.46), channel_id=1, source_target_pairs={{0,4},{1,5},{2,6},{3,7},{4,0},{5,1},{6,2},{7,3},{8,12},{9,13},{10,... | collective-permute-start | bytes 626696 | tf_op jit(solution)/shard_map/ppermute | solution.py:57
  13.3 1.2 %collective-permute-start.7 = (bf16[128,2048]{1,0:T(8,128)(2,1)S(1)}, bf16[128,2048]{1,0:T(8,128)(2,1)S(1)}, u32[]{:S(2)}, u32[]{:S(2)}) collective-permute-start(bf16[128,2048]{1,0:T(8,128)(2,1)S(1)} %shard_map.66.refs_0_), channel_id=1, source_target_pairs={{0,1},{1,0},{2,3},{3,2},{4,5},{5,4},{6,7},{7,6},{8,9},{9,8},{10,11... | collective-permute-start | bytes 1572872 | tf_op jit(solution)/shard_map/ppermute | solution.py:57
  15.7 2.3 %collective-permute-start.4 = (bf16[512,384]{1,0:T(8,128)(2,1)S(1)}, bf16[512,384]{1,0:T(8,128)(2,1)S(1)}, u32[]{:S(2)}, u32[]{:S(2)}) collective-permute-start(bf16[512,384]{1,0:T(8,128)(2,1)S(1)} %pad_maximum_fusion.refs_6_.refs_10_), channel_id=1, source_target_pairs={{0,16},{1,17},{2,18},{3,19},{4,20},{5,21},{6,22},{7,23},{8,24},{9,... | collective-permute-start | bytes 1179656 | tf_op jit(solution)/shard_map/ppermute | solution.py:57
  18.0 14.5 %collective-permute-done.5.refs_8_.refs_12_ = bf16[512,384]{1,0:T(8,128)(2,1)S(1)} collective-permute-done((bf16[512,384]{1,0:T(8,128)(2,1)S(1)}, bf16[512,384]{1,0:T(8,128)(2,1)S(1)}, u32[]{:S(2)}, u32[]{:S(2)}) %collective-permute-start.5) | collective-permute-done | bytes 393248 | tf_op jit(solution)/shard_map/ppermute | solution.py:57
  32.6 3.2 %collective-permute-done.4.refs_7_.refs_11_ = bf16[512,384]{1,0:T(8,128)(2,1)S(1)} collective-permute-done((bf16[512,384]{1,0:T(8,128)(2,1)S(1)}, bf16[512,384]{1,0:T(8,128)(2,1)S(1)}, u32[]{:S(2)}, u32[]{:S(2)}) %collective-permute-start.4) | collective-permute-done | bytes 393248 | tf_op jit(solution)/shard_map/ppermute | solution.py:57
  36.8 1.3 %collective-permute-start.11 = (bf16[512,384]{1,0:T(8,128)(2,1)S(1)}, bf16[512,384]{1,0:T(8,128)(2,1)S(1)}, u32[]{:S(2)}, u32[]{:S(2)}) collective-permute-start(bf16[512,384]{1,0:T(8,128)(2,1)S(1)} %collective-permute-done.4.refs_7_.refs_11_), channel_id=1, source_target_pairs={{0,8},{1,9},{2,10},{3,11},{4,12},{5,13},{6,14},{7,15},{8,0},{9,1},... | collective-permute-start | bytes 1179656 | tf_op jit(solution)/shard_map/ppermute | solution.py:57
  39.3 1.4 %shard_map.68.refs_14_ = f32[768,384]{1,0:T(8,128)S(1)} custom-call(bf16[128,2048]{1,0:T(8,128)(2,1)S(1)} %shard_map.66.refs_0_, bf16[128,2048]{1,0:T(8,128)(2,1)S(1)} %collective-permute-done.7.refs_1_, bf16[128,2048]{1,0:T(8,128)(2,1)S(1)} %collective-permute-done.8.refs_2_, bf16[128,2048]{1,0:T(8,128)(2,1)S(1)} %collective-permute-done.6.refs_3_, ...), custom_call_target="tpu_custom_call" | custom-call | flops 905969664 | tf_op jit(solution)/shard_map/pallas_call | solution.py:324
  40.7 4.6 %collective-permute-done.13.refs_7_ = bf16[128,1024]{1,0:T(8,128)(2,1)S(1)} collective-permute-done((bf16[128,1024]{1,0:T(8,128)(2,1)S(1)}, bf16[128,1024]{1,0:T(8,128)(2,1)S(1)}, u32[]{:S(2)}, u32[]{:S(2)}) %collective-permute-start.13) | collective-permute-done | bytes 262176 | tf_op jit(solution)/shard_map/ppermute | solution.py:57
  45.3 1.7 %collective-permute-done.11.refs_13_ = bf16[512,384]{1,0:T(8,128)(2,1)S(1)} collective-permute-done((bf16[512,384]{1,0:T(8,128)(2,1)S(1)}, bf16[512,384]{1,0:T(8,128)(2,1)S(1)}, u32[]{:S(2)}, u32[]{:S(2)}) %collective-permute-start.11) | collective-permute-done | bytes 393248 | tf_op jit(solution)/shard_map/ppermute | solution.py:57
  47.0 1.3 %collective-permute-start.14 = (bf16[128,1024]{1,0:T(8,128)(2,1)S(1)}, bf16[128,1024]{1,0:T(8,128)(2,1)S(1)}, u32[]{:S(2)}, u32[]{:S(2)}) collective-permute-start(bf16[128,1024]{1,0:T(8,128)(2,1)S(1)} %collective-permute-done.12.refs_6_), channel_id=1, source_target_pairs={{0,4},{1,5},{2,6},{3,7},{4,0},{5,1},{6,2},{7,3},{8,12},{9,13},{10,... | collective-permute-start | bytes 786440 | tf_op jit(solution)/shard_map/ppermute | solution.py:57
  48.3 1.2 %collective-permute-done.14.refs_8_ = bf16[128,1024]{1,0:T(8,128)(2,1)S(1)} collective-permute-done((bf16[128,1024]{1,0:T(8,128)(2,1)S(1)}, bf16[128,1024]{1,0:T(8,128)(2,1)S(1)}, u32[]{:S(2)}, u32[]{:S(2)}) %collective-permute-start.14) | collective-permute-done | bytes 262176 | tf_op jit(solution)/shard_map/ppermute | solution.py:57
  49.8 1.3 %shard_map.69 = (bf16[4,256,128]{2,1,0:T(8,128)(2,1)S(1)}, bf16[4,256,128]{2,1,0:T(8,128)(2,1)S(1)}, bf16[2,256,128]{2,1,0:T(8,128)(2,1)S(1)}, bf16[2,256,128]{2,1,0:T(8,128)(2,1)S(1)}) custom-call(bf16[128,2048]{1,0:T(8,128)(2,1)S(1)} %shard_map.66.refs_0_, bf16[128,2048]{1,0:T(8,128)(2,1)S(1)} %collective-permute-done.7.refs_1_, ...), custom_call_target="tpu_custom_call" | custom-call | flops 704643072 | tf_op jit(solution)/shard_map/pallas_call | solution.py:330
  51.1 3.0 %collective-permute-start.17 = (bf16[4,256,128]{2,1,0:T(8,128)(2,1)S(1)}, bf16[4,256,128]{2,1,0:T(8,128)(2,1)S(1)}, u32[]{:S(2)}, u32[]{:S(2)}) collective-permute-start(bf16[4,256,128]{2,1,0:T(8,128)(2,1)S(1)} %get-tuple-element.59.own), channel_id=1, source_target_pairs={{8,16},{9,17},{10,18},{11,19},{12,20},{13,21},{14,22},{15,23},{16,... | collective-permute-start | bytes 786440 | tf_op jit(solution)/shard_map/ppermute | solution.py:57
  54.2 2.2 %collective-permute-start.22 = (bf16[2,256,128]{2,1,0:T(8,128)(2,1)S(1)}, bf16[2,256,128]{2,1,0:T(8,128)(2,1)S(1)}, u32[]{:S(2)}, u32[]{:S(2)}) collective-permute-start(bf16[2,256,128]{2,1,0:T(8,128)(2,1)S(1)} %get-tuple-element.62.own), channel_id=1, source_target_pairs={{8,16},{9,17},{10,18},{11,19},{12,20},{13,21},{14,22},{15,23},{16,... | collective-permute-start | bytes 393224 | tf_op jit(solution)/shard_map/ppermute | solution.py:57
  56.6 3.0 %collective-permute-start.19 = (bf16[2,256,128]{2,1,0:T(8,128)(2,1)S(1)}, bf16[2,256,128]{2,1,0:T(8,128)(2,1)S(1)}, u32[]{:S(2)}, u32[]{:S(2)}) collective-permute-start(bf16[2,256,128]{2,1,0:T(8,128)(2,1)S(1)} %get-tuple-element.61.own), channel_id=1, source_target_pairs={{8,16},{9,17},{10,18},{11,19},{12,20},{13,21},{14,22},{15,23},{16,... | collective-permute-start | bytes 393224 | tf_op jit(solution)/shard_map/ppermute | solution.py:57
  61.4 1.2 %shard_map.70.weights = bf16[4,256,640]{2,1,0:T(8,128)(2,1)S(1)} custom-call(bf16[4,256,128]{2,1,0:T(8,128)(2,1)S(1)} %get-tuple-element.58.q_ref, bf16[4,256,128]{2,1,0:T(8,128)(2,1)S(1)} %collective-permute-done.16.outer, bf16[4,256,128]{2,1,0:T(8,128)(2,1)S(1)} %get-tuple-element.59.own, bf16[4,256,128]{2,1,0:T(8,128)(2,1)S(1)} %collective-permute-done.17.middle, ...), custom_call_target="tpu_custom_call" | custom-call | flops 167772160 | tf_op jit(solution)/shard_map/pallas_call | solution.py:338
  65.1 1.2 %collective-permute-start.27 = (bf16[256,128]{1,0:T(8,128)(2,1)S(1)}, bf16[256,128]{1,0:T(8,128)(2,1)S(1)}, u32[]{:S(2)}, u32[]{:S(2)}) collective-permute-start(bf16[256,128]{1,0:T(8,128)(2,1)S(1)} %shard_map.74), channel_id=1, source_target_pairs={{0,3},{1,2},{2,1},{3,0},{4,7},{5,6},{6,5},{7,4},{8,11},{9,10},{10,... | collective-permute-start | bytes 196616 | tf_op jit(solution)/shard_map/ppermute | solution.py:57
  68.1 3.5 %collective-permute-start.20 = (bf16[256,128]{1,0:T(8,128)(2,1)S(1)}, bf16[256,128]{1,0:T(8,128)(2,1)S(1)}, u32[]{:S(2)}, u32[]{:S(2)}) collective-permute-start(bf16[256,128]{1,0:T(8,128)(2,1)S(1)} %shard_map.71.refs_0_), channel_id=1, source_target_pairs={{0,4},{1,5},{2,6},{3,7},{4,0},{5,1},{6,2},{7,3},{8,12},{9,13},{10,... | collective-permute-start | bytes 196616 | tf_op jit(solution)/shard_map/ppermute | solution.py:57
  71.7 1.5 %collective-permute-start.28 = (bf16[256,128]{1,0:T(8,128)(2,1)S(1)}, bf16[256,128]{1,0:T(8,128)(2,1)S(1)}, u32[]{:S(2)}, u32[]{:S(2)}) collective-permute-start(bf16[256,128]{1,0:T(8,128)(2,1)S(1)} %collective-permute-done.27.refs_6_), channel_id=1, source_target_pairs={{0,4},{1,5},{2,6},{3,7},{4,0},{5,1},{6,2},{7,3},{8,12},{9,13},{10,... | collective-permute-start | bytes 196616 | tf_op jit(solution)/shard_map/ppermute | solution.py:57
  (65 shorter events, 17.7 us)
Async XLA Ops:
  3.1 6.1 %collective-permute-start = (bf16[272,256]{1,0:T(8,128)(2,1)S(1)}, bf16[272,256]{1,0:T(8,128)(2,1)S(1)}, u32[]{:S(2)}, u32[]{:S(2)}) collective-permute-start(bf16[272,256]{1,0:T(8,128)(2,1)S(1)} %get-tuple-element.34), channel_id=1, source_target_pairs={{0,1},{1,0},{2,3},{3,2},{4,5},{5,4},{6,7},{7,6},{8,9},{9,8},{10,11... | collective-permute-start | bytes 417800 | tf_op jit(solution)/shard_map/ppermute | solution.py:57
  4.4 4.9 %collective-permute-start.2 = (bf16[272,256]{1,0:T(8,128)(2,1)S(1)}, bf16[272,256]{1,0:T(8,128)(2,1)S(1)}, u32[]{:S(2)}, u32[]{:S(2)}) collective-permute-start(bf16[272,256]{1,0:T(8,128)(2,1)S(1)} %get-tuple-element.45.to_y), channel_id=1, source_target_pairs={{0,2},{1,3},{2,0},{3,1},{4,6},{5,7},{6,4},{7,5},{8,10},{9,11},{10,... | collective-permute-start | bytes 417800 | tf_op jit(solution)/shard_map/ppermute | solution.py:57
  5.6 3.6 %collective-permute-start.1 = (bf16[16,256]{1,0:T(8,128)(2,1)S(1)}, bf16[16,256]{1,0:T(8,128)(2,1)S(1)}, u32[]{:S(2)}, u32[]{:S(2)}) collective-permute-start(bf16[16,256]{1,0:T(8,128)(2,1)S(1)} %get-tuple-element.35), channel_id=1, source_target_pairs={{0,3},{1,2},{2,1},{3,0},{4,7},{5,6},{6,5},{7,4},{8,11},{9,10},{10,... | collective-permute-start | bytes 24584 | tf_op jit(solution)/shard_map/ppermute | solution.py:57
  9.4 3.3 %collective-permute-start.3 = (bf16[272,384]{1,0:T(8,128)(2,1)S(1)}, bf16[272,384]{1,0:T(8,128)(2,1)S(1)}, u32[]{:S(2)}, u32[]{:S(2)}) collective-permute-start(bf16[272,384]{1,0:T(8,128)(2,1)S(1)} %get-tuple-element.46), channel_id=1, source_target_pairs={{0,4},{1,5},{2,6},{3,7},{4,0},{5,1},{6,2},{7,3},{8,12},{9,13},{10,... | collective-permute-start | bytes 626696 | tf_op jit(solution)/shard_map/ppermute | solution.py:57
  12.7 23.1 %collective-permute-start.8 = (bf16[128,2048]{1,0:T(8,128)(2,1)S(1)}, bf16[128,2048]{1,0:T(8,128)(2,1)S(1)}, u32[]{:S(2)}, u32[]{:S(2)}) collective-permute-start(bf16[128,2048]{1,0:T(8,128)(2,1)S(1)} %shard_map.66.refs_0_), channel_id=1, source_target_pairs={{0,2},{1,3},{2,0},{3,1},{4,6},{5,7},{6,4},{7,5},{8,10},{9,11},{10,... | collective-permute-start | bytes 1572872 | tf_op jit(solution)/shard_map/ppermute | solution.py:57
  13.3 22.5 %collective-permute-start.7 = (bf16[128,2048]{1,0:T(8,128)(2,1)S(1)}, bf16[128,2048]{1,0:T(8,128)(2,1)S(1)}, u32[]{:S(2)}, u32[]{:S(2)}) collective-permute-start(bf16[128,2048]{1,0:T(8,128)(2,1)S(1)} %shard_map.66.refs_0_), channel_id=1, source_target_pairs={{0,1},{1,0},{2,3},{3,2},{4,5},{5,4},{6,7},{7,6},{8,9},{9,8},{10,11... | collective-permute-start | bytes 1572872 | tf_op jit(solution)/shard_map/ppermute | solution.py:57
  14.5 21.3 %collective-permute-start.6 = (bf16[128,2048]{1,0:T(8,128)(2,1)S(1)}, bf16[128,2048]{1,0:T(8,128)(2,1)S(1)}, u32[]{:S(2)}, u32[]{:S(2)}) collective-permute-start(bf16[128,2048]{1,0:T(8,128)(2,1)S(1)} %shard_map.66.refs_0_), channel_id=1, source_target_pairs={{0,4},{1,5},{2,6},{3,7},{4,0},{5,1},{6,2},{7,3},{8,12},{9,13},{10,... | collective-permute-start | bytes 1572872 | tf_op jit(solution)/shard_map/ppermute | solution.py:57
  15.5 17.1 %collective-permute-start.5 = (bf16[512,384]{1,0:T(8,128)(2,1)S(1)}, bf16[512,384]{1,0:T(8,128)(2,1)S(1)}, u32[]{:S(2)}, u32[]{:S(2)}) collective-permute-start(bf16[512,384]{1,0:T(8,128)(2,1)S(1)} %pad_maximum_fusion.refs_6_.refs_10_), channel_id=1, source_target_pairs={{0,8},{1,9},{2,10},{3,11},{4,12},{5,13},{6,14},{7,15},{8,0},{9,1},... | collective-permute-start | bytes 1179656 | tf_op jit(solution)/shard_map/ppermute | solution.py:57
  15.7 20.1 %collective-permute-start.4 = (bf16[512,384]{1,0:T(8,128)(2,1)S(1)}, bf16[512,384]{1,0:T(8,128)(2,1)S(1)}, u32[]{:S(2)}, u32[]{:S(2)}) collective-permute-start(bf16[512,384]{1,0:T(8,128)(2,1)S(1)} %pad_maximum_fusion.refs_6_.refs_10_), channel_id=1, source_target_pairs={{0,16},{1,17},{2,18},{3,19},{4,20},{5,21},{6,22},{7,23},{8,24},{9,... | collective-permute-start | bytes 1179656 | tf_op jit(solution)/shard_map/ppermute | solution.py:57
  35.8 3.5 %collective-permute-start.9 = (bf16[128,2048]{1,0:T(8,128)(2,1)S(1)}, bf16[128,2048]{1,0:T(8,128)(2,1)S(1)}, u32[]{:S(2)}, u32[]{:S(2)}) collective-permute-start(bf16[128,2048]{1,0:T(8,128)(2,1)S(1)} %collective-permute-done.7.refs_1_), channel_id=1, source_target_pairs={{0,4},{1,5},{2,6},{3,7},{4,0},{5,1},{6,2},{7,3},{8,12},{9,13},{10,... | collective-permute-start | bytes 1572872 | tf_op jit(solution)/shard_map/ppermute | solution.py:57
  36.7 2.6 %collective-permute-start.10 = (bf16[128,2048]{1,0:T(8,128)(2,1)S(1)}, bf16[128,2048]{1,0:T(8,128)(2,1)S(1)}, u32[]{:S(2)}, u32[]{:S(2)}) collective-permute-start(bf16[128,2048]{1,0:T(8,128)(2,1)S(1)} %collective-permute-done.8.refs_2_), channel_id=1, source_target_pairs={{0,4},{1,5},{2,6},{3,7},{4,0},{5,1},{6,2},{7,3},{8,12},{9,13},{10,... | collective-permute-start | bytes 1572872 | tf_op jit(solution)/shard_map/ppermute | solution.py:57
  36.8 10.3 %collective-permute-start.11 = (bf16[512,384]{1,0:T(8,128)(2,1)S(1)}, bf16[512,384]{1,0:T(8,128)(2,1)S(1)}, u32[]{:S(2)}, u32[]{:S(2)}) collective-permute-start(bf16[512,384]{1,0:T(8,128)(2,1)S(1)} %collective-permute-done.4.refs_7_.refs_11_), channel_id=1, source_target_pairs={{0,8},{1,9},{2,10},{3,11},{4,12},{5,13},{6,14},{7,15},{8,0},{9,1},... | collective-permute-start | bytes 1179656 | tf_op jit(solution)/shard_map/ppermute | solution.py:57
  38.1 7.2 %collective-permute-start.13 = (bf16[128,1024]{1,0:T(8,128)(2,1)S(1)}, bf16[128,1024]{1,0:T(8,128)(2,1)S(1)}, u32[]{:S(2)}, u32[]{:S(2)}) collective-permute-start(bf16[128,1024]{1,0:T(8,128)(2,1)S(1)} %slice.14), channel_id=1, source_target_pairs={{0,1},{1,0},{2,3},{3,2},{4,5},{5,4},{6,7},{7,6},{8,9},{9,8},{10,11... | collective-permute-start | bytes 786440 | tf_op jit(solution)/shard_map/ppermute | solution.py:57
  38.4 6.9 %collective-permute-start.12 = (bf16[128,1024]{1,0:T(8,128)(2,1)S(1)}, bf16[128,1024]{1,0:T(8,128)(2,1)S(1)}, u32[]{:S(2)}, u32[]{:S(2)}) collective-permute-start(bf16[128,1024]{1,0:T(8,128)(2,1)S(1)} %slice.13), channel_id=1, source_target_pairs={{0,2},{1,3},{2,0},{3,1},{4,6},{5,7},{6,4},{7,5},{8,10},{9,11},{10,... | collective-permute-start | bytes 786440 | tf_op jit(solution)/shard_map/ppermute | solution.py:57
  51.1 9.4 %collective-permute-start.17 = (bf16[4,256,128]{2,1,0:T(8,128)(2,1)S(1)}, bf16[4,256,128]{2,1,0:T(8,128)(2,1)S(1)}, u32[]{:S(2)}, u32[]{:S(2)}) collective-permute-start(bf16[4,256,128]{2,1,0:T(8,128)(2,1)S(1)} %get-tuple-element.59.own), channel_id=1, source_target_pairs={{8,16},{9,17},{10,18},{11,19},{12,20},{13,21},{14,22},{15,23},{16,... | collective-permute-start | bytes 786440 | tf_op jit(solution)/shard_map/ppermute | solution.py:57
  54.2 7.3 %collective-permute-start.16 = (bf16[4,256,128]{2,1,0:T(8,128)(2,1)S(1)}, bf16[4,256,128]{2,1,0:T(8,128)(2,1)S(1)}, u32[]{:S(2)}, u32[]{:S(2)}) collective-permute-start(bf16[4,256,128]{2,1,0:T(8,128)(2,1)S(1)} %get-tuple-element.59.own), channel_id=1, source_target_pairs={{0,8},{1,9},{2,10},{3,11},{4,12},{5,13},{6,14},{7,15},{8,0},{9,1},... | collective-permute-start | bytes 786440 | tf_op jit(solution)/shard_map/ppermute | solution.py:57
  54.2 9.1 %collective-permute-start.22 = (bf16[2,256,128]{2,1,0:T(8,128)(2,1)S(1)}, bf16[2,256,128]{2,1,0:T(8,128)(2,1)S(1)}, u32[]{:S(2)}, u32[]{:S(2)}) collective-permute-start(bf16[2,256,128]{2,1,0:T(8,128)(2,1)S(1)} %get-tuple-element.62.own), channel_id=1, source_target_pairs={{8,16},{9,17},{10,18},{11,19},{12,20},{13,21},{14,22},{15,23},{16,... | collective-permute-start | bytes 393224 | tf_op jit(solution)/shard_map/ppermute | solution.py:57
  56.5 7.7 %collective-permute-start.21 = (bf16[2,256,128]{2,1,0:T(8,128)(2,1)S(1)}, bf16[2,256,128]{2,1,0:T(8,128)(2,1)S(1)}, u32[]{:S(2)}, u32[]{:S(2)}) collective-permute-start(bf16[2,256,128]{2,1,0:T(8,128)(2,1)S(1)} %get-tuple-element.62.own), channel_id=1, source_target_pairs={{0,8},{1,9},{2,10},{3,11},{4,12},{5,13},{6,14},{7,15},{8,0},{9,1},... | collective-permute-start | bytes 393224 | tf_op jit(solution)/shard_map/ppermute | solution.py:57
  56.6 9.7 %collective-permute-start.19 = (bf16[2,256,128]{2,1,0:T(8,128)(2,1)S(1)}, bf16[2,256,128]{2,1,0:T(8,128)(2,1)S(1)}, u32[]{:S(2)}, u32[]{:S(2)}) collective-permute-start(bf16[2,256,128]{2,1,0:T(8,128)(2,1)S(1)} %get-tuple-element.61.own), channel_id=1, source_target_pairs={{8,16},{9,17},{10,18},{11,19},{12,20},{13,21},{14,22},{15,23},{16,... | collective-permute-start | bytes 393224 | tf_op jit(solution)/shard_map/ppermute | solution.py:57
  60.5 6.5 %collective-permute-start.18 = (bf16[2,256,128]{2,1,0:T(8,128)(2,1)S(1)}, bf16[2,256,128]{2,1,0:T(8,128)(2,1)S(1)}, u32[]{:S(2)}, u32[]{:S(2)}) collective-permute-start(bf16[2,256,128]{2,1,0:T(8,128)(2,1)S(1)} %get-tuple-element.61.own), channel_id=1, source_target_pairs={{0,8},{1,9},{2,10},{3,11},{4,12},{5,13},{6,14},{7,15},{8,0},{9,1},... | collective-permute-start | bytes 393224 | tf_op jit(solution)/shard_map/ppermute | solution.py:57
  64.5 7.1 %collective-permute-start.23 = (bf16[256,128]{1,0:T(8,128)(2,1)S(1)}, bf16[256,128]{1,0:T(8,128)(2,1)S(1)}, u32[]{:S(2)}, u32[]{:S(2)}) collective-permute-start(bf16[256,128]{1,0:T(8,128)(2,1)S(1)} %shard_map.72), channel_id=1, source_target_pairs={{0,1},{1,0},{2,3},{3,2},{4,5},{5,4},{6,7},{7,6},{8,9},{9,8},{10,11... | collective-permute-start | bytes 196616 | tf_op jit(solution)/shard_map/ppermute | solution.py:57
  65.1 6.7 %collective-permute-start.27 = (bf16[256,128]{1,0:T(8,128)(2,1)S(1)}, bf16[256,128]{1,0:T(8,128)(2,1)S(1)}, u32[]{:S(2)}, u32[]{:S(2)}) collective-permute-start(bf16[256,128]{1,0:T(8,128)(2,1)S(1)} %shard_map.74), channel_id=1, source_target_pairs={{0,3},{1,2},{2,1},{3,0},{4,7},{5,6},{6,5},{7,4},{8,11},{9,10},{10,... | collective-permute-start | bytes 196616 | tf_op jit(solution)/shard_map/ppermute | solution.py:57
  67.3 5.9 %collective-permute-start.25 = (bf16[256,128]{1,0:T(8,128)(2,1)S(1)}, bf16[256,128]{1,0:T(8,128)(2,1)S(1)}, u32[]{:S(2)}, u32[]{:S(2)}) collective-permute-start(bf16[256,128]{1,0:T(8,128)(2,1)S(1)} %shard_map.73), channel_id=1, source_target_pairs={{0,2},{1,3},{2,0},{3,1},{4,6},{5,7},{6,4},{7,5},{8,10},{9,11},{10,... | collective-permute-start | bytes 196616 | tf_op jit(solution)/shard_map/ppermute | solution.py:57
  68.1 6.0 %collective-permute-start.20 = (bf16[256,128]{1,0:T(8,128)(2,1)S(1)}, bf16[256,128]{1,0:T(8,128)(2,1)S(1)}, u32[]{:S(2)}, u32[]{:S(2)}) collective-permute-start(bf16[256,128]{1,0:T(8,128)(2,1)S(1)} %shard_map.71.refs_0_), channel_id=1, source_target_pairs={{0,4},{1,5},{2,6},{3,7},{4,0},{5,1},{6,2},{7,3},{8,12},{9,13},{10,... | collective-permute-start | bytes 196616 | tf_op jit(solution)/shard_map/ppermute | solution.py:57
  (12 other events, 25.3 us)

commit v6 on v5

--- a/solution.py
+++ b/solution.py
@@ -82,71 +82,78 @@
     return tm >> 1, tm & 1, lax.axis_index("depth")
 
 
-def split_kernel(mask, w, raw, to_x, to_y, to_across, keep, sites, sems):
+def edge_kernel(mask, raw, to_x, to_across, flags_ref):
     _, _, depth = where_am_i()
     odd = depth & 1
-    size = w.shape[0]
-    copies = [pltpu.make_async_copy(raw, sites, sems.at[3])]
-    for i, (at, ref) in enumerate(
-        ((PAIR, to_x.at[:size]), ((1 - odd) * 2 * PAIR, to_y.at[:size]), (odd * 2 * PAIR, keep))
-    ):
-        at = at if isinstance(at, int) else pl.multiple_of(at, PAIR)
-        copies.append(pltpu.make_async_copy(w.at[:, pl.ds(at, PAIR)], ref, sems.at[i]))
-    for copy in copies:
-        copy.start()
     lane = lax.broadcasted_iota(jnp.int32, (EXTRA, HD), 1)
     flags = jnp.zeros((EXTRA, HD), jnp.int32)
     for entry in range(mask.shape[0]):
         flags = jnp.where(lane == entry, mask[entry], flags)
     flags = flags.astype(jnp.float32).astype(jnp.bfloat16)
-    copies[0].wait()
-    values = sites[...].astype(jnp.float32)
+    flags_ref[...] = flags
+    values = raw[...].astype(jnp.float32)
     first, last = values[:, 0], values[:, values.shape[1] - 1]
-    for ref, use_last, at in ((to_x, odd == 0, size), (to_across, depth == 1, 0)):
-        ref[at : at + EXTRA, :HD] = jnp.where(use_last, last, first).astype(jnp.bfloat16)
-        ref[at : at + EXTRA, HD:] = flags
-    to_y[size:, :HD] = flags
-    to_y[size:, HD:] = flags
-    for copy in copies[1:]:
-        copy.wait()
-
-
-def sort_kernel(kept, from_x, from_y, across, to_y, keep_ref, send_ref, flags_ref):
+    for ref, use_last in ((to_x, odd == 0), (to_across, depth == 1)):
+        ref[:EXTRA] = jnp.where(use_last, last, first).astype(jnp.bfloat16)
+        ref[EXTRA:] = flags
+
+
+def split_kernel(w, to_x, to_y, keep):
+    _, _, depth = where_am_i()
+    even = (depth & 1) == 0
+    low, high = w[:, :PAIR], w[:, 2 * PAIR :]
+    to_x[...] = w[:, PAIR : 2 * PAIR]
+    to_y[: w.shape[0]] = jnp.where(even, high, low)
+    keep[...] = jnp.where(even, low, high)
+
+
+def split_far_kernel(w, flags, to_x, to_y, keep):
+    split_kernel(w, to_x, to_y, keep)
+    to_y[w.shape[0] :, :HD] = flags[...]
+    to_y[w.shape[0] :, HD:] = flags[...]
+
+
+def sorted_groups(kept, from_x, from_y):
     _, core, depth = where_am_i()
     first, even = core == 0, (depth & 1) == 0
     size = kept.shape[0]
     low = jnp.where(even, kept[...], from_y[:size])
     high = jnp.where(even, from_y[:size], kept[...])
-    for k, group in enumerate((low, from_x[:size], high)):
-        here = slice(k * HD, (k + 1) * HD)
-        keep_ref[:, here] = jnp.where(first, group[:, :HD], group[:, HD:])
-        send_ref[:size, here] = jnp.where(first, group[:, HD:], group[:, :HD])
+    groups = (low, from_x[:size], high)
+    turn = jnp.where(depth == 3, 0, depth)
+    for third in range(3):
+        group = jnp.where(turn == 0, groups[third], jnp.where(turn == 1, groups[(third + 1) % 3], groups[(third + 2) % 3]))
+        yield third, jnp.where(first, group[:, :HD], group[:, HD:]), jnp.where(first, group[:, HD:], group[:, :HD])
+
+
+def sort_kernel(kept, from_x, from_y, out_ref):
+    for third, mine, other in sorted_groups(kept, from_x, from_y):
+        out_ref[:, third * HD : (third + 1) * HD] = mine
+        out_ref[:, (3 + third) * HD : (4 + third) * HD] = other
+
+
+def sort_far_kernel(kept, from_x, from_y, edge_x, edge_across, own_flags, q_ref, kv_ref, send_ref, flags_ref):
+    for third, mine, other in sorted_groups(kept, from_x, from_y):
+        send_ref[:, third * HD : (third + 1) * HD] = other
+        if third:
+            kv_ref[:, (third - 1) * HD : third * HD] = mine
+        else:
+            q_ref[...] = mine
     row = lax.broadcasted_iota(jnp.int32, (EXTRA, HD), 0)
-    flags = to_y[size:, :HD].astype(jnp.float32)
-    for r, value in ((1, from_x[size:, HD:]), (2, from_y[size:, :HD]), (3, across[:, HD:])):
+    flags = own_flags[...].astype(jnp.float32)
+    for r, value in ((1, edge_x[EXTRA:]), (2, from_y[kept.shape[0] :, :HD]), (3, edge_across[EXTRA:])):
         flags = jnp.where(row == r, value.astype(jnp.float32), flags)
     flags = flags.astype(jnp.bfloat16)
-    flags_ref[...] = flags
     for k in range(3):
-        send_ref[size:, k * HD : (k + 1) * HD] = flags
-
-
-def load_kernel(*refs):
-    count = (len(refs) - 1) // 2
-    copies = [pltpu.make_async_copy(refs[i], refs[count + i], refs[-1].at[i]) for i in range(count)]
-    for copy in copies:
-        copy.start()
-    for copy in copies:
-        copy.wait()
-
-
-def embed_kernel(from_x, across, gain, raw, stream, conv_w, out_ref, acc):
+        flags_ref[:, k * HD : (k + 1) * HD] = flags
+
+
+def embed_kernel(edge_x, edge_across, gain, raw, stream, conv_w, out_ref, acc):
     time_len, site_len, feat_len = raw.shape
     _, _, depth = where_am_i()
     even = (depth & 1) == 0
     rows, width = stream.shape
-    side = from_x[from_x.shape[0] - EXTRA :, :HD].astype(jnp.float32)
-    far = across[:, :HD].astype(jnp.float32)
+    side, far = edge_x[:time_len].astype(jnp.float32), edge_across[:time_len].astype(jnp.float32)
     before = jnp.where(even, jnp.where(depth == 2, far, 0.0), side)
     behind = jnp.where(even, side, jnp.where(depth == 1, far, 0.0))
     padded = jnp.concatenate([before[:, None], raw[...].astype(jnp.float32), behind[:, None]], axis=1)
@@ -169,40 +176,55 @@
     return jnp.concatenate([jnp.concatenate([ref[:, at] for at in cuts], axis=1) for ref in refs], axis=0)
 
 
+def three_shards(x_refs, own, near, received, far_q, far_kv):
+    z, core, _ = where_am_i()
+    size, width = own.shape[0], 3 * HD
+    w = [own[:, :width], received[:size], jnp.concatenate([far_q[...], far_kv[...]], axis=1)]
+    w = jnp.concatenate(w + [near[:, :width], received[size : 2 * size]], axis=0)
+    x = [take(x_refs, source, core, 2 * size) for source in (z, z ^ 2, z ^ 1)]
+    return jnp.dot(jnp.concatenate(x, axis=1), w, preferred_element_type=jnp.float32)
+
+
 def partial_kernel(*refs):
-    x_refs, (own, far, near, acc_ref) = refs[:6], refs[6:]
+    refs[-1][...] = three_shards(refs[:6], *refs[6:-1])
+
+
+def diagonal_kernel(*refs):
+    pieces, weights, (acc_ref, x_ref) = refs[:6], refs[6:-2], refs[-2:]
+    block, half = pieces[0].shape
+    corners = ((0, 0), (0, half), (block, 0), (block + block // 2, 0), (block, half), (block + block // 2, half))
+    for (row, at), ref in zip(corners, pieces):
+        x_ref[row : row + ref.shape[0], at : at + half] = ref[...]
+    acc_ref[...] = three_shards([x_ref], *weights)
+
+
+ROW_ORDER = ((0, 1, 2, 6), (3, 4, 5, 7))
+
+
+def finish(x_refs, last, acc_in, acc_diagonal, columns):
     z, core, _ = where_am_i()
-    w = jnp.concatenate([ref[...] for ref in (own, far, near)], axis=0)
-    x = [take(x_refs, source, core, own.shape[0]) for source in (z, z ^ 2, z ^ 1)]
-    acc_ref[...] = jnp.dot(jnp.concatenate(x, axis=1), w, preferred_element_type=jnp.float32)
-
-
-def project_kernel(*refs):
-    early, late, (own, far, near, last, acc_in) = refs[:6], refs[6:10], refs[10:15]
-    q_ref, k_ref, v_first, v_second, acc_ref, x_all = refs[15:]
-    z, core, depth = where_am_i()
-    rows, block, half = own.shape[0], late[0].shape[0], late[0].shape[1]
-    for i, ref in enumerate(late):
-        x_all[(i // 2) * block : (i // 2 + 1) * block, (i % 2) * half : (i % 2 + 1) * half] = ref[...]
-    w = jnp.concatenate([ref[...] for ref in (own, far, near, last)], axis=0)
-    x = [take([x_all], source, core, rows) for source in (z, z ^ 2, z ^ 1, z ^ 3)]
-    acc_ref[6 * block :] = jnp.dot(jnp.concatenate(x, axis=1), w, preferred_element_type=jnp.float32)
-    x = take(early, z ^ 3, core, rows)
-    acc_ref[: 6 * block] = acc_in[...] + jnp.dot(x, last[...], preferred_element_type=jnp.float32)
-    order = ((0, 1, 2, 6), (3, 4, 5, 7))
-    turn = jnp.where(depth == 3, 0, depth)
+    value = jnp.dot(take(x_refs, z ^ 3, core, last.shape[0]), last[...], preferred_element_type=jnp.float32)
+    early = acc_in.shape[0]
+    return (
+        (acc_in[:, columns] + value[:early]).astype(jnp.bfloat16),
+        (acc_diagonal[:, columns] + value[early:]).astype(jnp.bfloat16),
+    )
+
+
+def finish_kernel(columns, *refs):
+    x_refs, (last, acc_in, acc_diagonal), out_refs = refs[:7], refs[7:10], refs[10:]
+    _, core, _ = where_am_i()
+    block = x_refs[0].shape[0]
+    values = jnp.concatenate(finish(x_refs, last, acc_in, acc_diagonal, columns), axis=0)
     for rel in range(2):
         at = pl.ds(pl.multiple_of((core ^ rel) * block, block), block)
         for r in range(4):
-            row = order[rel][r]
-            mine = slice(row * block, (row + 1) * block)
-            v_at = V_ORDER.index(r)
-            targets = (q_ref.at[r], k_ref.at[r], (v_first, v_second)[v_at // 2].at[v_at % 2])
-            for third, ref in enumerate(targets):
-                group = third + turn
-                group = jnp.where(group >= 3, group - 3, group)
-                lanes = pl.ds(pl.multiple_of(group * HD, HD), HD)
-                ref[at, :] = acc_ref[mine, lanes].astype(jnp.bfloat16)
+            row = ROW_ORDER[rel][r]
+            value = values[row * block : (row + 1) * block]
+            out_refs[0][r, at, :] = value[:, :HD]
+            if len(out_refs) > 1:
+                v_at = V_ORDER.index(r)
+                out_refs[1 + v_at // 2][v_at % 2, at, :] = value[:, HD:]
 
 
 def spans(u):
@@ -216,11 +238,11 @@
     return jnp.where(odd, outer, middle), own[index], jnp.where(odd, middle, outer)
 
 
-def weigh_kernel(q_ref, outer, own, middle, own_flags, other_flags, out_ref):
+def weigh_kernel(q_ref, outer, own, middle, own_flags, received, out_ref):
     _, core, _ = where_am_i()
     block = q_ref.shape[1] // 2
     inv_root = 1.0 / math.sqrt(HD)
-    flags = [own_flags[...].astype(jnp.float32), other_flags[...].astype(jnp.float32)]
+    flags = [own_flags[:, :HD].astype(jnp.float32), received[-EXTRA:, :HD].astype(jnp.float32)]
     flags = [jnp.where(core == u, flags[0], flags[1]) for u in range(2)]
     bias = [(f - 1.0) * 1e30 for f in flags]
     for r in range(4):
@@ -265,7 +287,7 @@
 
 
 def call(kernel, outs, places, scratch=(), macs=0):
-    spaces = {"s": SMEM, "v": VMEM, "h": pltpu.HBM}
+    spaces = {"s": SMEM, "v": VMEM}
     return pl.pallas_call(
         kernel,
         out_shape=outs,
@@ -286,57 +308,77 @@
     def array(*shape, kind=bf16):
         return jax.ShapeDtypeStruct(shape, kind)
 
-    to_x, to_y, to_across, kept = call(
-        split_kernel,
-        (array(size + EXTRA, PAIR), array(size + EXTRA, PAIR), array(EXTRA, PAIR), array(size, PAIR)),
-        "shh",
-        scratch=[VMEM(raw.shape, bf16), pltpu.SemaphoreType.DMA((4,))],
-    )(mask.reshape(mask.shape[2]), w_qkv, raw)
-    from_x, from_y, across = swap_depth(to_x, 1), swap_depth(to_y, 2), swap_depth(to_across, 3)
-    operands = (after(raw, to_x), stream.reshape(block, width), conv_w.reshape(3 * feat_len, width))
-    operands = call(
-        load_kernel, tuple(array(*t.shape) for t in operands), "hhh", scratch=[pltpu.SemaphoreType.DMA((3,))]
-    )(*operands)
-    kept, *operands = lax.optimization_barrier((kept, *operands))
-    keep, send, flags = call(
-        sort_kernel, (array(size, 3 * HD), array(size + EXTRA, 3 * HD), array(EXTRA, HD)), "v" * 5
-    )(kept, from_x, from_y, across, to_y)
-    received = swap_core(send)
-    other_flags = received[size:, :HD]
-    shard = jnp.concatenate([keep, received[:size]], axis=0)
-    far, near = swap_z(shard, 2), swap_z(shard, 1)
-
+    far_raw = swap_z(w_qkv, 2)
+
+    cut, cut_more = array(size, PAIR), array(size + EXTRA, PAIR)
+    to_x, to_y, kept = call(split_kernel, (cut,) * 3, "v")(w_qkv)
+    own = call(sort_kernel, array(size, 6 * HD), "vvv")(kept, swap_depth(to_x, 1), swap_depth(to_y, 2))
+    near = swap_z(own, 1)
+
+    edge_x, edge_across, own_flags = call(
+        edge_kernel, (array(2 * EXTRA, HD), array(2 * EXTRA, HD), array(EXTRA, HD)), "sv"
+    )(mask.reshape(mask.shape[2]), raw)
+    edge_x, edge_across = swap_depth(edge_x, 1), swap_depth(edge_across, 3)
     normed = call(
         embed_kernel,
         array(block, width),
         "v" * 6,
         scratch=[VMEM((block, width), f32)],
         macs=block * 3 * feat_len * width,
-    )(from_x, across, gain.reshape(1, width), *operands)
-    normed = after(normed, received)
+    )(
+        edge_x,
+        edge_across,
+        gain.reshape(1, width),
+        raw,
+        stream.reshape(block, width),
+        conv_w.reshape(3 * feat_len, width),
+    )
     beside, above = swap_depth(normed, 1), swap_depth(normed, 2)
-    opposite = swap_core(normed)
-    far, near, opposite, beside, above = lax.optimization_barrier((far, near, opposite, beside, above))
+
+    to_x, to_y, kept = call(split_far_kernel, (cut, cut_more, cut), "vv")(far_raw, own_flags)
+    from_x, from_y = swap_depth(to_x, 1), swap_depth(to_y, 2)
+    from_x, from_y, near, beside, above = lax.optimization_barrier((from_x, from_y, near, beside, above))
+    keep_q, keep_kv, send, flags = call(
+        sort_far_kernel,
+        (array(size, HD), array(size, PAIR), array(size, 3 * HD), array(EXTRA, 3 * HD)),
+        "v" * 6,
+    )(kept, from_x, from_y, edge_x, edge_across, own_flags)
+    received = swap_core(send)
+    far_q = jnp.concatenate([keep_q, received[:, :HD]], axis=0)
+    far_kv = jnp.concatenate([keep_kv, received[:, HD:]], axis=0)
+    last_kv = swap_z(far_kv, 1)
+    last_q = swap_z(far_q, 1)
+    received = swap_core(jnp.concatenate([own[:, 3 * HD :], near[:, 3 * HD :], flags], axis=0))
+    weights = (own, near, received, far_q, far_kv)
+    opposite = swap_core(after(normed, near))
+
+    diagonal = [swap_depth(beside[:, :half], 2), swap_depth(above[:, half:], 1)]
     early = (normed, beside, above, opposite, swap_core(beside), swap_core(above))
-    last = swap_z(far, 1)
-    diagonal = [swap_depth(early[1][:, :half], 2), swap_depth(early[2][:, half:], 1)]
     rows = 2 * size
-    total = call(partial_kernel, array(6 * block, 3 * HD, kind=f32), "v" * 9, macs=6 * block * 3 * rows * 3 * HD)(
-        *early, shard, far, near
-    )
-    last, total, *diagonal = lax.optimization_barrier((last, total, *diagonal))
-    late = diagonal + [swap_core(t) for t in diagonal]
+    total = call(partial_kernel, array(6 * block, 3 * HD, kind=f32), "v" * 11, macs=6 * block * 3 * rows * 3 * HD)(
+        *early, *weights
+    )
+    diagonal = [after(t, total) for t in diagonal]
+    diagonal += [swap_core(t[i * block // 2 : (i + 1) * block // 2]) for t in diagonal for i in range(2)]
+    total_diagonal, diagonal = call(
+        diagonal_kernel,
+        (array(2 * block, 3 * HD, kind=f32), array(2 * block, width)),
+        "v" * 11,
+        macs=2 * block * 3 * rows * 3 * HD,
+    )(*diagonal, *weights)
     one_head, half_head = array(4, 2 * block, HD), array(2, 2 * block, HD)
-    q, k, *v = call(
-        project_kernel,
-        (one_head, one_head, half_head, half_head),
-        "v" * 15,
-        scratch=[VMEM((8 * block, 3 * HD), f32), VMEM((2 * block, width), bf16)],
-        macs=14 * block * rows * 3 * HD,
-    )(*early, *late, shard, far, near, last, total)
+    k, *v = call(
+        functools.partial(finish_kernel, slice(HD, 3 * HD)),
+        (one_head, half_head, half_head),
+        "v" * 10,
+        macs=8 * block * rows * 2 * HD,
+    )(*early, diagonal, last_kv, total, total_diagonal)
+    (q,) = call(functools.partial(finish_kernel, slice(0, HD)), (one_head,), "v" * 10, macs=8 * block * rows * HD)(
+        *early, diagonal, last_q, total, total_diagonal
+    )
 
     weights = call(weigh_kernel, array(4, 2 * block, 5 * block), "v" * 6, macs=8 * block * 5 * block * HD)(
-        q, swap_z(k, 1), k, swap_middle(k), flags, other_flags
+        q, swap_z(k, 1), k, swap_middle(k), flags, received
     )
     values = [(swap_z(t, 1), t, swap_middle(t)) for t in v]
     pieces = {}

time: 76.8 us -> 77.9 us (1.014)
  starting transfers between devices: 31.5 us -> 41.1 us
  waiting for transfers between devices: 31.2 us -> 22.3 us
  local copies, waits for them, and re-layouts: 5.68 us -> 6.47 us
    ppermute x29 -> x36, starting transfers between devices: 31.5 us -> 41.1 us  [hop(): return lax.ppermute(value, ('tm', 'depth'), pairs)]
    ppermute x29 -> x36, waiting for transfers between devices: 31.2 us -> 22.3 us  [hop(): return lax.ppermute(value, ('tm', 'depth'), pairs)]
    pallas_call x5 -> x9, Pallas kernels: 3.61 us -> 3.77 us  [the longest x1 1.38 us: plane_device(): call(partial_kernel, array(6 * block, 3 * HD, kind=f32), 'v' * 11, macs=6...]
  transfers between devices with their start and end apart: 29 -> 36, of which waited for: 13 -> 9; matrix products, arithmetic and copies ran while one was open for 0% -> 0% of each run, Pallas kernels for 6% -> 7%
where the time goes in v6:
time: 77.9 us; the launch traced here: 77.5 us
  starting transfers between devices  41.1 us (53%)
  waiting for transfers between devices  22.3 us (29%)
  Pallas kernels  7.31 us (9%)
  local copies, waits for them, and re-layouts  6.47 us (8%)
    ppermute x36, starting transfers between devices, hop(): return lax.ppermute(value, ('tm', 'depth'), pairs)  41.1 us
    ppermute x36, waiting for transfers between devices, hop(): return lax.ppermute(value, ('tm', 'depth'), pairs)  22.3 us
    unnamed x14, local copies, waits for them, and re-layouts  6.34 us
  transfers between devices with their start and end apart: 36, of which 9 were waited for; matrix products, arithmetic and copies ran while one was open for 0% of the time, Pallas kernels for 7%

profile of v6, /device:TPU:9, one launch (start us, length us, event | category | flops | bytes accessed | tf_op | source)
XLA Modules:
  0.0 77.5 jit_solution(10639290312716591180)
XLA Ops:
  2.0 1.3 %collective-permute-start = (bf16[32,128]{1,0:T(8,128)(2,1)S(1)}, bf16[32,128]{1,0:T(8,128)(2,1)S(1)}, u32[]{:S(2)}, u32[]{:S(2)}) collective-permute-start(bf16[32,128]{1,0:T(8,128)(2,1)S(1)} %get-tuple-element.31), channel_id=1, source_target_pairs={{0,1},{1,0},{2,3},{3,2},{4,5},{5,4},{6,7},{7,6},{8,9},{9,8},{10,11... | collective-permute-start | bytes 24584 | tf_op jit(solution)/shard_map/ppermute | solution.py:57
  4.5 2.3 %collective-permute-start.2 = (bf16[256,768]{1,0:T(8,128)(2,1)}, bf16[256,768]{1,0:T(8,128)(2,1)S(1)}, u32[]{:S(2)}, u32[]{:S(2)}) collective-permute-start(bf16[256,768]{1,0:T(8,128)(2,1)} %w.1), channel_id=1, source_target_pairs={{0,16},{1,17},{2,18},{3,19},{4,20},{5,21},{6,22},{7,23},{8,24},{9,... | collective-permute-start | bytes 1179656 | tf_op jit(solution)/shard_map/ppermute | solution.py:57
  7.9 1.3 %collective-permute-start.5 = (bf16[256,256]{1,0:T(8,128)(2,1)S(1)}, bf16[256,256]{1,0:T(8,128)(2,1)S(1)}, u32[]{:S(2)}, u32[]{:S(2)}) collective-permute-start(bf16[256,256]{1,0:T(8,128)(2,1)S(1)} %get-tuple-element.37), channel_id=1, source_target_pairs={{0,1},{1,0},{2,3},{3,2},{4,5},{5,4},{6,7},{7,6},{8,9},{9,8},{10,11... | collective-permute-start | bytes 393224 | tf_op jit(solution)/shard_map/ppermute | solution.py:57
  9.4 1.4 %copy-done = bf16[3,128,2048]{2,1,0:T(8,128)(2,1)S(1)} copy-done((bf16[3,128,2048]{2,1,0:T(8,128)(2,1)S(1)}, bf16[3,128,2048]{2,1,0:T(8,128)(2,1)}, u32[]{:S(2)}) %copy-start) | copy-done | bytes 1572888
  14.2 1.2 %collective-permute-start.9 = (bf16[128,2048]{1,0:T(8,128)(2,1)S(1)}, bf16[128,2048]{1,0:T(8,128)(2,1)S(1)}, u32[]{:S(2)}, u32[]{:S(2)}) collective-permute-start(bf16[128,2048]{1,0:T(8,128)(2,1)S(1)} %shard_map.65.refs_0_), channel_id=1, source_target_pairs={{0,2},{1,3},{2,0},{3,1},{4,6},{5,7},{6,4},{7,5},{8,10},{9,11},{10,... | collective-permute-start | bytes 1572872 | tf_op jit(solution)/shard_map/ppermute | solution.py:57
  15.8 8.5 %collective-permute-done.2.w = bf16[256,768]{1,0:T(8,128)(2,1)S(1)} collective-permute-done((bf16[256,768]{1,0:T(8,128)(2,1)}, bf16[256,768]{1,0:T(8,128)(2,1)S(1)}, u32[]{:S(2)}, u32[]{:S(2)}) %collective-permute-start.2) | collective-permute-done | bytes 393248 | tf_op jit(solution)/shard_map/ppermute | solution.py:57
  25.9 5.6 %collective-permute-done.7.refs_7_ = bf16[256,768]{1,0:T(8,128)(2,1)S(1)} collective-permute-done((bf16[256,768]{1,0:T(8,128)(2,1)S(1)}, bf16[256,768]{1,0:T(8,128)(2,1)S(1)}, u32[]{:S(2)}, u32[]{:S(2)}) %collective-permute-start.7) | collective-permute-done | bytes 393248 | tf_op jit(solution)/shard_map/ppermute | solution.py:57
  33.4 1.3 %collective-permute-start.16 = (bf16[128,1024]{1,0:T(8,128)(2,1)S(1)}, bf16[128,1024]{1,0:T(8,128)(2,1)S(1)}, u32[]{:S(2)}, u32[]{:S(2)}) collective-permute-start(bf16[128,1024]{1,0:T(8,128)(2,1)S(1)} %slice.35), channel_id=1, source_target_pairs={{0,1},{1,0},{2,3},{3,2},{4,5},{5,4},{6,7},{7,6},{8,9},{9,8},{10,11... | collective-permute-start | bytes 786440 | tf_op jit(solution)/shard_map/ppermute | solution.py:57
  34.7 1.4 %collective-permute-done.14.refs_8_.received = bf16[528,384]{1,0:T(8,128)(2,1)S(1)} collective-permute-done((bf16[528,384]{1,0:T(8,128)(2,1)S(1)}, bf16[528,384]{1,0:T(8,128)(2,1)S(1)}, u32[]{:S(2)}, u32[]{:S(2)}) %collective-permute-start.14) | collective-permute-done | bytes 405536 | tf_op jit(solution)/shard_map/ppermute | solution.py:57
  37.0 1.6 %collective-permute-start.22 = (bf16[512,256]{1,0:T(8,128)(2,1)S(1)}, bf16[512,256]{1,0:T(8,128)(2,1)S(1)}, u32[]{:S(2)}, u32[]{:S(2)}) collective-permute-start(bf16[512,256]{1,0:T(8,128)(2,1)S(1)} %pad_maximum_fusion.1.refs_10_), channel_id=1, source_target_pairs={{0,8},{1,9},{2,10},{3,11},{4,12},{5,13},{6,14},{7,15},{8,0},{9,1},... | collective-permute-start | bytes 786440 | tf_op jit(solution)/shard_map/ppermute | solution.py:57
  38.6 1.4 %shard_map.70.refs_8_ = f32[768,384]{1,0:T(8,128)S(1)} custom-call(bf16[128,2048]{1,0:T(8,128)(2,1)S(1)} %shard_map.65.refs_0_, bf16[128,2048]{1,0:T(8,128)(2,1)S(1)} %collective-permute-done.8.refs_1_, bf16[128,2048]{1,0:T(8,128)(2,1)S(1)} %collective-permute-done.9.refs_2_, bf16[128,2048]{1,0:T(8,128)(2,1)S(1)} %collective-permute-done.10.refs_3_, ...), custom_call_target="tpu_custom_call" | custom-call | flops 905969664 | tf_op jit(solution)/shard_map/pallas_call | solution.py:358
  40.0 1.2 %collective-permute-done.16.refs_1_ = bf16[128,1024]{1,0:T(8,128)(2,1)S(1)} collective-permute-done((bf16[128,1024]{1,0:T(8,128)(2,1)S(1)}, bf16[128,1024]{1,0:T(8,128)(2,1)S(1)}, u32[]{:S(2)}, u32[]{:S(2)}) %collective-permute-start.16) | collective-permute-done | bytes 262176 | tf_op jit(solution)/shard_map/ppermute | solution.py:57
  42.3 1.5 %collective-permute-done.13.refs_0_ = bf16[128,1024]{1,0:T(8,128)(2,1)S(1)} collective-permute-done((bf16[128,1024]{1,0:T(8,128)(2,1)S(1)}, bf16[128,1024]{1,0:T(8,128)(2,1)S(1)}, u32[]{:S(2)}, u32[]{:S(2)}) %collective-permute-start.13) | collective-permute-done | bytes 262176 | tf_op jit(solution)/shard_map/ppermute | solution.py:57
  47.4 2.3 %collective-permute-start.23 = (bf16[4,256,128]{2,1,0:T(8,128)(2,1)S(1)}, bf16[4,256,128]{2,1,0:T(8,128)(2,1)S(1)}, u32[]{:S(2)}, u32[]{:S(2)}) collective-permute-start(bf16[4,256,128]{2,1,0:T(8,128)(2,1)S(1)} %get-tuple-element.54.own), channel_id=1, source_target_pairs={{0,8},{1,9},{2,10},{3,11},{4,12},{5,13},{6,14},{7,15},{8,0},{9,1},... | collective-permute-start | bytes 786440 | tf_op jit(solution)/shard_map/ppermute | solution.py:57
  49.7 3.6 %collective-permute-start.24 = (bf16[4,256,128]{2,1,0:T(8,128)(2,1)S(1)}, bf16[4,256,128]{2,1,0:T(8,128)(2,1)S(1)}, u32[]{:S(2)}, u32[]{:S(2)}) collective-permute-start(bf16[4,256,128]{2,1,0:T(8,128)(2,1)S(1)} %get-tuple-element.54.own), channel_id=1, source_target_pairs={{8,16},{9,17},{10,18},{11,19},{12,20},{13,21},{14,22},{15,23},{16,... | collective-permute-start | bytes 786440 | tf_op jit(solution)/shard_map/ppermute | solution.py:57
  53.4 1.5 %collective-permute-start.28 = (bf16[2,256,128]{2,1,0:T(8,128)(2,1)S(1)}, bf16[2,256,128]{2,1,0:T(8,128)(2,1)S(1)}, u32[]{:S(2)}, u32[]{:S(2)}) collective-permute-start(bf16[2,256,128]{2,1,0:T(8,128)(2,1)S(1)} %get-tuple-element.56.own), channel_id=1, source_target_pairs={{0,8},{1,9},{2,10},{3,11},{4,12},{5,13},{6,14},{7,15},{8,0},{9,1},... | collective-permute-start | bytes 393224 | tf_op jit(solution)/shard_map/ppermute | solution.py:57
  54.8 1.9 %collective-permute-start.29 = (bf16[2,256,128]{2,1,0:T(8,128)(2,1)S(1)}, bf16[2,256,128]{2,1,0:T(8,128)(2,1)S(1)}, u32[]{:S(2)}, u32[]{:S(2)}) collective-permute-start(bf16[2,256,128]{2,1,0:T(8,128)(2,1)S(1)} %get-tuple-element.56.own), channel_id=1, source_target_pairs={{8,16},{9,17},{10,18},{11,19},{12,20},{13,21},{14,22},{15,23},{16,... | collective-permute-start | bytes 393224 | tf_op jit(solution)/shard_map/ppermute | solution.py:57
  56.8 1.9 %collective-permute-done.21.refs_7_ = bf16[512,128]{1,0:T(8,128)(2,1)S(1)} collective-permute-done((bf16[512,128]{1,0:T(8,128)(2,1)S(1)}, bf16[512,128]{1,0:T(8,128)(2,1)S(1)}, u32[]{:S(2)}, u32[]{:S(2)}) %collective-permute-start.21) | collective-permute-done | bytes 131104 | tf_op jit(solution)/shard_map/ppermute | solution.py:57
  58.6 1.6 %collective-permute-start.25 = (bf16[2,256,128]{2,1,0:T(8,128)(2,1)S(1)}, bf16[2,256,128]{2,1,0:T(8,128)(2,1)S(1)}, u32[]{:S(2)}, u32[]{:S(2)}) collective-permute-start(bf16[2,256,128]{2,1,0:T(8,128)(2,1)S(1)} %get-tuple-element.55.own), channel_id=1, source_target_pairs={{0,8},{1,9},{2,10},{3,11},{4,12},{5,13},{6,14},{7,15},{8,0},{9,1},... | collective-permute-start | bytes 393224 | tf_op jit(solution)/shard_map/ppermute | solution.py:57
  60.3 3.6 %collective-permute-start.26 = (bf16[2,256,128]{2,1,0:T(8,128)(2,1)S(1)}, bf16[2,256,128]{2,1,0:T(8,128)(2,1)S(1)}, u32[]{:S(2)}, u32[]{:S(2)}) collective-permute-start(bf16[2,256,128]{2,1,0:T(8,128)(2,1)S(1)} %get-tuple-element.55.own), channel_id=1, source_target_pairs={{8,16},{9,17},{10,18},{11,19},{12,20},{13,21},{14,22},{15,23},{16,... | collective-permute-start | bytes 393224 | tf_op jit(solution)/shard_map/ppermute | solution.py:57
  65.8 1.2 %collective-permute-start.34 = (bf16[256,128]{1,0:T(8,128)(2,1)S(1)}, bf16[256,128]{1,0:T(8,128)(2,1)S(1)}, u32[]{:S(2)}, u32[]{:S(2)}) collective-permute-start(bf16[256,128]{1,0:T(8,128)(2,1)S(1)} %shard_map.78), channel_id=1, source_target_pairs={{0,3},{1,2},{2,1},{3,0},{4,7},{5,6},{6,5},{7,4},{8,11},{9,10},{10,... | collective-permute-start | bytes 196616 | tf_op jit(solution)/shard_map/ppermute | solution.py:57
  67.2 1.3 %collective-permute-start.32 = (bf16[256,128]{1,0:T(8,128)(2,1)S(1)}, bf16[256,128]{1,0:T(8,128)(2,1)S(1)}, u32[]{:S(2)}, u32[]{:S(2)}) collective-permute-start(bf16[256,128]{1,0:T(8,128)(2,1)S(1)} %shard_map.77), channel_id=1, source_target_pairs={{0,2},{1,3},{2,0},{3,1},{4,6},{5,7},{6,4},{7,5},{8,10},{9,11},{10,... | collective-permute-start | bytes 196616 | tf_op jit(solution)/shard_map/ppermute | solution.py:57
  69.4 3.1 %collective-permute-start.27 = (bf16[256,128]{1,0:T(8,128)(2,1)S(1)}, bf16[256,128]{1,0:T(8,128)(2,1)S(1)}, u32[]{:S(2)}, u32[]{:S(2)}) collective-permute-start(bf16[256,128]{1,0:T(8,128)(2,1)S(1)} %shard_map.75.refs_0_), channel_id=1, source_target_pairs={{0,4},{1,5},{2,6},{3,7},{4,0},{5,1},{6,2},{7,3},{8,12},{9,13},{10,... | collective-permute-start | bytes 196616 | tf_op jit(solution)/shard_map/ppermute | solution.py:57
  74.0 1.8 %collective-permute-start.31 = (bf16[256,128]{1,0:T(8,128)(2,1)S(1)}, bf16[256,128]{1,0:T(8,128)(2,1)S(1)}, u32[]{:S(2)}, u32[]{:S(2)}) collective-permute-start(bf16[256,128]{1,0:T(8,128)(2,1)S(1)} %collective-permute-done.30.refs_2_), channel_id=1, source_target_pairs={{0,4},{1,5},{2,6},{3,7},{4,0},{5,1},{6,2},{7,3},{8,12},{9,13},{10,... | collective-permute-start | bytes 196616 | tf_op jit(solution)/shard_map/ppermute | solution.py:57
  (89 shorter events, 23.6 us)
Async XLA Ops:
  2.0 7.4 %collective-permute-start = (bf16[32,128]{1,0:T(8,128)(2,1)S(1)}, bf16[32,128]{1,0:T(8,128)(2,1)S(1)}, u32[]{:S(2)}, u32[]{:S(2)}) collective-permute-start(bf16[32,128]{1,0:T(8,128)(2,1)S(1)} %get-tuple-element.31), channel_id=1, source_target_pairs={{0,1},{1,0},{2,3},{3,2},{4,5},{5,4},{6,7},{7,6},{8,9},{9,8},{10,11... | collective-permute-start | bytes 24584 | tf_op jit(solution)/shard_map/ppermute | solution.py:57
  3.3 6.1 %collective-permute-start.1 = (bf16[32,128]{1,0:T(8,128)(2,1)S(1)}, bf16[32,128]{1,0:T(8,128)(2,1)S(1)}, u32[]{:S(2)}, u32[]{:S(2)}) collective-permute-start(bf16[32,128]{1,0:T(8,128)(2,1)S(1)} %get-tuple-element.32), channel_id=1, source_target_pairs={{0,3},{1,2},{2,1},{3,0},{4,7},{5,6},{6,5},{7,4},{8,11},{9,10},{10,... | collective-permute-start | bytes 24584 | tf_op jit(solution)/shard_map/ppermute | solution.py:57
  4.5 19.8 %collective-permute-start.2 = (bf16[256,768]{1,0:T(8,128)(2,1)}, bf16[256,768]{1,0:T(8,128)(2,1)S(1)}, u32[]{:S(2)}, u32[]{:S(2)}) collective-permute-start(bf16[256,768]{1,0:T(8,128)(2,1)} %w.1), channel_id=1, source_target_pairs={{0,16},{1,17},{2,18},{3,19},{4,20},{5,21},{6,22},{7,23},{8,24},{9,... | collective-permute-start | bytes 1179656 | tf_op jit(solution)/shard_map/ppermute | solution.py:57
  7.9 7.6 %collective-permute-start.5 = (bf16[256,256]{1,0:T(8,128)(2,1)S(1)}, bf16[256,256]{1,0:T(8,128)(2,1)S(1)}, u32[]{:S(2)}, u32[]{:S(2)}) collective-permute-start(bf16[256,256]{1,0:T(8,128)(2,1)S(1)} %get-tuple-element.37), channel_id=1, source_target_pairs={{0,1},{1,0},{2,3},{3,2},{4,5},{5,4},{6,7},{7,6},{8,9},{9,8},{10,11... | collective-permute-start | bytes 393224 | tf_op jit(solution)/shard_map/ppermute | solution.py:57
  9.1 6.3 %collective-permute-start.6 = (bf16[256,256]{1,0:T(8,128)(2,1)S(1)}, bf16[256,256]{1,0:T(8,128)(2,1)S(1)}, u32[]{:S(2)}, u32[]{:S(2)}) collective-permute-start(bf16[256,256]{1,0:T(8,128)(2,1)S(1)} %get-tuple-element.38), channel_id=1, source_target_pairs={{0,2},{1,3},{2,0},{3,1},{4,6},{5,7},{6,4},{7,5},{8,10},{9,11},{10,... | collective-permute-start | bytes 393224 | tf_op jit(solution)/shard_map/ppermute | solution.py:57
  13.9 17.6 %collective-permute-start.8 = (bf16[128,2048]{1,0:T(8,128)(2,1)S(1)}, bf16[128,2048]{1,0:T(8,128)(2,1)S(1)}, u32[]{:S(2)}, u32[]{:S(2)}) collective-permute-start(bf16[128,2048]{1,0:T(8,128)(2,1)S(1)} %shard_map.65.refs_0_), channel_id=1, source_target_pairs={{0,1},{1,0},{2,3},{3,2},{4,5},{5,4},{6,7},{7,6},{8,9},{9,8},{10,11... | collective-permute-start | bytes 1572872 | tf_op jit(solution)/shard_map/ppermute | solution.py:57
  14.2 17.2 %collective-permute-start.9 = (bf16[128,2048]{1,0:T(8,128)(2,1)S(1)}, bf16[128,2048]{1,0:T(8,128)(2,1)S(1)}, u32[]{:S(2)}, u32[]{:S(2)}) collective-permute-start(bf16[128,2048]{1,0:T(8,128)(2,1)S(1)} %shard_map.65.refs_0_), channel_id=1, source_target_pairs={{0,2},{1,3},{2,0},{3,1},{4,6},{5,7},{6,4},{7,5},{8,10},{9,11},{10,... | collective-permute-start | bytes 1572872 | tf_op jit(solution)/shard_map/ppermute | solution.py:57
  15.6 15.9 %collective-permute-start.7 = (bf16[256,768]{1,0:T(8,128)(2,1)S(1)}, bf16[256,768]{1,0:T(8,128)(2,1)S(1)}, u32[]{:S(2)}, u32[]{:S(2)}) collective-permute-start(bf16[256,768]{1,0:T(8,128)(2,1)S(1)} %shard_map.68.refs_6_), channel_id=1, source_target_pairs={{0,8},{1,9},{2,10},{3,11},{4,12},{5,13},{6,14},{7,15},{8,0},{9,1},... | collective-permute-start | bytes 1179656 | tf_op jit(solution)/shard_map/ppermute | solution.py:57
  24.3 7.1 %collective-permute-start.4 = (bf16[272,256]{1,0:T(8,128)(2,1)S(1)}, bf16[272,256]{1,0:T(8,128)(2,1)S(1)}, u32[]{:S(2)}, u32[]{:S(2)}) collective-permute-start(bf16[272,256]{1,0:T(8,128)(2,1)S(1)} %get-tuple-element.35), channel_id=1, source_target_pairs={{0,2},{1,3},{2,0},{3,1},{4,6},{5,7},{6,4},{7,5},{8,10},{9,11},{10,... | collective-permute-start | bytes 417800 | tf_op jit(solution)/shard_map/ppermute | solution.py:57
  24.6 6.8 %collective-permute-start.3 = (bf16[256,256]{1,0:T(8,128)(2,1)S(1)}, bf16[256,256]{1,0:T(8,128)(2,1)S(1)}, u32[]{:S(2)}, u32[]{:S(2)}) collective-permute-start(bf16[256,256]{1,0:T(8,128)(2,1)S(1)} %get-tuple-element.34), channel_id=1, source_target_pairs={{0,1},{1,0},{2,3},{3,2},{4,5},{5,4},{6,7},{7,6},{8,9},{9,8},{10,11... | collective-permute-start | bytes 393224 | tf_op jit(solution)/shard_map/ppermute | solution.py:57
  32.3 6.3 %collective-permute-start.11 = (bf16[128,2048]{1,0:T(8,128)(2,1)S(1)}, bf16[128,2048]{1,0:T(8,128)(2,1)S(1)}, u32[]{:S(2)}, u32[]{:S(2)}) collective-permute-start(bf16[128,2048]{1,0:T(8,128)(2,1)S(1)} %collective-permute-done.8.refs_1_), channel_id=1, source_target_pairs={{0,4},{1,5},{2,6},{3,7},{4,0},{5,1},{6,2},{7,3},{8,12},{9,13},{10,... | collective-permute-start | bytes 1572872 | tf_op jit(solution)/shard_map/ppermute | solution.py:57
  32.7 5.9 %collective-permute-start.12 = (bf16[128,2048]{1,0:T(8,128)(2,1)S(1)}, bf16[128,2048]{1,0:T(8,128)(2,1)S(1)}, u32[]{:S(2)}, u32[]{:S(2)}) collective-permute-start(bf16[128,2048]{1,0:T(8,128)(2,1)S(1)} %collective-permute-done.9.refs_2_), channel_id=1, source_target_pairs={{0,4},{1,5},{2,6},{3,7},{4,0},{5,1},{6,2},{7,3},{8,12},{9,13},{10,... | collective-permute-start | bytes 1572872 | tf_op jit(solution)/shard_map/ppermute | solution.py:57
  33.4 7.8 %collective-permute-start.16 = (bf16[128,1024]{1,0:T(8,128)(2,1)S(1)}, bf16[128,1024]{1,0:T(8,128)(2,1)S(1)}, u32[]{:S(2)}, u32[]{:S(2)}) collective-permute-start(bf16[128,1024]{1,0:T(8,128)(2,1)S(1)} %slice.35), channel_id=1, source_target_pairs={{0,1},{1,0},{2,3},{3,2},{4,5},{5,4},{6,7},{7,6},{8,9},{9,8},{10,11... | collective-permute-start | bytes 786440 | tf_op jit(solution)/shard_map/ppermute | solution.py:57
  36.2 7.6 %collective-permute-start.13 = (bf16[128,1024]{1,0:T(8,128)(2,1)S(1)}, bf16[128,1024]{1,0:T(8,128)(2,1)S(1)}, u32[]{:S(2)}, u32[]{:S(2)}) collective-permute-start(bf16[128,1024]{1,0:T(8,128)(2,1)S(1)} %slice.30), channel_id=1, source_target_pairs={{0,2},{1,3},{2,0},{3,1},{4,6},{5,7},{6,4},{7,5},{8,10},{9,11},{10,... | collective-permute-start | bytes 786440 | tf_op jit(solution)/shard_map/ppermute | solution.py:57
  37.0 10.0 %collective-permute-start.22 = (bf16[512,256]{1,0:T(8,128)(2,1)S(1)}, bf16[512,256]{1,0:T(8,128)(2,1)S(1)}, u32[]{:S(2)}, u32[]{:S(2)}) collective-permute-start(bf16[512,256]{1,0:T(8,128)(2,1)S(1)} %pad_maximum_fusion.1.refs_10_), channel_id=1, source_target_pairs={{0,8},{1,9},{2,10},{3,11},{4,12},{5,13},{6,14},{7,15},{8,0},{9,1},... | collective-permute-start | bytes 786440 | tf_op jit(solution)/shard_map/ppermute | solution.py:57
  47.4 12.8 %collective-permute-start.23 = (bf16[4,256,128]{2,1,0:T(8,128)(2,1)S(1)}, bf16[4,256,128]{2,1,0:T(8,128)(2,1)S(1)}, u32[]{:S(2)}, u32[]{:S(2)}) collective-permute-start(bf16[4,256,128]{2,1,0:T(8,128)(2,1)S(1)} %get-tuple-element.54.own), channel_id=1, source_target_pairs={{0,8},{1,9},{2,10},{3,11},{4,12},{5,13},{6,14},{7,15},{8,0},{9,1},... | collective-permute-start | bytes 786440 | tf_op jit(solution)/shard_map/ppermute | solution.py:57
  49.7 14.6 %collective-permute-start.24 = (bf16[4,256,128]{2,1,0:T(8,128)(2,1)S(1)}, bf16[4,256,128]{2,1,0:T(8,128)(2,1)S(1)}, u32[]{:S(2)}, u32[]{:S(2)}) collective-permute-start(bf16[4,256,128]{2,1,0:T(8,128)(2,1)S(1)} %get-tuple-element.54.own), channel_id=1, source_target_pairs={{8,16},{9,17},{10,18},{11,19},{12,20},{13,21},{14,22},{15,23},{16,... | collective-permute-start | bytes 786440 | tf_op jit(solution)/shard_map/ppermute | solution.py:57
  53.4 12.1 %collective-permute-start.28 = (bf16[2,256,128]{2,1,0:T(8,128)(2,1)S(1)}, bf16[2,256,128]{2,1,0:T(8,128)(2,1)S(1)}, u32[]{:S(2)}, u32[]{:S(2)}) collective-permute-start(bf16[2,256,128]{2,1,0:T(8,128)(2,1)S(1)} %get-tuple-element.56.own), channel_id=1, source_target_pairs={{0,8},{1,9},{2,10},{3,11},{4,12},{5,13},{6,14},{7,15},{8,0},{9,1},... | collective-permute-start | bytes 393224 | tf_op jit(solution)/shard_map/ppermute | solution.py:57
  54.8 10.7 %collective-permute-start.29 = (bf16[2,256,128]{2,1,0:T(8,128)(2,1)S(1)}, bf16[2,256,128]{2,1,0:T(8,128)(2,1)S(1)}, u32[]{:S(2)}, u32[]{:S(2)}) collective-permute-start(bf16[2,256,128]{2,1,0:T(8,128)(2,1)S(1)} %get-tuple-element.56.own), channel_id=1, source_target_pairs={{8,16},{9,17},{10,18},{11,19},{12,20},{13,21},{14,22},{15,23},{16,... | collective-permute-start | bytes 393224 | tf_op jit(solution)/shard_map/ppermute | solution.py:57
  58.6 8.4 %collective-permute-start.25 = (bf16[2,256,128]{2,1,0:T(8,128)(2,1)S(1)}, bf16[2,256,128]{2,1,0:T(8,128)(2,1)S(1)}, u32[]{:S(2)}, u32[]{:S(2)}) collective-permute-start(bf16[2,256,128]{2,1,0:T(8,128)(2,1)S(1)} %get-tuple-element.55.own), channel_id=1, source_target_pairs={{0,8},{1,9},{2,10},{3,11},{4,12},{5,13},{6,14},{7,15},{8,0},{9,1},... | collective-permute-start | bytes 393224 | tf_op jit(solution)/shard_map/ppermute | solution.py:57
  60.3 6.7 %collective-permute-start.26 = (bf16[2,256,128]{2,1,0:T(8,128)(2,1)S(1)}, bf16[2,256,128]{2,1,0:T(8,128)(2,1)S(1)}, u32[]{:S(2)}, u32[]{:S(2)}) collective-permute-start(bf16[2,256,128]{2,1,0:T(8,128)(2,1)S(1)} %get-tuple-element.55.own), channel_id=1, source_target_pairs={{8,16},{9,17},{10,18},{11,19},{12,20},{13,21},{14,22},{15,23},{16,... | collective-permute-start | bytes 393224 | tf_op jit(solution)/shard_map/ppermute | solution.py:57
  65.8 6.7 %collective-permute-start.34 = (bf16[256,128]{1,0:T(8,128)(2,1)S(1)}, bf16[256,128]{1,0:T(8,128)(2,1)S(1)}, u32[]{:S(2)}, u32[]{:S(2)}) collective-permute-start(bf16[256,128]{1,0:T(8,128)(2,1)S(1)} %shard_map.78), channel_id=1, source_target_pairs={{0,3},{1,2},{2,1},{3,0},{4,7},{5,6},{6,5},{7,4},{8,11},{9,10},{10,... | collective-permute-start | bytes 196616 | tf_op jit(solution)/shard_map/ppermute | solution.py:57
  67.2 6.1 %collective-permute-start.32 = (bf16[256,128]{1,0:T(8,128)(2,1)S(1)}, bf16[256,128]{1,0:T(8,128)(2,1)S(1)}, u32[]{:S(2)}, u32[]{:S(2)}) collective-permute-start(bf16[256,128]{1,0:T(8,128)(2,1)S(1)} %shard_map.77), channel_id=1, source_target_pairs={{0,2},{1,3},{2,0},{3,1},{4,6},{5,7},{6,4},{7,5},{8,10},{9,11},{10,... | collective-permute-start | bytes 196616 | tf_op jit(solution)/shard_map/ppermute | solution.py:57
  69.4 6.5 %collective-permute-start.27 = (bf16[256,128]{1,0:T(8,128)(2,1)S(1)}, bf16[256,128]{1,0:T(8,128)(2,1)S(1)}, u32[]{:S(2)}, u32[]{:S(2)}) collective-permute-start(bf16[256,128]{1,0:T(8,128)(2,1)S(1)} %shard_map.75.refs_0_), channel_id=1, source_target_pairs={{0,4},{1,5},{2,6},{3,7},{4,0},{5,1},{6,2},{7,3},{8,12},{9,13},{10,... | collective-permute-start | bytes 196616 | tf_op jit(solution)/shard_map/ppermute | solution.py:57
  (19 other events, 45.6 us)

commit v7 on v6

--- a/solution.py
+++ b/solution.py
@@ -82,7 +82,7 @@
     return tm >> 1, tm & 1, lax.axis_index("depth")
 
 
-def edge_kernel(mask, raw, to_x, to_across, flags_ref):
+def edge_kernel(mask, raw, to_x, to_across, flags_ref, sites_ref):
     _, _, depth = where_am_i()
     odd = depth & 1
     lane = lax.broadcasted_iota(jnp.int32, (EXTRA, HD), 1)
@@ -91,6 +91,7 @@
         flags = jnp.where(lane == entry, mask[entry], flags)
     flags = flags.astype(jnp.float32).astype(jnp.bfloat16)
     flags_ref[...] = flags
+    sites_ref[...] = raw[...]
     values = raw[...].astype(jnp.float32)
     first, last = values[:, 0], values[:, values.shape[1] - 1]
     for ref, use_last in ((to_x, odd == 0), (to_across, depth == 1)):
@@ -107,8 +108,12 @@
     keep[...] = jnp.where(even, low, high)
 
 
-def split_far_kernel(w, flags, to_x, to_y, keep):
-    split_kernel(w, to_x, to_y, keep)
+def split_far_kernel(w, flags, to_y, keep):
+    _, _, depth = where_am_i()
+    even = (depth & 1) == 0
+    low, high = w[:, :PAIR], w[:, 2 * PAIR :]
+    to_y[: w.shape[0]] = jnp.where(even, high, low)
+    keep[...] = jnp.where(even, low, high)
     to_y[w.shape[0] :, :HD] = flags[...]
     to_y[w.shape[0] :, HD:] = flags[...]
 
@@ -132,13 +137,10 @@
         out_ref[:, (3 + third) * HD : (4 + third) * HD] = other
 
 
-def sort_far_kernel(kept, from_x, from_y, edge_x, edge_across, own_flags, q_ref, kv_ref, send_ref, flags_ref):
+def sort_far_kernel(kept, from_x, from_y, edge_x, edge_across, own_flags, keep_ref, send_ref, flags_ref):
     for third, mine, other in sorted_groups(kept, from_x, from_y):
         send_ref[:, third * HD : (third + 1) * HD] = other
-        if third:
-            kv_ref[:, (third - 1) * HD : third * HD] = mine
-        else:
-            q_ref[...] = mine
+        keep_ref[:, third * HD : (third + 1) * HD] = mine
     row = lax.broadcasted_iota(jnp.int32, (EXTRA, HD), 0)
     flags = own_flags[...].astype(jnp.float32)
     for r, value in ((1, edge_x[EXTRA:]), (2, from_y[kept.shape[0] :, :HD]), (3, edge_across[EXTRA:])):
@@ -148,23 +150,32 @@
         flags_ref[:, k * HD : (k + 1) * HD] = flags
 
 
-def embed_kernel(edge_x, edge_across, gain, raw, stream, conv_w, out_ref, acc):
+def embed_kernel(edge_x, edge_across, raw, gain, stream, conv_w, out_ref, acc, tokens, weights, sems):
     time_len, site_len, feat_len = raw.shape
     _, _, depth = where_am_i()
     even = (depth & 1) == 0
     rows, width = stream.shape
+    parts = weights.shape[0]
+    step = width // parts
+    copies = []
+    for i in range(parts):
+        here = pl.ds(i * step, step)
+        copies.append(pltpu.make_async_copy(conv_w.at[:, here], weights.at[i], sems.at[2 * i]))
+        copies.append(pltpu.make_async_copy(stream.at[:, here], tokens.at[i], sems.at[2 * i + 1]))
+    for copy in copies:
+        copy.start()
     side, far = edge_x[:time_len].astype(jnp.float32), edge_across[:time_len].astype(jnp.float32)
     before = jnp.where(even, jnp.where(depth == 2, far, 0.0), side)
     behind = jnp.where(even, side, jnp.where(depth == 1, far, 0.0))
     padded = jnp.concatenate([before[:, None], raw[...].astype(jnp.float32), behind[:, None]], axis=1)
     windows = [padded[:, j : j + site_len].reshape(rows, feat_len).astype(jnp.bfloat16) for j in range(3)]
     windows = jnp.concatenate(windows, axis=1)
-    total, step = jnp.zeros((rows, 1), jnp.float32), width // 4
-    for at in range(0, width, step):
-        here = slice(at, at + step)
-        part = jnp.dot(windows, conv_w[:, here], preferred_element_type=jnp.float32)
-        part += stream[:, here].astype(jnp.float32)
-        acc[:, here] = part
+    total = jnp.zeros((rows, 1), jnp.float32)
+    for i in range(parts):
+        copies[2 * i].wait()
+        copies[2 * i + 1].wait()
+        part = jnp.dot(windows, weights[i], preferred_element_type=jnp.float32) + tokens[i].astype(jnp.float32)
+        acc[:, i * step : (i + 1) * step] = part
         total += jnp.sum(part * part, axis=1, keepdims=True)
     scale = lax.rsqrt(total / width + 1e-05)
     out_ref[...] = (acc[...] * scale * gain[...]).astype(jnp.bfloat16)
@@ -176,17 +187,17 @@
     return jnp.concatenate([jnp.concatenate([ref[:, at] for at in cuts], axis=1) for ref in refs], axis=0)
 
 
-def three_shards(x_refs, own, near, received, far_q, far_kv):
+def three_shards(x_refs, own, near, received, far):
     z, core, _ = where_am_i()
     size, width = own.shape[0], 3 * HD
-    w = [own[:, :width], received[:size], jnp.concatenate([far_q[...], far_kv[...]], axis=1)]
+    w = [own[:, :width], received[:size], far[...]]
     w = jnp.concatenate(w + [near[:, :width], received[size : 2 * size]], axis=0)
     x = [take(x_refs, source, core, 2 * size) for source in (z, z ^ 2, z ^ 1)]
     return jnp.dot(jnp.concatenate(x, axis=1), w, preferred_element_type=jnp.float32)
 
 
 def partial_kernel(*refs):
-    refs[-1][...] = three_shards(refs[:6], *refs[6:-1])
+    refs[-1][...] = three_shards(refs[:2], *refs[2:-1])
 
 
 def diagonal_kernel(*refs):
@@ -201,30 +212,22 @@
 ROW_ORDER = ((0, 1, 2, 6), (3, 4, 5, 7))
 
 
-def finish(x_refs, last, acc_in, acc_diagonal, columns):
+def finish_kernel(*refs):
+    x_refs, (last, acc_in, acc_diagonal, q_ref, k_ref, v_first, v_second) = refs[:3], refs[3:]
     z, core, _ = where_am_i()
+    block, early = q_ref.shape[1] // 2, acc_in.shape[0]
     value = jnp.dot(take(x_refs, z ^ 3, core, last.shape[0]), last[...], preferred_element_type=jnp.float32)
-    early = acc_in.shape[0]
-    return (
-        (acc_in[:, columns] + value[:early]).astype(jnp.bfloat16),
-        (acc_diagonal[:, columns] + value[early:]).astype(jnp.bfloat16),
-    )
-
-
-def finish_kernel(columns, *refs):
-    x_refs, (last, acc_in, acc_diagonal), out_refs = refs[:7], refs[7:10], refs[10:]
-    _, core, _ = where_am_i()
-    block = x_refs[0].shape[0]
-    values = jnp.concatenate(finish(x_refs, last, acc_in, acc_diagonal, columns), axis=0)
+    value = [acc_in[...] + value[:early], acc_diagonal[...] + value[early:]]
+    value = jnp.concatenate(value, axis=0).astype(jnp.bfloat16)
     for rel in range(2):
         at = pl.ds(pl.multiple_of((core ^ rel) * block, block), block)
         for r in range(4):
             row = ROW_ORDER[rel][r]
-            value = values[row * block : (row + 1) * block]
-            out_refs[0][r, at, :] = value[:, :HD]
-            if len(out_refs) > 1:
-                v_at = V_ORDER.index(r)
-                out_refs[1 + v_at // 2][v_at % 2, at, :] = value[:, HD:]
+            mine = value[row * block : (row + 1) * block]
+            v_at = V_ORDER.index(r)
+            q_ref[r, at, :] = mine[:, :HD]
+            k_ref[r, at, :] = mine[:, HD:PAIR]
+            (v_first, v_second)[v_at // 2][v_at % 2, at, :] = mine[:, PAIR:]
 
 
 def spans(u):
@@ -286,8 +289,8 @@
         out_ref[:, pl.ds(at, HD)] = ref[mine, :]
 
 
-def call(kernel, outs, places, scratch=(), macs=0):
-    spaces = {"s": SMEM, "v": VMEM}
+def call(kernel, outs, places, scratch=(), macs=0, limit=32):
+    spaces = {"s": SMEM, "v": VMEM, "a": pl.ANY}
     return pl.pallas_call(
         kernel,
         out_shape=outs,
@@ -295,7 +298,7 @@
         out_specs=jax.tree.map(lambda _: pl.BlockSpec(memory_space=VMEM), outs),
         scratch_shapes=list(scratch),
         cost_estimate=pl.CostEstimate(flops=2 * macs, bytes_accessed=0, transcendentals=0),
-        compiler_params=pltpu.CompilerParams(vmem_limit_bytes=32 * 2**20),
+        compiler_params=pltpu.CompilerParams(vmem_limit_bytes=limit * 2**20),
     )
 
 
@@ -315,47 +318,53 @@
     own = call(sort_kernel, array(size, 6 * HD), "vvv")(kept, swap_depth(to_x, 1), swap_depth(to_y, 2))
     near = swap_z(own, 1)
 
-    edge_x, edge_across, own_flags = call(
-        edge_kernel, (array(2 * EXTRA, HD), array(2 * EXTRA, HD), array(EXTRA, HD)), "sv"
+    edge_x, edge_across, own_flags, sites = call(
+        edge_kernel, (array(2 * EXTRA, HD), array(2 * EXTRA, HD), array(EXTRA, HD), array(*raw.shape)), "sv"
     )(mask.reshape(mask.shape[2]), raw)
     edge_x, edge_across = swap_depth(edge_x, 1), swap_depth(edge_across, 3)
+    parts = 4
     normed = call(
         embed_kernel,
         array(block, width),
-        "v" * 6,
-        scratch=[VMEM((block, width), f32)],
+        "vvvvaa",
+        scratch=[
+            VMEM((block, width), f32),
+            VMEM((parts, block, width // parts), bf16),
+            VMEM((parts, 3 * feat_len, width // parts), bf16),
+            pltpu.SemaphoreType.DMA((2 * parts,)),
+        ],
         macs=block * 3 * feat_len * width,
+        limit=53,
     )(
         edge_x,
         edge_across,
+        sites,
         gain.reshape(1, width),
-        raw,
         stream.reshape(block, width),
         conv_w.reshape(3 * feat_len, width),
     )
     beside, above = swap_depth(normed, 1), swap_depth(normed, 2)
 
-    to_x, to_y, kept = call(split_far_kernel, (cut, cut_more, cut), "vv")(far_raw, own_flags)
+    to_y, kept = call(split_far_kernel, (cut_more, cut), "vv")(far_raw, own_flags)
+    to_x = far_raw[:, PAIR : 2 * PAIR]
     from_x, from_y = swap_depth(to_x, 1), swap_depth(to_y, 2)
-    from_x, from_y, near, beside, above = lax.optimization_barrier((from_x, from_y, near, beside, above))
-    keep_q, keep_kv, send, flags = call(
+    keep, send, flags = call(
         sort_far_kernel,
-        (array(size, HD), array(size, PAIR), array(size, 3 * HD), array(EXTRA, 3 * HD)),
+        (array(size, 3 * HD), array(size, 3 * HD), array(EXTRA, 3 * HD)),
         "v" * 6,
     )(kept, from_x, from_y, edge_x, edge_across, own_flags)
-    received = swap_core(send)
-    far_q = jnp.concatenate([keep_q, received[:, :HD]], axis=0)
-    far_kv = jnp.concatenate([keep_kv, received[:, HD:]], axis=0)
-    last_kv = swap_z(far_kv, 1)
-    last_q = swap_z(far_q, 1)
+    send, near, beside, above = lax.optimization_barrier((send, near, beside, above))
+    far = jnp.concatenate([keep, swap_core(send)], axis=0)
+    last = swap_z(far, 1)
+    stack = jnp.concatenate([normed, beside, above], axis=0)
+    far, near, stack = lax.optimization_barrier((far, near, stack))
     received = swap_core(jnp.concatenate([own[:, 3 * HD :], near[:, 3 * HD :], flags], axis=0))
-    weights = (own, near, received, far_q, far_kv)
-    opposite = swap_core(after(normed, near))
+    weights = (own, near, received, far)
+    early = (stack, swap_core(stack))
 
     diagonal = [swap_depth(beside[:, :half], 2), swap_depth(above[:, half:], 1)]
-    early = (normed, beside, above, opposite, swap_core(beside), swap_core(above))
     rows = 2 * size
-    total = call(partial_kernel, array(6 * block, 3 * HD, kind=f32), "v" * 11, macs=6 * block * 3 * rows * 3 * HD)(
+    total = call(partial_kernel, array(6 * block, 3 * HD, kind=f32), "v" * 6, macs=6 * block * 3 * rows * 3 * HD)(
         *early, *weights
     )
     diagonal = [after(t, total) for t in diagonal]
@@ -363,19 +372,13 @@
     total_diagonal, diagonal = call(
         diagonal_kernel,
         (array(2 * block, 3 * HD, kind=f32), array(2 * block, width)),
-        "v" * 11,
+        "v" * 10,
         macs=2 * block * 3 * rows * 3 * HD,
     )(*diagonal, *weights)
     one_head, half_head = array(4, 2 * block, HD), array(2, 2 * block, HD)
-    k, *v = call(
-        functools.partial(finish_kernel, slice(HD, 3 * HD)),
-        (one_head, half_head, half_head),
-        "v" * 10,
-        macs=8 * block * rows * 2 * HD,
-    )(*early, diagonal, last_kv, total, total_diagonal)
-    (q,) = call(functools.partial(finish_kernel, slice(0, HD)), (one_head,), "v" * 10, macs=8 * block * rows * HD)(
-        *early, diagonal, last_q, total, total_diagonal
-    )
+    q, k, *v = call(
+        finish_kernel, (one_head, one_head, half_head, half_head), "v" * 6, macs=8 * block * rows * 3 * HD
+    )(*early, diagonal, last, total, total_diagonal)
 
     weights = call(weigh_kernel, array(4, 2 * block, 5 * block), "v" * 6, macs=8 * block * 5 * block * HD)(
         q, swap_z(k, 1), k, swap_middle(k), flags, received

time: 77.9 us -> 72.4 us (0.929)
  starting transfers between devices: 41.1 us -> 37.4 us
  local copies, waits for them, and re-layouts: 6.47 us -> 3.31 us
  Pallas kernels: 7.31 us -> 8.95 us
    ppermute x36 -> x33, starting transfers between devices: 41.1 us -> 37.4 us  [hop(): return lax.ppermute(value, ('tm', 'depth'), pairs)]
    unnamed x14 -> x9, local copies, waits for them, and re-layouts: 6.34 us -> 3.16 us
    pallas_call x6 -> x5, Pallas kernels: 3.03 us -> 4.66 us  [the longest x1 2.42 us: plane_device(): call(embed_kernel, array(block, width), 'vvvvaa', scratch=[VMEM((block, w...]
    ppermute x36 -> x33, waiting for transfers between devices: 22.3 us -> 22 us  [hop(): return lax.ppermute(value, ('tm', 'depth'), pairs)]
  transfers between devices with their start and end apart: 36 -> 33, of which waited for: 9 -> 11; matrix products, arithmetic and copies ran while one was open for 0% -> 0% of each run, Pallas kernels for 7% -> 10%
where the time goes in v7:
time: 72.4 us; the launch traced here: 72 us
  starting transfers between devices  37.4 us (52%)
  waiting for transfers between devices  22 us (30%)
  Pallas kernels  8.95 us (12%)
  local copies, waits for them, and re-layouts  3.31 us (5%)
    ppermute x33, starting transfers between devices, hop(): return lax.ppermute(value, ('tm', 'depth'), pairs)  37.4 us
    ppermute x33, waiting for transfers between devices, hop(): return lax.ppermute(value, ('tm', 'depth'), pairs)  22 us
    unnamed x9, local copies, waits for them, and re-layouts  3.16 us
    pallas_call x1, Pallas kernels, plane_device(): call(embed_kernel, array(block, width), 'vvvvaa', scratch=[VMEM((block, w...  2.42 us
  transfers between devices with their start and end apart: 33, of which 11 were waited for; matrix products, arithmetic and copies ran while one was open for 0% of the time, Pallas kernels for 10%

profile of v7, /device:TPU:9, one launch (start us, length us, event | category | flops | bytes accessed | tf_op | source)
XLA Modules:
  0.0 72.0 jit_solution(17410718373570119229)
XLA Ops:
  2.0 1.3 %collective-permute-start.3 = (bf16[32,128]{1,0:T(8,128)(2,1)S(1)}, bf16[32,128]{1,0:T(8,128)(2,1)S(1)}, u32[]{:S(2)}, u32[]{:S(2)}) collective-permute-start(bf16[32,128]{1,0:T(8,128)(2,1)S(1)} %get-tuple-element.35), channel_id=1, source_target_pairs={{0,1},{1,0},{2,3},{3,2},{4,5},{5,4},{6,7},{7,6},{8,9},{9,8},{10,11... | collective-permute-start | bytes 24584 | tf_op jit(solution)/shard_map/ppermute | solution.py:57
  3.3 1.2 %collective-permute-start.4 = (bf16[32,128]{1,0:T(8,128)(2,1)S(1)}, bf16[32,128]{1,0:T(8,128)(2,1)S(1)}, u32[]{:S(2)}, u32[]{:S(2)}) collective-permute-start(bf16[32,128]{1,0:T(8,128)(2,1)S(1)} %get-tuple-element.36), channel_id=1, source_target_pairs={{0,3},{1,2},{2,1},{3,0},{4,7},{5,6},{6,5},{7,4},{8,11},{9,10},{10,... | collective-permute-start | bytes 24584 | tf_op jit(solution)/shard_map/ppermute | solution.py:57
  4.5 2.3 %collective-permute-start = (bf16[256,768]{1,0:T(8,128)(2,1)}, bf16[256,768]{1,0:T(8,128)(2,1)S(1)}, u32[]{:S(2)}, u32[]{:S(2)}) collective-permute-start(bf16[256,768]{1,0:T(8,128)(2,1)} %w.1), channel_id=1, source_target_pairs={{0,16},{1,17},{2,18},{3,19},{4,20},{5,21},{6,22},{7,23},{8,24},{9,... | collective-permute-start | bytes 1179656 | tf_op jit(solution)/shard_map/ppermute | solution.py:57
  7.9 1.3 %collective-permute-start.5 = (bf16[256,256]{1,0:T(8,128)(2,1)S(1)}, bf16[256,256]{1,0:T(8,128)(2,1)S(1)}, u32[]{:S(2)}, u32[]{:S(2)}) collective-permute-start(bf16[256,256]{1,0:T(8,128)(2,1)S(1)} %get-tuple-element.40), channel_id=1, source_target_pairs={{0,1},{1,0},{2,3},{3,2},{4,5},{5,4},{6,7},{7,6},{8,9},{9,8},{10,11... | collective-permute-start | bytes 393224 | tf_op jit(solution)/shard_map/ppermute | solution.py:57
  10.1 2.4 %shard_map.69 = bf16[128,2048]{1,0:T(8,128)(2,1)S(1)} custom-call(bf16[32,128]{1,0:T(8,128)(2,1)S(1)} %collective-permute-done.3.edge_x, bf16[32,128]{1,0:T(8,128)(2,1)S(1)} %collective-permute-done.4.edge_across, bf16[16,8,128]{2,1,0:T(8,128)(2,1)S(1)} %get-tuple-element.42.raw, f32[1,2048]{1,0:T(1,128)S(1)} %bitcast.5, bf16[128,2048]{1,0:T(8,128)(2,1)} %bitcast.8, ...), custom_call_target="tpu_custom_call" | custom-call | flops 201326592 | tf_op jit(solution)/shard_map/pallas_call | solution.py:326
  12.8 1.2 %collective-permute-start.9 = (bf16[128,2048]{1,0:T(8,128)(2,1)S(1)}, bf16[128,2048]{1,0:T(8,128)(2,1)S(1)}, u32[]{:S(2)}, u32[]{:S(2)}) collective-permute-start(bf16[128,2048]{1,0:T(8,128)(2,1)S(1)} %shard_map.69), channel_id=1, source_target_pairs={{0,2},{1,3},{2,0},{3,1},{4,6},{5,7},{6,4},{7,5},{8,10},{9,11},{10,... | collective-permute-start | bytes 1572872 | tf_op jit(solution)/shard_map/ppermute | solution.py:57
  14.4 9.9 %collective-permute-done.w = bf16[256,768]{1,0:T(8,128)(2,1)S(1)} collective-permute-done((bf16[256,768]{1,0:T(8,128)(2,1)}, bf16[256,768]{1,0:T(8,128)(2,1)S(1)}, u32[]{:S(2)}, u32[]{:S(2)}) %collective-permute-start) | collective-permute-done | bytes 393248 | tf_op jit(solution)/shard_map/ppermute | solution.py:57
  24.6 1.3 %collective-permute-start.1 = (bf16[256,256]{1,0:T(8,128)(2,1)S(1)}, bf16[256,256]{1,0:T(8,128)(2,1)S(1)}, u32[]{:S(2)}, u32[]{:S(2)}) collective-permute-start(bf16[256,256]{1,0:T(8,128)(2,1)S(1)} %slice.36), channel_id=1, source_target_pairs={{0,1},{1,0},{2,3},{3,2},{4,5},{5,4},{6,7},{7,6},{8,9},{9,8},{10,11... | collective-permute-start | bytes 393224 | tf_op jit(solution)/shard_map/ppermute | solution.py:57
  25.9 3.0 %collective-permute-done.1.from_x = bf16[256,256]{1,0:T(8,128)(2,1)S(1)} collective-permute-done((bf16[256,256]{1,0:T(8,128)(2,1)S(1)}, bf16[256,256]{1,0:T(8,128)(2,1)S(1)}, u32[]{:S(2)}, u32[]{:S(2)}) %collective-permute-start.1) | collective-permute-done | bytes 131104 | tf_op jit(solution)/shard_map/ppermute | solution.py:57
  29.6 1.5 %collective-permute-start.10 = (bf16[256,384]{1,0:T(8,128)(2,1)S(1)}, bf16[256,384]{1,0:T(8,128)(2,1)S(1)}, u32[]{:S(2)}, u32[]{:S(2)}) collective-permute-start(bf16[256,384]{1,0:T(8,128)(2,1)S(1)} %get-tuple-element.43), channel_id=1, source_target_pairs={{0,4},{1,5},{2,6},{3,7},{4,0},{5,1},{6,2},{7,3},{8,12},{9,13},{10,... | collective-permute-start | bytes 589832 | tf_op jit(solution)/shard_map/ppermute | solution.py:57
  32.9 1.3 %collective-permute-start.14 = (bf16[128,1024]{1,0:T(8,128)(2,1)S(1)}, bf16[128,1024]{1,0:T(8,128)(2,1)S(1)}, u32[]{:S(2)}, u32[]{:S(2)}) collective-permute-start(bf16[128,1024]{1,0:T(8,128)(2,1)S(1)} %slice.31), channel_id=1, source_target_pairs={{0,1},{1,0},{2,3},{3,2},{4,5},{5,4},{6,7},{7,6},{8,9},{9,8},{10,11... | collective-permute-start | bytes 786440 | tf_op jit(solution)/shard_map/ppermute | solution.py:57
  35.3 1.4 %collective-permute-start.19 = (bf16[512,384]{1,0:T(8,128)(2,1)S(1)}, bf16[512,384]{1,0:T(8,128)(2,1)S(1)}, u32[]{:S(2)}, u32[]{:S(2)}) collective-permute-start(bf16[512,384]{1,0:T(8,128)(2,1)S(1)} %constant_dynamic-update-slice_fusion.refs_5_.refs_9_), channel_id=1, source_target_pairs={{0,8},{1,9},{2,10},{3,11},{4,12},{5,13},{6,14},{7,15},{8,0},{9,1},... | collective-permute-start | bytes 1179656 | tf_op jit(solution)/shard_map/ppermute | solution.py:57
  36.7 1.4 %shard_map.70.refs_4_ = f32[768,384]{1,0:T(8,128)S(1)} custom-call(bf16[384,2048]{1,0:T(8,128)(2,1)S(1)} %pad_maximum_fusion.refs_0_, bf16[384,2048]{1,0:T(8,128)(2,1)S(1)} %collective-permute-done.11.refs_1_, bf16[256,768]{1,0:T(8,128)(2,1)S(1)} %shard_map.68.refs_2_.refs_6_, bf16[256,768]{1,0:T(8,128)(2,1)S(1)} %collective-permute-done.7.refs_3_.refs_7_, ...), custom_call_target="tpu_custom_call" | custom-call | flops 905969664 | tf_op jit(solution)/shard_map/pallas_call | solution.py:367
  38.1 2.4 %collective-permute-done.14.refs_1_ = bf16[128,1024]{1,0:T(8,128)(2,1)S(1)} collective-permute-done((bf16[128,1024]{1,0:T(8,128)(2,1)S(1)}, bf16[128,1024]{1,0:T(8,128)(2,1)S(1)}, u32[]{:S(2)}, u32[]{:S(2)}) %collective-permute-start.14) | collective-permute-done | bytes 262176 | tf_op jit(solution)/shard_map/ppermute | solution.py:57
  40.5 1.3 %collective-permute-start.17 = (bf16[64,1024]{1,0:T(8,128)(2,1)S(1)}, bf16[64,1024]{1,0:T(8,128)(2,1)S(1)}, u32[]{:S(2)}, u32[]{:S(2)}) collective-permute-start(bf16[64,1024]{1,0:T(8,128)(2,1)S(1)} %get-tuple-element.60), channel_id=1, source_target_pairs={{0,4},{1,5},{2,6},{3,7},{4,0},{5,1},{6,2},{7,3},{8,12},{9,13},{10,... | collective-permute-start | bytes 393224 | tf_op jit(solution)/shard_map/ppermute | solution.py:57
  45.8 2.3 %collective-permute-start.20 = (bf16[4,256,128]{2,1,0:T(8,128)(2,1)S(1)}, bf16[4,256,128]{2,1,0:T(8,128)(2,1)S(1)}, u32[]{:S(2)}, u32[]{:S(2)}) collective-permute-start(bf16[4,256,128]{2,1,0:T(8,128)(2,1)S(1)} %get-tuple-element.56.own), channel_id=1, source_target_pairs={{0,8},{1,9},{2,10},{3,11},{4,12},{5,13},{6,14},{7,15},{8,0},{9,1},... | collective-permute-start | bytes 786440 | tf_op jit(solution)/shard_map/ppermute | solution.py:57
  48.1 3.1 %collective-permute-start.21 = (bf16[4,256,128]{2,1,0:T(8,128)(2,1)S(1)}, bf16[4,256,128]{2,1,0:T(8,128)(2,1)S(1)}, u32[]{:S(2)}, u32[]{:S(2)}) collective-permute-start(bf16[4,256,128]{2,1,0:T(8,128)(2,1)S(1)} %get-tuple-element.56.own), channel_id=1, source_target_pairs={{8,16},{9,17},{10,18},{11,19},{12,20},{13,21},{14,22},{15,23},{16,... | collective-permute-start | bytes 786440 | tf_op jit(solution)/shard_map/ppermute | solution.py:57
  51.3 2.2 %collective-permute-start.26 = (bf16[2,256,128]{2,1,0:T(8,128)(2,1)S(1)}, bf16[2,256,128]{2,1,0:T(8,128)(2,1)S(1)}, u32[]{:S(2)}, u32[]{:S(2)}) collective-permute-start(bf16[2,256,128]{2,1,0:T(8,128)(2,1)S(1)} %get-tuple-element.58.own), channel_id=1, source_target_pairs={{8,16},{9,17},{10,18},{11,19},{12,20},{13,21},{14,22},{15,23},{16,... | collective-permute-start | bytes 393224 | tf_op jit(solution)/shard_map/ppermute | solution.py:57
  53.5 3.1 %collective-permute-start.23 = (bf16[2,256,128]{2,1,0:T(8,128)(2,1)S(1)}, bf16[2,256,128]{2,1,0:T(8,128)(2,1)S(1)}, u32[]{:S(2)}, u32[]{:S(2)}) collective-permute-start(bf16[2,256,128]{2,1,0:T(8,128)(2,1)S(1)} %get-tuple-element.57.own), channel_id=1, source_target_pairs={{8,16},{9,17},{10,18},{11,19},{12,20},{13,21},{14,22},{15,23},{16,... | collective-permute-start | bytes 393224 | tf_op jit(solution)/shard_map/ppermute | solution.py:57
  56.7 1.2 %shard_map.73.weights = bf16[4,256,640]{2,1,0:T(8,128)(2,1)S(1)} custom-call(bf16[4,256,128]{2,1,0:T(8,128)(2,1)S(1)} %get-tuple-element.55.q_ref, bf16[4,256,128]{2,1,0:T(8,128)(2,1)S(1)} %collective-permute-done.20.outer, bf16[4,256,128]{2,1,0:T(8,128)(2,1)S(1)} %get-tuple-element.56.own, bf16[4,256,128]{2,1,0:T(8,128)(2,1)S(1)} %collective-permute-done.21.middle, ...), custom_call_target="tpu_custom_call" | custom-call | flops 167772160 | tf_op jit(solution)/shard_map/pallas_call | solution.py:383
  57.9 1.3 %collective-permute-done.26.middle = bf16[2,256,128]{2,1,0:T(8,128)(2,1)S(1)} collective-permute-done((bf16[2,256,128]{2,1,0:T(8,128)(2,1)S(1)}, bf16[2,256,128]{2,1,0:T(8,128)(2,1)S(1)}, u32[]{:S(2)}, u32[]{:S(2)}) %collective-permute-start.26) | collective-permute-done | bytes 131104 | tf_op jit(solution)/shard_map/ppermute | solution.py:57
  60.2 1.7 %collective-permute-done.23.middle = bf16[2,256,128]{2,1,0:T(8,128)(2,1)S(1)} collective-permute-done((bf16[2,256,128]{2,1,0:T(8,128)(2,1)S(1)}, bf16[2,256,128]{2,1,0:T(8,128)(2,1)S(1)}, u32[]{:S(2)}, u32[]{:S(2)}) %collective-permute-start.23) | collective-permute-done | bytes 131104 | tf_op jit(solution)/shard_map/ppermute | solution.py:57
  63.9 3.8 %collective-permute-start.24 = (bf16[256,128]{1,0:T(8,128)(2,1)S(1)}, bf16[256,128]{1,0:T(8,128)(2,1)S(1)}, u32[]{:S(2)}, u32[]{:S(2)}) collective-permute-start(bf16[256,128]{1,0:T(8,128)(2,1)S(1)} %shard_map.74.refs_0_), channel_id=1, source_target_pairs={{0,4},{1,5},{2,6},{3,7},{4,0},{5,1},{6,2},{7,3},{8,12},{9,13},{10,... | collective-permute-start | bytes 196616 | tf_op jit(solution)/shard_map/ppermute | solution.py:57
  69.1 1.3 %collective-permute-start.28 = (bf16[256,128]{1,0:T(8,128)(2,1)S(1)}, bf16[256,128]{1,0:T(8,128)(2,1)S(1)}, u32[]{:S(2)}, u32[]{:S(2)}) collective-permute-start(bf16[256,128]{1,0:T(8,128)(2,1)S(1)} %collective-permute-done.27.refs_2_), channel_id=1, source_target_pairs={{0,4},{1,5},{2,6},{3,7},{4,0},{5,1},{6,2},{7,3},{8,12},{9,13},{10,... | collective-permute-start | bytes 196616 | tf_op jit(solution)/shard_map/ppermute | solution.py:57
  (76 shorter events, 18.7 us)
Async XLA Ops:
  2.0 7.4 %collective-permute-start.3 = (bf16[32,128]{1,0:T(8,128)(2,1)S(1)}, bf16[32,128]{1,0:T(8,128)(2,1)S(1)}, u32[]{:S(2)}, u32[]{:S(2)}) collective-permute-start(bf16[32,128]{1,0:T(8,128)(2,1)S(1)} %get-tuple-element.35), channel_id=1, source_target_pairs={{0,1},{1,0},{2,3},{3,2},{4,5},{5,4},{6,7},{7,6},{8,9},{9,8},{10,11... | collective-permute-start | bytes 24584 | tf_op jit(solution)/shard_map/ppermute | solution.py:57
  3.3 6.1 %collective-permute-start.4 = (bf16[32,128]{1,0:T(8,128)(2,1)S(1)}, bf16[32,128]{1,0:T(8,128)(2,1)S(1)}, u32[]{:S(2)}, u32[]{:S(2)}) collective-permute-start(bf16[32,128]{1,0:T(8,128)(2,1)S(1)} %get-tuple-element.36), channel_id=1, source_target_pairs={{0,3},{1,2},{2,1},{3,0},{4,7},{5,6},{6,5},{7,4},{8,11},{9,10},{10,... | collective-permute-start | bytes 24584 | tf_op jit(solution)/shard_map/ppermute | solution.py:57
  4.5 19.8 %collective-permute-start = (bf16[256,768]{1,0:T(8,128)(2,1)}, bf16[256,768]{1,0:T(8,128)(2,1)S(1)}, u32[]{:S(2)}, u32[]{:S(2)}) collective-permute-start(bf16[256,768]{1,0:T(8,128)(2,1)} %w.1), channel_id=1, source_target_pairs={{0,16},{1,17},{2,18},{3,19},{4,20},{5,21},{6,22},{7,23},{8,24},{9,... | collective-permute-start | bytes 1179656 | tf_op jit(solution)/shard_map/ppermute | solution.py:57
  7.9 6.2 %collective-permute-start.5 = (bf16[256,256]{1,0:T(8,128)(2,1)S(1)}, bf16[256,256]{1,0:T(8,128)(2,1)S(1)}, u32[]{:S(2)}, u32[]{:S(2)}) collective-permute-start(bf16[256,256]{1,0:T(8,128)(2,1)S(1)} %get-tuple-element.40), channel_id=1, source_target_pairs={{0,1},{1,0},{2,3},{3,2},{4,5},{5,4},{6,7},{7,6},{8,9},{9,8},{10,11... | collective-permute-start | bytes 393224 | tf_op jit(solution)/shard_map/ppermute | solution.py:57
  9.1 4.9 %collective-permute-start.6 = (bf16[256,256]{1,0:T(8,128)(2,1)S(1)}, bf16[256,256]{1,0:T(8,128)(2,1)S(1)}, u32[]{:S(2)}, u32[]{:S(2)}) collective-permute-start(bf16[256,256]{1,0:T(8,128)(2,1)S(1)} %get-tuple-element.41), channel_id=1, source_target_pairs={{0,2},{1,3},{2,0},{3,1},{4,6},{5,7},{6,4},{7,5},{8,10},{9,11},{10,... | collective-permute-start | bytes 393224 | tf_op jit(solution)/shard_map/ppermute | solution.py:57
  12.5 17.1 %collective-permute-start.8 = (bf16[128,2048]{1,0:T(8,128)(2,1)S(1)}, bf16[128,2048]{1,0:T(8,128)(2,1)S(1)}, u32[]{:S(2)}, u32[]{:S(2)}) collective-permute-start(bf16[128,2048]{1,0:T(8,128)(2,1)S(1)} %shard_map.69), channel_id=1, source_target_pairs={{0,1},{1,0},{2,3},{3,2},{4,5},{5,4},{6,7},{7,6},{8,9},{9,8},{10,11... | collective-permute-start | bytes 1572872 | tf_op jit(solution)/shard_map/ppermute | solution.py:57
  12.8 16.7 %collective-permute-start.9 = (bf16[128,2048]{1,0:T(8,128)(2,1)S(1)}, bf16[128,2048]{1,0:T(8,128)(2,1)S(1)}, u32[]{:S(2)}, u32[]{:S(2)}) collective-permute-start(bf16[128,2048]{1,0:T(8,128)(2,1)S(1)} %shard_map.69), channel_id=1, source_target_pairs={{0,2},{1,3},{2,0},{3,1},{4,6},{5,7},{6,4},{7,5},{8,10},{9,11},{10,... | collective-permute-start | bytes 1572872 | tf_op jit(solution)/shard_map/ppermute | solution.py:57
  14.2 15.4 %collective-permute-start.7 = (bf16[256,768]{1,0:T(8,128)(2,1)S(1)}, bf16[256,768]{1,0:T(8,128)(2,1)S(1)}, u32[]{:S(2)}, u32[]{:S(2)}) collective-permute-start(bf16[256,768]{1,0:T(8,128)(2,1)S(1)} %shard_map.68.refs_2_.refs_6_), channel_id=1, source_target_pairs={{0,8},{1,9},{2,10},{3,11},{4,12},{5,13},{6,14},{7,15},{8,0},{9,1},... | collective-permute-start | bytes 1179656 | tf_op jit(solution)/shard_map/ppermute | solution.py:57
  24.3 4.8 %collective-permute-start.2 = (bf16[272,256]{1,0:T(8,128)(2,1)S(1)}, bf16[272,256]{1,0:T(8,128)(2,1)S(1)}, u32[]{:S(2)}, u32[]{:S(2)}) collective-permute-start(bf16[272,256]{1,0:T(8,128)(2,1)S(1)} %get-tuple-element.34), channel_id=1, source_target_pairs={{0,2},{1,3},{2,0},{3,1},{4,6},{5,7},{6,4},{7,5},{8,10},{9,11},{10,... | collective-permute-start | bytes 417800 | tf_op jit(solution)/shard_map/ppermute | solution.py:57
  24.6 4.3 %collective-permute-start.1 = (bf16[256,256]{1,0:T(8,128)(2,1)S(1)}, bf16[256,256]{1,0:T(8,128)(2,1)S(1)}, u32[]{:S(2)}, u32[]{:S(2)}) collective-permute-start(bf16[256,256]{1,0:T(8,128)(2,1)S(1)} %slice.36), channel_id=1, source_target_pairs={{0,1},{1,0},{2,3},{3,2},{4,5},{5,4},{6,7},{7,6},{8,9},{9,8},{10,11... | collective-permute-start | bytes 393224 | tf_op jit(solution)/shard_map/ppermute | solution.py:57
  32.1 4.6 %collective-permute-start.11 = (bf16[384,2048]{1,0:T(8,128)(2,1)S(1)}, bf16[384,2048]{1,0:T(8,128)(2,1)S(1)}, u32[]{:S(2)}, u32[]{:S(2)}) collective-permute-start(bf16[384,2048]{1,0:T(8,128)(2,1)S(1)} %pad_maximum_fusion.refs_0_), channel_id=1, source_target_pairs={{0,4},{1,5},{2,6},{3,7},{4,0},{5,1},{6,2},{7,3},{8,12},{9,13},{10,... | collective-permute-start | bytes 4718600 | tf_op jit(solution)/shard_map/ppermute | solution.py:57
  32.9 7.6 %collective-permute-start.14 = (bf16[128,1024]{1,0:T(8,128)(2,1)S(1)}, bf16[128,1024]{1,0:T(8,128)(2,1)S(1)}, u32[]{:S(2)}, u32[]{:S(2)}) collective-permute-start(bf16[128,1024]{1,0:T(8,128)(2,1)S(1)} %slice.31), channel_id=1, source_target_pairs={{0,1},{1,0},{2,3},{3,2},{4,5},{5,4},{6,7},{7,6},{8,9},{9,8},{10,11... | collective-permute-start | bytes 786440 | tf_op jit(solution)/shard_map/ppermute | solution.py:57
  34.2 7.7 %collective-permute-start.12 = (bf16[128,1024]{1,0:T(8,128)(2,1)S(1)}, bf16[128,1024]{1,0:T(8,128)(2,1)S(1)}, u32[]{:S(2)}, u32[]{:S(2)}) collective-permute-start(bf16[128,1024]{1,0:T(8,128)(2,1)S(1)} %slice.28), channel_id=1, source_target_pairs={{0,2},{1,3},{2,0},{3,1},{4,6},{5,7},{6,4},{7,5},{8,10},{9,11},{10,... | collective-permute-start | bytes 786440 | tf_op jit(solution)/shard_map/ppermute | solution.py:57
  35.3 9.8 %collective-permute-start.19 = (bf16[512,384]{1,0:T(8,128)(2,1)S(1)}, bf16[512,384]{1,0:T(8,128)(2,1)S(1)}, u32[]{:S(2)}, u32[]{:S(2)}) collective-permute-start(bf16[512,384]{1,0:T(8,128)(2,1)S(1)} %constant_dynamic-update-slice_fusion.refs_5_.refs_9_), channel_id=1, source_target_pairs={{0,8},{1,9},{2,10},{3,11},{4,12},{5,13},{6,14},{7,15},{8,0},{9,1},... | collective-permute-start | bytes 1179656 | tf_op jit(solution)/shard_map/ppermute | solution.py:57
  45.8 7.7 %collective-permute-start.20 = (bf16[4,256,128]{2,1,0:T(8,128)(2,1)S(1)}, bf16[4,256,128]{2,1,0:T(8,128)(2,1)S(1)}, u32[]{:S(2)}, u32[]{:S(2)}) collective-permute-start(bf16[4,256,128]{2,1,0:T(8,128)(2,1)S(1)} %get-tuple-element.56.own), channel_id=1, source_target_pairs={{0,8},{1,9},{2,10},{3,11},{4,12},{5,13},{6,14},{7,15},{8,0},{9,1},... | collective-permute-start | bytes 786440 | tf_op jit(solution)/shard_map/ppermute | solution.py:57
  48.1 8.6 %collective-permute-start.21 = (bf16[4,256,128]{2,1,0:T(8,128)(2,1)S(1)}, bf16[4,256,128]{2,1,0:T(8,128)(2,1)S(1)}, u32[]{:S(2)}, u32[]{:S(2)}) collective-permute-start(bf16[4,256,128]{2,1,0:T(8,128)(2,1)S(1)} %get-tuple-element.56.own), channel_id=1, source_target_pairs={{8,16},{9,17},{10,18},{11,19},{12,20},{13,21},{14,22},{15,23},{16,... | collective-permute-start | bytes 786440 | tf_op jit(solution)/shard_map/ppermute | solution.py:57
  51.2 6.7 %collective-permute-start.25 = (bf16[2,256,128]{2,1,0:T(8,128)(2,1)S(1)}, bf16[2,256,128]{2,1,0:T(8,128)(2,1)S(1)}, u32[]{:S(2)}, u32[]{:S(2)}) collective-permute-start(bf16[2,256,128]{2,1,0:T(8,128)(2,1)S(1)} %get-tuple-element.58.own), channel_id=1, source_target_pairs={{0,8},{1,9},{2,10},{3,11},{4,12},{5,13},{6,14},{7,15},{8,0},{9,1},... | collective-permute-start | bytes 393224 | tf_op jit(solution)/shard_map/ppermute | solution.py:57
  51.3 7.9 %collective-permute-start.26 = (bf16[2,256,128]{2,1,0:T(8,128)(2,1)S(1)}, bf16[2,256,128]{2,1,0:T(8,128)(2,1)S(1)}, u32[]{:S(2)}, u32[]{:S(2)}) collective-permute-start(bf16[2,256,128]{2,1,0:T(8,128)(2,1)S(1)} %get-tuple-element.58.own), channel_id=1, source_target_pairs={{8,16},{9,17},{10,18},{11,19},{12,20},{13,21},{14,22},{15,23},{16,... | collective-permute-start | bytes 393224 | tf_op jit(solution)/shard_map/ppermute | solution.py:57
  53.4 6.8 %collective-permute-start.22 = (bf16[2,256,128]{2,1,0:T(8,128)(2,1)S(1)}, bf16[2,256,128]{2,1,0:T(8,128)(2,1)S(1)}, u32[]{:S(2)}, u32[]{:S(2)}) collective-permute-start(bf16[2,256,128]{2,1,0:T(8,128)(2,1)S(1)} %get-tuple-element.57.own), channel_id=1, source_target_pairs={{0,8},{1,9},{2,10},{3,11},{4,12},{5,13},{6,14},{7,15},{8,0},{9,1},... | collective-permute-start | bytes 393224 | tf_op jit(solution)/shard_map/ppermute | solution.py:57
  53.5 8.5 %collective-permute-start.23 = (bf16[2,256,128]{2,1,0:T(8,128)(2,1)S(1)}, bf16[2,256,128]{2,1,0:T(8,128)(2,1)S(1)}, u32[]{:S(2)}, u32[]{:S(2)}) collective-permute-start(bf16[2,256,128]{2,1,0:T(8,128)(2,1)S(1)} %get-tuple-element.57.own), channel_id=1, source_target_pairs={{8,16},{9,17},{10,18},{11,19},{12,20},{13,21},{14,22},{15,23},{16,... | collective-permute-start | bytes 393224 | tf_op jit(solution)/shard_map/ppermute | solution.py:57
  59.4 8.2 %collective-permute-start.31 = (bf16[256,128]{1,0:T(8,128)(2,1)S(1)}, bf16[256,128]{1,0:T(8,128)(2,1)S(1)}, u32[]{:S(2)}, u32[]{:S(2)}) collective-permute-start(bf16[256,128]{1,0:T(8,128)(2,1)S(1)} %shard_map.77), channel_id=1, source_target_pairs={{0,3},{1,2},{2,1},{3,0},{4,7},{5,6},{6,5},{7,4},{8,11},{9,10},{10,... | collective-permute-start | bytes 196616 | tf_op jit(solution)/shard_map/ppermute | solution.py:57
  62.2 6.1 %collective-permute-start.29 = (bf16[256,128]{1,0:T(8,128)(2,1)S(1)}, bf16[256,128]{1,0:T(8,128)(2,1)S(1)}, u32[]{:S(2)}, u32[]{:S(2)}) collective-permute-start(bf16[256,128]{1,0:T(8,128)(2,1)S(1)} %shard_map.76), channel_id=1, source_target_pairs={{0,2},{1,3},{2,0},{3,1},{4,6},{5,7},{6,4},{7,5},{8,10},{9,11},{10,... | collective-permute-start | bytes 196616 | tf_op jit(solution)/shard_map/ppermute | solution.py:57
  63.0 6.1 %collective-permute-start.27 = (bf16[256,128]{1,0:T(8,128)(2,1)S(1)}, bf16[256,128]{1,0:T(8,128)(2,1)S(1)}, u32[]{:S(2)}, u32[]{:S(2)}) collective-permute-start(bf16[256,128]{1,0:T(8,128)(2,1)S(1)} %shard_map.75), channel_id=1, source_target_pairs={{0,1},{1,0},{2,3},{3,2},{4,5},{5,4},{6,7},{7,6},{8,9},{9,8},{10,11... | collective-permute-start | bytes 196616 | tf_op jit(solution)/shard_map/ppermute | solution.py:57
  63.9 6.5 %collective-permute-start.24 = (bf16[256,128]{1,0:T(8,128)(2,1)S(1)}, bf16[256,128]{1,0:T(8,128)(2,1)S(1)}, u32[]{:S(2)}, u32[]{:S(2)}) collective-permute-start(bf16[256,128]{1,0:T(8,128)(2,1)S(1)} %shard_map.74.refs_0_), channel_id=1, source_target_pairs={{0,4},{1,5},{2,6},{3,7},{4,0},{5,1},{6,2},{7,3},{8,12},{9,13},{10,... | collective-permute-start | bytes 196616 | tf_op jit(solution)/shard_map/ppermute | solution.py:57
  (13 other events, 24.1 us)

commit v8 on v7

--- a/solution.py
+++ b/solution.py
@@ -106,16 +106,6 @@
     to_x[...] = w[:, PAIR : 2 * PAIR]
     to_y[: w.shape[0]] = jnp.where(even, high, low)
     keep[...] = jnp.where(even, low, high)
-
-
-def split_far_kernel(w, flags, to_y, keep):
-    _, _, depth = where_am_i()
-    even = (depth & 1) == 0
-    low, high = w[:, :PAIR], w[:, 2 * PAIR :]
-    to_y[: w.shape[0]] = jnp.where(even, high, low)
-    keep[...] = jnp.where(even, low, high)
-    to_y[w.shape[0] :, :HD] = flags[...]
-    to_y[w.shape[0] :, HD:] = flags[...]
 
 
 def sorted_groups(kept, from_x, from_y):
@@ -268,25 +258,27 @@
                 out_ref[r, u * block : (u + 1) * block, here] = (p * inverse).astype(jnp.bfloat16)
 
 
-def mix_kernel(r, weights, outer, own, middle, out_ref):
+def mix_kernel(r, weights, outer, own, middle, keep_ref, send_ref):
+    _, core, _ = where_am_i()
     block = weights.shape[1] // 2
     values = neighbours(outer, own, middle, V_ORDER.index(r) % 2)
+    results = []
     for u in range(2):
         w = weights[r, u * block : (u + 1) * block]
         v = [values[side][first * block : last * block] for side, first, last in spans(u)]
         result = jnp.dot(w, jnp.concatenate(v, axis=0), preferred_element_type=jnp.float32)
-        out_ref[u * block : (u + 1) * block] = result.astype(jnp.bfloat16)
+        results.append(result.astype(jnp.bfloat16))
+    keep_ref[...] = jnp.where(core == 0, results[0], results[1])
+    send_ref[...] = jnp.where(core == 0, results[1], results[0])
 
 
 def gather_kernel(*refs):
     out_ref = refs[-1]
     _, core, depth = where_am_i()
-    block = out_ref.shape[0]
-    mine = pl.ds(pl.multiple_of(core * block, block), block)
     for i, ref in enumerate(refs[:-1]):
         r, rel = i >> 1, i & 1
         at = pl.multiple_of((2 * (depth ^ r) + (core ^ rel)) * HD, HD)
-        out_ref[:, pl.ds(at, HD)] = ref[mine, :]
+        out_ref[:, pl.ds(at, HD)] = ref[...]
 
 
 def call(kernel, outs, places, scratch=(), macs=0, limit=32):
@@ -313,7 +305,7 @@
 
     far_raw = swap_z(w_qkv, 2)
 
-    cut, cut_more = array(size, PAIR), array(size + EXTRA, PAIR)
+    cut = array(size, PAIR)
     to_x, to_y, kept = call(split_kernel, (cut,) * 3, "v")(w_qkv)
     own = call(sort_kernel, array(size, 6 * HD), "vvv")(kept, swap_depth(to_x, 1), swap_depth(to_y, 2))
     near = swap_z(own, 1)
@@ -345,8 +337,10 @@
     )
     beside, above = swap_depth(normed, 1), swap_depth(normed, 2)
 
-    to_y, kept = call(split_far_kernel, (cut_more, cut), "vv")(far_raw, own_flags)
-    to_x = far_raw[:, PAIR : 2 * PAIR]
+    even = (lax.axis_index("depth") & 1) == 0
+    low, to_x, high = (far_raw[:, k * PAIR : (k + 1) * PAIR] for k in range(3))
+    kept = jnp.where(even, low, high)
+    to_y = jnp.concatenate([jnp.where(even, high, low), jnp.concatenate([own_flags, own_flags], axis=1)], axis=0)
     from_x, from_y = swap_depth(to_x, 1), swap_depth(to_y, 2)
     keep, send, flags = call(
         sort_far_kernel,
@@ -386,11 +380,12 @@
     values = [(swap_z(t, 1), t, swap_middle(t)) for t in v]
     pieces = {}
     for r in V_ORDER:
-        mixed = call(functools.partial(mix_kernel, r), array(2 * block, HD), "vvvv", macs=2 * block * 5 * block * HD)(
-            weights, *values[V_ORDER.index(r) // 2]
-        )
-        pieces[r] = swap_depth(mixed, r) if r else mixed
-    both = [t for r in range(4) for t in (pieces[r], swap_core(pieces[r]))]
+        kept, sent = call(
+            functools.partial(mix_kernel, r), (array(block, HD),) * 2, "vvvv", macs=2 * block * 5 * block * HD
+        )(weights, *values[V_ORDER.index(r) // 2])
+        sent = hop(sent, lambda z, c, d, r=r: (z, 1 - c, d ^ r))
+        pieces[r] = (swap_depth(kept, r) if r else kept, sent)
+    both = [t for r in range(4) for t in pieces[r]]
     context = call(gather_kernel, array(block, HEADS * HD), "v" * 8)(*both)
     return context.reshape(time_len, site_len, HEADS * HD)
 

time: 72.4 us -> 73.5 us (1.015)
  waiting for transfers between devices: 22 us -> 25.6 us
  starting transfers between devices: 37.4 us -> 34.3 us
    ppermute x33, waiting for transfers between devices: 22 us -> 25.6 us  [hop(): return lax.ppermute(value, ('tm', 'depth'), pairs)]
    ppermute x33, starting transfers between devices: 37.4 us -> 34.3 us  [hop(): return lax.ppermute(value, ('tm', 'depth'), pairs)]
  transfers between devices with their start and end apart: 33 -> 33, of which waited for: 11 -> 15; matrix products, arithmetic and copies ran while one was open for 0% -> 1% of each run, Pallas kernels for 10% -> 10%
where the time goes in v8:
time: 73.5 us; the launch traced here: 72.7 us
  starting transfers between devices  34.3 us (47%)
  waiting for transfers between devices  25.6 us (35%)
  Pallas kernels  8.93 us (12%)
  local copies, waits for them, and re-layouts  3.3 us (4%)
    ppermute x33, starting transfers between devices, hop(): return lax.ppermute(value, ('tm', 'depth'), pairs)  34.3 us
    ppermute x33, waiting for transfers between devices, hop(): return lax.ppermute(value, ('tm', 'depth'), pairs)  25.6 us
    unnamed x9, local copies, waits for them, and re-layouts  3.16 us
    pallas_call x1, Pallas kernels, plane_device(): call(embed_kernel, array(block, width), 'vvvvaa', scratch=[VMEM((block, w...  2.41 us
  transfers between devices with their start and end apart: 33, of which 15 were waited for; matrix products, arithmetic and copies ran while one was open for 1% of the time, Pallas kernels for 10%

profile of v8, /device:TPU:9, one launch (start us, length us, event | category | flops | bytes accessed | tf_op | source)
XLA Modules:
  0.0 72.7 jit_solution(10634593350573460690)
XLA Ops:
  0.0 2.3 %collective-permute-start = (bf16[256,768]{1,0:T(8,128)(2,1)}, bf16[256,768]{1,0:T(8,128)(2,1)S(1)}, u32[]{:S(2)}, u32[]{:S(2)}) collective-permute-start(bf16[256,768]{1,0:T(8,128)(2,1)} %w.1), channel_id=1, source_target_pairs={{0,16},{1,17},{2,18},{3,19},{4,20},{5,21},{6,22},{7,23},{8,24},{9,... | collective-permute-start | bytes 1179656 | tf_op jit(solution)/shard_map/ppermute | solution.py:57
  3.4 1.3 %collective-permute-start.5 = (bf16[256,256]{1,0:T(8,128)(2,1)S(1)}, bf16[256,256]{1,0:T(8,128)(2,1)S(1)}, u32[]{:S(2)}, u32[]{:S(2)}) collective-permute-start(bf16[256,256]{1,0:T(8,128)(2,1)S(1)} %get-tuple-element.44), channel_id=1, source_target_pairs={{0,1},{1,0},{2,3},{3,2},{4,5},{5,4},{6,7},{7,6},{8,9},{9,8},{10,11... | collective-permute-start | bytes 393224 | tf_op jit(solution)/shard_map/ppermute | solution.py:57
  4.7 1.2 %collective-permute-start.6 = (bf16[256,256]{1,0:T(8,128)(2,1)S(1)}, bf16[256,256]{1,0:T(8,128)(2,1)S(1)}, u32[]{:S(2)}, u32[]{:S(2)}) collective-permute-start(bf16[256,256]{1,0:T(8,128)(2,1)S(1)} %get-tuple-element.45), channel_id=1, source_target_pairs={{0,2},{1,3},{2,0},{3,1},{4,6},{5,7},{6,4},{7,5},{8,10},{9,11},{10,... | collective-permute-start | bytes 393224 | tf_op jit(solution)/shard_map/ppermute | solution.py:57
  9.4 1.4 %collective-permute-done.3.edge_x = bf16[32,128]{1,0:T(8,128)(2,1)S(1)} collective-permute-done((bf16[32,128]{1,0:T(8,128)(2,1)S(1)}, bf16[32,128]{1,0:T(8,128)(2,1)S(1)}, u32[]{:S(2)}, u32[]{:S(2)}) %collective-permute-start.3) | collective-permute-done | bytes 8224 | tf_op jit(solution)/shard_map/ppermute | solution.py:57
  12.6 2.4 %shard_map.68 = bf16[128,2048]{1,0:T(8,128)(2,1)S(1)} custom-call(bf16[32,128]{1,0:T(8,128)(2,1)S(1)} %collective-permute-done.3.edge_x, bf16[32,128]{1,0:T(8,128)(2,1)S(1)} %collective-permute-done.4.edge_across, bf16[16,8,128]{2,1,0:T(8,128)(2,1)S(1)} %get-tuple-element.46.raw, f32[1,2048]{1,0:T(1,128)S(1)} %bitcast.5, bf16[128,2048]{1,0:T(8,128)(2,1)} %bitcast.8, ...), custom_call_target="tpu_custom_call" | custom-call | flops 201326592 | tf_op jit(solution)/shard_map/pallas_call | solution.py:318
  15.0 1.3 %collective-permute-start.8 = (bf16[128,2048]{1,0:T(8,128)(2,1)S(1)}, bf16[128,2048]{1,0:T(8,128)(2,1)S(1)}, u32[]{:S(2)}, u32[]{:S(2)}) collective-permute-start(bf16[128,2048]{1,0:T(8,128)(2,1)S(1)} %shard_map.68), channel_id=1, source_target_pairs={{0,1},{1,0},{2,3},{3,2},{4,5},{5,4},{6,7},{7,6},{8,9},{9,8},{10,11... | collective-permute-start | bytes 1572872 | tf_op jit(solution)/shard_map/ppermute | solution.py:57
  16.7 3.1 %collective-permute-done = bf16[256,768]{1,0:T(8,128)(2,1)S(1)} collective-permute-done((bf16[256,768]{1,0:T(8,128)(2,1)}, bf16[256,768]{1,0:T(8,128)(2,1)S(1)}, u32[]{:S(2)}, u32[]{:S(2)}) %collective-permute-start) | collective-permute-done | bytes 393248 | tf_op jit(solution)/shard_map/ppermute | solution.py:57
  19.9 1.3 %collective-permute-start.2 = (bf16[272,256]{1,0:T(8,128)(2,1)S(1)}, bf16[272,256]{1,0:T(8,128)(2,1)S(1)}, u32[]{:S(2)}, u32[]{:S(2)}) collective-permute-start(bf16[272,256]{1,0:T(8,128)(2,1)S(1)} %maximum_maximum_fusion), channel_id=1, source_target_pairs={{0,2},{1,3},{2,0},{3,1},{4,6},{5,7},{6,4},{7,5},{8,10},{9,11},{10,... | collective-permute-start | bytes 417800 | tf_op jit(solution)/shard_map/ppermute | solution.py:57
  21.2 1.2 %collective-permute-start.1 = (bf16[256,256]{1,0:T(8,128)(2,1)S(1)}, bf16[256,256]{1,0:T(8,128)(2,1)S(1)}, u32[]{:S(2)}, u32[]{:S(2)}) collective-permute-start(bf16[256,256]{1,0:T(8,128)(2,1)S(1)} %get-tuple-element.72), channel_id=1, source_target_pairs={{0,1},{1,0},{2,3},{3,2},{4,5},{5,4},{6,7},{7,6},{8,9},{9,8},{10,11... | collective-permute-start | bytes 393224 | tf_op jit(solution)/shard_map/ppermute | solution.py:57
  22.4 6.3 %collective-permute-done.1.from_x = bf16[256,256]{1,0:T(8,128)(2,1)S(1)} collective-permute-done((bf16[256,256]{1,0:T(8,128)(2,1)S(1)}, bf16[256,256]{1,0:T(8,128)(2,1)S(1)}, u32[]{:S(2)}, u32[]{:S(2)}) %collective-permute-start.1) | collective-permute-done | bytes 131104 | tf_op jit(solution)/shard_map/ppermute | solution.py:57
  29.9 3.9 %collective-permute-start.10 = (bf16[256,384]{1,0:T(8,128)(2,1)S(1)}, bf16[256,384]{1,0:T(8,128)(2,1)S(1)}, u32[]{:S(2)}, u32[]{:S(2)}) collective-permute-start(bf16[256,384]{1,0:T(8,128)(2,1)S(1)} %get-tuple-element.47), channel_id=1, source_target_pairs={{0,4},{1,5},{2,6},{3,7},{4,0},{5,1},{6,2},{7,3},{8,12},{9,13},{10,... | collective-permute-start | bytes 589832 | tf_op jit(solution)/shard_map/ppermute | solution.py:57
  36.4 2.6 %collective-permute-done.13.refs_4_.refs_8_.received = bf16[528,384]{1,0:T(8,128)(2,1)S(1)} collective-permute-done((bf16[528,384]{1,0:T(8,128)(2,1)S(1)}, bf16[528,384]{1,0:T(8,128)(2,1)S(1)}, u32[]{:S(2)}, u32[]{:S(2)}) %collective-permute-start.13) | collective-permute-done | bytes 405536 | tf_op jit(solution)/shard_map/ppermute | solution.py:57
  39.0 1.4 %shard_map.69.refs_4_ = f32[768,384]{1,0:T(8,128)S(1)} custom-call(bf16[384,2048]{1,0:T(8,128)(2,1)S(1)} %pad_maximum_fusion.refs_0_, bf16[384,2048]{1,0:T(8,128)(2,1)S(1)} %collective-permute-done.11.refs_1_, bf16[256,768]{1,0:T(8,128)(2,1)S(1)} %shard_map.67.refs_2_.refs_6_, bf16[256,768]{1,0:T(8,128)(2,1)S(1)} %collective-permute-done.7.refs_3_.refs_7_, ...), custom_call_target="tpu_custom_call" | custom-call | flops 905969664 | tf_op jit(solution)/shard_map/pallas_call | solution.py:361
  40.4 2.9 %collective-permute-done.14.refs_1_ = bf16[128,1024]{1,0:T(8,128)(2,1)S(1)} collective-permute-done((bf16[128,1024]{1,0:T(8,128)(2,1)S(1)}, bf16[128,1024]{1,0:T(8,128)(2,1)S(1)}, u32[]{:S(2)}, u32[]{:S(2)}) %collective-permute-start.14) | collective-permute-done | bytes 262176 | tf_op jit(solution)/shard_map/ppermute | solution.py:57
  43.3 1.3 %collective-permute-start.17 = (bf16[64,1024]{1,0:T(8,128)(2,1)S(1)}, bf16[64,1024]{1,0:T(8,128)(2,1)S(1)}, u32[]{:S(2)}, u32[]{:S(2)}) collective-permute-start(bf16[64,1024]{1,0:T(8,128)(2,1)S(1)} %get-tuple-element.75), channel_id=1, source_target_pairs={{0,4},{1,5},{2,6},{3,7},{4,0},{5,1},{6,2},{7,3},{8,12},{9,13},{10,... | collective-permute-start | bytes 393224 | tf_op jit(solution)/shard_map/ppermute | solution.py:57
  48.0 1.9 %collective-permute-start.21 = (bf16[4,256,128]{2,1,0:T(8,128)(2,1)S(1)}, bf16[4,256,128]{2,1,0:T(8,128)(2,1)S(1)}, u32[]{:S(2)}, u32[]{:S(2)}) collective-permute-start(bf16[4,256,128]{2,1,0:T(8,128)(2,1)S(1)} %get-tuple-element.60.own), channel_id=1, source_target_pairs={{8,16},{9,17},{10,18},{11,19},{12,20},{13,21},{14,22},{15,23},{16,... | collective-permute-start | bytes 786440 | tf_op jit(solution)/shard_map/ppermute | solution.py:57
  50.2 3.2 %collective-permute-start.26 = (bf16[2,256,128]{2,1,0:T(8,128)(2,1)S(1)}, bf16[2,256,128]{2,1,0:T(8,128)(2,1)S(1)}, u32[]{:S(2)}, u32[]{:S(2)}) collective-permute-start(bf16[2,256,128]{2,1,0:T(8,128)(2,1)S(1)} %get-tuple-element.64.own), channel_id=1, source_target_pairs={{8,16},{9,17},{10,18},{11,19},{12,20},{13,21},{14,22},{15,23},{16,... | collective-permute-start | bytes 393224 | tf_op jit(solution)/shard_map/ppermute | solution.py:57
  53.5 1.7 %collective-permute-done.20.outer = bf16[4,256,128]{2,1,0:T(8,128)(2,1)S(1)} collective-permute-done((bf16[4,256,128]{2,1,0:T(8,128)(2,1)S(1)}, bf16[4,256,128]{2,1,0:T(8,128)(2,1)S(1)}, u32[]{:S(2)}, u32[]{:S(2)}) %collective-permute-start.20) | collective-permute-done | bytes 262176 | tf_op jit(solution)/shard_map/ppermute | solution.py:57
  55.1 1.9 %collective-permute-start.23 = (bf16[2,256,128]{2,1,0:T(8,128)(2,1)S(1)}, bf16[2,256,128]{2,1,0:T(8,128)(2,1)S(1)}, u32[]{:S(2)}, u32[]{:S(2)}) collective-permute-start(bf16[2,256,128]{2,1,0:T(8,128)(2,1)S(1)} %get-tuple-element.61.own), channel_id=1, source_target_pairs={{8,16},{9,17},{10,18},{11,19},{12,20},{13,21},{14,22},{15,23},{16,... | collective-permute-start | bytes 393224 | tf_op jit(solution)/shard_map/ppermute | solution.py:57
  58.3 1.3 %collective-permute-done.26.middle = bf16[2,256,128]{2,1,0:T(8,128)(2,1)S(1)} collective-permute-done((bf16[2,256,128]{2,1,0:T(8,128)(2,1)S(1)}, bf16[2,256,128]{2,1,0:T(8,128)(2,1)S(1)}, u32[]{:S(2)}, u32[]{:S(2)}) %collective-permute-start.26) | collective-permute-done | bytes 131104 | tf_op jit(solution)/shard_map/ppermute | solution.py:57
  60.0 5.5 %collective-permute-start.32 = (bf16[128,128]{1,0:T(8,128)(2,1)S(1)}, bf16[128,128]{1,0:T(8,128)(2,1)S(1)}, u32[]{:S(2)}, u32[]{:S(2)}) collective-permute-start(bf16[128,128]{1,0:T(8,128)(2,1)S(1)} %get-tuple-element.70), channel_id=1, source_target_pairs={{0,7},{1,6},{2,5},{3,4},{4,3},{5,2},{6,1},{7,0},{8,15},{9,14},{10,... | collective-permute-start | bytes 98312 | tf_op jit(solution)/shard_map/ppermute | solution.py:57
  66.9 1.3 %collective-permute-start.27 = (bf16[128,128]{1,0:T(8,128)(2,1)S(1)}, bf16[128,128]{1,0:T(8,128)(2,1)S(1)}, u32[]{:S(2)}, u32[]{:S(2)}) collective-permute-start(bf16[128,128]{1,0:T(8,128)(2,1)S(1)} %get-tuple-element.65), channel_id=1, source_target_pairs={{0,1},{1,0},{2,3},{3,2},{4,5},{5,4},{6,7},{7,6},{8,9},{9,8},{10,11... | collective-permute-start | bytes 98312 | tf_op jit(solution)/shard_map/ppermute | solution.py:57
  68.5 1.5 %collective-permute-start.28 = (bf16[128,128]{1,0:T(8,128)(2,1)S(1)}, bf16[128,128]{1,0:T(8,128)(2,1)S(1)}, u32[]{:S(2)}, u32[]{:S(2)}) collective-permute-start(bf16[128,128]{1,0:T(8,128)(2,1)S(1)} %get-tuple-element.66), channel_id=1, source_target_pairs={{0,5},{1,4},{2,7},{3,6},{4,1},{5,0},{6,3},{7,2},{8,13},{9,12},{10,... | collective-permute-start | bytes 98312 | tf_op jit(solution)/shard_map/ppermute | solution.py:57
  70.0 1.9 %collective-permute-done.28.refs_3_ = bf16[128,128]{1,0:T(8,128)(2,1)S(1)} collective-permute-done((bf16[128,128]{1,0:T(8,128)(2,1)S(1)}, bf16[128,128]{1,0:T(8,128)(2,1)S(1)}, u32[]{:S(2)}, u32[]{:S(2)}) %collective-permute-start.28) | collective-permute-done | bytes 32800 | tf_op jit(solution)/shard_map/ppermute | solution.py:57
  (76 shorter events, 18.3 us)
Async XLA Ops:
  0.0 19.8 %collective-permute-start = (bf16[256,768]{1,0:T(8,128)(2,1)}, bf16[256,768]{1,0:T(8,128)(2,1)S(1)}, u32[]{:S(2)}, u32[]{:S(2)}) collective-permute-start(bf16[256,768]{1,0:T(8,128)(2,1)} %w.1), channel_id=1, source_target_pairs={{0,16},{1,17},{2,18},{3,19},{4,20},{5,21},{6,22},{7,23},{8,24},{9,... | collective-permute-start | bytes 1179656 | tf_op jit(solution)/shard_map/ppermute | solution.py:57
  3.4 13.2 %collective-permute-start.5 = (bf16[256,256]{1,0:T(8,128)(2,1)S(1)}, bf16[256,256]{1,0:T(8,128)(2,1)S(1)}, u32[]{:S(2)}, u32[]{:S(2)}) collective-permute-start(bf16[256,256]{1,0:T(8,128)(2,1)S(1)} %get-tuple-element.44), channel_id=1, source_target_pairs={{0,1},{1,0},{2,3},{3,2},{4,5},{5,4},{6,7},{7,6},{8,9},{9,8},{10,11... | collective-permute-start | bytes 393224 | tf_op jit(solution)/shard_map/ppermute | solution.py:57
  4.7 11.9 %collective-permute-start.6 = (bf16[256,256]{1,0:T(8,128)(2,1)S(1)}, bf16[256,256]{1,0:T(8,128)(2,1)S(1)}, u32[]{:S(2)}, u32[]{:S(2)}) collective-permute-start(bf16[256,256]{1,0:T(8,128)(2,1)S(1)} %get-tuple-element.45), channel_id=1, source_target_pairs={{0,2},{1,3},{2,0},{3,1},{4,6},{5,7},{6,4},{7,5},{8,10},{9,11},{10,... | collective-permute-start | bytes 393224 | tf_op jit(solution)/shard_map/ppermute | solution.py:57
  8.2 3.7 %collective-permute-start.4 = (bf16[32,128]{1,0:T(8,128)(2,1)S(1)}, bf16[32,128]{1,0:T(8,128)(2,1)S(1)}, u32[]{:S(2)}, u32[]{:S(2)}) collective-permute-start(bf16[32,128]{1,0:T(8,128)(2,1)S(1)} %get-tuple-element.40), channel_id=1, source_target_pairs={{0,3},{1,2},{2,1},{3,0},{4,7},{5,6},{6,5},{7,4},{8,11},{9,10},{10,... | collective-permute-start | bytes 24584 | tf_op jit(solution)/shard_map/ppermute | solution.py:57
  15.0 14.9 %collective-permute-start.8 = (bf16[128,2048]{1,0:T(8,128)(2,1)S(1)}, bf16[128,2048]{1,0:T(8,128)(2,1)S(1)}, u32[]{:S(2)}, u32[]{:S(2)}) collective-permute-start(bf16[128,2048]{1,0:T(8,128)(2,1)S(1)} %shard_map.68), channel_id=1, source_target_pairs={{0,1},{1,0},{2,3},{3,2},{4,5},{5,4},{6,7},{7,6},{8,9},{9,8},{10,11... | collective-permute-start | bytes 1572872 | tf_op jit(solution)/shard_map/ppermute | solution.py:57
  16.3 13.6 %collective-permute-start.9 = (bf16[128,2048]{1,0:T(8,128)(2,1)S(1)}, bf16[128,2048]{1,0:T(8,128)(2,1)S(1)}, u32[]{:S(2)}, u32[]{:S(2)}) collective-permute-start(bf16[128,2048]{1,0:T(8,128)(2,1)S(1)} %shard_map.68), channel_id=1, source_target_pairs={{0,2},{1,3},{2,0},{3,1},{4,6},{5,7},{6,4},{7,5},{8,10},{9,11},{10,... | collective-permute-start | bytes 1572872 | tf_op jit(solution)/shard_map/ppermute | solution.py:57
  16.6 13.3 %collective-permute-start.7 = (bf16[256,768]{1,0:T(8,128)(2,1)S(1)}, bf16[256,768]{1,0:T(8,128)(2,1)S(1)}, u32[]{:S(2)}, u32[]{:S(2)}) collective-permute-start(bf16[256,768]{1,0:T(8,128)(2,1)S(1)} %shard_map.67.refs_2_.refs_6_), channel_id=1, source_target_pairs={{0,8},{1,9},{2,10},{3,11},{4,12},{5,13},{6,14},{7,15},{8,0},{9,1},... | collective-permute-start | bytes 1179656 | tf_op jit(solution)/shard_map/ppermute | solution.py:57
  19.9 9.9 %collective-permute-start.2 = (bf16[272,256]{1,0:T(8,128)(2,1)S(1)}, bf16[272,256]{1,0:T(8,128)(2,1)S(1)}, u32[]{:S(2)}, u32[]{:S(2)}) collective-permute-start(bf16[272,256]{1,0:T(8,128)(2,1)S(1)} %maximum_maximum_fusion), channel_id=1, source_target_pairs={{0,2},{1,3},{2,0},{3,1},{4,6},{5,7},{6,4},{7,5},{8,10},{9,11},{10,... | collective-permute-start | bytes 417800 | tf_op jit(solution)/shard_map/ppermute | solution.py:57
  21.2 7.5 %collective-permute-start.1 = (bf16[256,256]{1,0:T(8,128)(2,1)S(1)}, bf16[256,256]{1,0:T(8,128)(2,1)S(1)}, u32[]{:S(2)}, u32[]{:S(2)}) collective-permute-start(bf16[256,256]{1,0:T(8,128)(2,1)S(1)} %get-tuple-element.72), channel_id=1, source_target_pairs={{0,1},{1,0},{2,3},{3,2},{4,5},{5,4},{6,7},{7,6},{8,9},{9,8},{10,11... | collective-permute-start | bytes 393224 | tf_op jit(solution)/shard_map/ppermute | solution.py:57
  29.9 5.0 %collective-permute-start.10 = (bf16[256,384]{1,0:T(8,128)(2,1)S(1)}, bf16[256,384]{1,0:T(8,128)(2,1)S(1)}, u32[]{:S(2)}, u32[]{:S(2)}) collective-permute-start(bf16[256,384]{1,0:T(8,128)(2,1)S(1)} %get-tuple-element.47), channel_id=1, source_target_pairs={{0,4},{1,5},{2,6},{3,7},{4,0},{5,1},{6,2},{7,3},{8,12},{9,13},{10,... | collective-permute-start | bytes 589832 | tf_op jit(solution)/shard_map/ppermute | solution.py:57
  34.9 4.1 %collective-permute-start.11 = (bf16[384,2048]{1,0:T(8,128)(2,1)S(1)}, bf16[384,2048]{1,0:T(8,128)(2,1)S(1)}, u32[]{:S(2)}, u32[]{:S(2)}) collective-permute-start(bf16[384,2048]{1,0:T(8,128)(2,1)S(1)} %pad_maximum_fusion.refs_0_), channel_id=1, source_target_pairs={{0,4},{1,5},{2,6},{3,7},{4,0},{5,1},{6,2},{7,3},{8,12},{9,13},{10,... | collective-permute-start | bytes 4718600 | tf_op jit(solution)/shard_map/ppermute | solution.py:57
  35.7 7.6 %collective-permute-start.14 = (bf16[128,1024]{1,0:T(8,128)(2,1)S(1)}, bf16[128,1024]{1,0:T(8,128)(2,1)S(1)}, u32[]{:S(2)}, u32[]{:S(2)}) collective-permute-start(bf16[128,1024]{1,0:T(8,128)(2,1)S(1)} %slice.39), channel_id=1, source_target_pairs={{0,1},{1,0},{2,3},{3,2},{4,5},{5,4},{6,7},{7,6},{8,9},{9,8},{10,11... | collective-permute-start | bytes 786440 | tf_op jit(solution)/shard_map/ppermute | solution.py:57
  36.1 8.6 %collective-permute-start.12 = (bf16[128,1024]{1,0:T(8,128)(2,1)S(1)}, bf16[128,1024]{1,0:T(8,128)(2,1)S(1)}, u32[]{:S(2)}, u32[]{:S(2)}) collective-permute-start(bf16[128,1024]{1,0:T(8,128)(2,1)S(1)} %slice.36), channel_id=1, source_target_pairs={{0,2},{1,3},{2,0},{3,1},{4,6},{5,7},{6,4},{7,5},{8,10},{9,11},{10,... | collective-permute-start | bytes 786440 | tf_op jit(solution)/shard_map/ppermute | solution.py:57
  36.3 10.8 %collective-permute-start.19 = (bf16[512,384]{1,0:T(8,128)(2,1)S(1)}, bf16[512,384]{1,0:T(8,128)(2,1)S(1)}, u32[]{:S(2)}, u32[]{:S(2)}) collective-permute-start(bf16[512,384]{1,0:T(8,128)(2,1)S(1)} %constant_dynamic-update-slice_fusion.refs_5_.refs_9_), channel_id=1, source_target_pairs={{0,8},{1,9},{2,10},{3,11},{4,12},{5,13},{6,14},{7,15},{8,0},{9,1},... | collective-permute-start | bytes 1179656 | tf_op jit(solution)/shard_map/ppermute | solution.py:57
  47.9 7.2 %collective-permute-start.20 = (bf16[4,256,128]{2,1,0:T(8,128)(2,1)S(1)}, bf16[4,256,128]{2,1,0:T(8,128)(2,1)S(1)}, u32[]{:S(2)}, u32[]{:S(2)}) collective-permute-start(bf16[4,256,128]{2,1,0:T(8,128)(2,1)S(1)} %get-tuple-element.60.own), channel_id=1, source_target_pairs={{0,8},{1,9},{2,10},{3,11},{4,12},{5,13},{6,14},{7,15},{8,0},{9,1},... | collective-permute-start | bytes 786440 | tf_op jit(solution)/shard_map/ppermute | solution.py:57
  48.0 9.1 %collective-permute-start.21 = (bf16[4,256,128]{2,1,0:T(8,128)(2,1)S(1)}, bf16[4,256,128]{2,1,0:T(8,128)(2,1)S(1)}, u32[]{:S(2)}, u32[]{:S(2)}) collective-permute-start(bf16[4,256,128]{2,1,0:T(8,128)(2,1)S(1)} %get-tuple-element.60.own), channel_id=1, source_target_pairs={{8,16},{9,17},{10,18},{11,19},{12,20},{13,21},{14,22},{15,23},{16,... | collective-permute-start | bytes 786440 | tf_op jit(solution)/shard_map/ppermute | solution.py:57
  49.9 8.3 %collective-permute-start.25 = (bf16[2,256,128]{2,1,0:T(8,128)(2,1)S(1)}, bf16[2,256,128]{2,1,0:T(8,128)(2,1)S(1)}, u32[]{:S(2)}, u32[]{:S(2)}) collective-permute-start(bf16[2,256,128]{2,1,0:T(8,128)(2,1)S(1)} %get-tuple-element.64.own), channel_id=1, source_target_pairs={{0,8},{1,9},{2,10},{3,11},{4,12},{5,13},{6,14},{7,15},{8,0},{9,1},... | collective-permute-start | bytes 393224 | tf_op jit(solution)/shard_map/ppermute | solution.py:57
  50.2 9.4 %collective-permute-start.26 = (bf16[2,256,128]{2,1,0:T(8,128)(2,1)S(1)}, bf16[2,256,128]{2,1,0:T(8,128)(2,1)S(1)}, u32[]{:S(2)}, u32[]{:S(2)}) collective-permute-start(bf16[2,256,128]{2,1,0:T(8,128)(2,1)S(1)} %get-tuple-element.64.own), channel_id=1, source_target_pairs={{8,16},{9,17},{10,18},{11,19},{12,20},{13,21},{14,22},{15,23},{16,... | collective-permute-start | bytes 393224 | tf_op jit(solution)/shard_map/ppermute | solution.py:57
  53.4 12.1 %collective-permute-start.22 = (bf16[2,256,128]{2,1,0:T(8,128)(2,1)S(1)}, bf16[2,256,128]{2,1,0:T(8,128)(2,1)S(1)}, u32[]{:S(2)}, u32[]{:S(2)}) collective-permute-start(bf16[2,256,128]{2,1,0:T(8,128)(2,1)S(1)} %get-tuple-element.61.own), channel_id=1, source_target_pairs={{0,8},{1,9},{2,10},{3,11},{4,12},{5,13},{6,14},{7,15},{8,0},{9,1},... | collective-permute-start | bytes 393224 | tf_op jit(solution)/shard_map/ppermute | solution.py:57
  55.1 10.3 %collective-permute-start.23 = (bf16[2,256,128]{2,1,0:T(8,128)(2,1)S(1)}, bf16[2,256,128]{2,1,0:T(8,128)(2,1)S(1)}, u32[]{:S(2)}, u32[]{:S(2)}) collective-permute-start(bf16[2,256,128]{2,1,0:T(8,128)(2,1)S(1)} %get-tuple-element.61.own), channel_id=1, source_target_pairs={{8,16},{9,17},{10,18},{11,19},{12,20},{13,21},{14,22},{15,23},{16,... | collective-permute-start | bytes 393224 | tf_op jit(solution)/shard_map/ppermute | solution.py:57
  59.8 8.7 %collective-permute-start.31 = (bf16[128,128]{1,0:T(8,128)(2,1)S(1)}, bf16[128,128]{1,0:T(8,128)(2,1)S(1)}, u32[]{:S(2)}, u32[]{:S(2)}) collective-permute-start(bf16[128,128]{1,0:T(8,128)(2,1)S(1)} %get-tuple-element.69), channel_id=1, source_target_pairs={{0,3},{1,2},{2,1},{3,0},{4,7},{5,6},{6,5},{7,4},{8,11},{9,10},{10,... | collective-permute-start | bytes 98312 | tf_op jit(solution)/shard_map/ppermute | solution.py:57
  60.0 10.0 %collective-permute-start.32 = (bf16[128,128]{1,0:T(8,128)(2,1)S(1)}, bf16[128,128]{1,0:T(8,128)(2,1)S(1)}, u32[]{:S(2)}, u32[]{:S(2)}) collective-permute-start(bf16[128,128]{1,0:T(8,128)(2,1)S(1)} %get-tuple-element.70), channel_id=1, source_target_pairs={{0,7},{1,6},{2,5},{3,4},{4,3},{5,2},{6,1},{7,0},{8,15},{9,14},{10,... | collective-permute-start | bytes 98312 | tf_op jit(solution)/shard_map/ppermute | solution.py:57
  65.8 4.2 %collective-permute-start.29 = (bf16[128,128]{1,0:T(8,128)(2,1)S(1)}, bf16[128,128]{1,0:T(8,128)(2,1)S(1)}, u32[]{:S(2)}, u32[]{:S(2)}) collective-permute-start(bf16[128,128]{1,0:T(8,128)(2,1)S(1)} %get-tuple-element.67), channel_id=1, source_target_pairs={{0,2},{1,3},{2,0},{3,1},{4,6},{5,7},{6,4},{7,5},{8,10},{9,11},{10,... | collective-permute-start | bytes 98312 | tf_op jit(solution)/shard_map/ppermute | solution.py:57
  66.2 3.7 %collective-permute-start.30 = (bf16[128,128]{1,0:T(8,128)(2,1)S(1)}, bf16[128,128]{1,0:T(8,128)(2,1)S(1)}, u32[]{:S(2)}, u32[]{:S(2)}) collective-permute-start(bf16[128,128]{1,0:T(8,128)(2,1)S(1)} %get-tuple-element.68), channel_id=1, source_target_pairs={{0,6},{1,7},{2,4},{3,5},{4,2},{5,3},{6,0},{7,1},{8,14},{9,15},{10,... | collective-permute-start | bytes 98312 | tf_op jit(solution)/shard_map/ppermute | solution.py:57
  (13 other events, 24.4 us)

commit v9 on v8

--- a/solution.py
+++ b/solution.py
@@ -82,30 +82,28 @@
     return tm >> 1, tm & 1, lax.axis_index("depth")
 
 
-def edge_kernel(mask, raw, to_x, to_across, flags_ref, sites_ref):
+def split_kernel(mask, w, raw, to_x, to_y, to_across, keep, flags_ref):
     _, _, depth = where_am_i()
-    odd = depth & 1
+    even = (depth & 1) == 0
+    size, half = w.shape[0], raw.shape[0] // 2
+    low, high = w[:, :PAIR], w[:, 2 * PAIR :]
+    to_x[:size] = w[:, PAIR : 2 * PAIR]
+    to_y[:size] = jnp.where(even, high, low)
+    keep[...] = jnp.where(even, low, high)
     lane = lax.broadcasted_iota(jnp.int32, (EXTRA, HD), 1)
     flags = jnp.zeros((EXTRA, HD), jnp.int32)
     for entry in range(mask.shape[0]):
         flags = jnp.where(lane == entry, mask[entry], flags)
     flags = flags.astype(jnp.float32).astype(jnp.bfloat16)
     flags_ref[...] = flags
-    sites_ref[...] = raw[...]
-    values = raw[...].astype(jnp.float32)
-    first, last = values[:, 0], values[:, values.shape[1] - 1]
-    for ref, use_last in ((to_x, odd == 0), (to_across, depth == 1)):
-        ref[:EXTRA] = jnp.where(use_last, last, first).astype(jnp.bfloat16)
-        ref[EXTRA:] = flags
-
-
-def split_kernel(w, to_x, to_y, keep):
-    _, _, depth = where_am_i()
-    even = (depth & 1) == 0
-    low, high = w[:, :PAIR], w[:, 2 * PAIR :]
-    to_x[...] = w[:, PAIR : 2 * PAIR]
-    to_y[: w.shape[0]] = jnp.where(even, high, low)
-    keep[...] = jnp.where(even, low, high)
+    at = to_across.shape[0] - EXTRA - half
+    for i in range(2):
+        to_across[:at, i * HD : (i + 1) * HD] = raw[:at]
+    for ref, at in ((to_x, size), (to_y, size), (to_across, at)):
+        for i in range(2):
+            here = slice(i * HD, (i + 1) * HD)
+            ref[at : at + half, here] = raw[i * half : (i + 1) * half]
+            ref[at + half :, here] = flags
 
 
 def sorted_groups(kept, from_x, from_y):
@@ -127,48 +125,49 @@
         out_ref[:, (3 + third) * HD : (4 + third) * HD] = other
 
 
-def sort_far_kernel(kept, from_x, from_y, edge_x, edge_across, own_flags, keep_ref, send_ref, flags_ref):
+def sort_far_kernel(kept, from_x, from_y, plane_x, plane_y, across, own_flags, keep_ref, send_ref, flags_ref):
     for third, mine, other in sorted_groups(kept, from_x, from_y):
         send_ref[:, third * HD : (third + 1) * HD] = other
         keep_ref[:, third * HD : (third + 1) * HD] = mine
     row = lax.broadcasted_iota(jnp.int32, (EXTRA, HD), 0)
     flags = own_flags[...].astype(jnp.float32)
-    for r, value in ((1, edge_x[EXTRA:]), (2, from_y[kept.shape[0] :, :HD]), (3, edge_across[EXTRA:])):
-        flags = jnp.where(row == r, value.astype(jnp.float32), flags)
+    for r, ref in enumerate((plane_x, plane_y, across)):
+        flags = jnp.where(row == r + 1, ref[ref.shape[0] - EXTRA :, :HD].astype(jnp.float32), flags)
     flags = flags.astype(jnp.bfloat16)
     for k in range(3):
         flags_ref[:, k * HD : (k + 1) * HD] = flags
 
 
-def embed_kernel(edge_x, edge_across, raw, gain, stream, conv_w, out_ref, acc, tokens, weights, sems):
-    time_len, site_len, feat_len = raw.shape
+def embed_kernel(rs, raw, plane_x, plane_y, across, conv_w, gain, *refs):
+    streams, (out_ref, acc) = refs[: len(rs)], refs[-2:]
+    for ref in refs[len(rs) : -2]:
+        out_ref[: ref.shape[0]] = ref[...]
     _, _, depth = where_am_i()
-    even = (depth & 1) == 0
-    rows, width = stream.shape
-    parts = weights.shape[0]
-    step = width // parts
-    copies = []
-    for i in range(parts):
-        here = pl.ds(i * step, step)
-        copies.append(pltpu.make_async_copy(conv_w.at[:, here], weights.at[i], sems.at[2 * i]))
-        copies.append(pltpu.make_async_copy(stream.at[:, here], tokens.at[i], sems.at[2 * i + 1]))
-    for copy in copies:
-        copy.start()
-    side, far = edge_x[:time_len].astype(jnp.float32), edge_across[:time_len].astype(jnp.float32)
-    before = jnp.where(even, jnp.where(depth == 2, far, 0.0), side)
-    behind = jnp.where(even, side, jnp.where(depth == 1, far, 0.0))
-    padded = jnp.concatenate([before[:, None], raw[...].astype(jnp.float32), behind[:, None]], axis=1)
-    windows = [padded[:, j : j + site_len].reshape(rows, feat_len).astype(jnp.bfloat16) for j in range(3)]
-    windows = jnp.concatenate(windows, axis=1)
-    total = jnp.zeros((rows, 1), jnp.float32)
-    for i in range(parts):
-        copies[2 * i].wait()
-        copies[2 * i + 1].wait()
-        part = jnp.dot(windows, weights[i], preferred_element_type=jnp.float32) + tokens[i].astype(jnp.float32)
-        acc[:, i * step : (i + 1) * step] = part
-        total += jnp.sum(part * part, axis=1, keepdims=True)
-    scale = lax.rsqrt(total / width + 1e-05)
-    out_ref[...] = (acc[...] * scale * gain[...]).astype(jnp.bfloat16)
+    rows, width = raw.shape[0], conv_w.shape[1]
+    raws = [raw[...]]
+    for ref in (plane_x, plane_y, across):
+        at = ref.shape[0] - EXTRA - rows // 2
+        raws.append(jnp.concatenate([ref[at : at + rows // 2, :HD], ref[at : at + rows // 2, HD:]], axis=0))
+    raws = [value.astype(jnp.float32).reshape(rows // PP, PP, HD) for value in raws]
+    done = out_ref.shape[0] - len(rs) * rows
+    for i, r in enumerate(rs):
+        place = depth ^ r
+        even = (place & 1) == 0
+        side, far = raws[r ^ 1], raws[r ^ 3]
+        before = jnp.where(even, jnp.where(place == 2, far[:, PP - 1 :], 0.0), side[:, PP - 1 :])
+        behind = jnp.where(even, side[:, :1], jnp.where(place == 1, far[:, :1], 0.0))
+        padded = jnp.concatenate([before, raws[r], behind], axis=1)
+        windows = [padded[:, j : j + PP].reshape(rows, HD).astype(jnp.bfloat16) for j in range(3)]
+        windows = jnp.concatenate(windows, axis=1)
+        total, step = jnp.zeros((rows, 1), jnp.float32), width // 4
+        for at in range(0, width, step):
+            here = slice(at, at + step)
+            part = jnp.dot(windows, conv_w[:, here], preferred_element_type=jnp.float32)
+            part += streams[i][:, here].astype(jnp.float32)
+            acc[:, here] = part
+            total += jnp.sum(part * part, axis=1, keepdims=True)
+        scale = lax.rsqrt(total / width + 1e-05)
+        out_ref[done + i * rows : done + (i + 1) * rows] = (acc[...] * scale * gain[...]).astype(jnp.bfloat16)
 
 
 def take(refs, source, core, rows):
@@ -190,12 +189,12 @@
     refs[-1][...] = three_shards(refs[:2], *refs[2:-1])
 
 
-def diagonal_kernel(*refs):
-    pieces, weights, (acc_ref, x_ref) = refs[:6], refs[6:-2], refs[-2:]
-    block, half = pieces[0].shape
-    corners = ((0, 0), (0, half), (block, 0), (block + block // 2, 0), (block, half), (block + block // 2, half))
-    for (row, at), ref in zip(corners, pieces):
-        x_ref[row : row + ref.shape[0], at : at + half] = ref[...]
+def diagonal_kernel(mine, top, bottom, *refs):
+    weights, (acc_ref, x_ref) = refs[:-2], refs[-2:]
+    at = 0
+    for ref in (mine, top, bottom):
+        x_ref[at : at + ref.shape[0]] = ref[...]
+        at += ref.shape[0]
     acc_ref[...] = three_shards([x_ref], *weights)
 
 
@@ -305,70 +304,62 @@
 
     far_raw = swap_z(w_qkv, 2)
 
-    cut = array(size, PAIR)
-    to_x, to_y, kept = call(split_kernel, (cut,) * 3, "v")(w_qkv)
-    own = call(sort_kernel, array(size, 6 * HD), "vvv")(kept, swap_depth(to_x, 1), swap_depth(to_y, 2))
+    raw, stream = raw.reshape(block, feat_len), stream.reshape(block, width)
+    conv_w, gain = conv_w.reshape(3 * feat_len, width), gain.reshape(1, width)
+    more = block // 2 + EXTRA
+    *to, kept, own_flags = call(
+        split_kernel,
+        (array(size + more, PAIR), array(size + more, PAIR), array(block, PAIR), array(size, PAIR), array(EXTRA, HD)),
+        "svv",
+    )(mask.reshape(mask.shape[2]), w_qkv, raw)
+    plane = [swap_depth(t, r) for t, r in zip(to, (1, 2, 3))]
+    own = call(sort_kernel, array(size, 6 * HD), "vvv")(kept, *plane[:2])
     near = swap_z(own, 1)
 
-    edge_x, edge_across, own_flags, sites = call(
-        edge_kernel, (array(2 * EXTRA, HD), array(2 * EXTRA, HD), array(EXTRA, HD), array(*raw.shape)), "sv"
-    )(mask.reshape(mask.shape[2]), raw)
-    edge_x, edge_across = swap_depth(edge_x, 1), swap_depth(edge_across, 3)
-    parts = 4
-    normed = call(
-        embed_kernel,
-        array(block, width),
-        "vvvvaa",
-        scratch=[
-            VMEM((block, width), f32),
-            VMEM((parts, block, width // parts), bf16),
-            VMEM((parts, 3 * feat_len, width // parts), bf16),
-            pltpu.SemaphoreType.DMA((2 * parts,)),
-        ],
-        macs=block * 3 * feat_len * width,
-        limit=53,
-    )(
-        edge_x,
-        edge_across,
-        sites,
-        gain.reshape(1, width),
-        stream.reshape(block, width),
-        conv_w.reshape(3 * feat_len, width),
-    )
-    beside, above = swap_depth(normed, 1), swap_depth(normed, 2)
+    def embed(rs, *streams, finished=()):
+        return call(
+            functools.partial(embed_kernel, rs),
+            array((len(rs) + len(finished)) * block, width),
+            "v" * (6 + len(streams) + len(finished)),
+            scratch=[VMEM((block, width), f32)],
+            macs=len(rs) * block * 3 * feat_len * width,
+        )(raw, *plane, conv_w, gain, *streams, *finished)
+
+    tied = after(stream, plane[2])
+    beside, above = swap_depth(tied, 1), swap_depth(tied, 2)
+    normed = embed((0,), stream)
 
     even = (lax.axis_index("depth") & 1) == 0
     low, to_x, high = (far_raw[:, k * PAIR : (k + 1) * PAIR] for k in range(3))
-    kept = jnp.where(even, low, high)
-    to_y = jnp.concatenate([jnp.where(even, high, low), jnp.concatenate([own_flags, own_flags], axis=1)], axis=0)
+    kept, to_y = jnp.where(even, low, high), jnp.where(even, high, low)
     from_x, from_y = swap_depth(to_x, 1), swap_depth(to_y, 2)
+    beside, above = after(beside, to_x), after(above, to_y)
+    stack = embed((1, 2), beside, above, finished=(normed,))
+    from_x, from_y, stack, near = lax.optimization_barrier((from_x, from_y, stack, near))
     keep, send, flags = call(
         sort_far_kernel,
         (array(size, 3 * HD), array(size, 3 * HD), array(EXTRA, 3 * HD)),
-        "v" * 6,
-    )(kept, from_x, from_y, edge_x, edge_across, own_flags)
-    send, near, beside, above = lax.optimization_barrier((send, near, beside, above))
+        "v" * 7,
+    )(kept, from_x, from_y, *plane, own_flags)
+    diagonal = swap_depth(beside[:, :half], 2), swap_depth(above[:, half:], 1)
     far = jnp.concatenate([keep, swap_core(send)], axis=0)
     last = swap_z(far, 1)
-    stack = jnp.concatenate([normed, beside, above], axis=0)
-    far, near, stack = lax.optimization_barrier((far, near, stack))
+    far, near = lax.optimization_barrier((far, near))
     received = swap_core(jnp.concatenate([own[:, 3 * HD :], near[:, 3 * HD :], flags], axis=0))
     weights = (own, near, received, far)
     early = (stack, swap_core(stack))
-
-    diagonal = [swap_depth(beside[:, :half], 2), swap_depth(above[:, half:], 1)]
     rows = 2 * size
     total = call(partial_kernel, array(6 * block, 3 * HD, kind=f32), "v" * 6, macs=6 * block * 3 * rows * 3 * HD)(
         *early, *weights
     )
-    diagonal = [after(t, total) for t in diagonal]
-    diagonal += [swap_core(t[i * block // 2 : (i + 1) * block // 2]) for t in diagonal for i in range(2)]
+    diagonal = embed((3,), after(jnp.concatenate(diagonal, axis=1), total))
+    swapped = [swap_core(diagonal[i * block // 2 : (i + 1) * block // 2]) for i in range(2)]
     total_diagonal, diagonal = call(
         diagonal_kernel,
         (array(2 * block, 3 * HD, kind=f32), array(2 * block, width)),
-        "v" * 10,
+        "v" * 7,
         macs=2 * block * 3 * rows * 3 * HD,
-    )(*diagonal, *weights)
+    )(diagonal, *swapped, *weights)
     one_head, half_head = array(4, 2 * block, HD), array(2, 2 * block, HD)
     q, k, *v = call(
         finish_kernel, (one_head, one_head, half_head, half_head), "v" * 6, macs=8 * block * rows * 3 * HD

time: 73.5 us -> 72.7 us (0.989)
  waiting for transfers between devices: 25.6 us -> 19.1 us
  starting transfers between devices: 34.3 us -> 37 us
  local copies, waits for them, and re-layouts: 3.3 us -> 4.58 us
  Pallas kernels: 8.93 us -> 9.84 us
  other arithmetic: 0.24 us -> 1.14 us
    ppermute x33 -> x30, waiting for transfers between devices: 25.6 us -> 19.1 us  [hop(): return lax.ppermute(value, ('tm', 'depth'), pairs)]
    ppermute x33 -> x30, starting transfers between devices: 34.3 us -> 37 us  [hop(): return lax.ppermute(value, ('tm', 'depth'), pairs)]
    select_n x1, other arithmetic: 0.03 us -> 1.06 us  [plane_device(): kept, to_y = (jnp.where(even, low, high), jnp.where(even, high, low))]
    slice x4 -> x3, local copies, waits for them, and re-layouts: 0.07 us -> 1.03 us  [the longest x2 0.99 us: plane_device(): diagonal = (swap_depth(beside[:, :half], 2), swap_depth(above[:, half:], 1))]
    pallas_call x4 -> x5, Pallas kernels: 3.13 us -> 4.04 us  [the longest x3 3.34 us: embed(): call(functools.partial(embed_kernel, rs), array((len(rs) + len(finished))...]
    unnamed x9 -> x15, local copies, waits for them, and re-layouts: 3.16 us -> 3.48 us
  transfers between devices with their start and end apart: 33 -> 30, of which waited for: 15 -> 14; matrix products, arithmetic and copies ran while one was open for 1% -> 3% of each run, Pallas kernels for 10% -> 12%
where the time goes in v9:
time: 72.7 us; the launch traced here: 71.9 us
  starting transfers between devices  37 us (51%)
  waiting for transfers between devices  19.1 us (26%)
  Pallas kernels  9.84 us (14%)
  local copies, waits for them, and re-layouts  4.58 us (6%)
  other arithmetic  1.14 us (2%)
    ppermute x30, starting transfers between devices, hop(): return lax.ppermute(value, ('tm', 'depth'), pairs)  37 us
    ppermute x30, waiting for transfers between devices, hop(): return lax.ppermute(value, ('tm', 'depth'), pairs)  19.1 us
    unnamed x15, local copies, waits for them, and re-layouts  3.48 us
    pallas_call x3, Pallas kernels, embed(): call(functools.partial(embed_kernel, rs), array((len(rs) + len(finished))...  3.34 us
  transfers between devices with their start and end apart: 30, of which 14 were waited for; matrix products, arithmetic and copies ran while one was open for 3% of the time, Pallas kernels for 12%

profile of v9, /device:TPU:9, one launch (start us, length us, event | category | flops | bytes accessed | tf_op | source)
XLA Modules:
  0.0 71.9 jit_solution(9946351505888304999)
XLA Ops:
  0.0 2.3 %collective-permute-start = (bf16[256,768]{1,0:T(8,128)(2,1)}, bf16[256,768]{1,0:T(8,128)(2,1)}, u32[]{:S(2)}, u32[]{:S(2)}) collective-permute-start(bf16[256,768]{1,0:T(8,128)(2,1)} %w.1), channel_id=1, source_target_pairs={{0,16},{1,17},{2,18},{3,19},{4,20},{5,21},{6,22},{7,23},{8,24},{9,... | collective-permute-start | bytes 1179656 | tf_op jit(solution)/shard_map/ppermute | solution.py:57
  5.3 2.2 %collective-permute-start.5 = (bf16[128,256]{1,0:T(8,128)(2,1)S(1)}, bf16[128,256]{1,0:T(8,128)(2,1)S(1)}, u32[]{:S(2)}, u32[]{:S(2)}) collective-permute-start(bf16[128,256]{1,0:T(8,128)(2,1)S(1)} %get-tuple-element.39), channel_id=1, source_target_pairs={{0,3},{1,2},{2,1},{3,0},{4,7},{5,6},{6,5},{7,4},{8,11},{9,10},{10,... | collective-permute-start | bytes 196616 | tf_op jit(solution)/shard_map/ppermute | solution.py:57
  8.0 1.8 %collective-permute-done.5.across = bf16[128,256]{1,0:T(8,128)(2,1)S(1)} collective-permute-done((bf16[128,256]{1,0:T(8,128)(2,1)S(1)}, bf16[128,256]{1,0:T(8,128)(2,1)S(1)}, u32[]{:S(2)}, u32[]{:S(2)}) %collective-permute-start.5) | collective-permute-done | bytes 65568 | tf_op jit(solution)/shard_map/ppermute | solution.py:57
  9.8 1.2 %collective-permute-start.6 = (bf16[128,2048]{1,0:T(8,128)(2,1)}, bf16[128,2048]{1,0:T(8,128)(2,1)S(1)}, u32[]{:S(2)}, u32[]{:S(2)}) collective-permute-start(bf16[128,2048]{1,0:T(8,128)(2,1)} %bitcast.13), channel_id=1, source_target_pairs={{0,1},{1,0},{2,3},{3,2},{4,5},{5,4},{6,7},{7,6},{8,9},{9,8},{10,11... | collective-permute-start | bytes 1572872 | tf_op jit(solution)/shard_map/ppermute | solution.py:57
  11.0 1.2 %collective-permute-start.7 = (bf16[128,2048]{1,0:T(8,128)(2,1)}, bf16[128,2048]{1,0:T(8,128)(2,1)}, u32[]{:S(2)}, u32[]{:S(2)}) collective-permute-start(bf16[128,2048]{1,0:T(8,128)(2,1)} %bitcast.14), channel_id=1, source_target_pairs={{0,2},{1,3},{2,0},{3,1},{4,6},{5,7},{6,4},{7,5},{8,10},{9,11},{10,... | collective-permute-start | bytes 1572872 | tf_op jit(solution)/shard_map/ppermute | solution.py:57
  12.3 1.3 %collective-permute-done.3.plane_x.from_x = bf16[336,256]{1,0:T(8,128)(2,1)S(1)} collective-permute-done((bf16[336,256]{1,0:T(8,128)(2,1)S(1)}, bf16[336,256]{1,0:T(8,128)(2,1)S(1)}, u32[]{:S(2)}, u32[]{:S(2)}) %collective-permute-start.3) | collective-permute-done | bytes 172064 | tf_op jit(solution)/shard_map/ppermute | solution.py:57
  14.0 5.8 %collective-permute-done = bf16[256,768]{1,0:T(8,128)(2,1)} collective-permute-done((bf16[256,768]{1,0:T(8,128)(2,1)}, bf16[256,768]{1,0:T(8,128)(2,1)}, u32[]{:S(2)}, u32[]{:S(2)}) %collective-permute-start) | collective-permute-done | bytes 393248 | tf_op jit(solution)/shard_map/ppermute | solution.py:57
  20.9 1.3 %collective-permute-start.1 = (bf16[256,256]{1,0:T(8,128)(2,1)S(1)}, bf16[256,256]{1,0:T(8,128)(2,1)S(1)}, u32[]{:S(2)}, u32[]{:S(2)}) collective-permute-start(bf16[256,256]{1,0:T(8,128)(2,1)S(1)} %get-tuple-element.72), channel_id=1, source_target_pairs={{0,1},{1,0},{2,3},{3,2},{4,5},{5,4},{6,7},{7,6},{8,9},{9,8},{10,11... | collective-permute-start | bytes 393224 | tf_op jit(solution)/shard_map/ppermute | solution.py:57
  22.2 1.2 %collective-permute-start.2 = (bf16[256,256]{1,0:T(8,128)(2,1)S(1)}, bf16[256,256]{1,0:T(8,128)(2,1)S(1)}, u32[]{:S(2)}, u32[]{:S(2)}) collective-permute-start(bf16[256,256]{1,0:T(8,128)(2,1)S(1)} %get-tuple-element.73), channel_id=1, source_target_pairs={{0,2},{1,3},{2,0},{3,1},{4,6},{5,7},{6,4},{7,5},{8,10},{9,11},{10,... | collective-permute-start | bytes 393224 | tf_op jit(solution)/shard_map/ppermute | solution.py:57
  25.1 2.1 %shard_map.66.refs_0_ = bf16[384,2048]{1,0:T(8,128)(2,1)S(1)} custom-call(bf16[128,128]{1,0:T(8,128)(2,1)S(1)} %bitcast.11, bf16[336,256]{1,0:T(8,128)(2,1)S(1)} %collective-permute-done.3.plane_x.from_x, bf16[336,256]{1,0:T(8,128)(2,1)S(1)} %collective-permute-done.4.plane_y.from_y, bf16[128,256]{1,0:T(8,128)(2,1)S(1)} %collective-permute-done.5.across, ...), custom_call_target="tpu_custom_call" | custom-call | flops 402653184 | tf_op jit(solution)/shard_map/pallas_call | solution.py:320
  27.8 2.2 %collective-permute-start.9 = (bf16[384,2048]{1,0:T(8,128)(2,1)S(1)}, bf16[384,2048]{1,0:T(8,128)(2,1)S(1)}, u32[]{:S(2)}, u32[]{:S(2)}) collective-permute-start(bf16[384,2048]{1,0:T(8,128)(2,1)S(1)} %shard_map.66.refs_0_), channel_id=1, source_target_pairs={{0,4},{1,5},{2,6},{3,7},{4,0},{5,1},{6,2},{7,3},{8,12},{9,13},{10,... | collective-permute-start | bytes 4718600 | tf_op jit(solution)/shard_map/ppermute | solution.py:57
  31.3 1.9 %collective-permute-start.11 = (bf16[128,1024]{1,0:T(8,128)(2,1)S(1)}, bf16[128,1024]{1,0:T(8,128)(2,1)S(1)}, u32[]{:S(2)}, u32[]{:S(2)}) collective-permute-start(bf16[128,1024]{1,0:T(8,128)(2,1)S(1)} %slice.31), channel_id=1, source_target_pairs={{0,1},{1,0},{2,3},{3,2},{4,5},{5,4},{6,7},{7,6},{8,9},{9,8},{10,11... | collective-permute-start | bytes 786440 | tf_op jit(solution)/shard_map/ppermute | solution.py:57
  34.7 3.9 %collective-permute-done.10 = bf16[128,1024]{1,0:T(8,128)(2,1)S(1)} collective-permute-done((bf16[128,1024]{1,0:T(8,128)(2,1)S(1)}, bf16[128,1024]{1,0:T(8,128)(2,1)S(1)}, u32[]{:S(2)}, u32[]{:S(2)}) %collective-permute-start.10) | collective-permute-done | bytes 262176 | tf_op jit(solution)/shard_map/ppermute | solution.py:57
  39.1 1.4 %shard_map.69.refs_4_ = f32[768,384]{1,0:T(8,128)S(1)} custom-call(bf16[384,2048]{1,0:T(8,128)(2,1)S(1)} %shard_map.66.refs_0_, bf16[384,2048]{1,0:T(8,128)(2,1)S(1)} %collective-permute-done.9.refs_1_, bf16[256,768]{1,0:T(8,128)(2,1)S(1)} %shard_map.67.refs_2_.refs_0_, bf16[256,768]{1,0:T(8,128)(2,1)S(1)} %collective-permute-done.8.refs_3_.refs_1_, ...), custom_call_target="tpu_custom_call" | custom-call | flops 905969664 | tf_op jit(solution)/shard_map/pallas_call | solution.py:352
  41.2 1.4 %collective-permute-start.14 = (bf16[64,2048]{1,0:T(8,128)(2,1)S(1)}, bf16[64,2048]{1,0:T(8,128)(2,1)S(1)}, u32[]{:S(2)}, u32[]{:S(2)}) collective-permute-start(bf16[64,2048]{1,0:T(8,128)(2,1)S(1)} %get-tuple-element.70), channel_id=1, source_target_pairs={{0,4},{1,5},{2,6},{3,7},{4,0},{5,1},{6,2},{7,3},{8,12},{9,13},{10,... | collective-permute-start | bytes 786440 | tf_op jit(solution)/shard_map/ppermute | solution.py:57
  46.2 4.2 %collective-permute-start.18 = (bf16[4,256,128]{2,1,0:T(8,128)(2,1)S(1)}, bf16[4,256,128]{2,1,0:T(8,128)(2,1)S(1)}, u32[]{:S(2)}, u32[]{:S(2)}) collective-permute-start(bf16[4,256,128]{2,1,0:T(8,128)(2,1)S(1)} %get-tuple-element.58.own), channel_id=1, source_target_pairs={{8,16},{9,17},{10,18},{11,19},{12,20},{13,21},{14,22},{15,23},{16,... | collective-permute-start | bytes 786440 | tf_op jit(solution)/shard_map/ppermute | solution.py:57
  50.4 1.9 %collective-permute-start.23 = (bf16[2,256,128]{2,1,0:T(8,128)(2,1)S(1)}, bf16[2,256,128]{2,1,0:T(8,128)(2,1)S(1)}, u32[]{:S(2)}, u32[]{:S(2)}) collective-permute-start(bf16[2,256,128]{2,1,0:T(8,128)(2,1)S(1)} %get-tuple-element.62.own), channel_id=1, source_target_pairs={{8,16},{9,17},{10,18},{11,19},{12,20},{13,21},{14,22},{15,23},{16,... | collective-permute-start | bytes 393224 | tf_op jit(solution)/shard_map/ppermute | solution.py:57
  52.8 3.4 %collective-permute-start.20 = (bf16[2,256,128]{2,1,0:T(8,128)(2,1)S(1)}, bf16[2,256,128]{2,1,0:T(8,128)(2,1)S(1)}, u32[]{:S(2)}, u32[]{:S(2)}) collective-permute-start(bf16[2,256,128]{2,1,0:T(8,128)(2,1)S(1)} %get-tuple-element.59.own), channel_id=1, source_target_pairs={{8,16},{9,17},{10,18},{11,19},{12,20},{13,21},{14,22},{15,23},{16,... | collective-permute-start | bytes 393224 | tf_op jit(solution)/shard_map/ppermute | solution.py:57
  56.3 1.2 %shard_map.73.weights = bf16[4,256,640]{2,1,0:T(8,128)(2,1)S(1)} custom-call(bf16[4,256,128]{2,1,0:T(8,128)(2,1)S(1)} %get-tuple-element.57.q_ref, bf16[4,256,128]{2,1,0:T(8,128)(2,1)S(1)} %collective-permute-done.17.outer, bf16[4,256,128]{2,1,0:T(8,128)(2,1)S(1)} %get-tuple-element.58.own, bf16[4,256,128]{2,1,0:T(8,128)(2,1)S(1)} %collective-permute-done.18.middle, ...), custom_call_target="tpu_custom_call" | custom-call | flops 167772160 | tf_op jit(solution)/shard_map/pallas_call | solution.py:368
  57.5 1.2 %collective-permute-done.23.middle = bf16[2,256,128]{2,1,0:T(8,128)(2,1)S(1)} collective-permute-done((bf16[2,256,128]{2,1,0:T(8,128)(2,1)S(1)}, bf16[2,256,128]{2,1,0:T(8,128)(2,1)S(1)}, u32[]{:S(2)}, u32[]{:S(2)}) %collective-permute-start.23) | collective-permute-done | bytes 131104 | tf_op jit(solution)/shard_map/ppermute | solution.py:57
  58.9 1.2 %collective-permute-start.28 = (bf16[128,128]{1,0:T(8,128)(2,1)S(1)}, bf16[128,128]{1,0:T(8,128)(2,1)S(1)}, u32[]{:S(2)}, u32[]{:S(2)}) collective-permute-start(bf16[128,128]{1,0:T(8,128)(2,1)S(1)} %get-tuple-element.67), channel_id=1, source_target_pairs={{0,3},{1,2},{2,1},{3,0},{4,7},{5,6},{6,5},{7,4},{8,11},{9,10},{10,... | collective-permute-start | bytes 98312 | tf_op jit(solution)/shard_map/ppermute | solution.py:57
  60.1 4.5 %collective-permute-start.29 = (bf16[128,128]{1,0:T(8,128)(2,1)S(1)}, bf16[128,128]{1,0:T(8,128)(2,1)S(1)}, u32[]{:S(2)}, u32[]{:S(2)}) collective-permute-start(bf16[128,128]{1,0:T(8,128)(2,1)S(1)} %get-tuple-element.68), channel_id=1, source_target_pairs={{0,7},{1,6},{2,5},{3,4},{4,3},{5,2},{6,1},{7,0},{8,15},{9,14},{10,... | collective-permute-start | bytes 98312 | tf_op jit(solution)/shard_map/ppermute | solution.py:57
  66.9 2.2 %collective-permute-start.25 = (bf16[128,128]{1,0:T(8,128)(2,1)S(1)}, bf16[128,128]{1,0:T(8,128)(2,1)S(1)}, u32[]{:S(2)}, u32[]{:S(2)}) collective-permute-start(bf16[128,128]{1,0:T(8,128)(2,1)S(1)} %get-tuple-element.64), channel_id=1, source_target_pairs={{0,5},{1,4},{2,7},{3,6},{4,1},{5,0},{6,3},{7,2},{8,13},{9,12},{10,... | collective-permute-start | bytes 98312 | tf_op jit(solution)/shard_map/ppermute | solution.py:57
  69.1 2.0 %collective-permute-done.25.refs_3_ = bf16[128,128]{1,0:T(8,128)(2,1)S(1)} collective-permute-done((bf16[128,128]{1,0:T(8,128)(2,1)S(1)}, bf16[128,128]{1,0:T(8,128)(2,1)S(1)}, u32[]{:S(2)}, u32[]{:S(2)}) %collective-permute-start.25) | collective-permute-done | bytes 32800 | tf_op jit(solution)/shard_map/ppermute | solution.py:57
  (75 shorter events, 18.5 us)
Async XLA Ops:
  0.0 19.8 %collective-permute-start = (bf16[256,768]{1,0:T(8,128)(2,1)}, bf16[256,768]{1,0:T(8,128)(2,1)}, u32[]{:S(2)}, u32[]{:S(2)}) collective-permute-start(bf16[256,768]{1,0:T(8,128)(2,1)} %w.1), channel_id=1, source_target_pairs={{0,16},{1,17},{2,18},{3,19},{4,20},{5,21},{6,22},{7,23},{8,24},{9,... | collective-permute-start | bytes 1179656 | tf_op jit(solution)/shard_map/ppermute | solution.py:57
  5.3 4.5 %collective-permute-start.5 = (bf16[128,256]{1,0:T(8,128)(2,1)S(1)}, bf16[128,256]{1,0:T(8,128)(2,1)S(1)}, u32[]{:S(2)}, u32[]{:S(2)}) collective-permute-start(bf16[128,256]{1,0:T(8,128)(2,1)S(1)} %get-tuple-element.39), channel_id=1, source_target_pairs={{0,3},{1,2},{2,1},{3,0},{4,7},{5,6},{6,5},{7,4},{8,11},{9,10},{10,... | collective-permute-start | bytes 196616 | tf_op jit(solution)/shard_map/ppermute | solution.py:57
  7.6 6.0 %collective-permute-start.3 = (bf16[336,256]{1,0:T(8,128)(2,1)S(1)}, bf16[336,256]{1,0:T(8,128)(2,1)S(1)}, u32[]{:S(2)}, u32[]{:S(2)}) collective-permute-start(bf16[336,256]{1,0:T(8,128)(2,1)S(1)} %get-tuple-element.37), channel_id=1, source_target_pairs={{0,1},{1,0},{2,3},{3,2},{4,5},{5,4},{6,7},{7,6},{8,9},{9,8},{10,11... | collective-permute-start | bytes 516104 | tf_op jit(solution)/shard_map/ppermute | solution.py:57
  7.8 5.8 %collective-permute-start.4 = (bf16[336,256]{1,0:T(8,128)(2,1)S(1)}, bf16[336,256]{1,0:T(8,128)(2,1)S(1)}, u32[]{:S(2)}, u32[]{:S(2)}) collective-permute-start(bf16[336,256]{1,0:T(8,128)(2,1)S(1)} %get-tuple-element.38), channel_id=1, source_target_pairs={{0,2},{1,3},{2,0},{3,1},{4,6},{5,7},{6,4},{7,5},{8,10},{9,11},{10,... | collective-permute-start | bytes 516104 | tf_op jit(solution)/shard_map/ppermute | solution.py:57
  9.8 15.3 %collective-permute-start.6 = (bf16[128,2048]{1,0:T(8,128)(2,1)}, bf16[128,2048]{1,0:T(8,128)(2,1)S(1)}, u32[]{:S(2)}, u32[]{:S(2)}) collective-permute-start(bf16[128,2048]{1,0:T(8,128)(2,1)} %bitcast.13), channel_id=1, source_target_pairs={{0,1},{1,0},{2,3},{3,2},{4,5},{5,4},{6,7},{7,6},{8,9},{9,8},{10,11... | collective-permute-start | bytes 1572872 | tf_op jit(solution)/shard_map/ppermute | solution.py:57
  11.0 14.1 %collective-permute-start.7 = (bf16[128,2048]{1,0:T(8,128)(2,1)}, bf16[128,2048]{1,0:T(8,128)(2,1)}, u32[]{:S(2)}, u32[]{:S(2)}) collective-permute-start(bf16[128,2048]{1,0:T(8,128)(2,1)} %bitcast.14), channel_id=1, source_target_pairs={{0,2},{1,3},{2,0},{3,1},{4,6},{5,7},{6,4},{7,5},{8,10},{9,11},{10,... | collective-permute-start | bytes 1572872 | tf_op jit(solution)/shard_map/ppermute | solution.py:57
  13.7 14.0 %collective-permute-start.8 = (bf16[256,768]{1,0:T(8,128)(2,1)S(1)}, bf16[256,768]{1,0:T(8,128)(2,1)S(1)}, u32[]{:S(2)}, u32[]{:S(2)}) collective-permute-start(bf16[256,768]{1,0:T(8,128)(2,1)S(1)} %shard_map.67.refs_2_.refs_0_), channel_id=1, source_target_pairs={{0,8},{1,9},{2,10},{3,11},{4,12},{5,13},{6,14},{7,15},{8,0},{9,1},... | collective-permute-start | bytes 1179656 | tf_op jit(solution)/shard_map/ppermute | solution.py:57
  20.9 6.7 %collective-permute-start.1 = (bf16[256,256]{1,0:T(8,128)(2,1)S(1)}, bf16[256,256]{1,0:T(8,128)(2,1)S(1)}, u32[]{:S(2)}, u32[]{:S(2)}) collective-permute-start(bf16[256,256]{1,0:T(8,128)(2,1)S(1)} %get-tuple-element.72), channel_id=1, source_target_pairs={{0,1},{1,0},{2,3},{3,2},{4,5},{5,4},{6,7},{7,6},{8,9},{9,8},{10,11... | collective-permute-start | bytes 393224 | tf_op jit(solution)/shard_map/ppermute | solution.py:57
  22.2 5.6 %collective-permute-start.2 = (bf16[256,256]{1,0:T(8,128)(2,1)S(1)}, bf16[256,256]{1,0:T(8,128)(2,1)S(1)}, u32[]{:S(2)}, u32[]{:S(2)}) collective-permute-start(bf16[256,256]{1,0:T(8,128)(2,1)S(1)} %get-tuple-element.73), channel_id=1, source_target_pairs={{0,2},{1,3},{2,0},{3,1},{4,6},{5,7},{6,4},{7,5},{8,10},{9,11},{10,... | collective-permute-start | bytes 393224 | tf_op jit(solution)/shard_map/ppermute | solution.py:57
  27.8 11.3 %collective-permute-start.9 = (bf16[384,2048]{1,0:T(8,128)(2,1)S(1)}, bf16[384,2048]{1,0:T(8,128)(2,1)S(1)}, u32[]{:S(2)}, u32[]{:S(2)}) collective-permute-start(bf16[384,2048]{1,0:T(8,128)(2,1)S(1)} %shard_map.66.refs_0_), channel_id=1, source_target_pairs={{0,4},{1,5},{2,6},{3,7},{4,0},{5,1},{6,2},{7,3},{8,12},{9,13},{10,... | collective-permute-start | bytes 4718600 | tf_op jit(solution)/shard_map/ppermute | solution.py:57
  31.2 7.5 %collective-permute-start.10 = (bf16[128,1024]{1,0:T(8,128)(2,1)S(1)}, bf16[128,1024]{1,0:T(8,128)(2,1)S(1)}, u32[]{:S(2)}, u32[]{:S(2)}) collective-permute-start(bf16[128,1024]{1,0:T(8,128)(2,1)S(1)} %slice.30), channel_id=1, source_target_pairs={{0,2},{1,3},{2,0},{3,1},{4,6},{5,7},{6,4},{7,5},{8,10},{9,11},{10,... | collective-permute-start | bytes 786440 | tf_op jit(solution)/shard_map/ppermute | solution.py:57
  31.3 7.8 %collective-permute-start.11 = (bf16[128,1024]{1,0:T(8,128)(2,1)S(1)}, bf16[128,1024]{1,0:T(8,128)(2,1)S(1)}, u32[]{:S(2)}, u32[]{:S(2)}) collective-permute-start(bf16[128,1024]{1,0:T(8,128)(2,1)S(1)} %slice.31), channel_id=1, source_target_pairs={{0,1},{1,0},{2,3},{3,2},{4,5},{5,4},{6,7},{7,6},{8,9},{9,8},{10,11... | collective-permute-start | bytes 786440 | tf_op jit(solution)/shard_map/ppermute | solution.py:57
  33.4 5.7 %collective-permute-start.13 = (bf16[528,384]{1,0:T(8,128)(2,1)S(1)}, bf16[528,384]{1,0:T(8,128)(2,1)S(1)}, u32[]{:S(2)}, u32[]{:S(2)}) collective-permute-start(bf16[528,384]{1,0:T(8,128)(2,1)S(1)} %pad_maximum_fusion.1), channel_id=1, source_target_pairs={{0,4},{1,5},{2,6},{3,7},{4,0},{5,1},{6,2},{7,3},{8,12},{9,13},{10,... | collective-permute-start | bytes 1216520 | tf_op jit(solution)/shard_map/ppermute | solution.py:57
  34.4 10.7 %collective-permute-start.16 = (bf16[512,384]{1,0:T(8,128)(2,1)S(1)}, bf16[512,384]{1,0:T(8,128)(2,1)S(1)}, u32[]{:S(2)}, u32[]{:S(2)}) collective-permute-start(bf16[512,384]{1,0:T(8,128)(2,1)S(1)} %constant_dynamic-update-slice_fusion.refs_5_.refs_3_), channel_id=1, source_target_pairs={{0,8},{1,9},{2,10},{3,11},{4,12},{5,13},{6,14},{7,15},{8,0},{9,1},... | collective-permute-start | bytes 1179656 | tf_op jit(solution)/shard_map/ppermute | solution.py:57
  45.8 7.0 %collective-permute-start.17 = (bf16[4,256,128]{2,1,0:T(8,128)(2,1)S(1)}, bf16[4,256,128]{2,1,0:T(8,128)(2,1)S(1)}, u32[]{:S(2)}, u32[]{:S(2)}) collective-permute-start(bf16[4,256,128]{2,1,0:T(8,128)(2,1)S(1)} %get-tuple-element.58.own), channel_id=1, source_target_pairs={{0,8},{1,9},{2,10},{3,11},{4,12},{5,13},{6,14},{7,15},{8,0},{9,1},... | collective-permute-start | bytes 786440 | tf_op jit(solution)/shard_map/ppermute | solution.py:57
  46.2 10.1 %collective-permute-start.18 = (bf16[4,256,128]{2,1,0:T(8,128)(2,1)S(1)}, bf16[4,256,128]{2,1,0:T(8,128)(2,1)S(1)}, u32[]{:S(2)}, u32[]{:S(2)}) collective-permute-start(bf16[4,256,128]{2,1,0:T(8,128)(2,1)S(1)} %get-tuple-element.58.own), channel_id=1, source_target_pairs={{8,16},{9,17},{10,18},{11,19},{12,20},{13,21},{14,22},{15,23},{16,... | collective-permute-start | bytes 786440 | tf_op jit(solution)/shard_map/ppermute | solution.py:57
  50.4 7.1 %collective-permute-start.22 = (bf16[2,256,128]{2,1,0:T(8,128)(2,1)S(1)}, bf16[2,256,128]{2,1,0:T(8,128)(2,1)S(1)}, u32[]{:S(2)}, u32[]{:S(2)}) collective-permute-start(bf16[2,256,128]{2,1,0:T(8,128)(2,1)S(1)} %get-tuple-element.62.own), channel_id=1, source_target_pairs={{0,8},{1,9},{2,10},{3,11},{4,12},{5,13},{6,14},{7,15},{8,0},{9,1},... | collective-permute-start | bytes 393224 | tf_op jit(solution)/shard_map/ppermute | solution.py:57
  50.4 8.2 %collective-permute-start.23 = (bf16[2,256,128]{2,1,0:T(8,128)(2,1)S(1)}, bf16[2,256,128]{2,1,0:T(8,128)(2,1)S(1)}, u32[]{:S(2)}, u32[]{:S(2)}) collective-permute-start(bf16[2,256,128]{2,1,0:T(8,128)(2,1)S(1)} %get-tuple-element.62.own), channel_id=1, source_target_pairs={{8,16},{9,17},{10,18},{11,19},{12,20},{13,21},{14,22},{15,23},{16,... | collective-permute-start | bytes 393224 | tf_op jit(solution)/shard_map/ppermute | solution.py:57
  52.4 12.2 %collective-permute-start.19 = (bf16[2,256,128]{2,1,0:T(8,128)(2,1)S(1)}, bf16[2,256,128]{2,1,0:T(8,128)(2,1)S(1)}, u32[]{:S(2)}, u32[]{:S(2)}) collective-permute-start(bf16[2,256,128]{2,1,0:T(8,128)(2,1)S(1)} %get-tuple-element.59.own), channel_id=1, source_target_pairs={{0,8},{1,9},{2,10},{3,11},{4,12},{5,13},{6,14},{7,15},{8,0},{9,1},... | collective-permute-start | bytes 393224 | tf_op jit(solution)/shard_map/ppermute | solution.py:57
  52.8 11.8 %collective-permute-start.20 = (bf16[2,256,128]{2,1,0:T(8,128)(2,1)S(1)}, bf16[2,256,128]{2,1,0:T(8,128)(2,1)S(1)}, u32[]{:S(2)}, u32[]{:S(2)}) collective-permute-start(bf16[2,256,128]{2,1,0:T(8,128)(2,1)S(1)} %get-tuple-element.59.own), channel_id=1, source_target_pairs={{8,16},{9,17},{10,18},{11,19},{12,20},{13,21},{14,22},{15,23},{16,... | collective-permute-start | bytes 393224 | tf_op jit(solution)/shard_map/ppermute | solution.py:57
  58.9 8.0 %collective-permute-start.28 = (bf16[128,128]{1,0:T(8,128)(2,1)S(1)}, bf16[128,128]{1,0:T(8,128)(2,1)S(1)}, u32[]{:S(2)}, u32[]{:S(2)}) collective-permute-start(bf16[128,128]{1,0:T(8,128)(2,1)S(1)} %get-tuple-element.67), channel_id=1, source_target_pairs={{0,3},{1,2},{2,1},{3,0},{4,7},{5,6},{6,5},{7,4},{8,11},{9,10},{10,... | collective-permute-start | bytes 98312 | tf_op jit(solution)/shard_map/ppermute | solution.py:57
  60.1 9.0 %collective-permute-start.29 = (bf16[128,128]{1,0:T(8,128)(2,1)S(1)}, bf16[128,128]{1,0:T(8,128)(2,1)S(1)}, u32[]{:S(2)}, u32[]{:S(2)}) collective-permute-start(bf16[128,128]{1,0:T(8,128)(2,1)S(1)} %get-tuple-element.68), channel_id=1, source_target_pairs={{0,7},{1,6},{2,5},{3,4},{4,3},{5,2},{6,1},{7,0},{8,15},{9,14},{10,... | collective-permute-start | bytes 98312 | tf_op jit(solution)/shard_map/ppermute | solution.py:57
  64.9 4.2 %collective-permute-start.26 = (bf16[128,128]{1,0:T(8,128)(2,1)S(1)}, bf16[128,128]{1,0:T(8,128)(2,1)S(1)}, u32[]{:S(2)}, u32[]{:S(2)}) collective-permute-start(bf16[128,128]{1,0:T(8,128)(2,1)S(1)} %get-tuple-element.65), channel_id=1, source_target_pairs={{0,2},{1,3},{2,0},{3,1},{4,6},{5,7},{6,4},{7,5},{8,10},{9,11},{10,... | collective-permute-start | bytes 98312 | tf_op jit(solution)/shard_map/ppermute | solution.py:57
  66.9 4.2 %collective-permute-start.25 = (bf16[128,128]{1,0:T(8,128)(2,1)S(1)}, bf16[128,128]{1,0:T(8,128)(2,1)S(1)}, u32[]{:S(2)}, u32[]{:S(2)}) collective-permute-start(bf16[128,128]{1,0:T(8,128)(2,1)S(1)} %get-tuple-element.64), channel_id=1, source_target_pairs={{0,5},{1,4},{2,7},{3,6},{4,1},{5,0},{6,3},{7,2},{8,13},{9,12},{10,... | collective-permute-start | bytes 98312 | tf_op jit(solution)/shard_map/ppermute | solution.py:57
  (13 other events, 81.0 us)

commit v10 on v9

--- a/solution.py
+++ b/solution.py
@@ -138,10 +138,14 @@
         flags_ref[:, k * HD : (k + 1) * HD] = flags
 
 
-def embed_kernel(rs, raw, plane_x, plane_y, across, conv_w, gain, *refs):
-    streams, (out_ref, acc) = refs[: len(rs)], refs[-2:]
-    for ref in refs[len(rs) : -2]:
+def embed_kernel(rs, more, raw, plane_x, plane_y, across, conv_w, gain, *refs):
+    count = len(rs)
+    streams, finished, (out_ref, *onward, acc) = refs[:count], refs[count : count + more], refs[count + more :]
+    for ref in finished:
         out_ref[: ref.shape[0]] = ref[...]
+    for i, ref in enumerate(onward):
+        half = ref.shape[1]
+        ref[...] = streams[i][:, i * half : (i + 1) * half]
     _, _, depth = where_am_i()
     rows, width = raw.shape[0], conv_w.shape[1]
     raws = [raw[...]]
@@ -317,9 +321,10 @@
     near = swap_z(own, 1)
 
     def embed(rs, *streams, finished=()):
+        out = (array((len(rs) + len(finished)) * block, width),) + (array(block, half),) * (len(rs) - 1) * 2
         return call(
-            functools.partial(embed_kernel, rs),
-            array((len(rs) + len(finished)) * block, width),
+            functools.partial(embed_kernel, rs, len(finished)),
+            out,
             "v" * (6 + len(streams) + len(finished)),
             scratch=[VMEM((block, width), f32)],
             macs=len(rs) * block * 3 * feat_len * width,
@@ -327,33 +332,35 @@
 
     tied = after(stream, plane[2])
     beside, above = swap_depth(tied, 1), swap_depth(tied, 2)
-    normed = embed((0,), stream)
+    (normed,) = embed((0,), stream)
+    far_raw = after(far_raw, normed)
 
     even = (lax.axis_index("depth") & 1) == 0
     low, to_x, high = (far_raw[:, k * PAIR : (k + 1) * PAIR] for k in range(3))
     kept, to_y = jnp.where(even, low, high), jnp.where(even, high, low)
     from_x, from_y = swap_depth(to_x, 1), swap_depth(to_y, 2)
     beside, above = after(beside, to_x), after(above, to_y)
-    stack = embed((1, 2), beside, above, finished=(normed,))
+    stack, *diagonal = embed((1, 2), beside, above, finished=(normed,))
     from_x, from_y, stack, near = lax.optimization_barrier((from_x, from_y, stack, near))
     keep, send, flags = call(
         sort_far_kernel,
         (array(size, 3 * HD), array(size, 3 * HD), array(EXTRA, 3 * HD)),
         "v" * 7,
     )(kept, from_x, from_y, *plane, own_flags)
-    diagonal = swap_depth(beside[:, :half], 2), swap_depth(above[:, half:], 1)
+    diagonal = swap_depth(diagonal[0], 2), swap_depth(diagonal[1], 1)
     far = jnp.concatenate([keep, swap_core(send)], axis=0)
     last = swap_z(far, 1)
-    far, near = lax.optimization_barrier((far, near))
+    far, near, stack = lax.optimization_barrier((far, near, stack))
     received = swap_core(jnp.concatenate([own[:, 3 * HD :], near[:, 3 * HD :], flags], axis=0))
     weights = (own, near, received, far)
+    piece = block // 2
     early = (stack, swap_core(stack))
     rows = 2 * size
     total = call(partial_kernel, array(6 * block, 3 * HD, kind=f32), "v" * 6, macs=6 * block * 3 * rows * 3 * HD)(
         *early, *weights
     )
-    diagonal = embed((3,), after(jnp.concatenate(diagonal, axis=1), total))
-    swapped = [swap_core(diagonal[i * block // 2 : (i + 1) * block // 2]) for i in range(2)]
+    (diagonal,) = embed((3,), after(jnp.concatenate(diagonal, axis=1), total))
+    swapped = [swap_core(diagonal[:piece]), swap_core(diagonal[piece:])]
     total_diagonal, diagonal = call(
         diagonal_kernel,
         (array(2 * block, 3 * HD, kind=f32), array(2 * block, width)),

time: 72.7 us -> 73.2 us (level)
  the two profiles are of different devices: /device:TPU:9 before, /device:TPU:16 now
where the time goes in v10:
time: 73.2 us; the launch traced here: 72.8 us
  starting transfers between devices  34 us (46%)
  waiting for transfers between devices  24.1 us (33%)
  Pallas kernels  8.82 us (12%)
  local copies, waits for them, and re-layouts  5.42 us (7%)
    ppermute x30, starting transfers between devices, hop(): return lax.ppermute(value, ('tm', 'depth'), pairs)  34 us
    ppermute x30, waiting for transfers between devices, hop(): return lax.ppermute(value, ('tm', 'depth'), pairs)  24.1 us
    unnamed x21, local copies, waits for them, and re-layouts  5.31 us
    pallas_call x3, Pallas kernels, embed(): call(functools.partial(embed_kernel, rs, len(finished)), out, 'v' * (6 +...  2.35 us
  transfers between devices with their start and end apart: 30, of which 17 were waited for; matrix products, arithmetic and copies ran while one was open for 0% of the time, Pallas kernels for 10%

profile of v10, /device:TPU:16, one launch (start us, length us, event | category | flops | bytes accessed | tf_op | source)
XLA Modules:
  0.0 72.8 jit_solution(6169661792362309481)
XLA Ops:
  3.0 2.8 %collective-permute-start.3 = (bf16[128,256]{1,0:T(8,128)(2,1)S(1)}, bf16[128,256]{1,0:T(8,128)(2,1)S(1)}, u32[]{:S(2)}, u32[]{:S(2)}) collective-permute-start(bf16[128,256]{1,0:T(8,128)(2,1)S(1)} %get-tuple-element.44), channel_id=1, source_target_pairs={{0,3},{1,2},{2,1},{3,0},{4,7},{5,6},{6,5},{7,4},{8,11},{9,10},{10,... | collective-permute-start | bytes 196616 | tf_op jit(solution)/shard_map/ppermute | solution.py:57
  6.6 2.2 %collective-permute-done.3.across = bf16[128,256]{1,0:T(8,128)(2,1)S(1)} collective-permute-done((bf16[128,256]{1,0:T(8,128)(2,1)S(1)}, bf16[128,256]{1,0:T(8,128)(2,1)S(1)}, u32[]{:S(2)}, u32[]{:S(2)}) %collective-permute-start.3) | collective-permute-done | bytes 65568 | tf_op jit(solution)/shard_map/ppermute | solution.py:57
  8.8 2.0 %collective-permute-start.7 = (bf16[128,2048]{1,0:T(8,128)(2,1)}, bf16[128,2048]{1,0:T(8,128)(2,1)S(1)}, u32[]{:S(2)}, u32[]{:S(2)}) collective-permute-start(bf16[128,2048]{1,0:T(8,128)(2,1)} %bitcast.13), channel_id=1, source_target_pairs={{0,2},{1,3},{2,0},{3,1},{4,6},{5,7},{6,4},{7,5},{8,10},{9,11},{10,... | collective-permute-start | bytes 1572872 | tf_op jit(solution)/shard_map/ppermute | solution.py:57
  10.8 1.5 %collective-permute-start.6 = (bf16[128,2048]{1,0:T(8,128)(2,1)}, bf16[128,2048]{1,0:T(8,128)(2,1)S(1)}, u32[]{:S(2)}, u32[]{:S(2)}) collective-permute-start(bf16[128,2048]{1,0:T(8,128)(2,1)} %bitcast.14), channel_id=1, source_target_pairs={{0,1},{1,0},{2,3},{3,2},{4,5},{5,4},{6,7},{7,6},{8,9},{9,8},{10,11... | collective-permute-start | bytes 1572872 | tf_op jit(solution)/shard_map/ppermute | solution.py:57
  13.8 1.6 %collective-permute-start.8 = (bf16[256,768]{1,0:T(8,128)(2,1)S(1)}, bf16[256,768]{1,0:T(8,128)(2,1)S(1)}, u32[]{:S(2)}, u32[]{:S(2)}) collective-permute-start(bf16[256,768]{1,0:T(8,128)(2,1)S(1)} %shard_map.67.refs_2_.refs_0_), channel_id=1, source_target_pairs={{0,8},{1,9},{2,10},{3,11},{4,12},{5,13},{6,14},{7,15},{8,0},{9,1},... | collective-permute-start | bytes 1179656 | tf_op jit(solution)/shard_map/ppermute | solution.py:57
  15.5 1.4 %copy-done = bf16[3,128,2048]{2,1,0:T(8,128)(2,1)S(1)} copy-done((bf16[3,128,2048]{2,1,0:T(8,128)(2,1)S(1)}, bf16[3,128,2048]{2,1,0:T(8,128)(2,1)}, u32[]{:S(2)}) %copy-start) | copy-done | bytes 1572888
  19.0 1.6 %collective-permute-start.4 = (bf16[256,256]{1,0:T(8,128)(2,1)S(1)}, bf16[256,256]{1,0:T(8,128)(2,1)S(1)}, u32[]{:S(2)}, u32[]{:S(2)}) collective-permute-start(bf16[256,256]{1,0:T(8,128)(2,1)S(1)} %get-tuple-element.82), channel_id=1, source_target_pairs={{0,1},{1,0},{2,3},{3,2},{4,5},{5,4},{6,7},{7,6},{8,9},{9,8},{10,11... | collective-permute-start | bytes 393224 | tf_op jit(solution)/shard_map/ppermute | solution.py:57
  21.3 3.5 %collective-permute-done.7.refs_1_ = bf16[128,2048]{1,0:T(8,128)(2,1)S(1)} collective-permute-done((bf16[128,2048]{1,0:T(8,128)(2,1)}, bf16[128,2048]{1,0:T(8,128)(2,1)S(1)}, u32[]{:S(2)}, u32[]{:S(2)}) %collective-permute-start.7) | collective-permute-done | bytes 524320 | tf_op jit(solution)/shard_map/ppermute | solution.py:57
  26.2 1.6 %collective-permute-done.8.refs_3_.refs_1_ = bf16[256,768]{1,0:T(8,128)(2,1)S(1)} collective-permute-done((bf16[256,768]{1,0:T(8,128)(2,1)S(1)}, bf16[256,768]{1,0:T(8,128)(2,1)S(1)}, u32[]{:S(2)}, u32[]{:S(2)}) %collective-permute-start.8) | collective-permute-done | bytes 393248 | tf_op jit(solution)/shard_map/ppermute | solution.py:57
  28.0 1.4 %collective-permute-done.9 = bf16[256,384]{1,0:T(8,128)(2,1)S(1)} collective-permute-done((bf16[256,384]{1,0:T(8,128)(2,1)S(1)}, bf16[256,384]{1,0:T(8,128)(2,1)S(1)}, u32[]{:S(2)}, u32[]{:S(2)}) %collective-permute-start.9) | collective-permute-done | bytes 196640 | tf_op jit(solution)/shard_map/ppermute | solution.py:57
  29.7 1.6 %collective-permute-start.11 = (bf16[128,1024]{1,0:T(8,128)(2,1)S(1)}, bf16[128,1024]{1,0:T(8,128)(2,1)S(1)}, u32[]{:S(2)}, u32[]{:S(2)}) collective-permute-start(bf16[128,1024]{1,0:T(8,128)(2,1)S(1)} %get-tuple-element.59), channel_id=1, source_target_pairs={{0,2},{1,3},{2,0},{3,1},{4,6},{5,7},{6,4},{7,5},{8,10},{9,11},{10,... | collective-permute-start | bytes 786440 | tf_op jit(solution)/shard_map/ppermute | solution.py:57
  31.3 1.5 %collective-permute-start.12 = (bf16[128,1024]{1,0:T(8,128)(2,1)S(1)}, bf16[128,1024]{1,0:T(8,128)(2,1)S(1)}, u32[]{:S(2)}, u32[]{:S(2)}) collective-permute-start(bf16[128,1024]{1,0:T(8,128)(2,1)S(1)} %get-tuple-element.60), channel_id=1, source_target_pairs={{0,1},{1,0},{2,3},{3,2},{4,5},{5,4},{6,7},{7,6},{8,9},{9,8},{10,11... | collective-permute-start | bytes 786440 | tf_op jit(solution)/shard_map/ppermute | solution.py:57
  32.9 2.5 %collective-permute-start.16 = (bf16[512,384]{1,0:T(8,128)(2,1)S(1)}, bf16[512,384]{1,0:T(8,128)(2,1)S(1)}, u32[]{:S(2)}, u32[]{:S(2)}) collective-permute-start(bf16[512,384]{1,0:T(8,128)(2,1)S(1)} %constant_dynamic-update-slice_fusion.refs_5_.refs_3_), channel_id=1, source_target_pairs={{0,8},{1,9},{2,10},{3,11},{4,12},{5,13},{6,14},{7,15},{8,0},{9,1},... | collective-permute-start | bytes 1179656 | tf_op jit(solution)/shard_map/ppermute | solution.py:57
  35.5 2.9 %collective-permute-done.11 = bf16[128,1024]{1,0:T(8,128)(2,1)S(1)} collective-permute-done((bf16[128,1024]{1,0:T(8,128)(2,1)S(1)}, bf16[128,1024]{1,0:T(8,128)(2,1)S(1)}, u32[]{:S(2)}, u32[]{:S(2)}) %collective-permute-start.11) | collective-permute-done | bytes 262176 | tf_op jit(solution)/shard_map/ppermute | solution.py:57
  45.9 1.8 %collective-permute-start.17 = (bf16[4,256,128]{2,1,0:T(8,128)(2,1)S(1)}, bf16[4,256,128]{2,1,0:T(8,128)(2,1)S(1)}, u32[]{:S(2)}, u32[]{:S(2)}) collective-permute-start(bf16[4,256,128]{2,1,0:T(8,128)(2,1)S(1)} %get-tuple-element.68.own), channel_id=1, source_target_pairs={{0,8},{1,9},{2,10},{3,11},{4,12},{5,13},{6,14},{7,15},{8,0},{9,1},... | collective-permute-start | bytes 786440 | tf_op jit(solution)/shard_map/ppermute | solution.py:57
  47.7 1.9 %collective-permute-start.18 = (bf16[4,256,128]{2,1,0:T(8,128)(2,1)S(1)}, bf16[4,256,128]{2,1,0:T(8,128)(2,1)S(1)}, u32[]{:S(2)}, u32[]{:S(2)}) collective-permute-start(bf16[4,256,128]{2,1,0:T(8,128)(2,1)S(1)} %get-tuple-element.68.own), channel_id=1, source_target_pairs={{8,16},{9,17},{10,18},{11,19},{12,20},{13,21},{14,22},{15,23},{16,... | collective-permute-start | bytes 786440 | tf_op jit(solution)/shard_map/ppermute | solution.py:57
  49.7 3.9 %collective-permute-start.23 = (bf16[2,256,128]{2,1,0:T(8,128)(2,1)S(1)}, bf16[2,256,128]{2,1,0:T(8,128)(2,1)S(1)}, u32[]{:S(2)}, u32[]{:S(2)}) collective-permute-start(bf16[2,256,128]{2,1,0:T(8,128)(2,1)S(1)} %get-tuple-element.72.own), channel_id=1, source_target_pairs={{8,16},{9,17},{10,18},{11,19},{12,20},{13,21},{14,22},{15,23},{16,... | collective-permute-start | bytes 393224 | tf_op jit(solution)/shard_map/ppermute | solution.py:57
  55.1 1.9 %collective-permute-start.20 = (bf16[2,256,128]{2,1,0:T(8,128)(2,1)S(1)}, bf16[2,256,128]{2,1,0:T(8,128)(2,1)S(1)}, u32[]{:S(2)}, u32[]{:S(2)}) collective-permute-start(bf16[2,256,128]{2,1,0:T(8,128)(2,1)S(1)} %get-tuple-element.69.own), channel_id=1, source_target_pairs={{8,16},{9,17},{10,18},{11,19},{12,20},{13,21},{14,22},{15,23},{16,... | collective-permute-start | bytes 393224 | tf_op jit(solution)/shard_map/ppermute | solution.py:57
  57.0 1.8 %collective-permute-done.18.middle = bf16[4,256,128]{2,1,0:T(8,128)(2,1)S(1)} collective-permute-done((bf16[4,256,128]{2,1,0:T(8,128)(2,1)S(1)}, bf16[4,256,128]{2,1,0:T(8,128)(2,1)S(1)}, u32[]{:S(2)}, u32[]{:S(2)}) %collective-permute-start.18) | collective-permute-done | bytes 262176 | tf_op jit(solution)/shard_map/ppermute | solution.py:57
  60.0 1.6 %collective-permute-done.23.middle = bf16[2,256,128]{2,1,0:T(8,128)(2,1)S(1)} collective-permute-done((bf16[2,256,128]{2,1,0:T(8,128)(2,1)S(1)}, bf16[2,256,128]{2,1,0:T(8,128)(2,1)S(1)}, u32[]{:S(2)}, u32[]{:S(2)}) %collective-permute-start.23) | collective-permute-done | bytes 131104 | tf_op jit(solution)/shard_map/ppermute | solution.py:57
  63.5 1.6 %collective-permute-start.26 = (bf16[128,128]{1,0:T(8,128)(2,1)S(1)}, bf16[128,128]{1,0:T(8,128)(2,1)S(1)}, u32[]{:S(2)}, u32[]{:S(2)}) collective-permute-start(bf16[128,128]{1,0:T(8,128)(2,1)S(1)} %get-tuple-element.75), channel_id=1, source_target_pairs={{0,2},{1,3},{2,0},{3,1},{4,6},{5,7},{6,4},{7,5},{8,10},{9,11},{10,... | collective-permute-start | bytes 98312 | tf_op jit(solution)/shard_map/ppermute | solution.py:57
  65.1 1.5 %collective-permute-start.27 = (bf16[128,128]{1,0:T(8,128)(2,1)S(1)}, bf16[128,128]{1,0:T(8,128)(2,1)S(1)}, u32[]{:S(2)}, u32[]{:S(2)}) collective-permute-start(bf16[128,128]{1,0:T(8,128)(2,1)S(1)} %get-tuple-element.76), channel_id=1, source_target_pairs={{0,6},{1,7},{2,4},{3,5},{4,2},{5,3},{6,0},{7,1},{8,14},{9,15},{10,... | collective-permute-start | bytes 98312 | tf_op jit(solution)/shard_map/ppermute | solution.py:57
  66.9 1.4 %collective-permute-start.24 = (bf16[128,128]{1,0:T(8,128)(2,1)S(1)}, bf16[128,128]{1,0:T(8,128)(2,1)S(1)}, u32[]{:S(2)}, u32[]{:S(2)}) collective-permute-start(bf16[128,128]{1,0:T(8,128)(2,1)S(1)} %get-tuple-element.73), channel_id=1, source_target_pairs={{0,1},{1,0},{2,3},{3,2},{4,5},{5,4},{6,7},{7,6},{8,9},{9,8},{10,11... | collective-permute-start | bytes 98312 | tf_op jit(solution)/shard_map/ppermute | solution.py:57
  69.5 1.4 %collective-permute-done.24.refs_2_ = bf16[128,128]{1,0:T(8,128)(2,1)S(1)} collective-permute-done((bf16[128,128]{1,0:T(8,128)(2,1)S(1)}, bf16[128,128]{1,0:T(8,128)(2,1)S(1)}, u32[]{:S(2)}, u32[]{:S(2)}) %collective-permute-start.24) | collective-permute-done | bytes 32800 | tf_op jit(solution)/shard_map/ppermute | solution.py:57
  (79 shorter events, 25.3 us)
Async XLA Ops:
  0.0 19.0 %collective-permute-start = (bf16[256,768]{1,0:T(8,128)(2,1)}, bf16[256,768]{1,0:T(8,128)(2,1)S(1)}, u32[]{:S(2)}, u32[]{:S(2)}) collective-permute-start(bf16[256,768]{1,0:T(8,128)(2,1)} %w.1), channel_id=1, source_target_pairs={{0,16},{1,17},{2,18},{3,19},{4,20},{5,21},{6,22},{7,23},{8,24},{9,... | collective-permute-start | bytes 1179656 | tf_op jit(solution)/shard_map/ppermute | solution.py:57
  3.0 5.8 %collective-permute-start.3 = (bf16[128,256]{1,0:T(8,128)(2,1)S(1)}, bf16[128,256]{1,0:T(8,128)(2,1)S(1)}, u32[]{:S(2)}, u32[]{:S(2)}) collective-permute-start(bf16[128,256]{1,0:T(8,128)(2,1)S(1)} %get-tuple-element.44), channel_id=1, source_target_pairs={{0,3},{1,2},{2,1},{3,0},{4,7},{5,6},{6,5},{7,4},{8,11},{9,10},{10,... | collective-permute-start | bytes 196616 | tf_op jit(solution)/shard_map/ppermute | solution.py:57
  5.9 7.0 %collective-permute-start.1 = (bf16[336,256]{1,0:T(8,128)(2,1)S(1)}, bf16[336,256]{1,0:T(8,128)(2,1)S(1)}, u32[]{:S(2)}, u32[]{:S(2)}) collective-permute-start(bf16[336,256]{1,0:T(8,128)(2,1)S(1)} %get-tuple-element.42), channel_id=1, source_target_pairs={{0,1},{1,0},{2,3},{3,2},{4,5},{5,4},{6,7},{7,6},{8,9},{9,8},{10,11... | collective-permute-start | bytes 516104 | tf_op jit(solution)/shard_map/ppermute | solution.py:57
  6.4 7.3 %collective-permute-start.2 = (bf16[336,256]{1,0:T(8,128)(2,1)S(1)}, bf16[336,256]{1,0:T(8,128)(2,1)S(1)}, u32[]{:S(2)}, u32[]{:S(2)}) collective-permute-start(bf16[336,256]{1,0:T(8,128)(2,1)S(1)} %get-tuple-element.43), channel_id=1, source_target_pairs={{0,2},{1,3},{2,0},{3,1},{4,6},{5,7},{6,4},{7,5},{8,10},{9,11},{10,... | collective-permute-start | bytes 516104 | tf_op jit(solution)/shard_map/ppermute | solution.py:57
  8.8 15.9 %collective-permute-start.7 = (bf16[128,2048]{1,0:T(8,128)(2,1)}, bf16[128,2048]{1,0:T(8,128)(2,1)S(1)}, u32[]{:S(2)}, u32[]{:S(2)}) collective-permute-start(bf16[128,2048]{1,0:T(8,128)(2,1)} %bitcast.13), channel_id=1, source_target_pairs={{0,2},{1,3},{2,0},{3,1},{4,6},{5,7},{6,4},{7,5},{8,10},{9,11},{10,... | collective-permute-start | bytes 1572872 | tf_op jit(solution)/shard_map/ppermute | solution.py:57
  10.8 14.0 %collective-permute-start.6 = (bf16[128,2048]{1,0:T(8,128)(2,1)}, bf16[128,2048]{1,0:T(8,128)(2,1)S(1)}, u32[]{:S(2)}, u32[]{:S(2)}) collective-permute-start(bf16[128,2048]{1,0:T(8,128)(2,1)} %bitcast.14), channel_id=1, source_target_pairs={{0,1},{1,0},{2,3},{3,2},{4,5},{5,4},{6,7},{7,6},{8,9},{9,8},{10,11... | collective-permute-start | bytes 1572872 | tf_op jit(solution)/shard_map/ppermute | solution.py:57
  13.8 14.0 %collective-permute-start.8 = (bf16[256,768]{1,0:T(8,128)(2,1)S(1)}, bf16[256,768]{1,0:T(8,128)(2,1)S(1)}, u32[]{:S(2)}, u32[]{:S(2)}) collective-permute-start(bf16[256,768]{1,0:T(8,128)(2,1)S(1)} %shard_map.67.refs_2_.refs_0_), channel_id=1, source_target_pairs={{0,8},{1,9},{2,10},{3,11},{4,12},{5,13},{6,14},{7,15},{8,0},{9,1},... | collective-permute-start | bytes 1179656 | tf_op jit(solution)/shard_map/ppermute | solution.py:57
  19.0 7.2 %collective-permute-start.4 = (bf16[256,256]{1,0:T(8,128)(2,1)S(1)}, bf16[256,256]{1,0:T(8,128)(2,1)S(1)}, u32[]{:S(2)}, u32[]{:S(2)}) collective-permute-start(bf16[256,256]{1,0:T(8,128)(2,1)S(1)} %get-tuple-element.82), channel_id=1, source_target_pairs={{0,1},{1,0},{2,3},{3,2},{4,5},{5,4},{6,7},{7,6},{8,9},{9,8},{10,11... | collective-permute-start | bytes 393224 | tf_op jit(solution)/shard_map/ppermute | solution.py:57
  20.6 5.6 %collective-permute-start.5 = (bf16[256,256]{1,0:T(8,128)(2,1)S(1)}, bf16[256,256]{1,0:T(8,128)(2,1)S(1)}, u32[]{:S(2)}, u32[]{:S(2)}) collective-permute-start(bf16[256,256]{1,0:T(8,128)(2,1)S(1)} %get-tuple-element.81), channel_id=1, source_target_pairs={{0,2},{1,3},{2,0},{3,1},{4,6},{5,7},{6,4},{7,5},{8,10},{9,11},{10,... | collective-permute-start | bytes 393224 | tf_op jit(solution)/shard_map/ppermute | solution.py:57
  29.5 10.2 %collective-permute-start.10 = (bf16[384,2048]{1,0:T(8,128)(2,1)S(1)}, bf16[384,2048]{1,0:T(8,128)(2,1)S(1)}, u32[]{:S(2)}, u32[]{:S(2)}) collective-permute-start(bf16[384,2048]{1,0:T(8,128)(2,1)S(1)} %get-tuple-element.58.refs_0_), channel_id=1, source_target_pairs={{0,4},{1,5},{2,6},{3,7},{4,0},{5,1},{6,2},{7,3},{8,12},{9,13},{10,... | collective-permute-start | bytes 4718600 | tf_op jit(solution)/shard_map/ppermute | solution.py:57
  29.7 8.6 %collective-permute-start.11 = (bf16[128,1024]{1,0:T(8,128)(2,1)S(1)}, bf16[128,1024]{1,0:T(8,128)(2,1)S(1)}, u32[]{:S(2)}, u32[]{:S(2)}) collective-permute-start(bf16[128,1024]{1,0:T(8,128)(2,1)S(1)} %get-tuple-element.59), channel_id=1, source_target_pairs={{0,2},{1,3},{2,0},{3,1},{4,6},{5,7},{6,4},{7,5},{8,10},{9,11},{10,... | collective-permute-start | bytes 786440 | tf_op jit(solution)/shard_map/ppermute | solution.py:57
  31.3 8.3 %collective-permute-start.12 = (bf16[128,1024]{1,0:T(8,128)(2,1)S(1)}, bf16[128,1024]{1,0:T(8,128)(2,1)S(1)}, u32[]{:S(2)}, u32[]{:S(2)}) collective-permute-start(bf16[128,1024]{1,0:T(8,128)(2,1)S(1)} %get-tuple-element.60), channel_id=1, source_target_pairs={{0,1},{1,0},{2,3},{3,2},{4,5},{5,4},{6,7},{7,6},{8,9},{9,8},{10,11... | collective-permute-start | bytes 786440 | tf_op jit(solution)/shard_map/ppermute | solution.py:57
  32.9 6.8 %collective-permute-start.13 = (bf16[528,384]{1,0:T(8,128)(2,1)S(1)}, bf16[528,384]{1,0:T(8,128)(2,1)S(1)}, u32[]{:S(2)}, u32[]{:S(2)}) collective-permute-start(bf16[528,384]{1,0:T(8,128)(2,1)S(1)} %pad_maximum_fusion.1), channel_id=1, source_target_pairs={{0,4},{1,5},{2,6},{3,7},{4,0},{5,1},{6,2},{7,3},{8,12},{9,13},{10,... | collective-permute-start | bytes 1216520 | tf_op jit(solution)/shard_map/ppermute | solution.py:57
  32.9 12.3 %collective-permute-start.16 = (bf16[512,384]{1,0:T(8,128)(2,1)S(1)}, bf16[512,384]{1,0:T(8,128)(2,1)S(1)}, u32[]{:S(2)}, u32[]{:S(2)}) collective-permute-start(bf16[512,384]{1,0:T(8,128)(2,1)S(1)} %constant_dynamic-update-slice_fusion.refs_5_.refs_3_), channel_id=1, source_target_pairs={{0,8},{1,9},{2,10},{3,11},{4,12},{5,13},{6,14},{7,15},{8,0},{9,1},... | collective-permute-start | bytes 1179656 | tf_op jit(solution)/shard_map/ppermute | solution.py:57
  45.9 9.2 %collective-permute-start.17 = (bf16[4,256,128]{2,1,0:T(8,128)(2,1)S(1)}, bf16[4,256,128]{2,1,0:T(8,128)(2,1)S(1)}, u32[]{:S(2)}, u32[]{:S(2)}) collective-permute-start(bf16[4,256,128]{2,1,0:T(8,128)(2,1)S(1)} %get-tuple-element.68.own), channel_id=1, source_target_pairs={{0,8},{1,9},{2,10},{3,11},{4,12},{5,13},{6,14},{7,15},{8,0},{9,1},... | collective-permute-start | bytes 786440 | tf_op jit(solution)/shard_map/ppermute | solution.py:57
  47.7 11.1 %collective-permute-start.18 = (bf16[4,256,128]{2,1,0:T(8,128)(2,1)S(1)}, bf16[4,256,128]{2,1,0:T(8,128)(2,1)S(1)}, u32[]{:S(2)}, u32[]{:S(2)}) collective-permute-start(bf16[4,256,128]{2,1,0:T(8,128)(2,1)S(1)} %get-tuple-element.68.own), channel_id=1, source_target_pairs={{8,16},{9,17},{10,18},{11,19},{12,20},{13,21},{14,22},{15,23},{16,... | collective-permute-start | bytes 786440 | tf_op jit(solution)/shard_map/ppermute | solution.py:57
  49.6 10.4 %collective-permute-start.22 = (bf16[2,256,128]{2,1,0:T(8,128)(2,1)S(1)}, bf16[2,256,128]{2,1,0:T(8,128)(2,1)S(1)}, u32[]{:S(2)}, u32[]{:S(2)}) collective-permute-start(bf16[2,256,128]{2,1,0:T(8,128)(2,1)S(1)} %get-tuple-element.72.own), channel_id=1, source_target_pairs={{0,8},{1,9},{2,10},{3,11},{4,12},{5,13},{6,14},{7,15},{8,0},{9,1},... | collective-permute-start | bytes 393224 | tf_op jit(solution)/shard_map/ppermute | solution.py:57
  49.7 11.9 %collective-permute-start.23 = (bf16[2,256,128]{2,1,0:T(8,128)(2,1)S(1)}, bf16[2,256,128]{2,1,0:T(8,128)(2,1)S(1)}, u32[]{:S(2)}, u32[]{:S(2)}) collective-permute-start(bf16[2,256,128]{2,1,0:T(8,128)(2,1)S(1)} %get-tuple-element.72.own), channel_id=1, source_target_pairs={{8,16},{9,17},{10,18},{11,19},{12,20},{13,21},{14,22},{15,23},{16,... | collective-permute-start | bytes 393224 | tf_op jit(solution)/shard_map/ppermute | solution.py:57
  53.7 9.6 %collective-permute-start.19 = (bf16[2,256,128]{2,1,0:T(8,128)(2,1)S(1)}, bf16[2,256,128]{2,1,0:T(8,128)(2,1)S(1)}, u32[]{:S(2)}, u32[]{:S(2)}) collective-permute-start(bf16[2,256,128]{2,1,0:T(8,128)(2,1)S(1)} %get-tuple-element.69.own), channel_id=1, source_target_pairs={{0,8},{1,9},{2,10},{3,11},{4,12},{5,13},{6,14},{7,15},{8,0},{9,1},... | collective-permute-start | bytes 393224 | tf_op jit(solution)/shard_map/ppermute | solution.py:57
  55.1 8.1 %collective-permute-start.20 = (bf16[2,256,128]{2,1,0:T(8,128)(2,1)S(1)}, bf16[2,256,128]{2,1,0:T(8,128)(2,1)S(1)}, u32[]{:S(2)}, u32[]{:S(2)}) collective-permute-start(bf16[2,256,128]{2,1,0:T(8,128)(2,1)S(1)} %get-tuple-element.69.own), channel_id=1, source_target_pairs={{8,16},{9,17},{10,18},{11,19},{12,20},{13,21},{14,22},{15,23},{16,... | collective-permute-start | bytes 393224 | tf_op jit(solution)/shard_map/ppermute | solution.py:57
  61.9 6.7 %collective-permute-start.28 = (bf16[128,128]{1,0:T(8,128)(2,1)S(1)}, bf16[128,128]{1,0:T(8,128)(2,1)S(1)}, u32[]{:S(2)}, u32[]{:S(2)}) collective-permute-start(bf16[128,128]{1,0:T(8,128)(2,1)S(1)} %get-tuple-element.77), channel_id=1, source_target_pairs={{0,3},{1,2},{2,1},{3,0},{4,7},{5,6},{6,5},{7,4},{8,11},{9,10},{10,... | collective-permute-start | bytes 98312 | tf_op jit(solution)/shard_map/ppermute | solution.py:57
  63.3 5.4 %collective-permute-start.29 = (bf16[128,128]{1,0:T(8,128)(2,1)S(1)}, bf16[128,128]{1,0:T(8,128)(2,1)S(1)}, u32[]{:S(2)}, u32[]{:S(2)}) collective-permute-start(bf16[128,128]{1,0:T(8,128)(2,1)S(1)} %get-tuple-element.78), channel_id=1, source_target_pairs={{0,7},{1,6},{2,5},{3,4},{4,3},{5,2},{6,1},{7,0},{8,15},{9,14},{10,... | collective-permute-start | bytes 98312 | tf_op jit(solution)/shard_map/ppermute | solution.py:57
  63.5 5.9 %collective-permute-start.26 = (bf16[128,128]{1,0:T(8,128)(2,1)S(1)}, bf16[128,128]{1,0:T(8,128)(2,1)S(1)}, u32[]{:S(2)}, u32[]{:S(2)}) collective-permute-start(bf16[128,128]{1,0:T(8,128)(2,1)S(1)} %get-tuple-element.75), channel_id=1, source_target_pairs={{0,2},{1,3},{2,0},{3,1},{4,6},{5,7},{6,4},{7,5},{8,10},{9,11},{10,... | collective-permute-start | bytes 98312 | tf_op jit(solution)/shard_map/ppermute | solution.py:57
  65.1 4.3 %collective-permute-start.27 = (bf16[128,128]{1,0:T(8,128)(2,1)S(1)}, bf16[128,128]{1,0:T(8,128)(2,1)S(1)}, u32[]{:S(2)}, u32[]{:S(2)}) collective-permute-start(bf16[128,128]{1,0:T(8,128)(2,1)S(1)} %get-tuple-element.76), channel_id=1, source_target_pairs={{0,6},{1,7},{2,4},{3,5},{4,2},{5,3},{6,0},{7,1},{8,14},{9,15},{10,... | collective-permute-start | bytes 98312 | tf_op jit(solution)/shard_map/ppermute | solution.py:57
  (16 other events, 43.3 us)

commit v11 on v10

--- a/solution.py
+++ b/solution.py
@@ -261,27 +261,31 @@
                 out_ref[r, u * block : (u + 1) * block, here] = (p * inverse).astype(jnp.bfloat16)
 
 
-def mix_kernel(r, weights, outer, own, middle, keep_ref, send_ref):
-    _, core, _ = where_am_i()
+def mix_kernel(r, weights, outer, own, middle, out_ref):
     block = weights.shape[1] // 2
     values = neighbours(outer, own, middle, V_ORDER.index(r) % 2)
-    results = []
     for u in range(2):
         w = weights[r, u * block : (u + 1) * block]
         v = [values[side][first * block : last * block] for side, first, last in spans(u)]
         result = jnp.dot(w, jnp.concatenate(v, axis=0), preferred_element_type=jnp.float32)
-        results.append(result.astype(jnp.bfloat16))
-    keep_ref[...] = jnp.where(core == 0, results[0], results[1])
-    send_ref[...] = jnp.where(core == 0, results[1], results[0])
-
-
-def gather_kernel(*refs):
-    out_ref = refs[-1]
+        out_ref[u * block : (u + 1) * block] = result.astype(jnp.bfloat16)
+
+
+def pack_kernel(*refs):
+    keep_ref, send_ref = refs[4:]
+    _, core, _ = where_am_i()
+    block = keep_ref.shape[1]
+    for r, ref in enumerate(refs[:4]):
+        for rel, out_ref in enumerate((keep_ref, send_ref)):
+            out_ref[r] = ref[pl.ds(pl.multiple_of((core ^ rel) * block, block), block), :]
+
+
+def gather_kernel(mine, other, out_ref):
     _, core, depth = where_am_i()
-    for i, ref in enumerate(refs[:-1]):
-        r, rel = i >> 1, i & 1
-        at = pl.multiple_of((2 * (depth ^ r) + (core ^ rel)) * HD, HD)
-        out_ref[:, pl.ds(at, HD)] = ref[...]
+    for rel, ref in enumerate((mine, other)):
+        for r in range(4):
+            at = pl.multiple_of((2 * (depth ^ r) + (core ^ rel)) * HD, HD)
+            out_ref[:, pl.ds(at, HD)] = ref[r]
 
 
 def call(kernel, outs, places, scratch=(), macs=0, limit=32):
@@ -353,13 +357,13 @@
     far, near, stack = lax.optimization_barrier((far, near, stack))
     received = swap_core(jnp.concatenate([own[:, 3 * HD :], near[:, 3 * HD :], flags], axis=0))
     weights = (own, near, received, far)
-    piece = block // 2
+    piece = 5 * block // 8
     early = (stack, swap_core(stack))
     rows = 2 * size
     total = call(partial_kernel, array(6 * block, 3 * HD, kind=f32), "v" * 6, macs=6 * block * 3 * rows * 3 * HD)(
         *early, *weights
     )
-    (diagonal,) = embed((3,), after(jnp.concatenate(diagonal, axis=1), total))
+    (diagonal,) = embed((3,), jnp.concatenate([after(t, total) for t in diagonal], axis=1))
     swapped = [swap_core(diagonal[:piece]), swap_core(diagonal[piece:])]
     total_diagonal, diagonal = call(
         diagonal_kernel,
@@ -378,13 +382,12 @@
     values = [(swap_z(t, 1), t, swap_middle(t)) for t in v]
     pieces = {}
     for r in V_ORDER:
-        kept, sent = call(
-            functools.partial(mix_kernel, r), (array(block, HD),) * 2, "vvvv", macs=2 * block * 5 * block * HD
-        )(weights, *values[V_ORDER.index(r) // 2])
-        sent = hop(sent, lambda z, c, d, r=r: (z, 1 - c, d ^ r))
-        pieces[r] = (swap_depth(kept, r) if r else kept, sent)
-    both = [t for r in range(4) for t in pieces[r]]
-    context = call(gather_kernel, array(block, HEADS * HD), "v" * 8)(*both)
+        mixed = call(functools.partial(mix_kernel, r), array(2 * block, HD), "vvvv", macs=2 * block * 5 * block * HD)(
+            weights, *values[V_ORDER.index(r) // 2]
+        )
+        pieces[r] = swap_depth(mixed, r) if r else mixed
+    kept, sent = call(pack_kernel, (array(4, block, HD),) * 2, "vvvv")(*[pieces[r] for r in range(4)])
+    context = call(gather_kernel, array(block, HEADS * HD), "vv")(kept, swap_core(sent))
     return context.reshape(time_len, site_len, HEADS * HD)
 
 

time: 73.2 us -> 71.4 us (0.975)
  the two profiles are of different devices: /device:TPU:16 before, /device:TPU:9 now
where the time goes in v11:
time: 71.4 us; the launch traced here: 70.5 us
  starting transfers between devices  35.2 us (49%)
  waiting for transfers between devices  20.7 us (29%)
  Pallas kernels  8.83 us (12%)
  local copies, waits for them, and re-layouts  5.41 us (8%)
    ppermute x27, starting transfers between devices, hop(): return lax.ppermute(value, ('tm', 'depth'), pairs)  35.2 us
    ppermute x27, waiting for transfers between devices, hop(): return lax.ppermute(value, ('tm', 'depth'), pairs)  20.7 us
    unnamed x21, local copies, waits for them, and re-layouts  5.3 us
    pallas_call x3, Pallas kernels, embed(): call(functools.partial(embed_kernel, rs, len(finished)), out, 'v' * (6 +...  2.35 us
  transfers between devices with their start and end apart: 27, of which 16 were waited for; matrix products, arithmetic and copies ran while one was open for 0% of the time, Pallas kernels for 10%

profile of v11, /device:TPU:9, one launch (start us, length us, event | category | flops | bytes accessed | tf_op | source)
XLA Modules:
  0.0 70.5 jit_solution(3227083403301890490)
XLA Ops:
  0.0 2.3 %collective-permute-start = (bf16[256,768]{1,0:T(8,128)(2,1)}, bf16[256,768]{1,0:T(8,128)(2,1)S(1)}, u32[]{:S(2)}, u32[]{:S(2)}) collective-permute-start(bf16[256,768]{1,0:T(8,128)(2,1)} %w.1), channel_id=1, source_target_pairs={{0,16},{1,17},{2,18},{3,19},{4,20},{5,21},{6,22},{7,23},{8,24},{9,... | collective-permute-start | bytes 1179656 | tf_op jit(solution)/shard_map/ppermute | solution.py:57
  5.3 2.2 %collective-permute-start.3 = (bf16[128,256]{1,0:T(8,128)(2,1)S(1)}, bf16[128,256]{1,0:T(8,128)(2,1)S(1)}, u32[]{:S(2)}, u32[]{:S(2)}) collective-permute-start(bf16[128,256]{1,0:T(8,128)(2,1)S(1)} %get-tuple-element.39), channel_id=1, source_target_pairs={{0,3},{1,2},{2,1},{3,0},{4,7},{5,6},{6,5},{7,4},{8,11},{9,10},{10,... | collective-permute-start | bytes 196616 | tf_op jit(solution)/shard_map/ppermute | solution.py:57
  8.0 1.7 %collective-permute-done.3.across = bf16[128,256]{1,0:T(8,128)(2,1)S(1)} collective-permute-done((bf16[128,256]{1,0:T(8,128)(2,1)S(1)}, bf16[128,256]{1,0:T(8,128)(2,1)S(1)}, u32[]{:S(2)}, u32[]{:S(2)}) %collective-permute-start.3) | collective-permute-done | bytes 65568 | tf_op jit(solution)/shard_map/ppermute | solution.py:57
  9.7 1.2 %collective-permute-start.7 = (bf16[128,2048]{1,0:T(8,128)(2,1)}, bf16[128,2048]{1,0:T(8,128)(2,1)S(1)}, u32[]{:S(2)}, u32[]{:S(2)}) collective-permute-start(bf16[128,2048]{1,0:T(8,128)(2,1)} %bitcast.13), channel_id=1, source_target_pairs={{0,2},{1,3},{2,0},{3,1},{4,6},{5,7},{6,4},{7,5},{8,10},{9,11},{10,... | collective-permute-start | bytes 1572872 | tf_op jit(solution)/shard_map/ppermute | solution.py:57
  12.1 1.4 %collective-permute-done.1.plane_x.from_x = bf16[336,256]{1,0:T(8,128)(2,1)S(1)} collective-permute-done((bf16[336,256]{1,0:T(8,128)(2,1)S(1)}, bf16[336,256]{1,0:T(8,128)(2,1)S(1)}, u32[]{:S(2)}, u32[]{:S(2)}) %collective-permute-start.1) | collective-permute-done | bytes 172064 | tf_op jit(solution)/shard_map/ppermute | solution.py:57
  13.9 1.4 %copy-done = bf16[3,128,2048]{2,1,0:T(8,128)(2,1)S(1)} copy-done((bf16[3,128,2048]{2,1,0:T(8,128)(2,1)S(1)}, bf16[3,128,2048]{2,1,0:T(8,128)(2,1)}, u32[]{:S(2)}) %copy-start) | copy-done | bytes 1572888
  17.4 2.4 %collective-permute-done = bf16[256,768]{1,0:T(8,128)(2,1)S(1)} collective-permute-done((bf16[256,768]{1,0:T(8,128)(2,1)}, bf16[256,768]{1,0:T(8,128)(2,1)S(1)}, u32[]{:S(2)}, u32[]{:S(2)}) %collective-permute-start) | collective-permute-done | bytes 393248 | tf_op jit(solution)/shard_map/ppermute | solution.py:57
  19.9 1.3 %collective-permute-start.4 = (bf16[256,256]{1,0:T(8,128)(2,1)S(1)}, bf16[256,256]{1,0:T(8,128)(2,1)S(1)}, u32[]{:S(2)}, u32[]{:S(2)}) collective-permute-start(bf16[256,256]{1,0:T(8,128)(2,1)S(1)} %get-tuple-element.70), channel_id=1, source_target_pairs={{0,1},{1,0},{2,3},{3,2},{4,5},{5,4},{6,7},{7,6},{8,9},{9,8},{10,11... | collective-permute-start | bytes 393224 | tf_op jit(solution)/shard_map/ppermute | solution.py:57
  21.1 1.2 %collective-permute-start.5 = (bf16[256,256]{1,0:T(8,128)(2,1)S(1)}, bf16[256,256]{1,0:T(8,128)(2,1)S(1)}, u32[]{:S(2)}, u32[]{:S(2)}) collective-permute-start(bf16[256,256]{1,0:T(8,128)(2,1)S(1)} %get-tuple-element.69), channel_id=1, source_target_pairs={{0,2},{1,3},{2,0},{3,1},{4,6},{5,7},{6,4},{7,5},{8,10},{9,11},{10,... | collective-permute-start | bytes 393224 | tf_op jit(solution)/shard_map/ppermute | solution.py:57
  22.4 2.3 %collective-permute-done.7.refs_1_ = bf16[128,2048]{1,0:T(8,128)(2,1)S(1)} collective-permute-done((bf16[128,2048]{1,0:T(8,128)(2,1)}, bf16[128,2048]{1,0:T(8,128)(2,1)S(1)}, u32[]{:S(2)}, u32[]{:S(2)}) %collective-permute-start.7) | collective-permute-done | bytes 524320 | tf_op jit(solution)/shard_map/ppermute | solution.py:57
  26.2 1.3 %collective-permute-done.5.from_y = bf16[256,256]{1,0:T(8,128)(2,1)S(1)} collective-permute-done((bf16[256,256]{1,0:T(8,128)(2,1)S(1)}, bf16[256,256]{1,0:T(8,128)(2,1)S(1)}, u32[]{:S(2)}, u32[]{:S(2)}) %collective-permute-start.5) | collective-permute-done | bytes 131104 | tf_op jit(solution)/shard_map/ppermute | solution.py:57
  27.6 1.9 %collective-permute-start.9 = (bf16[256,384]{1,0:T(8,128)(2,1)S(1)}, bf16[256,384]{1,0:T(8,128)(2,1)S(1)}, u32[]{:S(2)}, u32[]{:S(2)}) collective-permute-start(bf16[256,384]{1,0:T(8,128)(2,1)S(1)} %get-tuple-element.50), channel_id=1, source_target_pairs={{0,4},{1,5},{2,6},{3,7},{4,0},{5,1},{6,2},{7,3},{8,12},{9,13},{10,... | collective-permute-start | bytes 589832 | tf_op jit(solution)/shard_map/ppermute | solution.py:57
  34.6 1.4 %shard_map.69.refs_4_ = f32[768,384]{1,0:T(8,128)S(1)} custom-call(bf16[384,2048]{1,0:T(8,128)(2,1)S(1)} %get-tuple-element.53.refs_0_, bf16[384,2048]{1,0:T(8,128)(2,1)S(1)} %collective-permute-done.10.refs_1_, bf16[256,768]{1,0:T(8,128)(2,1)S(1)} %shard_map.67.refs_2_.refs_0_, bf16[256,768]{1,0:T(8,128)(2,1)S(1)} %collective-permute-done.8.refs_3_.refs_1_, ...), custom_call_target="tpu_custom_call" | custom-call | flops 905969664 | tf_op jit(solution)/shard_map/pallas_call | solution.py:363
  36.0 2.8 %collective-permute-done.11 = bf16[128,1024]{1,0:T(8,128)(2,1)S(1)} collective-permute-done((bf16[128,1024]{1,0:T(8,128)(2,1)S(1)}, bf16[128,1024]{1,0:T(8,128)(2,1)S(1)}, u32[]{:S(2)}, u32[]{:S(2)}) %collective-permute-start.11) | collective-permute-done | bytes 262176 | tf_op jit(solution)/shard_map/ppermute | solution.py:57
  39.7 1.6 %collective-permute-start.14 = (bf16[80,2048]{1,0:T(8,128)(2,1)S(1)}, bf16[80,2048]{1,0:T(8,128)(2,1)S(1)}, u32[]{:S(2)}, u32[]{:S(2)}) collective-permute-start(bf16[80,2048]{1,0:T(8,128)(2,1)S(1)} %slice.29), channel_id=1, source_target_pairs={{0,4},{1,5},{2,6},{3,7},{4,0},{5,1},{6,2},{7,3},{8,12},{9,13},{10,... | collective-permute-start | bytes 983048 | tf_op jit(solution)/shard_map/ppermute | solution.py:57
  41.4 1.4 %collective-permute-done.15.bottom = bf16[48,2048]{1,0:T(8,128)(2,1)S(1)} collective-permute-done((bf16[48,2048]{1,0:T(8,128)(2,1)S(1)}, bf16[48,2048]{1,0:T(8,128)(2,1)S(1)}, u32[]{:S(2)}, u32[]{:S(2)}) %collective-permute-start.15) | collective-permute-done | bytes 196640 | tf_op jit(solution)/shard_map/ppermute | solution.py:57
  45.4 4.2 %collective-permute-start.18 = (bf16[4,256,128]{2,1,0:T(8,128)(2,1)S(1)}, bf16[4,256,128]{2,1,0:T(8,128)(2,1)S(1)}, u32[]{:S(2)}, u32[]{:S(2)}) collective-permute-start(bf16[4,256,128]{2,1,0:T(8,128)(2,1)S(1)} %get-tuple-element.64.own), channel_id=1, source_target_pairs={{8,16},{9,17},{10,18},{11,19},{12,20},{13,21},{14,22},{15,23},{16,... | collective-permute-start | bytes 786440 | tf_op jit(solution)/shard_map/ppermute | solution.py:57
  49.7 1.9 %collective-permute-start.22 = (bf16[2,256,128]{2,1,0:T(8,128)(2,1)S(1)}, bf16[2,256,128]{2,1,0:T(8,128)(2,1)S(1)}, u32[]{:S(2)}, u32[]{:S(2)}) collective-permute-start(bf16[2,256,128]{2,1,0:T(8,128)(2,1)S(1)} %get-tuple-element.66.own), channel_id=1, source_target_pairs={{8,16},{9,17},{10,18},{11,19},{12,20},{13,21},{14,22},{15,23},{16,... | collective-permute-start | bytes 393224 | tf_op jit(solution)/shard_map/ppermute | solution.py:57
  51.9 3.2 %collective-permute-start.20 = (bf16[2,256,128]{2,1,0:T(8,128)(2,1)S(1)}, bf16[2,256,128]{2,1,0:T(8,128)(2,1)S(1)}, u32[]{:S(2)}, u32[]{:S(2)}) collective-permute-start(bf16[2,256,128]{2,1,0:T(8,128)(2,1)S(1)} %get-tuple-element.65.own), channel_id=1, source_target_pairs={{8,16},{9,17},{10,18},{11,19},{12,20},{13,21},{14,22},{15,23},{16,... | collective-permute-start | bytes 393224 | tf_op jit(solution)/shard_map/ppermute | solution.py:57
  56.3 1.4 %collective-permute-done.22.middle = bf16[2,256,128]{2,1,0:T(8,128)(2,1)S(1)} collective-permute-done((bf16[2,256,128]{2,1,0:T(8,128)(2,1)S(1)}, bf16[2,256,128]{2,1,0:T(8,128)(2,1)S(1)}, u32[]{:S(2)}, u32[]{:S(2)}) %collective-permute-start.22) | collective-permute-done | bytes 131104 | tf_op jit(solution)/shard_map/ppermute | solution.py:57
  58.0 2.0 %collective-permute-start.25 = (bf16[256,128]{1,0:T(8,128)(2,1)S(1)}, bf16[256,128]{1,0:T(8,128)(2,1)S(1)}, u32[]{:S(2)}, u32[]{:S(2)}) collective-permute-start(bf16[256,128]{1,0:T(8,128)(2,1)S(1)} %shard_map.77), channel_id=1, source_target_pairs={{0,3},{1,2},{2,1},{3,0},{4,7},{5,6},{6,5},{7,4},{8,11},{9,10},{10,... | collective-permute-start | bytes 196616 | tf_op jit(solution)/shard_map/ppermute | solution.py:57
  61.8 1.6 %collective-permute-start.23 = (bf16[256,128]{1,0:T(8,128)(2,1)S(1)}, bf16[256,128]{1,0:T(8,128)(2,1)S(1)}, u32[]{:S(2)}, u32[]{:S(2)}) collective-permute-start(bf16[256,128]{1,0:T(8,128)(2,1)S(1)} %shard_map.75), channel_id=1, source_target_pairs={{0,1},{1,0},{2,3},{3,2},{4,5},{5,4},{6,7},{7,6},{8,9},{9,8},{10,11... | collective-permute-start | bytes 196616 | tf_op jit(solution)/shard_map/ppermute | solution.py:57
  64.0 2.0 %collective-permute-done.23.refs_1_ = bf16[256,128]{1,0:T(8,128)(2,1)S(1)} collective-permute-done((bf16[256,128]{1,0:T(8,128)(2,1)S(1)}, bf16[256,128]{1,0:T(8,128)(2,1)S(1)}, u32[]{:S(2)}, u32[]{:S(2)}) %collective-permute-start.23) | collective-permute-done | bytes 65568 | tf_op jit(solution)/shard_map/ppermute | solution.py:57
  65.9 2.8 %collective-permute-start.26 = (bf16[4,128,128]{2,1,0:T(8,128)(2,1)S(1)}, bf16[4,128,128]{2,1,0:T(8,128)(2,1)S(1)}, u32[]{:S(2)}, u32[]{:S(2)}) collective-permute-start(bf16[4,128,128]{2,1,0:T(8,128)(2,1)S(1)} %get-tuple-element.68), channel_id=1, source_target_pairs={{0,4},{1,5},{2,6},{3,7},{4,0},{5,1},{6,2},{7,3},{8,12},{9,13},{10,... | collective-permute-start | bytes 393224 | tf_op jit(solution)/shard_map/ppermute | solution.py:57
  (75 shorter events, 23.3 us)
Async XLA Ops:
  0.0 19.8 %collective-permute-start = (bf16[256,768]{1,0:T(8,128)(2,1)}, bf16[256,768]{1,0:T(8,128)(2,1)S(1)}, u32[]{:S(2)}, u32[]{:S(2)}) collective-permute-start(bf16[256,768]{1,0:T(8,128)(2,1)} %w.1), channel_id=1, source_target_pairs={{0,16},{1,17},{2,18},{3,19},{4,20},{5,21},{6,22},{7,23},{8,24},{9,... | collective-permute-start | bytes 1179656 | tf_op jit(solution)/shard_map/ppermute | solution.py:57
  5.3 4.4 %collective-permute-start.3 = (bf16[128,256]{1,0:T(8,128)(2,1)S(1)}, bf16[128,256]{1,0:T(8,128)(2,1)S(1)}, u32[]{:S(2)}, u32[]{:S(2)}) collective-permute-start(bf16[128,256]{1,0:T(8,128)(2,1)S(1)} %get-tuple-element.39), channel_id=1, source_target_pairs={{0,3},{1,2},{2,1},{3,0},{4,7},{5,6},{6,5},{7,4},{8,11},{9,10},{10,... | collective-permute-start | bytes 196616 | tf_op jit(solution)/shard_map/ppermute | solution.py:57
  7.6 6.0 %collective-permute-start.1 = (bf16[336,256]{1,0:T(8,128)(2,1)S(1)}, bf16[336,256]{1,0:T(8,128)(2,1)S(1)}, u32[]{:S(2)}, u32[]{:S(2)}) collective-permute-start(bf16[336,256]{1,0:T(8,128)(2,1)S(1)} %get-tuple-element.37), channel_id=1, source_target_pairs={{0,1},{1,0},{2,3},{3,2},{4,5},{5,4},{6,7},{7,6},{8,9},{9,8},{10,11... | collective-permute-start | bytes 516104 | tf_op jit(solution)/shard_map/ppermute | solution.py:57
  7.8 5.8 %collective-permute-start.2 = (bf16[336,256]{1,0:T(8,128)(2,1)S(1)}, bf16[336,256]{1,0:T(8,128)(2,1)S(1)}, u32[]{:S(2)}, u32[]{:S(2)}) collective-permute-start(bf16[336,256]{1,0:T(8,128)(2,1)S(1)} %get-tuple-element.38), channel_id=1, source_target_pairs={{0,2},{1,3},{2,0},{3,1},{4,6},{5,7},{6,4},{7,5},{8,10},{9,11},{10,... | collective-permute-start | bytes 516104 | tf_op jit(solution)/shard_map/ppermute | solution.py:57
  9.7 15.0 %collective-permute-start.7 = (bf16[128,2048]{1,0:T(8,128)(2,1)}, bf16[128,2048]{1,0:T(8,128)(2,1)S(1)}, u32[]{:S(2)}, u32[]{:S(2)}) collective-permute-start(bf16[128,2048]{1,0:T(8,128)(2,1)} %bitcast.13), channel_id=1, source_target_pairs={{0,2},{1,3},{2,0},{3,1},{4,6},{5,7},{6,4},{7,5},{8,10},{9,11},{10,... | collective-permute-start | bytes 1572872 | tf_op jit(solution)/shard_map/ppermute | solution.py:57
  10.9 13.8 %collective-permute-start.6 = (bf16[128,2048]{1,0:T(8,128)(2,1)}, bf16[128,2048]{1,0:T(8,128)(2,1)S(1)}, u32[]{:S(2)}, u32[]{:S(2)}) collective-permute-start(bf16[128,2048]{1,0:T(8,128)(2,1)} %bitcast.14), channel_id=1, source_target_pairs={{0,1},{1,0},{2,3},{3,2},{4,5},{5,4},{6,7},{7,6},{8,9},{9,8},{10,11... | collective-permute-start | bytes 1572872 | tf_op jit(solution)/shard_map/ppermute | solution.py:57
  13.7 13.8 %collective-permute-start.8 = (bf16[256,768]{1,0:T(8,128)(2,1)S(1)}, bf16[256,768]{1,0:T(8,128)(2,1)S(1)}, u32[]{:S(2)}, u32[]{:S(2)}) collective-permute-start(bf16[256,768]{1,0:T(8,128)(2,1)S(1)} %shard_map.67.refs_2_.refs_0_), channel_id=1, source_target_pairs={{0,8},{1,9},{2,10},{3,11},{4,12},{5,13},{6,14},{7,15},{8,0},{9,1},... | collective-permute-start | bytes 1179656 | tf_op jit(solution)/shard_map/ppermute | solution.py:57
  19.9 6.3 %collective-permute-start.4 = (bf16[256,256]{1,0:T(8,128)(2,1)S(1)}, bf16[256,256]{1,0:T(8,128)(2,1)S(1)}, u32[]{:S(2)}, u32[]{:S(2)}) collective-permute-start(bf16[256,256]{1,0:T(8,128)(2,1)S(1)} %get-tuple-element.70), channel_id=1, source_target_pairs={{0,1},{1,0},{2,3},{3,2},{4,5},{5,4},{6,7},{7,6},{8,9},{9,8},{10,11... | collective-permute-start | bytes 393224 | tf_op jit(solution)/shard_map/ppermute | solution.py:57
  21.1 6.4 %collective-permute-start.5 = (bf16[256,256]{1,0:T(8,128)(2,1)S(1)}, bf16[256,256]{1,0:T(8,128)(2,1)S(1)}, u32[]{:S(2)}, u32[]{:S(2)}) collective-permute-start(bf16[256,256]{1,0:T(8,128)(2,1)S(1)} %get-tuple-element.69), channel_id=1, source_target_pairs={{0,2},{1,3},{2,0},{3,1},{4,6},{5,7},{6,4},{7,5},{8,10},{9,11},{10,... | collective-permute-start | bytes 393224 | tf_op jit(solution)/shard_map/ppermute | solution.py:57
  30.6 4.1 %collective-permute-start.10 = (bf16[384,2048]{1,0:T(8,128)(2,1)S(1)}, bf16[384,2048]{1,0:T(8,128)(2,1)S(1)}, u32[]{:S(2)}, u32[]{:S(2)}) collective-permute-start(bf16[384,2048]{1,0:T(8,128)(2,1)S(1)} %get-tuple-element.53.refs_0_), channel_id=1, source_target_pairs={{0,4},{1,5},{2,6},{3,7},{4,0},{5,1},{6,2},{7,3},{8,12},{9,13},{10,... | collective-permute-start | bytes 4718600 | tf_op jit(solution)/shard_map/ppermute | solution.py:57
  31.1 3.5 %collective-permute-start.12 = (bf16[528,384]{1,0:T(8,128)(2,1)S(1)}, bf16[528,384]{1,0:T(8,128)(2,1)S(1)}, u32[]{:S(2)}, u32[]{:S(2)}) collective-permute-start(bf16[528,384]{1,0:T(8,128)(2,1)S(1)} %pad_maximum_fusion.1), channel_id=1, source_target_pairs={{0,4},{1,5},{2,6},{3,7},{4,0},{5,1},{6,2},{7,3},{8,12},{9,13},{10,... | collective-permute-start | bytes 1216520 | tf_op jit(solution)/shard_map/ppermute | solution.py:57
  31.3 7.5 %collective-permute-start.11 = (bf16[128,1024]{1,0:T(8,128)(2,1)S(1)}, bf16[128,1024]{1,0:T(8,128)(2,1)S(1)}, u32[]{:S(2)}, u32[]{:S(2)}) collective-permute-start(bf16[128,1024]{1,0:T(8,128)(2,1)S(1)} %get-tuple-element.54), channel_id=1, source_target_pairs={{0,2},{1,3},{2,0},{3,1},{4,6},{5,7},{6,4},{7,5},{8,10},{9,11},{10,... | collective-permute-start | bytes 786440 | tf_op jit(solution)/shard_map/ppermute | solution.py:57
  31.8 7.2 %collective-permute-start.13 = (bf16[128,1024]{1,0:T(8,128)(2,1)S(1)}, bf16[128,1024]{1,0:T(8,128)(2,1)S(1)}, u32[]{:S(2)}, u32[]{:S(2)}) collective-permute-start(bf16[128,1024]{1,0:T(8,128)(2,1)S(1)} %get-tuple-element.59), channel_id=1, source_target_pairs={{0,1},{1,0},{2,3},{3,2},{4,5},{5,4},{6,7},{7,6},{8,9},{9,8},{10,11... | collective-permute-start | bytes 786440 | tf_op jit(solution)/shard_map/ppermute | solution.py:57
  33.0 10.5 %collective-permute-start.16 = (bf16[512,384]{1,0:T(8,128)(2,1)S(1)}, bf16[512,384]{1,0:T(8,128)(2,1)S(1)}, u32[]{:S(2)}, u32[]{:S(2)}) collective-permute-start(bf16[512,384]{1,0:T(8,128)(2,1)S(1)} %constant_dynamic-update-slice_fusion.refs_5_.refs_3_), channel_id=1, source_target_pairs={{0,8},{1,9},{2,10},{3,11},{4,12},{5,13},{6,14},{7,15},{8,0},{9,1},... | collective-permute-start | bytes 1179656 | tf_op jit(solution)/shard_map/ppermute | solution.py:57
  44.2 7.7 %collective-permute-start.17 = (bf16[4,256,128]{2,1,0:T(8,128)(2,1)S(1)}, bf16[4,256,128]{2,1,0:T(8,128)(2,1)S(1)}, u32[]{:S(2)}, u32[]{:S(2)}) collective-permute-start(bf16[4,256,128]{2,1,0:T(8,128)(2,1)S(1)} %get-tuple-element.64.own), channel_id=1, source_target_pairs={{0,8},{1,9},{2,10},{3,11},{4,12},{5,13},{6,14},{7,15},{8,0},{9,1},... | collective-permute-start | bytes 786440 | tf_op jit(solution)/shard_map/ppermute | solution.py:57
  45.4 9.7 %collective-permute-start.18 = (bf16[4,256,128]{2,1,0:T(8,128)(2,1)S(1)}, bf16[4,256,128]{2,1,0:T(8,128)(2,1)S(1)}, u32[]{:S(2)}, u32[]{:S(2)}) collective-permute-start(bf16[4,256,128]{2,1,0:T(8,128)(2,1)S(1)} %get-tuple-element.64.own), channel_id=1, source_target_pairs={{8,16},{9,17},{10,18},{11,19},{12,20},{13,21},{14,22},{15,23},{16,... | collective-permute-start | bytes 786440 | tf_op jit(solution)/shard_map/ppermute | solution.py:57
  49.6 6.7 %collective-permute-start.21 = (bf16[2,256,128]{2,1,0:T(8,128)(2,1)S(1)}, bf16[2,256,128]{2,1,0:T(8,128)(2,1)S(1)}, u32[]{:S(2)}, u32[]{:S(2)}) collective-permute-start(bf16[2,256,128]{2,1,0:T(8,128)(2,1)S(1)} %get-tuple-element.66.own), channel_id=1, source_target_pairs={{0,8},{1,9},{2,10},{3,11},{4,12},{5,13},{6,14},{7,15},{8,0},{9,1},... | collective-permute-start | bytes 393224 | tf_op jit(solution)/shard_map/ppermute | solution.py:57
  49.7 8.0 %collective-permute-start.22 = (bf16[2,256,128]{2,1,0:T(8,128)(2,1)S(1)}, bf16[2,256,128]{2,1,0:T(8,128)(2,1)S(1)}, u32[]{:S(2)}, u32[]{:S(2)}) collective-permute-start(bf16[2,256,128]{2,1,0:T(8,128)(2,1)S(1)} %get-tuple-element.66.own), channel_id=1, source_target_pairs={{8,16},{9,17},{10,18},{11,19},{12,20},{13,21},{14,22},{15,23},{16,... | collective-permute-start | bytes 393224 | tf_op jit(solution)/shard_map/ppermute | solution.py:57
  51.6 8.3 %collective-permute-start.19 = (bf16[2,256,128]{2,1,0:T(8,128)(2,1)S(1)}, bf16[2,256,128]{2,1,0:T(8,128)(2,1)S(1)}, u32[]{:S(2)}, u32[]{:S(2)}) collective-permute-start(bf16[2,256,128]{2,1,0:T(8,128)(2,1)S(1)} %get-tuple-element.65.own), channel_id=1, source_target_pairs={{0,8},{1,9},{2,10},{3,11},{4,12},{5,13},{6,14},{7,15},{8,0},{9,1},... | collective-permute-start | bytes 393224 | tf_op jit(solution)/shard_map/ppermute | solution.py:57
  51.9 8.6 %collective-permute-start.20 = (bf16[2,256,128]{2,1,0:T(8,128)(2,1)S(1)}, bf16[2,256,128]{2,1,0:T(8,128)(2,1)S(1)}, u32[]{:S(2)}, u32[]{:S(2)}) collective-permute-start(bf16[2,256,128]{2,1,0:T(8,128)(2,1)S(1)} %get-tuple-element.65.own), channel_id=1, source_target_pairs={{8,16},{9,17},{10,18},{11,19},{12,20},{13,21},{14,22},{15,23},{16,... | collective-permute-start | bytes 393224 | tf_op jit(solution)/shard_map/ppermute | solution.py:57
  58.0 5.6 %collective-permute-start.25 = (bf16[256,128]{1,0:T(8,128)(2,1)S(1)}, bf16[256,128]{1,0:T(8,128)(2,1)S(1)}, u32[]{:S(2)}, u32[]{:S(2)}) collective-permute-start(bf16[256,128]{1,0:T(8,128)(2,1)S(1)} %shard_map.77), channel_id=1, source_target_pairs={{0,3},{1,2},{2,1},{3,0},{4,7},{5,6},{6,5},{7,4},{8,11},{9,10},{10,... | collective-permute-start | bytes 196616 | tf_op jit(solution)/shard_map/ppermute | solution.py:57
  60.8 3.2 %collective-permute-start.24 = (bf16[256,128]{1,0:T(8,128)(2,1)S(1)}, bf16[256,128]{1,0:T(8,128)(2,1)S(1)}, u32[]{:S(2)}, u32[]{:S(2)}) collective-permute-start(bf16[256,128]{1,0:T(8,128)(2,1)S(1)} %shard_map.76), channel_id=1, source_target_pairs={{0,2},{1,3},{2,0},{3,1},{4,6},{5,7},{6,4},{7,5},{8,10},{9,11},{10,... | collective-permute-start | bytes 196616 | tf_op jit(solution)/shard_map/ppermute | solution.py:57
  61.8 4.2 %collective-permute-start.23 = (bf16[256,128]{1,0:T(8,128)(2,1)S(1)}, bf16[256,128]{1,0:T(8,128)(2,1)S(1)}, u32[]{:S(2)}, u32[]{:S(2)}) collective-permute-start(bf16[256,128]{1,0:T(8,128)(2,1)S(1)} %shard_map.75), channel_id=1, source_target_pairs={{0,1},{1,0},{2,3},{3,2},{4,5},{5,4},{6,7},{7,6},{8,9},{9,8},{10,11... | collective-permute-start | bytes 196616 | tf_op jit(solution)/shard_map/ppermute | solution.py:57
  65.9 3.8 %collective-permute-start.26 = (bf16[4,128,128]{2,1,0:T(8,128)(2,1)S(1)}, bf16[4,128,128]{2,1,0:T(8,128)(2,1)S(1)}, u32[]{:S(2)}, u32[]{:S(2)}) collective-permute-start(bf16[4,128,128]{2,1,0:T(8,128)(2,1)S(1)} %get-tuple-element.68), channel_id=1, source_target_pairs={{0,4},{1,5},{2,6},{3,7},{4,0},{5,1},{6,2},{7,3},{8,12},{9,13},{10,... | collective-permute-start | bytes 393224 | tf_op jit(solution)/shard_map/ppermute | solution.py:57
  (13 other events, 41.6 us)

commit v12 on v11

--- a/solution.py
+++ b/solution.py
@@ -82,20 +82,14 @@
     return tm >> 1, tm & 1, lax.axis_index("depth")
 
 
-def split_kernel(mask, w, raw, to_x, to_y, to_across, keep, flags_ref):
+def split_kernel(w, raw, to_x, to_y, to_across, keep):
     _, _, depth = where_am_i()
     even = (depth & 1) == 0
-    size, half = w.shape[0], raw.shape[0] // 2
+    size, half = w.shape[0], (raw.shape[0] - EXTRA) // 2
     low, high = w[:, :PAIR], w[:, 2 * PAIR :]
     to_x[:size] = w[:, PAIR : 2 * PAIR]
     to_y[:size] = jnp.where(even, high, low)
     keep[...] = jnp.where(even, low, high)
-    lane = lax.broadcasted_iota(jnp.int32, (EXTRA, HD), 1)
-    flags = jnp.zeros((EXTRA, HD), jnp.int32)
-    for entry in range(mask.shape[0]):
-        flags = jnp.where(lane == entry, mask[entry], flags)
-    flags = flags.astype(jnp.float32).astype(jnp.bfloat16)
-    flags_ref[...] = flags
     at = to_across.shape[0] - EXTRA - half
     for i in range(2):
         to_across[:at, i * HD : (i + 1) * HD] = raw[:at]
@@ -103,7 +97,7 @@
         for i in range(2):
             here = slice(i * HD, (i + 1) * HD)
             ref[at : at + half, here] = raw[i * half : (i + 1) * half]
-            ref[at + half :, here] = flags
+            ref[at + half :, here] = raw[2 * half :]
 
 
 def sorted_groups(kept, from_x, from_y):
@@ -125,12 +119,12 @@
         out_ref[:, (3 + third) * HD : (4 + third) * HD] = other
 
 
-def sort_far_kernel(kept, from_x, from_y, plane_x, plane_y, across, own_flags, keep_ref, send_ref, flags_ref):
+def sort_far_kernel(kept, from_x, from_y, plane_x, plane_y, across, raw, keep_ref, send_ref, flags_ref):
     for third, mine, other in sorted_groups(kept, from_x, from_y):
         send_ref[:, third * HD : (third + 1) * HD] = other
         keep_ref[:, third * HD : (third + 1) * HD] = mine
     row = lax.broadcasted_iota(jnp.int32, (EXTRA, HD), 0)
-    flags = own_flags[...].astype(jnp.float32)
+    flags = raw[raw.shape[0] - EXTRA :].astype(jnp.float32)
     for r, ref in enumerate((plane_x, plane_y, across)):
         flags = jnp.where(row == r + 1, ref[ref.shape[0] - EXTRA :, :HD].astype(jnp.float32), flags)
     flags = flags.astype(jnp.bfloat16)
@@ -147,8 +141,8 @@
         half = ref.shape[1]
         ref[...] = streams[i][:, i * half : (i + 1) * half]
     _, _, depth = where_am_i()
-    rows, width = raw.shape[0], conv_w.shape[1]
-    raws = [raw[...]]
+    rows, width = raw.shape[0] - EXTRA, conv_w.shape[1]
+    raws = [raw[:rows]]
     for ref in (plane_x, plane_y, across):
         at = ref.shape[0] - EXTRA - rows // 2
         raws.append(jnp.concatenate([ref[at : at + rows // 2, :HD], ref[at : at + rows // 2, HD:]], axis=0))
@@ -220,7 +214,7 @@
             v_at = V_ORDER.index(r)
             q_ref[r, at, :] = mine[:, :HD]
             k_ref[r, at, :] = mine[:, HD:PAIR]
-            (v_first, v_second)[v_at // 2][v_at % 2, at, :] = mine[:, PAIR:]
+            (v_first, v_second)[v_at // 3][v_at % 3, at, :] = mine[:, PAIR:]
 
 
 def spans(u):
@@ -263,7 +257,7 @@
 
 def mix_kernel(r, weights, outer, own, middle, out_ref):
     block = weights.shape[1] // 2
-    values = neighbours(outer, own, middle, V_ORDER.index(r) % 2)
+    values = neighbours(outer, own, middle, V_ORDER.index(r) % 3)
     for u in range(2):
         w = weights[r, u * block : (u + 1) * block]
         v = [values[side][first * block : last * block] for side, first, last in spans(u)]
@@ -289,7 +283,7 @@
 
 
 def call(kernel, outs, places, scratch=(), macs=0, limit=32):
-    spaces = {"s": SMEM, "v": VMEM, "a": pl.ANY}
+    spaces = {"v": VMEM}
     return pl.pallas_call(
         kernel,
         out_shape=outs,
@@ -312,14 +306,16 @@
 
     far_raw = swap_z(w_qkv, 2)
 
-    raw, stream = raw.reshape(block, feat_len), stream.reshape(block, width)
+    mask_row = jnp.pad(mask.reshape(1, mask.shape[2]), ((0, 0), (0, feat_len - mask.shape[2]))).astype(bf16)
+    raw = jnp.concatenate([raw.reshape(block, feat_len), jnp.broadcast_to(mask_row, (EXTRA, feat_len))], axis=0)
+    stream = stream.reshape(block, width)
     conv_w, gain = conv_w.reshape(3 * feat_len, width), gain.reshape(1, width)
     more = block // 2 + EXTRA
-    *to, kept, own_flags = call(
+    *to, kept = call(
         split_kernel,
-        (array(size + more, PAIR), array(size + more, PAIR), array(block, PAIR), array(size, PAIR), array(EXTRA, HD)),
-        "svv",
-    )(mask.reshape(mask.shape[2]), w_qkv, raw)
+        (array(size + more, PAIR), array(size + more, PAIR), array(block, PAIR), array(size, PAIR)),
+        "vv",
+    )(w_qkv, raw)
     plane = [swap_depth(t, r) for t, r in zip(to, (1, 2, 3))]
     own = call(sort_kernel, array(size, 6 * HD), "vvv")(kept, *plane[:2])
     near = swap_z(own, 1)
@@ -350,7 +346,7 @@
         sort_far_kernel,
         (array(size, 3 * HD), array(size, 3 * HD), array(EXTRA, 3 * HD)),
         "v" * 7,
-    )(kept, from_x, from_y, *plane, own_flags)
+    )(kept, from_x, from_y, *plane, raw)
     diagonal = swap_depth(diagonal[0], 2), swap_depth(diagonal[1], 1)
     far = jnp.concatenate([keep, swap_core(send)], axis=0)
     last = swap_z(far, 1)
@@ -371,9 +367,9 @@
         "v" * 7,
         macs=2 * block * 3 * rows * 3 * HD,
     )(diagonal, *swapped, *weights)
-    one_head, half_head = array(4, 2 * block, HD), array(2, 2 * block, HD)
+    one_head = array(4, 2 * block, HD)
     q, k, *v = call(
-        finish_kernel, (one_head, one_head, half_head, half_head), "v" * 6, macs=8 * block * rows * 3 * HD
+        finish_kernel, (one_head, one_head, array(3, 2 * block, HD), array(1, 2 * block, HD)), "v" * 6, macs=8 * block * rows * 3 * HD
     )(*early, diagonal, last, total, total_diagonal)
 
     weights = call(weigh_kernel, array(4, 2 * block, 5 * block), "v" * 6, macs=8 * block * 5 * block * HD)(
@@ -381,9 +377,9 @@
     )
     values = [(swap_z(t, 1), t, swap_middle(t)) for t in v]
     pieces = {}
-    for r in V_ORDER:
+    for i, r in enumerate(V_ORDER):
         mixed = call(functools.partial(mix_kernel, r), array(2 * block, HD), "vvvv", macs=2 * block * 5 * block * HD)(
-            weights, *values[V_ORDER.index(r) // 2]
+            weights, *values[i // 3]
         )
         pieces[r] = swap_depth(mixed, r) if r else mixed
     kept, sent = call(pack_kernel, (array(4, block, HD),) * 2, "vvvv")(*[pieces[r] for r in range(4)])

time: 71.4 us -> 72.3 us (1.013)
  local copies, waits for them, and re-layouts: 5.41 us -> 3.26 us
  waiting for transfers between devices: 20.7 us -> 22.5 us
  other arithmetic: 0.11 us -> 1.52 us
    unnamed x21 -> x13, local copies, waits for them, and re-layouts: 5.3 us -> 3.13 us
    ppermute x27, waiting for transfers between devices: 20.7 us -> 22.5 us  [hop(): return lax.ppermute(value, ('tm', 'depth'), pairs)]
    concatenate x0 -> x1, other arithmetic: none -> 0.76 us  [plane_device(): jnp.concatenate([raw.reshape(block, feat_len), jnp.broadcast_to(mask_row,...]
  transfers between devices with their start and end apart: 27 -> 27, of which waited for: 16 -> 14; matrix products, arithmetic and copies ran while one was open for 0% -> 2% of each run, Pallas kernels for 10% -> 9%
where the time goes in v12:
time: 72.3 us; the launch traced here: 71.8 us
  starting transfers between devices  35.9 us (50%)
  waiting for transfers between devices  22.5 us (31%)
  Pallas kernels  8.34 us (12%)
  local copies, waits for them, and re-layouts  3.26 us (5%)
  other arithmetic  1.52 us (2%)
    ppermute x27, starting transfers between devices, hop(): return lax.ppermute(value, ('tm', 'depth'), pairs)  35.9 us
    ppermute x27, waiting for transfers between devices, hop(): return lax.ppermute(value, ('tm', 'depth'), pairs)  22.5 us
    unnamed x13, local copies, waits for them, and re-layouts  3.13 us
    pallas_call x3, Pallas kernels, embed(): call(functools.partial(embed_kernel, rs, len(finished)), out, 'v' * (6 +...  2.38 us
  transfers between devices with their start and end apart: 27, of which 14 were waited for; matrix products, arithmetic and copies ran while one was open for 2% of the time, Pallas kernels for 9%

profile of v12, /device:TPU:9, one launch (start us, length us, event | category | flops | bytes accessed | tf_op | source)
XLA Modules:
  0.0 71.8 jit_solution(5230780671968822138)
XLA Ops:
  0.0 2.3 %collective-permute-start = (bf16[256,768]{1,0:T(8,128)(2,1)}, bf16[256,768]{1,0:T(8,128)(2,1)S(1)}, u32[]{:S(2)}, u32[]{:S(2)}) collective-permute-start(bf16[256,768]{1,0:T(8,128)(2,1)} %w.1), channel_id=1, source_target_pairs={{0,16},{1,17},{2,18},{3,19},{4,20},{5,21},{6,22},{7,23},{8,24},{9,... | collective-permute-start | bytes 1179656 | tf_op jit(solution)/shard_map/ppermute | solution.py:57
  4.8 2.2 %collective-permute-start.3 = (bf16[128,256]{1,0:T(8,128)(2,1)S(1)}, bf16[128,256]{1,0:T(8,128)(2,1)S(1)}, u32[]{:S(2)}, u32[]{:S(2)}) collective-permute-start(bf16[128,256]{1,0:T(8,128)(2,1)S(1)} %get-tuple-element.38), channel_id=1, source_target_pairs={{0,3},{1,2},{2,1},{3,0},{4,7},{5,6},{6,5},{7,4},{8,11},{9,10},{10,... | collective-permute-start | bytes 196616 | tf_op jit(solution)/shard_map/ppermute | solution.py:57
  7.5 1.7 %collective-permute-done.3.across = bf16[128,256]{1,0:T(8,128)(2,1)S(1)} collective-permute-done((bf16[128,256]{1,0:T(8,128)(2,1)S(1)}, bf16[128,256]{1,0:T(8,128)(2,1)S(1)}, u32[]{:S(2)}, u32[]{:S(2)}) %collective-permute-start.3) | collective-permute-done | bytes 65568 | tf_op jit(solution)/shard_map/ppermute | solution.py:57
  11.6 1.4 %collective-permute-done.1.plane_x.from_x = bf16[336,256]{1,0:T(8,128)(2,1)S(1)} collective-permute-done((bf16[336,256]{1,0:T(8,128)(2,1)S(1)}, bf16[336,256]{1,0:T(8,128)(2,1)S(1)}, u32[]{:S(2)}, u32[]{:S(2)}) %collective-permute-start.1) | collective-permute-done | bytes 172064 | tf_op jit(solution)/shard_map/ppermute | solution.py:57
  13.4 1.4 %copy-done = bf16[3,128,2048]{2,1,0:T(8,128)(2,1)S(1)} copy-done((bf16[3,128,2048]{2,1,0:T(8,128)(2,1)S(1)}, bf16[3,128,2048]{2,1,0:T(8,128)(2,1)}, u32[]{:S(2)}) %copy-start) | copy-done | bytes 1572888
  16.1 3.7 %collective-permute-done = bf16[256,768]{1,0:T(8,128)(2,1)S(1)} collective-permute-done((bf16[256,768]{1,0:T(8,128)(2,1)}, bf16[256,768]{1,0:T(8,128)(2,1)S(1)}, u32[]{:S(2)}, u32[]{:S(2)}) %collective-permute-start) | collective-permute-done | bytes 393248 | tf_op jit(solution)/shard_map/ppermute | solution.py:57
  19.9 1.3 %collective-permute-start.4 = (bf16[256,256]{1,0:T(8,128)(2,1)S(1)}, bf16[256,256]{1,0:T(8,128)(2,1)S(1)}, u32[]{:S(2)}, u32[]{:S(2)}) collective-permute-start(bf16[256,256]{1,0:T(8,128)(2,1)S(1)} %get-tuple-element.68), channel_id=1, source_target_pairs={{0,1},{1,0},{2,3},{3,2},{4,5},{5,4},{6,7},{7,6},{8,9},{9,8},{10,11... | collective-permute-start | bytes 393224 | tf_op jit(solution)/shard_map/ppermute | solution.py:57
  22.4 1.8 %collective-permute-done.7.refs_1_ = bf16[128,2048]{1,0:T(8,128)(2,1)S(1)} collective-permute-done((bf16[128,2048]{1,0:T(8,128)(2,1)}, bf16[128,2048]{1,0:T(8,128)(2,1)S(1)}, u32[]{:S(2)}, u32[]{:S(2)}) %collective-permute-start.7) | collective-permute-done | bytes 524320 | tf_op jit(solution)/shard_map/ppermute | solution.py:57
  25.6 1.3 %collective-permute-done.5.from_y = bf16[256,256]{1,0:T(8,128)(2,1)S(1)} collective-permute-done((bf16[256,256]{1,0:T(8,128)(2,1)S(1)}, bf16[256,256]{1,0:T(8,128)(2,1)S(1)}, u32[]{:S(2)}, u32[]{:S(2)}) %collective-permute-start.5) | collective-permute-done | bytes 131104 | tf_op jit(solution)/shard_map/ppermute | solution.py:57
  27.1 1.9 %collective-permute-start.9 = (bf16[256,384]{1,0:T(8,128)(2,1)S(1)}, bf16[256,384]{1,0:T(8,128)(2,1)S(1)}, u32[]{:S(2)}, u32[]{:S(2)}) collective-permute-start(bf16[256,384]{1,0:T(8,128)(2,1)S(1)} %get-tuple-element.48), channel_id=1, source_target_pairs={{0,4},{1,5},{2,6},{3,7},{4,0},{5,1},{6,2},{7,3},{8,12},{9,13},{10,... | collective-permute-start | bytes 589832 | tf_op jit(solution)/shard_map/ppermute | solution.py:57
  32.5 1.7 %collective-permute-start.16 = (bf16[512,384]{1,0:T(8,128)(2,1)S(1)}, bf16[512,384]{1,0:T(8,128)(2,1)S(1)}, u32[]{:S(2)}, u32[]{:S(2)}) collective-permute-start(bf16[512,384]{1,0:T(8,128)(2,1)S(1)} %constant_dynamic-update-slice_fusion.refs_5_.refs_3_), channel_id=1, source_target_pairs={{0,8},{1,9},{2,10},{3,11},{4,12},{5,13},{6,14},{7,15},{8,0},{9,1},... | collective-permute-start | bytes 1179656 | tf_op jit(solution)/shard_map/ppermute | solution.py:57
  34.2 1.4 %shard_map.69.refs_4_ = f32[768,384]{1,0:T(8,128)S(1)} custom-call(bf16[384,2048]{1,0:T(8,128)(2,1)S(1)} %get-tuple-element.51.refs_0_, bf16[384,2048]{1,0:T(8,128)(2,1)S(1)} %collective-permute-done.10.refs_1_, bf16[256,768]{1,0:T(8,128)(2,1)S(1)} %shard_map.67.refs_2_.refs_0_, bf16[256,768]{1,0:T(8,128)(2,1)S(1)} %collective-permute-done.8.refs_3_.refs_1_, ...), custom_call_target="tpu_custom_call" | custom-call | flops 905969664 | tf_op jit(solution)/shard_map/pallas_call | solution.py:359
  35.5 2.8 %collective-permute-done.11 = bf16[128,1024]{1,0:T(8,128)(2,1)S(1)} collective-permute-done((bf16[128,1024]{1,0:T(8,128)(2,1)S(1)}, bf16[128,1024]{1,0:T(8,128)(2,1)S(1)}, u32[]{:S(2)}, u32[]{:S(2)}) %collective-permute-start.11) | collective-permute-done | bytes 262176 | tf_op jit(solution)/shard_map/ppermute | solution.py:57
  39.2 1.6 %collective-permute-start.14 = (bf16[80,2048]{1,0:T(8,128)(2,1)S(1)}, bf16[80,2048]{1,0:T(8,128)(2,1)S(1)}, u32[]{:S(2)}, u32[]{:S(2)}) collective-permute-start(bf16[80,2048]{1,0:T(8,128)(2,1)S(1)} %slice.29), channel_id=1, source_target_pairs={{0,4},{1,5},{2,6},{3,7},{4,0},{5,1},{6,2},{7,3},{8,12},{9,13},{10,... | collective-permute-start | bytes 983048 | tf_op jit(solution)/shard_map/ppermute | solution.py:57
  40.9 1.4 %collective-permute-done.15.bottom = bf16[48,2048]{1,0:T(8,128)(2,1)S(1)} collective-permute-done((bf16[48,2048]{1,0:T(8,128)(2,1)S(1)}, bf16[48,2048]{1,0:T(8,128)(2,1)S(1)}, u32[]{:S(2)}, u32[]{:S(2)}) %collective-permute-start.15) | collective-permute-done | bytes 196640 | tf_op jit(solution)/shard_map/ppermute | solution.py:57
  43.7 1.7 %collective-permute-start.17 = (bf16[4,256,128]{2,1,0:T(8,128)(2,1)S(1)}, bf16[4,256,128]{2,1,0:T(8,128)(2,1)S(1)}, u32[]{:S(2)}, u32[]{:S(2)}) collective-permute-start(bf16[4,256,128]{2,1,0:T(8,128)(2,1)S(1)} %get-tuple-element.62.own), channel_id=1, source_target_pairs={{0,8},{1,9},{2,10},{3,11},{4,12},{5,13},{6,14},{7,15},{8,0},{9,1},... | collective-permute-start | bytes 786440 | tf_op jit(solution)/shard_map/ppermute | solution.py:57
  45.4 4.2 %collective-permute-start.18 = (bf16[4,256,128]{2,1,0:T(8,128)(2,1)S(1)}, bf16[4,256,128]{2,1,0:T(8,128)(2,1)S(1)}, u32[]{:S(2)}, u32[]{:S(2)}) collective-permute-start(bf16[4,256,128]{2,1,0:T(8,128)(2,1)S(1)} %get-tuple-element.62.own), channel_id=1, source_target_pairs={{8,16},{9,17},{10,18},{11,19},{12,20},{13,21},{14,22},{15,23},{16,... | collective-permute-start | bytes 786440 | tf_op jit(solution)/shard_map/ppermute | solution.py:57
  49.7 1.9 %collective-permute-start.22 = (bf16[3,256,128]{2,1,0:T(8,128)(2,1)S(1)}, bf16[3,256,128]{2,1,0:T(8,128)(2,1)S(1)}, u32[]{:S(2)}, u32[]{:S(2)}) collective-permute-start(bf16[3,256,128]{2,1,0:T(8,128)(2,1)S(1)} %get-tuple-element.64.own), channel_id=1, source_target_pairs={{8,16},{9,17},{10,18},{11,19},{12,20},{13,21},{14,22},{15,23},{16,... | collective-permute-start | bytes 589832 | tf_op jit(solution)/shard_map/ppermute | solution.py:57
  51.9 3.2 %collective-permute-start.20 = (bf16[1,256,128]{2,1,0:T(8,128)(2,1)S(1)}, bf16[1,256,128]{2,1,0:T(8,128)(2,1)S(1)}, u32[]{:S(2)}, u32[]{:S(2)}) collective-permute-start(bf16[1,256,128]{2,1,0:T(8,128)(2,1)S(1)} %get-tuple-element.63.own), channel_id=1, source_target_pairs={{8,16},{9,17},{10,18},{11,19},{12,20},{13,21},{14,22},{15,23},{16,... | collective-permute-start | bytes 196616 | tf_op jit(solution)/shard_map/ppermute | solution.py:57
  56.3 2.8 %collective-permute-done.22.middle = bf16[3,256,128]{2,1,0:T(8,128)(2,1)S(1)} collective-permute-done((bf16[3,256,128]{2,1,0:T(8,128)(2,1)S(1)}, bf16[3,256,128]{2,1,0:T(8,128)(2,1)S(1)}, u32[]{:S(2)}, u32[]{:S(2)}) %collective-permute-start.22) | collective-permute-done | bytes 196640 | tf_op jit(solution)/shard_map/ppermute | solution.py:57
  59.4 2.0 %collective-permute-start.25 = (bf16[256,128]{1,0:T(8,128)(2,1)S(1)}, bf16[256,128]{1,0:T(8,128)(2,1)S(1)}, u32[]{:S(2)}, u32[]{:S(2)}) collective-permute-start(bf16[256,128]{1,0:T(8,128)(2,1)S(1)} %shard_map.77), channel_id=1, source_target_pairs={{0,3},{1,2},{2,1},{3,0},{4,7},{5,6},{6,5},{7,4},{8,11},{9,10},{10,... | collective-permute-start | bytes 196616 | tf_op jit(solution)/shard_map/ppermute | solution.py:57
  61.6 1.3 %collective-permute-start.24 = (bf16[256,128]{1,0:T(8,128)(2,1)S(1)}, bf16[256,128]{1,0:T(8,128)(2,1)S(1)}, u32[]{:S(2)}, u32[]{:S(2)}) collective-permute-start(bf16[256,128]{1,0:T(8,128)(2,1)S(1)} %shard_map.76), channel_id=1, source_target_pairs={{0,2},{1,3},{2,0},{3,1},{4,6},{5,7},{6,4},{7,5},{8,10},{9,11},{10,... | collective-permute-start | bytes 196616 | tf_op jit(solution)/shard_map/ppermute | solution.py:57
  64.8 1.8 %collective-permute-done.23.refs_1_ = bf16[256,128]{1,0:T(8,128)(2,1)S(1)} collective-permute-done((bf16[256,128]{1,0:T(8,128)(2,1)S(1)}, bf16[256,128]{1,0:T(8,128)(2,1)S(1)}, u32[]{:S(2)}, u32[]{:S(2)}) %collective-permute-start.23) | collective-permute-done | bytes 65568 | tf_op jit(solution)/shard_map/ppermute | solution.py:57
  66.6 3.4 %collective-permute-start.26 = (bf16[4,128,128]{2,1,0:T(8,128)(2,1)S(1)}, bf16[4,128,128]{2,1,0:T(8,128)(2,1)S(1)}, u32[]{:S(2)}, u32[]{:S(2)}) collective-permute-start(bf16[4,128,128]{2,1,0:T(8,128)(2,1)S(1)} %get-tuple-element.66), channel_id=1, source_target_pairs={{0,4},{1,5},{2,6},{3,7},{4,0},{5,1},{6,2},{7,3},{8,12},{9,13},{10,... | collective-permute-start | bytes 393224 | tf_op jit(solution)/shard_map/ppermute | solution.py:57
  (71 shorter events, 21.4 us)
Async XLA Ops:
  0.0 19.8 %collective-permute-start = (bf16[256,768]{1,0:T(8,128)(2,1)}, bf16[256,768]{1,0:T(8,128)(2,1)S(1)}, u32[]{:S(2)}, u32[]{:S(2)}) collective-permute-start(bf16[256,768]{1,0:T(8,128)(2,1)} %w.1), channel_id=1, source_target_pairs={{0,16},{1,17},{2,18},{3,19},{4,20},{5,21},{6,22},{7,23},{8,24},{9,... | collective-permute-start | bytes 1179656 | tf_op jit(solution)/shard_map/ppermute | solution.py:57
  4.8 4.4 %collective-permute-start.3 = (bf16[128,256]{1,0:T(8,128)(2,1)S(1)}, bf16[128,256]{1,0:T(8,128)(2,1)S(1)}, u32[]{:S(2)}, u32[]{:S(2)}) collective-permute-start(bf16[128,256]{1,0:T(8,128)(2,1)S(1)} %get-tuple-element.38), channel_id=1, source_target_pairs={{0,3},{1,2},{2,1},{3,0},{4,7},{5,6},{6,5},{7,4},{8,11},{9,10},{10,... | collective-permute-start | bytes 196616 | tf_op jit(solution)/shard_map/ppermute | solution.py:57
  7.0 6.0 %collective-permute-start.1 = (bf16[336,256]{1,0:T(8,128)(2,1)S(1)}, bf16[336,256]{1,0:T(8,128)(2,1)S(1)}, u32[]{:S(2)}, u32[]{:S(2)}) collective-permute-start(bf16[336,256]{1,0:T(8,128)(2,1)S(1)} %get-tuple-element.36), channel_id=1, source_target_pairs={{0,1},{1,0},{2,3},{3,2},{4,5},{5,4},{6,7},{7,6},{8,9},{9,8},{10,11... | collective-permute-start | bytes 516104 | tf_op jit(solution)/shard_map/ppermute | solution.py:57
  7.3 5.8 %collective-permute-start.2 = (bf16[336,256]{1,0:T(8,128)(2,1)S(1)}, bf16[336,256]{1,0:T(8,128)(2,1)S(1)}, u32[]{:S(2)}, u32[]{:S(2)}) collective-permute-start(bf16[336,256]{1,0:T(8,128)(2,1)S(1)} %get-tuple-element.37), channel_id=1, source_target_pairs={{0,2},{1,3},{2,0},{3,1},{4,6},{5,7},{6,4},{7,5},{8,10},{9,11},{10,... | collective-permute-start | bytes 516104 | tf_op jit(solution)/shard_map/ppermute | solution.py:57
  9.2 15.0 %collective-permute-start.7 = (bf16[128,2048]{1,0:T(8,128)(2,1)}, bf16[128,2048]{1,0:T(8,128)(2,1)S(1)}, u32[]{:S(2)}, u32[]{:S(2)}) collective-permute-start(bf16[128,2048]{1,0:T(8,128)(2,1)} %bitcast.12), channel_id=1, source_target_pairs={{0,2},{1,3},{2,0},{3,1},{4,6},{5,7},{6,4},{7,5},{8,10},{9,11},{10,... | collective-permute-start | bytes 1572872 | tf_op jit(solution)/shard_map/ppermute | solution.py:57
  10.4 13.8 %collective-permute-start.6 = (bf16[128,2048]{1,0:T(8,128)(2,1)}, bf16[128,2048]{1,0:T(8,128)(2,1)S(1)}, u32[]{:S(2)}, u32[]{:S(2)}) collective-permute-start(bf16[128,2048]{1,0:T(8,128)(2,1)} %bitcast.13), channel_id=1, source_target_pairs={{0,1},{1,0},{2,3},{3,2},{4,5},{5,4},{6,7},{7,6},{8,9},{9,8},{10,11... | collective-permute-start | bytes 1572872 | tf_op jit(solution)/shard_map/ppermute | solution.py:57
  13.2 13.8 %collective-permute-start.8 = (bf16[256,768]{1,0:T(8,128)(2,1)S(1)}, bf16[256,768]{1,0:T(8,128)(2,1)S(1)}, u32[]{:S(2)}, u32[]{:S(2)}) collective-permute-start(bf16[256,768]{1,0:T(8,128)(2,1)S(1)} %shard_map.67.refs_2_.refs_0_), channel_id=1, source_target_pairs={{0,8},{1,9},{2,10},{3,11},{4,12},{5,13},{6,14},{7,15},{8,0},{9,1},... | collective-permute-start | bytes 1179656 | tf_op jit(solution)/shard_map/ppermute | solution.py:57
  19.9 5.8 %collective-permute-start.4 = (bf16[256,256]{1,0:T(8,128)(2,1)S(1)}, bf16[256,256]{1,0:T(8,128)(2,1)S(1)}, u32[]{:S(2)}, u32[]{:S(2)}) collective-permute-start(bf16[256,256]{1,0:T(8,128)(2,1)S(1)} %get-tuple-element.68), channel_id=1, source_target_pairs={{0,1},{1,0},{2,3},{3,2},{4,5},{5,4},{6,7},{7,6},{8,9},{9,8},{10,11... | collective-permute-start | bytes 393224 | tf_op jit(solution)/shard_map/ppermute | solution.py:57
  21.1 5.8 %collective-permute-start.5 = (bf16[256,256]{1,0:T(8,128)(2,1)S(1)}, bf16[256,256]{1,0:T(8,128)(2,1)S(1)}, u32[]{:S(2)}, u32[]{:S(2)}) collective-permute-start(bf16[256,256]{1,0:T(8,128)(2,1)S(1)} %get-tuple-element.67), channel_id=1, source_target_pairs={{0,2},{1,3},{2,0},{3,1},{4,6},{5,7},{6,4},{7,5},{8,10},{9,11},{10,... | collective-permute-start | bytes 393224 | tf_op jit(solution)/shard_map/ppermute | solution.py:57
  30.1 4.1 %collective-permute-start.10 = (bf16[384,2048]{1,0:T(8,128)(2,1)S(1)}, bf16[384,2048]{1,0:T(8,128)(2,1)S(1)}, u32[]{:S(2)}, u32[]{:S(2)}) collective-permute-start(bf16[384,2048]{1,0:T(8,128)(2,1)S(1)} %get-tuple-element.51.refs_0_), channel_id=1, source_target_pairs={{0,4},{1,5},{2,6},{3,7},{4,0},{5,1},{6,2},{7,3},{8,12},{9,13},{10,... | collective-permute-start | bytes 4718600 | tf_op jit(solution)/shard_map/ppermute | solution.py:57
  30.6 3.6 %collective-permute-start.12 = (bf16[528,384]{1,0:T(8,128)(2,1)S(1)}, bf16[528,384]{1,0:T(8,128)(2,1)S(1)}, u32[]{:S(2)}, u32[]{:S(2)}) collective-permute-start(bf16[528,384]{1,0:T(8,128)(2,1)S(1)} %pad_maximum_fusion.1), channel_id=1, source_target_pairs={{0,4},{1,5},{2,6},{3,7},{4,0},{5,1},{6,2},{7,3},{8,12},{9,13},{10,... | collective-permute-start | bytes 1216520 | tf_op jit(solution)/shard_map/ppermute | solution.py:57
  30.8 7.5 %collective-permute-start.11 = (bf16[128,1024]{1,0:T(8,128)(2,1)S(1)}, bf16[128,1024]{1,0:T(8,128)(2,1)S(1)}, u32[]{:S(2)}, u32[]{:S(2)}) collective-permute-start(bf16[128,1024]{1,0:T(8,128)(2,1)S(1)} %get-tuple-element.52), channel_id=1, source_target_pairs={{0,2},{1,3},{2,0},{3,1},{4,6},{5,7},{6,4},{7,5},{8,10},{9,11},{10,... | collective-permute-start | bytes 786440 | tf_op jit(solution)/shard_map/ppermute | solution.py:57
  31.3 7.2 %collective-permute-start.13 = (bf16[128,1024]{1,0:T(8,128)(2,1)S(1)}, bf16[128,1024]{1,0:T(8,128)(2,1)S(1)}, u32[]{:S(2)}, u32[]{:S(2)}) collective-permute-start(bf16[128,1024]{1,0:T(8,128)(2,1)S(1)} %get-tuple-element.57), channel_id=1, source_target_pairs={{0,1},{1,0},{2,3},{3,2},{4,5},{5,4},{6,7},{7,6},{8,9},{9,8},{10,11... | collective-permute-start | bytes 786440 | tf_op jit(solution)/shard_map/ppermute | solution.py:57
  32.5 10.5 %collective-permute-start.16 = (bf16[512,384]{1,0:T(8,128)(2,1)S(1)}, bf16[512,384]{1,0:T(8,128)(2,1)S(1)}, u32[]{:S(2)}, u32[]{:S(2)}) collective-permute-start(bf16[512,384]{1,0:T(8,128)(2,1)S(1)} %constant_dynamic-update-slice_fusion.refs_5_.refs_3_), channel_id=1, source_target_pairs={{0,8},{1,9},{2,10},{3,11},{4,12},{5,13},{6,14},{7,15},{8,0},{9,1},... | collective-permute-start | bytes 1179656 | tf_op jit(solution)/shard_map/ppermute | solution.py:57
  43.7 8.2 %collective-permute-start.17 = (bf16[4,256,128]{2,1,0:T(8,128)(2,1)S(1)}, bf16[4,256,128]{2,1,0:T(8,128)(2,1)S(1)}, u32[]{:S(2)}, u32[]{:S(2)}) collective-permute-start(bf16[4,256,128]{2,1,0:T(8,128)(2,1)S(1)} %get-tuple-element.62.own), channel_id=1, source_target_pairs={{0,8},{1,9},{2,10},{3,11},{4,12},{5,13},{6,14},{7,15},{8,0},{9,1},... | collective-permute-start | bytes 786440 | tf_op jit(solution)/shard_map/ppermute | solution.py:57
  45.4 9.7 %collective-permute-start.18 = (bf16[4,256,128]{2,1,0:T(8,128)(2,1)S(1)}, bf16[4,256,128]{2,1,0:T(8,128)(2,1)S(1)}, u32[]{:S(2)}, u32[]{:S(2)}) collective-permute-start(bf16[4,256,128]{2,1,0:T(8,128)(2,1)S(1)} %get-tuple-element.62.own), channel_id=1, source_target_pairs={{8,16},{9,17},{10,18},{11,19},{12,20},{13,21},{14,22},{15,23},{16,... | collective-permute-start | bytes 786440 | tf_op jit(solution)/shard_map/ppermute | solution.py:57
  49.6 6.7 %collective-permute-start.21 = (bf16[3,256,128]{2,1,0:T(8,128)(2,1)S(1)}, bf16[3,256,128]{2,1,0:T(8,128)(2,1)S(1)}, u32[]{:S(2)}, u32[]{:S(2)}) collective-permute-start(bf16[3,256,128]{2,1,0:T(8,128)(2,1)S(1)} %get-tuple-element.64.own), channel_id=1, source_target_pairs={{0,8},{1,9},{2,10},{3,11},{4,12},{5,13},{6,14},{7,15},{8,0},{9,1},... | collective-permute-start | bytes 589832 | tf_op jit(solution)/shard_map/ppermute | solution.py:57
  49.7 9.4 %collective-permute-start.22 = (bf16[3,256,128]{2,1,0:T(8,128)(2,1)S(1)}, bf16[3,256,128]{2,1,0:T(8,128)(2,1)S(1)}, u32[]{:S(2)}, u32[]{:S(2)}) collective-permute-start(bf16[3,256,128]{2,1,0:T(8,128)(2,1)S(1)} %get-tuple-element.64.own), channel_id=1, source_target_pairs={{8,16},{9,17},{10,18},{11,19},{12,20},{13,21},{14,22},{15,23},{16,... | collective-permute-start | bytes 589832 | tf_op jit(solution)/shard_map/ppermute | solution.py:57
  51.6 11.6 %collective-permute-start.19 = (bf16[1,256,128]{2,1,0:T(8,128)(2,1)S(1)}, bf16[1,256,128]{2,1,0:T(8,128)(2,1)S(1)}, u32[]{:S(2)}, u32[]{:S(2)}) collective-permute-start(bf16[1,256,128]{2,1,0:T(8,128)(2,1)S(1)} %get-tuple-element.63.own), channel_id=1, source_target_pairs={{0,8},{1,9},{2,10},{3,11},{4,12},{5,13},{6,14},{7,15},{8,0},{9,1},... | collective-permute-start | bytes 196616 | tf_op jit(solution)/shard_map/ppermute | solution.py:57
  51.9 11.3 %collective-permute-start.20 = (bf16[1,256,128]{2,1,0:T(8,128)(2,1)S(1)}, bf16[1,256,128]{2,1,0:T(8,128)(2,1)S(1)}, u32[]{:S(2)}, u32[]{:S(2)}) collective-permute-start(bf16[1,256,128]{2,1,0:T(8,128)(2,1)S(1)} %get-tuple-element.63.own), channel_id=1, source_target_pairs={{8,16},{9,17},{10,18},{11,19},{12,20},{13,21},{14,22},{15,23},{16,... | collective-permute-start | bytes 196616 | tf_op jit(solution)/shard_map/ppermute | solution.py:57
  59.4 4.1 %collective-permute-start.25 = (bf16[256,128]{1,0:T(8,128)(2,1)S(1)}, bf16[256,128]{1,0:T(8,128)(2,1)S(1)}, u32[]{:S(2)}, u32[]{:S(2)}) collective-permute-start(bf16[256,128]{1,0:T(8,128)(2,1)S(1)} %shard_map.77), channel_id=1, source_target_pairs={{0,3},{1,2},{2,1},{3,0},{4,7},{5,6},{6,5},{7,4},{8,11},{9,10},{10,... | collective-permute-start | bytes 196616 | tf_op jit(solution)/shard_map/ppermute | solution.py:57
  61.6 3.2 %collective-permute-start.24 = (bf16[256,128]{1,0:T(8,128)(2,1)S(1)}, bf16[256,128]{1,0:T(8,128)(2,1)S(1)}, u32[]{:S(2)}, u32[]{:S(2)}) collective-permute-start(bf16[256,128]{1,0:T(8,128)(2,1)S(1)} %shard_map.76), channel_id=1, source_target_pairs={{0,2},{1,3},{2,0},{3,1},{4,6},{5,7},{6,4},{7,5},{8,10},{9,11},{10,... | collective-permute-start | bytes 196616 | tf_op jit(solution)/shard_map/ppermute | solution.py:57
  63.1 3.5 %collective-permute-start.23 = (bf16[256,128]{1,0:T(8,128)(2,1)S(1)}, bf16[256,128]{1,0:T(8,128)(2,1)S(1)}, u32[]{:S(2)}, u32[]{:S(2)}) collective-permute-start(bf16[256,128]{1,0:T(8,128)(2,1)S(1)} %shard_map.75), channel_id=1, source_target_pairs={{0,1},{1,0},{2,3},{3,2},{4,5},{5,4},{6,7},{7,6},{8,9},{9,8},{10,11... | collective-permute-start | bytes 196616 | tf_op jit(solution)/shard_map/ppermute | solution.py:57
  66.6 4.4 %collective-permute-start.26 = (bf16[4,128,128]{2,1,0:T(8,128)(2,1)S(1)}, bf16[4,128,128]{2,1,0:T(8,128)(2,1)S(1)}, u32[]{:S(2)}, u32[]{:S(2)}) collective-permute-start(bf16[4,128,128]{2,1,0:T(8,128)(2,1)S(1)} %get-tuple-element.66), channel_id=1, source_target_pairs={{0,4},{1,5},{2,6},{3,7},{4,0},{5,1},{6,2},{7,3},{8,12},{9,13},{10,... | collective-permute-start | bytes 393224 | tf_op jit(solution)/shard_map/ppermute | solution.py:57
  (9 other events, 37.1 us)

commit v13 on v12

--- a/solution.py
+++ b/solution.py
@@ -228,7 +228,7 @@
     return jnp.where(odd, outer, middle), own[index], jnp.where(odd, middle, outer)
 
 
-def weigh_kernel(q_ref, outer, own, middle, own_flags, received, out_ref):
+def weigh_kernel(q_ref, middle, own, outer, own_flags, received, out_ref):
     _, core, _ = where_am_i()
     block = q_ref.shape[1] // 2
     inv_root = 1.0 / math.sqrt(HD)
@@ -255,7 +255,7 @@
                 out_ref[r, u * block : (u + 1) * block, here] = (p * inverse).astype(jnp.bfloat16)
 
 
-def mix_kernel(r, weights, outer, own, middle, out_ref):
+def mix_kernel(r, weights, middle, own, outer, out_ref):
     block = weights.shape[1] // 2
     values = neighbours(outer, own, middle, V_ORDER.index(r) % 3)
     for u in range(2):
@@ -372,10 +372,15 @@
         finish_kernel, (one_head, one_head, array(3, 2 * block, HD), array(1, 2 * block, HD)), "v" * 6, macs=8 * block * rows * 3 * HD
     )(*early, diagonal, last, total, total_diagonal)
 
+    middle = swap_middle(k)
+    outer = swap_z(k, 1)
     weights = call(weigh_kernel, array(4, 2 * block, 5 * block), "v" * 6, macs=8 * block * 5 * block * HD)(
-        q, swap_z(k, 1), k, swap_middle(k), flags, received
-    )
-    values = [(swap_z(t, 1), t, swap_middle(t)) for t in v]
+        q, middle, k, outer, flags, received
+    )
+    values = []
+    for t in v:
+        middle = swap_middle(t)
+        values.append((middle, t, swap_z(t, 1)))
     pieces = {}
     for i, r in enumerate(V_ORDER):
         mixed = call(functools.partial(mix_kernel, r), array(2 * block, HD), "vvvv", macs=2 * block * 5 * block * HD)(

time: 72.3 us -> 72.4 us (level); the launches traced: 71.8 us -> 71.1 us
  starting transfers between devices: 35.9 us -> 34.3 us
  waiting for transfers between devices: 22.5 us -> 23.4 us
    ppermute x27, starting transfers between devices: 35.9 us -> 34.3 us  [hop(): return lax.ppermute(value, ('tm', 'depth'), pairs)]
    ppermute x27, waiting for transfers between devices: 22.5 us -> 23.4 us  [hop(): return lax.ppermute(value, ('tm', 'depth'), pairs)]
  transfers between devices with their start and end apart: 27 -> 27, of which waited for: 14 -> 17; matrix products, arithmetic and copies ran while one was open for 2% -> 2% of each run, Pallas kernels for 9% -> 9%
where the time goes in v13:
time: 72.4 us; the launch traced here: 71.1 us
  starting transfers between devices  34.3 us (47%)
  waiting for transfers between devices  23.4 us (32%)
  Pallas kernels  8.34 us (12%)
  local copies, waits for them, and re-layouts  3.26 us (5%)
  other arithmetic  1.52 us (2%)
    ppermute x27, starting transfers between devices, hop(): return lax.ppermute(value, ('tm', 'depth'), pairs)  34.3 us
    ppermute x27, waiting for transfers between devices, hop(): return lax.ppermute(value, ('tm', 'depth'), pairs)  23.4 us
    unnamed x13, local copies, waits for them, and re-layouts  3.13 us
    pallas_call x3, Pallas kernels, embed(): call(functools.partial(embed_kernel, rs, len(finished)), out, 'v' * (6 +...  2.38 us
  transfers between devices with their start and end apart: 27, of which 17 were waited for; matrix products, arithmetic and copies ran while one was open for 2% of the time, Pallas kernels for 9%

profile of v13, /device:TPU:9, one launch (start us, length us, event | category | flops | bytes accessed | tf_op | source)
XLA Modules:
  0.0 71.1 jit_solution(18196426846667082257)
XLA Ops:
  0.0 2.3 %collective-permute-start = (bf16[256,768]{1,0:T(8,128)(2,1)}, bf16[256,768]{1,0:T(8,128)(2,1)S(1)}, u32[]{:S(2)}, u32[]{:S(2)}) collective-permute-start(bf16[256,768]{1,0:T(8,128)(2,1)} %w.1), channel_id=1, source_target_pairs={{0,16},{1,17},{2,18},{3,19},{4,20},{5,21},{6,22},{7,23},{8,24},{9,... | collective-permute-start | bytes 1179656 | tf_op jit(solution)/shard_map/ppermute | solution.py:57
  4.8 2.2 %collective-permute-start.3 = (bf16[128,256]{1,0:T(8,128)(2,1)S(1)}, bf16[128,256]{1,0:T(8,128)(2,1)S(1)}, u32[]{:S(2)}, u32[]{:S(2)}) collective-permute-start(bf16[128,256]{1,0:T(8,128)(2,1)S(1)} %get-tuple-element.38), channel_id=1, source_target_pairs={{0,3},{1,2},{2,1},{3,0},{4,7},{5,6},{6,5},{7,4},{8,11},{9,10},{10,... | collective-permute-start | bytes 196616 | tf_op jit(solution)/shard_map/ppermute | solution.py:57
  7.5 1.7 %collective-permute-done.3.across = bf16[128,256]{1,0:T(8,128)(2,1)S(1)} collective-permute-done((bf16[128,256]{1,0:T(8,128)(2,1)S(1)}, bf16[128,256]{1,0:T(8,128)(2,1)S(1)}, u32[]{:S(2)}, u32[]{:S(2)}) %collective-permute-start.3) | collective-permute-done | bytes 65568 | tf_op jit(solution)/shard_map/ppermute | solution.py:57
  9.2 1.2 %collective-permute-start.7 = (bf16[128,2048]{1,0:T(8,128)(2,1)}, bf16[128,2048]{1,0:T(8,128)(2,1)S(1)}, u32[]{:S(2)}, u32[]{:S(2)}) collective-permute-start(bf16[128,2048]{1,0:T(8,128)(2,1)} %bitcast.12), channel_id=1, source_target_pairs={{0,2},{1,3},{2,0},{3,1},{4,6},{5,7},{6,4},{7,5},{8,10},{9,11},{10,... | collective-permute-start | bytes 1572872 | tf_op jit(solution)/shard_map/ppermute | solution.py:57
  11.6 1.4 %collective-permute-done.1.plane_x.from_x = bf16[336,256]{1,0:T(8,128)(2,1)S(1)} collective-permute-done((bf16[336,256]{1,0:T(8,128)(2,1)S(1)}, bf16[336,256]{1,0:T(8,128)(2,1)S(1)}, u32[]{:S(2)}, u32[]{:S(2)}) %collective-permute-start.1) | collective-permute-done | bytes 172064 | tf_op jit(solution)/shard_map/ppermute | solution.py:57
  13.4 1.4 %copy-done = bf16[3,128,2048]{2,1,0:T(8,128)(2,1)S(1)} copy-done((bf16[3,128,2048]{2,1,0:T(8,128)(2,1)S(1)}, bf16[3,128,2048]{2,1,0:T(8,128)(2,1)}, u32[]{:S(2)}) %copy-start) | copy-done | bytes 1572888
  16.1 3.7 %collective-permute-done = bf16[256,768]{1,0:T(8,128)(2,1)S(1)} collective-permute-done((bf16[256,768]{1,0:T(8,128)(2,1)}, bf16[256,768]{1,0:T(8,128)(2,1)S(1)}, u32[]{:S(2)}, u32[]{:S(2)}) %collective-permute-start) | collective-permute-done | bytes 393248 | tf_op jit(solution)/shard_map/ppermute | solution.py:57
  19.9 1.3 %collective-permute-start.4 = (bf16[256,256]{1,0:T(8,128)(2,1)S(1)}, bf16[256,256]{1,0:T(8,128)(2,1)S(1)}, u32[]{:S(2)}, u32[]{:S(2)}) collective-permute-start(bf16[256,256]{1,0:T(8,128)(2,1)S(1)} %get-tuple-element.68), channel_id=1, source_target_pairs={{0,1},{1,0},{2,3},{3,2},{4,5},{5,4},{6,7},{7,6},{8,9},{9,8},{10,11... | collective-permute-start | bytes 393224 | tf_op jit(solution)/shard_map/ppermute | solution.py:57
  22.4 1.8 %collective-permute-done.7.refs_1_ = bf16[128,2048]{1,0:T(8,128)(2,1)S(1)} collective-permute-done((bf16[128,2048]{1,0:T(8,128)(2,1)}, bf16[128,2048]{1,0:T(8,128)(2,1)S(1)}, u32[]{:S(2)}, u32[]{:S(2)}) %collective-permute-start.7) | collective-permute-done | bytes 524320 | tf_op jit(solution)/shard_map/ppermute | solution.py:57
  25.6 1.3 %collective-permute-done.5.from_y = bf16[256,256]{1,0:T(8,128)(2,1)S(1)} collective-permute-done((bf16[256,256]{1,0:T(8,128)(2,1)S(1)}, bf16[256,256]{1,0:T(8,128)(2,1)S(1)}, u32[]{:S(2)}, u32[]{:S(2)}) %collective-permute-start.5) | collective-permute-done | bytes 131104 | tf_op jit(solution)/shard_map/ppermute | solution.py:57
  27.1 1.9 %collective-permute-start.9 = (bf16[256,384]{1,0:T(8,128)(2,1)S(1)}, bf16[256,384]{1,0:T(8,128)(2,1)S(1)}, u32[]{:S(2)}, u32[]{:S(2)}) collective-permute-start(bf16[256,384]{1,0:T(8,128)(2,1)S(1)} %get-tuple-element.48), channel_id=1, source_target_pairs={{0,4},{1,5},{2,6},{3,7},{4,0},{5,1},{6,2},{7,3},{8,12},{9,13},{10,... | collective-permute-start | bytes 589832 | tf_op jit(solution)/shard_map/ppermute | solution.py:57
  32.5 1.7 %collective-permute-start.16 = (bf16[512,384]{1,0:T(8,128)(2,1)S(1)}, bf16[512,384]{1,0:T(8,128)(2,1)S(1)}, u32[]{:S(2)}, u32[]{:S(2)}) collective-permute-start(bf16[512,384]{1,0:T(8,128)(2,1)S(1)} %constant_dynamic-update-slice_fusion.refs_5_.refs_3_), channel_id=1, source_target_pairs={{0,8},{1,9},{2,10},{3,11},{4,12},{5,13},{6,14},{7,15},{8,0},{9,1},... | collective-permute-start | bytes 1179656 | tf_op jit(solution)/shard_map/ppermute | solution.py:57
  34.2 1.4 %shard_map.69.refs_4_ = f32[768,384]{1,0:T(8,128)S(1)} custom-call(bf16[384,2048]{1,0:T(8,128)(2,1)S(1)} %get-tuple-element.51.refs_0_, bf16[384,2048]{1,0:T(8,128)(2,1)S(1)} %collective-permute-done.10.refs_1_, bf16[256,768]{1,0:T(8,128)(2,1)S(1)} %shard_map.67.refs_2_.refs_0_, bf16[256,768]{1,0:T(8,128)(2,1)S(1)} %collective-permute-done.8.refs_3_.refs_1_, ...), custom_call_target="tpu_custom_call" | custom-call | flops 905969664 | tf_op jit(solution)/shard_map/pallas_call | solution.py:359
  35.5 2.8 %collective-permute-done.11 = bf16[128,1024]{1,0:T(8,128)(2,1)S(1)} collective-permute-done((bf16[128,1024]{1,0:T(8,128)(2,1)S(1)}, bf16[128,1024]{1,0:T(8,128)(2,1)S(1)}, u32[]{:S(2)}, u32[]{:S(2)}) %collective-permute-start.11) | collective-permute-done | bytes 262176 | tf_op jit(solution)/shard_map/ppermute | solution.py:57
  39.2 1.6 %collective-permute-start.14 = (bf16[80,2048]{1,0:T(8,128)(2,1)S(1)}, bf16[80,2048]{1,0:T(8,128)(2,1)S(1)}, u32[]{:S(2)}, u32[]{:S(2)}) collective-permute-start(bf16[80,2048]{1,0:T(8,128)(2,1)S(1)} %slice.29), channel_id=1, source_target_pairs={{0,4},{1,5},{2,6},{3,7},{4,0},{5,1},{6,2},{7,3},{8,12},{9,13},{10,... | collective-permute-start | bytes 983048 | tf_op jit(solution)/shard_map/ppermute | solution.py:57
  40.9 1.4 %collective-permute-done.15.bottom = bf16[48,2048]{1,0:T(8,128)(2,1)S(1)} collective-permute-done((bf16[48,2048]{1,0:T(8,128)(2,1)S(1)}, bf16[48,2048]{1,0:T(8,128)(2,1)S(1)}, u32[]{:S(2)}, u32[]{:S(2)}) %collective-permute-start.15) | collective-permute-done | bytes 196640 | tf_op jit(solution)/shard_map/ppermute | solution.py:57
  43.7 4.0 %collective-permute-start.17 = (bf16[4,256,128]{2,1,0:T(8,128)(2,1)S(1)}, bf16[4,256,128]{2,1,0:T(8,128)(2,1)S(1)}, u32[]{:S(2)}, u32[]{:S(2)}) collective-permute-start(bf16[4,256,128]{2,1,0:T(8,128)(2,1)S(1)} %get-tuple-element.62.own), channel_id=1, source_target_pairs={{8,16},{9,17},{10,18},{11,19},{12,20},{13,21},{14,22},{15,23},{16,... | collective-permute-start | bytes 786440 | tf_op jit(solution)/shard_map/ppermute | solution.py:57
  47.7 2.6 %collective-permute-start.21 = (bf16[3,256,128]{2,1,0:T(8,128)(2,1)S(1)}, bf16[3,256,128]{2,1,0:T(8,128)(2,1)S(1)}, u32[]{:S(2)}, u32[]{:S(2)}) collective-permute-start(bf16[3,256,128]{2,1,0:T(8,128)(2,1)S(1)} %get-tuple-element.64.own), channel_id=1, source_target_pairs={{8,16},{9,17},{10,18},{11,19},{12,20},{13,21},{14,22},{15,23},{16,... | collective-permute-start | bytes 589832 | tf_op jit(solution)/shard_map/ppermute | solution.py:57
  50.4 2.7 %collective-permute-start.19 = (bf16[1,256,128]{2,1,0:T(8,128)(2,1)S(1)}, bf16[1,256,128]{2,1,0:T(8,128)(2,1)S(1)}, u32[]{:S(2)}, u32[]{:S(2)}) collective-permute-start(bf16[1,256,128]{2,1,0:T(8,128)(2,1)S(1)} %get-tuple-element.63.own), channel_id=1, source_target_pairs={{8,16},{9,17},{10,18},{11,19},{12,20},{13,21},{14,22},{15,23},{16,... | collective-permute-start | bytes 196616 | tf_op jit(solution)/shard_map/ppermute | solution.py:57
  54.9 2.0 %collective-permute-done.21.middle = bf16[3,256,128]{2,1,0:T(8,128)(2,1)S(1)} collective-permute-done((bf16[3,256,128]{2,1,0:T(8,128)(2,1)S(1)}, bf16[3,256,128]{2,1,0:T(8,128)(2,1)S(1)}, u32[]{:S(2)}, u32[]{:S(2)}) %collective-permute-start.21) | collective-permute-done | bytes 196640 | tf_op jit(solution)/shard_map/ppermute | solution.py:57
  58.2 1.6 %collective-permute-start.25 = (bf16[256,128]{1,0:T(8,128)(2,1)S(1)}, bf16[256,128]{1,0:T(8,128)(2,1)S(1)}, u32[]{:S(2)}, u32[]{:S(2)}) collective-permute-start(bf16[256,128]{1,0:T(8,128)(2,1)S(1)} %shard_map.77), channel_id=1, source_target_pairs={{0,3},{1,2},{2,1},{3,0},{4,7},{5,6},{6,5},{7,4},{8,11},{9,10},{10,... | collective-permute-start | bytes 196616 | tf_op jit(solution)/shard_map/ppermute | solution.py:57
  60.1 1.3 %collective-permute-start.24 = (bf16[256,128]{1,0:T(8,128)(2,1)S(1)}, bf16[256,128]{1,0:T(8,128)(2,1)S(1)}, u32[]{:S(2)}, u32[]{:S(2)}) collective-permute-start(bf16[256,128]{1,0:T(8,128)(2,1)S(1)} %shard_map.76), channel_id=1, source_target_pairs={{0,2},{1,3},{2,0},{3,1},{4,6},{5,7},{6,4},{7,5},{8,10},{9,11},{10,... | collective-permute-start | bytes 196616 | tf_op jit(solution)/shard_map/ppermute | solution.py:57
  63.2 2.0 %collective-permute-done.23.refs_1_ = bf16[256,128]{1,0:T(8,128)(2,1)S(1)} collective-permute-done((bf16[256,128]{1,0:T(8,128)(2,1)S(1)}, bf16[256,128]{1,0:T(8,128)(2,1)S(1)}, u32[]{:S(2)}, u32[]{:S(2)}) %collective-permute-start.23) | collective-permute-done | bytes 65568 | tf_op jit(solution)/shard_map/ppermute | solution.py:57
  65.2 4.1 %collective-permute-start.26 = (bf16[4,128,128]{2,1,0:T(8,128)(2,1)S(1)}, bf16[4,128,128]{2,1,0:T(8,128)(2,1)S(1)}, u32[]{:S(2)}, u32[]{:S(2)}) collective-permute-start(bf16[4,128,128]{2,1,0:T(8,128)(2,1)S(1)} %get-tuple-element.66), channel_id=1, source_target_pairs={{0,4},{1,5},{2,6},{3,7},{4,0},{5,1},{6,2},{7,3},{8,12},{9,13},{10,... | collective-permute-start | bytes 393224 | tf_op jit(solution)/shard_map/ppermute | solution.py:57
  (71 shorter events, 21.5 us)
Async XLA Ops:
  0.0 19.8 %collective-permute-start = (bf16[256,768]{1,0:T(8,128)(2,1)}, bf16[256,768]{1,0:T(8,128)(2,1)S(1)}, u32[]{:S(2)}, u32[]{:S(2)}) collective-permute-start(bf16[256,768]{1,0:T(8,128)(2,1)} %w.1), channel_id=1, source_target_pairs={{0,16},{1,17},{2,18},{3,19},{4,20},{5,21},{6,22},{7,23},{8,24},{9,... | collective-permute-start | bytes 1179656 | tf_op jit(solution)/shard_map/ppermute | solution.py:57
  4.8 4.4 %collective-permute-start.3 = (bf16[128,256]{1,0:T(8,128)(2,1)S(1)}, bf16[128,256]{1,0:T(8,128)(2,1)S(1)}, u32[]{:S(2)}, u32[]{:S(2)}) collective-permute-start(bf16[128,256]{1,0:T(8,128)(2,1)S(1)} %get-tuple-element.38), channel_id=1, source_target_pairs={{0,3},{1,2},{2,1},{3,0},{4,7},{5,6},{6,5},{7,4},{8,11},{9,10},{10,... | collective-permute-start | bytes 196616 | tf_op jit(solution)/shard_map/ppermute | solution.py:57
  7.0 6.0 %collective-permute-start.1 = (bf16[336,256]{1,0:T(8,128)(2,1)S(1)}, bf16[336,256]{1,0:T(8,128)(2,1)S(1)}, u32[]{:S(2)}, u32[]{:S(2)}) collective-permute-start(bf16[336,256]{1,0:T(8,128)(2,1)S(1)} %get-tuple-element.36), channel_id=1, source_target_pairs={{0,1},{1,0},{2,3},{3,2},{4,5},{5,4},{6,7},{7,6},{8,9},{9,8},{10,11... | collective-permute-start | bytes 516104 | tf_op jit(solution)/shard_map/ppermute | solution.py:57
  7.3 5.8 %collective-permute-start.2 = (bf16[336,256]{1,0:T(8,128)(2,1)S(1)}, bf16[336,256]{1,0:T(8,128)(2,1)S(1)}, u32[]{:S(2)}, u32[]{:S(2)}) collective-permute-start(bf16[336,256]{1,0:T(8,128)(2,1)S(1)} %get-tuple-element.37), channel_id=1, source_target_pairs={{0,2},{1,3},{2,0},{3,1},{4,6},{5,7},{6,4},{7,5},{8,10},{9,11},{10,... | collective-permute-start | bytes 516104 | tf_op jit(solution)/shard_map/ppermute | solution.py:57
  9.2 15.0 %collective-permute-start.7 = (bf16[128,2048]{1,0:T(8,128)(2,1)}, bf16[128,2048]{1,0:T(8,128)(2,1)S(1)}, u32[]{:S(2)}, u32[]{:S(2)}) collective-permute-start(bf16[128,2048]{1,0:T(8,128)(2,1)} %bitcast.12), channel_id=1, source_target_pairs={{0,2},{1,3},{2,0},{3,1},{4,6},{5,7},{6,4},{7,5},{8,10},{9,11},{10,... | collective-permute-start | bytes 1572872 | tf_op jit(solution)/shard_map/ppermute | solution.py:57
  10.4 13.8 %collective-permute-start.6 = (bf16[128,2048]{1,0:T(8,128)(2,1)}, bf16[128,2048]{1,0:T(8,128)(2,1)S(1)}, u32[]{:S(2)}, u32[]{:S(2)}) collective-permute-start(bf16[128,2048]{1,0:T(8,128)(2,1)} %bitcast.13), channel_id=1, source_target_pairs={{0,1},{1,0},{2,3},{3,2},{4,5},{5,4},{6,7},{7,6},{8,9},{9,8},{10,11... | collective-permute-start | bytes 1572872 | tf_op jit(solution)/shard_map/ppermute | solution.py:57
  13.2 13.8 %collective-permute-start.8 = (bf16[256,768]{1,0:T(8,128)(2,1)S(1)}, bf16[256,768]{1,0:T(8,128)(2,1)S(1)}, u32[]{:S(2)}, u32[]{:S(2)}) collective-permute-start(bf16[256,768]{1,0:T(8,128)(2,1)S(1)} %shard_map.67.refs_2_.refs_0_), channel_id=1, source_target_pairs={{0,8},{1,9},{2,10},{3,11},{4,12},{5,13},{6,14},{7,15},{8,0},{9,1},... | collective-permute-start | bytes 1179656 | tf_op jit(solution)/shard_map/ppermute | solution.py:57
  19.9 5.8 %collective-permute-start.4 = (bf16[256,256]{1,0:T(8,128)(2,1)S(1)}, bf16[256,256]{1,0:T(8,128)(2,1)S(1)}, u32[]{:S(2)}, u32[]{:S(2)}) collective-permute-start(bf16[256,256]{1,0:T(8,128)(2,1)S(1)} %get-tuple-element.68), channel_id=1, source_target_pairs={{0,1},{1,0},{2,3},{3,2},{4,5},{5,4},{6,7},{7,6},{8,9},{9,8},{10,11... | collective-permute-start | bytes 393224 | tf_op jit(solution)/shard_map/ppermute | solution.py:57
  21.1 5.8 %collective-permute-start.5 = (bf16[256,256]{1,0:T(8,128)(2,1)S(1)}, bf16[256,256]{1,0:T(8,128)(2,1)S(1)}, u32[]{:S(2)}, u32[]{:S(2)}) collective-permute-start(bf16[256,256]{1,0:T(8,128)(2,1)S(1)} %get-tuple-element.67), channel_id=1, source_target_pairs={{0,2},{1,3},{2,0},{3,1},{4,6},{5,7},{6,4},{7,5},{8,10},{9,11},{10,... | collective-permute-start | bytes 393224 | tf_op jit(solution)/shard_map/ppermute | solution.py:57
  30.1 4.1 %collective-permute-start.10 = (bf16[384,2048]{1,0:T(8,128)(2,1)S(1)}, bf16[384,2048]{1,0:T(8,128)(2,1)S(1)}, u32[]{:S(2)}, u32[]{:S(2)}) collective-permute-start(bf16[384,2048]{1,0:T(8,128)(2,1)S(1)} %get-tuple-element.51.refs_0_), channel_id=1, source_target_pairs={{0,4},{1,5},{2,6},{3,7},{4,0},{5,1},{6,2},{7,3},{8,12},{9,13},{10,... | collective-permute-start | bytes 4718600 | tf_op jit(solution)/shard_map/ppermute | solution.py:57
  30.6 3.6 %collective-permute-start.12 = (bf16[528,384]{1,0:T(8,128)(2,1)S(1)}, bf16[528,384]{1,0:T(8,128)(2,1)S(1)}, u32[]{:S(2)}, u32[]{:S(2)}) collective-permute-start(bf16[528,384]{1,0:T(8,128)(2,1)S(1)} %pad_maximum_fusion.1), channel_id=1, source_target_pairs={{0,4},{1,5},{2,6},{3,7},{4,0},{5,1},{6,2},{7,3},{8,12},{9,13},{10,... | collective-permute-start | bytes 1216520 | tf_op jit(solution)/shard_map/ppermute | solution.py:57
  30.8 7.5 %collective-permute-start.11 = (bf16[128,1024]{1,0:T(8,128)(2,1)S(1)}, bf16[128,1024]{1,0:T(8,128)(2,1)S(1)}, u32[]{:S(2)}, u32[]{:S(2)}) collective-permute-start(bf16[128,1024]{1,0:T(8,128)(2,1)S(1)} %get-tuple-element.52), channel_id=1, source_target_pairs={{0,2},{1,3},{2,0},{3,1},{4,6},{5,7},{6,4},{7,5},{8,10},{9,11},{10,... | collective-permute-start | bytes 786440 | tf_op jit(solution)/shard_map/ppermute | solution.py:57
  31.3 7.2 %collective-permute-start.13 = (bf16[128,1024]{1,0:T(8,128)(2,1)S(1)}, bf16[128,1024]{1,0:T(8,128)(2,1)S(1)}, u32[]{:S(2)}, u32[]{:S(2)}) collective-permute-start(bf16[128,1024]{1,0:T(8,128)(2,1)S(1)} %get-tuple-element.57), channel_id=1, source_target_pairs={{0,1},{1,0},{2,3},{3,2},{4,5},{5,4},{6,7},{7,6},{8,9},{9,8},{10,11... | collective-permute-start | bytes 786440 | tf_op jit(solution)/shard_map/ppermute | solution.py:57
  32.5 10.5 %collective-permute-start.16 = (bf16[512,384]{1,0:T(8,128)(2,1)S(1)}, bf16[512,384]{1,0:T(8,128)(2,1)S(1)}, u32[]{:S(2)}, u32[]{:S(2)}) collective-permute-start(bf16[512,384]{1,0:T(8,128)(2,1)S(1)} %constant_dynamic-update-slice_fusion.refs_5_.refs_3_), channel_id=1, source_target_pairs={{0,8},{1,9},{2,10},{3,11},{4,12},{5,13},{6,14},{7,15},{8,0},{9,1},... | collective-permute-start | bytes 1179656 | tf_op jit(solution)/shard_map/ppermute | solution.py:57
  43.7 9.4 %collective-permute-start.17 = (bf16[4,256,128]{2,1,0:T(8,128)(2,1)S(1)}, bf16[4,256,128]{2,1,0:T(8,128)(2,1)S(1)}, u32[]{:S(2)}, u32[]{:S(2)}) collective-permute-start(bf16[4,256,128]{2,1,0:T(8,128)(2,1)S(1)} %get-tuple-element.62.own), channel_id=1, source_target_pairs={{8,16},{9,17},{10,18},{11,19},{12,20},{13,21},{14,22},{15,23},{16,... | collective-permute-start | bytes 786440 | tf_op jit(solution)/shard_map/ppermute | solution.py:57
  47.6 6.1 %collective-permute-start.18 = (bf16[4,256,128]{2,1,0:T(8,128)(2,1)S(1)}, bf16[4,256,128]{2,1,0:T(8,128)(2,1)S(1)}, u32[]{:S(2)}, u32[]{:S(2)}) collective-permute-start(bf16[4,256,128]{2,1,0:T(8,128)(2,1)S(1)} %get-tuple-element.62.own), channel_id=1, source_target_pairs={{0,8},{1,9},{2,10},{3,11},{4,12},{5,13},{6,14},{7,15},{8,0},{9,1},... | collective-permute-start | bytes 786440 | tf_op jit(solution)/shard_map/ppermute | solution.py:57
  47.7 9.2 %collective-permute-start.21 = (bf16[3,256,128]{2,1,0:T(8,128)(2,1)S(1)}, bf16[3,256,128]{2,1,0:T(8,128)(2,1)S(1)}, u32[]{:S(2)}, u32[]{:S(2)}) collective-permute-start(bf16[3,256,128]{2,1,0:T(8,128)(2,1)S(1)} %get-tuple-element.64.own), channel_id=1, source_target_pairs={{8,16},{9,17},{10,18},{11,19},{12,20},{13,21},{14,22},{15,23},{16,... | collective-permute-start | bytes 589832 | tf_op jit(solution)/shard_map/ppermute | solution.py:57
  50.3 7.6 %collective-permute-start.22 = (bf16[3,256,128]{2,1,0:T(8,128)(2,1)S(1)}, bf16[3,256,128]{2,1,0:T(8,128)(2,1)S(1)}, u32[]{:S(2)}, u32[]{:S(2)}) collective-permute-start(bf16[3,256,128]{2,1,0:T(8,128)(2,1)S(1)} %get-tuple-element.64.own), channel_id=1, source_target_pairs={{0,8},{1,9},{2,10},{3,11},{4,12},{5,13},{6,14},{7,15},{8,0},{9,1},... | collective-permute-start | bytes 589832 | tf_op jit(solution)/shard_map/ppermute | solution.py:57
  50.4 11.3 %collective-permute-start.19 = (bf16[1,256,128]{2,1,0:T(8,128)(2,1)S(1)}, bf16[1,256,128]{2,1,0:T(8,128)(2,1)S(1)}, u32[]{:S(2)}, u32[]{:S(2)}) collective-permute-start(bf16[1,256,128]{2,1,0:T(8,128)(2,1)S(1)} %get-tuple-element.63.own), channel_id=1, source_target_pairs={{8,16},{9,17},{10,18},{11,19},{12,20},{13,21},{14,22},{15,23},{16,... | collective-permute-start | bytes 196616 | tf_op jit(solution)/shard_map/ppermute | solution.py:57
  53.1 8.6 %collective-permute-start.20 = (bf16[1,256,128]{2,1,0:T(8,128)(2,1)S(1)}, bf16[1,256,128]{2,1,0:T(8,128)(2,1)S(1)}, u32[]{:S(2)}, u32[]{:S(2)}) collective-permute-start(bf16[1,256,128]{2,1,0:T(8,128)(2,1)S(1)} %get-tuple-element.63.own), channel_id=1, source_target_pairs={{0,8},{1,9},{2,10},{3,11},{4,12},{5,13},{6,14},{7,15},{8,0},{9,1},... | collective-permute-start | bytes 196616 | tf_op jit(solution)/shard_map/ppermute | solution.py:57
  58.2 4.1 %collective-permute-start.25 = (bf16[256,128]{1,0:T(8,128)(2,1)S(1)}, bf16[256,128]{1,0:T(8,128)(2,1)S(1)}, u32[]{:S(2)}, u32[]{:S(2)}) collective-permute-start(bf16[256,128]{1,0:T(8,128)(2,1)S(1)} %shard_map.77), channel_id=1, source_target_pairs={{0,3},{1,2},{2,1},{3,0},{4,7},{5,6},{6,5},{7,4},{8,11},{9,10},{10,... | collective-permute-start | bytes 196616 | tf_op jit(solution)/shard_map/ppermute | solution.py:57
  60.1 3.2 %collective-permute-start.24 = (bf16[256,128]{1,0:T(8,128)(2,1)S(1)}, bf16[256,128]{1,0:T(8,128)(2,1)S(1)}, u32[]{:S(2)}, u32[]{:S(2)}) collective-permute-start(bf16[256,128]{1,0:T(8,128)(2,1)S(1)} %shard_map.76), channel_id=1, source_target_pairs={{0,2},{1,3},{2,0},{3,1},{4,6},{5,7},{6,4},{7,5},{8,10},{9,11},{10,... | collective-permute-start | bytes 196616 | tf_op jit(solution)/shard_map/ppermute | solution.py:57
  61.6 3.6 %collective-permute-start.23 = (bf16[256,128]{1,0:T(8,128)(2,1)S(1)}, bf16[256,128]{1,0:T(8,128)(2,1)S(1)}, u32[]{:S(2)}, u32[]{:S(2)}) collective-permute-start(bf16[256,128]{1,0:T(8,128)(2,1)S(1)} %shard_map.75), channel_id=1, source_target_pairs={{0,1},{1,0},{2,3},{3,2},{4,5},{5,4},{6,7},{7,6},{8,9},{9,8},{10,11... | collective-permute-start | bytes 196616 | tf_op jit(solution)/shard_map/ppermute | solution.py:57
  65.2 5.1 %collective-permute-start.26 = (bf16[4,128,128]{2,1,0:T(8,128)(2,1)S(1)}, bf16[4,128,128]{2,1,0:T(8,128)(2,1)S(1)}, u32[]{:S(2)}, u32[]{:S(2)}) collective-permute-start(bf16[4,128,128]{2,1,0:T(8,128)(2,1)S(1)} %get-tuple-element.66), channel_id=1, source_target_pairs={{0,4},{1,5},{2,6},{3,7},{4,0},{5,1},{6,2},{7,3},{8,12},{9,13},{10,... | collective-permute-start | bytes 393224 | tf_op jit(solution)/shard_map/ppermute | solution.py:57
  (9 other events, 37.1 us)

commit v14 on v13

--- a/solution.py
+++ b/solution.py
@@ -200,7 +200,7 @@
 
 
 def finish_kernel(*refs):
-    x_refs, (last, acc_in, acc_diagonal, q_ref, k_ref, v_first, v_second) = refs[:3], refs[3:]
+    x_refs, (last, acc_in, acc_diagonal, q_ref, k_ref, v_ref) = refs[:3], refs[3:]
     z, core, _ = where_am_i()
     block, early = q_ref.shape[1] // 2, acc_in.shape[0]
     value = jnp.dot(take(x_refs, z ^ 3, core, last.shape[0]), last[...], preferred_element_type=jnp.float32)
@@ -211,10 +211,8 @@
         for r in range(4):
             row = ROW_ORDER[rel][r]
             mine = value[row * block : (row + 1) * block]
-            v_at = V_ORDER.index(r)
-            q_ref[r, at, :] = mine[:, :HD]
-            k_ref[r, at, :] = mine[:, HD:PAIR]
-            (v_first, v_second)[v_at // 3][v_at % 3, at, :] = mine[:, PAIR:]
+            for third, ref in enumerate((q_ref, k_ref, v_ref)):
+                ref[r, at, :] = mine[:, third * HD : (third + 1) * HD]
 
 
 def spans(u):
@@ -257,7 +255,7 @@
 
 def mix_kernel(r, weights, middle, own, outer, out_ref):
     block = weights.shape[1] // 2
-    values = neighbours(outer, own, middle, V_ORDER.index(r) % 3)
+    values = neighbours(outer, own, middle, r)
     for u in range(2):
         w = weights[r, u * block : (u + 1) * block]
         v = [values[side][first * block : last * block] for side, first, last in spans(u)]
@@ -368,8 +366,8 @@
         macs=2 * block * 3 * rows * 3 * HD,
     )(diagonal, *swapped, *weights)
     one_head = array(4, 2 * block, HD)
-    q, k, *v = call(
-        finish_kernel, (one_head, one_head, array(3, 2 * block, HD), array(1, 2 * block, HD)), "v" * 6, macs=8 * block * rows * 3 * HD
+    q, k, v = call(
+        finish_kernel, (one_head,) * 3, "v" * 6, macs=8 * block * rows * 3 * HD
     )(*early, diagonal, last, total, total_diagonal)
 
     middle = swap_middle(k)
@@ -377,14 +375,11 @@
     weights = call(weigh_kernel, array(4, 2 * block, 5 * block), "v" * 6, macs=8 * block * 5 * block * HD)(
         q, middle, k, outer, flags, received
     )
-    values = []
-    for t in v:
-        middle = swap_middle(t)
-        values.append((middle, t, swap_z(t, 1)))
+    values = (swap_middle(v), v, swap_z(v, 1))
     pieces = {}
-    for i, r in enumerate(V_ORDER):
+    for r in V_ORDER:
         mixed = call(functools.partial(mix_kernel, r), array(2 * block, HD), "vvvv", macs=2 * block * 5 * block * HD)(
-            weights, *values[i // 3]
+            weights, *values
         )
         pieces[r] = swap_depth(mixed, r) if r else mixed
     kept, sent = call(pack_kernel, (array(4, block, HD),) * 2, "vvvv")(*[pieces[r] for r in range(4)])

time: 72.4 us -> 73.1 us (level)
  waiting for transfers between devices: 23.4 us -> 27.9 us
  starting transfers between devices: 34.3 us -> 30.6 us
    ppermute x27 -> x25, waiting for transfers between devices: 23.4 us -> 27.9 us  [hop(): return lax.ppermute(value, ('tm', 'depth'), pairs)]
    ppermute x27 -> x25, starting transfers between devices: 34.3 us -> 30.6 us  [hop(): return lax.ppermute(value, ('tm', 'depth'), pairs)]
  transfers between devices with their start and end apart: 27 -> 25, of which waited for: 17 -> 18; matrix products, arithmetic and copies ran while one was open for 2% -> 2% of each run, Pallas kernels for 9% -> 9%
where the time goes in v14:
time: 73.1 us; the launch traced here: 71.8 us
  starting transfers between devices  30.6 us (42%)
  waiting for transfers between devices  27.9 us (38%)
  Pallas kernels  8.32 us (11%)
  local copies, waits for them, and re-layouts  3.26 us (4%)
  other arithmetic  1.52 us (2%)
    ppermute x25, starting transfers between devices, hop(): return lax.ppermute(value, ('tm', 'depth'), pairs)  30.6 us
    ppermute x25, waiting for transfers between devices, hop(): return lax.ppermute(value, ('tm', 'depth'), pairs)  27.9 us
    unnamed x13, local copies, waits for them, and re-layouts  3.13 us
    pallas_call x3, Pallas kernels, embed(): call(functools.partial(embed_kernel, rs, len(finished)), out, 'v' * (6 +...  2.38 us
  transfers between devices with their start and end apart: 25, of which 18 were waited for; matrix products, arithmetic and copies ran while one was open for 2% of the time, Pallas kernels for 9%

profile of v14, /device:TPU:9, one launch (start us, length us, event | category | flops | bytes accessed | tf_op | source)
XLA Modules:
  0.0 71.8 jit_solution(5447336322149269172)
XLA Ops:
  0.0 2.3 %collective-permute-start = (bf16[256,768]{1,0:T(8,128)(2,1)}, bf16[256,768]{1,0:T(8,128)(2,1)S(1)}, u32[]{:S(2)}, u32[]{:S(2)}) collective-permute-start(bf16[256,768]{1,0:T(8,128)(2,1)} %w.1), channel_id=1, source_target_pairs={{0,16},{1,17},{2,18},{3,19},{4,20},{5,21},{6,22},{7,23},{8,24},{9,... | collective-permute-start | bytes 1179656 | tf_op jit(solution)/shard_map/ppermute | solution.py:57
  4.8 2.2 %collective-permute-start.3 = (bf16[128,256]{1,0:T(8,128)(2,1)S(1)}, bf16[128,256]{1,0:T(8,128)(2,1)S(1)}, u32[]{:S(2)}, u32[]{:S(2)}) collective-permute-start(bf16[128,256]{1,0:T(8,128)(2,1)S(1)} %get-tuple-element.37), channel_id=1, source_target_pairs={{0,3},{1,2},{2,1},{3,0},{4,7},{5,6},{6,5},{7,4},{8,11},{9,10},{10,... | collective-permute-start | bytes 196616 | tf_op jit(solution)/shard_map/ppermute | solution.py:57
  7.5 1.7 %collective-permute-done.3.across = bf16[128,256]{1,0:T(8,128)(2,1)S(1)} collective-permute-done((bf16[128,256]{1,0:T(8,128)(2,1)S(1)}, bf16[128,256]{1,0:T(8,128)(2,1)S(1)}, u32[]{:S(2)}, u32[]{:S(2)}) %collective-permute-start.3) | collective-permute-done | bytes 65568 | tf_op jit(solution)/shard_map/ppermute | solution.py:57
  9.2 1.2 %collective-permute-start.7 = (bf16[128,2048]{1,0:T(8,128)(2,1)}, bf16[128,2048]{1,0:T(8,128)(2,1)S(1)}, u32[]{:S(2)}, u32[]{:S(2)}) collective-permute-start(bf16[128,2048]{1,0:T(8,128)(2,1)} %bitcast.12), channel_id=1, source_target_pairs={{0,2},{1,3},{2,0},{3,1},{4,6},{5,7},{6,4},{7,5},{8,10},{9,11},{10,... | collective-permute-start | bytes 1572872 | tf_op jit(solution)/shard_map/ppermute | solution.py:57
  11.6 1.4 %collective-permute-done.1.plane_x.from_x = bf16[336,256]{1,0:T(8,128)(2,1)S(1)} collective-permute-done((bf16[336,256]{1,0:T(8,128)(2,1)S(1)}, bf16[336,256]{1,0:T(8,128)(2,1)S(1)}, u32[]{:S(2)}, u32[]{:S(2)}) %collective-permute-start.1) | collective-permute-done | bytes 172064 | tf_op jit(solution)/shard_map/ppermute | solution.py:57
  13.4 1.4 %copy-done = bf16[3,128,2048]{2,1,0:T(8,128)(2,1)S(1)} copy-done((bf16[3,128,2048]{2,1,0:T(8,128)(2,1)S(1)}, bf16[3,128,2048]{2,1,0:T(8,128)(2,1)}, u32[]{:S(2)}) %copy-start) | copy-done | bytes 1572888
  16.1 3.7 %collective-permute-done = bf16[256,768]{1,0:T(8,128)(2,1)S(1)} collective-permute-done((bf16[256,768]{1,0:T(8,128)(2,1)}, bf16[256,768]{1,0:T(8,128)(2,1)S(1)}, u32[]{:S(2)}, u32[]{:S(2)}) %collective-permute-start) | collective-permute-done | bytes 393248 | tf_op jit(solution)/shard_map/ppermute | solution.py:57
  19.9 1.3 %collective-permute-start.4 = (bf16[256,256]{1,0:T(8,128)(2,1)S(1)}, bf16[256,256]{1,0:T(8,128)(2,1)S(1)}, u32[]{:S(2)}, u32[]{:S(2)}) collective-permute-start(bf16[256,256]{1,0:T(8,128)(2,1)S(1)} %get-tuple-element.66), channel_id=1, source_target_pairs={{0,1},{1,0},{2,3},{3,2},{4,5},{5,4},{6,7},{7,6},{8,9},{9,8},{10,11... | collective-permute-start | bytes 393224 | tf_op jit(solution)/shard_map/ppermute | solution.py:57
  22.4 1.8 %collective-permute-done.7.refs_1_ = bf16[128,2048]{1,0:T(8,128)(2,1)S(1)} collective-permute-done((bf16[128,2048]{1,0:T(8,128)(2,1)}, bf16[128,2048]{1,0:T(8,128)(2,1)S(1)}, u32[]{:S(2)}, u32[]{:S(2)}) %collective-permute-start.7) | collective-permute-done | bytes 524320 | tf_op jit(solution)/shard_map/ppermute | solution.py:57
  25.6 1.3 %collective-permute-done.5.from_y = bf16[256,256]{1,0:T(8,128)(2,1)S(1)} collective-permute-done((bf16[256,256]{1,0:T(8,128)(2,1)S(1)}, bf16[256,256]{1,0:T(8,128)(2,1)S(1)}, u32[]{:S(2)}, u32[]{:S(2)}) %collective-permute-start.5) | collective-permute-done | bytes 131104 | tf_op jit(solution)/shard_map/ppermute | solution.py:57
  27.1 1.9 %collective-permute-start.9 = (bf16[256,384]{1,0:T(8,128)(2,1)S(1)}, bf16[256,384]{1,0:T(8,128)(2,1)S(1)}, u32[]{:S(2)}, u32[]{:S(2)}) collective-permute-start(bf16[256,384]{1,0:T(8,128)(2,1)S(1)} %get-tuple-element.47), channel_id=1, source_target_pairs={{0,4},{1,5},{2,6},{3,7},{4,0},{5,1},{6,2},{7,3},{8,12},{9,13},{10,... | collective-permute-start | bytes 589832 | tf_op jit(solution)/shard_map/ppermute | solution.py:57
  32.5 1.7 %collective-permute-start.16 = (bf16[512,384]{1,0:T(8,128)(2,1)S(1)}, bf16[512,384]{1,0:T(8,128)(2,1)S(1)}, u32[]{:S(2)}, u32[]{:S(2)}) collective-permute-start(bf16[512,384]{1,0:T(8,128)(2,1)S(1)} %constant_dynamic-update-slice_fusion.refs_5_.refs_3_), channel_id=1, source_target_pairs={{0,8},{1,9},{2,10},{3,11},{4,12},{5,13},{6,14},{7,15},{8,0},{9,1},... | collective-permute-start | bytes 1179656 | tf_op jit(solution)/shard_map/ppermute | solution.py:57
  34.2 1.4 %shard_map.69.refs_4_ = f32[768,384]{1,0:T(8,128)S(1)} custom-call(bf16[384,2048]{1,0:T(8,128)(2,1)S(1)} %get-tuple-element.50.refs_0_, bf16[384,2048]{1,0:T(8,128)(2,1)S(1)} %collective-permute-done.10.refs_1_, bf16[256,768]{1,0:T(8,128)(2,1)S(1)} %shard_map.67.refs_2_.refs_0_, bf16[256,768]{1,0:T(8,128)(2,1)S(1)} %collective-permute-done.8.refs_3_.refs_1_, ...), custom_call_target="tpu_custom_call" | custom-call | flops 905969664 | tf_op jit(solution)/shard_map/pallas_call | solution.py:357
  35.5 2.8 %collective-permute-done.11 = bf16[128,1024]{1,0:T(8,128)(2,1)S(1)} collective-permute-done((bf16[128,1024]{1,0:T(8,128)(2,1)S(1)}, bf16[128,1024]{1,0:T(8,128)(2,1)S(1)}, u32[]{:S(2)}, u32[]{:S(2)}) %collective-permute-start.11) | collective-permute-done | bytes 262176 | tf_op jit(solution)/shard_map/ppermute | solution.py:57
  39.2 1.6 %collective-permute-start.14 = (bf16[80,2048]{1,0:T(8,128)(2,1)S(1)}, bf16[80,2048]{1,0:T(8,128)(2,1)S(1)}, u32[]{:S(2)}, u32[]{:S(2)}) collective-permute-start(bf16[80,2048]{1,0:T(8,128)(2,1)S(1)} %slice.29), channel_id=1, source_target_pairs={{0,4},{1,5},{2,6},{3,7},{4,0},{5,1},{6,2},{7,3},{8,12},{9,13},{10,... | collective-permute-start | bytes 983048 | tf_op jit(solution)/shard_map/ppermute | solution.py:57
  40.9 1.4 %collective-permute-done.15.bottom = bf16[48,2048]{1,0:T(8,128)(2,1)S(1)} collective-permute-done((bf16[48,2048]{1,0:T(8,128)(2,1)S(1)}, bf16[48,2048]{1,0:T(8,128)(2,1)S(1)}, u32[]{:S(2)}, u32[]{:S(2)}) %collective-permute-start.15) | collective-permute-done | bytes 196640 | tf_op jit(solution)/shard_map/ppermute | solution.py:57
  43.7 4.0 %collective-permute-start.17 = (bf16[4,256,128]{2,1,0:T(8,128)(2,1)S(1)}, bf16[4,256,128]{2,1,0:T(8,128)(2,1)S(1)}, u32[]{:S(2)}, u32[]{:S(2)}) collective-permute-start(bf16[4,256,128]{2,1,0:T(8,128)(2,1)S(1)} %get-tuple-element.61.own), channel_id=1, source_target_pairs={{8,16},{9,17},{10,18},{11,19},{12,20},{13,21},{14,22},{15,23},{16,... | collective-permute-start | bytes 786440 | tf_op jit(solution)/shard_map/ppermute | solution.py:57
  47.7 2.6 %collective-permute-start.19 = (bf16[4,256,128]{2,1,0:T(8,128)(2,1)S(1)}, bf16[4,256,128]{2,1,0:T(8,128)(2,1)S(1)}, u32[]{:S(2)}, u32[]{:S(2)}) collective-permute-start(bf16[4,256,128]{2,1,0:T(8,128)(2,1)S(1)} %get-tuple-element.62.own), channel_id=1, source_target_pairs={{8,16},{9,17},{10,18},{11,19},{12,20},{13,21},{14,22},{15,23},{16,... | collective-permute-start | bytes 786440 | tf_op jit(solution)/shard_map/ppermute | solution.py:57
  50.4 2.3 %collective-permute-done.17.middle = bf16[4,256,128]{2,1,0:T(8,128)(2,1)S(1)} collective-permute-done((bf16[4,256,128]{2,1,0:T(8,128)(2,1)S(1)}, bf16[4,256,128]{2,1,0:T(8,128)(2,1)S(1)}, u32[]{:S(2)}, u32[]{:S(2)}) %collective-permute-start.17) | collective-permute-done | bytes 262176 | tf_op jit(solution)/shard_map/ppermute | solution.py:57
  54.9 3.5 %collective-permute-done.19.middle = bf16[4,256,128]{2,1,0:T(8,128)(2,1)S(1)} collective-permute-done((bf16[4,256,128]{2,1,0:T(8,128)(2,1)S(1)}, bf16[4,256,128]{2,1,0:T(8,128)(2,1)S(1)}, u32[]{:S(2)}, u32[]{:S(2)}) %collective-permute-start.19) | collective-permute-done | bytes 262176 | tf_op jit(solution)/shard_map/ppermute | solution.py:57
  59.6 1.6 %collective-permute-start.23 = (bf16[256,128]{1,0:T(8,128)(2,1)S(1)}, bf16[256,128]{1,0:T(8,128)(2,1)S(1)}, u32[]{:S(2)}, u32[]{:S(2)}) collective-permute-start(bf16[256,128]{1,0:T(8,128)(2,1)S(1)} %shard_map.77), channel_id=1, source_target_pairs={{0,3},{1,2},{2,1},{3,0},{4,7},{5,6},{6,5},{7,4},{8,11},{9,10},{10,... | collective-permute-start | bytes 196616 | tf_op jit(solution)/shard_map/ppermute | solution.py:57
  61.5 1.3 %collective-permute-start.22 = (bf16[256,128]{1,0:T(8,128)(2,1)S(1)}, bf16[256,128]{1,0:T(8,128)(2,1)S(1)}, u32[]{:S(2)}, u32[]{:S(2)}) collective-permute-start(bf16[256,128]{1,0:T(8,128)(2,1)S(1)} %shard_map.76), channel_id=1, source_target_pairs={{0,2},{1,3},{2,0},{3,1},{4,6},{5,7},{6,4},{7,5},{8,10},{9,11},{10,... | collective-permute-start | bytes 196616 | tf_op jit(solution)/shard_map/ppermute | solution.py:57
  64.6 2.2 %collective-permute-done.21.refs_1_ = bf16[256,128]{1,0:T(8,128)(2,1)S(1)} collective-permute-done((bf16[256,128]{1,0:T(8,128)(2,1)S(1)}, bf16[256,128]{1,0:T(8,128)(2,1)S(1)}, u32[]{:S(2)}, u32[]{:S(2)}) %collective-permute-start.21) | collective-permute-done | bytes 65568 | tf_op jit(solution)/shard_map/ppermute | solution.py:57
  66.9 3.1 %collective-permute-start.24 = (bf16[4,128,128]{2,1,0:T(8,128)(2,1)S(1)}, bf16[4,128,128]{2,1,0:T(8,128)(2,1)S(1)}, u32[]{:S(2)}, u32[]{:S(2)}) collective-permute-start(bf16[4,128,128]{2,1,0:T(8,128)(2,1)S(1)} %get-tuple-element.64), channel_id=1, source_target_pairs={{0,4},{1,5},{2,6},{3,7},{4,0},{5,1},{6,2},{7,3},{8,12},{9,13},{10,... | collective-permute-start | bytes 393224 | tf_op jit(solution)/shard_map/ppermute | solution.py:57
  (67 shorter events, 21.9 us)
Async XLA Ops:
  0.0 19.8 %collective-permute-start = (bf16[256,768]{1,0:T(8,128)(2,1)}, bf16[256,768]{1,0:T(8,128)(2,1)S(1)}, u32[]{:S(2)}, u32[]{:S(2)}) collective-permute-start(bf16[256,768]{1,0:T(8,128)(2,1)} %w.1), channel_id=1, source_target_pairs={{0,16},{1,17},{2,18},{3,19},{4,20},{5,21},{6,22},{7,23},{8,24},{9,... | collective-permute-start | bytes 1179656 | tf_op jit(solution)/shard_map/ppermute | solution.py:57
  4.8 4.4 %collective-permute-start.3 = (bf16[128,256]{1,0:T(8,128)(2,1)S(1)}, bf16[128,256]{1,0:T(8,128)(2,1)S(1)}, u32[]{:S(2)}, u32[]{:S(2)}) collective-permute-start(bf16[128,256]{1,0:T(8,128)(2,1)S(1)} %get-tuple-element.37), channel_id=1, source_target_pairs={{0,3},{1,2},{2,1},{3,0},{4,7},{5,6},{6,5},{7,4},{8,11},{9,10},{10,... | collective-permute-start | bytes 196616 | tf_op jit(solution)/shard_map/ppermute | solution.py:57
  7.0 6.0 %collective-permute-start.1 = (bf16[336,256]{1,0:T(8,128)(2,1)S(1)}, bf16[336,256]{1,0:T(8,128)(2,1)S(1)}, u32[]{:S(2)}, u32[]{:S(2)}) collective-permute-start(bf16[336,256]{1,0:T(8,128)(2,1)S(1)} %get-tuple-element.35), channel_id=1, source_target_pairs={{0,1},{1,0},{2,3},{3,2},{4,5},{5,4},{6,7},{7,6},{8,9},{9,8},{10,11... | collective-permute-start | bytes 516104 | tf_op jit(solution)/shard_map/ppermute | solution.py:57
  7.3 5.8 %collective-permute-start.2 = (bf16[336,256]{1,0:T(8,128)(2,1)S(1)}, bf16[336,256]{1,0:T(8,128)(2,1)S(1)}, u32[]{:S(2)}, u32[]{:S(2)}) collective-permute-start(bf16[336,256]{1,0:T(8,128)(2,1)S(1)} %get-tuple-element.36), channel_id=1, source_target_pairs={{0,2},{1,3},{2,0},{3,1},{4,6},{5,7},{6,4},{7,5},{8,10},{9,11},{10,... | collective-permute-start | bytes 516104 | tf_op jit(solution)/shard_map/ppermute | solution.py:57
  9.2 15.0 %collective-permute-start.7 = (bf16[128,2048]{1,0:T(8,128)(2,1)}, bf16[128,2048]{1,0:T(8,128)(2,1)S(1)}, u32[]{:S(2)}, u32[]{:S(2)}) collective-permute-start(bf16[128,2048]{1,0:T(8,128)(2,1)} %bitcast.12), channel_id=1, source_target_pairs={{0,2},{1,3},{2,0},{3,1},{4,6},{5,7},{6,4},{7,5},{8,10},{9,11},{10,... | collective-permute-start | bytes 1572872 | tf_op jit(solution)/shard_map/ppermute | solution.py:57
  10.4 13.8 %collective-permute-start.6 = (bf16[128,2048]{1,0:T(8,128)(2,1)}, bf16[128,2048]{1,0:T(8,128)(2,1)S(1)}, u32[]{:S(2)}, u32[]{:S(2)}) collective-permute-start(bf16[128,2048]{1,0:T(8,128)(2,1)} %bitcast.13), channel_id=1, source_target_pairs={{0,1},{1,0},{2,3},{3,2},{4,5},{5,4},{6,7},{7,6},{8,9},{9,8},{10,11... | collective-permute-start | bytes 1572872 | tf_op jit(solution)/shard_map/ppermute | solution.py:57
  13.2 13.8 %collective-permute-start.8 = (bf16[256,768]{1,0:T(8,128)(2,1)S(1)}, bf16[256,768]{1,0:T(8,128)(2,1)S(1)}, u32[]{:S(2)}, u32[]{:S(2)}) collective-permute-start(bf16[256,768]{1,0:T(8,128)(2,1)S(1)} %shard_map.67.refs_2_.refs_0_), channel_id=1, source_target_pairs={{0,8},{1,9},{2,10},{3,11},{4,12},{5,13},{6,14},{7,15},{8,0},{9,1},... | collective-permute-start | bytes 1179656 | tf_op jit(solution)/shard_map/ppermute | solution.py:57
  19.9 5.8 %collective-permute-start.4 = (bf16[256,256]{1,0:T(8,128)(2,1)S(1)}, bf16[256,256]{1,0:T(8,128)(2,1)S(1)}, u32[]{:S(2)}, u32[]{:S(2)}) collective-permute-start(bf16[256,256]{1,0:T(8,128)(2,1)S(1)} %get-tuple-element.66), channel_id=1, source_target_pairs={{0,1},{1,0},{2,3},{3,2},{4,5},{5,4},{6,7},{7,6},{8,9},{9,8},{10,11... | collective-permute-start | bytes 393224 | tf_op jit(solution)/shard_map/ppermute | solution.py:57
  21.1 5.8 %collective-permute-start.5 = (bf16[256,256]{1,0:T(8,128)(2,1)S(1)}, bf16[256,256]{1,0:T(8,128)(2,1)S(1)}, u32[]{:S(2)}, u32[]{:S(2)}) collective-permute-start(bf16[256,256]{1,0:T(8,128)(2,1)S(1)} %get-tuple-element.65), channel_id=1, source_target_pairs={{0,2},{1,3},{2,0},{3,1},{4,6},{5,7},{6,4},{7,5},{8,10},{9,11},{10,... | collective-permute-start | bytes 393224 | tf_op jit(solution)/shard_map/ppermute | solution.py:57
  27.1 2.9 %collective-permute-start.9 = (bf16[256,384]{1,0:T(8,128)(2,1)S(1)}, bf16[256,384]{1,0:T(8,128)(2,1)S(1)}, u32[]{:S(2)}, u32[]{:S(2)}) collective-permute-start(bf16[256,384]{1,0:T(8,128)(2,1)S(1)} %get-tuple-element.47), channel_id=1, source_target_pairs={{0,4},{1,5},{2,6},{3,7},{4,0},{5,1},{6,2},{7,3},{8,12},{9,13},{10,... | collective-permute-start | bytes 589832 | tf_op jit(solution)/shard_map/ppermute | solution.py:57
  30.1 4.1 %collective-permute-start.10 = (bf16[384,2048]{1,0:T(8,128)(2,1)S(1)}, bf16[384,2048]{1,0:T(8,128)(2,1)S(1)}, u32[]{:S(2)}, u32[]{:S(2)}) collective-permute-start(bf16[384,2048]{1,0:T(8,128)(2,1)S(1)} %get-tuple-element.50.refs_0_), channel_id=1, source_target_pairs={{0,4},{1,5},{2,6},{3,7},{4,0},{5,1},{6,2},{7,3},{8,12},{9,13},{10,... | collective-permute-start | bytes 4718600 | tf_op jit(solution)/shard_map/ppermute | solution.py:57
  30.6 3.6 %collective-permute-start.12 = (bf16[528,384]{1,0:T(8,128)(2,1)S(1)}, bf16[528,384]{1,0:T(8,128)(2,1)S(1)}, u32[]{:S(2)}, u32[]{:S(2)}) collective-permute-start(bf16[528,384]{1,0:T(8,128)(2,1)S(1)} %pad_maximum_fusion.1), channel_id=1, source_target_pairs={{0,4},{1,5},{2,6},{3,7},{4,0},{5,1},{6,2},{7,3},{8,12},{9,13},{10,... | collective-permute-start | bytes 1216520 | tf_op jit(solution)/shard_map/ppermute | solution.py:57
  30.8 7.5 %collective-permute-start.11 = (bf16[128,1024]{1,0:T(8,128)(2,1)S(1)}, bf16[128,1024]{1,0:T(8,128)(2,1)S(1)}, u32[]{:S(2)}, u32[]{:S(2)}) collective-permute-start(bf16[128,1024]{1,0:T(8,128)(2,1)S(1)} %get-tuple-element.51), channel_id=1, source_target_pairs={{0,2},{1,3},{2,0},{3,1},{4,6},{5,7},{6,4},{7,5},{8,10},{9,11},{10,... | collective-permute-start | bytes 786440 | tf_op jit(solution)/shard_map/ppermute | solution.py:57
  31.3 7.2 %collective-permute-start.13 = (bf16[128,1024]{1,0:T(8,128)(2,1)S(1)}, bf16[128,1024]{1,0:T(8,128)(2,1)S(1)}, u32[]{:S(2)}, u32[]{:S(2)}) collective-permute-start(bf16[128,1024]{1,0:T(8,128)(2,1)S(1)} %get-tuple-element.56), channel_id=1, source_target_pairs={{0,1},{1,0},{2,3},{3,2},{4,5},{5,4},{6,7},{7,6},{8,9},{9,8},{10,11... | collective-permute-start | bytes 786440 | tf_op jit(solution)/shard_map/ppermute | solution.py:57
  32.5 10.5 %collective-permute-start.16 = (bf16[512,384]{1,0:T(8,128)(2,1)S(1)}, bf16[512,384]{1,0:T(8,128)(2,1)S(1)}, u32[]{:S(2)}, u32[]{:S(2)}) collective-permute-start(bf16[512,384]{1,0:T(8,128)(2,1)S(1)} %constant_dynamic-update-slice_fusion.refs_5_.refs_3_), channel_id=1, source_target_pairs={{0,8},{1,9},{2,10},{3,11},{4,12},{5,13},{6,14},{7,15},{8,0},{9,1},... | collective-permute-start | bytes 1179656 | tf_op jit(solution)/shard_map/ppermute | solution.py:57
  39.2 3.1 %collective-permute-start.14 = (bf16[80,2048]{1,0:T(8,128)(2,1)S(1)}, bf16[80,2048]{1,0:T(8,128)(2,1)S(1)}, u32[]{:S(2)}, u32[]{:S(2)}) collective-permute-start(bf16[80,2048]{1,0:T(8,128)(2,1)S(1)} %slice.29), channel_id=1, source_target_pairs={{0,4},{1,5},{2,6},{3,7},{4,0},{5,1},{6,2},{7,3},{8,12},{9,13},{10,... | collective-permute-start | bytes 983048 | tf_op jit(solution)/shard_map/ppermute | solution.py:57
  43.7 9.0 %collective-permute-start.17 = (bf16[4,256,128]{2,1,0:T(8,128)(2,1)S(1)}, bf16[4,256,128]{2,1,0:T(8,128)(2,1)S(1)}, u32[]{:S(2)}, u32[]{:S(2)}) collective-permute-start(bf16[4,256,128]{2,1,0:T(8,128)(2,1)S(1)} %get-tuple-element.61.own), channel_id=1, source_target_pairs={{8,16},{9,17},{10,18},{11,19},{12,20},{13,21},{14,22},{15,23},{16,... | collective-permute-start | bytes 786440 | tf_op jit(solution)/shard_map/ppermute | solution.py:57
  47.6 6.1 %collective-permute-start.18 = (bf16[4,256,128]{2,1,0:T(8,128)(2,1)S(1)}, bf16[4,256,128]{2,1,0:T(8,128)(2,1)S(1)}, u32[]{:S(2)}, u32[]{:S(2)}) collective-permute-start(bf16[4,256,128]{2,1,0:T(8,128)(2,1)S(1)} %get-tuple-element.61.own), channel_id=1, source_target_pairs={{0,8},{1,9},{2,10},{3,11},{4,12},{5,13},{6,14},{7,15},{8,0},{9,1},... | collective-permute-start | bytes 786440 | tf_op jit(solution)/shard_map/ppermute | solution.py:57
  47.7 10.6 %collective-permute-start.19 = (bf16[4,256,128]{2,1,0:T(8,128)(2,1)S(1)}, bf16[4,256,128]{2,1,0:T(8,128)(2,1)S(1)}, u32[]{:S(2)}, u32[]{:S(2)}) collective-permute-start(bf16[4,256,128]{2,1,0:T(8,128)(2,1)S(1)} %get-tuple-element.62.own), channel_id=1, source_target_pairs={{8,16},{9,17},{10,18},{11,19},{12,20},{13,21},{14,22},{15,23},{16,... | collective-permute-start | bytes 786440 | tf_op jit(solution)/shard_map/ppermute | solution.py:57
  50.3 9.0 %collective-permute-start.20 = (bf16[4,256,128]{2,1,0:T(8,128)(2,1)S(1)}, bf16[4,256,128]{2,1,0:T(8,128)(2,1)S(1)}, u32[]{:S(2)}, u32[]{:S(2)}) collective-permute-start(bf16[4,256,128]{2,1,0:T(8,128)(2,1)S(1)} %get-tuple-element.62.own), channel_id=1, source_target_pairs={{0,8},{1,9},{2,10},{3,11},{4,12},{5,13},{6,14},{7,15},{8,0},{9,1},... | collective-permute-start | bytes 786440 | tf_op jit(solution)/shard_map/ppermute | solution.py:57
  59.6 4.1 %collective-permute-start.23 = (bf16[256,128]{1,0:T(8,128)(2,1)S(1)}, bf16[256,128]{1,0:T(8,128)(2,1)S(1)}, u32[]{:S(2)}, u32[]{:S(2)}) collective-permute-start(bf16[256,128]{1,0:T(8,128)(2,1)S(1)} %shard_map.77), channel_id=1, source_target_pairs={{0,3},{1,2},{2,1},{3,0},{4,7},{5,6},{6,5},{7,4},{8,11},{9,10},{10,... | collective-permute-start | bytes 196616 | tf_op jit(solution)/shard_map/ppermute | solution.py:57
  61.5 3.2 %collective-permute-start.22 = (bf16[256,128]{1,0:T(8,128)(2,1)S(1)}, bf16[256,128]{1,0:T(8,128)(2,1)S(1)}, u32[]{:S(2)}, u32[]{:S(2)}) collective-permute-start(bf16[256,128]{1,0:T(8,128)(2,1)S(1)} %shard_map.76), channel_id=1, source_target_pairs={{0,2},{1,3},{2,0},{3,1},{4,6},{5,7},{6,4},{7,5},{8,10},{9,11},{10,... | collective-permute-start | bytes 196616 | tf_op jit(solution)/shard_map/ppermute | solution.py:57
  63.0 3.9 %collective-permute-start.21 = (bf16[256,128]{1,0:T(8,128)(2,1)S(1)}, bf16[256,128]{1,0:T(8,128)(2,1)S(1)}, u32[]{:S(2)}, u32[]{:S(2)}) collective-permute-start(bf16[256,128]{1,0:T(8,128)(2,1)S(1)} %shard_map.75), channel_id=1, source_target_pairs={{0,1},{1,0},{2,3},{3,2},{4,5},{5,4},{6,7},{7,6},{8,9},{9,8},{10,11... | collective-permute-start | bytes 196616 | tf_op jit(solution)/shard_map/ppermute | solution.py:57
  66.9 4.1 %collective-permute-start.24 = (bf16[4,128,128]{2,1,0:T(8,128)(2,1)S(1)}, bf16[4,128,128]{2,1,0:T(8,128)(2,1)S(1)}, u32[]{:S(2)}, u32[]{:S(2)}) collective-permute-start(bf16[4,128,128]{2,1,0:T(8,128)(2,1)S(1)} %get-tuple-element.64), channel_id=1, source_target_pairs={{0,4},{1,5},{2,6},{3,7},{4,0},{5,1},{6,2},{7,3},{8,12},{9,13},{10,... | collective-permute-start | bytes 393224 | tf_op jit(solution)/shard_map/ppermute | solution.py:57
  (7 other events, 31.0 us)

commit v15 on v14

--- a/solution.py
+++ b/solution.py
@@ -42,7 +42,6 @@
 
 
 PAIR = 2 * HD
-V_ORDER = (3, 1, 2, 0)
 EXTRA = 16
 
 
@@ -253,31 +252,34 @@
                 out_ref[r, u * block : (u + 1) * block, here] = (p * inverse).astype(jnp.bfloat16)
 
 
-def mix_kernel(r, weights, middle, own, outer, out_ref):
+def mix_kernel(weights, middle, own, outer, keep_ref, send_ref):
+    _, core, _ = where_am_i()
     block = weights.shape[1] // 2
-    values = neighbours(outer, own, middle, r)
-    for u in range(2):
-        w = weights[r, u * block : (u + 1) * block]
-        v = [values[side][first * block : last * block] for side, first, last in spans(u)]
-        result = jnp.dot(w, jnp.concatenate(v, axis=0), preferred_element_type=jnp.float32)
-        out_ref[u * block : (u + 1) * block] = result.astype(jnp.bfloat16)
-
-
-def pack_kernel(*refs):
-    keep_ref, send_ref = refs[4:]
-    _, core, _ = where_am_i()
-    block = keep_ref.shape[1]
-    for r, ref in enumerate(refs[:4]):
-        for rel, out_ref in enumerate((keep_ref, send_ref)):
-            out_ref[r] = ref[pl.ds(pl.multiple_of((core ^ rel) * block, block), block), :]
-
-
-def gather_kernel(mine, other, out_ref):
+    for r in range(4):
+        values = neighbours(outer, own, middle, r)
+        results = []
+        for u in range(2):
+            w = weights[r, u * block : (u + 1) * block]
+            v = [values[side][first * block : last * block] for side, first, last in spans(u)]
+            result = jnp.dot(w, jnp.concatenate(v, axis=0), preferred_element_type=jnp.float32)
+            results.append(result.astype(jnp.bfloat16))
+        keep_ref[r] = jnp.where(core == 0, results[0], results[1])
+        send_ref[r] = jnp.where(core == 0, results[1], results[0])
+
+
+def pair_kernel(mine, other, x_ref, y_ref, diagonal_ref):
+    for r, ref in enumerate((x_ref, y_ref, diagonal_ref)):
+        ref[:, :HD] = mine[r + 1]
+        ref[:, HD:] = other[r + 1]
+
+
+def gather_kernel(mine, other, x, y, diagonal, out_ref):
     _, core, depth = where_am_i()
-    for rel, ref in enumerate((mine, other)):
-        for r in range(4):
+    pairs = [(mine[0], other[0])] + [(ref[:, :HD], ref[:, HD:]) for ref in (x, y, diagonal)]
+    for r, pair in enumerate(pairs):
+        for rel in range(2):
             at = pl.multiple_of((2 * (depth ^ r) + (core ^ rel)) * HD, HD)
-            out_ref[:, pl.ds(at, HD)] = ref[r]
+            out_ref[:, pl.ds(at, HD)] = pair[rel]
 
 
 def call(kernel, outs, places, scratch=(), macs=0, limit=32):
@@ -376,14 +378,11 @@
         q, middle, k, outer, flags, received
     )
     values = (swap_middle(v), v, swap_z(v, 1))
-    pieces = {}
-    for r in V_ORDER:
-        mixed = call(functools.partial(mix_kernel, r), array(2 * block, HD), "vvvv", macs=2 * block * 5 * block * HD)(
-            weights, *values
-        )
-        pieces[r] = swap_depth(mixed, r) if r else mixed
-    kept, sent = call(pack_kernel, (array(4, block, HD),) * 2, "vvvv")(*[pieces[r] for r in range(4)])
-    context = call(gather_kernel, array(block, HEADS * HD), "vv")(kept, swap_core(sent))
+    kept, sent = call(mix_kernel, (array(4, block, HD),) * 2, "vvvv", macs=8 * block * 5 * block * HD)(weights, *values)
+    received = swap_core(sent)
+    x, y, across = call(pair_kernel, (array(block, PAIR),) * 3, "vv")(kept, received)
+    across, x, y = swap_depth(across, 3), swap_depth(x, 1), swap_depth(y, 2)
+    context = call(gather_kernel, array(block, HEADS * HD), "v" * 5)(kept, received, x, y, across)
     return context.reshape(time_len, site_len, HEADS * HD)
 
 

time: 73.1 us -> 72.7 us (level)
  the two profiles are of different devices: /device:TPU:9 before, /device:TPU:0 now
where the time goes in v15:
time: 72.7 us; the launch traced here: 72.4 us
  starting transfers between devices  30.9 us (43%)
  waiting for transfers between devices  28.6 us (39%)
  Pallas kernels  7.89 us (11%)
  local copies, waits for them, and re-layouts  3.26 us (4%)
  other arithmetic  1.52 us (2%)
    ppermute x25, starting transfers between devices, hop(): return lax.ppermute(value, ('tm', 'depth'), pairs)  30.9 us
    ppermute x25, waiting for transfers between devices, hop(): return lax.ppermute(value, ('tm', 'depth'), pairs)  28.6 us
    unnamed x13, local copies, waits for them, and re-layouts  3.13 us
    pallas_call x3, Pallas kernels, embed(): call(functools.partial(embed_kernel, rs, len(finished)), out, 'v' * (6 +...  2.38 us
  transfers between devices with their start and end apart: 25, of which 19 were waited for; matrix products, arithmetic and copies ran while one was open for 2% of the time, Pallas kernels for 8%

profile of v15, /device:TPU:0, one launch (start us, length us, event | category | flops | bytes accessed | tf_op | source)
XLA Modules:
  0.0 72.4 jit_solution(15213570615007531410)
XLA Ops:
  0.0 4.0 %collective-permute-start = (bf16[256,768]{1,0:T(8,128)(2,1)}, bf16[256,768]{1,0:T(8,128)(2,1)S(1)}, u32[]{:S(2)}, u32[]{:S(2)}) collective-permute-start(bf16[256,768]{1,0:T(8,128)(2,1)} %w.1), channel_id=1, source_target_pairs={{0,16},{1,17},{2,18},{3,19},{4,20},{5,21},{6,22},{7,23},{8,24},{9,... | collective-permute-start | bytes 1179656 | tf_op jit(solution)/shard_map/ppermute | solution.py:56
  6.5 2.5 %collective-permute-start.3 = (bf16[128,256]{1,0:T(8,128)(2,1)S(1)}, bf16[128,256]{1,0:T(8,128)(2,1)S(1)}, u32[]{:S(2)}, u32[]{:S(2)}) collective-permute-start(bf16[128,256]{1,0:T(8,128)(2,1)S(1)} %get-tuple-element.40), channel_id=1, source_target_pairs={{0,3},{1,2},{2,1},{3,0},{4,7},{5,6},{6,5},{7,4},{8,11},{9,10},{10,... | collective-permute-start | bytes 196616 | tf_op jit(solution)/shard_map/ppermute | solution.py:56
  10.1 2.4 %collective-permute-done.3.across = bf16[128,256]{1,0:T(8,128)(2,1)S(1)} collective-permute-done((bf16[128,256]{1,0:T(8,128)(2,1)S(1)}, bf16[128,256]{1,0:T(8,128)(2,1)S(1)}, u32[]{:S(2)}, u32[]{:S(2)}) %collective-permute-start.3) | collective-permute-done | bytes 65568 | tf_op jit(solution)/shard_map/ppermute | solution.py:56
  12.5 1.5 %collective-permute-start.7 = (bf16[128,2048]{1,0:T(8,128)(2,1)}, bf16[128,2048]{1,0:T(8,128)(2,1)S(1)}, u32[]{:S(2)}, u32[]{:S(2)}) collective-permute-start(bf16[128,2048]{1,0:T(8,128)(2,1)} %bitcast.12), channel_id=1, source_target_pairs={{0,2},{1,3},{2,0},{3,1},{4,6},{5,7},{6,4},{7,5},{8,10},{9,11},{10,... | collective-permute-start | bytes 1572872 | tf_op jit(solution)/shard_map/ppermute | solution.py:56
  14.0 1.5 %collective-permute-start.6 = (bf16[128,2048]{1,0:T(8,128)(2,1)}, bf16[128,2048]{1,0:T(8,128)(2,1)S(1)}, u32[]{:S(2)}, u32[]{:S(2)}) collective-permute-start(bf16[128,2048]{1,0:T(8,128)(2,1)} %bitcast.13), channel_id=1, source_target_pairs={{0,1},{1,0},{2,3},{3,2},{4,5},{5,4},{6,7},{7,6},{8,9},{9,8},{10,11... | collective-permute-start | bytes 1572872 | tf_op jit(solution)/shard_map/ppermute | solution.py:56
  17.0 1.6 %collective-permute-start.8 = (bf16[256,768]{1,0:T(8,128)(2,1)S(1)}, bf16[256,768]{1,0:T(8,128)(2,1)S(1)}, u32[]{:S(2)}, u32[]{:S(2)}) collective-permute-start(bf16[256,768]{1,0:T(8,128)(2,1)S(1)} %shard_map.67.refs_2_.refs_0_), channel_id=1, source_target_pairs={{0,8},{1,9},{2,10},{3,11},{4,12},{5,13},{6,14},{7,15},{8,0},{9,1},... | collective-permute-start | bytes 1179656 | tf_op jit(solution)/shard_map/ppermute | solution.py:56
  18.6 1.4 %copy-done = bf16[3,128,2048]{2,1,0:T(8,128)(2,1)S(1)} copy-done((bf16[3,128,2048]{2,1,0:T(8,128)(2,1)S(1)}, bf16[3,128,2048]{2,1,0:T(8,128)(2,1)}, u32[]{:S(2)}) %copy-start) | copy-done | bytes 1572888
  21.9 1.6 %collective-permute-start.4 = (bf16[256,256]{1,0:T(8,128)(2,1)S(1)}, bf16[256,256]{1,0:T(8,128)(2,1)S(1)}, u32[]{:S(2)}, u32[]{:S(2)}) collective-permute-start(bf16[256,256]{1,0:T(8,128)(2,1)S(1)} %get-tuple-element.72), channel_id=1, source_target_pairs={{0,1},{1,0},{2,3},{3,2},{4,5},{5,4},{6,7},{7,6},{8,9},{9,8},{10,11... | collective-permute-start | bytes 393224 | tf_op jit(solution)/shard_map/ppermute | solution.py:56
  23.5 1.5 %collective-permute-start.5 = (bf16[256,256]{1,0:T(8,128)(2,1)S(1)}, bf16[256,256]{1,0:T(8,128)(2,1)S(1)}, u32[]{:S(2)}, u32[]{:S(2)}) collective-permute-start(bf16[256,256]{1,0:T(8,128)(2,1)S(1)} %get-tuple-element.71), channel_id=1, source_target_pairs={{0,2},{1,3},{2,0},{3,1},{4,6},{5,7},{6,4},{7,5},{8,10},{9,11},{10,... | collective-permute-start | bytes 393224 | tf_op jit(solution)/shard_map/ppermute | solution.py:56
  25.1 3.1 %collective-permute-done.7.refs_1_ = bf16[128,2048]{1,0:T(8,128)(2,1)S(1)} collective-permute-done((bf16[128,2048]{1,0:T(8,128)(2,1)}, bf16[128,2048]{1,0:T(8,128)(2,1)S(1)}, u32[]{:S(2)}, u32[]{:S(2)}) %collective-permute-start.7) | collective-permute-done | bytes 524320 | tf_op jit(solution)/shard_map/ppermute | solution.py:56
  30.4 1.4 %collective-permute-done.9 = bf16[256,384]{1,0:T(8,128)(2,1)S(1)} collective-permute-done((bf16[256,384]{1,0:T(8,128)(2,1)S(1)}, bf16[256,384]{1,0:T(8,128)(2,1)S(1)}, u32[]{:S(2)}, u32[]{:S(2)}) %collective-permute-start.9) | collective-permute-done | bytes 196640 | tf_op jit(solution)/shard_map/ppermute | solution.py:56
  32.6 1.6 %collective-permute-start.11 = (bf16[128,1024]{1,0:T(8,128)(2,1)S(1)}, bf16[128,1024]{1,0:T(8,128)(2,1)S(1)}, u32[]{:S(2)}, u32[]{:S(2)}) collective-permute-start(bf16[128,1024]{1,0:T(8,128)(2,1)S(1)} %get-tuple-element.54), channel_id=1, source_target_pairs={{0,2},{1,3},{2,0},{3,1},{4,6},{5,7},{6,4},{7,5},{8,10},{9,11},{10,... | collective-permute-start | bytes 786440 | tf_op jit(solution)/shard_map/ppermute | solution.py:56
  34.2 1.5 %collective-permute-start.13 = (bf16[128,1024]{1,0:T(8,128)(2,1)S(1)}, bf16[128,1024]{1,0:T(8,128)(2,1)S(1)}, u32[]{:S(2)}, u32[]{:S(2)}) collective-permute-start(bf16[128,1024]{1,0:T(8,128)(2,1)S(1)} %get-tuple-element.59), channel_id=1, source_target_pairs={{0,1},{1,0},{2,3},{3,2},{4,5},{5,4},{6,7},{7,6},{8,9},{9,8},{10,11... | collective-permute-start | bytes 786440 | tf_op jit(solution)/shard_map/ppermute | solution.py:56
  35.9 1.4 %shard_map.69.refs_4_ = f32[768,384]{1,0:T(8,128)S(1)} custom-call(bf16[384,2048]{1,0:T(8,128)(2,1)S(1)} %get-tuple-element.53.refs_0_, bf16[384,2048]{1,0:T(8,128)(2,1)S(1)} %collective-permute-done.10.refs_1_, bf16[256,768]{1,0:T(8,128)(2,1)S(1)} %shard_map.67.refs_2_.refs_0_, bf16[256,768]{1,0:T(8,128)(2,1)S(1)} %collective-permute-done.8.refs_3_.refs_1_, ...), custom_call_target="tpu_custom_call" | custom-call | flops 905969664 | tf_op jit(solution)/shard_map/pallas_call | solution.py:359
  37.3 3.6 %collective-permute-done.11 = bf16[128,1024]{1,0:T(8,128)(2,1)S(1)} collective-permute-done((bf16[128,1024]{1,0:T(8,128)(2,1)S(1)}, bf16[128,1024]{1,0:T(8,128)(2,1)S(1)}, u32[]{:S(2)}, u32[]{:S(2)}) %collective-permute-start.11) | collective-permute-done | bytes 262176 | tf_op jit(solution)/shard_map/ppermute | solution.py:56
  41.0 1.3 %collective-permute-done.13 = bf16[128,1024]{1,0:T(8,128)(2,1)S(1)} collective-permute-done((bf16[128,1024]{1,0:T(8,128)(2,1)S(1)}, bf16[128,1024]{1,0:T(8,128)(2,1)S(1)}, u32[]{:S(2)}, u32[]{:S(2)}) %collective-permute-start.13) | collective-permute-done | bytes 262176 | tf_op jit(solution)/shard_map/ppermute | solution.py:56
  43.6 1.3 %collective-permute-done.15.bottom = bf16[48,2048]{1,0:T(8,128)(2,1)S(1)} collective-permute-done((bf16[48,2048]{1,0:T(8,128)(2,1)S(1)}, bf16[48,2048]{1,0:T(8,128)(2,1)S(1)}, u32[]{:S(2)}, u32[]{:S(2)}) %collective-permute-start.15) | collective-permute-done | bytes 196640 | tf_op jit(solution)/shard_map/ppermute | solution.py:56
  47.7 4.2 %collective-permute-start.18 = (bf16[4,256,128]{2,1,0:T(8,128)(2,1)S(1)}, bf16[4,256,128]{2,1,0:T(8,128)(2,1)S(1)}, u32[]{:S(2)}, u32[]{:S(2)}) collective-permute-start(bf16[4,256,128]{2,1,0:T(8,128)(2,1)S(1)} %get-tuple-element.64.own), channel_id=1, source_target_pairs={{0,8},{1,9},{2,10},{3,11},{4,12},{5,13},{6,14},{7,15},{8,0},{9,1},... | collective-permute-start | bytes 786440 | tf_op jit(solution)/shard_map/ppermute | solution.py:56
  52.5 1.8 %collective-permute-start.20 = (bf16[4,256,128]{2,1,0:T(8,128)(2,1)S(1)}, bf16[4,256,128]{2,1,0:T(8,128)(2,1)S(1)}, u32[]{:S(2)}, u32[]{:S(2)}) collective-permute-start(bf16[4,256,128]{2,1,0:T(8,128)(2,1)S(1)} %get-tuple-element.65.own), channel_id=1, source_target_pairs={{0,8},{1,9},{2,10},{3,11},{4,12},{5,13},{6,14},{7,15},{8,0},{9,1},... | collective-permute-start | bytes 786440 | tf_op jit(solution)/shard_map/ppermute | solution.py:56
  54.3 4.7 %collective-permute-done.18.outer = bf16[4,256,128]{2,1,0:T(8,128)(2,1)S(1)} collective-permute-done((bf16[4,256,128]{2,1,0:T(8,128)(2,1)S(1)}, bf16[4,256,128]{2,1,0:T(8,128)(2,1)S(1)}, u32[]{:S(2)}, u32[]{:S(2)}) %collective-permute-start.18) | collective-permute-done | bytes 262176 | tf_op jit(solution)/shard_map/ppermute | solution.py:56
  60.3 2.4 %collective-permute-done.20.outer = bf16[4,256,128]{2,1,0:T(8,128)(2,1)S(1)} collective-permute-done((bf16[4,256,128]{2,1,0:T(8,128)(2,1)S(1)}, bf16[4,256,128]{2,1,0:T(8,128)(2,1)S(1)}, u32[]{:S(2)}, u32[]{:S(2)}) %collective-permute-start.20) | collective-permute-done | bytes 262176 | tf_op jit(solution)/shard_map/ppermute | solution.py:56
  63.2 1.3 %collective-permute-done.21.other = bf16[4,128,128]{2,1,0:T(8,128)(2,1)S(1)} collective-permute-done((bf16[4,128,128]{2,1,0:T(8,128)(2,1)S(1)}, bf16[4,128,128]{2,1,0:T(8,128)(2,1)S(1)}, u32[]{:S(2)}, u32[]{:S(2)}) %collective-permute-start.21) | collective-permute-done | bytes 131104 | tf_op jit(solution)/shard_map/ppermute | solution.py:56
  66.4 1.8 %collective-permute-start.24 = (bf16[128,256]{1,0:T(8,128)(2,1)S(1)}, bf16[128,256]{1,0:T(8,128)(2,1)S(1)}, u32[]{:S(2)}, u32[]{:S(2)}) collective-permute-start(bf16[128,256]{1,0:T(8,128)(2,1)S(1)} %get-tuple-element.70), channel_id=1, source_target_pairs={{0,3},{1,2},{2,1},{3,0},{4,7},{5,6},{6,5},{7,4},{8,11},{9,10},{10,... | collective-permute-start | bytes 196616 | tf_op jit(solution)/shard_map/ppermute | solution.py:56
  69.0 1.9 %collective-permute-done.23.y = bf16[128,256]{1,0:T(8,128)(2,1)S(1)} collective-permute-done((bf16[128,256]{1,0:T(8,128)(2,1)S(1)}, bf16[128,256]{1,0:T(8,128)(2,1)S(1)}, u32[]{:S(2)}, u32[]{:S(2)}) %collective-permute-start.23) | collective-permute-done | bytes 65568 | tf_op jit(solution)/shard_map/ppermute | solution.py:56
  (64 shorter events, 20.7 us)
Async XLA Ops:
  0.0 21.9 %collective-permute-start = (bf16[256,768]{1,0:T(8,128)(2,1)}, bf16[256,768]{1,0:T(8,128)(2,1)S(1)}, u32[]{:S(2)}, u32[]{:S(2)}) collective-permute-start(bf16[256,768]{1,0:T(8,128)(2,1)} %w.1), channel_id=1, source_target_pairs={{0,16},{1,17},{2,18},{3,19},{4,20},{5,21},{6,22},{7,23},{8,24},{9,... | collective-permute-start | bytes 1179656 | tf_op jit(solution)/shard_map/ppermute | solution.py:56
  6.5 5.9 %collective-permute-start.3 = (bf16[128,256]{1,0:T(8,128)(2,1)S(1)}, bf16[128,256]{1,0:T(8,128)(2,1)S(1)}, u32[]{:S(2)}, u32[]{:S(2)}) collective-permute-start(bf16[128,256]{1,0:T(8,128)(2,1)S(1)} %get-tuple-element.40), channel_id=1, source_target_pairs={{0,3},{1,2},{2,1},{3,0},{4,7},{5,6},{6,5},{7,4},{8,11},{9,10},{10,... | collective-permute-start | bytes 196616 | tf_op jit(solution)/shard_map/ppermute | solution.py:56
  9.0 7.3 %collective-permute-start.1 = (bf16[336,256]{1,0:T(8,128)(2,1)S(1)}, bf16[336,256]{1,0:T(8,128)(2,1)S(1)}, u32[]{:S(2)}, u32[]{:S(2)}) collective-permute-start(bf16[336,256]{1,0:T(8,128)(2,1)S(1)} %get-tuple-element.38), channel_id=1, source_target_pairs={{0,1},{1,0},{2,3},{3,2},{4,5},{5,4},{6,7},{7,6},{8,9},{9,8},{10,11... | collective-permute-start | bytes 516104 | tf_op jit(solution)/shard_map/ppermute | solution.py:56
  9.6 7.3 %collective-permute-start.2 = (bf16[336,256]{1,0:T(8,128)(2,1)S(1)}, bf16[336,256]{1,0:T(8,128)(2,1)S(1)}, u32[]{:S(2)}, u32[]{:S(2)}) collective-permute-start(bf16[336,256]{1,0:T(8,128)(2,1)S(1)} %get-tuple-element.39), channel_id=1, source_target_pairs={{0,2},{1,3},{2,0},{3,1},{4,6},{5,7},{6,4},{7,5},{8,10},{9,11},{10,... | collective-permute-start | bytes 516104 | tf_op jit(solution)/shard_map/ppermute | solution.py:56
  12.5 15.7 %collective-permute-start.7 = (bf16[128,2048]{1,0:T(8,128)(2,1)}, bf16[128,2048]{1,0:T(8,128)(2,1)S(1)}, u32[]{:S(2)}, u32[]{:S(2)}) collective-permute-start(bf16[128,2048]{1,0:T(8,128)(2,1)} %bitcast.12), channel_id=1, source_target_pairs={{0,2},{1,3},{2,0},{3,1},{4,6},{5,7},{6,4},{7,5},{8,10},{9,11},{10,... | collective-permute-start | bytes 1572872 | tf_op jit(solution)/shard_map/ppermute | solution.py:56
  14.0 14.2 %collective-permute-start.6 = (bf16[128,2048]{1,0:T(8,128)(2,1)}, bf16[128,2048]{1,0:T(8,128)(2,1)S(1)}, u32[]{:S(2)}, u32[]{:S(2)}) collective-permute-start(bf16[128,2048]{1,0:T(8,128)(2,1)} %bitcast.13), channel_id=1, source_target_pairs={{0,1},{1,0},{2,3},{3,2},{4,5},{5,4},{6,7},{7,6},{8,9},{9,8},{10,11... | collective-permute-start | bytes 1572872 | tf_op jit(solution)/shard_map/ppermute | solution.py:56
  17.0 13.2 %collective-permute-start.8 = (bf16[256,768]{1,0:T(8,128)(2,1)S(1)}, bf16[256,768]{1,0:T(8,128)(2,1)S(1)}, u32[]{:S(2)}, u32[]{:S(2)}) collective-permute-start(bf16[256,768]{1,0:T(8,128)(2,1)S(1)} %shard_map.67.refs_2_.refs_0_), channel_id=1, source_target_pairs={{0,8},{1,9},{2,10},{3,11},{4,12},{5,13},{6,14},{7,15},{8,0},{9,1},... | collective-permute-start | bytes 1179656 | tf_op jit(solution)/shard_map/ppermute | solution.py:56
  21.9 7.4 %collective-permute-start.4 = (bf16[256,256]{1,0:T(8,128)(2,1)S(1)}, bf16[256,256]{1,0:T(8,128)(2,1)S(1)}, u32[]{:S(2)}, u32[]{:S(2)}) collective-permute-start(bf16[256,256]{1,0:T(8,128)(2,1)S(1)} %get-tuple-element.72), channel_id=1, source_target_pairs={{0,1},{1,0},{2,3},{3,2},{4,5},{5,4},{6,7},{7,6},{8,9},{9,8},{10,11... | collective-permute-start | bytes 393224 | tf_op jit(solution)/shard_map/ppermute | solution.py:56
  23.5 6.0 %collective-permute-start.5 = (bf16[256,256]{1,0:T(8,128)(2,1)S(1)}, bf16[256,256]{1,0:T(8,128)(2,1)S(1)}, u32[]{:S(2)}, u32[]{:S(2)}) collective-permute-start(bf16[256,256]{1,0:T(8,128)(2,1)S(1)} %get-tuple-element.71), channel_id=1, source_target_pairs={{0,2},{1,3},{2,0},{3,1},{4,6},{5,7},{6,4},{7,5},{8,10},{9,11},{10,... | collective-permute-start | bytes 393224 | tf_op jit(solution)/shard_map/ppermute | solution.py:56
  30.3 1.5 %collective-permute-start.9 = (bf16[256,384]{1,0:T(8,128)(2,1)S(1)}, bf16[256,384]{1,0:T(8,128)(2,1)S(1)}, u32[]{:S(2)}, u32[]{:S(2)}) collective-permute-start(bf16[256,384]{1,0:T(8,128)(2,1)S(1)} %get-tuple-element.50), channel_id=1, source_target_pairs={{0,4},{1,5},{2,6},{3,7},{4,0},{5,1},{6,2},{7,3},{8,12},{9,13},{10,... | collective-permute-start | bytes 589832 | tf_op jit(solution)/shard_map/ppermute | solution.py:56
  31.9 4.1 %collective-permute-start.10 = (bf16[384,2048]{1,0:T(8,128)(2,1)S(1)}, bf16[384,2048]{1,0:T(8,128)(2,1)S(1)}, u32[]{:S(2)}, u32[]{:S(2)}) collective-permute-start(bf16[384,2048]{1,0:T(8,128)(2,1)S(1)} %get-tuple-element.53.refs_0_), channel_id=1, source_target_pairs={{0,4},{1,5},{2,6},{3,7},{4,0},{5,1},{6,2},{7,3},{8,12},{9,13},{10,... | collective-permute-start | bytes 4718600 | tf_op jit(solution)/shard_map/ppermute | solution.py:56
  32.2 3.7 %collective-permute-start.12 = (bf16[528,384]{1,0:T(8,128)(2,1)S(1)}, bf16[528,384]{1,0:T(8,128)(2,1)S(1)}, u32[]{:S(2)}, u32[]{:S(2)}) collective-permute-start(bf16[528,384]{1,0:T(8,128)(2,1)S(1)} %pad_maximum_fusion.1), channel_id=1, source_target_pairs={{0,4},{1,5},{2,6},{3,7},{4,0},{5,1},{6,2},{7,3},{8,12},{9,13},{10,... | collective-permute-start | bytes 1216520 | tf_op jit(solution)/shard_map/ppermute | solution.py:56
  32.6 8.3 %collective-permute-start.11 = (bf16[128,1024]{1,0:T(8,128)(2,1)S(1)}, bf16[128,1024]{1,0:T(8,128)(2,1)S(1)}, u32[]{:S(2)}, u32[]{:S(2)}) collective-permute-start(bf16[128,1024]{1,0:T(8,128)(2,1)S(1)} %get-tuple-element.54), channel_id=1, source_target_pairs={{0,2},{1,3},{2,0},{3,1},{4,6},{5,7},{6,4},{7,5},{8,10},{9,11},{10,... | collective-permute-start | bytes 786440 | tf_op jit(solution)/shard_map/ppermute | solution.py:56
  34.2 8.1 %collective-permute-start.13 = (bf16[128,1024]{1,0:T(8,128)(2,1)S(1)}, bf16[128,1024]{1,0:T(8,128)(2,1)S(1)}, u32[]{:S(2)}, u32[]{:S(2)}) collective-permute-start(bf16[128,1024]{1,0:T(8,128)(2,1)S(1)} %get-tuple-element.59), channel_id=1, source_target_pairs={{0,1},{1,0},{2,3},{3,2},{4,5},{5,4},{6,7},{7,6},{8,9},{9,8},{10,11... | collective-permute-start | bytes 786440 | tf_op jit(solution)/shard_map/ppermute | solution.py:56
  35.7 10.6 %collective-permute-start.16 = (bf16[512,384]{1,0:T(8,128)(2,1)S(1)}, bf16[512,384]{1,0:T(8,128)(2,1)S(1)}, u32[]{:S(2)}, u32[]{:S(2)}) collective-permute-start(bf16[512,384]{1,0:T(8,128)(2,1)S(1)} %constant_dynamic-update-slice_fusion.refs_5_.refs_3_), channel_id=1, source_target_pairs={{0,8},{1,9},{2,10},{3,11},{4,12},{5,13},{6,14},{7,15},{8,0},{9,1},... | collective-permute-start | bytes 1179656 | tf_op jit(solution)/shard_map/ppermute | solution.py:56
  43.0 2.0 %collective-permute-start.14 = (bf16[80,2048]{1,0:T(8,128)(2,1)S(1)}, bf16[80,2048]{1,0:T(8,128)(2,1)S(1)}, u32[]{:S(2)}, u32[]{:S(2)}) collective-permute-start(bf16[80,2048]{1,0:T(8,128)(2,1)S(1)} %slice.29), channel_id=1, source_target_pairs={{0,4},{1,5},{2,6},{3,7},{4,0},{5,1},{6,2},{7,3},{8,12},{9,13},{10,... | collective-permute-start | bytes 983048 | tf_op jit(solution)/shard_map/ppermute | solution.py:56
  43.1 1.9 %collective-permute-start.15 = (bf16[48,2048]{1,0:T(8,128)(2,1)S(1)}, bf16[48,2048]{1,0:T(8,128)(2,1)S(1)}, u32[]{:S(2)}, u32[]{:S(2)}) collective-permute-start(bf16[48,2048]{1,0:T(8,128)(2,1)S(1)} %slice.30), channel_id=1, source_target_pairs={{0,4},{1,5},{2,6},{3,7},{4,0},{5,1},{6,2},{7,3},{8,12},{9,13},{10,... | collective-permute-start | bytes 589832 | tf_op jit(solution)/shard_map/ppermute | solution.py:56
  47.0 7.3 %collective-permute-start.17 = (bf16[4,256,128]{2,1,0:T(8,128)(2,1)S(1)}, bf16[4,256,128]{2,1,0:T(8,128)(2,1)S(1)}, u32[]{:S(2)}, u32[]{:S(2)}) collective-permute-start(bf16[4,256,128]{2,1,0:T(8,128)(2,1)S(1)} %get-tuple-element.64.own), channel_id=1, source_target_pairs={{8,16},{9,17},{10,18},{11,19},{12,20},{13,21},{14,22},{15,23},{16,... | collective-permute-start | bytes 786440 | tf_op jit(solution)/shard_map/ppermute | solution.py:56
  47.7 11.4 %collective-permute-start.18 = (bf16[4,256,128]{2,1,0:T(8,128)(2,1)S(1)}, bf16[4,256,128]{2,1,0:T(8,128)(2,1)S(1)}, u32[]{:S(2)}, u32[]{:S(2)}) collective-permute-start(bf16[4,256,128]{2,1,0:T(8,128)(2,1)S(1)} %get-tuple-element.64.own), channel_id=1, source_target_pairs={{0,8},{1,9},{2,10},{3,11},{4,12},{5,13},{6,14},{7,15},{8,0},{9,1},... | collective-permute-start | bytes 786440 | tf_op jit(solution)/shard_map/ppermute | solution.py:56
  51.9 8.4 %collective-permute-start.19 = (bf16[4,256,128]{2,1,0:T(8,128)(2,1)S(1)}, bf16[4,256,128]{2,1,0:T(8,128)(2,1)S(1)}, u32[]{:S(2)}, u32[]{:S(2)}) collective-permute-start(bf16[4,256,128]{2,1,0:T(8,128)(2,1)S(1)} %get-tuple-element.65.own), channel_id=1, source_target_pairs={{8,16},{9,17},{10,18},{11,19},{12,20},{13,21},{14,22},{15,23},{16,... | collective-permute-start | bytes 786440 | tf_op jit(solution)/shard_map/ppermute | solution.py:56
  52.5 10.1 %collective-permute-start.20 = (bf16[4,256,128]{2,1,0:T(8,128)(2,1)S(1)}, bf16[4,256,128]{2,1,0:T(8,128)(2,1)S(1)}, u32[]{:S(2)}, u32[]{:S(2)}) collective-permute-start(bf16[4,256,128]{2,1,0:T(8,128)(2,1)S(1)} %get-tuple-element.65.own), channel_id=1, source_target_pairs={{0,8},{1,9},{2,10},{3,11},{4,12},{5,13},{6,14},{7,15},{8,0},{9,1},... | collective-permute-start | bytes 786440 | tf_op jit(solution)/shard_map/ppermute | solution.py:56
  64.6 4.3 %collective-permute-start.22 = (bf16[128,256]{1,0:T(8,128)(2,1)S(1)}, bf16[128,256]{1,0:T(8,128)(2,1)S(1)}, u32[]{:S(2)}, u32[]{:S(2)}) collective-permute-start(bf16[128,256]{1,0:T(8,128)(2,1)S(1)} %get-tuple-element.68), channel_id=1, source_target_pairs={{0,1},{1,0},{2,3},{3,2},{4,5},{5,4},{6,7},{7,6},{8,9},{9,8},{10,11... | collective-permute-start | bytes 196616 | tf_op jit(solution)/shard_map/ppermute | solution.py:56
  65.9 5.0 %collective-permute-start.23 = (bf16[128,256]{1,0:T(8,128)(2,1)S(1)}, bf16[128,256]{1,0:T(8,128)(2,1)S(1)}, u32[]{:S(2)}, u32[]{:S(2)}) collective-permute-start(bf16[128,256]{1,0:T(8,128)(2,1)S(1)} %get-tuple-element.69), channel_id=1, source_target_pairs={{0,2},{1,3},{2,0},{3,1},{4,6},{5,7},{6,4},{7,5},{8,10},{9,11},{10,... | collective-permute-start | bytes 196616 | tf_op jit(solution)/shard_map/ppermute | solution.py:56
  66.4 5.2 %collective-permute-start.24 = (bf16[128,256]{1,0:T(8,128)(2,1)S(1)}, bf16[128,256]{1,0:T(8,128)(2,1)S(1)}, u32[]{:S(2)}, u32[]{:S(2)}) collective-permute-start(bf16[128,256]{1,0:T(8,128)(2,1)S(1)} %get-tuple-element.70), channel_id=1, source_target_pairs={{0,3},{1,2},{2,1},{3,0},{4,7},{5,6},{6,5},{7,4},{8,11},{9,10},{10,... | collective-permute-start | bytes 196616 | tf_op jit(solution)/shard_map/ppermute | solution.py:56
  (7 other events, 36.9 us)

commit v16 on v15

--- a/solution.py
+++ b/solution.py
@@ -273,7 +273,7 @@
         ref[:, HD:] = other[r + 1]
 
 
-def gather_kernel(mine, other, x, y, diagonal, out_ref):
+def gather_kernel(mine, other, diagonal, x, y, out_ref):
     _, core, depth = where_am_i()
     pairs = [(mine[0], other[0])] + [(ref[:, :HD], ref[:, HD:]) for ref in (x, y, diagonal)]
     for r, pair in enumerate(pairs):
@@ -382,7 +382,7 @@
     received = swap_core(sent)
     x, y, across = call(pair_kernel, (array(block, PAIR),) * 3, "vv")(kept, received)
     across, x, y = swap_depth(across, 3), swap_depth(x, 1), swap_depth(y, 2)
-    context = call(gather_kernel, array(block, HEADS * HD), "v" * 5)(kept, received, x, y, across)
+    context = call(gather_kernel, array(block, HEADS * HD), "v" * 5)(kept, received, across, x, y)
     return context.reshape(time_len, site_len, HEADS * HD)
 
 

time: 72.7 us -> 72.2 us (level)
  transfers between devices with their start and end apart: 25 -> 25, of which waited for: 19 -> 18; matrix products, arithmetic and copies ran while one was open for 2% -> 2% of each run, Pallas kernels for 8% -> 8%
where the time goes in v16:
time: 72.2 us; the launch traced here: 71.9 us
  starting transfers between devices  30.9 us (43%)
  waiting for transfers between devices  28.2 us (39%)
  Pallas kernels  7.89 us (11%)
  local copies, waits for them, and re-layouts  3.26 us (5%)
  other arithmetic  1.52 us (2%)
    ppermute x25, starting transfers between devices, hop(): return lax.ppermute(value, ('tm', 'depth'), pairs)  30.9 us
    ppermute x25, waiting for transfers between devices, hop(): return lax.ppermute(value, ('tm', 'depth'), pairs)  28.2 us
    unnamed x13, local copies, waits for them, and re-layouts  3.13 us
    pallas_call x3, Pallas kernels, embed(): call(functools.partial(embed_kernel, rs, len(finished)), out, 'v' * (6 +...  2.38 us
  transfers between devices with their start and end apart: 25, of which 18 were waited for; matrix products, arithmetic and copies ran while one was open for 2% of the time, Pallas kernels for 8%

profile of v16, /device:TPU:0, one launch (start us, length us, event | category | flops | bytes accessed | tf_op | source)
XLA Modules:
  0.0 71.9 jit_solution(1369820756413477051)
XLA Ops:
  0.0 4.0 %collective-permute-start = (bf16[256,768]{1,0:T(8,128)(2,1)}, bf16[256,768]{1,0:T(8,128)(2,1)S(1)}, u32[]{:S(2)}, u32[]{:S(2)}) collective-permute-start(bf16[256,768]{1,0:T(8,128)(2,1)} %w.1), channel_id=1, source_target_pairs={{0,16},{1,17},{2,18},{3,19},{4,20},{5,21},{6,22},{7,23},{8,24},{9,... | collective-permute-start | bytes 1179656 | tf_op jit(solution)/shard_map/ppermute | solution.py:56
  6.5 2.5 %collective-permute-start.3 = (bf16[128,256]{1,0:T(8,128)(2,1)S(1)}, bf16[128,256]{1,0:T(8,128)(2,1)S(1)}, u32[]{:S(2)}, u32[]{:S(2)}) collective-permute-start(bf16[128,256]{1,0:T(8,128)(2,1)S(1)} %get-tuple-element.40), channel_id=1, source_target_pairs={{0,3},{1,2},{2,1},{3,0},{4,7},{5,6},{6,5},{7,4},{8,11},{9,10},{10,... | collective-permute-start | bytes 196616 | tf_op jit(solution)/shard_map/ppermute | solution.py:56
  10.1 2.4 %collective-permute-done.3.across = bf16[128,256]{1,0:T(8,128)(2,1)S(1)} collective-permute-done((bf16[128,256]{1,0:T(8,128)(2,1)S(1)}, bf16[128,256]{1,0:T(8,128)(2,1)S(1)}, u32[]{:S(2)}, u32[]{:S(2)}) %collective-permute-start.3) | collective-permute-done | bytes 65568 | tf_op jit(solution)/shard_map/ppermute | solution.py:56
  12.5 1.5 %collective-permute-start.7 = (bf16[128,2048]{1,0:T(8,128)(2,1)}, bf16[128,2048]{1,0:T(8,128)(2,1)S(1)}, u32[]{:S(2)}, u32[]{:S(2)}) collective-permute-start(bf16[128,2048]{1,0:T(8,128)(2,1)} %bitcast.12), channel_id=1, source_target_pairs={{0,2},{1,3},{2,0},{3,1},{4,6},{5,7},{6,4},{7,5},{8,10},{9,11},{10,... | collective-permute-start | bytes 1572872 | tf_op jit(solution)/shard_map/ppermute | solution.py:56
  14.0 1.5 %collective-permute-start.6 = (bf16[128,2048]{1,0:T(8,128)(2,1)}, bf16[128,2048]{1,0:T(8,128)(2,1)S(1)}, u32[]{:S(2)}, u32[]{:S(2)}) collective-permute-start(bf16[128,2048]{1,0:T(8,128)(2,1)} %bitcast.13), channel_id=1, source_target_pairs={{0,1},{1,0},{2,3},{3,2},{4,5},{5,4},{6,7},{7,6},{8,9},{9,8},{10,11... | collective-permute-start | bytes 1572872 | tf_op jit(solution)/shard_map/ppermute | solution.py:56
  17.0 1.6 %collective-permute-start.8 = (bf16[256,768]{1,0:T(8,128)(2,1)S(1)}, bf16[256,768]{1,0:T(8,128)(2,1)S(1)}, u32[]{:S(2)}, u32[]{:S(2)}) collective-permute-start(bf16[256,768]{1,0:T(8,128)(2,1)S(1)} %shard_map.67.refs_2_.refs_0_), channel_id=1, source_target_pairs={{0,8},{1,9},{2,10},{3,11},{4,12},{5,13},{6,14},{7,15},{8,0},{9,1},... | collective-permute-start | bytes 1179656 | tf_op jit(solution)/shard_map/ppermute | solution.py:56
  18.6 1.4 %copy-done = bf16[3,128,2048]{2,1,0:T(8,128)(2,1)S(1)} copy-done((bf16[3,128,2048]{2,1,0:T(8,128)(2,1)S(1)}, bf16[3,128,2048]{2,1,0:T(8,128)(2,1)}, u32[]{:S(2)}) %copy-start) | copy-done | bytes 1572888
  21.9 1.6 %collective-permute-start.4 = (bf16[256,256]{1,0:T(8,128)(2,1)S(1)}, bf16[256,256]{1,0:T(8,128)(2,1)S(1)}, u32[]{:S(2)}, u32[]{:S(2)}) collective-permute-start(bf16[256,256]{1,0:T(8,128)(2,1)S(1)} %get-tuple-element.72), channel_id=1, source_target_pairs={{0,1},{1,0},{2,3},{3,2},{4,5},{5,4},{6,7},{7,6},{8,9},{9,8},{10,11... | collective-permute-start | bytes 393224 | tf_op jit(solution)/shard_map/ppermute | solution.py:56
  23.5 1.5 %collective-permute-start.5 = (bf16[256,256]{1,0:T(8,128)(2,1)S(1)}, bf16[256,256]{1,0:T(8,128)(2,1)S(1)}, u32[]{:S(2)}, u32[]{:S(2)}) collective-permute-start(bf16[256,256]{1,0:T(8,128)(2,1)S(1)} %get-tuple-element.71), channel_id=1, source_target_pairs={{0,2},{1,3},{2,0},{3,1},{4,6},{5,7},{6,4},{7,5},{8,10},{9,11},{10,... | collective-permute-start | bytes 393224 | tf_op jit(solution)/shard_map/ppermute | solution.py:56
  25.1 3.1 %collective-permute-done.7.refs_1_ = bf16[128,2048]{1,0:T(8,128)(2,1)S(1)} collective-permute-done((bf16[128,2048]{1,0:T(8,128)(2,1)}, bf16[128,2048]{1,0:T(8,128)(2,1)S(1)}, u32[]{:S(2)}, u32[]{:S(2)}) %collective-permute-start.7) | collective-permute-done | bytes 524320 | tf_op jit(solution)/shard_map/ppermute | solution.py:56
  30.4 1.4 %collective-permute-done.9 = bf16[256,384]{1,0:T(8,128)(2,1)S(1)} collective-permute-done((bf16[256,384]{1,0:T(8,128)(2,1)S(1)}, bf16[256,384]{1,0:T(8,128)(2,1)S(1)}, u32[]{:S(2)}, u32[]{:S(2)}) %collective-permute-start.9) | collective-permute-done | bytes 196640 | tf_op jit(solution)/shard_map/ppermute | solution.py:56
  32.6 1.6 %collective-permute-start.11 = (bf16[128,1024]{1,0:T(8,128)(2,1)S(1)}, bf16[128,1024]{1,0:T(8,128)(2,1)S(1)}, u32[]{:S(2)}, u32[]{:S(2)}) collective-permute-start(bf16[128,1024]{1,0:T(8,128)(2,1)S(1)} %get-tuple-element.54), channel_id=1, source_target_pairs={{0,2},{1,3},{2,0},{3,1},{4,6},{5,7},{6,4},{7,5},{8,10},{9,11},{10,... | collective-permute-start | bytes 786440 | tf_op jit(solution)/shard_map/ppermute | solution.py:56
  34.2 1.5 %collective-permute-start.13 = (bf16[128,1024]{1,0:T(8,128)(2,1)S(1)}, bf16[128,1024]{1,0:T(8,128)(2,1)S(1)}, u32[]{:S(2)}, u32[]{:S(2)}) collective-permute-start(bf16[128,1024]{1,0:T(8,128)(2,1)S(1)} %get-tuple-element.59), channel_id=1, source_target_pairs={{0,1},{1,0},{2,3},{3,2},{4,5},{5,4},{6,7},{7,6},{8,9},{9,8},{10,11... | collective-permute-start | bytes 786440 | tf_op jit(solution)/shard_map/ppermute | solution.py:56
  35.9 1.4 %shard_map.69.refs_4_ = f32[768,384]{1,0:T(8,128)S(1)} custom-call(bf16[384,2048]{1,0:T(8,128)(2,1)S(1)} %get-tuple-element.53.refs_0_, bf16[384,2048]{1,0:T(8,128)(2,1)S(1)} %collective-permute-done.10.refs_1_, bf16[256,768]{1,0:T(8,128)(2,1)S(1)} %shard_map.67.refs_2_.refs_0_, bf16[256,768]{1,0:T(8,128)(2,1)S(1)} %collective-permute-done.8.refs_3_.refs_1_, ...), custom_call_target="tpu_custom_call" | custom-call | flops 905969664 | tf_op jit(solution)/shard_map/pallas_call | solution.py:359
  37.3 3.6 %collective-permute-done.11 = bf16[128,1024]{1,0:T(8,128)(2,1)S(1)} collective-permute-done((bf16[128,1024]{1,0:T(8,128)(2,1)S(1)}, bf16[128,1024]{1,0:T(8,128)(2,1)S(1)}, u32[]{:S(2)}, u32[]{:S(2)}) %collective-permute-start.11) | collective-permute-done | bytes 262176 | tf_op jit(solution)/shard_map/ppermute | solution.py:56
  41.0 1.3 %collective-permute-done.13 = bf16[128,1024]{1,0:T(8,128)(2,1)S(1)} collective-permute-done((bf16[128,1024]{1,0:T(8,128)(2,1)S(1)}, bf16[128,1024]{1,0:T(8,128)(2,1)S(1)}, u32[]{:S(2)}, u32[]{:S(2)}) %collective-permute-start.13) | collective-permute-done | bytes 262176 | tf_op jit(solution)/shard_map/ppermute | solution.py:56
  43.6 1.3 %collective-permute-done.15.bottom = bf16[48,2048]{1,0:T(8,128)(2,1)S(1)} collective-permute-done((bf16[48,2048]{1,0:T(8,128)(2,1)S(1)}, bf16[48,2048]{1,0:T(8,128)(2,1)S(1)}, u32[]{:S(2)}, u32[]{:S(2)}) %collective-permute-start.15) | collective-permute-done | bytes 196640 | tf_op jit(solution)/shard_map/ppermute | solution.py:56
  47.7 4.2 %collective-permute-start.18 = (bf16[4,256,128]{2,1,0:T(8,128)(2,1)S(1)}, bf16[4,256,128]{2,1,0:T(8,128)(2,1)S(1)}, u32[]{:S(2)}, u32[]{:S(2)}) collective-permute-start(bf16[4,256,128]{2,1,0:T(8,128)(2,1)S(1)} %get-tuple-element.64.own), channel_id=1, source_target_pairs={{0,8},{1,9},{2,10},{3,11},{4,12},{5,13},{6,14},{7,15},{8,0},{9,1},... | collective-permute-start | bytes 786440 | tf_op jit(solution)/shard_map/ppermute | solution.py:56
  52.5 1.8 %collective-permute-start.20 = (bf16[4,256,128]{2,1,0:T(8,128)(2,1)S(1)}, bf16[4,256,128]{2,1,0:T(8,128)(2,1)S(1)}, u32[]{:S(2)}, u32[]{:S(2)}) collective-permute-start(bf16[4,256,128]{2,1,0:T(8,128)(2,1)S(1)} %get-tuple-element.65.own), channel_id=1, source_target_pairs={{0,8},{1,9},{2,10},{3,11},{4,12},{5,13},{6,14},{7,15},{8,0},{9,1},... | collective-permute-start | bytes 786440 | tf_op jit(solution)/shard_map/ppermute | solution.py:56
  54.3 4.7 %collective-permute-done.18.outer = bf16[4,256,128]{2,1,0:T(8,128)(2,1)S(1)} collective-permute-done((bf16[4,256,128]{2,1,0:T(8,128)(2,1)S(1)}, bf16[4,256,128]{2,1,0:T(8,128)(2,1)S(1)}, u32[]{:S(2)}, u32[]{:S(2)}) %collective-permute-start.18) | collective-permute-done | bytes 262176 | tf_op jit(solution)/shard_map/ppermute | solution.py:56
  60.3 2.4 %collective-permute-done.20.outer = bf16[4,256,128]{2,1,0:T(8,128)(2,1)S(1)} collective-permute-done((bf16[4,256,128]{2,1,0:T(8,128)(2,1)S(1)}, bf16[4,256,128]{2,1,0:T(8,128)(2,1)S(1)}, u32[]{:S(2)}, u32[]{:S(2)}) %collective-permute-start.20) | collective-permute-done | bytes 262176 | tf_op jit(solution)/shard_map/ppermute | solution.py:56
  63.2 1.3 %collective-permute-done.21.other = bf16[4,128,128]{2,1,0:T(8,128)(2,1)S(1)} collective-permute-done((bf16[4,128,128]{2,1,0:T(8,128)(2,1)S(1)}, bf16[4,128,128]{2,1,0:T(8,128)(2,1)S(1)}, u32[]{:S(2)}, u32[]{:S(2)}) %collective-permute-start.21) | collective-permute-done | bytes 131104 | tf_op jit(solution)/shard_map/ppermute | solution.py:56
  66.7 1.5 %collective-permute-start.24 = (bf16[128,256]{1,0:T(8,128)(2,1)S(1)}, bf16[128,256]{1,0:T(8,128)(2,1)S(1)}, u32[]{:S(2)}, u32[]{:S(2)}) collective-permute-start(bf16[128,256]{1,0:T(8,128)(2,1)S(1)} %get-tuple-element.70), channel_id=1, source_target_pairs={{0,2},{1,3},{2,0},{3,1},{4,6},{5,7},{6,4},{7,5},{8,10},{9,11},{10,... | collective-permute-start | bytes 196616 | tf_op jit(solution)/shard_map/ppermute | solution.py:56
  68.2 2.3 %collective-permute-done.22.diagonal = bf16[128,256]{1,0:T(8,128)(2,1)S(1)} collective-permute-done((bf16[128,256]{1,0:T(8,128)(2,1)S(1)}, bf16[128,256]{1,0:T(8,128)(2,1)S(1)}, u32[]{:S(2)}, u32[]{:S(2)}) %collective-permute-start.22) | collective-permute-done | bytes 65568 | tf_op jit(solution)/shard_map/ppermute | solution.py:56
  (64 shorter events, 20.2 us)
Async XLA Ops:
  0.0 21.9 %collective-permute-start = (bf16[256,768]{1,0:T(8,128)(2,1)}, bf16[256,768]{1,0:T(8,128)(2,1)S(1)}, u32[]{:S(2)}, u32[]{:S(2)}) collective-permute-start(bf16[256,768]{1,0:T(8,128)(2,1)} %w.1), channel_id=1, source_target_pairs={{0,16},{1,17},{2,18},{3,19},{4,20},{5,21},{6,22},{7,23},{8,24},{9,... | collective-permute-start | bytes 1179656 | tf_op jit(solution)/shard_map/ppermute | solution.py:56
  6.5 5.9 %collective-permute-start.3 = (bf16[128,256]{1,0:T(8,128)(2,1)S(1)}, bf16[128,256]{1,0:T(8,128)(2,1)S(1)}, u32[]{:S(2)}, u32[]{:S(2)}) collective-permute-start(bf16[128,256]{1,0:T(8,128)(2,1)S(1)} %get-tuple-element.40), channel_id=1, source_target_pairs={{0,3},{1,2},{2,1},{3,0},{4,7},{5,6},{6,5},{7,4},{8,11},{9,10},{10,... | collective-permute-start | bytes 196616 | tf_op jit(solution)/shard_map/ppermute | solution.py:56
  9.0 7.3 %collective-permute-start.1 = (bf16[336,256]{1,0:T(8,128)(2,1)S(1)}, bf16[336,256]{1,0:T(8,128)(2,1)S(1)}, u32[]{:S(2)}, u32[]{:S(2)}) collective-permute-start(bf16[336,256]{1,0:T(8,128)(2,1)S(1)} %get-tuple-element.38), channel_id=1, source_target_pairs={{0,1},{1,0},{2,3},{3,2},{4,5},{5,4},{6,7},{7,6},{8,9},{9,8},{10,11... | collective-permute-start | bytes 516104 | tf_op jit(solution)/shard_map/ppermute | solution.py:56
  9.6 7.3 %collective-permute-start.2 = (bf16[336,256]{1,0:T(8,128)(2,1)S(1)}, bf16[336,256]{1,0:T(8,128)(2,1)S(1)}, u32[]{:S(2)}, u32[]{:S(2)}) collective-permute-start(bf16[336,256]{1,0:T(8,128)(2,1)S(1)} %get-tuple-element.39), channel_id=1, source_target_pairs={{0,2},{1,3},{2,0},{3,1},{4,6},{5,7},{6,4},{7,5},{8,10},{9,11},{10,... | collective-permute-start | bytes 516104 | tf_op jit(solution)/shard_map/ppermute | solution.py:56
  12.5 15.7 %collective-permute-start.7 = (bf16[128,2048]{1,0:T(8,128)(2,1)}, bf16[128,2048]{1,0:T(8,128)(2,1)S(1)}, u32[]{:S(2)}, u32[]{:S(2)}) collective-permute-start(bf16[128,2048]{1,0:T(8,128)(2,1)} %bitcast.12), channel_id=1, source_target_pairs={{0,2},{1,3},{2,0},{3,1},{4,6},{5,7},{6,4},{7,5},{8,10},{9,11},{10,... | collective-permute-start | bytes 1572872 | tf_op jit(solution)/shard_map/ppermute | solution.py:56
  14.0 14.2 %collective-permute-start.6 = (bf16[128,2048]{1,0:T(8,128)(2,1)}, bf16[128,2048]{1,0:T(8,128)(2,1)S(1)}, u32[]{:S(2)}, u32[]{:S(2)}) collective-permute-start(bf16[128,2048]{1,0:T(8,128)(2,1)} %bitcast.13), channel_id=1, source_target_pairs={{0,1},{1,0},{2,3},{3,2},{4,5},{5,4},{6,7},{7,6},{8,9},{9,8},{10,11... | collective-permute-start | bytes 1572872 | tf_op jit(solution)/shard_map/ppermute | solution.py:56
  17.0 13.2 %collective-permute-start.8 = (bf16[256,768]{1,0:T(8,128)(2,1)S(1)}, bf16[256,768]{1,0:T(8,128)(2,1)S(1)}, u32[]{:S(2)}, u32[]{:S(2)}) collective-permute-start(bf16[256,768]{1,0:T(8,128)(2,1)S(1)} %shard_map.67.refs_2_.refs_0_), channel_id=1, source_target_pairs={{0,8},{1,9},{2,10},{3,11},{4,12},{5,13},{6,14},{7,15},{8,0},{9,1},... | collective-permute-start | bytes 1179656 | tf_op jit(solution)/shard_map/ppermute | solution.py:56
  21.9 7.4 %collective-permute-start.4 = (bf16[256,256]{1,0:T(8,128)(2,1)S(1)}, bf16[256,256]{1,0:T(8,128)(2,1)S(1)}, u32[]{:S(2)}, u32[]{:S(2)}) collective-permute-start(bf16[256,256]{1,0:T(8,128)(2,1)S(1)} %get-tuple-element.72), channel_id=1, source_target_pairs={{0,1},{1,0},{2,3},{3,2},{4,5},{5,4},{6,7},{7,6},{8,9},{9,8},{10,11... | collective-permute-start | bytes 393224 | tf_op jit(solution)/shard_map/ppermute | solution.py:56
  23.5 6.0 %collective-permute-start.5 = (bf16[256,256]{1,0:T(8,128)(2,1)S(1)}, bf16[256,256]{1,0:T(8,128)(2,1)S(1)}, u32[]{:S(2)}, u32[]{:S(2)}) collective-permute-start(bf16[256,256]{1,0:T(8,128)(2,1)S(1)} %get-tuple-element.71), channel_id=1, source_target_pairs={{0,2},{1,3},{2,0},{3,1},{4,6},{5,7},{6,4},{7,5},{8,10},{9,11},{10,... | collective-permute-start | bytes 393224 | tf_op jit(solution)/shard_map/ppermute | solution.py:56
  30.3 1.5 %collective-permute-start.9 = (bf16[256,384]{1,0:T(8,128)(2,1)S(1)}, bf16[256,384]{1,0:T(8,128)(2,1)S(1)}, u32[]{:S(2)}, u32[]{:S(2)}) collective-permute-start(bf16[256,384]{1,0:T(8,128)(2,1)S(1)} %get-tuple-element.50), channel_id=1, source_target_pairs={{0,4},{1,5},{2,6},{3,7},{4,0},{5,1},{6,2},{7,3},{8,12},{9,13},{10,... | collective-permute-start | bytes 589832 | tf_op jit(solution)/shard_map/ppermute | solution.py:56
  31.9 4.1 %collective-permute-start.10 = (bf16[384,2048]{1,0:T(8,128)(2,1)S(1)}, bf16[384,2048]{1,0:T(8,128)(2,1)S(1)}, u32[]{:S(2)}, u32[]{:S(2)}) collective-permute-start(bf16[384,2048]{1,0:T(8,128)(2,1)S(1)} %get-tuple-element.53.refs_0_), channel_id=1, source_target_pairs={{0,4},{1,5},{2,6},{3,7},{4,0},{5,1},{6,2},{7,3},{8,12},{9,13},{10,... | collective-permute-start | bytes 4718600 | tf_op jit(solution)/shard_map/ppermute | solution.py:56
  32.2 3.7 %collective-permute-start.12 = (bf16[528,384]{1,0:T(8,128)(2,1)S(1)}, bf16[528,384]{1,0:T(8,128)(2,1)S(1)}, u32[]{:S(2)}, u32[]{:S(2)}) collective-permute-start(bf16[528,384]{1,0:T(8,128)(2,1)S(1)} %pad_maximum_fusion.1), channel_id=1, source_target_pairs={{0,4},{1,5},{2,6},{3,7},{4,0},{5,1},{6,2},{7,3},{8,12},{9,13},{10,... | collective-permute-start | bytes 1216520 | tf_op jit(solution)/shard_map/ppermute | solution.py:56
  32.6 8.3 %collective-permute-start.11 = (bf16[128,1024]{1,0:T(8,128)(2,1)S(1)}, bf16[128,1024]{1,0:T(8,128)(2,1)S(1)}, u32[]{:S(2)}, u32[]{:S(2)}) collective-permute-start(bf16[128,1024]{1,0:T(8,128)(2,1)S(1)} %get-tuple-element.54), channel_id=1, source_target_pairs={{0,2},{1,3},{2,0},{3,1},{4,6},{5,7},{6,4},{7,5},{8,10},{9,11},{10,... | collective-permute-start | bytes 786440 | tf_op jit(solution)/shard_map/ppermute | solution.py:56
  34.2 8.1 %collective-permute-start.13 = (bf16[128,1024]{1,0:T(8,128)(2,1)S(1)}, bf16[128,1024]{1,0:T(8,128)(2,1)S(1)}, u32[]{:S(2)}, u32[]{:S(2)}) collective-permute-start(bf16[128,1024]{1,0:T(8,128)(2,1)S(1)} %get-tuple-element.59), channel_id=1, source_target_pairs={{0,1},{1,0},{2,3},{3,2},{4,5},{5,4},{6,7},{7,6},{8,9},{9,8},{10,11... | collective-permute-start | bytes 786440 | tf_op jit(solution)/shard_map/ppermute | solution.py:56
  35.7 10.6 %collective-permute-start.16 = (bf16[512,384]{1,0:T(8,128)(2,1)S(1)}, bf16[512,384]{1,0:T(8,128)(2,1)S(1)}, u32[]{:S(2)}, u32[]{:S(2)}) collective-permute-start(bf16[512,384]{1,0:T(8,128)(2,1)S(1)} %constant_dynamic-update-slice_fusion.refs_5_.refs_3_), channel_id=1, source_target_pairs={{0,8},{1,9},{2,10},{3,11},{4,12},{5,13},{6,14},{7,15},{8,0},{9,1},... | collective-permute-start | bytes 1179656 | tf_op jit(solution)/shard_map/ppermute | solution.py:56
  43.0 2.0 %collective-permute-start.14 = (bf16[80,2048]{1,0:T(8,128)(2,1)S(1)}, bf16[80,2048]{1,0:T(8,128)(2,1)S(1)}, u32[]{:S(2)}, u32[]{:S(2)}) collective-permute-start(bf16[80,2048]{1,0:T(8,128)(2,1)S(1)} %slice.29), channel_id=1, source_target_pairs={{0,4},{1,5},{2,6},{3,7},{4,0},{5,1},{6,2},{7,3},{8,12},{9,13},{10,... | collective-permute-start | bytes 983048 | tf_op jit(solution)/shard_map/ppermute | solution.py:56
  43.1 1.9 %collective-permute-start.15 = (bf16[48,2048]{1,0:T(8,128)(2,1)S(1)}, bf16[48,2048]{1,0:T(8,128)(2,1)S(1)}, u32[]{:S(2)}, u32[]{:S(2)}) collective-permute-start(bf16[48,2048]{1,0:T(8,128)(2,1)S(1)} %slice.30), channel_id=1, source_target_pairs={{0,4},{1,5},{2,6},{3,7},{4,0},{5,1},{6,2},{7,3},{8,12},{9,13},{10,... | collective-permute-start | bytes 589832 | tf_op jit(solution)/shard_map/ppermute | solution.py:56
  47.0 7.3 %collective-permute-start.17 = (bf16[4,256,128]{2,1,0:T(8,128)(2,1)S(1)}, bf16[4,256,128]{2,1,0:T(8,128)(2,1)S(1)}, u32[]{:S(2)}, u32[]{:S(2)}) collective-permute-start(bf16[4,256,128]{2,1,0:T(8,128)(2,1)S(1)} %get-tuple-element.64.own), channel_id=1, source_target_pairs={{8,16},{9,17},{10,18},{11,19},{12,20},{13,21},{14,22},{15,23},{16,... | collective-permute-start | bytes 786440 | tf_op jit(solution)/shard_map/ppermute | solution.py:56
  47.7 11.4 %collective-permute-start.18 = (bf16[4,256,128]{2,1,0:T(8,128)(2,1)S(1)}, bf16[4,256,128]{2,1,0:T(8,128)(2,1)S(1)}, u32[]{:S(2)}, u32[]{:S(2)}) collective-permute-start(bf16[4,256,128]{2,1,0:T(8,128)(2,1)S(1)} %get-tuple-element.64.own), channel_id=1, source_target_pairs={{0,8},{1,9},{2,10},{3,11},{4,12},{5,13},{6,14},{7,15},{8,0},{9,1},... | collective-permute-start | bytes 786440 | tf_op jit(solution)/shard_map/ppermute | solution.py:56
  51.9 8.4 %collective-permute-start.19 = (bf16[4,256,128]{2,1,0:T(8,128)(2,1)S(1)}, bf16[4,256,128]{2,1,0:T(8,128)(2,1)S(1)}, u32[]{:S(2)}, u32[]{:S(2)}) collective-permute-start(bf16[4,256,128]{2,1,0:T(8,128)(2,1)S(1)} %get-tuple-element.65.own), channel_id=1, source_target_pairs={{8,16},{9,17},{10,18},{11,19},{12,20},{13,21},{14,22},{15,23},{16,... | collective-permute-start | bytes 786440 | tf_op jit(solution)/shard_map/ppermute | solution.py:56
  52.5 10.1 %collective-permute-start.20 = (bf16[4,256,128]{2,1,0:T(8,128)(2,1)S(1)}, bf16[4,256,128]{2,1,0:T(8,128)(2,1)S(1)}, u32[]{:S(2)}, u32[]{:S(2)}) collective-permute-start(bf16[4,256,128]{2,1,0:T(8,128)(2,1)S(1)} %get-tuple-element.65.own), channel_id=1, source_target_pairs={{0,8},{1,9},{2,10},{3,11},{4,12},{5,13},{6,14},{7,15},{8,0},{9,1},... | collective-permute-start | bytes 786440 | tf_op jit(solution)/shard_map/ppermute | solution.py:56
  64.6 5.8 %collective-permute-start.22 = (bf16[128,256]{1,0:T(8,128)(2,1)S(1)}, bf16[128,256]{1,0:T(8,128)(2,1)S(1)}, u32[]{:S(2)}, u32[]{:S(2)}) collective-permute-start(bf16[128,256]{1,0:T(8,128)(2,1)S(1)} %get-tuple-element.68), channel_id=1, source_target_pairs={{0,3},{1,2},{2,1},{3,0},{4,7},{5,6},{6,5},{7,4},{8,11},{9,10},{10,... | collective-permute-start | bytes 196616 | tf_op jit(solution)/shard_map/ppermute | solution.py:56
  65.9 4.6 %collective-permute-start.23 = (bf16[128,256]{1,0:T(8,128)(2,1)S(1)}, bf16[128,256]{1,0:T(8,128)(2,1)S(1)}, u32[]{:S(2)}, u32[]{:S(2)}) collective-permute-start(bf16[128,256]{1,0:T(8,128)(2,1)S(1)} %get-tuple-element.69), channel_id=1, source_target_pairs={{0,1},{1,0},{2,3},{3,2},{4,5},{5,4},{6,7},{7,6},{8,9},{9,8},{10,11... | collective-permute-start | bytes 196616 | tf_op jit(solution)/shard_map/ppermute | solution.py:56
  66.7 4.5 %collective-permute-start.24 = (bf16[128,256]{1,0:T(8,128)(2,1)S(1)}, bf16[128,256]{1,0:T(8,128)(2,1)S(1)}, u32[]{:S(2)}, u32[]{:S(2)}) collective-permute-start(bf16[128,256]{1,0:T(8,128)(2,1)S(1)} %get-tuple-element.70), channel_id=1, source_target_pairs={{0,2},{1,3},{2,0},{3,1},{4,6},{5,7},{6,4},{7,5},{8,10},{9,11},{10,... | collective-permute-start | bytes 196616 | tf_op jit(solution)/shard_map/ppermute | solution.py:56
  (7 other events, 36.9 us)

commit v17 on v11

--- a/solution.py
+++ b/solution.py
@@ -234,7 +234,7 @@
     return jnp.where(odd, outer, middle), own[index], jnp.where(odd, middle, outer)
 
 
-def weigh_kernel(q_ref, outer, own, middle, own_flags, received, out_ref):
+def weigh_kernel(q_ref, middle, own, outer, own_flags, received, out_ref):
     _, core, _ = where_am_i()
     block = q_ref.shape[1] // 2
     inv_root = 1.0 / math.sqrt(HD)
@@ -261,7 +261,7 @@
                 out_ref[r, u * block : (u + 1) * block, here] = (p * inverse).astype(jnp.bfloat16)
 
 
-def mix_kernel(r, weights, outer, own, middle, out_ref):
+def mix_kernel(r, weights, middle, own, outer, out_ref):
     block = weights.shape[1] // 2
     values = neighbours(outer, own, middle, V_ORDER.index(r) % 2)
     for u in range(2):
@@ -377,9 +377,9 @@
     )(*early, diagonal, last, total, total_diagonal)
 
     weights = call(weigh_kernel, array(4, 2 * block, 5 * block), "v" * 6, macs=8 * block * 5 * block * HD)(
-        q, swap_z(k, 1), k, swap_middle(k), flags, received
-    )
-    values = [(swap_z(t, 1), t, swap_middle(t)) for t in v]
+        q, swap_middle(k), k, swap_z(k, 1), flags, received
+    )
+    values = [(swap_middle(t), t, swap_z(t, 1)) for t in v]
     pieces = {}
     for r in V_ORDER:
         mixed = call(functools.partial(mix_kernel, r), array(2 * block, HD), "vvvv", macs=2 * block * 5 * block * HD)(

time: 71.4 us -> 71.7 us (level)
  transfers between devices with their start and end apart: 27 -> 27, of which waited for: 16 -> 18; matrix products, arithmetic and copies ran while one was open for 0% -> 0% of each run, Pallas kernels for 10% -> 10%
where the time goes in v17:
time: 71.7 us; the launch traced here: 70.4 us
  starting transfers between devices  35.1 us (49%)
  waiting for transfers between devices  20.7 us (29%)
  Pallas kernels  8.82 us (12%)
  local copies, waits for them, and re-layouts  5.41 us (8%)
    ppermute x27, starting transfers between devices, hop(): return lax.ppermute(value, ('tm', 'depth'), pairs)  35.1 us
    ppermute x27, waiting for transfers between devices, hop(): return lax.ppermute(value, ('tm', 'depth'), pairs)  20.7 us
    unnamed x21, local copies, waits for them, and re-layouts  5.3 us
    pallas_call x3, Pallas kernels, embed(): call(functools.partial(embed_kernel, rs, len(finished)), out, 'v' * (6 +...  2.35 us
  transfers between devices with their start and end apart: 27, of which 18 were waited for; matrix products, arithmetic and copies ran while one was open for 0% of the time, Pallas kernels for 10%

profile of v17, /device:TPU:9, one launch (start us, length us, event | category | flops | bytes accessed | tf_op | source)
XLA Modules:
  0.0 70.4 jit_solution(8411550103620208568)
XLA Ops:
  0.0 2.3 %collective-permute-start = (bf16[256,768]{1,0:T(8,128)(2,1)}, bf16[256,768]{1,0:T(8,128)(2,1)S(1)}, u32[]{:S(2)}, u32[]{:S(2)}) collective-permute-start(bf16[256,768]{1,0:T(8,128)(2,1)} %w.1), channel_id=1, source_target_pairs={{0,16},{1,17},{2,18},{3,19},{4,20},{5,21},{6,22},{7,23},{8,24},{9,... | collective-permute-start | bytes 1179656 | tf_op jit(solution)/shard_map/ppermute | solution.py:57
  5.3 2.2 %collective-permute-start.3 = (bf16[128,256]{1,0:T(8,128)(2,1)S(1)}, bf16[128,256]{1,0:T(8,128)(2,1)S(1)}, u32[]{:S(2)}, u32[]{:S(2)}) collective-permute-start(bf16[128,256]{1,0:T(8,128)(2,1)S(1)} %get-tuple-element.39), channel_id=1, source_target_pairs={{0,3},{1,2},{2,1},{3,0},{4,7},{5,6},{6,5},{7,4},{8,11},{9,10},{10,... | collective-permute-start | bytes 196616 | tf_op jit(solution)/shard_map/ppermute | solution.py:57
  8.0 1.7 %collective-permute-done.3.across = bf16[128,256]{1,0:T(8,128)(2,1)S(1)} collective-permute-done((bf16[128,256]{1,0:T(8,128)(2,1)S(1)}, bf16[128,256]{1,0:T(8,128)(2,1)S(1)}, u32[]{:S(2)}, u32[]{:S(2)}) %collective-permute-start.3) | collective-permute-done | bytes 65568 | tf_op jit(solution)/shard_map/ppermute | solution.py:57
  9.7 1.2 %collective-permute-start.7 = (bf16[128,2048]{1,0:T(8,128)(2,1)}, bf16[128,2048]{1,0:T(8,128)(2,1)S(1)}, u32[]{:S(2)}, u32[]{:S(2)}) collective-permute-start(bf16[128,2048]{1,0:T(8,128)(2,1)} %bitcast.13), channel_id=1, source_target_pairs={{0,2},{1,3},{2,0},{3,1},{4,6},{5,7},{6,4},{7,5},{8,10},{9,11},{10,... | collective-permute-start | bytes 1572872 | tf_op jit(solution)/shard_map/ppermute | solution.py:57
  10.9 1.2 %collective-permute-start.6 = (bf16[128,2048]{1,0:T(8,128)(2,1)}, bf16[128,2048]{1,0:T(8,128)(2,1)S(1)}, u32[]{:S(2)}, u32[]{:S(2)}) collective-permute-start(bf16[128,2048]{1,0:T(8,128)(2,1)} %bitcast.14), channel_id=1, source_target_pairs={{0,1},{1,0},{2,3},{3,2},{4,5},{5,4},{6,7},{7,6},{8,9},{9,8},{10,11... | collective-permute-start | bytes 1572872 | tf_op jit(solution)/shard_map/ppermute | solution.py:57
  12.1 1.4 %collective-permute-done.1.plane_x.from_x = bf16[336,256]{1,0:T(8,128)(2,1)S(1)} collective-permute-done((bf16[336,256]{1,0:T(8,128)(2,1)S(1)}, bf16[336,256]{1,0:T(8,128)(2,1)S(1)}, u32[]{:S(2)}, u32[]{:S(2)}) %collective-permute-start.1) | collective-permute-done | bytes 172064 | tf_op jit(solution)/shard_map/ppermute | solution.py:57
  13.9 1.4 %copy-done = bf16[3,128,2048]{2,1,0:T(8,128)(2,1)S(1)} copy-done((bf16[3,128,2048]{2,1,0:T(8,128)(2,1)S(1)}, bf16[3,128,2048]{2,1,0:T(8,128)(2,1)}, u32[]{:S(2)}) %copy-start) | copy-done | bytes 1572888
  17.4 2.4 %collective-permute-done = bf16[256,768]{1,0:T(8,128)(2,1)S(1)} collective-permute-done((bf16[256,768]{1,0:T(8,128)(2,1)}, bf16[256,768]{1,0:T(8,128)(2,1)S(1)}, u32[]{:S(2)}, u32[]{:S(2)}) %collective-permute-start) | collective-permute-done | bytes 393248 | tf_op jit(solution)/shard_map/ppermute | solution.py:57
  19.9 1.3 %collective-permute-start.4 = (bf16[256,256]{1,0:T(8,128)(2,1)S(1)}, bf16[256,256]{1,0:T(8,128)(2,1)S(1)}, u32[]{:S(2)}, u32[]{:S(2)}) collective-permute-start(bf16[256,256]{1,0:T(8,128)(2,1)S(1)} %get-tuple-element.70), channel_id=1, source_target_pairs={{0,1},{1,0},{2,3},{3,2},{4,5},{5,4},{6,7},{7,6},{8,9},{9,8},{10,11... | collective-permute-start | bytes 393224 | tf_op jit(solution)/shard_map/ppermute | solution.py:57
  21.1 1.2 %collective-permute-start.5 = (bf16[256,256]{1,0:T(8,128)(2,1)S(1)}, bf16[256,256]{1,0:T(8,128)(2,1)S(1)}, u32[]{:S(2)}, u32[]{:S(2)}) collective-permute-start(bf16[256,256]{1,0:T(8,128)(2,1)S(1)} %get-tuple-element.69), channel_id=1, source_target_pairs={{0,2},{1,3},{2,0},{3,1},{4,6},{5,7},{6,4},{7,5},{8,10},{9,11},{10,... | collective-permute-start | bytes 393224 | tf_op jit(solution)/shard_map/ppermute | solution.py:57
  22.4 2.3 %collective-permute-done.7.refs_1_ = bf16[128,2048]{1,0:T(8,128)(2,1)S(1)} collective-permute-done((bf16[128,2048]{1,0:T(8,128)(2,1)}, bf16[128,2048]{1,0:T(8,128)(2,1)S(1)}, u32[]{:S(2)}, u32[]{:S(2)}) %collective-permute-start.7) | collective-permute-done | bytes 524320 | tf_op jit(solution)/shard_map/ppermute | solution.py:57
  26.2 1.3 %collective-permute-done.5.from_y = bf16[256,256]{1,0:T(8,128)(2,1)S(1)} collective-permute-done((bf16[256,256]{1,0:T(8,128)(2,1)S(1)}, bf16[256,256]{1,0:T(8,128)(2,1)S(1)}, u32[]{:S(2)}, u32[]{:S(2)}) %collective-permute-start.5) | collective-permute-done | bytes 131104 | tf_op jit(solution)/shard_map/ppermute | solution.py:57
  27.6 1.9 %collective-permute-start.9 = (bf16[256,384]{1,0:T(8,128)(2,1)S(1)}, bf16[256,384]{1,0:T(8,128)(2,1)S(1)}, u32[]{:S(2)}, u32[]{:S(2)}) collective-permute-start(bf16[256,384]{1,0:T(8,128)(2,1)S(1)} %get-tuple-element.50), channel_id=1, source_target_pairs={{0,4},{1,5},{2,6},{3,7},{4,0},{5,1},{6,2},{7,3},{8,12},{9,13},{10,... | collective-permute-start | bytes 589832 | tf_op jit(solution)/shard_map/ppermute | solution.py:57
  31.8 1.2 %collective-permute-start.13 = (bf16[128,1024]{1,0:T(8,128)(2,1)S(1)}, bf16[128,1024]{1,0:T(8,128)(2,1)S(1)}, u32[]{:S(2)}, u32[]{:S(2)}) collective-permute-start(bf16[128,1024]{1,0:T(8,128)(2,1)S(1)} %get-tuple-element.59), channel_id=1, source_target_pairs={{0,1},{1,0},{2,3},{3,2},{4,5},{5,4},{6,7},{7,6},{8,9},{9,8},{10,11... | collective-permute-start | bytes 786440 | tf_op jit(solution)/shard_map/ppermute | solution.py:57
  34.6 1.4 %shard_map.69.refs_4_ = f32[768,384]{1,0:T(8,128)S(1)} custom-call(bf16[384,2048]{1,0:T(8,128)(2,1)S(1)} %get-tuple-element.53.refs_0_, bf16[384,2048]{1,0:T(8,128)(2,1)S(1)} %collective-permute-done.10.refs_1_, bf16[256,768]{1,0:T(8,128)(2,1)S(1)} %shard_map.67.refs_2_.refs_0_, bf16[256,768]{1,0:T(8,128)(2,1)S(1)} %collective-permute-done.8.refs_3_.refs_1_, ...), custom_call_target="tpu_custom_call" | custom-call | flops 905969664 | tf_op jit(solution)/shard_map/pallas_call | solution.py:363
  36.0 2.8 %collective-permute-done.11 = bf16[128,1024]{1,0:T(8,128)(2,1)S(1)} collective-permute-done((bf16[128,1024]{1,0:T(8,128)(2,1)S(1)}, bf16[128,1024]{1,0:T(8,128)(2,1)S(1)}, u32[]{:S(2)}, u32[]{:S(2)}) %collective-permute-start.11) | collective-permute-done | bytes 262176 | tf_op jit(solution)/shard_map/ppermute | solution.py:57
  39.7 1.6 %collective-permute-start.14 = (bf16[80,2048]{1,0:T(8,128)(2,1)S(1)}, bf16[80,2048]{1,0:T(8,128)(2,1)S(1)}, u32[]{:S(2)}, u32[]{:S(2)}) collective-permute-start(bf16[80,2048]{1,0:T(8,128)(2,1)S(1)} %slice.29), channel_id=1, source_target_pairs={{0,4},{1,5},{2,6},{3,7},{4,0},{5,1},{6,2},{7,3},{8,12},{9,13},{10,... | collective-permute-start | bytes 983048 | tf_op jit(solution)/shard_map/ppermute | solution.py:57
  41.4 1.4 %collective-permute-done.15.bottom = bf16[48,2048]{1,0:T(8,128)(2,1)S(1)} collective-permute-done((bf16[48,2048]{1,0:T(8,128)(2,1)S(1)}, bf16[48,2048]{1,0:T(8,128)(2,1)S(1)}, u32[]{:S(2)}, u32[]{:S(2)}) %collective-permute-start.15) | collective-permute-done | bytes 196640 | tf_op jit(solution)/shard_map/ppermute | solution.py:57
  44.2 3.4 %collective-permute-start.17 = (bf16[4,256,128]{2,1,0:T(8,128)(2,1)S(1)}, bf16[4,256,128]{2,1,0:T(8,128)(2,1)S(1)}, u32[]{:S(2)}, u32[]{:S(2)}) collective-permute-start(bf16[4,256,128]{2,1,0:T(8,128)(2,1)S(1)} %get-tuple-element.64.own), channel_id=1, source_target_pairs={{8,16},{9,17},{10,18},{11,19},{12,20},{13,21},{14,22},{15,23},{16,... | collective-permute-start | bytes 786440 | tf_op jit(solution)/shard_map/ppermute | solution.py:57
  47.7 2.6 %collective-permute-start.21 = (bf16[2,256,128]{2,1,0:T(8,128)(2,1)S(1)}, bf16[2,256,128]{2,1,0:T(8,128)(2,1)S(1)}, u32[]{:S(2)}, u32[]{:S(2)}) collective-permute-start(bf16[2,256,128]{2,1,0:T(8,128)(2,1)S(1)} %get-tuple-element.66.own), channel_id=1, source_target_pairs={{8,16},{9,17},{10,18},{11,19},{12,20},{13,21},{14,22},{15,23},{16,... | collective-permute-start | bytes 393224 | tf_op jit(solution)/shard_map/ppermute | solution.py:57
  50.4 2.7 %collective-permute-start.19 = (bf16[2,256,128]{2,1,0:T(8,128)(2,1)S(1)}, bf16[2,256,128]{2,1,0:T(8,128)(2,1)S(1)}, u32[]{:S(2)}, u32[]{:S(2)}) collective-permute-start(bf16[2,256,128]{2,1,0:T(8,128)(2,1)S(1)} %get-tuple-element.65.own), channel_id=1, source_target_pairs={{8,16},{9,17},{10,18},{11,19},{12,20},{13,21},{14,22},{15,23},{16,... | collective-permute-start | bytes 393224 | tf_op jit(solution)/shard_map/ppermute | solution.py:57
  56.8 1.9 %collective-permute-start.25 = (bf16[256,128]{1,0:T(8,128)(2,1)S(1)}, bf16[256,128]{1,0:T(8,128)(2,1)S(1)}, u32[]{:S(2)}, u32[]{:S(2)}) collective-permute-start(bf16[256,128]{1,0:T(8,128)(2,1)S(1)} %shard_map.77), channel_id=1, source_target_pairs={{0,3},{1,2},{2,1},{3,0},{4,7},{5,6},{6,5},{7,4},{8,11},{9,10},{10,... | collective-permute-start | bytes 196616 | tf_op jit(solution)/shard_map/ppermute | solution.py:57
  60.2 1.9 %collective-permute-start.23 = (bf16[256,128]{1,0:T(8,128)(2,1)S(1)}, bf16[256,128]{1,0:T(8,128)(2,1)S(1)}, u32[]{:S(2)}, u32[]{:S(2)}) collective-permute-start(bf16[256,128]{1,0:T(8,128)(2,1)S(1)} %shard_map.75), channel_id=1, source_target_pairs={{0,1},{1,0},{2,3},{3,2},{4,5},{5,4},{6,7},{7,6},{8,9},{9,8},{10,11... | collective-permute-start | bytes 196616 | tf_op jit(solution)/shard_map/ppermute | solution.py:57
  63.8 4.8 %collective-permute-start.26 = (bf16[4,128,128]{2,1,0:T(8,128)(2,1)S(1)}, bf16[4,128,128]{2,1,0:T(8,128)(2,1)S(1)}, u32[]{:S(2)}, u32[]{:S(2)}) collective-permute-start(bf16[4,128,128]{2,1,0:T(8,128)(2,1)S(1)} %get-tuple-element.68), channel_id=1, source_target_pairs={{0,4},{1,5},{2,6},{3,7},{4,0},{5,1},{6,2},{7,3},{8,12},{9,13},{10,... | collective-permute-start | bytes 393224 | tf_op jit(solution)/shard_map/ppermute | solution.py:57
  (75 shorter events, 22.5 us)
Async XLA Ops:
  0.0 19.8 %collective-permute-start = (bf16[256,768]{1,0:T(8,128)(2,1)}, bf16[256,768]{1,0:T(8,128)(2,1)S(1)}, u32[]{:S(2)}, u32[]{:S(2)}) collective-permute-start(bf16[256,768]{1,0:T(8,128)(2,1)} %w.1), channel_id=1, source_target_pairs={{0,16},{1,17},{2,18},{3,19},{4,20},{5,21},{6,22},{7,23},{8,24},{9,... | collective-permute-start | bytes 1179656 | tf_op jit(solution)/shard_map/ppermute | solution.py:57
  5.3 4.4 %collective-permute-start.3 = (bf16[128,256]{1,0:T(8,128)(2,1)S(1)}, bf16[128,256]{1,0:T(8,128)(2,1)S(1)}, u32[]{:S(2)}, u32[]{:S(2)}) collective-permute-start(bf16[128,256]{1,0:T(8,128)(2,1)S(1)} %get-tuple-element.39), channel_id=1, source_target_pairs={{0,3},{1,2},{2,1},{3,0},{4,7},{5,6},{6,5},{7,4},{8,11},{9,10},{10,... | collective-permute-start | bytes 196616 | tf_op jit(solution)/shard_map/ppermute | solution.py:57
  7.6 6.0 %collective-permute-start.1 = (bf16[336,256]{1,0:T(8,128)(2,1)S(1)}, bf16[336,256]{1,0:T(8,128)(2,1)S(1)}, u32[]{:S(2)}, u32[]{:S(2)}) collective-permute-start(bf16[336,256]{1,0:T(8,128)(2,1)S(1)} %get-tuple-element.37), channel_id=1, source_target_pairs={{0,1},{1,0},{2,3},{3,2},{4,5},{5,4},{6,7},{7,6},{8,9},{9,8},{10,11... | collective-permute-start | bytes 516104 | tf_op jit(solution)/shard_map/ppermute | solution.py:57
  7.8 5.8 %collective-permute-start.2 = (bf16[336,256]{1,0:T(8,128)(2,1)S(1)}, bf16[336,256]{1,0:T(8,128)(2,1)S(1)}, u32[]{:S(2)}, u32[]{:S(2)}) collective-permute-start(bf16[336,256]{1,0:T(8,128)(2,1)S(1)} %get-tuple-element.38), channel_id=1, source_target_pairs={{0,2},{1,3},{2,0},{3,1},{4,6},{5,7},{6,4},{7,5},{8,10},{9,11},{10,... | collective-permute-start | bytes 516104 | tf_op jit(solution)/shard_map/ppermute | solution.py:57
  9.7 15.0 %collective-permute-start.7 = (bf16[128,2048]{1,0:T(8,128)(2,1)}, bf16[128,2048]{1,0:T(8,128)(2,1)S(1)}, u32[]{:S(2)}, u32[]{:S(2)}) collective-permute-start(bf16[128,2048]{1,0:T(8,128)(2,1)} %bitcast.13), channel_id=1, source_target_pairs={{0,2},{1,3},{2,0},{3,1},{4,6},{5,7},{6,4},{7,5},{8,10},{9,11},{10,... | collective-permute-start | bytes 1572872 | tf_op jit(solution)/shard_map/ppermute | solution.py:57
  10.9 13.8 %collective-permute-start.6 = (bf16[128,2048]{1,0:T(8,128)(2,1)}, bf16[128,2048]{1,0:T(8,128)(2,1)S(1)}, u32[]{:S(2)}, u32[]{:S(2)}) collective-permute-start(bf16[128,2048]{1,0:T(8,128)(2,1)} %bitcast.14), channel_id=1, source_target_pairs={{0,1},{1,0},{2,3},{3,2},{4,5},{5,4},{6,7},{7,6},{8,9},{9,8},{10,11... | collective-permute-start | bytes 1572872 | tf_op jit(solution)/shard_map/ppermute | solution.py:57
  13.7 13.8 %collective-permute-start.8 = (bf16[256,768]{1,0:T(8,128)(2,1)S(1)}, bf16[256,768]{1,0:T(8,128)(2,1)S(1)}, u32[]{:S(2)}, u32[]{:S(2)}) collective-permute-start(bf16[256,768]{1,0:T(8,128)(2,1)S(1)} %shard_map.67.refs_2_.refs_0_), channel_id=1, source_target_pairs={{0,8},{1,9},{2,10},{3,11},{4,12},{5,13},{6,14},{7,15},{8,0},{9,1},... | collective-permute-start | bytes 1179656 | tf_op jit(solution)/shard_map/ppermute | solution.py:57
  19.9 6.3 %collective-permute-start.4 = (bf16[256,256]{1,0:T(8,128)(2,1)S(1)}, bf16[256,256]{1,0:T(8,128)(2,1)S(1)}, u32[]{:S(2)}, u32[]{:S(2)}) collective-permute-start(bf16[256,256]{1,0:T(8,128)(2,1)S(1)} %get-tuple-element.70), channel_id=1, source_target_pairs={{0,1},{1,0},{2,3},{3,2},{4,5},{5,4},{6,7},{7,6},{8,9},{9,8},{10,11... | collective-permute-start | bytes 393224 | tf_op jit(solution)/shard_map/ppermute | solution.py:57
  21.1 6.4 %collective-permute-start.5 = (bf16[256,256]{1,0:T(8,128)(2,1)S(1)}, bf16[256,256]{1,0:T(8,128)(2,1)S(1)}, u32[]{:S(2)}, u32[]{:S(2)}) collective-permute-start(bf16[256,256]{1,0:T(8,128)(2,1)S(1)} %get-tuple-element.69), channel_id=1, source_target_pairs={{0,2},{1,3},{2,0},{3,1},{4,6},{5,7},{6,4},{7,5},{8,10},{9,11},{10,... | collective-permute-start | bytes 393224 | tf_op jit(solution)/shard_map/ppermute | solution.py:57
  30.6 4.1 %collective-permute-start.10 = (bf16[384,2048]{1,0:T(8,128)(2,1)S(1)}, bf16[384,2048]{1,0:T(8,128)(2,1)S(1)}, u32[]{:S(2)}, u32[]{:S(2)}) collective-permute-start(bf16[384,2048]{1,0:T(8,128)(2,1)S(1)} %get-tuple-element.53.refs_0_), channel_id=1, source_target_pairs={{0,4},{1,5},{2,6},{3,7},{4,0},{5,1},{6,2},{7,3},{8,12},{9,13},{10,... | collective-permute-start | bytes 4718600 | tf_op jit(solution)/shard_map/ppermute | solution.py:57
  31.1 3.5 %collective-permute-start.12 = (bf16[528,384]{1,0:T(8,128)(2,1)S(1)}, bf16[528,384]{1,0:T(8,128)(2,1)S(1)}, u32[]{:S(2)}, u32[]{:S(2)}) collective-permute-start(bf16[528,384]{1,0:T(8,128)(2,1)S(1)} %pad_maximum_fusion.1), channel_id=1, source_target_pairs={{0,4},{1,5},{2,6},{3,7},{4,0},{5,1},{6,2},{7,3},{8,12},{9,13},{10,... | collective-permute-start | bytes 1216520 | tf_op jit(solution)/shard_map/ppermute | solution.py:57
  31.3 7.5 %collective-permute-start.11 = (bf16[128,1024]{1,0:T(8,128)(2,1)S(1)}, bf16[128,1024]{1,0:T(8,128)(2,1)S(1)}, u32[]{:S(2)}, u32[]{:S(2)}) collective-permute-start(bf16[128,1024]{1,0:T(8,128)(2,1)S(1)} %get-tuple-element.54), channel_id=1, source_target_pairs={{0,2},{1,3},{2,0},{3,1},{4,6},{5,7},{6,4},{7,5},{8,10},{9,11},{10,... | collective-permute-start | bytes 786440 | tf_op jit(solution)/shard_map/ppermute | solution.py:57
  31.8 7.2 %collective-permute-start.13 = (bf16[128,1024]{1,0:T(8,128)(2,1)S(1)}, bf16[128,1024]{1,0:T(8,128)(2,1)S(1)}, u32[]{:S(2)}, u32[]{:S(2)}) collective-permute-start(bf16[128,1024]{1,0:T(8,128)(2,1)S(1)} %get-tuple-element.59), channel_id=1, source_target_pairs={{0,1},{1,0},{2,3},{3,2},{4,5},{5,4},{6,7},{7,6},{8,9},{9,8},{10,11... | collective-permute-start | bytes 786440 | tf_op jit(solution)/shard_map/ppermute | solution.py:57
  33.0 10.5 %collective-permute-start.16 = (bf16[512,384]{1,0:T(8,128)(2,1)S(1)}, bf16[512,384]{1,0:T(8,128)(2,1)S(1)}, u32[]{:S(2)}, u32[]{:S(2)}) collective-permute-start(bf16[512,384]{1,0:T(8,128)(2,1)S(1)} %constant_dynamic-update-slice_fusion.refs_5_.refs_3_), channel_id=1, source_target_pairs={{0,8},{1,9},{2,10},{3,11},{4,12},{5,13},{6,14},{7,15},{8,0},{9,1},... | collective-permute-start | bytes 1179656 | tf_op jit(solution)/shard_map/ppermute | solution.py:57
  44.2 8.9 %collective-permute-start.17 = (bf16[4,256,128]{2,1,0:T(8,128)(2,1)S(1)}, bf16[4,256,128]{2,1,0:T(8,128)(2,1)S(1)}, u32[]{:S(2)}, u32[]{:S(2)}) collective-permute-start(bf16[4,256,128]{2,1,0:T(8,128)(2,1)S(1)} %get-tuple-element.64.own), channel_id=1, source_target_pairs={{8,16},{9,17},{10,18},{11,19},{12,20},{13,21},{14,22},{15,23},{16,... | collective-permute-start | bytes 786440 | tf_op jit(solution)/shard_map/ppermute | solution.py:57
  47.6 6.1 %collective-permute-start.18 = (bf16[4,256,128]{2,1,0:T(8,128)(2,1)S(1)}, bf16[4,256,128]{2,1,0:T(8,128)(2,1)S(1)}, u32[]{:S(2)}, u32[]{:S(2)}) collective-permute-start(bf16[4,256,128]{2,1,0:T(8,128)(2,1)S(1)} %get-tuple-element.64.own), channel_id=1, source_target_pairs={{0,8},{1,9},{2,10},{3,11},{4,12},{5,13},{6,14},{7,15},{8,0},{9,1},... | collective-permute-start | bytes 786440 | tf_op jit(solution)/shard_map/ppermute | solution.py:57
  47.7 7.8 %collective-permute-start.21 = (bf16[2,256,128]{2,1,0:T(8,128)(2,1)S(1)}, bf16[2,256,128]{2,1,0:T(8,128)(2,1)S(1)}, u32[]{:S(2)}, u32[]{:S(2)}) collective-permute-start(bf16[2,256,128]{2,1,0:T(8,128)(2,1)S(1)} %get-tuple-element.66.own), channel_id=1, source_target_pairs={{8,16},{9,17},{10,18},{11,19},{12,20},{13,21},{14,22},{15,23},{16,... | collective-permute-start | bytes 393224 | tf_op jit(solution)/shard_map/ppermute | solution.py:57
  50.3 6.2 %collective-permute-start.22 = (bf16[2,256,128]{2,1,0:T(8,128)(2,1)S(1)}, bf16[2,256,128]{2,1,0:T(8,128)(2,1)S(1)}, u32[]{:S(2)}, u32[]{:S(2)}) collective-permute-start(bf16[2,256,128]{2,1,0:T(8,128)(2,1)S(1)} %get-tuple-element.66.own), channel_id=1, source_target_pairs={{0,8},{1,9},{2,10},{3,11},{4,12},{5,13},{6,14},{7,15},{8,0},{9,1},... | collective-permute-start | bytes 393224 | tf_op jit(solution)/shard_map/ppermute | solution.py:57
  50.4 8.3 %collective-permute-start.19 = (bf16[2,256,128]{2,1,0:T(8,128)(2,1)S(1)}, bf16[2,256,128]{2,1,0:T(8,128)(2,1)S(1)}, u32[]{:S(2)}, u32[]{:S(2)}) collective-permute-start(bf16[2,256,128]{2,1,0:T(8,128)(2,1)S(1)} %get-tuple-element.65.own), channel_id=1, source_target_pairs={{8,16},{9,17},{10,18},{11,19},{12,20},{13,21},{14,22},{15,23},{16,... | collective-permute-start | bytes 393224 | tf_op jit(solution)/shard_map/ppermute | solution.py:57
  53.1 6.2 %collective-permute-start.20 = (bf16[2,256,128]{2,1,0:T(8,128)(2,1)S(1)}, bf16[2,256,128]{2,1,0:T(8,128)(2,1)S(1)}, u32[]{:S(2)}, u32[]{:S(2)}) collective-permute-start(bf16[2,256,128]{2,1,0:T(8,128)(2,1)S(1)} %get-tuple-element.65.own), channel_id=1, source_target_pairs={{0,8},{1,9},{2,10},{3,11},{4,12},{5,13},{6,14},{7,15},{8,0},{9,1},... | collective-permute-start | bytes 393224 | tf_op jit(solution)/shard_map/ppermute | solution.py:57
  56.8 5.6 %collective-permute-start.25 = (bf16[256,128]{1,0:T(8,128)(2,1)S(1)}, bf16[256,128]{1,0:T(8,128)(2,1)S(1)}, u32[]{:S(2)}, u32[]{:S(2)}) collective-permute-start(bf16[256,128]{1,0:T(8,128)(2,1)S(1)} %shard_map.77), channel_id=1, source_target_pairs={{0,3},{1,2},{2,1},{3,0},{4,7},{5,6},{6,5},{7,4},{8,11},{9,10},{10,... | collective-permute-start | bytes 196616 | tf_op jit(solution)/shard_map/ppermute | solution.py:57
  59.6 3.2 %collective-permute-start.24 = (bf16[256,128]{1,0:T(8,128)(2,1)S(1)}, bf16[256,128]{1,0:T(8,128)(2,1)S(1)}, u32[]{:S(2)}, u32[]{:S(2)}) collective-permute-start(bf16[256,128]{1,0:T(8,128)(2,1)S(1)} %shard_map.76), channel_id=1, source_target_pairs={{0,2},{1,3},{2,0},{3,1},{4,6},{5,7},{6,4},{7,5},{8,10},{9,11},{10,... | collective-permute-start | bytes 196616 | tf_op jit(solution)/shard_map/ppermute | solution.py:57
  60.2 3.6 %collective-permute-start.23 = (bf16[256,128]{1,0:T(8,128)(2,1)S(1)}, bf16[256,128]{1,0:T(8,128)(2,1)S(1)}, u32[]{:S(2)}, u32[]{:S(2)}) collective-permute-start(bf16[256,128]{1,0:T(8,128)(2,1)S(1)} %shard_map.75), channel_id=1, source_target_pairs={{0,1},{1,0},{2,3},{3,2},{4,5},{5,4},{6,7},{7,6},{8,9},{9,8},{10,11... | collective-permute-start | bytes 196616 | tf_op jit(solution)/shard_map/ppermute | solution.py:57
  63.8 5.8 %collective-permute-start.26 = (bf16[4,128,128]{2,1,0:T(8,128)(2,1)S(1)}, bf16[4,128,128]{2,1,0:T(8,128)(2,1)S(1)}, u32[]{:S(2)}, u32[]{:S(2)}) collective-permute-start(bf16[4,128,128]{2,1,0:T(8,128)(2,1)S(1)} %get-tuple-element.68), channel_id=1, source_target_pairs={{0,4},{1,5},{2,6},{3,7},{4,0},{5,1},{6,2},{7,3},{8,12},{9,13},{10,... | collective-permute-start | bytes 393224 | tf_op jit(solution)/shard_map/ppermute | solution.py:57
  (13 other events, 41.6 us)

commit v18 on v12

--- a/solution.py
+++ b/solution.py
@@ -214,7 +214,7 @@
             v_at = V_ORDER.index(r)
             q_ref[r, at, :] = mine[:, :HD]
             k_ref[r, at, :] = mine[:, HD:PAIR]
-            (v_first, v_second)[v_at // 3][v_at % 3, at, :] = mine[:, PAIR:]
+            (v_first, v_second)[v_at // 2][v_at % 2, at, :] = mine[:, PAIR:]
 
 
 def spans(u):
@@ -257,7 +257,7 @@
 
 def mix_kernel(r, weights, outer, own, middle, out_ref):
     block = weights.shape[1] // 2
-    values = neighbours(outer, own, middle, V_ORDER.index(r) % 3)
+    values = neighbours(outer, own, middle, V_ORDER.index(r) % 2)
     for u in range(2):
         w = weights[r, u * block : (u + 1) * block]
         v = [values[side][first * block : last * block] for side, first, last in spans(u)]
@@ -367,9 +367,9 @@
         "v" * 7,
         macs=2 * block * 3 * rows * 3 * HD,
     )(diagonal, *swapped, *weights)
-    one_head = array(4, 2 * block, HD)
+    one_head, half_head = array(4, 2 * block, HD), array(2, 2 * block, HD)
     q, k, *v = call(
-        finish_kernel, (one_head, one_head, array(3, 2 * block, HD), array(1, 2 * block, HD)), "v" * 6, macs=8 * block * rows * 3 * HD
+        finish_kernel, (one_head, one_head, half_head, half_head), "v" * 6, macs=8 * block * rows * 3 * HD
     )(*early, diagonal, last, total, total_diagonal)
 
     weights = call(weigh_kernel, array(4, 2 * block, 5 * block), "v" * 6, macs=8 * block * 5 * block * HD)(
@@ -379,7 +379,7 @@
     pieces = {}
     for i, r in enumerate(V_ORDER):
         mixed = call(functools.partial(mix_kernel, r), array(2 * block, HD), "vvvv", macs=2 * block * 5 * block * HD)(
-            weights, *values[i // 3]
+            weights, *values[i // 2]
         )
         pieces[r] = swap_depth(mixed, r) if r else mixed
     kept, sent = call(pack_kernel, (array(4, block, HD),) * 2, "vvvv")(*[pieces[r] for r in range(4)])

time: 72.3 us -> 71.3 us (0.986)
  waiting for transfers between devices: 22.5 us -> 20.9 us
    ppermute x27, waiting for transfers between devices: 22.5 us -> 20.9 us  [hop(): return lax.ppermute(value, ('tm', 'depth'), pairs)]
  transfers between devices with their start and end apart: 27 -> 27, of which waited for: 14 -> 15; matrix products, arithmetic and copies ran while one was open for 2% -> 2% of each run, Pallas kernels for 9% -> 10%
where the time goes in v18:
time: 71.3 us; the launch traced here: 70.5 us
  starting transfers between devices  36.2 us (51%)
  waiting for transfers between devices  20.9 us (29%)
  Pallas kernels  8.32 us (12%)
  local copies, waits for them, and re-layouts  3.26 us (5%)
  other arithmetic  1.53 us (2%)
    ppermute x27, starting transfers between devices, hop(): return lax.ppermute(value, ('tm', 'depth'), pairs)  36.2 us
    ppermute x27, waiting for transfers between devices, hop(): return lax.ppermute(value, ('tm', 'depth'), pairs)  20.9 us
    unnamed x13, local copies, waits for them, and re-layouts  3.13 us
    pallas_call x3, Pallas kernels, embed(): call(functools.partial(embed_kernel, rs, len(finished)), out, 'v' * (6 +...  2.38 us
  transfers between devices with their start and end apart: 27, of which 15 were waited for; matrix products, arithmetic and copies ran while one was open for 2% of the time, Pallas kernels for 10%

profile of v18, /device:TPU:9, one launch (start us, length us, event | category | flops | bytes accessed | tf_op | source)
XLA Modules:
  0.0 70.5 jit_solution(9216761410755125783)
XLA Ops:
  0.0 2.3 %collective-permute-start = (bf16[256,768]{1,0:T(8,128)(2,1)}, bf16[256,768]{1,0:T(8,128)(2,1)S(1)}, u32[]{:S(2)}, u32[]{:S(2)}) collective-permute-start(bf16[256,768]{1,0:T(8,128)(2,1)} %w.1), channel_id=1, source_target_pairs={{0,16},{1,17},{2,18},{3,19},{4,20},{5,21},{6,22},{7,23},{8,24},{9,... | collective-permute-start | bytes 1179656 | tf_op jit(solution)/shard_map/ppermute | solution.py:57
  4.8 2.2 %collective-permute-start.3 = (bf16[128,256]{1,0:T(8,128)(2,1)S(1)}, bf16[128,256]{1,0:T(8,128)(2,1)S(1)}, u32[]{:S(2)}, u32[]{:S(2)}) collective-permute-start(bf16[128,256]{1,0:T(8,128)(2,1)S(1)} %get-tuple-element.38), channel_id=1, source_target_pairs={{0,3},{1,2},{2,1},{3,0},{4,7},{5,6},{6,5},{7,4},{8,11},{9,10},{10,... | collective-permute-start | bytes 196616 | tf_op jit(solution)/shard_map/ppermute | solution.py:57
  7.5 1.7 %collective-permute-done.3.across = bf16[128,256]{1,0:T(8,128)(2,1)S(1)} collective-permute-done((bf16[128,256]{1,0:T(8,128)(2,1)S(1)}, bf16[128,256]{1,0:T(8,128)(2,1)S(1)}, u32[]{:S(2)}, u32[]{:S(2)}) %collective-permute-start.3) | collective-permute-done | bytes 65568 | tf_op jit(solution)/shard_map/ppermute | solution.py:57
  11.6 1.4 %collective-permute-done.1.plane_x.from_x = bf16[336,256]{1,0:T(8,128)(2,1)S(1)} collective-permute-done((bf16[336,256]{1,0:T(8,128)(2,1)S(1)}, bf16[336,256]{1,0:T(8,128)(2,1)S(1)}, u32[]{:S(2)}, u32[]{:S(2)}) %collective-permute-start.1) | collective-permute-done | bytes 172064 | tf_op jit(solution)/shard_map/ppermute | solution.py:57
  13.4 1.4 %copy-done = bf16[3,128,2048]{2,1,0:T(8,128)(2,1)S(1)} copy-done((bf16[3,128,2048]{2,1,0:T(8,128)(2,1)S(1)}, bf16[3,128,2048]{2,1,0:T(8,128)(2,1)}, u32[]{:S(2)}) %copy-start) | copy-done | bytes 1572888
  16.1 3.7 %collective-permute-done = bf16[256,768]{1,0:T(8,128)(2,1)S(1)} collective-permute-done((bf16[256,768]{1,0:T(8,128)(2,1)}, bf16[256,768]{1,0:T(8,128)(2,1)S(1)}, u32[]{:S(2)}, u32[]{:S(2)}) %collective-permute-start) | collective-permute-done | bytes 393248 | tf_op jit(solution)/shard_map/ppermute | solution.py:57
  19.9 1.3 %collective-permute-start.4 = (bf16[256,256]{1,0:T(8,128)(2,1)S(1)}, bf16[256,256]{1,0:T(8,128)(2,1)S(1)}, u32[]{:S(2)}, u32[]{:S(2)}) collective-permute-start(bf16[256,256]{1,0:T(8,128)(2,1)S(1)} %get-tuple-element.68), channel_id=1, source_target_pairs={{0,1},{1,0},{2,3},{3,2},{4,5},{5,4},{6,7},{7,6},{8,9},{9,8},{10,11... | collective-permute-start | bytes 393224 | tf_op jit(solution)/shard_map/ppermute | solution.py:57
  22.4 1.8 %collective-permute-done.7.refs_1_ = bf16[128,2048]{1,0:T(8,128)(2,1)S(1)} collective-permute-done((bf16[128,2048]{1,0:T(8,128)(2,1)}, bf16[128,2048]{1,0:T(8,128)(2,1)S(1)}, u32[]{:S(2)}, u32[]{:S(2)}) %collective-permute-start.7) | collective-permute-done | bytes 524320 | tf_op jit(solution)/shard_map/ppermute | solution.py:57
  25.6 1.3 %collective-permute-done.5.from_y = bf16[256,256]{1,0:T(8,128)(2,1)S(1)} collective-permute-done((bf16[256,256]{1,0:T(8,128)(2,1)S(1)}, bf16[256,256]{1,0:T(8,128)(2,1)S(1)}, u32[]{:S(2)}, u32[]{:S(2)}) %collective-permute-start.5) | collective-permute-done | bytes 131104 | tf_op jit(solution)/shard_map/ppermute | solution.py:57
  27.1 1.9 %collective-permute-start.9 = (bf16[256,384]{1,0:T(8,128)(2,1)S(1)}, bf16[256,384]{1,0:T(8,128)(2,1)S(1)}, u32[]{:S(2)}, u32[]{:S(2)}) collective-permute-start(bf16[256,384]{1,0:T(8,128)(2,1)S(1)} %get-tuple-element.48), channel_id=1, source_target_pairs={{0,4},{1,5},{2,6},{3,7},{4,0},{5,1},{6,2},{7,3},{8,12},{9,13},{10,... | collective-permute-start | bytes 589832 | tf_op jit(solution)/shard_map/ppermute | solution.py:57
  32.5 1.7 %collective-permute-start.16 = (bf16[512,384]{1,0:T(8,128)(2,1)S(1)}, bf16[512,384]{1,0:T(8,128)(2,1)S(1)}, u32[]{:S(2)}, u32[]{:S(2)}) collective-permute-start(bf16[512,384]{1,0:T(8,128)(2,1)S(1)} %constant_dynamic-update-slice_fusion.refs_5_.refs_3_), channel_id=1, source_target_pairs={{0,8},{1,9},{2,10},{3,11},{4,12},{5,13},{6,14},{7,15},{8,0},{9,1},... | collective-permute-start | bytes 1179656 | tf_op jit(solution)/shard_map/ppermute | solution.py:57
  34.2 1.4 %shard_map.69.refs_4_ = f32[768,384]{1,0:T(8,128)S(1)} custom-call(bf16[384,2048]{1,0:T(8,128)(2,1)S(1)} %get-tuple-element.51.refs_0_, bf16[384,2048]{1,0:T(8,128)(2,1)S(1)} %collective-permute-done.10.refs_1_, bf16[256,768]{1,0:T(8,128)(2,1)S(1)} %shard_map.67.refs_2_.refs_0_, bf16[256,768]{1,0:T(8,128)(2,1)S(1)} %collective-permute-done.8.refs_3_.refs_1_, ...), custom_call_target="tpu_custom_call" | custom-call | flops 905969664 | tf_op jit(solution)/shard_map/pallas_call | solution.py:359
  35.5 2.8 %collective-permute-done.11 = bf16[128,1024]{1,0:T(8,128)(2,1)S(1)} collective-permute-done((bf16[128,1024]{1,0:T(8,128)(2,1)S(1)}, bf16[128,1024]{1,0:T(8,128)(2,1)S(1)}, u32[]{:S(2)}, u32[]{:S(2)}) %collective-permute-start.11) | collective-permute-done | bytes 262176 | tf_op jit(solution)/shard_map/ppermute | solution.py:57
  39.2 1.6 %collective-permute-start.14 = (bf16[80,2048]{1,0:T(8,128)(2,1)S(1)}, bf16[80,2048]{1,0:T(8,128)(2,1)S(1)}, u32[]{:S(2)}, u32[]{:S(2)}) collective-permute-start(bf16[80,2048]{1,0:T(8,128)(2,1)S(1)} %slice.29), channel_id=1, source_target_pairs={{0,4},{1,5},{2,6},{3,7},{4,0},{5,1},{6,2},{7,3},{8,12},{9,13},{10,... | collective-permute-start | bytes 983048 | tf_op jit(solution)/shard_map/ppermute | solution.py:57
  40.9 1.4 %collective-permute-done.15.bottom = bf16[48,2048]{1,0:T(8,128)(2,1)S(1)} collective-permute-done((bf16[48,2048]{1,0:T(8,128)(2,1)S(1)}, bf16[48,2048]{1,0:T(8,128)(2,1)S(1)}, u32[]{:S(2)}, u32[]{:S(2)}) %collective-permute-start.15) | collective-permute-done | bytes 196640 | tf_op jit(solution)/shard_map/ppermute | solution.py:57
  43.7 1.7 %collective-permute-start.17 = (bf16[4,256,128]{2,1,0:T(8,128)(2,1)S(1)}, bf16[4,256,128]{2,1,0:T(8,128)(2,1)S(1)}, u32[]{:S(2)}, u32[]{:S(2)}) collective-permute-start(bf16[4,256,128]{2,1,0:T(8,128)(2,1)S(1)} %get-tuple-element.62.own), channel_id=1, source_target_pairs={{0,8},{1,9},{2,10},{3,11},{4,12},{5,13},{6,14},{7,15},{8,0},{9,1},... | collective-permute-start | bytes 786440 | tf_op jit(solution)/shard_map/ppermute | solution.py:57
  45.4 4.2 %collective-permute-start.18 = (bf16[4,256,128]{2,1,0:T(8,128)(2,1)S(1)}, bf16[4,256,128]{2,1,0:T(8,128)(2,1)S(1)}, u32[]{:S(2)}, u32[]{:S(2)}) collective-permute-start(bf16[4,256,128]{2,1,0:T(8,128)(2,1)S(1)} %get-tuple-element.62.own), channel_id=1, source_target_pairs={{8,16},{9,17},{10,18},{11,19},{12,20},{13,21},{14,22},{15,23},{16,... | collective-permute-start | bytes 786440 | tf_op jit(solution)/shard_map/ppermute | solution.py:57
  49.7 1.9 %collective-permute-start.22 = (bf16[2,256,128]{2,1,0:T(8,128)(2,1)S(1)}, bf16[2,256,128]{2,1,0:T(8,128)(2,1)S(1)}, u32[]{:S(2)}, u32[]{:S(2)}) collective-permute-start(bf16[2,256,128]{2,1,0:T(8,128)(2,1)S(1)} %get-tuple-element.64.own), channel_id=1, source_target_pairs={{8,16},{9,17},{10,18},{11,19},{12,20},{13,21},{14,22},{15,23},{16,... | collective-permute-start | bytes 393224 | tf_op jit(solution)/shard_map/ppermute | solution.py:57
  51.9 3.2 %collective-permute-start.20 = (bf16[2,256,128]{2,1,0:T(8,128)(2,1)S(1)}, bf16[2,256,128]{2,1,0:T(8,128)(2,1)S(1)}, u32[]{:S(2)}, u32[]{:S(2)}) collective-permute-start(bf16[2,256,128]{2,1,0:T(8,128)(2,1)S(1)} %get-tuple-element.63.own), channel_id=1, source_target_pairs={{8,16},{9,17},{10,18},{11,19},{12,20},{13,21},{14,22},{15,23},{16,... | collective-permute-start | bytes 393224 | tf_op jit(solution)/shard_map/ppermute | solution.py:57
  56.3 1.4 %collective-permute-done.22.middle = bf16[2,256,128]{2,1,0:T(8,128)(2,1)S(1)} collective-permute-done((bf16[2,256,128]{2,1,0:T(8,128)(2,1)S(1)}, bf16[2,256,128]{2,1,0:T(8,128)(2,1)S(1)}, u32[]{:S(2)}, u32[]{:S(2)}) %collective-permute-start.22) | collective-permute-done | bytes 131104 | tf_op jit(solution)/shard_map/ppermute | solution.py:57
  58.0 2.0 %collective-permute-start.25 = (bf16[256,128]{1,0:T(8,128)(2,1)S(1)}, bf16[256,128]{1,0:T(8,128)(2,1)S(1)}, u32[]{:S(2)}, u32[]{:S(2)}) collective-permute-start(bf16[256,128]{1,0:T(8,128)(2,1)S(1)} %shard_map.77), channel_id=1, source_target_pairs={{0,3},{1,2},{2,1},{3,0},{4,7},{5,6},{6,5},{7,4},{8,11},{9,10},{10,... | collective-permute-start | bytes 196616 | tf_op jit(solution)/shard_map/ppermute | solution.py:57
  61.8 1.6 %collective-permute-start.23 = (bf16[256,128]{1,0:T(8,128)(2,1)S(1)}, bf16[256,128]{1,0:T(8,128)(2,1)S(1)}, u32[]{:S(2)}, u32[]{:S(2)}) collective-permute-start(bf16[256,128]{1,0:T(8,128)(2,1)S(1)} %shard_map.75), channel_id=1, source_target_pairs={{0,1},{1,0},{2,3},{3,2},{4,5},{5,4},{6,7},{7,6},{8,9},{9,8},{10,11... | collective-permute-start | bytes 196616 | tf_op jit(solution)/shard_map/ppermute | solution.py:57
  63.9 2.0 %collective-permute-done.23.refs_1_ = bf16[256,128]{1,0:T(8,128)(2,1)S(1)} collective-permute-done((bf16[256,128]{1,0:T(8,128)(2,1)S(1)}, bf16[256,128]{1,0:T(8,128)(2,1)S(1)}, u32[]{:S(2)}, u32[]{:S(2)}) %collective-permute-start.23) | collective-permute-done | bytes 65568 | tf_op jit(solution)/shard_map/ppermute | solution.py:57
  65.9 2.8 %collective-permute-start.26 = (bf16[4,128,128]{2,1,0:T(8,128)(2,1)S(1)}, bf16[4,128,128]{2,1,0:T(8,128)(2,1)S(1)}, u32[]{:S(2)}, u32[]{:S(2)}) collective-permute-start(bf16[4,128,128]{2,1,0:T(8,128)(2,1)S(1)} %get-tuple-element.66), channel_id=1, source_target_pairs={{0,4},{1,5},{2,6},{3,7},{4,0},{5,1},{6,2},{7,3},{8,12},{9,13},{10,... | collective-permute-start | bytes 393224 | tf_op jit(solution)/shard_map/ppermute | solution.py:57
  (71 shorter events, 21.6 us)
Async XLA Ops:
  0.0 19.8 %collective-permute-start = (bf16[256,768]{1,0:T(8,128)(2,1)}, bf16[256,768]{1,0:T(8,128)(2,1)S(1)}, u32[]{:S(2)}, u32[]{:S(2)}) collective-permute-start(bf16[256,768]{1,0:T(8,128)(2,1)} %w.1), channel_id=1, source_target_pairs={{0,16},{1,17},{2,18},{3,19},{4,20},{5,21},{6,22},{7,23},{8,24},{9,... | collective-permute-start | bytes 1179656 | tf_op jit(solution)/shard_map/ppermute | solution.py:57
  4.8 4.4 %collective-permute-start.3 = (bf16[128,256]{1,0:T(8,128)(2,1)S(1)}, bf16[128,256]{1,0:T(8,128)(2,1)S(1)}, u32[]{:S(2)}, u32[]{:S(2)}) collective-permute-start(bf16[128,256]{1,0:T(8,128)(2,1)S(1)} %get-tuple-element.38), channel_id=1, source_target_pairs={{0,3},{1,2},{2,1},{3,0},{4,7},{5,6},{6,5},{7,4},{8,11},{9,10},{10,... | collective-permute-start | bytes 196616 | tf_op jit(solution)/shard_map/ppermute | solution.py:57
  7.0 6.0 %collective-permute-start.1 = (bf16[336,256]{1,0:T(8,128)(2,1)S(1)}, bf16[336,256]{1,0:T(8,128)(2,1)S(1)}, u32[]{:S(2)}, u32[]{:S(2)}) collective-permute-start(bf16[336,256]{1,0:T(8,128)(2,1)S(1)} %get-tuple-element.36), channel_id=1, source_target_pairs={{0,1},{1,0},{2,3},{3,2},{4,5},{5,4},{6,7},{7,6},{8,9},{9,8},{10,11... | collective-permute-start | bytes 516104 | tf_op jit(solution)/shard_map/ppermute | solution.py:57
  7.3 5.8 %collective-permute-start.2 = (bf16[336,256]{1,0:T(8,128)(2,1)S(1)}, bf16[336,256]{1,0:T(8,128)(2,1)S(1)}, u32[]{:S(2)}, u32[]{:S(2)}) collective-permute-start(bf16[336,256]{1,0:T(8,128)(2,1)S(1)} %get-tuple-element.37), channel_id=1, source_target_pairs={{0,2},{1,3},{2,0},{3,1},{4,6},{5,7},{6,4},{7,5},{8,10},{9,11},{10,... | collective-permute-start | bytes 516104 | tf_op jit(solution)/shard_map/ppermute | solution.py:57
  9.2 15.0 %collective-permute-start.7 = (bf16[128,2048]{1,0:T(8,128)(2,1)}, bf16[128,2048]{1,0:T(8,128)(2,1)S(1)}, u32[]{:S(2)}, u32[]{:S(2)}) collective-permute-start(bf16[128,2048]{1,0:T(8,128)(2,1)} %bitcast.12), channel_id=1, source_target_pairs={{0,2},{1,3},{2,0},{3,1},{4,6},{5,7},{6,4},{7,5},{8,10},{9,11},{10,... | collective-permute-start | bytes 1572872 | tf_op jit(solution)/shard_map/ppermute | solution.py:57
  10.4 13.8 %collective-permute-start.6 = (bf16[128,2048]{1,0:T(8,128)(2,1)}, bf16[128,2048]{1,0:T(8,128)(2,1)S(1)}, u32[]{:S(2)}, u32[]{:S(2)}) collective-permute-start(bf16[128,2048]{1,0:T(8,128)(2,1)} %bitcast.13), channel_id=1, source_target_pairs={{0,1},{1,0},{2,3},{3,2},{4,5},{5,4},{6,7},{7,6},{8,9},{9,8},{10,11... | collective-permute-start | bytes 1572872 | tf_op jit(solution)/shard_map/ppermute | solution.py:57
  13.2 13.8 %collective-permute-start.8 = (bf16[256,768]{1,0:T(8,128)(2,1)S(1)}, bf16[256,768]{1,0:T(8,128)(2,1)S(1)}, u32[]{:S(2)}, u32[]{:S(2)}) collective-permute-start(bf16[256,768]{1,0:T(8,128)(2,1)S(1)} %shard_map.67.refs_2_.refs_0_), channel_id=1, source_target_pairs={{0,8},{1,9},{2,10},{3,11},{4,12},{5,13},{6,14},{7,15},{8,0},{9,1},... | collective-permute-start | bytes 1179656 | tf_op jit(solution)/shard_map/ppermute | solution.py:57
  19.9 5.8 %collective-permute-start.4 = (bf16[256,256]{1,0:T(8,128)(2,1)S(1)}, bf16[256,256]{1,0:T(8,128)(2,1)S(1)}, u32[]{:S(2)}, u32[]{:S(2)}) collective-permute-start(bf16[256,256]{1,0:T(8,128)(2,1)S(1)} %get-tuple-element.68), channel_id=1, source_target_pairs={{0,1},{1,0},{2,3},{3,2},{4,5},{5,4},{6,7},{7,6},{8,9},{9,8},{10,11... | collective-permute-start | bytes 393224 | tf_op jit(solution)/shard_map/ppermute | solution.py:57
  21.1 5.8 %collective-permute-start.5 = (bf16[256,256]{1,0:T(8,128)(2,1)S(1)}, bf16[256,256]{1,0:T(8,128)(2,1)S(1)}, u32[]{:S(2)}, u32[]{:S(2)}) collective-permute-start(bf16[256,256]{1,0:T(8,128)(2,1)S(1)} %get-tuple-element.67), channel_id=1, source_target_pairs={{0,2},{1,3},{2,0},{3,1},{4,6},{5,7},{6,4},{7,5},{8,10},{9,11},{10,... | collective-permute-start | bytes 393224 | tf_op jit(solution)/shard_map/ppermute | solution.py:57
  30.1 4.1 %collective-permute-start.10 = (bf16[384,2048]{1,0:T(8,128)(2,1)S(1)}, bf16[384,2048]{1,0:T(8,128)(2,1)S(1)}, u32[]{:S(2)}, u32[]{:S(2)}) collective-permute-start(bf16[384,2048]{1,0:T(8,128)(2,1)S(1)} %get-tuple-element.51.refs_0_), channel_id=1, source_target_pairs={{0,4},{1,5},{2,6},{3,7},{4,0},{5,1},{6,2},{7,3},{8,12},{9,13},{10,... | collective-permute-start | bytes 4718600 | tf_op jit(solution)/shard_map/ppermute | solution.py:57
  30.6 3.6 %collective-permute-start.12 = (bf16[528,384]{1,0:T(8,128)(2,1)S(1)}, bf16[528,384]{1,0:T(8,128)(2,1)S(1)}, u32[]{:S(2)}, u32[]{:S(2)}) collective-permute-start(bf16[528,384]{1,0:T(8,128)(2,1)S(1)} %pad_maximum_fusion.1), channel_id=1, source_target_pairs={{0,4},{1,5},{2,6},{3,7},{4,0},{5,1},{6,2},{7,3},{8,12},{9,13},{10,... | collective-permute-start | bytes 1216520 | tf_op jit(solution)/shard_map/ppermute | solution.py:57
  30.8 7.5 %collective-permute-start.11 = (bf16[128,1024]{1,0:T(8,128)(2,1)S(1)}, bf16[128,1024]{1,0:T(8,128)(2,1)S(1)}, u32[]{:S(2)}, u32[]{:S(2)}) collective-permute-start(bf16[128,1024]{1,0:T(8,128)(2,1)S(1)} %get-tuple-element.52), channel_id=1, source_target_pairs={{0,2},{1,3},{2,0},{3,1},{4,6},{5,7},{6,4},{7,5},{8,10},{9,11},{10,... | collective-permute-start | bytes 786440 | tf_op jit(solution)/shard_map/ppermute | solution.py:57
  31.3 7.2 %collective-permute-start.13 = (bf16[128,1024]{1,0:T(8,128)(2,1)S(1)}, bf16[128,1024]{1,0:T(8,128)(2,1)S(1)}, u32[]{:S(2)}, u32[]{:S(2)}) collective-permute-start(bf16[128,1024]{1,0:T(8,128)(2,1)S(1)} %get-tuple-element.57), channel_id=1, source_target_pairs={{0,1},{1,0},{2,3},{3,2},{4,5},{5,4},{6,7},{7,6},{8,9},{9,8},{10,11... | collective-permute-start | bytes 786440 | tf_op jit(solution)/shard_map/ppermute | solution.py:57
  32.5 10.5 %collective-permute-start.16 = (bf16[512,384]{1,0:T(8,128)(2,1)S(1)}, bf16[512,384]{1,0:T(8,128)(2,1)S(1)}, u32[]{:S(2)}, u32[]{:S(2)}) collective-permute-start(bf16[512,384]{1,0:T(8,128)(2,1)S(1)} %constant_dynamic-update-slice_fusion.refs_5_.refs_3_), channel_id=1, source_target_pairs={{0,8},{1,9},{2,10},{3,11},{4,12},{5,13},{6,14},{7,15},{8,0},{9,1},... | collective-permute-start | bytes 1179656 | tf_op jit(solution)/shard_map/ppermute | solution.py:57
  43.7 8.2 %collective-permute-start.17 = (bf16[4,256,128]{2,1,0:T(8,128)(2,1)S(1)}, bf16[4,256,128]{2,1,0:T(8,128)(2,1)S(1)}, u32[]{:S(2)}, u32[]{:S(2)}) collective-permute-start(bf16[4,256,128]{2,1,0:T(8,128)(2,1)S(1)} %get-tuple-element.62.own), channel_id=1, source_target_pairs={{0,8},{1,9},{2,10},{3,11},{4,12},{5,13},{6,14},{7,15},{8,0},{9,1},... | collective-permute-start | bytes 786440 | tf_op jit(solution)/shard_map/ppermute | solution.py:57
  45.4 9.7 %collective-permute-start.18 = (bf16[4,256,128]{2,1,0:T(8,128)(2,1)S(1)}, bf16[4,256,128]{2,1,0:T(8,128)(2,1)S(1)}, u32[]{:S(2)}, u32[]{:S(2)}) collective-permute-start(bf16[4,256,128]{2,1,0:T(8,128)(2,1)S(1)} %get-tuple-element.62.own), channel_id=1, source_target_pairs={{8,16},{9,17},{10,18},{11,19},{12,20},{13,21},{14,22},{15,23},{16,... | collective-permute-start | bytes 786440 | tf_op jit(solution)/shard_map/ppermute | solution.py:57
  49.6 6.7 %collective-permute-start.21 = (bf16[2,256,128]{2,1,0:T(8,128)(2,1)S(1)}, bf16[2,256,128]{2,1,0:T(8,128)(2,1)S(1)}, u32[]{:S(2)}, u32[]{:S(2)}) collective-permute-start(bf16[2,256,128]{2,1,0:T(8,128)(2,1)S(1)} %get-tuple-element.64.own), channel_id=1, source_target_pairs={{0,8},{1,9},{2,10},{3,11},{4,12},{5,13},{6,14},{7,15},{8,0},{9,1},... | collective-permute-start | bytes 393224 | tf_op jit(solution)/shard_map/ppermute | solution.py:57
  49.7 8.0 %collective-permute-start.22 = (bf16[2,256,128]{2,1,0:T(8,128)(2,1)S(1)}, bf16[2,256,128]{2,1,0:T(8,128)(2,1)S(1)}, u32[]{:S(2)}, u32[]{:S(2)}) collective-permute-start(bf16[2,256,128]{2,1,0:T(8,128)(2,1)S(1)} %get-tuple-element.64.own), channel_id=1, source_target_pairs={{8,16},{9,17},{10,18},{11,19},{12,20},{13,21},{14,22},{15,23},{16,... | collective-permute-start | bytes 393224 | tf_op jit(solution)/shard_map/ppermute | solution.py:57
  51.6 8.3 %collective-permute-start.19 = (bf16[2,256,128]{2,1,0:T(8,128)(2,1)S(1)}, bf16[2,256,128]{2,1,0:T(8,128)(2,1)S(1)}, u32[]{:S(2)}, u32[]{:S(2)}) collective-permute-start(bf16[2,256,128]{2,1,0:T(8,128)(2,1)S(1)} %get-tuple-element.63.own), channel_id=1, source_target_pairs={{0,8},{1,9},{2,10},{3,11},{4,12},{5,13},{6,14},{7,15},{8,0},{9,1},... | collective-permute-start | bytes 393224 | tf_op jit(solution)/shard_map/ppermute | solution.py:57
  51.9 8.6 %collective-permute-start.20 = (bf16[2,256,128]{2,1,0:T(8,128)(2,1)S(1)}, bf16[2,256,128]{2,1,0:T(8,128)(2,1)S(1)}, u32[]{:S(2)}, u32[]{:S(2)}) collective-permute-start(bf16[2,256,128]{2,1,0:T(8,128)(2,1)S(1)} %get-tuple-element.63.own), channel_id=1, source_target_pairs={{8,16},{9,17},{10,18},{11,19},{12,20},{13,21},{14,22},{15,23},{16,... | collective-permute-start | bytes 393224 | tf_op jit(solution)/shard_map/ppermute | solution.py:57
  58.0 5.6 %collective-permute-start.25 = (bf16[256,128]{1,0:T(8,128)(2,1)S(1)}, bf16[256,128]{1,0:T(8,128)(2,1)S(1)}, u32[]{:S(2)}, u32[]{:S(2)}) collective-permute-start(bf16[256,128]{1,0:T(8,128)(2,1)S(1)} %shard_map.77), channel_id=1, source_target_pairs={{0,3},{1,2},{2,1},{3,0},{4,7},{5,6},{6,5},{7,4},{8,11},{9,10},{10,... | collective-permute-start | bytes 196616 | tf_op jit(solution)/shard_map/ppermute | solution.py:57
  60.8 3.2 %collective-permute-start.24 = (bf16[256,128]{1,0:T(8,128)(2,1)S(1)}, bf16[256,128]{1,0:T(8,128)(2,1)S(1)}, u32[]{:S(2)}, u32[]{:S(2)}) collective-permute-start(bf16[256,128]{1,0:T(8,128)(2,1)S(1)} %shard_map.76), channel_id=1, source_target_pairs={{0,2},{1,3},{2,0},{3,1},{4,6},{5,7},{6,4},{7,5},{8,10},{9,11},{10,... | collective-permute-start | bytes 196616 | tf_op jit(solution)/shard_map/ppermute | solution.py:57
  61.8 4.2 %collective-permute-start.23 = (bf16[256,128]{1,0:T(8,128)(2,1)S(1)}, bf16[256,128]{1,0:T(8,128)(2,1)S(1)}, u32[]{:S(2)}, u32[]{:S(2)}) collective-permute-start(bf16[256,128]{1,0:T(8,128)(2,1)S(1)} %shard_map.75), channel_id=1, source_target_pairs={{0,1},{1,0},{2,3},{3,2},{4,5},{5,4},{6,7},{7,6},{8,9},{9,8},{10,11... | collective-permute-start | bytes 196616 | tf_op jit(solution)/shard_map/ppermute | solution.py:57
  65.9 3.8 %collective-permute-start.26 = (bf16[4,128,128]{2,1,0:T(8,128)(2,1)S(1)}, bf16[4,128,128]{2,1,0:T(8,128)(2,1)S(1)}, u32[]{:S(2)}, u32[]{:S(2)}) collective-permute-start(bf16[4,128,128]{2,1,0:T(8,128)(2,1)S(1)} %get-tuple-element.66), channel_id=1, source_target_pairs={{0,4},{1,5},{2,6},{3,7},{4,0},{5,1},{6,2},{7,3},{8,12},{9,13},{10,... | collective-permute-start | bytes 393224 | tf_op jit(solution)/shard_map/ppermute | solution.py:57
  (9 other events, 37.1 us)

commit v19 on v18

--- a/solution.py
+++ b/solution.py
@@ -132,14 +132,24 @@
         flags_ref[:, k * HD : (k + 1) * HD] = flags
 
 
+def other_kernel(own, near, flags, out_ref):
+    size, width = own.shape[0], 3 * HD
+    out_ref[:size] = own[:, width:]
+    out_ref[size : 2 * size] = near[:, width:]
+    out_ref[2 * size :] = flags[...]
+
+
 def embed_kernel(rs, more, raw, plane_x, plane_y, across, conv_w, gain, *refs):
     count = len(rs)
+    halves = 2 if rs == (3,) else 1
+    count *= halves
     streams, finished, (out_ref, *onward, acc) = refs[:count], refs[count : count + more], refs[count + more :]
     for ref in finished:
         out_ref[: ref.shape[0]] = ref[...]
-    for i, ref in enumerate(onward):
-        half = ref.shape[1]
-        ref[...] = streams[i][:, i * half : (i + 1) * half]
+    if len(rs) > 1:
+        for i, ref in enumerate(onward):
+            half = ref.shape[1]
+            ref[...] = streams[i][:, i * half : (i + 1) * half]
     _, _, depth = where_am_i()
     rows, width = raw.shape[0] - EXTRA, conv_w.shape[1]
     raws = [raw[:rows]]
@@ -161,11 +171,16 @@
         for at in range(0, width, step):
             here = slice(at, at + step)
             part = jnp.dot(windows, conv_w[:, here], preferred_element_type=jnp.float32)
-            part += streams[i][:, here].astype(jnp.float32)
+            each = width // halves
+            part += streams[i + at // each][:, at % each : at % each + step].astype(jnp.float32)
             acc[:, here] = part
             total += jnp.sum(part * part, axis=1, keepdims=True)
         scale = lax.rsqrt(total / width + 1e-05)
-        out_ref[done + i * rows : done + (i + 1) * rows] = (acc[...] * scale * gain[...]).astype(jnp.bfloat16)
+        normed = (acc[...] * scale * gain[...]).astype(jnp.bfloat16)
+        out_ref[done + i * rows : done + (i + 1) * rows] = normed
+        if halves > 1:
+            cut = onward[0].shape[0]
+            onward[0][...], onward[1][...] = normed[:cut], normed[cut:]
 
 
 def take(refs, source, core, rows):
@@ -320,8 +335,12 @@
     own = call(sort_kernel, array(size, 6 * HD), "vvv")(kept, *plane[:2])
     near = swap_z(own, 1)
 
+    piece = 5 * block // 8
     def embed(rs, *streams, finished=()):
-        out = (array((len(rs) + len(finished)) * block, width),) + (array(block, half),) * (len(rs) - 1) * 2
+        onward = {1: (), 2: (array(block, half),) * 2}[len(rs)]
+        if rs == (3,):
+            onward = (array(piece, width), array(block - piece, width))
+        out = (array((len(rs) + len(finished)) * block, width), *onward)
         return call(
             functools.partial(embed_kernel, rs, len(finished)),
             out,
@@ -351,16 +370,16 @@
     far = jnp.concatenate([keep, swap_core(send)], axis=0)
     last = swap_z(far, 1)
     far, near, stack = lax.optimization_barrier((far, near, stack))
-    received = swap_core(jnp.concatenate([own[:, 3 * HD :], near[:, 3 * HD :], flags], axis=0))
+    to_other = call(other_kernel, array(2 * size + EXTRA, 3 * HD), "vvv")(own, near, flags)
+    received = swap_core(to_other)
     weights = (own, near, received, far)
-    piece = 5 * block // 8
     early = (stack, swap_core(stack))
     rows = 2 * size
     total = call(partial_kernel, array(6 * block, 3 * HD, kind=f32), "v" * 6, macs=6 * block * 3 * rows * 3 * HD)(
         *early, *weights
     )
-    (diagonal,) = embed((3,), jnp.concatenate([after(t, total) for t in diagonal], axis=1))
-    swapped = [swap_core(diagonal[:piece]), swap_core(diagonal[piece:])]
+    diagonal, *parts = embed((3,), *[after(t, total) for t in diagonal])
+    swapped = [swap_core(t) for t in parts]
     total_diagonal, diagonal = call(
         diagonal_kernel,
         (array(2 * block, 3 * HD, kind=f32), array(2 * block, width)),

time: 71.3 us -> 71.1 us (level)
  waiting for transfers between devices: 20.9 us -> 22.1 us
  starting transfers between devices: 36.2 us -> 35.3 us
    ppermute x27, waiting for transfers between devices: 20.9 us -> 22.1 us  [hop(): return lax.ppermute(value, ('tm', 'depth'), pairs)]
    ppermute x27, starting transfers between devices: 36.2 us -> 35.3 us  [hop(): return lax.ppermute(value, ('tm', 'depth'), pairs)]
where the time goes in v19:
time: 71.1 us; the launch traced here: 70.6 us
  starting transfers between devices  35.3 us (50%)
  waiting for transfers between devices  22.1 us (31%)
  Pallas kernels  8.36 us (12%)
  local copies, waits for them, and re-layouts  3.18 us (4%)
  other arithmetic  1.45 us (2%)
    ppermute x27, starting transfers between devices, hop(): return lax.ppermute(value, ('tm', 'depth'), pairs)  35.3 us
    ppermute x27, waiting for transfers between devices, hop(): return lax.ppermute(value, ('tm', 'depth'), pairs)  22.1 us
    unnamed x13, local copies, waits for them, and re-layouts  3.13 us
    pallas_call x3, Pallas kernels, embed(): call(functools.partial(embed_kernel, rs, len(finished)), out, 'v' * (6 +...  2.39 us
  transfers between devices with their start and end apart: 27, of which 15 were waited for; matrix products, arithmetic and copies ran while one was open for 2% of the time, Pallas kernels for 10%

profile of v19, /device:TPU:9, one launch (start us, length us, event | category | flops | bytes accessed | tf_op | source)
XLA Modules:
  0.0 70.6 jit_solution(13052800404304464309)
XLA Ops:
  0.0 2.3 %collective-permute-start = (bf16[256,768]{1,0:T(8,128)(2,1)}, bf16[256,768]{1,0:T(8,128)(2,1)S(1)}, u32[]{:S(2)}, u32[]{:S(2)}) collective-permute-start(bf16[256,768]{1,0:T(8,128)(2,1)} %w.1), channel_id=1, source_target_pairs={{0,16},{1,17},{2,18},{3,19},{4,20},{5,21},{6,22},{7,23},{8,24},{9,... | collective-permute-start | bytes 1179656 | tf_op jit(solution)/shard_map/ppermute | solution.py:57
  4.8 2.2 %collective-permute-start.3 = (bf16[128,256]{1,0:T(8,128)(2,1)S(1)}, bf16[128,256]{1,0:T(8,128)(2,1)S(1)}, u32[]{:S(2)}, u32[]{:S(2)}) collective-permute-start(bf16[128,256]{1,0:T(8,128)(2,1)S(1)} %get-tuple-element.41), channel_id=1, source_target_pairs={{0,3},{1,2},{2,1},{3,0},{4,7},{5,6},{6,5},{7,4},{8,11},{9,10},{10,... | collective-permute-start | bytes 196616 | tf_op jit(solution)/shard_map/ppermute | solution.py:57
  7.5 1.7 %collective-permute-done.3.across = bf16[128,256]{1,0:T(8,128)(2,1)S(1)} collective-permute-done((bf16[128,256]{1,0:T(8,128)(2,1)S(1)}, bf16[128,256]{1,0:T(8,128)(2,1)S(1)}, u32[]{:S(2)}, u32[]{:S(2)}) %collective-permute-start.3) | collective-permute-done | bytes 65568 | tf_op jit(solution)/shard_map/ppermute | solution.py:57
  11.6 1.4 %collective-permute-done.1.plane_x.from_x = bf16[336,256]{1,0:T(8,128)(2,1)S(1)} collective-permute-done((bf16[336,256]{1,0:T(8,128)(2,1)S(1)}, bf16[336,256]{1,0:T(8,128)(2,1)S(1)}, u32[]{:S(2)}, u32[]{:S(2)}) %collective-permute-start.1) | collective-permute-done | bytes 172064 | tf_op jit(solution)/shard_map/ppermute | solution.py:57
  13.4 1.4 %copy-done = bf16[3,128,2048]{2,1,0:T(8,128)(2,1)S(1)} copy-done((bf16[3,128,2048]{2,1,0:T(8,128)(2,1)S(1)}, bf16[3,128,2048]{2,1,0:T(8,128)(2,1)}, u32[]{:S(2)}) %copy-start) | copy-done | bytes 1572888
  16.1 3.7 %collective-permute-done = bf16[256,768]{1,0:T(8,128)(2,1)S(1)} collective-permute-done((bf16[256,768]{1,0:T(8,128)(2,1)}, bf16[256,768]{1,0:T(8,128)(2,1)S(1)}, u32[]{:S(2)}, u32[]{:S(2)}) %collective-permute-start) | collective-permute-done | bytes 393248 | tf_op jit(solution)/shard_map/ppermute | solution.py:57
  19.9 1.3 %collective-permute-start.4 = (bf16[256,256]{1,0:T(8,128)(2,1)S(1)}, bf16[256,256]{1,0:T(8,128)(2,1)S(1)}, u32[]{:S(2)}, u32[]{:S(2)}) collective-permute-start(bf16[256,256]{1,0:T(8,128)(2,1)S(1)} %get-tuple-element.74), channel_id=1, source_target_pairs={{0,1},{1,0},{2,3},{3,2},{4,5},{5,4},{6,7},{7,6},{8,9},{9,8},{10,11... | collective-permute-start | bytes 393224 | tf_op jit(solution)/shard_map/ppermute | solution.py:57
  21.1 1.2 %collective-permute-start.5 = (bf16[256,256]{1,0:T(8,128)(2,1)S(1)}, bf16[256,256]{1,0:T(8,128)(2,1)S(1)}, u32[]{:S(2)}, u32[]{:S(2)}) collective-permute-start(bf16[256,256]{1,0:T(8,128)(2,1)S(1)} %get-tuple-element.73), channel_id=1, source_target_pairs={{0,2},{1,3},{2,0},{3,1},{4,6},{5,7},{6,4},{7,5},{8,10},{9,11},{10,... | collective-permute-start | bytes 393224 | tf_op jit(solution)/shard_map/ppermute | solution.py:57
  22.4 1.8 %collective-permute-done.7.refs_1_ = bf16[128,2048]{1,0:T(8,128)(2,1)S(1)} collective-permute-done((bf16[128,2048]{1,0:T(8,128)(2,1)}, bf16[128,2048]{1,0:T(8,128)(2,1)S(1)}, u32[]{:S(2)}, u32[]{:S(2)}) %collective-permute-start.7) | collective-permute-done | bytes 524320 | tf_op jit(solution)/shard_map/ppermute | solution.py:57
  25.6 1.3 %collective-permute-done.5.from_y = bf16[256,256]{1,0:T(8,128)(2,1)S(1)} collective-permute-done((bf16[256,256]{1,0:T(8,128)(2,1)S(1)}, bf16[256,256]{1,0:T(8,128)(2,1)S(1)}, u32[]{:S(2)}, u32[]{:S(2)}) %collective-permute-start.5) | collective-permute-done | bytes 131104 | tf_op jit(solution)/shard_map/ppermute | solution.py:57
  27.1 1.9 %collective-permute-start.9 = (bf16[256,384]{1,0:T(8,128)(2,1)S(1)}, bf16[256,384]{1,0:T(8,128)(2,1)S(1)}, u32[]{:S(2)}, u32[]{:S(2)}) collective-permute-start(bf16[256,384]{1,0:T(8,128)(2,1)S(1)} %get-tuple-element.51), channel_id=1, source_target_pairs={{0,4},{1,5},{2,6},{3,7},{4,0},{5,1},{6,2},{7,3},{8,12},{9,13},{10,... | collective-permute-start | bytes 589832 | tf_op jit(solution)/shard_map/ppermute | solution.py:57
  32.4 1.7 %collective-permute-start.16 = (bf16[512,384]{1,0:T(8,128)(2,1)S(1)}, bf16[512,384]{1,0:T(8,128)(2,1)S(1)}, u32[]{:S(2)}, u32[]{:S(2)}) collective-permute-start(bf16[512,384]{1,0:T(8,128)(2,1)S(1)} %constant_dynamic-update-slice_fusion.refs_5_.refs_3_), channel_id=1, source_target_pairs={{0,8},{1,9},{2,10},{3,11},{4,12},{5,13},{6,14},{7,15},{8,0},{9,1},... | collective-permute-start | bytes 1179656 | tf_op jit(solution)/shard_map/ppermute | solution.py:57
  34.1 1.4 %shard_map.70.refs_4_ = f32[768,384]{1,0:T(8,128)S(1)} custom-call(bf16[384,2048]{1,0:T(8,128)(2,1)S(1)} %get-tuple-element.54.refs_0_, bf16[384,2048]{1,0:T(8,128)(2,1)S(1)} %collective-permute-done.10.refs_1_, bf16[256,768]{1,0:T(8,128)(2,1)S(1)} %shard_map.67.own.refs_2_.refs_0_, bf16[256,768]{1,0:T(8,128)(2,1)S(1)} %collective-permute-done.8.near.refs_3_.refs_1_, ...), custom_call_target="tpu_custom_call" | custom-call | flops 905969664 | tf_op jit(solution)/shard_map/pallas_call | solution.py:378
  35.5 2.8 %collective-permute-done.13.refs_1_ = bf16[128,1024]{1,0:T(8,128)(2,1)S(1)} collective-permute-done((bf16[128,1024]{1,0:T(8,128)(2,1)S(1)}, bf16[128,1024]{1,0:T(8,128)(2,1)S(1)}, u32[]{:S(2)}, u32[]{:S(2)}) %collective-permute-start.13) | collective-permute-done | bytes 262176 | tf_op jit(solution)/shard_map/ppermute | solution.py:57
  39.8 1.6 %collective-permute-start.14 = (bf16[80,2048]{1,0:T(8,128)(2,1)S(1)}, bf16[80,2048]{1,0:T(8,128)(2,1)S(1)}, u32[]{:S(2)}, u32[]{:S(2)}) collective-permute-start(bf16[80,2048]{1,0:T(8,128)(2,1)S(1)} %get-tuple-element.63), channel_id=1, source_target_pairs={{0,4},{1,5},{2,6},{3,7},{4,0},{5,1},{6,2},{7,3},{8,12},{9,13},{10,... | collective-permute-start | bytes 983048 | tf_op jit(solution)/shard_map/ppermute | solution.py:57
  41.5 1.5 %collective-permute-done.15.bottom = bf16[48,2048]{1,0:T(8,128)(2,1)S(1)} collective-permute-done((bf16[48,2048]{1,0:T(8,128)(2,1)S(1)}, bf16[48,2048]{1,0:T(8,128)(2,1)S(1)}, u32[]{:S(2)}, u32[]{:S(2)}) %collective-permute-start.15) | collective-permute-done | bytes 196640 | tf_op jit(solution)/shard_map/ppermute | solution.py:57
  45.3 4.2 %collective-permute-start.18 = (bf16[4,256,128]{2,1,0:T(8,128)(2,1)S(1)}, bf16[4,256,128]{2,1,0:T(8,128)(2,1)S(1)}, u32[]{:S(2)}, u32[]{:S(2)}) collective-permute-start(bf16[4,256,128]{2,1,0:T(8,128)(2,1)S(1)} %get-tuple-element.68.own), channel_id=1, source_target_pairs={{8,16},{9,17},{10,18},{11,19},{12,20},{13,21},{14,22},{15,23},{16,... | collective-permute-start | bytes 786440 | tf_op jit(solution)/shard_map/ppermute | solution.py:57
  49.5 1.9 %collective-permute-start.22 = (bf16[2,256,128]{2,1,0:T(8,128)(2,1)S(1)}, bf16[2,256,128]{2,1,0:T(8,128)(2,1)S(1)}, u32[]{:S(2)}, u32[]{:S(2)}) collective-permute-start(bf16[2,256,128]{2,1,0:T(8,128)(2,1)S(1)} %get-tuple-element.70.own), channel_id=1, source_target_pairs={{8,16},{9,17},{10,18},{11,19},{12,20},{13,21},{14,22},{15,23},{16,... | collective-permute-start | bytes 393224 | tf_op jit(solution)/shard_map/ppermute | solution.py:57
  51.7 3.2 %collective-permute-start.20 = (bf16[2,256,128]{2,1,0:T(8,128)(2,1)S(1)}, bf16[2,256,128]{2,1,0:T(8,128)(2,1)S(1)}, u32[]{:S(2)}, u32[]{:S(2)}) collective-permute-start(bf16[2,256,128]{2,1,0:T(8,128)(2,1)S(1)} %get-tuple-element.69.own), channel_id=1, source_target_pairs={{8,16},{9,17},{10,18},{11,19},{12,20},{13,21},{14,22},{15,23},{16,... | collective-permute-start | bytes 393224 | tf_op jit(solution)/shard_map/ppermute | solution.py:57
  56.1 1.3 %collective-permute-done.22.middle = bf16[2,256,128]{2,1,0:T(8,128)(2,1)S(1)} collective-permute-done((bf16[2,256,128]{2,1,0:T(8,128)(2,1)S(1)}, bf16[2,256,128]{2,1,0:T(8,128)(2,1)S(1)}, u32[]{:S(2)}, u32[]{:S(2)}) %collective-permute-start.22) | collective-permute-done | bytes 131104 | tf_op jit(solution)/shard_map/ppermute | solution.py:57
  57.7 2.1 %collective-permute-start.25 = (bf16[256,128]{1,0:T(8,128)(2,1)S(1)}, bf16[256,128]{1,0:T(8,128)(2,1)S(1)}, u32[]{:S(2)}, u32[]{:S(2)}) collective-permute-start(bf16[256,128]{1,0:T(8,128)(2,1)S(1)} %shard_map.78), channel_id=1, source_target_pairs={{0,3},{1,2},{2,1},{3,0},{4,7},{5,6},{6,5},{7,4},{8,11},{9,10},{10,... | collective-permute-start | bytes 196616 | tf_op jit(solution)/shard_map/ppermute | solution.py:57
  60.5 2.2 %collective-permute-start.24 = (bf16[256,128]{1,0:T(8,128)(2,1)S(1)}, bf16[256,128]{1,0:T(8,128)(2,1)S(1)}, u32[]{:S(2)}, u32[]{:S(2)}) collective-permute-start(bf16[256,128]{1,0:T(8,128)(2,1)S(1)} %shard_map.77), channel_id=1, source_target_pairs={{0,2},{1,3},{2,0},{3,1},{4,6},{5,7},{6,4},{7,5},{8,10},{9,11},{10,... | collective-permute-start | bytes 196616 | tf_op jit(solution)/shard_map/ppermute | solution.py:57
  64.3 2.1 %collective-permute-done.23.refs_1_ = bf16[256,128]{1,0:T(8,128)(2,1)S(1)} collective-permute-done((bf16[256,128]{1,0:T(8,128)(2,1)S(1)}, bf16[256,128]{1,0:T(8,128)(2,1)S(1)}, u32[]{:S(2)}, u32[]{:S(2)}) %collective-permute-start.23) | collective-permute-done | bytes 65568 | tf_op jit(solution)/shard_map/ppermute | solution.py:57
  66.4 2.4 %collective-permute-start.26 = (bf16[4,128,128]{2,1,0:T(8,128)(2,1)S(1)}, bf16[4,128,128]{2,1,0:T(8,128)(2,1)S(1)}, u32[]{:S(2)}, u32[]{:S(2)}) collective-permute-start(bf16[4,128,128]{2,1,0:T(8,128)(2,1)S(1)} %get-tuple-element.72), channel_id=1, source_target_pairs={{0,4},{1,5},{2,6},{3,7},{4,0},{5,1},{6,2},{7,3},{8,12},{9,13},{10,... | collective-permute-start | bytes 393224 | tf_op jit(solution)/shard_map/ppermute | solution.py:57
  (66 shorter events, 21.9 us)
Async XLA Ops:
  0.0 19.8 %collective-permute-start = (bf16[256,768]{1,0:T(8,128)(2,1)}, bf16[256,768]{1,0:T(8,128)(2,1)S(1)}, u32[]{:S(2)}, u32[]{:S(2)}) collective-permute-start(bf16[256,768]{1,0:T(8,128)(2,1)} %w.1), channel_id=1, source_target_pairs={{0,16},{1,17},{2,18},{3,19},{4,20},{5,21},{6,22},{7,23},{8,24},{9,... | collective-permute-start | bytes 1179656 | tf_op jit(solution)/shard_map/ppermute | solution.py:57
  4.8 4.4 %collective-permute-start.3 = (bf16[128,256]{1,0:T(8,128)(2,1)S(1)}, bf16[128,256]{1,0:T(8,128)(2,1)S(1)}, u32[]{:S(2)}, u32[]{:S(2)}) collective-permute-start(bf16[128,256]{1,0:T(8,128)(2,1)S(1)} %get-tuple-element.41), channel_id=1, source_target_pairs={{0,3},{1,2},{2,1},{3,0},{4,7},{5,6},{6,5},{7,4},{8,11},{9,10},{10,... | collective-permute-start | bytes 196616 | tf_op jit(solution)/shard_map/ppermute | solution.py:57
  7.0 6.0 %collective-permute-start.1 = (bf16[336,256]{1,0:T(8,128)(2,1)S(1)}, bf16[336,256]{1,0:T(8,128)(2,1)S(1)}, u32[]{:S(2)}, u32[]{:S(2)}) collective-permute-start(bf16[336,256]{1,0:T(8,128)(2,1)S(1)} %get-tuple-element.39), channel_id=1, source_target_pairs={{0,1},{1,0},{2,3},{3,2},{4,5},{5,4},{6,7},{7,6},{8,9},{9,8},{10,11... | collective-permute-start | bytes 516104 | tf_op jit(solution)/shard_map/ppermute | solution.py:57
  7.3 5.8 %collective-permute-start.2 = (bf16[336,256]{1,0:T(8,128)(2,1)S(1)}, bf16[336,256]{1,0:T(8,128)(2,1)S(1)}, u32[]{:S(2)}, u32[]{:S(2)}) collective-permute-start(bf16[336,256]{1,0:T(8,128)(2,1)S(1)} %get-tuple-element.40), channel_id=1, source_target_pairs={{0,2},{1,3},{2,0},{3,1},{4,6},{5,7},{6,4},{7,5},{8,10},{9,11},{10,... | collective-permute-start | bytes 516104 | tf_op jit(solution)/shard_map/ppermute | solution.py:57
  9.2 15.0 %collective-permute-start.7 = (bf16[128,2048]{1,0:T(8,128)(2,1)}, bf16[128,2048]{1,0:T(8,128)(2,1)S(1)}, u32[]{:S(2)}, u32[]{:S(2)}) collective-permute-start(bf16[128,2048]{1,0:T(8,128)(2,1)} %bitcast.12), channel_id=1, source_target_pairs={{0,2},{1,3},{2,0},{3,1},{4,6},{5,7},{6,4},{7,5},{8,10},{9,11},{10,... | collective-permute-start | bytes 1572872 | tf_op jit(solution)/shard_map/ppermute | solution.py:57
  10.4 13.8 %collective-permute-start.6 = (bf16[128,2048]{1,0:T(8,128)(2,1)}, bf16[128,2048]{1,0:T(8,128)(2,1)S(1)}, u32[]{:S(2)}, u32[]{:S(2)}) collective-permute-start(bf16[128,2048]{1,0:T(8,128)(2,1)} %bitcast.13), channel_id=1, source_target_pairs={{0,1},{1,0},{2,3},{3,2},{4,5},{5,4},{6,7},{7,6},{8,9},{9,8},{10,11... | collective-permute-start | bytes 1572872 | tf_op jit(solution)/shard_map/ppermute | solution.py:57
  13.2 13.8 %collective-permute-start.8 = (bf16[256,768]{1,0:T(8,128)(2,1)S(1)}, bf16[256,768]{1,0:T(8,128)(2,1)S(1)}, u32[]{:S(2)}, u32[]{:S(2)}) collective-permute-start(bf16[256,768]{1,0:T(8,128)(2,1)S(1)} %shard_map.67.own.refs_2_.refs_0_), channel_id=1, source_target_pairs={{0,8},{1,9},{2,10},{3,11},{4,12},{5,13},{6,14},{7,15},{8,0},{9,1},... | collective-permute-start | bytes 1179656 | tf_op jit(solution)/shard_map/ppermute | solution.py:57
  19.9 5.8 %collective-permute-start.4 = (bf16[256,256]{1,0:T(8,128)(2,1)S(1)}, bf16[256,256]{1,0:T(8,128)(2,1)S(1)}, u32[]{:S(2)}, u32[]{:S(2)}) collective-permute-start(bf16[256,256]{1,0:T(8,128)(2,1)S(1)} %get-tuple-element.74), channel_id=1, source_target_pairs={{0,1},{1,0},{2,3},{3,2},{4,5},{5,4},{6,7},{7,6},{8,9},{9,8},{10,11... | collective-permute-start | bytes 393224 | tf_op jit(solution)/shard_map/ppermute | solution.py:57
  21.1 5.8 %collective-permute-start.5 = (bf16[256,256]{1,0:T(8,128)(2,1)S(1)}, bf16[256,256]{1,0:T(8,128)(2,1)S(1)}, u32[]{:S(2)}, u32[]{:S(2)}) collective-permute-start(bf16[256,256]{1,0:T(8,128)(2,1)S(1)} %get-tuple-element.73), channel_id=1, source_target_pairs={{0,2},{1,3},{2,0},{3,1},{4,6},{5,7},{6,4},{7,5},{8,10},{9,11},{10,... | collective-permute-start | bytes 393224 | tf_op jit(solution)/shard_map/ppermute | solution.py:57
  30.1 4.1 %collective-permute-start.10 = (bf16[384,2048]{1,0:T(8,128)(2,1)S(1)}, bf16[384,2048]{1,0:T(8,128)(2,1)S(1)}, u32[]{:S(2)}, u32[]{:S(2)}) collective-permute-start(bf16[384,2048]{1,0:T(8,128)(2,1)S(1)} %get-tuple-element.54.refs_0_), channel_id=1, source_target_pairs={{0,4},{1,5},{2,6},{3,7},{4,0},{5,1},{6,2},{7,3},{8,12},{9,13},{10,... | collective-permute-start | bytes 4718600 | tf_op jit(solution)/shard_map/ppermute | solution.py:57
  30.5 3.6 %collective-permute-start.12 = (bf16[528,384]{1,0:T(8,128)(2,1)S(1)}, bf16[528,384]{1,0:T(8,128)(2,1)S(1)}, u32[]{:S(2)}, u32[]{:S(2)}) collective-permute-start(bf16[528,384]{1,0:T(8,128)(2,1)S(1)} %shard_map.69), channel_id=1, source_target_pairs={{0,4},{1,5},{2,6},{3,7},{4,0},{5,1},{6,2},{7,3},{8,12},{9,13},{10,... | collective-permute-start | bytes 1216520 | tf_op jit(solution)/shard_map/ppermute | solution.py:57
  30.7 7.5 %collective-permute-start.13 = (bf16[128,1024]{1,0:T(8,128)(2,1)S(1)}, bf16[128,1024]{1,0:T(8,128)(2,1)S(1)}, u32[]{:S(2)}, u32[]{:S(2)}) collective-permute-start(bf16[128,1024]{1,0:T(8,128)(2,1)S(1)} %get-tuple-element.60), channel_id=1, source_target_pairs={{0,1},{1,0},{2,3},{3,2},{4,5},{5,4},{6,7},{7,6},{8,9},{9,8},{10,11... | collective-permute-start | bytes 786440 | tf_op jit(solution)/shard_map/ppermute | solution.py:57
  32.0 7.2 %collective-permute-start.11 = (bf16[128,1024]{1,0:T(8,128)(2,1)S(1)}, bf16[128,1024]{1,0:T(8,128)(2,1)S(1)}, u32[]{:S(2)}, u32[]{:S(2)}) collective-permute-start(bf16[128,1024]{1,0:T(8,128)(2,1)S(1)} %get-tuple-element.55), channel_id=1, source_target_pairs={{0,2},{1,3},{2,0},{3,1},{4,6},{5,7},{6,4},{7,5},{8,10},{9,11},{10,... | collective-permute-start | bytes 786440 | tf_op jit(solution)/shard_map/ppermute | solution.py:57
  32.4 11.2 %collective-permute-start.16 = (bf16[512,384]{1,0:T(8,128)(2,1)S(1)}, bf16[512,384]{1,0:T(8,128)(2,1)S(1)}, u32[]{:S(2)}, u32[]{:S(2)}) collective-permute-start(bf16[512,384]{1,0:T(8,128)(2,1)S(1)} %constant_dynamic-update-slice_fusion.refs_5_.refs_3_), channel_id=1, source_target_pairs={{0,8},{1,9},{2,10},{3,11},{4,12},{5,13},{6,14},{7,15},{8,0},{9,1},... | collective-permute-start | bytes 1179656 | tf_op jit(solution)/shard_map/ppermute | solution.py:57
  44.3 7.4 %collective-permute-start.17 = (bf16[4,256,128]{2,1,0:T(8,128)(2,1)S(1)}, bf16[4,256,128]{2,1,0:T(8,128)(2,1)S(1)}, u32[]{:S(2)}, u32[]{:S(2)}) collective-permute-start(bf16[4,256,128]{2,1,0:T(8,128)(2,1)S(1)} %get-tuple-element.68.own), channel_id=1, source_target_pairs={{0,8},{1,9},{2,10},{3,11},{4,12},{5,13},{6,14},{7,15},{8,0},{9,1},... | collective-permute-start | bytes 786440 | tf_op jit(solution)/shard_map/ppermute | solution.py:57
  45.3 9.7 %collective-permute-start.18 = (bf16[4,256,128]{2,1,0:T(8,128)(2,1)S(1)}, bf16[4,256,128]{2,1,0:T(8,128)(2,1)S(1)}, u32[]{:S(2)}, u32[]{:S(2)}) collective-permute-start(bf16[4,256,128]{2,1,0:T(8,128)(2,1)S(1)} %get-tuple-element.68.own), channel_id=1, source_target_pairs={{8,16},{9,17},{10,18},{11,19},{12,20},{13,21},{14,22},{15,23},{16,... | collective-permute-start | bytes 786440 | tf_op jit(solution)/shard_map/ppermute | solution.py:57
  49.5 6.7 %collective-permute-start.21 = (bf16[2,256,128]{2,1,0:T(8,128)(2,1)S(1)}, bf16[2,256,128]{2,1,0:T(8,128)(2,1)S(1)}, u32[]{:S(2)}, u32[]{:S(2)}) collective-permute-start(bf16[2,256,128]{2,1,0:T(8,128)(2,1)S(1)} %get-tuple-element.70.own), channel_id=1, source_target_pairs={{0,8},{1,9},{2,10},{3,11},{4,12},{5,13},{6,14},{7,15},{8,0},{9,1},... | collective-permute-start | bytes 393224 | tf_op jit(solution)/shard_map/ppermute | solution.py:57
  49.5 7.9 %collective-permute-start.22 = (bf16[2,256,128]{2,1,0:T(8,128)(2,1)S(1)}, bf16[2,256,128]{2,1,0:T(8,128)(2,1)S(1)}, u32[]{:S(2)}, u32[]{:S(2)}) collective-permute-start(bf16[2,256,128]{2,1,0:T(8,128)(2,1)S(1)} %get-tuple-element.70.own), channel_id=1, source_target_pairs={{8,16},{9,17},{10,18},{11,19},{12,20},{13,21},{14,22},{15,23},{16,... | collective-permute-start | bytes 393224 | tf_op jit(solution)/shard_map/ppermute | solution.py:57
  51.5 8.4 %collective-permute-start.19 = (bf16[2,256,128]{2,1,0:T(8,128)(2,1)S(1)}, bf16[2,256,128]{2,1,0:T(8,128)(2,1)S(1)}, u32[]{:S(2)}, u32[]{:S(2)}) collective-permute-start(bf16[2,256,128]{2,1,0:T(8,128)(2,1)S(1)} %get-tuple-element.69.own), channel_id=1, source_target_pairs={{0,8},{1,9},{2,10},{3,11},{4,12},{5,13},{6,14},{7,15},{8,0},{9,1},... | collective-permute-start | bytes 393224 | tf_op jit(solution)/shard_map/ppermute | solution.py:57
  51.7 8.5 %collective-permute-start.20 = (bf16[2,256,128]{2,1,0:T(8,128)(2,1)S(1)}, bf16[2,256,128]{2,1,0:T(8,128)(2,1)S(1)}, u32[]{:S(2)}, u32[]{:S(2)}) collective-permute-start(bf16[2,256,128]{2,1,0:T(8,128)(2,1)S(1)} %get-tuple-element.69.own), channel_id=1, source_target_pairs={{8,16},{9,17},{10,18},{11,19},{12,20},{13,21},{14,22},{15,23},{16,... | collective-permute-start | bytes 393224 | tf_op jit(solution)/shard_map/ppermute | solution.py:57
  57.7 5.8 %collective-permute-start.25 = (bf16[256,128]{1,0:T(8,128)(2,1)S(1)}, bf16[256,128]{1,0:T(8,128)(2,1)S(1)}, u32[]{:S(2)}, u32[]{:S(2)}) collective-permute-start(bf16[256,128]{1,0:T(8,128)(2,1)S(1)} %shard_map.78), channel_id=1, source_target_pairs={{0,3},{1,2},{2,1},{3,0},{4,7},{5,6},{6,5},{7,4},{8,11},{9,10},{10,... | collective-permute-start | bytes 196616 | tf_op jit(solution)/shard_map/ppermute | solution.py:57
  60.5 3.8 %collective-permute-start.24 = (bf16[256,128]{1,0:T(8,128)(2,1)S(1)}, bf16[256,128]{1,0:T(8,128)(2,1)S(1)}, u32[]{:S(2)}, u32[]{:S(2)}) collective-permute-start(bf16[256,128]{1,0:T(8,128)(2,1)S(1)} %shard_map.77), channel_id=1, source_target_pairs={{0,2},{1,3},{2,0},{3,1},{4,6},{5,7},{6,4},{7,5},{8,10},{9,11},{10,... | collective-permute-start | bytes 196616 | tf_op jit(solution)/shard_map/ppermute | solution.py:57
  62.9 3.5 %collective-permute-start.23 = (bf16[256,128]{1,0:T(8,128)(2,1)S(1)}, bf16[256,128]{1,0:T(8,128)(2,1)S(1)}, u32[]{:S(2)}, u32[]{:S(2)}) collective-permute-start(bf16[256,128]{1,0:T(8,128)(2,1)S(1)} %shard_map.76), channel_id=1, source_target_pairs={{0,1},{1,0},{2,3},{3,2},{4,5},{5,4},{6,7},{7,6},{8,9},{9,8},{10,11... | collective-permute-start | bytes 196616 | tf_op jit(solution)/shard_map/ppermute | solution.py:57
  66.4 3.4 %collective-permute-start.26 = (bf16[4,128,128]{2,1,0:T(8,128)(2,1)S(1)}, bf16[4,128,128]{2,1,0:T(8,128)(2,1)S(1)}, u32[]{:S(2)}, u32[]{:S(2)}) collective-permute-start(bf16[4,128,128]{2,1,0:T(8,128)(2,1)S(1)} %get-tuple-element.72), channel_id=1, source_target_pairs={{0,4},{1,5},{2,6},{3,7},{4,0},{5,1},{6,2},{7,3},{8,12},{9,13},{10,... | collective-permute-start | bytes 393224 | tf_op jit(solution)/shard_map/ppermute | solution.py:57
  (9 other events, 40.0 us)

commit v20 on v19

--- a/solution.py
+++ b/solution.py
@@ -214,22 +214,26 @@
 ROW_ORDER = ((0, 1, 2, 6), (3, 4, 5, 7))
 
 
-def finish_kernel(*refs):
-    x_refs, (last, acc_in, acc_diagonal, q_ref, k_ref, v_first, v_second) = refs[:3], refs[3:]
+def finish_kernel(thirds, *refs):
+    x_refs, (last, acc_in, acc_diagonal), out_refs = refs[:3], refs[3:6], refs[6:]
     z, core, _ = where_am_i()
-    block, early = q_ref.shape[1] // 2, acc_in.shape[0]
-    value = jnp.dot(take(x_refs, z ^ 3, core, last.shape[0]), last[...], preferred_element_type=jnp.float32)
-    value = [acc_in[...] + value[:early], acc_diagonal[...] + value[early:]]
-    value = jnp.concatenate(value, axis=0).astype(jnp.bfloat16)
-    for rel in range(2):
-        at = pl.ds(pl.multiple_of((core ^ rel) * block, block), block)
-        for r in range(4):
-            row = ROW_ORDER[rel][r]
-            mine = value[row * block : (row + 1) * block]
-            v_at = V_ORDER.index(r)
-            q_ref[r, at, :] = mine[:, :HD]
-            k_ref[r, at, :] = mine[:, HD:PAIR]
-            (v_first, v_second)[v_at // 2][v_at % 2, at, :] = mine[:, PAIR:]
+    early = acc_in.shape[0]
+    block = early // 6
+    x = take(x_refs, z ^ 3, core, last.shape[0])
+    for third in thirds:
+        columns = slice(third * HD, (third + 1) * HD)
+        value = jnp.dot(x, last[:, columns], preferred_element_type=jnp.float32)
+        value = [acc_in[:, columns] + value[:early], acc_diagonal[:, columns] + value[early:]]
+        value = jnp.concatenate(value, axis=0).astype(jnp.bfloat16)
+        for rel in range(2):
+            at = pl.ds(pl.multiple_of((core ^ rel) * block, block), block)
+            for r in range(4):
+                mine = value[ROW_ORDER[rel][r] * block : (ROW_ORDER[rel][r] + 1) * block]
+                v_at = V_ORDER.index(r)
+                if third == 2:
+                    out_refs[1 + v_at // 2][v_at % 2, at, :] = mine
+                else:
+                    out_refs[0][r, at, :] = mine
 
 
 def spans(u):
@@ -387,9 +391,10 @@
         macs=2 * block * 3 * rows * 3 * HD,
     )(diagonal, *swapped, *weights)
     one_head, half_head = array(4, 2 * block, HD), array(2, 2 * block, HD)
-    q, k, *v = call(
-        finish_kernel, (one_head, one_head, half_head, half_head), "v" * 6, macs=8 * block * rows * 3 * HD
-    )(*early, diagonal, last, total, total_diagonal)
+    sums = (*early, diagonal, last, total, total_diagonal)
+    macs = 8 * block * rows * HD
+    (k,) = call(functools.partial(finish_kernel, (1,)), (one_head,), "v" * 6, macs=macs)(*sums)
+    q, *v = call(functools.partial(finish_kernel, (0, 2)), (one_head, half_head, half_head), "v" * 6, macs=2 * macs)(*sums)
 
     weights = call(weigh_kernel, array(4, 2 * block, 5 * block), "v" * 6, macs=8 * block * 5 * block * HD)(
         q, swap_z(k, 1), k, swap_middle(k), flags, received

time: 71.1 us -> 70.8 us (level)
  transfers between devices with their start and end apart: 27 -> 27, of which waited for: 15 -> 15; matrix products, arithmetic and copies ran while one was open for 2% -> 2% of each run, Pallas kernels for 10% -> 11%
where the time goes in v20:
time: 70.8 us; the launch traced here: 70.3 us
  starting transfers between devices  34.8 us (49%)
  waiting for transfers between devices  21.9 us (31%)
  Pallas kernels  8.81 us (12%)
  local copies, waits for them, and re-layouts  3.18 us (4%)
  other arithmetic  1.45 us (2%)
    ppermute x27, starting transfers between devices, hop(): return lax.ppermute(value, ('tm', 'depth'), pairs)  34.8 us
    ppermute x27, waiting for transfers between devices, hop(): return lax.ppermute(value, ('tm', 'depth'), pairs)  21.9 us
    unnamed x13, local copies, waits for them, and re-layouts  3.13 us
    pallas_call x3, Pallas kernels, embed(): call(functools.partial(embed_kernel, rs, len(finished)), out, 'v' * (6 +...  2.39 us
  transfers between devices with their start and end apart: 27, of which 15 were waited for; matrix products, arithmetic and copies ran while one was open for 2% of the time, Pallas kernels for 11%

profile of v20, /device:TPU:9, one launch (start us, length us, event | category | flops | bytes accessed | tf_op | source)
XLA Modules:
  0.0 70.3 jit_solution(12725203922075112014)
XLA Ops:
  0.0 2.3 %collective-permute-start = (bf16[256,768]{1,0:T(8,128)(2,1)}, bf16[256,768]{1,0:T(8,128)(2,1)S(1)}, u32[]{:S(2)}, u32[]{:S(2)}) collective-permute-start(bf16[256,768]{1,0:T(8,128)(2,1)} %w.1), channel_id=1, source_target_pairs={{0,16},{1,17},{2,18},{3,19},{4,20},{5,21},{6,22},{7,23},{8,24},{9,... | collective-permute-start | bytes 1179656 | tf_op jit(solution)/shard_map/ppermute | solution.py:57
  4.8 2.2 %collective-permute-start.3 = (bf16[128,256]{1,0:T(8,128)(2,1)S(1)}, bf16[128,256]{1,0:T(8,128)(2,1)S(1)}, u32[]{:S(2)}, u32[]{:S(2)}) collective-permute-start(bf16[128,256]{1,0:T(8,128)(2,1)S(1)} %get-tuple-element.40), channel_id=1, source_target_pairs={{0,3},{1,2},{2,1},{3,0},{4,7},{5,6},{6,5},{7,4},{8,11},{9,10},{10,... | collective-permute-start | bytes 196616 | tf_op jit(solution)/shard_map/ppermute | solution.py:57
  7.5 1.7 %collective-permute-done.3.across = bf16[128,256]{1,0:T(8,128)(2,1)S(1)} collective-permute-done((bf16[128,256]{1,0:T(8,128)(2,1)S(1)}, bf16[128,256]{1,0:T(8,128)(2,1)S(1)}, u32[]{:S(2)}, u32[]{:S(2)}) %collective-permute-start.3) | collective-permute-done | bytes 65568 | tf_op jit(solution)/shard_map/ppermute | solution.py:57
  9.2 1.2 %collective-permute-start.7 = (bf16[128,2048]{1,0:T(8,128)(2,1)}, bf16[128,2048]{1,0:T(8,128)(2,1)S(1)}, u32[]{:S(2)}, u32[]{:S(2)}) collective-permute-start(bf16[128,2048]{1,0:T(8,128)(2,1)} %bitcast.12), channel_id=1, source_target_pairs={{0,2},{1,3},{2,0},{3,1},{4,6},{5,7},{6,4},{7,5},{8,10},{9,11},{10,... | collective-permute-start | bytes 1572872 | tf_op jit(solution)/shard_map/ppermute | solution.py:57
  11.6 1.4 %collective-permute-done.1.plane_x.from_x = bf16[336,256]{1,0:T(8,128)(2,1)S(1)} collective-permute-done((bf16[336,256]{1,0:T(8,128)(2,1)S(1)}, bf16[336,256]{1,0:T(8,128)(2,1)S(1)}, u32[]{:S(2)}, u32[]{:S(2)}) %collective-permute-start.1) | collective-permute-done | bytes 172064 | tf_op jit(solution)/shard_map/ppermute | solution.py:57
  13.4 1.4 %copy-done = bf16[3,128,2048]{2,1,0:T(8,128)(2,1)S(1)} copy-done((bf16[3,128,2048]{2,1,0:T(8,128)(2,1)S(1)}, bf16[3,128,2048]{2,1,0:T(8,128)(2,1)}, u32[]{:S(2)}) %copy-start) | copy-done | bytes 1572888
  16.1 3.7 %collective-permute-done = bf16[256,768]{1,0:T(8,128)(2,1)S(1)} collective-permute-done((bf16[256,768]{1,0:T(8,128)(2,1)}, bf16[256,768]{1,0:T(8,128)(2,1)S(1)}, u32[]{:S(2)}, u32[]{:S(2)}) %collective-permute-start) | collective-permute-done | bytes 393248 | tf_op jit(solution)/shard_map/ppermute | solution.py:57
  19.9 1.3 %collective-permute-start.4 = (bf16[256,256]{1,0:T(8,128)(2,1)S(1)}, bf16[256,256]{1,0:T(8,128)(2,1)S(1)}, u32[]{:S(2)}, u32[]{:S(2)}) collective-permute-start(bf16[256,256]{1,0:T(8,128)(2,1)S(1)} %get-tuple-element.72), channel_id=1, source_target_pairs={{0,1},{1,0},{2,3},{3,2},{4,5},{5,4},{6,7},{7,6},{8,9},{9,8},{10,11... | collective-permute-start | bytes 393224 | tf_op jit(solution)/shard_map/ppermute | solution.py:57
  21.1 1.2 %collective-permute-start.5 = (bf16[256,256]{1,0:T(8,128)(2,1)S(1)}, bf16[256,256]{1,0:T(8,128)(2,1)S(1)}, u32[]{:S(2)}, u32[]{:S(2)}) collective-permute-start(bf16[256,256]{1,0:T(8,128)(2,1)S(1)} %get-tuple-element.71), channel_id=1, source_target_pairs={{0,2},{1,3},{2,0},{3,1},{4,6},{5,7},{6,4},{7,5},{8,10},{9,11},{10,... | collective-permute-start | bytes 393224 | tf_op jit(solution)/shard_map/ppermute | solution.py:57
  22.4 1.8 %collective-permute-done.7.refs_1_ = bf16[128,2048]{1,0:T(8,128)(2,1)S(1)} collective-permute-done((bf16[128,2048]{1,0:T(8,128)(2,1)}, bf16[128,2048]{1,0:T(8,128)(2,1)S(1)}, u32[]{:S(2)}, u32[]{:S(2)}) %collective-permute-start.7) | collective-permute-done | bytes 524320 | tf_op jit(solution)/shard_map/ppermute | solution.py:57
  25.6 1.3 %collective-permute-done.5.from_y = bf16[256,256]{1,0:T(8,128)(2,1)S(1)} collective-permute-done((bf16[256,256]{1,0:T(8,128)(2,1)S(1)}, bf16[256,256]{1,0:T(8,128)(2,1)S(1)}, u32[]{:S(2)}, u32[]{:S(2)}) %collective-permute-start.5) | collective-permute-done | bytes 131104 | tf_op jit(solution)/shard_map/ppermute | solution.py:57
  27.1 1.9 %collective-permute-start.9 = (bf16[256,384]{1,0:T(8,128)(2,1)S(1)}, bf16[256,384]{1,0:T(8,128)(2,1)S(1)}, u32[]{:S(2)}, u32[]{:S(2)}) collective-permute-start(bf16[256,384]{1,0:T(8,128)(2,1)S(1)} %get-tuple-element.50), channel_id=1, source_target_pairs={{0,4},{1,5},{2,6},{3,7},{4,0},{5,1},{6,2},{7,3},{8,12},{9,13},{10,... | collective-permute-start | bytes 589832 | tf_op jit(solution)/shard_map/ppermute | solution.py:57
  32.4 1.7 %collective-permute-start.16 = (bf16[512,384]{1,0:T(8,128)(2,1)S(1)}, bf16[512,384]{1,0:T(8,128)(2,1)S(1)}, u32[]{:S(2)}, u32[]{:S(2)}) collective-permute-start(bf16[512,384]{1,0:T(8,128)(2,1)S(1)} %constant_dynamic-update-slice_fusion.refs_5_.refs_3_), channel_id=1, source_target_pairs={{0,8},{1,9},{2,10},{3,11},{4,12},{5,13},{6,14},{7,15},{8,0},{9,1},... | collective-permute-start | bytes 1179656 | tf_op jit(solution)/shard_map/ppermute | solution.py:57
  34.1 1.4 %shard_map.70.refs_4_ = f32[768,384]{1,0:T(8,128)S(1)} custom-call(bf16[384,2048]{1,0:T(8,128)(2,1)S(1)} %get-tuple-element.53.refs_0_, bf16[384,2048]{1,0:T(8,128)(2,1)S(1)} %collective-permute-done.10.refs_1_, bf16[256,768]{1,0:T(8,128)(2,1)S(1)} %shard_map.67.own.refs_2_.refs_0_, bf16[256,768]{1,0:T(8,128)(2,1)S(1)} %collective-permute-done.8.near.refs_3_.refs_1_, ...), custom_call_target="tpu_custom_call" | custom-call | flops 905969664 | tf_op jit(solution)/shard_map/pallas_call | solution.py:382
  35.5 2.8 %collective-permute-done.13.refs_1_ = bf16[128,1024]{1,0:T(8,128)(2,1)S(1)} collective-permute-done((bf16[128,1024]{1,0:T(8,128)(2,1)S(1)}, bf16[128,1024]{1,0:T(8,128)(2,1)S(1)}, u32[]{:S(2)}, u32[]{:S(2)}) %collective-permute-start.13) | collective-permute-done | bytes 262176 | tf_op jit(solution)/shard_map/ppermute | solution.py:57
  39.8 1.6 %collective-permute-start.14 = (bf16[80,2048]{1,0:T(8,128)(2,1)S(1)}, bf16[80,2048]{1,0:T(8,128)(2,1)S(1)}, u32[]{:S(2)}, u32[]{:S(2)}) collective-permute-start(bf16[80,2048]{1,0:T(8,128)(2,1)S(1)} %get-tuple-element.62), channel_id=1, source_target_pairs={{0,4},{1,5},{2,6},{3,7},{4,0},{5,1},{6,2},{7,3},{8,12},{9,13},{10,... | collective-permute-start | bytes 983048 | tf_op jit(solution)/shard_map/ppermute | solution.py:57
  41.5 1.5 %collective-permute-done.15.bottom = bf16[48,2048]{1,0:T(8,128)(2,1)S(1)} collective-permute-done((bf16[48,2048]{1,0:T(8,128)(2,1)S(1)}, bf16[48,2048]{1,0:T(8,128)(2,1)S(1)}, u32[]{:S(2)}, u32[]{:S(2)}) %collective-permute-start.15) | collective-permute-done | bytes 196640 | tf_op jit(solution)/shard_map/ppermute | solution.py:57
  45.0 4.2 %collective-permute-start.18 = (bf16[4,256,128]{2,1,0:T(8,128)(2,1)S(1)}, bf16[4,256,128]{2,1,0:T(8,128)(2,1)S(1)}, u32[]{:S(2)}, u32[]{:S(2)}) collective-permute-start(bf16[4,256,128]{2,1,0:T(8,128)(2,1)S(1)} %shard_map.74.own), channel_id=1, source_target_pairs={{8,16},{9,17},{10,18},{11,19},{12,20},{13,21},{14,22},{15,23},{16,... | collective-permute-start | bytes 786440 | tf_op jit(solution)/shard_map/ppermute | solution.py:57
  50.0 1.9 %collective-permute-start.22 = (bf16[2,256,128]{2,1,0:T(8,128)(2,1)S(1)}, bf16[2,256,128]{2,1,0:T(8,128)(2,1)S(1)}, u32[]{:S(2)}, u32[]{:S(2)}) collective-permute-start(bf16[2,256,128]{2,1,0:T(8,128)(2,1)S(1)} %get-tuple-element.68.own), channel_id=1, source_target_pairs={{8,16},{9,17},{10,18},{11,19},{12,20},{13,21},{14,22},{15,23},{16,... | collective-permute-start | bytes 393224 | tf_op jit(solution)/shard_map/ppermute | solution.py:57
  52.2 3.2 %collective-permute-start.20 = (bf16[2,256,128]{2,1,0:T(8,128)(2,1)S(1)}, bf16[2,256,128]{2,1,0:T(8,128)(2,1)S(1)}, u32[]{:S(2)}, u32[]{:S(2)}) collective-permute-start(bf16[2,256,128]{2,1,0:T(8,128)(2,1)S(1)} %get-tuple-element.67.own), channel_id=1, source_target_pairs={{8,16},{9,17},{10,18},{11,19},{12,20},{13,21},{14,22},{15,23},{16,... | collective-permute-start | bytes 393224 | tf_op jit(solution)/shard_map/ppermute | solution.py:57
  57.7 1.9 %collective-permute-start.25 = (bf16[256,128]{1,0:T(8,128)(2,1)S(1)}, bf16[256,128]{1,0:T(8,128)(2,1)S(1)}, u32[]{:S(2)}, u32[]{:S(2)}) collective-permute-start(bf16[256,128]{1,0:T(8,128)(2,1)S(1)} %shard_map.79), channel_id=1, source_target_pairs={{0,3},{1,2},{2,1},{3,0},{4,7},{5,6},{6,5},{7,4},{8,11},{9,10},{10,... | collective-permute-start | bytes 196616 | tf_op jit(solution)/shard_map/ppermute | solution.py:57
  60.5 1.9 %collective-permute-start.24 = (bf16[256,128]{1,0:T(8,128)(2,1)S(1)}, bf16[256,128]{1,0:T(8,128)(2,1)S(1)}, u32[]{:S(2)}, u32[]{:S(2)}) collective-permute-start(bf16[256,128]{1,0:T(8,128)(2,1)S(1)} %shard_map.78), channel_id=1, source_target_pairs={{0,2},{1,3},{2,0},{3,1},{4,6},{5,7},{6,4},{7,5},{8,10},{9,11},{10,... | collective-permute-start | bytes 196616 | tf_op jit(solution)/shard_map/ppermute | solution.py:57
  64.0 2.1 %collective-permute-done.23.refs_1_ = bf16[256,128]{1,0:T(8,128)(2,1)S(1)} collective-permute-done((bf16[256,128]{1,0:T(8,128)(2,1)S(1)}, bf16[256,128]{1,0:T(8,128)(2,1)S(1)}, u32[]{:S(2)}, u32[]{:S(2)}) %collective-permute-start.23) | collective-permute-done | bytes 65568 | tf_op jit(solution)/shard_map/ppermute | solution.py:57
  66.1 2.4 %collective-permute-start.26 = (bf16[4,128,128]{2,1,0:T(8,128)(2,1)S(1)}, bf16[4,128,128]{2,1,0:T(8,128)(2,1)S(1)}, u32[]{:S(2)}, u32[]{:S(2)}) collective-permute-start(bf16[4,128,128]{2,1,0:T(8,128)(2,1)S(1)} %get-tuple-element.70), channel_id=1, source_target_pairs={{0,4},{1,5},{2,6},{3,7},{4,0},{5,1},{6,2},{7,3},{8,12},{9,13},{10,... | collective-permute-start | bytes 393224 | tf_op jit(solution)/shard_map/ppermute | solution.py:57
  (67 shorter events, 22.3 us)
Async XLA Ops:
  0.0 19.8 %collective-permute-start = (bf16[256,768]{1,0:T(8,128)(2,1)}, bf16[256,768]{1,0:T(8,128)(2,1)S(1)}, u32[]{:S(2)}, u32[]{:S(2)}) collective-permute-start(bf16[256,768]{1,0:T(8,128)(2,1)} %w.1), channel_id=1, source_target_pairs={{0,16},{1,17},{2,18},{3,19},{4,20},{5,21},{6,22},{7,23},{8,24},{9,... | collective-permute-start | bytes 1179656 | tf_op jit(solution)/shard_map/ppermute | solution.py:57
  4.8 4.4 %collective-permute-start.3 = (bf16[128,256]{1,0:T(8,128)(2,1)S(1)}, bf16[128,256]{1,0:T(8,128)(2,1)S(1)}, u32[]{:S(2)}, u32[]{:S(2)}) collective-permute-start(bf16[128,256]{1,0:T(8,128)(2,1)S(1)} %get-tuple-element.40), channel_id=1, source_target_pairs={{0,3},{1,2},{2,1},{3,0},{4,7},{5,6},{6,5},{7,4},{8,11},{9,10},{10,... | collective-permute-start | bytes 196616 | tf_op jit(solution)/shard_map/ppermute | solution.py:57
  7.0 6.0 %collective-permute-start.1 = (bf16[336,256]{1,0:T(8,128)(2,1)S(1)}, bf16[336,256]{1,0:T(8,128)(2,1)S(1)}, u32[]{:S(2)}, u32[]{:S(2)}) collective-permute-start(bf16[336,256]{1,0:T(8,128)(2,1)S(1)} %get-tuple-element.38), channel_id=1, source_target_pairs={{0,1},{1,0},{2,3},{3,2},{4,5},{5,4},{6,7},{7,6},{8,9},{9,8},{10,11... | collective-permute-start | bytes 516104 | tf_op jit(solution)/shard_map/ppermute | solution.py:57
  7.3 5.8 %collective-permute-start.2 = (bf16[336,256]{1,0:T(8,128)(2,1)S(1)}, bf16[336,256]{1,0:T(8,128)(2,1)S(1)}, u32[]{:S(2)}, u32[]{:S(2)}) collective-permute-start(bf16[336,256]{1,0:T(8,128)(2,1)S(1)} %get-tuple-element.39), channel_id=1, source_target_pairs={{0,2},{1,3},{2,0},{3,1},{4,6},{5,7},{6,4},{7,5},{8,10},{9,11},{10,... | collective-permute-start | bytes 516104 | tf_op jit(solution)/shard_map/ppermute | solution.py:57
  9.2 15.0 %collective-permute-start.7 = (bf16[128,2048]{1,0:T(8,128)(2,1)}, bf16[128,2048]{1,0:T(8,128)(2,1)S(1)}, u32[]{:S(2)}, u32[]{:S(2)}) collective-permute-start(bf16[128,2048]{1,0:T(8,128)(2,1)} %bitcast.12), channel_id=1, source_target_pairs={{0,2},{1,3},{2,0},{3,1},{4,6},{5,7},{6,4},{7,5},{8,10},{9,11},{10,... | collective-permute-start | bytes 1572872 | tf_op jit(solution)/shard_map/ppermute | solution.py:57
  10.4 13.8 %collective-permute-start.6 = (bf16[128,2048]{1,0:T(8,128)(2,1)}, bf16[128,2048]{1,0:T(8,128)(2,1)S(1)}, u32[]{:S(2)}, u32[]{:S(2)}) collective-permute-start(bf16[128,2048]{1,0:T(8,128)(2,1)} %bitcast.13), channel_id=1, source_target_pairs={{0,1},{1,0},{2,3},{3,2},{4,5},{5,4},{6,7},{7,6},{8,9},{9,8},{10,11... | collective-permute-start | bytes 1572872 | tf_op jit(solution)/shard_map/ppermute | solution.py:57
  13.2 13.8 %collective-permute-start.8 = (bf16[256,768]{1,0:T(8,128)(2,1)S(1)}, bf16[256,768]{1,0:T(8,128)(2,1)S(1)}, u32[]{:S(2)}, u32[]{:S(2)}) collective-permute-start(bf16[256,768]{1,0:T(8,128)(2,1)S(1)} %shard_map.67.own.refs_2_.refs_0_), channel_id=1, source_target_pairs={{0,8},{1,9},{2,10},{3,11},{4,12},{5,13},{6,14},{7,15},{8,0},{9,1},... | collective-permute-start | bytes 1179656 | tf_op jit(solution)/shard_map/ppermute | solution.py:57
  19.9 5.8 %collective-permute-start.4 = (bf16[256,256]{1,0:T(8,128)(2,1)S(1)}, bf16[256,256]{1,0:T(8,128)(2,1)S(1)}, u32[]{:S(2)}, u32[]{:S(2)}) collective-permute-start(bf16[256,256]{1,0:T(8,128)(2,1)S(1)} %get-tuple-element.72), channel_id=1, source_target_pairs={{0,1},{1,0},{2,3},{3,2},{4,5},{5,4},{6,7},{7,6},{8,9},{9,8},{10,11... | collective-permute-start | bytes 393224 | tf_op jit(solution)/shard_map/ppermute | solution.py:57
  21.1 5.8 %collective-permute-start.5 = (bf16[256,256]{1,0:T(8,128)(2,1)S(1)}, bf16[256,256]{1,0:T(8,128)(2,1)S(1)}, u32[]{:S(2)}, u32[]{:S(2)}) collective-permute-start(bf16[256,256]{1,0:T(8,128)(2,1)S(1)} %get-tuple-element.71), channel_id=1, source_target_pairs={{0,2},{1,3},{2,0},{3,1},{4,6},{5,7},{6,4},{7,5},{8,10},{9,11},{10,... | collective-permute-start | bytes 393224 | tf_op jit(solution)/shard_map/ppermute | solution.py:57
  30.1 4.1 %collective-permute-start.10 = (bf16[384,2048]{1,0:T(8,128)(2,1)S(1)}, bf16[384,2048]{1,0:T(8,128)(2,1)S(1)}, u32[]{:S(2)}, u32[]{:S(2)}) collective-permute-start(bf16[384,2048]{1,0:T(8,128)(2,1)S(1)} %get-tuple-element.53.refs_0_), channel_id=1, source_target_pairs={{0,4},{1,5},{2,6},{3,7},{4,0},{5,1},{6,2},{7,3},{8,12},{9,13},{10,... | collective-permute-start | bytes 4718600 | tf_op jit(solution)/shard_map/ppermute | solution.py:57
  30.5 3.6 %collective-permute-start.12 = (bf16[528,384]{1,0:T(8,128)(2,1)S(1)}, bf16[528,384]{1,0:T(8,128)(2,1)S(1)}, u32[]{:S(2)}, u32[]{:S(2)}) collective-permute-start(bf16[528,384]{1,0:T(8,128)(2,1)S(1)} %shard_map.69), channel_id=1, source_target_pairs={{0,4},{1,5},{2,6},{3,7},{4,0},{5,1},{6,2},{7,3},{8,12},{9,13},{10,... | collective-permute-start | bytes 1216520 | tf_op jit(solution)/shard_map/ppermute | solution.py:57
  30.7 7.5 %collective-permute-start.13 = (bf16[128,1024]{1,0:T(8,128)(2,1)S(1)}, bf16[128,1024]{1,0:T(8,128)(2,1)S(1)}, u32[]{:S(2)}, u32[]{:S(2)}) collective-permute-start(bf16[128,1024]{1,0:T(8,128)(2,1)S(1)} %get-tuple-element.59), channel_id=1, source_target_pairs={{0,1},{1,0},{2,3},{3,2},{4,5},{5,4},{6,7},{7,6},{8,9},{9,8},{10,11... | collective-permute-start | bytes 786440 | tf_op jit(solution)/shard_map/ppermute | solution.py:57
  32.0 7.2 %collective-permute-start.11 = (bf16[128,1024]{1,0:T(8,128)(2,1)S(1)}, bf16[128,1024]{1,0:T(8,128)(2,1)S(1)}, u32[]{:S(2)}, u32[]{:S(2)}) collective-permute-start(bf16[128,1024]{1,0:T(8,128)(2,1)S(1)} %get-tuple-element.54), channel_id=1, source_target_pairs={{0,2},{1,3},{2,0},{3,1},{4,6},{5,7},{6,4},{7,5},{8,10},{9,11},{10,... | collective-permute-start | bytes 786440 | tf_op jit(solution)/shard_map/ppermute | solution.py:57
  32.4 11.2 %collective-permute-start.16 = (bf16[512,384]{1,0:T(8,128)(2,1)S(1)}, bf16[512,384]{1,0:T(8,128)(2,1)S(1)}, u32[]{:S(2)}, u32[]{:S(2)}) collective-permute-start(bf16[512,384]{1,0:T(8,128)(2,1)S(1)} %constant_dynamic-update-slice_fusion.refs_5_.refs_3_), channel_id=1, source_target_pairs={{0,8},{1,9},{2,10},{3,11},{4,12},{5,13},{6,14},{7,15},{8,0},{9,1},... | collective-permute-start | bytes 1179656 | tf_op jit(solution)/shard_map/ppermute | solution.py:57
  44.0 8.1 %collective-permute-start.17 = (bf16[4,256,128]{2,1,0:T(8,128)(2,1)S(1)}, bf16[4,256,128]{2,1,0:T(8,128)(2,1)S(1)}, u32[]{:S(2)}, u32[]{:S(2)}) collective-permute-start(bf16[4,256,128]{2,1,0:T(8,128)(2,1)S(1)} %shard_map.74.own), channel_id=1, source_target_pairs={{0,8},{1,9},{2,10},{3,11},{4,12},{5,13},{6,14},{7,15},{8,0},{9,1},... | collective-permute-start | bytes 786440 | tf_op jit(solution)/shard_map/ppermute | solution.py:57
  45.0 10.4 %collective-permute-start.18 = (bf16[4,256,128]{2,1,0:T(8,128)(2,1)S(1)}, bf16[4,256,128]{2,1,0:T(8,128)(2,1)S(1)}, u32[]{:S(2)}, u32[]{:S(2)}) collective-permute-start(bf16[4,256,128]{2,1,0:T(8,128)(2,1)S(1)} %shard_map.74.own), channel_id=1, source_target_pairs={{8,16},{9,17},{10,18},{11,19},{12,20},{13,21},{14,22},{15,23},{16,... | collective-permute-start | bytes 786440 | tf_op jit(solution)/shard_map/ppermute | solution.py:57
  49.9 6.7 %collective-permute-start.21 = (bf16[2,256,128]{2,1,0:T(8,128)(2,1)S(1)}, bf16[2,256,128]{2,1,0:T(8,128)(2,1)S(1)}, u32[]{:S(2)}, u32[]{:S(2)}) collective-permute-start(bf16[2,256,128]{2,1,0:T(8,128)(2,1)S(1)} %get-tuple-element.68.own), channel_id=1, source_target_pairs={{0,8},{1,9},{2,10},{3,11},{4,12},{5,13},{6,14},{7,15},{8,0},{9,1},... | collective-permute-start | bytes 393224 | tf_op jit(solution)/shard_map/ppermute | solution.py:57
  50.0 7.5 %collective-permute-start.22 = (bf16[2,256,128]{2,1,0:T(8,128)(2,1)S(1)}, bf16[2,256,128]{2,1,0:T(8,128)(2,1)S(1)}, u32[]{:S(2)}, u32[]{:S(2)}) collective-permute-start(bf16[2,256,128]{2,1,0:T(8,128)(2,1)S(1)} %get-tuple-element.68.own), channel_id=1, source_target_pairs={{8,16},{9,17},{10,18},{11,19},{12,20},{13,21},{14,22},{15,23},{16,... | collective-permute-start | bytes 393224 | tf_op jit(solution)/shard_map/ppermute | solution.py:57
  51.9 7.7 %collective-permute-start.19 = (bf16[2,256,128]{2,1,0:T(8,128)(2,1)S(1)}, bf16[2,256,128]{2,1,0:T(8,128)(2,1)S(1)}, u32[]{:S(2)}, u32[]{:S(2)}) collective-permute-start(bf16[2,256,128]{2,1,0:T(8,128)(2,1)S(1)} %get-tuple-element.67.own), channel_id=1, source_target_pairs={{0,8},{1,9},{2,10},{3,11},{4,12},{5,13},{6,14},{7,15},{8,0},{9,1},... | collective-permute-start | bytes 393224 | tf_op jit(solution)/shard_map/ppermute | solution.py:57
  52.2 8.1 %collective-permute-start.20 = (bf16[2,256,128]{2,1,0:T(8,128)(2,1)S(1)}, bf16[2,256,128]{2,1,0:T(8,128)(2,1)S(1)}, u32[]{:S(2)}, u32[]{:S(2)}) collective-permute-start(bf16[2,256,128]{2,1,0:T(8,128)(2,1)S(1)} %get-tuple-element.67.own), channel_id=1, source_target_pairs={{8,16},{9,17},{10,18},{11,19},{12,20},{13,21},{14,22},{15,23},{16,... | collective-permute-start | bytes 393224 | tf_op jit(solution)/shard_map/ppermute | solution.py:57
  57.7 5.5 %collective-permute-start.25 = (bf16[256,128]{1,0:T(8,128)(2,1)S(1)}, bf16[256,128]{1,0:T(8,128)(2,1)S(1)}, u32[]{:S(2)}, u32[]{:S(2)}) collective-permute-start(bf16[256,128]{1,0:T(8,128)(2,1)S(1)} %shard_map.79), channel_id=1, source_target_pairs={{0,3},{1,2},{2,1},{3,0},{4,7},{5,6},{6,5},{7,4},{8,11},{9,10},{10,... | collective-permute-start | bytes 196616 | tf_op jit(solution)/shard_map/ppermute | solution.py:57
  60.5 3.5 %collective-permute-start.24 = (bf16[256,128]{1,0:T(8,128)(2,1)S(1)}, bf16[256,128]{1,0:T(8,128)(2,1)S(1)}, u32[]{:S(2)}, u32[]{:S(2)}) collective-permute-start(bf16[256,128]{1,0:T(8,128)(2,1)S(1)} %shard_map.78), channel_id=1, source_target_pairs={{0,2},{1,3},{2,0},{3,1},{4,6},{5,7},{6,4},{7,5},{8,10},{9,11},{10,... | collective-permute-start | bytes 196616 | tf_op jit(solution)/shard_map/ppermute | solution.py:57
  62.6 3.5 %collective-permute-start.23 = (bf16[256,128]{1,0:T(8,128)(2,1)S(1)}, bf16[256,128]{1,0:T(8,128)(2,1)S(1)}, u32[]{:S(2)}, u32[]{:S(2)}) collective-permute-start(bf16[256,128]{1,0:T(8,128)(2,1)S(1)} %shard_map.77), channel_id=1, source_target_pairs={{0,1},{1,0},{2,3},{3,2},{4,5},{5,4},{6,7},{7,6},{8,9},{9,8},{10,11... | collective-permute-start | bytes 196616 | tf_op jit(solution)/shard_map/ppermute | solution.py:57
  66.1 3.4 %collective-permute-start.26 = (bf16[4,128,128]{2,1,0:T(8,128)(2,1)S(1)}, bf16[4,128,128]{2,1,0:T(8,128)(2,1)S(1)}, u32[]{:S(2)}, u32[]{:S(2)}) collective-permute-start(bf16[4,128,128]{2,1,0:T(8,128)(2,1)S(1)} %get-tuple-element.70), channel_id=1, source_target_pairs={{0,4},{1,5},{2,6},{3,7},{4,0},{5,1},{6,2},{7,3},{8,12},{9,13},{10,... | collective-permute-start | bytes 393224 | tf_op jit(solution)/shard_map/ppermute | solution.py:57
  (9 other events, 40.0 us)

commit v21 on v20

--- a/solution.py
+++ b/solution.py
@@ -323,7 +323,6 @@
     def array(*shape, kind=bf16):
         return jax.ShapeDtypeStruct(shape, kind)
 
-    far_raw = swap_z(w_qkv, 2)
 
     mask_row = jnp.pad(mask.reshape(1, mask.shape[2]), ((0, 0), (0, feat_len - mask.shape[2]))).astype(bf16)
     raw = jnp.concatenate([raw.reshape(block, feat_len), jnp.broadcast_to(mask_row, (EXTRA, feat_len))], axis=0)
@@ -335,6 +334,7 @@
         (array(size + more, PAIR), array(size + more, PAIR), array(block, PAIR), array(size, PAIR)),
         "vv",
     )(w_qkv, raw)
+    far_raw = swap_z(after(w_qkv, kept), 2)
     plane = [swap_depth(t, r) for t, r in zip(to, (1, 2, 3))]
     own = call(sort_kernel, array(size, 6 * HD), "vvv")(kept, *plane[:2])
     near = swap_z(own, 1)

time: 70.8 us -> 71.7 us (1.013)
  waiting for transfers between devices: 21.9 us -> 25.9 us
  starting transfers between devices: 34.8 us -> 31.6 us
  local copies, waits for them, and re-layouts: 3.18 us -> 2.18 us
  Pallas kernels: 8.81 us -> 9.8 us
    ppermute x27, waiting for transfers between devices: 21.9 us -> 25.9 us  [hop(): return lax.ppermute(value, ('tm', 'depth'), pairs)]
    ppermute x27, starting transfers between devices: 34.8 us -> 31.6 us  [hop(): return lax.ppermute(value, ('tm', 'depth'), pairs)]
    unnamed x13 -> x11, local copies, waits for them, and re-layouts: 3.13 us -> 2.14 us
    pallas_call x1, Pallas kernels: 0.05 us -> 1.04 us  [plane_device(): call(split_kernel, (array(size + more, PAIR), array(size + more, PAIR), a...]
  transfers between devices with their start and end apart: 27 -> 27, of which waited for: 15 -> 16; matrix products, arithmetic and copies ran while one was open for 2% -> 0% of each run, Pallas kernels for 11% -> 10%
where the time goes in v21:
time: 71.7 us; the launch traced here: 71.3 us
  starting transfers between devices  31.6 us (44%)
  waiting for transfers between devices  25.9 us (36%)
  Pallas kernels  9.8 us (14%)
  local copies, waits for them, and re-layouts  2.18 us (3%)
  other arithmetic  1.51 us (2%)
    ppermute x27, starting transfers between devices, hop(): return lax.ppermute(value, ('tm', 'depth'), pairs)  31.6 us
    ppermute x27, waiting for transfers between devices, hop(): return lax.ppermute(value, ('tm', 'depth'), pairs)  25.9 us
    pallas_call x3, Pallas kernels, embed(): call(functools.partial(embed_kernel, rs, len(finished)), out, 'v' * (6 +...  2.39 us
    unnamed x11, local copies, waits for them, and re-layouts  2.14 us
  transfers between devices with their start and end apart: 27, of which 16 were waited for; matrix products, arithmetic and copies ran while one was open for 0% of the time, Pallas kernels for 10%

profile of v21, /device:TPU:9, one launch (start us, length us, event | category | flops | bytes accessed | tf_op | source)
XLA Modules:
  0.0 71.3 jit_solution(1014460194843947916)
XLA Ops:
  2.5 2.4 %collective-permute-start = (bf16[256,768]{1,0:T(8,128)(2,1)}, bf16[256,768]{1,0:T(8,128)(2,1)S(1)}, u32[]{:S(2)}, u32[]{:S(2)}) collective-permute-start(bf16[256,768]{1,0:T(8,128)(2,1)} %w.1), channel_id=1, source_target_pairs={{0,16},{1,17},{2,18},{3,19},{4,20},{5,21},{6,22},{7,23},{8,24},{9,... | collective-permute-start | bytes 1179656 | tf_op jit(solution)/shard_map/ppermute | solution.py:57
  4.9 2.2 %collective-permute-start.3 = (bf16[128,256]{1,0:T(8,128)(2,1)S(1)}, bf16[128,256]{1,0:T(8,128)(2,1)S(1)}, u32[]{:S(2)}, u32[]{:S(2)}) collective-permute-start(bf16[128,256]{1,0:T(8,128)(2,1)S(1)} %get-tuple-element.43), channel_id=1, source_target_pairs={{0,3},{1,2},{2,1},{3,0},{4,7},{5,6},{6,5},{7,4},{8,11},{9,10},{10,... | collective-permute-start | bytes 196616 | tf_op jit(solution)/shard_map/ppermute | solution.py:57
  7.6 1.7 %collective-permute-done.3.across = bf16[128,256]{1,0:T(8,128)(2,1)S(1)} collective-permute-done((bf16[128,256]{1,0:T(8,128)(2,1)S(1)}, bf16[128,256]{1,0:T(8,128)(2,1)S(1)}, u32[]{:S(2)}, u32[]{:S(2)}) %collective-permute-start.3) | collective-permute-done | bytes 65568 | tf_op jit(solution)/shard_map/ppermute | solution.py:57
  9.2 1.2 %collective-permute-start.7 = (bf16[128,2048]{1,0:T(8,128)(2,1)}, bf16[128,2048]{1,0:T(8,128)(2,1)S(1)}, u32[]{:S(2)}, u32[]{:S(2)}) collective-permute-start(bf16[128,2048]{1,0:T(8,128)(2,1)} %bitcast.12), channel_id=1, source_target_pairs={{0,2},{1,3},{2,0},{3,1},{4,6},{5,7},{6,4},{7,5},{8,10},{9,11},{10,... | collective-permute-start | bytes 1572872 | tf_op jit(solution)/shard_map/ppermute | solution.py:57
  11.7 1.4 %collective-permute-done.1.plane_x.from_x = bf16[336,256]{1,0:T(8,128)(2,1)S(1)} collective-permute-done((bf16[336,256]{1,0:T(8,128)(2,1)S(1)}, bf16[336,256]{1,0:T(8,128)(2,1)S(1)}, u32[]{:S(2)}, u32[]{:S(2)}) %collective-permute-start.1) | collective-permute-done | bytes 172064 | tf_op jit(solution)/shard_map/ppermute | solution.py:57
  13.5 1.4 %copy-done = bf16[3,128,2048]{2,1,0:T(8,128)(2,1)S(1)} copy-done((bf16[3,128,2048]{2,1,0:T(8,128)(2,1)S(1)}, bf16[3,128,2048]{2,1,0:T(8,128)(2,1)}, u32[]{:S(2)}) %copy-start) | copy-done | bytes 1572888
  16.2 6.2 %collective-permute-done = bf16[256,768]{1,0:T(8,128)(2,1)S(1)} collective-permute-done((bf16[256,768]{1,0:T(8,128)(2,1)}, bf16[256,768]{1,0:T(8,128)(2,1)S(1)}, u32[]{:S(2)}, u32[]{:S(2)}) %collective-permute-start) | collective-permute-done | bytes 393248 | tf_op jit(solution)/shard_map/ppermute | solution.py:57
  22.5 1.3 %collective-permute-start.4 = (bf16[256,256]{1,0:T(8,128)(2,1)S(1)}, bf16[256,256]{1,0:T(8,128)(2,1)S(1)}, u32[]{:S(2)}, u32[]{:S(2)}) collective-permute-start(bf16[256,256]{1,0:T(8,128)(2,1)S(1)} %get-tuple-element.74), channel_id=1, source_target_pairs={{0,1},{1,0},{2,3},{3,2},{4,5},{5,4},{6,7},{7,6},{8,9},{9,8},{10,11... | collective-permute-start | bytes 393224 | tf_op jit(solution)/shard_map/ppermute | solution.py:57
  23.7 1.2 %collective-permute-start.5 = (bf16[256,256]{1,0:T(8,128)(2,1)S(1)}, bf16[256,256]{1,0:T(8,128)(2,1)S(1)}, u32[]{:S(2)}, u32[]{:S(2)}) collective-permute-start(bf16[256,256]{1,0:T(8,128)(2,1)S(1)} %get-tuple-element.73), channel_id=1, source_target_pairs={{0,2},{1,3},{2,0},{3,1},{4,6},{5,7},{6,4},{7,5},{8,10},{9,11},{10,... | collective-permute-start | bytes 393224 | tf_op jit(solution)/shard_map/ppermute | solution.py:57
  26.1 1.3 %collective-permute-done.4.from_x = bf16[256,256]{1,0:T(8,128)(2,1)S(1)} collective-permute-done((bf16[256,256]{1,0:T(8,128)(2,1)S(1)}, bf16[256,256]{1,0:T(8,128)(2,1)S(1)}, u32[]{:S(2)}, u32[]{:S(2)}) %collective-permute-start.4) | collective-permute-done | bytes 131104 | tf_op jit(solution)/shard_map/ppermute | solution.py:57
  28.0 1.5 %collective-permute-done.8.near.refs_3_.refs_1_ = bf16[256,768]{1,0:T(8,128)(2,1)S(1)} collective-permute-done((bf16[256,768]{1,0:T(8,128)(2,1)S(1)}, bf16[256,768]{1,0:T(8,128)(2,1)S(1)}, u32[]{:S(2)}, u32[]{:S(2)}) %collective-permute-start.8) | collective-permute-done | bytes 393248 | tf_op jit(solution)/shard_map/ppermute | solution.py:57
  33.7 2.2 %collective-permute-start.16 = (bf16[512,384]{1,0:T(8,128)(2,1)S(1)}, bf16[512,384]{1,0:T(8,128)(2,1)S(1)}, u32[]{:S(2)}, u32[]{:S(2)}) collective-permute-start(bf16[512,384]{1,0:T(8,128)(2,1)S(1)} %constant_dynamic-update-slice_fusion.refs_5_.refs_3_), channel_id=1, source_target_pairs={{0,8},{1,9},{2,10},{3,11},{4,12},{5,13},{6,14},{7,15},{8,0},{9,1},... | collective-permute-start | bytes 1179656 | tf_op jit(solution)/shard_map/ppermute | solution.py:57
  35.9 1.4 %shard_map.70.refs_4_ = f32[768,384]{1,0:T(8,128)S(1)} custom-call(bf16[384,2048]{1,0:T(8,128)(2,1)S(1)} %get-tuple-element.55.refs_0_, bf16[384,2048]{1,0:T(8,128)(2,1)S(1)} %collective-permute-done.10.refs_1_, bf16[256,768]{1,0:T(8,128)(2,1)S(1)} %shard_map.67.own.refs_2_.refs_0_, bf16[256,768]{1,0:T(8,128)(2,1)S(1)} %collective-permute-done.8.near.refs_3_.refs_1_, ...), custom_call_target="tpu_custom_call" | custom-call | flops 905969664 | tf_op jit(solution)/shard_map/pallas_call | solution.py:382
  37.3 2.2 %collective-permute-done.13.refs_1_ = bf16[128,1024]{1,0:T(8,128)(2,1)S(1)} collective-permute-done((bf16[128,1024]{1,0:T(8,128)(2,1)S(1)}, bf16[128,1024]{1,0:T(8,128)(2,1)S(1)}, u32[]{:S(2)}, u32[]{:S(2)}) %collective-permute-start.13) | collective-permute-done | bytes 262176 | tf_op jit(solution)/shard_map/ppermute | solution.py:57
  41.0 1.6 %collective-permute-start.14 = (bf16[80,2048]{1,0:T(8,128)(2,1)S(1)}, bf16[80,2048]{1,0:T(8,128)(2,1)S(1)}, u32[]{:S(2)}, u32[]{:S(2)}) collective-permute-start(bf16[80,2048]{1,0:T(8,128)(2,1)S(1)} %get-tuple-element.64), channel_id=1, source_target_pairs={{0,4},{1,5},{2,6},{3,7},{4,0},{5,1},{6,2},{7,3},{8,12},{9,13},{10,... | collective-permute-start | bytes 983048 | tf_op jit(solution)/shard_map/ppermute | solution.py:57
  42.7 1.5 %collective-permute-done.15.bottom = bf16[48,2048]{1,0:T(8,128)(2,1)S(1)} collective-permute-done((bf16[48,2048]{1,0:T(8,128)(2,1)S(1)}, bf16[48,2048]{1,0:T(8,128)(2,1)S(1)}, u32[]{:S(2)}, u32[]{:S(2)}) %collective-permute-start.15) | collective-permute-done | bytes 196640 | tf_op jit(solution)/shard_map/ppermute | solution.py:57
  45.3 2.3 %collective-permute-start.17 = (bf16[4,256,128]{2,1,0:T(8,128)(2,1)S(1)}, bf16[4,256,128]{2,1,0:T(8,128)(2,1)S(1)}, u32[]{:S(2)}, u32[]{:S(2)}) collective-permute-start(bf16[4,256,128]{2,1,0:T(8,128)(2,1)S(1)} %shard_map.74.own), channel_id=1, source_target_pairs={{0,8},{1,9},{2,10},{3,11},{4,12},{5,13},{6,14},{7,15},{8,0},{9,1},... | collective-permute-start | bytes 786440 | tf_op jit(solution)/shard_map/ppermute | solution.py:57
  47.5 3.1 %collective-permute-start.18 = (bf16[4,256,128]{2,1,0:T(8,128)(2,1)S(1)}, bf16[4,256,128]{2,1,0:T(8,128)(2,1)S(1)}, u32[]{:S(2)}, u32[]{:S(2)}) collective-permute-start(bf16[4,256,128]{2,1,0:T(8,128)(2,1)S(1)} %shard_map.74.own), channel_id=1, source_target_pairs={{8,16},{9,17},{10,18},{11,19},{12,20},{13,21},{14,22},{15,23},{16,... | collective-permute-start | bytes 786440 | tf_op jit(solution)/shard_map/ppermute | solution.py:57
  51.4 2.2 %collective-permute-start.22 = (bf16[2,256,128]{2,1,0:T(8,128)(2,1)S(1)}, bf16[2,256,128]{2,1,0:T(8,128)(2,1)S(1)}, u32[]{:S(2)}, u32[]{:S(2)}) collective-permute-start(bf16[2,256,128]{2,1,0:T(8,128)(2,1)S(1)} %get-tuple-element.70.own), channel_id=1, source_target_pairs={{8,16},{9,17},{10,18},{11,19},{12,20},{13,21},{14,22},{15,23},{16,... | collective-permute-start | bytes 393224 | tf_op jit(solution)/shard_map/ppermute | solution.py:57
  53.7 3.1 %collective-permute-start.20 = (bf16[2,256,128]{2,1,0:T(8,128)(2,1)S(1)}, bf16[2,256,128]{2,1,0:T(8,128)(2,1)S(1)}, u32[]{:S(2)}, u32[]{:S(2)}) collective-permute-start(bf16[2,256,128]{2,1,0:T(8,128)(2,1)S(1)} %get-tuple-element.69.own), channel_id=1, source_target_pairs={{8,16},{9,17},{10,18},{11,19},{12,20},{13,21},{14,22},{15,23},{16,... | collective-permute-start | bytes 393224 | tf_op jit(solution)/shard_map/ppermute | solution.py:57
  58.0 1.4 %collective-permute-done.22.middle = bf16[2,256,128]{2,1,0:T(8,128)(2,1)S(1)} collective-permute-done((bf16[2,256,128]{2,1,0:T(8,128)(2,1)S(1)}, bf16[2,256,128]{2,1,0:T(8,128)(2,1)S(1)}, u32[]{:S(2)}, u32[]{:S(2)}) %collective-permute-start.22) | collective-permute-done | bytes 131104 | tf_op jit(solution)/shard_map/ppermute | solution.py:57
  59.9 2.3 %collective-permute-done.20.middle = bf16[2,256,128]{2,1,0:T(8,128)(2,1)S(1)} collective-permute-done((bf16[2,256,128]{2,1,0:T(8,128)(2,1)S(1)}, bf16[2,256,128]{2,1,0:T(8,128)(2,1)S(1)}, u32[]{:S(2)}, u32[]{:S(2)}) %collective-permute-start.20) | collective-permute-done | bytes 131104 | tf_op jit(solution)/shard_map/ppermute | solution.py:57
  63.7 1.9 %collective-permute-done.24.refs_2_ = bf16[256,128]{1,0:T(8,128)(2,1)S(1)} collective-permute-done((bf16[256,128]{1,0:T(8,128)(2,1)S(1)}, bf16[256,128]{1,0:T(8,128)(2,1)S(1)}, u32[]{:S(2)}, u32[]{:S(2)}) %collective-permute-start.24) | collective-permute-done | bytes 65568 | tf_op jit(solution)/shard_map/ppermute | solution.py:57
  66.6 2.9 %collective-permute-start.26 = (bf16[4,128,128]{2,1,0:T(8,128)(2,1)S(1)}, bf16[4,128,128]{2,1,0:T(8,128)(2,1)S(1)}, u32[]{:S(2)}, u32[]{:S(2)}) collective-permute-start(bf16[4,128,128]{2,1,0:T(8,128)(2,1)S(1)} %get-tuple-element.72), channel_id=1, source_target_pairs={{0,4},{1,5},{2,6},{3,7},{4,0},{5,1},{6,2},{7,3},{8,12},{9,13},{10,... | collective-permute-start | bytes 393224 | tf_op jit(solution)/shard_map/ppermute | solution.py:57
  (65 shorter events, 21.2 us)
Async XLA Ops:
  2.5 19.9 %collective-permute-start = (bf16[256,768]{1,0:T(8,128)(2,1)}, bf16[256,768]{1,0:T(8,128)(2,1)S(1)}, u32[]{:S(2)}, u32[]{:S(2)}) collective-permute-start(bf16[256,768]{1,0:T(8,128)(2,1)} %w.1), channel_id=1, source_target_pairs={{0,16},{1,17},{2,18},{3,19},{4,20},{5,21},{6,22},{7,23},{8,24},{9,... | collective-permute-start | bytes 1179656 | tf_op jit(solution)/shard_map/ppermute | solution.py:57
  4.9 4.3 %collective-permute-start.3 = (bf16[128,256]{1,0:T(8,128)(2,1)S(1)}, bf16[128,256]{1,0:T(8,128)(2,1)S(1)}, u32[]{:S(2)}, u32[]{:S(2)}) collective-permute-start(bf16[128,256]{1,0:T(8,128)(2,1)S(1)} %get-tuple-element.43), channel_id=1, source_target_pairs={{0,3},{1,2},{2,1},{3,0},{4,7},{5,6},{6,5},{7,4},{8,11},{9,10},{10,... | collective-permute-start | bytes 196616 | tf_op jit(solution)/shard_map/ppermute | solution.py:57
  7.1 6.0 %collective-permute-start.1 = (bf16[336,256]{1,0:T(8,128)(2,1)S(1)}, bf16[336,256]{1,0:T(8,128)(2,1)S(1)}, u32[]{:S(2)}, u32[]{:S(2)}) collective-permute-start(bf16[336,256]{1,0:T(8,128)(2,1)S(1)} %get-tuple-element.41), channel_id=1, source_target_pairs={{0,1},{1,0},{2,3},{3,2},{4,5},{5,4},{6,7},{7,6},{8,9},{9,8},{10,11... | collective-permute-start | bytes 516104 | tf_op jit(solution)/shard_map/ppermute | solution.py:57
  7.3 5.8 %collective-permute-start.2 = (bf16[336,256]{1,0:T(8,128)(2,1)S(1)}, bf16[336,256]{1,0:T(8,128)(2,1)S(1)}, u32[]{:S(2)}, u32[]{:S(2)}) collective-permute-start(bf16[336,256]{1,0:T(8,128)(2,1)S(1)} %get-tuple-element.42), channel_id=1, source_target_pairs={{0,2},{1,3},{2,0},{3,1},{4,6},{5,7},{6,4},{7,5},{8,10},{9,11},{10,... | collective-permute-start | bytes 516104 | tf_op jit(solution)/shard_map/ppermute | solution.py:57
  9.2 15.8 %collective-permute-start.7 = (bf16[128,2048]{1,0:T(8,128)(2,1)}, bf16[128,2048]{1,0:T(8,128)(2,1)S(1)}, u32[]{:S(2)}, u32[]{:S(2)}) collective-permute-start(bf16[128,2048]{1,0:T(8,128)(2,1)} %bitcast.12), channel_id=1, source_target_pairs={{0,2},{1,3},{2,0},{3,1},{4,6},{5,7},{6,4},{7,5},{8,10},{9,11},{10,... | collective-permute-start | bytes 1572872 | tf_op jit(solution)/shard_map/ppermute | solution.py:57
  10.5 14.5 %collective-permute-start.6 = (bf16[128,2048]{1,0:T(8,128)(2,1)}, bf16[128,2048]{1,0:T(8,128)(2,1)S(1)}, u32[]{:S(2)}, u32[]{:S(2)}) collective-permute-start(bf16[128,2048]{1,0:T(8,128)(2,1)} %bitcast.13), channel_id=1, source_target_pairs={{0,1},{1,0},{2,3},{3,2},{4,5},{5,4},{6,7},{7,6},{8,9},{9,8},{10,11... | collective-permute-start | bytes 1572872 | tf_op jit(solution)/shard_map/ppermute | solution.py:57
  13.2 16.3 %collective-permute-start.8 = (bf16[256,768]{1,0:T(8,128)(2,1)S(1)}, bf16[256,768]{1,0:T(8,128)(2,1)S(1)}, u32[]{:S(2)}, u32[]{:S(2)}) collective-permute-start(bf16[256,768]{1,0:T(8,128)(2,1)S(1)} %shard_map.67.own.refs_2_.refs_0_), channel_id=1, source_target_pairs={{0,8},{1,9},{2,10},{3,11},{4,12},{5,13},{6,14},{7,15},{8,0},{9,1},... | collective-permute-start | bytes 1179656 | tf_op jit(solution)/shard_map/ppermute | solution.py:57
  22.5 5.0 %collective-permute-start.4 = (bf16[256,256]{1,0:T(8,128)(2,1)S(1)}, bf16[256,256]{1,0:T(8,128)(2,1)S(1)}, u32[]{:S(2)}, u32[]{:S(2)}) collective-permute-start(bf16[256,256]{1,0:T(8,128)(2,1)S(1)} %get-tuple-element.74), channel_id=1, source_target_pairs={{0,1},{1,0},{2,3},{3,2},{4,5},{5,4},{6,7},{7,6},{8,9},{9,8},{10,11... | collective-permute-start | bytes 393224 | tf_op jit(solution)/shard_map/ppermute | solution.py:57
  23.7 4.2 %collective-permute-start.5 = (bf16[256,256]{1,0:T(8,128)(2,1)S(1)}, bf16[256,256]{1,0:T(8,128)(2,1)S(1)}, u32[]{:S(2)}, u32[]{:S(2)}) collective-permute-start(bf16[256,256]{1,0:T(8,128)(2,1)S(1)} %get-tuple-element.73), channel_id=1, source_target_pairs={{0,2},{1,3},{2,0},{3,1},{4,6},{5,7},{6,4},{7,5},{8,10},{9,11},{10,... | collective-permute-start | bytes 393224 | tf_op jit(solution)/shard_map/ppermute | solution.py:57
  31.3 4.6 %collective-permute-start.10 = (bf16[384,2048]{1,0:T(8,128)(2,1)S(1)}, bf16[384,2048]{1,0:T(8,128)(2,1)S(1)}, u32[]{:S(2)}, u32[]{:S(2)}) collective-permute-start(bf16[384,2048]{1,0:T(8,128)(2,1)S(1)} %get-tuple-element.55.refs_0_), channel_id=1, source_target_pairs={{0,4},{1,5},{2,6},{3,7},{4,0},{5,1},{6,2},{7,3},{8,12},{9,13},{10,... | collective-permute-start | bytes 4718600 | tf_op jit(solution)/shard_map/ppermute | solution.py:57
  31.8 4.1 %collective-permute-start.12 = (bf16[528,384]{1,0:T(8,128)(2,1)S(1)}, bf16[528,384]{1,0:T(8,128)(2,1)S(1)}, u32[]{:S(2)}, u32[]{:S(2)}) collective-permute-start(bf16[528,384]{1,0:T(8,128)(2,1)S(1)} %shard_map.69), channel_id=1, source_target_pairs={{0,4},{1,5},{2,6},{3,7},{4,0},{5,1},{6,2},{7,3},{8,12},{9,13},{10,... | collective-permute-start | bytes 1216520 | tf_op jit(solution)/shard_map/ppermute | solution.py:57
  32.0 7.5 %collective-permute-start.13 = (bf16[128,1024]{1,0:T(8,128)(2,1)S(1)}, bf16[128,1024]{1,0:T(8,128)(2,1)S(1)}, u32[]{:S(2)}, u32[]{:S(2)}) collective-permute-start(bf16[128,1024]{1,0:T(8,128)(2,1)S(1)} %get-tuple-element.61), channel_id=1, source_target_pairs={{0,1},{1,0},{2,3},{3,2},{4,5},{5,4},{6,7},{7,6},{8,9},{9,8},{10,11... | collective-permute-start | bytes 786440 | tf_op jit(solution)/shard_map/ppermute | solution.py:57
  33.2 7.2 %collective-permute-start.11 = (bf16[128,1024]{1,0:T(8,128)(2,1)S(1)}, bf16[128,1024]{1,0:T(8,128)(2,1)S(1)}, u32[]{:S(2)}, u32[]{:S(2)}) collective-permute-start(bf16[128,1024]{1,0:T(8,128)(2,1)S(1)} %get-tuple-element.56), channel_id=1, source_target_pairs={{0,2},{1,3},{2,0},{3,1},{4,6},{5,7},{6,4},{7,5},{8,10},{9,11},{10,... | collective-permute-start | bytes 786440 | tf_op jit(solution)/shard_map/ppermute | solution.py:57
  33.7 11.1 %collective-permute-start.16 = (bf16[512,384]{1,0:T(8,128)(2,1)S(1)}, bf16[512,384]{1,0:T(8,128)(2,1)S(1)}, u32[]{:S(2)}, u32[]{:S(2)}) collective-permute-start(bf16[512,384]{1,0:T(8,128)(2,1)S(1)} %constant_dynamic-update-slice_fusion.refs_5_.refs_3_), channel_id=1, source_target_pairs={{0,8},{1,9},{2,10},{3,11},{4,12},{5,13},{6,14},{7,15},{8,0},{9,1},... | collective-permute-start | bytes 1179656 | tf_op jit(solution)/shard_map/ppermute | solution.py:57
  45.3 8.4 %collective-permute-start.17 = (bf16[4,256,128]{2,1,0:T(8,128)(2,1)S(1)}, bf16[4,256,128]{2,1,0:T(8,128)(2,1)S(1)}, u32[]{:S(2)}, u32[]{:S(2)}) collective-permute-start(bf16[4,256,128]{2,1,0:T(8,128)(2,1)S(1)} %shard_map.74.own), channel_id=1, source_target_pairs={{0,8},{1,9},{2,10},{3,11},{4,12},{5,13},{6,14},{7,15},{8,0},{9,1},... | collective-permute-start | bytes 786440 | tf_op jit(solution)/shard_map/ppermute | solution.py:57
  47.5 9.3 %collective-permute-start.18 = (bf16[4,256,128]{2,1,0:T(8,128)(2,1)S(1)}, bf16[4,256,128]{2,1,0:T(8,128)(2,1)S(1)}, u32[]{:S(2)}, u32[]{:S(2)}) collective-permute-start(bf16[4,256,128]{2,1,0:T(8,128)(2,1)S(1)} %shard_map.74.own), channel_id=1, source_target_pairs={{8,16},{9,17},{10,18},{11,19},{12,20},{13,21},{14,22},{15,23},{16,... | collective-permute-start | bytes 786440 | tf_op jit(solution)/shard_map/ppermute | solution.py:57
  51.4 6.7 %collective-permute-start.21 = (bf16[2,256,128]{2,1,0:T(8,128)(2,1)S(1)}, bf16[2,256,128]{2,1,0:T(8,128)(2,1)S(1)}, u32[]{:S(2)}, u32[]{:S(2)}) collective-permute-start(bf16[2,256,128]{2,1,0:T(8,128)(2,1)S(1)} %get-tuple-element.70.own), channel_id=1, source_target_pairs={{0,8},{1,9},{2,10},{3,11},{4,12},{5,13},{6,14},{7,15},{8,0},{9,1},... | collective-permute-start | bytes 393224 | tf_op jit(solution)/shard_map/ppermute | solution.py:57
  51.4 7.9 %collective-permute-start.22 = (bf16[2,256,128]{2,1,0:T(8,128)(2,1)S(1)}, bf16[2,256,128]{2,1,0:T(8,128)(2,1)S(1)}, u32[]{:S(2)}, u32[]{:S(2)}) collective-permute-start(bf16[2,256,128]{2,1,0:T(8,128)(2,1)S(1)} %get-tuple-element.70.own), channel_id=1, source_target_pairs={{8,16},{9,17},{10,18},{11,19},{12,20},{13,21},{14,22},{15,23},{16,... | collective-permute-start | bytes 393224 | tf_op jit(solution)/shard_map/ppermute | solution.py:57
  53.6 6.3 %collective-permute-start.19 = (bf16[2,256,128]{2,1,0:T(8,128)(2,1)S(1)}, bf16[2,256,128]{2,1,0:T(8,128)(2,1)S(1)}, u32[]{:S(2)}, u32[]{:S(2)}) collective-permute-start(bf16[2,256,128]{2,1,0:T(8,128)(2,1)S(1)} %get-tuple-element.69.own), channel_id=1, source_target_pairs={{0,8},{1,9},{2,10},{3,11},{4,12},{5,13},{6,14},{7,15},{8,0},{9,1},... | collective-permute-start | bytes 393224 | tf_op jit(solution)/shard_map/ppermute | solution.py:57
  53.7 8.5 %collective-permute-start.20 = (bf16[2,256,128]{2,1,0:T(8,128)(2,1)S(1)}, bf16[2,256,128]{2,1,0:T(8,128)(2,1)S(1)}, u32[]{:S(2)}, u32[]{:S(2)}) collective-permute-start(bf16[2,256,128]{2,1,0:T(8,128)(2,1)S(1)} %get-tuple-element.69.own), channel_id=1, source_target_pairs={{8,16},{9,17},{10,18},{11,19},{12,20},{13,21},{14,22},{15,23},{16,... | collective-permute-start | bytes 393224 | tf_op jit(solution)/shard_map/ppermute | solution.py:57
  59.6 4.1 %collective-permute-start.25 = (bf16[256,128]{1,0:T(8,128)(2,1)S(1)}, bf16[256,128]{1,0:T(8,128)(2,1)S(1)}, u32[]{:S(2)}, u32[]{:S(2)}) collective-permute-start(bf16[256,128]{1,0:T(8,128)(2,1)S(1)} %shard_map.79), channel_id=1, source_target_pairs={{0,3},{1,2},{2,1},{3,0},{4,7},{5,6},{6,5},{7,4},{8,11},{9,10},{10,... | collective-permute-start | bytes 196616 | tf_op jit(solution)/shard_map/ppermute | solution.py:57
  62.4 3.2 %collective-permute-start.24 = (bf16[256,128]{1,0:T(8,128)(2,1)S(1)}, bf16[256,128]{1,0:T(8,128)(2,1)S(1)}, u32[]{:S(2)}, u32[]{:S(2)}) collective-permute-start(bf16[256,128]{1,0:T(8,128)(2,1)S(1)} %shard_map.78), channel_id=1, source_target_pairs={{0,2},{1,3},{2,0},{3,1},{4,6},{5,7},{6,4},{7,5},{8,10},{9,11},{10,... | collective-permute-start | bytes 196616 | tf_op jit(solution)/shard_map/ppermute | solution.py:57
  62.8 3.8 %collective-permute-start.23 = (bf16[256,128]{1,0:T(8,128)(2,1)S(1)}, bf16[256,128]{1,0:T(8,128)(2,1)S(1)}, u32[]{:S(2)}, u32[]{:S(2)}) collective-permute-start(bf16[256,128]{1,0:T(8,128)(2,1)S(1)} %shard_map.77), channel_id=1, source_target_pairs={{0,1},{1,0},{2,3},{3,2},{4,5},{5,4},{6,7},{7,6},{8,9},{9,8},{10,11... | collective-permute-start | bytes 196616 | tf_op jit(solution)/shard_map/ppermute | solution.py:57
  66.6 3.9 %collective-permute-start.26 = (bf16[4,128,128]{2,1,0:T(8,128)(2,1)S(1)}, bf16[4,128,128]{2,1,0:T(8,128)(2,1)S(1)}, u32[]{:S(2)}, u32[]{:S(2)}) collective-permute-start(bf16[4,128,128]{2,1,0:T(8,128)(2,1)S(1)} %get-tuple-element.72), channel_id=1, source_target_pairs={{0,4},{1,5},{2,6},{3,7},{4,0},{5,1},{6,2},{7,3},{8,12},{9,13},{10,... | collective-permute-start | bytes 393224 | tf_op jit(solution)/shard_map/ppermute | solution.py:57
  (8 other events, 38.5 us)

commit v22 on v20

--- a/solution.py
+++ b/solution.py
@@ -274,7 +274,7 @@
                 out_ref[r, u * block : (u + 1) * block, here] = (p * inverse).astype(jnp.bfloat16)
 
 
-def mix_kernel(r, weights, outer, own, middle, out_ref):
+def mix_kernel(r, weights, middle, own, outer, out_ref):
     block = weights.shape[1] // 2
     values = neighbours(outer, own, middle, V_ORDER.index(r) % 2)
     for u in range(2):
@@ -399,7 +399,7 @@
     weights = call(weigh_kernel, array(4, 2 * block, 5 * block), "v" * 6, macs=8 * block * 5 * block * HD)(
         q, swap_z(k, 1), k, swap_middle(k), flags, received
     )
-    values = [(swap_z(t, 1), t, swap_middle(t)) for t in v]
+    values = [(swap_middle(t), t, swap_z(t, 1)) for t in v]
     pieces = {}
     for i, r in enumerate(V_ORDER):
         mixed = call(functools.partial(mix_kernel, r), array(2 * block, HD), "vvvv", macs=2 * block * 5 * block * HD)(

time: 70.8 us -> 71.1 us (level)
  no operation moved by 1% of the time
where the time goes in v22:
time: 71.1 us; the launch traced here: 70.3 us
  starting transfers between devices  34.9 us (49%)
  waiting for transfers between devices  21.7 us (31%)
  Pallas kernels  8.81 us (12%)
  local copies, waits for them, and re-layouts  3.18 us (4%)
  other arithmetic  1.45 us (2%)
    ppermute x27, starting transfers between devices, hop(): return lax.ppermute(value, ('tm', 'depth'), pairs)  34.9 us
    ppermute x27, waiting for transfers between devices, hop(): return lax.ppermute(value, ('tm', 'depth'), pairs)  21.7 us
    unnamed x13, local copies, waits for them, and re-layouts  3.13 us
    pallas_call x3, Pallas kernels, embed(): call(functools.partial(embed_kernel, rs, len(finished)), out, 'v' * (6 +...  2.39 us
  transfers between devices with their start and end apart: 27, of which 15 were waited for; matrix products, arithmetic and copies ran while one was open for 2% of the time, Pallas kernels for 11%

profile of v22, /device:TPU:9, one launch (start us, length us, event | category | flops | bytes accessed | tf_op | source)
XLA Modules:
  0.0 70.3 jit_solution(13787717292708445421)
XLA Ops:
  0.0 2.3 %collective-permute-start = (bf16[256,768]{1,0:T(8,128)(2,1)}, bf16[256,768]{1,0:T(8,128)(2,1)S(1)}, u32[]{:S(2)}, u32[]{:S(2)}) collective-permute-start(bf16[256,768]{1,0:T(8,128)(2,1)} %w.1), channel_id=1, source_target_pairs={{0,16},{1,17},{2,18},{3,19},{4,20},{5,21},{6,22},{7,23},{8,24},{9,... | collective-permute-start | bytes 1179656 | tf_op jit(solution)/shard_map/ppermute | solution.py:57
  4.8 2.2 %collective-permute-start.3 = (bf16[128,256]{1,0:T(8,128)(2,1)S(1)}, bf16[128,256]{1,0:T(8,128)(2,1)S(1)}, u32[]{:S(2)}, u32[]{:S(2)}) collective-permute-start(bf16[128,256]{1,0:T(8,128)(2,1)S(1)} %get-tuple-element.40), channel_id=1, source_target_pairs={{0,3},{1,2},{2,1},{3,0},{4,7},{5,6},{6,5},{7,4},{8,11},{9,10},{10,... | collective-permute-start | bytes 196616 | tf_op jit(solution)/shard_map/ppermute | solution.py:57
  7.5 1.7 %collective-permute-done.3.across = bf16[128,256]{1,0:T(8,128)(2,1)S(1)} collective-permute-done((bf16[128,256]{1,0:T(8,128)(2,1)S(1)}, bf16[128,256]{1,0:T(8,128)(2,1)S(1)}, u32[]{:S(2)}, u32[]{:S(2)}) %collective-permute-start.3) | collective-permute-done | bytes 65568 | tf_op jit(solution)/shard_map/ppermute | solution.py:57
  9.2 1.2 %collective-permute-start.7 = (bf16[128,2048]{1,0:T(8,128)(2,1)}, bf16[128,2048]{1,0:T(8,128)(2,1)S(1)}, u32[]{:S(2)}, u32[]{:S(2)}) collective-permute-start(bf16[128,2048]{1,0:T(8,128)(2,1)} %bitcast.12), channel_id=1, source_target_pairs={{0,2},{1,3},{2,0},{3,1},{4,6},{5,7},{6,4},{7,5},{8,10},{9,11},{10,... | collective-permute-start | bytes 1572872 | tf_op jit(solution)/shard_map/ppermute | solution.py:57
  11.6 1.4 %collective-permute-done.1.plane_x.from_x = bf16[336,256]{1,0:T(8,128)(2,1)S(1)} collective-permute-done((bf16[336,256]{1,0:T(8,128)(2,1)S(1)}, bf16[336,256]{1,0:T(8,128)(2,1)S(1)}, u32[]{:S(2)}, u32[]{:S(2)}) %collective-permute-start.1) | collective-permute-done | bytes 172064 | tf_op jit(solution)/shard_map/ppermute | solution.py:57
  13.4 1.4 %copy-done = bf16[3,128,2048]{2,1,0:T(8,128)(2,1)S(1)} copy-done((bf16[3,128,2048]{2,1,0:T(8,128)(2,1)S(1)}, bf16[3,128,2048]{2,1,0:T(8,128)(2,1)}, u32[]{:S(2)}) %copy-start) | copy-done | bytes 1572888
  16.1 3.7 %collective-permute-done = bf16[256,768]{1,0:T(8,128)(2,1)S(1)} collective-permute-done((bf16[256,768]{1,0:T(8,128)(2,1)}, bf16[256,768]{1,0:T(8,128)(2,1)S(1)}, u32[]{:S(2)}, u32[]{:S(2)}) %collective-permute-start) | collective-permute-done | bytes 393248 | tf_op jit(solution)/shard_map/ppermute | solution.py:57
  19.9 1.3 %collective-permute-start.4 = (bf16[256,256]{1,0:T(8,128)(2,1)S(1)}, bf16[256,256]{1,0:T(8,128)(2,1)S(1)}, u32[]{:S(2)}, u32[]{:S(2)}) collective-permute-start(bf16[256,256]{1,0:T(8,128)(2,1)S(1)} %get-tuple-element.72), channel_id=1, source_target_pairs={{0,1},{1,0},{2,3},{3,2},{4,5},{5,4},{6,7},{7,6},{8,9},{9,8},{10,11... | collective-permute-start | bytes 393224 | tf_op jit(solution)/shard_map/ppermute | solution.py:57
  21.1 1.2 %collective-permute-start.5 = (bf16[256,256]{1,0:T(8,128)(2,1)S(1)}, bf16[256,256]{1,0:T(8,128)(2,1)S(1)}, u32[]{:S(2)}, u32[]{:S(2)}) collective-permute-start(bf16[256,256]{1,0:T(8,128)(2,1)S(1)} %get-tuple-element.71), channel_id=1, source_target_pairs={{0,2},{1,3},{2,0},{3,1},{4,6},{5,7},{6,4},{7,5},{8,10},{9,11},{10,... | collective-permute-start | bytes 393224 | tf_op jit(solution)/shard_map/ppermute | solution.py:57
  22.4 1.8 %collective-permute-done.7.refs_1_ = bf16[128,2048]{1,0:T(8,128)(2,1)S(1)} collective-permute-done((bf16[128,2048]{1,0:T(8,128)(2,1)}, bf16[128,2048]{1,0:T(8,128)(2,1)S(1)}, u32[]{:S(2)}, u32[]{:S(2)}) %collective-permute-start.7) | collective-permute-done | bytes 524320 | tf_op jit(solution)/shard_map/ppermute | solution.py:57
  25.6 1.3 %collective-permute-done.5.from_y = bf16[256,256]{1,0:T(8,128)(2,1)S(1)} collective-permute-done((bf16[256,256]{1,0:T(8,128)(2,1)S(1)}, bf16[256,256]{1,0:T(8,128)(2,1)S(1)}, u32[]{:S(2)}, u32[]{:S(2)}) %collective-permute-start.5) | collective-permute-done | bytes 131104 | tf_op jit(solution)/shard_map/ppermute | solution.py:57
  27.1 1.9 %collective-permute-start.9 = (bf16[256,384]{1,0:T(8,128)(2,1)S(1)}, bf16[256,384]{1,0:T(8,128)(2,1)S(1)}, u32[]{:S(2)}, u32[]{:S(2)}) collective-permute-start(bf16[256,384]{1,0:T(8,128)(2,1)S(1)} %get-tuple-element.50), channel_id=1, source_target_pairs={{0,4},{1,5},{2,6},{3,7},{4,0},{5,1},{6,2},{7,3},{8,12},{9,13},{10,... | collective-permute-start | bytes 589832 | tf_op jit(solution)/shard_map/ppermute | solution.py:57
  32.4 1.7 %collective-permute-start.16 = (bf16[512,384]{1,0:T(8,128)(2,1)S(1)}, bf16[512,384]{1,0:T(8,128)(2,1)S(1)}, u32[]{:S(2)}, u32[]{:S(2)}) collective-permute-start(bf16[512,384]{1,0:T(8,128)(2,1)S(1)} %constant_dynamic-update-slice_fusion.refs_5_.refs_3_), channel_id=1, source_target_pairs={{0,8},{1,9},{2,10},{3,11},{4,12},{5,13},{6,14},{7,15},{8,0},{9,1},... | collective-permute-start | bytes 1179656 | tf_op jit(solution)/shard_map/ppermute | solution.py:57
  34.1 1.4 %shard_map.70.refs_4_ = f32[768,384]{1,0:T(8,128)S(1)} custom-call(bf16[384,2048]{1,0:T(8,128)(2,1)S(1)} %get-tuple-element.53.refs_0_, bf16[384,2048]{1,0:T(8,128)(2,1)S(1)} %collective-permute-done.10.refs_1_, bf16[256,768]{1,0:T(8,128)(2,1)S(1)} %shard_map.67.own.refs_2_.refs_0_, bf16[256,768]{1,0:T(8,128)(2,1)S(1)} %collective-permute-done.8.near.refs_3_.refs_1_, ...), custom_call_target="tpu_custom_call" | custom-call | flops 905969664 | tf_op jit(solution)/shard_map/pallas_call | solution.py:382
  35.5 2.8 %collective-permute-done.13.refs_1_ = bf16[128,1024]{1,0:T(8,128)(2,1)S(1)} collective-permute-done((bf16[128,1024]{1,0:T(8,128)(2,1)S(1)}, bf16[128,1024]{1,0:T(8,128)(2,1)S(1)}, u32[]{:S(2)}, u32[]{:S(2)}) %collective-permute-start.13) | collective-permute-done | bytes 262176 | tf_op jit(solution)/shard_map/ppermute | solution.py:57
  39.8 1.6 %collective-permute-start.14 = (bf16[80,2048]{1,0:T(8,128)(2,1)S(1)}, bf16[80,2048]{1,0:T(8,128)(2,1)S(1)}, u32[]{:S(2)}, u32[]{:S(2)}) collective-permute-start(bf16[80,2048]{1,0:T(8,128)(2,1)S(1)} %get-tuple-element.62), channel_id=1, source_target_pairs={{0,4},{1,5},{2,6},{3,7},{4,0},{5,1},{6,2},{7,3},{8,12},{9,13},{10,... | collective-permute-start | bytes 983048 | tf_op jit(solution)/shard_map/ppermute | solution.py:57
  41.5 1.5 %collective-permute-done.15.bottom = bf16[48,2048]{1,0:T(8,128)(2,1)S(1)} collective-permute-done((bf16[48,2048]{1,0:T(8,128)(2,1)S(1)}, bf16[48,2048]{1,0:T(8,128)(2,1)S(1)}, u32[]{:S(2)}, u32[]{:S(2)}) %collective-permute-start.15) | collective-permute-done | bytes 196640 | tf_op jit(solution)/shard_map/ppermute | solution.py:57
  45.0 4.2 %collective-permute-start.18 = (bf16[4,256,128]{2,1,0:T(8,128)(2,1)S(1)}, bf16[4,256,128]{2,1,0:T(8,128)(2,1)S(1)}, u32[]{:S(2)}, u32[]{:S(2)}) collective-permute-start(bf16[4,256,128]{2,1,0:T(8,128)(2,1)S(1)} %shard_map.74.own), channel_id=1, source_target_pairs={{8,16},{9,17},{10,18},{11,19},{12,20},{13,21},{14,22},{15,23},{16,... | collective-permute-start | bytes 786440 | tf_op jit(solution)/shard_map/ppermute | solution.py:57
  49.9 1.9 %collective-permute-start.21 = (bf16[2,256,128]{2,1,0:T(8,128)(2,1)S(1)}, bf16[2,256,128]{2,1,0:T(8,128)(2,1)S(1)}, u32[]{:S(2)}, u32[]{:S(2)}) collective-permute-start(bf16[2,256,128]{2,1,0:T(8,128)(2,1)S(1)} %get-tuple-element.68.own), channel_id=1, source_target_pairs={{8,16},{9,17},{10,18},{11,19},{12,20},{13,21},{14,22},{15,23},{16,... | collective-permute-start | bytes 393224 | tf_op jit(solution)/shard_map/ppermute | solution.py:57
  51.9 3.4 %collective-permute-start.19 = (bf16[2,256,128]{2,1,0:T(8,128)(2,1)S(1)}, bf16[2,256,128]{2,1,0:T(8,128)(2,1)S(1)}, u32[]{:S(2)}, u32[]{:S(2)}) collective-permute-start(bf16[2,256,128]{2,1,0:T(8,128)(2,1)S(1)} %get-tuple-element.67.own), channel_id=1, source_target_pairs={{8,16},{9,17},{10,18},{11,19},{12,20},{13,21},{14,22},{15,23},{16,... | collective-permute-start | bytes 393224 | tf_op jit(solution)/shard_map/ppermute | solution.py:57
  57.6 1.9 %collective-permute-start.25 = (bf16[256,128]{1,0:T(8,128)(2,1)S(1)}, bf16[256,128]{1,0:T(8,128)(2,1)S(1)}, u32[]{:S(2)}, u32[]{:S(2)}) collective-permute-start(bf16[256,128]{1,0:T(8,128)(2,1)S(1)} %shard_map.79), channel_id=1, source_target_pairs={{0,3},{1,2},{2,1},{3,0},{4,7},{5,6},{6,5},{7,4},{8,11},{9,10},{10,... | collective-permute-start | bytes 196616 | tf_op jit(solution)/shard_map/ppermute | solution.py:57
  60.4 2.0 %collective-permute-start.24 = (bf16[256,128]{1,0:T(8,128)(2,1)S(1)}, bf16[256,128]{1,0:T(8,128)(2,1)S(1)}, u32[]{:S(2)}, u32[]{:S(2)}) collective-permute-start(bf16[256,128]{1,0:T(8,128)(2,1)S(1)} %shard_map.78), channel_id=1, source_target_pairs={{0,2},{1,3},{2,0},{3,1},{4,6},{5,7},{6,4},{7,5},{8,10},{9,11},{10,... | collective-permute-start | bytes 196616 | tf_op jit(solution)/shard_map/ppermute | solution.py:57
  64.0 2.1 %collective-permute-done.23.refs_1_ = bf16[256,128]{1,0:T(8,128)(2,1)S(1)} collective-permute-done((bf16[256,128]{1,0:T(8,128)(2,1)S(1)}, bf16[256,128]{1,0:T(8,128)(2,1)S(1)}, u32[]{:S(2)}, u32[]{:S(2)}) %collective-permute-start.23) | collective-permute-done | bytes 65568 | tf_op jit(solution)/shard_map/ppermute | solution.py:57
  66.1 2.4 %collective-permute-start.26 = (bf16[4,128,128]{2,1,0:T(8,128)(2,1)S(1)}, bf16[4,128,128]{2,1,0:T(8,128)(2,1)S(1)}, u32[]{:S(2)}, u32[]{:S(2)}) collective-permute-start(bf16[4,128,128]{2,1,0:T(8,128)(2,1)S(1)} %get-tuple-element.70), channel_id=1, source_target_pairs={{0,4},{1,5},{2,6},{3,7},{4,0},{5,1},{6,2},{7,3},{8,12},{9,13},{10,... | collective-permute-start | bytes 393224 | tf_op jit(solution)/shard_map/ppermute | solution.py:57
  (67 shorter events, 21.9 us)
Async XLA Ops:
  0.0 19.8 %collective-permute-start = (bf16[256,768]{1,0:T(8,128)(2,1)}, bf16[256,768]{1,0:T(8,128)(2,1)S(1)}, u32[]{:S(2)}, u32[]{:S(2)}) collective-permute-start(bf16[256,768]{1,0:T(8,128)(2,1)} %w.1), channel_id=1, source_target_pairs={{0,16},{1,17},{2,18},{3,19},{4,20},{5,21},{6,22},{7,23},{8,24},{9,... | collective-permute-start | bytes 1179656 | tf_op jit(solution)/shard_map/ppermute | solution.py:57
  4.8 4.4 %collective-permute-start.3 = (bf16[128,256]{1,0:T(8,128)(2,1)S(1)}, bf16[128,256]{1,0:T(8,128)(2,1)S(1)}, u32[]{:S(2)}, u32[]{:S(2)}) collective-permute-start(bf16[128,256]{1,0:T(8,128)(2,1)S(1)} %get-tuple-element.40), channel_id=1, source_target_pairs={{0,3},{1,2},{2,1},{3,0},{4,7},{5,6},{6,5},{7,4},{8,11},{9,10},{10,... | collective-permute-start | bytes 196616 | tf_op jit(solution)/shard_map/ppermute | solution.py:57
  7.0 6.0 %collective-permute-start.1 = (bf16[336,256]{1,0:T(8,128)(2,1)S(1)}, bf16[336,256]{1,0:T(8,128)(2,1)S(1)}, u32[]{:S(2)}, u32[]{:S(2)}) collective-permute-start(bf16[336,256]{1,0:T(8,128)(2,1)S(1)} %get-tuple-element.38), channel_id=1, source_target_pairs={{0,1},{1,0},{2,3},{3,2},{4,5},{5,4},{6,7},{7,6},{8,9},{9,8},{10,11... | collective-permute-start | bytes 516104 | tf_op jit(solution)/shard_map/ppermute | solution.py:57
  7.3 5.8 %collective-permute-start.2 = (bf16[336,256]{1,0:T(8,128)(2,1)S(1)}, bf16[336,256]{1,0:T(8,128)(2,1)S(1)}, u32[]{:S(2)}, u32[]{:S(2)}) collective-permute-start(bf16[336,256]{1,0:T(8,128)(2,1)S(1)} %get-tuple-element.39), channel_id=1, source_target_pairs={{0,2},{1,3},{2,0},{3,1},{4,6},{5,7},{6,4},{7,5},{8,10},{9,11},{10,... | collective-permute-start | bytes 516104 | tf_op jit(solution)/shard_map/ppermute | solution.py:57
  9.2 15.0 %collective-permute-start.7 = (bf16[128,2048]{1,0:T(8,128)(2,1)}, bf16[128,2048]{1,0:T(8,128)(2,1)S(1)}, u32[]{:S(2)}, u32[]{:S(2)}) collective-permute-start(bf16[128,2048]{1,0:T(8,128)(2,1)} %bitcast.12), channel_id=1, source_target_pairs={{0,2},{1,3},{2,0},{3,1},{4,6},{5,7},{6,4},{7,5},{8,10},{9,11},{10,... | collective-permute-start | bytes 1572872 | tf_op jit(solution)/shard_map/ppermute | solution.py:57
  10.4 13.8 %collective-permute-start.6 = (bf16[128,2048]{1,0:T(8,128)(2,1)}, bf16[128,2048]{1,0:T(8,128)(2,1)S(1)}, u32[]{:S(2)}, u32[]{:S(2)}) collective-permute-start(bf16[128,2048]{1,0:T(8,128)(2,1)} %bitcast.13), channel_id=1, source_target_pairs={{0,1},{1,0},{2,3},{3,2},{4,5},{5,4},{6,7},{7,6},{8,9},{9,8},{10,11... | collective-permute-start | bytes 1572872 | tf_op jit(solution)/shard_map/ppermute | solution.py:57
  13.2 13.8 %collective-permute-start.8 = (bf16[256,768]{1,0:T(8,128)(2,1)S(1)}, bf16[256,768]{1,0:T(8,128)(2,1)S(1)}, u32[]{:S(2)}, u32[]{:S(2)}) collective-permute-start(bf16[256,768]{1,0:T(8,128)(2,1)S(1)} %shard_map.67.own.refs_2_.refs_0_), channel_id=1, source_target_pairs={{0,8},{1,9},{2,10},{3,11},{4,12},{5,13},{6,14},{7,15},{8,0},{9,1},... | collective-permute-start | bytes 1179656 | tf_op jit(solution)/shard_map/ppermute | solution.py:57
  19.9 5.8 %collective-permute-start.4 = (bf16[256,256]{1,0:T(8,128)(2,1)S(1)}, bf16[256,256]{1,0:T(8,128)(2,1)S(1)}, u32[]{:S(2)}, u32[]{:S(2)}) collective-permute-start(bf16[256,256]{1,0:T(8,128)(2,1)S(1)} %get-tuple-element.72), channel_id=1, source_target_pairs={{0,1},{1,0},{2,3},{3,2},{4,5},{5,4},{6,7},{7,6},{8,9},{9,8},{10,11... | collective-permute-start | bytes 393224 | tf_op jit(solution)/shard_map/ppermute | solution.py:57
  21.1 5.8 %collective-permute-start.5 = (bf16[256,256]{1,0:T(8,128)(2,1)S(1)}, bf16[256,256]{1,0:T(8,128)(2,1)S(1)}, u32[]{:S(2)}, u32[]{:S(2)}) collective-permute-start(bf16[256,256]{1,0:T(8,128)(2,1)S(1)} %get-tuple-element.71), channel_id=1, source_target_pairs={{0,2},{1,3},{2,0},{3,1},{4,6},{5,7},{6,4},{7,5},{8,10},{9,11},{10,... | collective-permute-start | bytes 393224 | tf_op jit(solution)/shard_map/ppermute | solution.py:57
  30.1 4.1 %collective-permute-start.10 = (bf16[384,2048]{1,0:T(8,128)(2,1)S(1)}, bf16[384,2048]{1,0:T(8,128)(2,1)S(1)}, u32[]{:S(2)}, u32[]{:S(2)}) collective-permute-start(bf16[384,2048]{1,0:T(8,128)(2,1)S(1)} %get-tuple-element.53.refs_0_), channel_id=1, source_target_pairs={{0,4},{1,5},{2,6},{3,7},{4,0},{5,1},{6,2},{7,3},{8,12},{9,13},{10,... | collective-permute-start | bytes 4718600 | tf_op jit(solution)/shard_map/ppermute | solution.py:57
  30.5 3.6 %collective-permute-start.12 = (bf16[528,384]{1,0:T(8,128)(2,1)S(1)}, bf16[528,384]{1,0:T(8,128)(2,1)S(1)}, u32[]{:S(2)}, u32[]{:S(2)}) collective-permute-start(bf16[528,384]{1,0:T(8,128)(2,1)S(1)} %shard_map.69), channel_id=1, source_target_pairs={{0,4},{1,5},{2,6},{3,7},{4,0},{5,1},{6,2},{7,3},{8,12},{9,13},{10,... | collective-permute-start | bytes 1216520 | tf_op jit(solution)/shard_map/ppermute | solution.py:57
  30.7 7.5 %collective-permute-start.13 = (bf16[128,1024]{1,0:T(8,128)(2,1)S(1)}, bf16[128,1024]{1,0:T(8,128)(2,1)S(1)}, u32[]{:S(2)}, u32[]{:S(2)}) collective-permute-start(bf16[128,1024]{1,0:T(8,128)(2,1)S(1)} %get-tuple-element.59), channel_id=1, source_target_pairs={{0,1},{1,0},{2,3},{3,2},{4,5},{5,4},{6,7},{7,6},{8,9},{9,8},{10,11... | collective-permute-start | bytes 786440 | tf_op jit(solution)/shard_map/ppermute | solution.py:57
  32.0 7.2 %collective-permute-start.11 = (bf16[128,1024]{1,0:T(8,128)(2,1)S(1)}, bf16[128,1024]{1,0:T(8,128)(2,1)S(1)}, u32[]{:S(2)}, u32[]{:S(2)}) collective-permute-start(bf16[128,1024]{1,0:T(8,128)(2,1)S(1)} %get-tuple-element.54), channel_id=1, source_target_pairs={{0,2},{1,3},{2,0},{3,1},{4,6},{5,7},{6,4},{7,5},{8,10},{9,11},{10,... | collective-permute-start | bytes 786440 | tf_op jit(solution)/shard_map/ppermute | solution.py:57
  32.4 11.2 %collective-permute-start.16 = (bf16[512,384]{1,0:T(8,128)(2,1)S(1)}, bf16[512,384]{1,0:T(8,128)(2,1)S(1)}, u32[]{:S(2)}, u32[]{:S(2)}) collective-permute-start(bf16[512,384]{1,0:T(8,128)(2,1)S(1)} %constant_dynamic-update-slice_fusion.refs_5_.refs_3_), channel_id=1, source_target_pairs={{0,8},{1,9},{2,10},{3,11},{4,12},{5,13},{6,14},{7,15},{8,0},{9,1},... | collective-permute-start | bytes 1179656 | tf_op jit(solution)/shard_map/ppermute | solution.py:57
  44.0 11.2 %collective-permute-start.17 = (bf16[4,256,128]{2,1,0:T(8,128)(2,1)S(1)}, bf16[4,256,128]{2,1,0:T(8,128)(2,1)S(1)}, u32[]{:S(2)}, u32[]{:S(2)}) collective-permute-start(bf16[4,256,128]{2,1,0:T(8,128)(2,1)S(1)} %shard_map.74.own), channel_id=1, source_target_pairs={{0,8},{1,9},{2,10},{3,11},{4,12},{5,13},{6,14},{7,15},{8,0},{9,1},... | collective-permute-start | bytes 786440 | tf_op jit(solution)/shard_map/ppermute | solution.py:57
  45.0 10.4 %collective-permute-start.18 = (bf16[4,256,128]{2,1,0:T(8,128)(2,1)S(1)}, bf16[4,256,128]{2,1,0:T(8,128)(2,1)S(1)}, u32[]{:S(2)}, u32[]{:S(2)}) collective-permute-start(bf16[4,256,128]{2,1,0:T(8,128)(2,1)S(1)} %shard_map.74.own), channel_id=1, source_target_pairs={{8,16},{9,17},{10,18},{11,19},{12,20},{13,21},{14,22},{15,23},{16,... | collective-permute-start | bytes 786440 | tf_op jit(solution)/shard_map/ppermute | solution.py:57
  49.9 7.5 %collective-permute-start.21 = (bf16[2,256,128]{2,1,0:T(8,128)(2,1)S(1)}, bf16[2,256,128]{2,1,0:T(8,128)(2,1)S(1)}, u32[]{:S(2)}, u32[]{:S(2)}) collective-permute-start(bf16[2,256,128]{2,1,0:T(8,128)(2,1)S(1)} %get-tuple-element.68.own), channel_id=1, source_target_pairs={{8,16},{9,17},{10,18},{11,19},{12,20},{13,21},{14,22},{15,23},{16,... | collective-permute-start | bytes 393224 | tf_op jit(solution)/shard_map/ppermute | solution.py:57
  51.8 5.5 %collective-permute-start.22 = (bf16[2,256,128]{2,1,0:T(8,128)(2,1)S(1)}, bf16[2,256,128]{2,1,0:T(8,128)(2,1)S(1)}, u32[]{:S(2)}, u32[]{:S(2)}) collective-permute-start(bf16[2,256,128]{2,1,0:T(8,128)(2,1)S(1)} %get-tuple-element.68.own), channel_id=1, source_target_pairs={{0,8},{1,9},{2,10},{3,11},{4,12},{5,13},{6,14},{7,15},{8,0},{9,1},... | collective-permute-start | bytes 393224 | tf_op jit(solution)/shard_map/ppermute | solution.py:57
  51.9 8.3 %collective-permute-start.19 = (bf16[2,256,128]{2,1,0:T(8,128)(2,1)S(1)}, bf16[2,256,128]{2,1,0:T(8,128)(2,1)S(1)}, u32[]{:S(2)}, u32[]{:S(2)}) collective-permute-start(bf16[2,256,128]{2,1,0:T(8,128)(2,1)S(1)} %get-tuple-element.67.own), channel_id=1, source_target_pairs={{8,16},{9,17},{10,18},{11,19},{12,20},{13,21},{14,22},{15,23},{16,... | collective-permute-start | bytes 393224 | tf_op jit(solution)/shard_map/ppermute | solution.py:57
  55.3 4.9 %collective-permute-start.20 = (bf16[2,256,128]{2,1,0:T(8,128)(2,1)S(1)}, bf16[2,256,128]{2,1,0:T(8,128)(2,1)S(1)}, u32[]{:S(2)}, u32[]{:S(2)}) collective-permute-start(bf16[2,256,128]{2,1,0:T(8,128)(2,1)S(1)} %get-tuple-element.67.own), channel_id=1, source_target_pairs={{0,8},{1,9},{2,10},{3,11},{4,12},{5,13},{6,14},{7,15},{8,0},{9,1},... | collective-permute-start | bytes 393224 | tf_op jit(solution)/shard_map/ppermute | solution.py:57
  57.6 5.6 %collective-permute-start.25 = (bf16[256,128]{1,0:T(8,128)(2,1)S(1)}, bf16[256,128]{1,0:T(8,128)(2,1)S(1)}, u32[]{:S(2)}, u32[]{:S(2)}) collective-permute-start(bf16[256,128]{1,0:T(8,128)(2,1)S(1)} %shard_map.79), channel_id=1, source_target_pairs={{0,3},{1,2},{2,1},{3,0},{4,7},{5,6},{6,5},{7,4},{8,11},{9,10},{10,... | collective-permute-start | bytes 196616 | tf_op jit(solution)/shard_map/ppermute | solution.py:57
  60.4 3.6 %collective-permute-start.24 = (bf16[256,128]{1,0:T(8,128)(2,1)S(1)}, bf16[256,128]{1,0:T(8,128)(2,1)S(1)}, u32[]{:S(2)}, u32[]{:S(2)}) collective-permute-start(bf16[256,128]{1,0:T(8,128)(2,1)S(1)} %shard_map.78), channel_id=1, source_target_pairs={{0,2},{1,3},{2,0},{3,1},{4,6},{5,7},{6,4},{7,5},{8,10},{9,11},{10,... | collective-permute-start | bytes 196616 | tf_op jit(solution)/shard_map/ppermute | solution.py:57
  62.6 3.5 %collective-permute-start.23 = (bf16[256,128]{1,0:T(8,128)(2,1)S(1)}, bf16[256,128]{1,0:T(8,128)(2,1)S(1)}, u32[]{:S(2)}, u32[]{:S(2)}) collective-permute-start(bf16[256,128]{1,0:T(8,128)(2,1)S(1)} %shard_map.77), channel_id=1, source_target_pairs={{0,1},{1,0},{2,3},{3,2},{4,5},{5,4},{6,7},{7,6},{8,9},{9,8},{10,11... | collective-permute-start | bytes 196616 | tf_op jit(solution)/shard_map/ppermute | solution.py:57
  66.1 3.4 %collective-permute-start.26 = (bf16[4,128,128]{2,1,0:T(8,128)(2,1)S(1)}, bf16[4,128,128]{2,1,0:T(8,128)(2,1)S(1)}, u32[]{:S(2)}, u32[]{:S(2)}) collective-permute-start(bf16[4,128,128]{2,1,0:T(8,128)(2,1)S(1)} %get-tuple-element.70), channel_id=1, source_target_pairs={{0,4},{1,5},{2,6},{3,7},{4,0},{5,1},{6,2},{7,3},{8,12},{9,13},{10,... | collective-permute-start | bytes 393224 | tf_op jit(solution)/shard_map/ppermute | solution.py:57
  (9 other events, 40.0 us)

commit v23 on v20

--- a/solution.py
+++ b/solution.py
@@ -90,10 +90,7 @@
     to_x[:size] = w[:, PAIR : 2 * PAIR]
     to_y[:size] = jnp.where(even, high, low)
     keep[...] = jnp.where(even, low, high)
-    at = to_across.shape[0] - EXTRA - half
-    for i in range(2):
-        to_across[:at, i * HD : (i + 1) * HD] = raw[:at]
-    for ref, at in ((to_x, size), (to_y, size), (to_across, at)):
+    for ref, at in ((to_x, size), (to_y, size), (to_across, 0)):
         for i in range(2):
             here = slice(i * HD, (i + 1) * HD)
             ref[at : at + half, here] = raw[i * half : (i + 1) * half]
@@ -332,7 +329,7 @@
     more = block // 2 + EXTRA
     *to, kept = call(
         split_kernel,
-        (array(size + more, PAIR), array(size + more, PAIR), array(block, PAIR), array(size, PAIR)),
+        (array(size + more, PAIR), array(size + more, PAIR), array(more, PAIR), array(size, PAIR)),
         "vv",
     )(w_qkv, raw)
     plane = [swap_depth(t, r) for t, r in zip(to, (1, 2, 3))]
@@ -353,10 +350,9 @@
             macs=len(rs) * block * 3 * feat_len * width,
         )(raw, *plane, conv_w, gain, *streams, *finished)
 
-    tied = after(stream, plane[2])
+    tied = after(stream, to[0])
     beside, above = swap_depth(tied, 1), swap_depth(tied, 2)
     (normed,) = embed((0,), stream)
-    far_raw = after(far_raw, normed)
 
     even = (lax.axis_index("depth") & 1) == 0
     low, to_x, high = (far_raw[:, k * PAIR : (k + 1) * PAIR] for k in range(3))

time: 70.8 us -> 69.7 us (0.984)
  starting transfers between devices: 34.8 us -> 29.9 us
  waiting for transfers between devices: 21.9 us -> 25.4 us
  local copies, waits for them, and re-layouts: 3.18 us -> 1.07 us
  Pallas kernels: 8.81 us -> 9.98 us
  other arithmetic: 1.45 us -> 2.48 us
    ppermute x27, starting transfers between devices: 34.8 us -> 29.9 us  [hop(): return lax.ppermute(value, ('tm', 'depth'), pairs)]
    ppermute x27, waiting for transfers between devices: 21.9 us -> 25.4 us  [hop(): return lax.ppermute(value, ('tm', 'depth'), pairs)]
    unnamed x13 -> x9, local copies, waits for them, and re-layouts: 3.13 us -> 1.03 us
    pallas_call x3, Pallas kernels: 2.39 us -> 3.56 us  [embed(): call(functools.partial(embed_kernel, rs, len(finished)), out, 'v' * (6 +...]
    select_n x1, other arithmetic: 0.03 us -> 1.06 us  [plane_device(): kept, to_y = (jnp.where(even, low, high), jnp.where(even, high, low))]
  transfers between devices with their start and end apart: 27 -> 27, of which waited for: 15 -> 16; matrix products, arithmetic and copies ran while one was open for 2% -> 4% of each run, Pallas kernels for 11% -> 13%
where the time goes in v23:
time: 69.7 us; the launch traced here: 69 us
  starting transfers between devices  29.9 us (43%)
  waiting for transfers between devices  25.4 us (36%)
  Pallas kernels  9.98 us (14%)
  other arithmetic  2.48 us (4%)
  local copies, waits for them, and re-layouts  1.07 us (2%)
    ppermute x27, starting transfers between devices, hop(): return lax.ppermute(value, ('tm', 'depth'), pairs)  29.9 us
    ppermute x27, waiting for transfers between devices, hop(): return lax.ppermute(value, ('tm', 'depth'), pairs)  25.4 us
    pallas_call x3, Pallas kernels, embed(): call(functools.partial(embed_kernel, rs, len(finished)), out, 'v' * (6 +...  3.56 us
  transfers between devices with their start and end apart: 27, of which 16 were waited for; matrix products, arithmetic and copies ran while one was open for 4% of the time, Pallas kernels for 13%

profile of v23, /device:TPU:9, one launch (start us, length us, event | category | flops | bytes accessed | tf_op | source)
XLA Modules:
  0.0 69.0 jit_solution(6626168439112595566)
XLA Ops:
  0.0 2.3 %collective-permute-start = (bf16[256,768]{1,0:T(8,128)(2,1)}, bf16[256,768]{1,0:T(8,128)(2,1)}, u32[]{:S(2)}, u32[]{:S(2)}) collective-permute-start(bf16[256,768]{1,0:T(8,128)(2,1)} %w.1), channel_id=1, source_target_pairs={{0,16},{1,17},{2,18},{3,19},{4,20},{5,21},{6,22},{7,23},{8,24},{9,... | collective-permute-start | bytes 1179656 | tf_op jit(solution)/shard_map/ppermute | solution.py:57
  4.8 1.3 %collective-permute-start.3 = (bf16[336,256]{1,0:T(8,128)(2,1)S(1)}, bf16[336,256]{1,0:T(8,128)(2,1)S(1)}, u32[]{:S(2)}, u32[]{:S(2)}) collective-permute-start(bf16[336,256]{1,0:T(8,128)(2,1)S(1)} %get-tuple-element.37), channel_id=1, source_target_pairs={{0,1},{1,0},{2,3},{3,2},{4,5},{5,4},{6,7},{7,6},{8,9},{9,8},{10,11... | collective-permute-start | bytes 516104 | tf_op jit(solution)/shard_map/ppermute | solution.py:57
  6.1 1.2 %collective-permute-start.4 = (bf16[336,256]{1,0:T(8,128)(2,1)S(1)}, bf16[336,256]{1,0:T(8,128)(2,1)S(1)}, u32[]{:S(2)}, u32[]{:S(2)}) collective-permute-start(bf16[336,256]{1,0:T(8,128)(2,1)S(1)} %get-tuple-element.38), channel_id=1, source_target_pairs={{0,2},{1,3},{2,0},{3,1},{4,6},{5,7},{6,4},{7,5},{8,10},{9,11},{10,... | collective-permute-start | bytes 516104 | tf_op jit(solution)/shard_map/ppermute | solution.py:57
  7.8 2.1 %collective-permute-done.3.plane_x.from_x = bf16[336,256]{1,0:T(8,128)(2,1)S(1)} collective-permute-done((bf16[336,256]{1,0:T(8,128)(2,1)S(1)}, bf16[336,256]{1,0:T(8,128)(2,1)S(1)}, u32[]{:S(2)}, u32[]{:S(2)}) %collective-permute-start.3) | collective-permute-done | bytes 172064 | tf_op jit(solution)/shard_map/ppermute | solution.py:57
  11.2 1.2 %collective-permute-start.5 = (bf16[80,256]{1,0:T(8,128)(2,1)S(1)}, bf16[80,256]{1,0:T(8,128)(2,1)S(1)}, u32[]{:S(2)}, u32[]{:S(2)}) collective-permute-start(bf16[80,256]{1,0:T(8,128)(2,1)S(1)} %get-tuple-element.39), channel_id=1, source_target_pairs={{0,3},{1,2},{2,1},{3,0},{4,7},{5,6},{6,5},{7,4},{8,11},{9,10},{10,... | collective-permute-start | bytes 122888 | tf_op jit(solution)/shard_map/ppermute | solution.py:57
  12.3 7.5 %collective-permute-done = bf16[256,768]{1,0:T(8,128)(2,1)} collective-permute-done((bf16[256,768]{1,0:T(8,128)(2,1)}, bf16[256,768]{1,0:T(8,128)(2,1)}, u32[]{:S(2)}, u32[]{:S(2)}) %collective-permute-start) | collective-permute-done | bytes 393248 | tf_op jit(solution)/shard_map/ppermute | solution.py:57
  20.9 1.3 %collective-permute-start.1 = (bf16[256,256]{1,0:T(8,128)(2,1)S(1)}, bf16[256,256]{1,0:T(8,128)(2,1)S(1)}, u32[]{:S(2)}, u32[]{:S(2)}) collective-permute-start(bf16[256,256]{1,0:T(8,128)(2,1)S(1)} %get-tuple-element.70), channel_id=1, source_target_pairs={{0,1},{1,0},{2,3},{3,2},{4,5},{5,4},{6,7},{7,6},{8,9},{9,8},{10,11... | collective-permute-start | bytes 393224 | tf_op jit(solution)/shard_map/ppermute | solution.py:57
  24.1 2.3 %shard_map.66 = (bf16[384,2048]{1,0:T(8,128)(2,1)S(1)}, bf16[128,1024]{1,0:T(8,128)(2,1)S(1)}, bf16[128,1024]{1,0:T(8,128)(2,1)S(1)}) custom-call(bf16[144,128]{1,0:T(8,128)(2,1)S(1)} %pad_maximum_fusion.raw, bf16[336,256]{1,0:T(8,128)(2,1)S(1)} %collective-permute-done.3.plane_x.from_x, bf16[336,256]{1,0:T(8,128)(2,1)S(1)} %collective-permute-done.4.plane_y.from_y, ...), custom_call_target="tpu_custom_call" | custom-call | flops 402653184 | tf_op jit(solution)/shard_map/pallas_call | solution.py:345
  27.0 2.9 %collective-permute-start.9 = (bf16[256,384]{1,0:T(8,128)(2,1)S(1)}, bf16[256,384]{1,0:T(8,128)(2,1)S(1)}, u32[]{:S(2)}, u32[]{:S(2)}) collective-permute-start(bf16[256,384]{1,0:T(8,128)(2,1)S(1)} %get-tuple-element.48), channel_id=1, source_target_pairs={{0,4},{1,5},{2,6},{3,7},{4,0},{5,1},{6,2},{7,3},{8,12},{9,13},{10,... | collective-permute-start | bytes 589832 | tf_op jit(solution)/shard_map/ppermute | solution.py:57
  33.4 1.7 %collective-permute-done.12.refs_4_.refs_2_.received = bf16[528,384]{1,0:T(8,128)(2,1)S(1)} collective-permute-done((bf16[528,384]{1,0:T(8,128)(2,1)S(1)}, bf16[528,384]{1,0:T(8,128)(2,1)S(1)}, u32[]{:S(2)}, u32[]{:S(2)}) %collective-permute-start.12) | collective-permute-done | bytes 405536 | tf_op jit(solution)/shard_map/ppermute | solution.py:57
  35.1 1.4 %shard_map.70.refs_4_ = f32[768,384]{1,0:T(8,128)S(1)} custom-call(bf16[384,2048]{1,0:T(8,128)(2,1)S(1)} %get-tuple-element.51.refs_0_, bf16[384,2048]{1,0:T(8,128)(2,1)S(1)} %collective-permute-done.10.refs_1_, bf16[256,768]{1,0:T(8,128)(2,1)S(1)} %shard_map.67.own.refs_2_.refs_0_, bf16[256,768]{1,0:T(8,128)(2,1)S(1)} %collective-permute-done.8.near.refs_3_.refs_1_, ...), custom_call_target="tpu_custom_call" | custom-call | flops 905969664 | tf_op jit(solution)/shard_map/pallas_call | solution.py:378
  36.5 2.8 %collective-permute-done.13.refs_1_ = bf16[128,1024]{1,0:T(8,128)(2,1)S(1)} collective-permute-done((bf16[128,1024]{1,0:T(8,128)(2,1)S(1)}, bf16[128,1024]{1,0:T(8,128)(2,1)S(1)}, u32[]{:S(2)}, u32[]{:S(2)}) %collective-permute-start.13) | collective-permute-done | bytes 262176 | tf_op jit(solution)/shard_map/ppermute | solution.py:57
  40.7 1.6 %collective-permute-start.14 = (bf16[80,2048]{1,0:T(8,128)(2,1)S(1)}, bf16[80,2048]{1,0:T(8,128)(2,1)S(1)}, u32[]{:S(2)}, u32[]{:S(2)}) collective-permute-start(bf16[80,2048]{1,0:T(8,128)(2,1)S(1)} %get-tuple-element.60), channel_id=1, source_target_pairs={{0,4},{1,5},{2,6},{3,7},{4,0},{5,1},{6,2},{7,3},{8,12},{9,13},{10,... | collective-permute-start | bytes 983048 | tf_op jit(solution)/shard_map/ppermute | solution.py:57
  42.4 1.5 %collective-permute-done.15.bottom = bf16[48,2048]{1,0:T(8,128)(2,1)S(1)} collective-permute-done((bf16[48,2048]{1,0:T(8,128)(2,1)S(1)}, bf16[48,2048]{1,0:T(8,128)(2,1)S(1)}, u32[]{:S(2)}, u32[]{:S(2)}) %collective-permute-start.15) | collective-permute-done | bytes 196640 | tf_op jit(solution)/shard_map/ppermute | solution.py:57
  45.2 2.6 %collective-permute-start.18 = (bf16[4,256,128]{2,1,0:T(8,128)(2,1)S(1)}, bf16[4,256,128]{2,1,0:T(8,128)(2,1)S(1)}, u32[]{:S(2)}, u32[]{:S(2)}) collective-permute-start(bf16[4,256,128]{2,1,0:T(8,128)(2,1)S(1)} %shard_map.74.own), channel_id=1, source_target_pairs={{8,16},{9,17},{10,18},{11,19},{12,20},{13,21},{14,22},{15,23},{16,... | collective-permute-start | bytes 786440 | tf_op jit(solution)/shard_map/ppermute | solution.py:57
  48.5 2.7 %collective-permute-start.22 = (bf16[2,256,128]{2,1,0:T(8,128)(2,1)S(1)}, bf16[2,256,128]{2,1,0:T(8,128)(2,1)S(1)}, u32[]{:S(2)}, u32[]{:S(2)}) collective-permute-start(bf16[2,256,128]{2,1,0:T(8,128)(2,1)S(1)} %get-tuple-element.66.own), channel_id=1, source_target_pairs={{8,16},{9,17},{10,18},{11,19},{12,20},{13,21},{14,22},{15,23},{16,... | collective-permute-start | bytes 393224 | tf_op jit(solution)/shard_map/ppermute | solution.py:57
  51.3 1.2 %collective-permute-done.17.outer = bf16[4,256,128]{2,1,0:T(8,128)(2,1)S(1)} collective-permute-done((bf16[4,256,128]{2,1,0:T(8,128)(2,1)S(1)}, bf16[4,256,128]{2,1,0:T(8,128)(2,1)S(1)}, u32[]{:S(2)}, u32[]{:S(2)}) %collective-permute-start.17) | collective-permute-done | bytes 262176 | tf_op jit(solution)/shard_map/ppermute | solution.py:57
  52.5 1.9 %collective-permute-start.20 = (bf16[2,256,128]{2,1,0:T(8,128)(2,1)S(1)}, bf16[2,256,128]{2,1,0:T(8,128)(2,1)S(1)}, u32[]{:S(2)}, u32[]{:S(2)}) collective-permute-start(bf16[2,256,128]{2,1,0:T(8,128)(2,1)S(1)} %get-tuple-element.65.own), channel_id=1, source_target_pairs={{8,16},{9,17},{10,18},{11,19},{12,20},{13,21},{14,22},{15,23},{16,... | collective-permute-start | bytes 393224 | tf_op jit(solution)/shard_map/ppermute | solution.py:57
  54.4 1.2 %shard_map.75.weights = bf16[4,256,640]{2,1,0:T(8,128)(2,1)S(1)} custom-call(bf16[4,256,128]{2,1,0:T(8,128)(2,1)S(1)} %get-tuple-element.64.q_ref, bf16[4,256,128]{2,1,0:T(8,128)(2,1)S(1)} %collective-permute-done.17.outer, bf16[4,256,128]{2,1,0:T(8,128)(2,1)S(1)} %shard_map.74.own, bf16[4,256,128]{2,1,0:T(8,128)(2,1)S(1)} %collective-permute-done.18.middle, ...), custom_call_target="tpu_custom_call" | custom-call | flops 167772160 | tf_op jit(solution)/shard_map/pallas_call | solution.py:395
  55.6 1.4 %collective-permute-done.22.middle = bf16[2,256,128]{2,1,0:T(8,128)(2,1)S(1)} collective-permute-done((bf16[2,256,128]{2,1,0:T(8,128)(2,1)S(1)}, bf16[2,256,128]{2,1,0:T(8,128)(2,1)S(1)}, u32[]{:S(2)}, u32[]{:S(2)}) %collective-permute-start.22) | collective-permute-done | bytes 131104 | tf_op jit(solution)/shard_map/ppermute | solution.py:57
  57.3 1.7 %collective-permute-start.25 = (bf16[256,128]{1,0:T(8,128)(2,1)S(1)}, bf16[256,128]{1,0:T(8,128)(2,1)S(1)}, u32[]{:S(2)}, u32[]{:S(2)}) collective-permute-start(bf16[256,128]{1,0:T(8,128)(2,1)S(1)} %shard_map.79), channel_id=1, source_target_pairs={{0,3},{1,2},{2,1},{3,0},{4,7},{5,6},{6,5},{7,4},{8,11},{9,10},{10,... | collective-permute-start | bytes 196616 | tf_op jit(solution)/shard_map/ppermute | solution.py:57
  60.6 1.9 %collective-permute-start.23 = (bf16[256,128]{1,0:T(8,128)(2,1)S(1)}, bf16[256,128]{1,0:T(8,128)(2,1)S(1)}, u32[]{:S(2)}, u32[]{:S(2)}) collective-permute-start(bf16[256,128]{1,0:T(8,128)(2,1)S(1)} %shard_map.77), channel_id=1, source_target_pairs={{0,1},{1,0},{2,3},{3,2},{4,5},{5,4},{6,7},{7,6},{8,9},{9,8},{10,11... | collective-permute-start | bytes 196616 | tf_op jit(solution)/shard_map/ppermute | solution.py:57
  62.7 2.3 %collective-permute-done.23.refs_1_ = bf16[256,128]{1,0:T(8,128)(2,1)S(1)} collective-permute-done((bf16[256,128]{1,0:T(8,128)(2,1)S(1)}, bf16[256,128]{1,0:T(8,128)(2,1)S(1)}, u32[]{:S(2)}, u32[]{:S(2)}) %collective-permute-start.23) | collective-permute-done | bytes 65568 | tf_op jit(solution)/shard_map/ppermute | solution.py:57
  65.0 2.3 %collective-permute-start.26 = (bf16[4,128,128]{2,1,0:T(8,128)(2,1)S(1)}, bf16[4,128,128]{2,1,0:T(8,128)(2,1)S(1)}, u32[]{:S(2)}, u32[]{:S(2)}) collective-permute-start(bf16[4,128,128]{2,1,0:T(8,128)(2,1)S(1)} %get-tuple-element.68), channel_id=1, source_target_pairs={{0,4},{1,5},{2,6},{3,7},{4,0},{5,1},{6,2},{7,3},{8,12},{9,13},{10,... | collective-permute-start | bytes 393224 | tf_op jit(solution)/shard_map/ppermute | solution.py:57
  (63 shorter events, 18.7 us)
Async XLA Ops:
  0.0 19.8 %collective-permute-start = (bf16[256,768]{1,0:T(8,128)(2,1)}, bf16[256,768]{1,0:T(8,128)(2,1)}, u32[]{:S(2)}, u32[]{:S(2)}) collective-permute-start(bf16[256,768]{1,0:T(8,128)(2,1)} %w.1), channel_id=1, source_target_pairs={{0,16},{1,17},{2,18},{3,19},{4,20},{5,21},{6,22},{7,23},{8,24},{9,... | collective-permute-start | bytes 1179656 | tf_op jit(solution)/shard_map/ppermute | solution.py:57
  4.8 5.1 %collective-permute-start.3 = (bf16[336,256]{1,0:T(8,128)(2,1)S(1)}, bf16[336,256]{1,0:T(8,128)(2,1)S(1)}, u32[]{:S(2)}, u32[]{:S(2)}) collective-permute-start(bf16[336,256]{1,0:T(8,128)(2,1)S(1)} %get-tuple-element.37), channel_id=1, source_target_pairs={{0,1},{1,0},{2,3},{3,2},{4,5},{5,4},{6,7},{7,6},{8,9},{9,8},{10,11... | collective-permute-start | bytes 516104 | tf_op jit(solution)/shard_map/ppermute | solution.py:57
  6.1 4.7 %collective-permute-start.4 = (bf16[336,256]{1,0:T(8,128)(2,1)S(1)}, bf16[336,256]{1,0:T(8,128)(2,1)S(1)}, u32[]{:S(2)}, u32[]{:S(2)}) collective-permute-start(bf16[336,256]{1,0:T(8,128)(2,1)S(1)} %get-tuple-element.38), channel_id=1, source_target_pairs={{0,2},{1,3},{2,0},{3,1},{4,6},{5,7},{6,4},{7,5},{8,10},{9,11},{10,... | collective-permute-start | bytes 516104 | tf_op jit(solution)/shard_map/ppermute | solution.py:57
  7.3 16.7 %collective-permute-start.6 = (bf16[128,2048]{1,0:T(8,128)(2,1)}, bf16[128,2048]{1,0:T(8,128)(2,1)}, u32[]{:S(2)}, u32[]{:S(2)}) collective-permute-start(bf16[128,2048]{1,0:T(8,128)(2,1)} %bitcast.12), channel_id=1, source_target_pairs={{0,1},{1,0},{2,3},{3,2},{4,5},{5,4},{6,7},{7,6},{8,9},{9,8},{10,11... | collective-permute-start | bytes 1572872 | tf_op jit(solution)/shard_map/ppermute | solution.py:57
  7.6 16.5 %collective-permute-start.7 = (bf16[128,2048]{1,0:T(8,128)(2,1)}, bf16[128,2048]{1,0:T(8,128)(2,1)}, u32[]{:S(2)}, u32[]{:S(2)}) collective-permute-start(bf16[128,2048]{1,0:T(8,128)(2,1)} %bitcast.13), channel_id=1, source_target_pairs={{0,2},{1,3},{2,0},{3,1},{4,6},{5,7},{6,4},{7,5},{8,10},{9,11},{10,... | collective-permute-start | bytes 1572872 | tf_op jit(solution)/shard_map/ppermute | solution.py:57
  10.9 16.0 %collective-permute-start.8 = (bf16[256,768]{1,0:T(8,128)(2,1)S(1)}, bf16[256,768]{1,0:T(8,128)(2,1)S(1)}, u32[]{:S(2)}, u32[]{:S(2)}) collective-permute-start(bf16[256,768]{1,0:T(8,128)(2,1)S(1)} %shard_map.67.own.refs_2_.refs_0_), channel_id=1, source_target_pairs={{0,8},{1,9},{2,10},{3,11},{4,12},{5,13},{6,14},{7,15},{8,0},{9,1},... | collective-permute-start | bytes 1179656 | tf_op jit(solution)/shard_map/ppermute | solution.py:57
  11.2 11.4 %collective-permute-start.5 = (bf16[80,256]{1,0:T(8,128)(2,1)S(1)}, bf16[80,256]{1,0:T(8,128)(2,1)S(1)}, u32[]{:S(2)}, u32[]{:S(2)}) collective-permute-start(bf16[80,256]{1,0:T(8,128)(2,1)S(1)} %get-tuple-element.39), channel_id=1, source_target_pairs={{0,3},{1,2},{2,1},{3,0},{4,7},{5,6},{6,5},{7,4},{8,11},{9,10},{10,... | collective-permute-start | bytes 122888 | tf_op jit(solution)/shard_map/ppermute | solution.py:57
  20.9 5.5 %collective-permute-start.1 = (bf16[256,256]{1,0:T(8,128)(2,1)S(1)}, bf16[256,256]{1,0:T(8,128)(2,1)S(1)}, u32[]{:S(2)}, u32[]{:S(2)}) collective-permute-start(bf16[256,256]{1,0:T(8,128)(2,1)S(1)} %get-tuple-element.70), channel_id=1, source_target_pairs={{0,1},{1,0},{2,3},{3,2},{4,5},{5,4},{6,7},{7,6},{8,9},{9,8},{10,11... | collective-permute-start | bytes 393224 | tf_op jit(solution)/shard_map/ppermute | solution.py:57
  22.6 3.9 %collective-permute-start.2 = (bf16[256,256]{1,0:T(8,128)(2,1)S(1)}, bf16[256,256]{1,0:T(8,128)(2,1)S(1)}, u32[]{:S(2)}, u32[]{:S(2)}) collective-permute-start(bf16[256,256]{1,0:T(8,128)(2,1)S(1)} %get-tuple-element.69), channel_id=1, source_target_pairs={{0,2},{1,3},{2,0},{3,1},{4,6},{5,7},{6,4},{7,5},{8,10},{9,11},{10,... | collective-permute-start | bytes 393224 | tf_op jit(solution)/shard_map/ppermute | solution.py:57
  27.0 4.0 %collective-permute-start.9 = (bf16[256,384]{1,0:T(8,128)(2,1)S(1)}, bf16[256,384]{1,0:T(8,128)(2,1)S(1)}, u32[]{:S(2)}, u32[]{:S(2)}) collective-permute-start(bf16[256,384]{1,0:T(8,128)(2,1)S(1)} %get-tuple-element.48), channel_id=1, source_target_pairs={{0,4},{1,5},{2,6},{3,7},{4,0},{5,1},{6,2},{7,3},{8,12},{9,13},{10,... | collective-permute-start | bytes 589832 | tf_op jit(solution)/shard_map/ppermute | solution.py:57
  31.1 4.1 %collective-permute-start.10 = (bf16[384,2048]{1,0:T(8,128)(2,1)S(1)}, bf16[384,2048]{1,0:T(8,128)(2,1)S(1)}, u32[]{:S(2)}, u32[]{:S(2)}) collective-permute-start(bf16[384,2048]{1,0:T(8,128)(2,1)S(1)} %get-tuple-element.51.refs_0_), channel_id=1, source_target_pairs={{0,4},{1,5},{2,6},{3,7},{4,0},{5,1},{6,2},{7,3},{8,12},{9,13},{10,... | collective-permute-start | bytes 4718600 | tf_op jit(solution)/shard_map/ppermute | solution.py:57
  31.6 3.6 %collective-permute-start.12 = (bf16[528,384]{1,0:T(8,128)(2,1)S(1)}, bf16[528,384]{1,0:T(8,128)(2,1)S(1)}, u32[]{:S(2)}, u32[]{:S(2)}) collective-permute-start(bf16[528,384]{1,0:T(8,128)(2,1)S(1)} %shard_map.69), channel_id=1, source_target_pairs={{0,4},{1,5},{2,6},{3,7},{4,0},{5,1},{6,2},{7,3},{8,12},{9,13},{10,... | collective-permute-start | bytes 1216520 | tf_op jit(solution)/shard_map/ppermute | solution.py:57
  31.8 7.5 %collective-permute-start.13 = (bf16[128,1024]{1,0:T(8,128)(2,1)S(1)}, bf16[128,1024]{1,0:T(8,128)(2,1)S(1)}, u32[]{:S(2)}, u32[]{:S(2)}) collective-permute-start(bf16[128,1024]{1,0:T(8,128)(2,1)S(1)} %get-tuple-element.57), channel_id=1, source_target_pairs={{0,1},{1,0},{2,3},{3,2},{4,5},{5,4},{6,7},{7,6},{8,9},{9,8},{10,11... | collective-permute-start | bytes 786440 | tf_op jit(solution)/shard_map/ppermute | solution.py:57
  32.9 7.2 %collective-permute-start.11 = (bf16[128,1024]{1,0:T(8,128)(2,1)S(1)}, bf16[128,1024]{1,0:T(8,128)(2,1)S(1)}, u32[]{:S(2)}, u32[]{:S(2)}) collective-permute-start(bf16[128,1024]{1,0:T(8,128)(2,1)S(1)} %get-tuple-element.52), channel_id=1, source_target_pairs={{0,2},{1,3},{2,0},{3,1},{4,6},{5,7},{6,4},{7,5},{8,10},{9,11},{10,... | collective-permute-start | bytes 786440 | tf_op jit(solution)/shard_map/ppermute | solution.py:57
  33.2 11.3 %collective-permute-start.16 = (bf16[512,384]{1,0:T(8,128)(2,1)S(1)}, bf16[512,384]{1,0:T(8,128)(2,1)S(1)}, u32[]{:S(2)}, u32[]{:S(2)}) collective-permute-start(bf16[512,384]{1,0:T(8,128)(2,1)S(1)} %constant_dynamic-update-slice_fusion.refs_5_.refs_3_), channel_id=1, source_target_pairs={{0,8},{1,9},{2,10},{3,11},{4,12},{5,13},{6,14},{7,15},{8,0},{9,1},... | collective-permute-start | bytes 1179656 | tf_op jit(solution)/shard_map/ppermute | solution.py:57
  44.9 7.6 %collective-permute-start.17 = (bf16[4,256,128]{2,1,0:T(8,128)(2,1)S(1)}, bf16[4,256,128]{2,1,0:T(8,128)(2,1)S(1)}, u32[]{:S(2)}, u32[]{:S(2)}) collective-permute-start(bf16[4,256,128]{2,1,0:T(8,128)(2,1)S(1)} %shard_map.74.own), channel_id=1, source_target_pairs={{0,8},{1,9},{2,10},{3,11},{4,12},{5,13},{6,14},{7,15},{8,0},{9,1},... | collective-permute-start | bytes 786440 | tf_op jit(solution)/shard_map/ppermute | solution.py:57
  45.2 9.3 %collective-permute-start.18 = (bf16[4,256,128]{2,1,0:T(8,128)(2,1)S(1)}, bf16[4,256,128]{2,1,0:T(8,128)(2,1)S(1)}, u32[]{:S(2)}, u32[]{:S(2)}) collective-permute-start(bf16[4,256,128]{2,1,0:T(8,128)(2,1)S(1)} %shard_map.74.own), channel_id=1, source_target_pairs={{8,16},{9,17},{10,18},{11,19},{12,20},{13,21},{14,22},{15,23},{16,... | collective-permute-start | bytes 786440 | tf_op jit(solution)/shard_map/ppermute | solution.py:57
  48.4 7.2 %collective-permute-start.21 = (bf16[2,256,128]{2,1,0:T(8,128)(2,1)S(1)}, bf16[2,256,128]{2,1,0:T(8,128)(2,1)S(1)}, u32[]{:S(2)}, u32[]{:S(2)}) collective-permute-start(bf16[2,256,128]{2,1,0:T(8,128)(2,1)S(1)} %get-tuple-element.66.own), channel_id=1, source_target_pairs={{0,8},{1,9},{2,10},{3,11},{4,12},{5,13},{6,14},{7,15},{8,0},{9,1},... | collective-permute-start | bytes 393224 | tf_op jit(solution)/shard_map/ppermute | solution.py:57
  48.5 8.5 %collective-permute-start.22 = (bf16[2,256,128]{2,1,0:T(8,128)(2,1)S(1)}, bf16[2,256,128]{2,1,0:T(8,128)(2,1)S(1)}, u32[]{:S(2)}, u32[]{:S(2)}) collective-permute-start(bf16[2,256,128]{2,1,0:T(8,128)(2,1)S(1)} %get-tuple-element.66.own), channel_id=1, source_target_pairs={{8,16},{9,17},{10,18},{11,19},{12,20},{13,21},{14,22},{15,23},{16,... | collective-permute-start | bytes 393224 | tf_op jit(solution)/shard_map/ppermute | solution.py:57
  51.2 7.8 %collective-permute-start.19 = (bf16[2,256,128]{2,1,0:T(8,128)(2,1)S(1)}, bf16[2,256,128]{2,1,0:T(8,128)(2,1)S(1)}, u32[]{:S(2)}, u32[]{:S(2)}) collective-permute-start(bf16[2,256,128]{2,1,0:T(8,128)(2,1)S(1)} %get-tuple-element.65.own), channel_id=1, source_target_pairs={{0,8},{1,9},{2,10},{3,11},{4,12},{5,13},{6,14},{7,15},{8,0},{9,1},... | collective-permute-start | bytes 393224 | tf_op jit(solution)/shard_map/ppermute | solution.py:57
  52.5 6.8 %collective-permute-start.20 = (bf16[2,256,128]{2,1,0:T(8,128)(2,1)S(1)}, bf16[2,256,128]{2,1,0:T(8,128)(2,1)S(1)}, u32[]{:S(2)}, u32[]{:S(2)}) collective-permute-start(bf16[2,256,128]{2,1,0:T(8,128)(2,1)S(1)} %get-tuple-element.65.own), channel_id=1, source_target_pairs={{8,16},{9,17},{10,18},{11,19},{12,20},{13,21},{14,22},{15,23},{16,... | collective-permute-start | bytes 393224 | tf_op jit(solution)/shard_map/ppermute | solution.py:57
  57.3 5.4 %collective-permute-start.25 = (bf16[256,128]{1,0:T(8,128)(2,1)S(1)}, bf16[256,128]{1,0:T(8,128)(2,1)S(1)}, u32[]{:S(2)}, u32[]{:S(2)}) collective-permute-start(bf16[256,128]{1,0:T(8,128)(2,1)S(1)} %shard_map.79), channel_id=1, source_target_pairs={{0,3},{1,2},{2,1},{3,0},{4,7},{5,6},{6,5},{7,4},{8,11},{9,10},{10,... | collective-permute-start | bytes 196616 | tf_op jit(solution)/shard_map/ppermute | solution.py:57
  60.6 4.4 %collective-permute-start.23 = (bf16[256,128]{1,0:T(8,128)(2,1)S(1)}, bf16[256,128]{1,0:T(8,128)(2,1)S(1)}, u32[]{:S(2)}, u32[]{:S(2)}) collective-permute-start(bf16[256,128]{1,0:T(8,128)(2,1)S(1)} %shard_map.77), channel_id=1, source_target_pairs={{0,1},{1,0},{2,3},{3,2},{4,5},{5,4},{6,7},{7,6},{8,9},{9,8},{10,11... | collective-permute-start | bytes 196616 | tf_op jit(solution)/shard_map/ppermute | solution.py:57
  65.0 3.3 %collective-permute-start.26 = (bf16[4,128,128]{2,1,0:T(8,128)(2,1)S(1)}, bf16[4,128,128]{2,1,0:T(8,128)(2,1)S(1)}, u32[]{:S(2)}, u32[]{:S(2)}) collective-permute-start(bf16[4,128,128]{2,1,0:T(8,128)(2,1)S(1)} %get-tuple-element.68), channel_id=1, source_target_pairs={{0,4},{1,5},{2,6},{3,7},{4,0},{5,1},{6,2},{7,3},{8,12},{9,13},{10,... | collective-permute-start | bytes 393224 | tf_op jit(solution)/shard_map/ppermute | solution.py:57
  (7 other events, 74.3 us)

commit v24 on v23

--- a/solution.py
+++ b/solution.py
@@ -335,6 +335,7 @@
     plane = [swap_depth(t, r) for t, r in zip(to, (1, 2, 3))]
     own = call(sort_kernel, array(size, 6 * HD), "vvv")(kept, *plane[:2])
     near = swap_z(own, 1)
+    far_raw = after(far_raw, own)
 
     piece = 5 * block // 8
     def embed(rs, *streams, finished=()):

time: 69.7 us -> 69.7 us (level)
  no operation moved by 1% of the time
where the time goes in v24:
time: 69.7 us; the launch traced here: 69 us
  starting transfers between devices  30 us (43%)
  waiting for transfers between devices  25.3 us (36%)
  Pallas kernels  9.98 us (14%)
  other arithmetic  2.48 us (4%)
  local copies, waits for them, and re-layouts  1.07 us (2%)
    ppermute x27, starting transfers between devices, hop(): return lax.ppermute(value, ('tm', 'depth'), pairs)  30 us
    ppermute x27, waiting for transfers between devices, hop(): return lax.ppermute(value, ('tm', 'depth'), pairs)  25.3 us
    pallas_call x3, Pallas kernels, embed(): call(functools.partial(embed_kernel, rs, len(finished)), out, 'v' * (6 +...  3.56 us
  transfers between devices with their start and end apart: 27, of which 16 were waited for; matrix products, arithmetic and copies ran while one was open for 4% of the time, Pallas kernels for 13%

profile of v24, /device:TPU:9, one launch (start us, length us, event | category | flops | bytes accessed | tf_op | source)
XLA Modules:
  0.0 69.0 jit_solution(16523942499575198985)
XLA Ops:
  0.0 2.3 %collective-permute-start = (bf16[256,768]{1,0:T(8,128)(2,1)}, bf16[256,768]{1,0:T(8,128)(2,1)}, u32[]{:S(2)}, u32[]{:S(2)}) collective-permute-start(bf16[256,768]{1,0:T(8,128)(2,1)} %w.1), channel_id=1, source_target_pairs={{0,16},{1,17},{2,18},{3,19},{4,20},{5,21},{6,22},{7,23},{8,24},{9,... | collective-permute-start | bytes 1179656 | tf_op jit(solution)/shard_map/ppermute | solution.py:57
  4.8 1.3 %collective-permute-start.1 = (bf16[336,256]{1,0:T(8,128)(2,1)S(1)}, bf16[336,256]{1,0:T(8,128)(2,1)S(1)}, u32[]{:S(2)}, u32[]{:S(2)}) collective-permute-start(bf16[336,256]{1,0:T(8,128)(2,1)S(1)} %get-tuple-element.39), channel_id=1, source_target_pairs={{0,1},{1,0},{2,3},{3,2},{4,5},{5,4},{6,7},{7,6},{8,9},{9,8},{10,11... | collective-permute-start | bytes 516104 | tf_op jit(solution)/shard_map/ppermute | solution.py:57
  6.1 1.2 %collective-permute-start.2 = (bf16[336,256]{1,0:T(8,128)(2,1)S(1)}, bf16[336,256]{1,0:T(8,128)(2,1)S(1)}, u32[]{:S(2)}, u32[]{:S(2)}) collective-permute-start(bf16[336,256]{1,0:T(8,128)(2,1)S(1)} %get-tuple-element.40), channel_id=1, source_target_pairs={{0,2},{1,3},{2,0},{3,1},{4,6},{5,7},{6,4},{7,5},{8,10},{9,11},{10,... | collective-permute-start | bytes 516104 | tf_op jit(solution)/shard_map/ppermute | solution.py:57
  7.8 2.1 %collective-permute-done.1.from_x.plane_x = bf16[336,256]{1,0:T(8,128)(2,1)S(1)} collective-permute-done((bf16[336,256]{1,0:T(8,128)(2,1)S(1)}, bf16[336,256]{1,0:T(8,128)(2,1)S(1)}, u32[]{:S(2)}, u32[]{:S(2)}) %collective-permute-start.1) | collective-permute-done | bytes 172064 | tf_op jit(solution)/shard_map/ppermute | solution.py:57
  11.2 1.2 %collective-permute-start.5 = (bf16[80,256]{1,0:T(8,128)(2,1)S(1)}, bf16[80,256]{1,0:T(8,128)(2,1)S(1)}, u32[]{:S(2)}, u32[]{:S(2)}) collective-permute-start(bf16[80,256]{1,0:T(8,128)(2,1)S(1)} %get-tuple-element.42), channel_id=1, source_target_pairs={{0,3},{1,2},{2,1},{3,0},{4,7},{5,6},{6,5},{7,4},{8,11},{9,10},{10,... | collective-permute-start | bytes 122888 | tf_op jit(solution)/shard_map/ppermute | solution.py:57
  12.3 7.5 %collective-permute-done = bf16[256,768]{1,0:T(8,128)(2,1)} collective-permute-done((bf16[256,768]{1,0:T(8,128)(2,1)}, bf16[256,768]{1,0:T(8,128)(2,1)}, u32[]{:S(2)}, u32[]{:S(2)}) %collective-permute-start) | collective-permute-done | bytes 393248 | tf_op jit(solution)/shard_map/ppermute | solution.py:57
  20.9 1.3 %collective-permute-start.3 = (bf16[256,256]{1,0:T(8,128)(2,1)S(1)}, bf16[256,256]{1,0:T(8,128)(2,1)S(1)}, u32[]{:S(2)}, u32[]{:S(2)}) collective-permute-start(bf16[256,256]{1,0:T(8,128)(2,1)S(1)} %get-tuple-element.72), channel_id=1, source_target_pairs={{0,1},{1,0},{2,3},{3,2},{4,5},{5,4},{6,7},{7,6},{8,9},{9,8},{10,11... | collective-permute-start | bytes 393224 | tf_op jit(solution)/shard_map/ppermute | solution.py:57
  24.1 2.3 %shard_map.67 = (bf16[384,2048]{1,0:T(8,128)(2,1)S(1)}, bf16[128,1024]{1,0:T(8,128)(2,1)S(1)}, bf16[128,1024]{1,0:T(8,128)(2,1)S(1)}) custom-call(bf16[144,128]{1,0:T(8,128)(2,1)S(1)} %pad_maximum_fusion.raw, bf16[336,256]{1,0:T(8,128)(2,1)S(1)} %collective-permute-done.1.from_x.plane_x, bf16[336,256]{1,0:T(8,128)(2,1)S(1)} %collective-permute-done.2.from_y.plane_y, ...), custom_call_target="tpu_custom_call" | custom-call | flops 402653184 | tf_op jit(solution)/shard_map/pallas_call | solution.py:346
  27.0 2.9 %collective-permute-start.9 = (bf16[256,384]{1,0:T(8,128)(2,1)S(1)}, bf16[256,384]{1,0:T(8,128)(2,1)S(1)}, u32[]{:S(2)}, u32[]{:S(2)}) collective-permute-start(bf16[256,384]{1,0:T(8,128)(2,1)S(1)} %get-tuple-element.50), channel_id=1, source_target_pairs={{0,4},{1,5},{2,6},{3,7},{4,0},{5,1},{6,2},{7,3},{8,12},{9,13},{10,... | collective-permute-start | bytes 589832 | tf_op jit(solution)/shard_map/ppermute | solution.py:57
  33.4 1.7 %collective-permute-done.12.refs_4_.refs_2_.received = bf16[528,384]{1,0:T(8,128)(2,1)S(1)} collective-permute-done((bf16[528,384]{1,0:T(8,128)(2,1)S(1)}, bf16[528,384]{1,0:T(8,128)(2,1)S(1)}, u32[]{:S(2)}, u32[]{:S(2)}) %collective-permute-start.12) | collective-permute-done | bytes 405536 | tf_op jit(solution)/shard_map/ppermute | solution.py:57
  35.1 1.4 %shard_map.70.refs_4_ = f32[768,384]{1,0:T(8,128)S(1)} custom-call(bf16[384,2048]{1,0:T(8,128)(2,1)S(1)} %get-tuple-element.53.refs_0_, bf16[384,2048]{1,0:T(8,128)(2,1)S(1)} %collective-permute-done.10.refs_1_, bf16[256,768]{1,0:T(8,128)(2,1)S(1)} %shard_map.65.own.refs_2_.refs_0_, bf16[256,768]{1,0:T(8,128)(2,1)S(1)} %collective-permute-done.8.near.refs_3_.refs_1_, ...), custom_call_target="tpu_custom_call" | custom-call | flops 905969664 | tf_op jit(solution)/shard_map/pallas_call | solution.py:379
  36.5 2.8 %collective-permute-done.13.refs_1_ = bf16[128,1024]{1,0:T(8,128)(2,1)S(1)} collective-permute-done((bf16[128,1024]{1,0:T(8,128)(2,1)S(1)}, bf16[128,1024]{1,0:T(8,128)(2,1)S(1)}, u32[]{:S(2)}, u32[]{:S(2)}) %collective-permute-start.13) | collective-permute-done | bytes 262176 | tf_op jit(solution)/shard_map/ppermute | solution.py:57
  40.7 1.6 %collective-permute-start.14 = (bf16[80,2048]{1,0:T(8,128)(2,1)S(1)}, bf16[80,2048]{1,0:T(8,128)(2,1)S(1)}, u32[]{:S(2)}, u32[]{:S(2)}) collective-permute-start(bf16[80,2048]{1,0:T(8,128)(2,1)S(1)} %get-tuple-element.62), channel_id=1, source_target_pairs={{0,4},{1,5},{2,6},{3,7},{4,0},{5,1},{6,2},{7,3},{8,12},{9,13},{10,... | collective-permute-start | bytes 983048 | tf_op jit(solution)/shard_map/ppermute | solution.py:57
  42.4 1.5 %collective-permute-done.15.bottom = bf16[48,2048]{1,0:T(8,128)(2,1)S(1)} collective-permute-done((bf16[48,2048]{1,0:T(8,128)(2,1)S(1)}, bf16[48,2048]{1,0:T(8,128)(2,1)S(1)}, u32[]{:S(2)}, u32[]{:S(2)}) %collective-permute-start.15) | collective-permute-done | bytes 196640 | tf_op jit(solution)/shard_map/ppermute | solution.py:57
  45.2 2.6 %collective-permute-start.18 = (bf16[4,256,128]{2,1,0:T(8,128)(2,1)S(1)}, bf16[4,256,128]{2,1,0:T(8,128)(2,1)S(1)}, u32[]{:S(2)}, u32[]{:S(2)}) collective-permute-start(bf16[4,256,128]{2,1,0:T(8,128)(2,1)S(1)} %shard_map.74.own), channel_id=1, source_target_pairs={{8,16},{9,17},{10,18},{11,19},{12,20},{13,21},{14,22},{15,23},{16,... | collective-permute-start | bytes 786440 | tf_op jit(solution)/shard_map/ppermute | solution.py:57
  48.5 2.7 %collective-permute-start.22 = (bf16[2,256,128]{2,1,0:T(8,128)(2,1)S(1)}, bf16[2,256,128]{2,1,0:T(8,128)(2,1)S(1)}, u32[]{:S(2)}, u32[]{:S(2)}) collective-permute-start(bf16[2,256,128]{2,1,0:T(8,128)(2,1)S(1)} %get-tuple-element.68.own), channel_id=1, source_target_pairs={{8,16},{9,17},{10,18},{11,19},{12,20},{13,21},{14,22},{15,23},{16,... | collective-permute-start | bytes 393224 | tf_op jit(solution)/shard_map/ppermute | solution.py:57
  51.3 1.2 %collective-permute-done.17.outer = bf16[4,256,128]{2,1,0:T(8,128)(2,1)S(1)} collective-permute-done((bf16[4,256,128]{2,1,0:T(8,128)(2,1)S(1)}, bf16[4,256,128]{2,1,0:T(8,128)(2,1)S(1)}, u32[]{:S(2)}, u32[]{:S(2)}) %collective-permute-start.17) | collective-permute-done | bytes 262176 | tf_op jit(solution)/shard_map/ppermute | solution.py:57
  52.5 1.9 %collective-permute-start.20 = (bf16[2,256,128]{2,1,0:T(8,128)(2,1)S(1)}, bf16[2,256,128]{2,1,0:T(8,128)(2,1)S(1)}, u32[]{:S(2)}, u32[]{:S(2)}) collective-permute-start(bf16[2,256,128]{2,1,0:T(8,128)(2,1)S(1)} %get-tuple-element.67.own), channel_id=1, source_target_pairs={{8,16},{9,17},{10,18},{11,19},{12,20},{13,21},{14,22},{15,23},{16,... | collective-permute-start | bytes 393224 | tf_op jit(solution)/shard_map/ppermute | solution.py:57
  54.4 1.2 %shard_map.75.weights = bf16[4,256,640]{2,1,0:T(8,128)(2,1)S(1)} custom-call(bf16[4,256,128]{2,1,0:T(8,128)(2,1)S(1)} %get-tuple-element.66.q_ref, bf16[4,256,128]{2,1,0:T(8,128)(2,1)S(1)} %collective-permute-done.17.outer, bf16[4,256,128]{2,1,0:T(8,128)(2,1)S(1)} %shard_map.74.own, bf16[4,256,128]{2,1,0:T(8,128)(2,1)S(1)} %collective-permute-done.18.middle, ...), custom_call_target="tpu_custom_call" | custom-call | flops 167772160 | tf_op jit(solution)/shard_map/pallas_call | solution.py:396
  55.6 1.4 %collective-permute-done.22.middle = bf16[2,256,128]{2,1,0:T(8,128)(2,1)S(1)} collective-permute-done((bf16[2,256,128]{2,1,0:T(8,128)(2,1)S(1)}, bf16[2,256,128]{2,1,0:T(8,128)(2,1)S(1)}, u32[]{:S(2)}, u32[]{:S(2)}) %collective-permute-start.22) | collective-permute-done | bytes 131104 | tf_op jit(solution)/shard_map/ppermute | solution.py:57
  57.3 1.7 %collective-permute-start.25 = (bf16[256,128]{1,0:T(8,128)(2,1)S(1)}, bf16[256,128]{1,0:T(8,128)(2,1)S(1)}, u32[]{:S(2)}, u32[]{:S(2)}) collective-permute-start(bf16[256,128]{1,0:T(8,128)(2,1)S(1)} %shard_map.79), channel_id=1, source_target_pairs={{0,3},{1,2},{2,1},{3,0},{4,7},{5,6},{6,5},{7,4},{8,11},{9,10},{10,... | collective-permute-start | bytes 196616 | tf_op jit(solution)/shard_map/ppermute | solution.py:57
  60.6 1.9 %collective-permute-start.23 = (bf16[256,128]{1,0:T(8,128)(2,1)S(1)}, bf16[256,128]{1,0:T(8,128)(2,1)S(1)}, u32[]{:S(2)}, u32[]{:S(2)}) collective-permute-start(bf16[256,128]{1,0:T(8,128)(2,1)S(1)} %shard_map.77), channel_id=1, source_target_pairs={{0,1},{1,0},{2,3},{3,2},{4,5},{5,4},{6,7},{7,6},{8,9},{9,8},{10,11... | collective-permute-start | bytes 196616 | tf_op jit(solution)/shard_map/ppermute | solution.py:57
  62.7 2.3 %collective-permute-done.23.refs_1_ = bf16[256,128]{1,0:T(8,128)(2,1)S(1)} collective-permute-done((bf16[256,128]{1,0:T(8,128)(2,1)S(1)}, bf16[256,128]{1,0:T(8,128)(2,1)S(1)}, u32[]{:S(2)}, u32[]{:S(2)}) %collective-permute-start.23) | collective-permute-done | bytes 65568 | tf_op jit(solution)/shard_map/ppermute | solution.py:57
  65.0 2.3 %collective-permute-start.26 = (bf16[4,128,128]{2,1,0:T(8,128)(2,1)S(1)}, bf16[4,128,128]{2,1,0:T(8,128)(2,1)S(1)}, u32[]{:S(2)}, u32[]{:S(2)}) collective-permute-start(bf16[4,128,128]{2,1,0:T(8,128)(2,1)S(1)} %get-tuple-element.70), channel_id=1, source_target_pairs={{0,4},{1,5},{2,6},{3,7},{4,0},{5,1},{6,2},{7,3},{8,12},{9,13},{10,... | collective-permute-start | bytes 393224 | tf_op jit(solution)/shard_map/ppermute | solution.py:57
  (63 shorter events, 18.7 us)
Async XLA Ops:
  0.0 19.8 %collective-permute-start = (bf16[256,768]{1,0:T(8,128)(2,1)}, bf16[256,768]{1,0:T(8,128)(2,1)}, u32[]{:S(2)}, u32[]{:S(2)}) collective-permute-start(bf16[256,768]{1,0:T(8,128)(2,1)} %w.1), channel_id=1, source_target_pairs={{0,16},{1,17},{2,18},{3,19},{4,20},{5,21},{6,22},{7,23},{8,24},{9,... | collective-permute-start | bytes 1179656 | tf_op jit(solution)/shard_map/ppermute | solution.py:57
  4.8 5.1 %collective-permute-start.1 = (bf16[336,256]{1,0:T(8,128)(2,1)S(1)}, bf16[336,256]{1,0:T(8,128)(2,1)S(1)}, u32[]{:S(2)}, u32[]{:S(2)}) collective-permute-start(bf16[336,256]{1,0:T(8,128)(2,1)S(1)} %get-tuple-element.39), channel_id=1, source_target_pairs={{0,1},{1,0},{2,3},{3,2},{4,5},{5,4},{6,7},{7,6},{8,9},{9,8},{10,11... | collective-permute-start | bytes 516104 | tf_op jit(solution)/shard_map/ppermute | solution.py:57
  6.1 4.7 %collective-permute-start.2 = (bf16[336,256]{1,0:T(8,128)(2,1)S(1)}, bf16[336,256]{1,0:T(8,128)(2,1)S(1)}, u32[]{:S(2)}, u32[]{:S(2)}) collective-permute-start(bf16[336,256]{1,0:T(8,128)(2,1)S(1)} %get-tuple-element.40), channel_id=1, source_target_pairs={{0,2},{1,3},{2,0},{3,1},{4,6},{5,7},{6,4},{7,5},{8,10},{9,11},{10,... | collective-permute-start | bytes 516104 | tf_op jit(solution)/shard_map/ppermute | solution.py:57
  7.3 16.7 %collective-permute-start.7 = (bf16[128,2048]{1,0:T(8,128)(2,1)}, bf16[128,2048]{1,0:T(8,128)(2,1)}, u32[]{:S(2)}, u32[]{:S(2)}) collective-permute-start(bf16[128,2048]{1,0:T(8,128)(2,1)} %bitcast.12), channel_id=1, source_target_pairs={{0,2},{1,3},{2,0},{3,1},{4,6},{5,7},{6,4},{7,5},{8,10},{9,11},{10,... | collective-permute-start | bytes 1572872 | tf_op jit(solution)/shard_map/ppermute | solution.py:57
  7.5 16.5 %collective-permute-start.6 = (bf16[128,2048]{1,0:T(8,128)(2,1)}, bf16[128,2048]{1,0:T(8,128)(2,1)}, u32[]{:S(2)}, u32[]{:S(2)}) collective-permute-start(bf16[128,2048]{1,0:T(8,128)(2,1)} %bitcast.13), channel_id=1, source_target_pairs={{0,1},{1,0},{2,3},{3,2},{4,5},{5,4},{6,7},{7,6},{8,9},{9,8},{10,11... | collective-permute-start | bytes 1572872 | tf_op jit(solution)/shard_map/ppermute | solution.py:57
  10.9 16.0 %collective-permute-start.8 = (bf16[256,768]{1,0:T(8,128)(2,1)S(1)}, bf16[256,768]{1,0:T(8,128)(2,1)S(1)}, u32[]{:S(2)}, u32[]{:S(2)}) collective-permute-start(bf16[256,768]{1,0:T(8,128)(2,1)S(1)} %shard_map.65.own.refs_2_.refs_0_), channel_id=1, source_target_pairs={{0,8},{1,9},{2,10},{3,11},{4,12},{5,13},{6,14},{7,15},{8,0},{9,1},... | collective-permute-start | bytes 1179656 | tf_op jit(solution)/shard_map/ppermute | solution.py:57
  11.2 11.4 %collective-permute-start.5 = (bf16[80,256]{1,0:T(8,128)(2,1)S(1)}, bf16[80,256]{1,0:T(8,128)(2,1)S(1)}, u32[]{:S(2)}, u32[]{:S(2)}) collective-permute-start(bf16[80,256]{1,0:T(8,128)(2,1)S(1)} %get-tuple-element.42), channel_id=1, source_target_pairs={{0,3},{1,2},{2,1},{3,0},{4,7},{5,6},{6,5},{7,4},{8,11},{9,10},{10,... | collective-permute-start | bytes 122888 | tf_op jit(solution)/shard_map/ppermute | solution.py:57
  20.9 5.5 %collective-permute-start.3 = (bf16[256,256]{1,0:T(8,128)(2,1)S(1)}, bf16[256,256]{1,0:T(8,128)(2,1)S(1)}, u32[]{:S(2)}, u32[]{:S(2)}) collective-permute-start(bf16[256,256]{1,0:T(8,128)(2,1)S(1)} %get-tuple-element.72), channel_id=1, source_target_pairs={{0,1},{1,0},{2,3},{3,2},{4,5},{5,4},{6,7},{7,6},{8,9},{9,8},{10,11... | collective-permute-start | bytes 393224 | tf_op jit(solution)/shard_map/ppermute | solution.py:57
  22.5 4.0 %collective-permute-start.4 = (bf16[256,256]{1,0:T(8,128)(2,1)S(1)}, bf16[256,256]{1,0:T(8,128)(2,1)S(1)}, u32[]{:S(2)}, u32[]{:S(2)}) collective-permute-start(bf16[256,256]{1,0:T(8,128)(2,1)S(1)} %get-tuple-element.71), channel_id=1, source_target_pairs={{0,2},{1,3},{2,0},{3,1},{4,6},{5,7},{6,4},{7,5},{8,10},{9,11},{10,... | collective-permute-start | bytes 393224 | tf_op jit(solution)/shard_map/ppermute | solution.py:57
  27.0 4.0 %collective-permute-start.9 = (bf16[256,384]{1,0:T(8,128)(2,1)S(1)}, bf16[256,384]{1,0:T(8,128)(2,1)S(1)}, u32[]{:S(2)}, u32[]{:S(2)}) collective-permute-start(bf16[256,384]{1,0:T(8,128)(2,1)S(1)} %get-tuple-element.50), channel_id=1, source_target_pairs={{0,4},{1,5},{2,6},{3,7},{4,0},{5,1},{6,2},{7,3},{8,12},{9,13},{10,... | collective-permute-start | bytes 589832 | tf_op jit(solution)/shard_map/ppermute | solution.py:57
  31.1 4.1 %collective-permute-start.10 = (bf16[384,2048]{1,0:T(8,128)(2,1)S(1)}, bf16[384,2048]{1,0:T(8,128)(2,1)S(1)}, u32[]{:S(2)}, u32[]{:S(2)}) collective-permute-start(bf16[384,2048]{1,0:T(8,128)(2,1)S(1)} %get-tuple-element.53.refs_0_), channel_id=1, source_target_pairs={{0,4},{1,5},{2,6},{3,7},{4,0},{5,1},{6,2},{7,3},{8,12},{9,13},{10,... | collective-permute-start | bytes 4718600 | tf_op jit(solution)/shard_map/ppermute | solution.py:57
  31.6 3.6 %collective-permute-start.12 = (bf16[528,384]{1,0:T(8,128)(2,1)S(1)}, bf16[528,384]{1,0:T(8,128)(2,1)S(1)}, u32[]{:S(2)}, u32[]{:S(2)}) collective-permute-start(bf16[528,384]{1,0:T(8,128)(2,1)S(1)} %shard_map.69), channel_id=1, source_target_pairs={{0,4},{1,5},{2,6},{3,7},{4,0},{5,1},{6,2},{7,3},{8,12},{9,13},{10,... | collective-permute-start | bytes 1216520 | tf_op jit(solution)/shard_map/ppermute | solution.py:57
  31.8 7.5 %collective-permute-start.13 = (bf16[128,1024]{1,0:T(8,128)(2,1)S(1)}, bf16[128,1024]{1,0:T(8,128)(2,1)S(1)}, u32[]{:S(2)}, u32[]{:S(2)}) collective-permute-start(bf16[128,1024]{1,0:T(8,128)(2,1)S(1)} %get-tuple-element.59), channel_id=1, source_target_pairs={{0,1},{1,0},{2,3},{3,2},{4,5},{5,4},{6,7},{7,6},{8,9},{9,8},{10,11... | collective-permute-start | bytes 786440 | tf_op jit(solution)/shard_map/ppermute | solution.py:57
  32.9 7.2 %collective-permute-start.11 = (bf16[128,1024]{1,0:T(8,128)(2,1)S(1)}, bf16[128,1024]{1,0:T(8,128)(2,1)S(1)}, u32[]{:S(2)}, u32[]{:S(2)}) collective-permute-start(bf16[128,1024]{1,0:T(8,128)(2,1)S(1)} %get-tuple-element.54), channel_id=1, source_target_pairs={{0,2},{1,3},{2,0},{3,1},{4,6},{5,7},{6,4},{7,5},{8,10},{9,11},{10,... | collective-permute-start | bytes 786440 | tf_op jit(solution)/shard_map/ppermute | solution.py:57
  33.2 11.3 %collective-permute-start.16 = (bf16[512,384]{1,0:T(8,128)(2,1)S(1)}, bf16[512,384]{1,0:T(8,128)(2,1)S(1)}, u32[]{:S(2)}, u32[]{:S(2)}) collective-permute-start(bf16[512,384]{1,0:T(8,128)(2,1)S(1)} %constant_dynamic-update-slice_fusion.refs_5_.refs_3_), channel_id=1, source_target_pairs={{0,8},{1,9},{2,10},{3,11},{4,12},{5,13},{6,14},{7,15},{8,0},{9,1},... | collective-permute-start | bytes 1179656 | tf_op jit(solution)/shard_map/ppermute | solution.py:57
  44.9 7.6 %collective-permute-start.17 = (bf16[4,256,128]{2,1,0:T(8,128)(2,1)S(1)}, bf16[4,256,128]{2,1,0:T(8,128)(2,1)S(1)}, u32[]{:S(2)}, u32[]{:S(2)}) collective-permute-start(bf16[4,256,128]{2,1,0:T(8,128)(2,1)S(1)} %shard_map.74.own), channel_id=1, source_target_pairs={{0,8},{1,9},{2,10},{3,11},{4,12},{5,13},{6,14},{7,15},{8,0},{9,1},... | collective-permute-start | bytes 786440 | tf_op jit(solution)/shard_map/ppermute | solution.py:57
  45.2 9.3 %collective-permute-start.18 = (bf16[4,256,128]{2,1,0:T(8,128)(2,1)S(1)}, bf16[4,256,128]{2,1,0:T(8,128)(2,1)S(1)}, u32[]{:S(2)}, u32[]{:S(2)}) collective-permute-start(bf16[4,256,128]{2,1,0:T(8,128)(2,1)S(1)} %shard_map.74.own), channel_id=1, source_target_pairs={{8,16},{9,17},{10,18},{11,19},{12,20},{13,21},{14,22},{15,23},{16,... | collective-permute-start | bytes 786440 | tf_op jit(solution)/shard_map/ppermute | solution.py:57
  48.4 7.2 %collective-permute-start.21 = (bf16[2,256,128]{2,1,0:T(8,128)(2,1)S(1)}, bf16[2,256,128]{2,1,0:T(8,128)(2,1)S(1)}, u32[]{:S(2)}, u32[]{:S(2)}) collective-permute-start(bf16[2,256,128]{2,1,0:T(8,128)(2,1)S(1)} %get-tuple-element.68.own), channel_id=1, source_target_pairs={{0,8},{1,9},{2,10},{3,11},{4,12},{5,13},{6,14},{7,15},{8,0},{9,1},... | collective-permute-start | bytes 393224 | tf_op jit(solution)/shard_map/ppermute | solution.py:57
  48.5 8.5 %collective-permute-start.22 = (bf16[2,256,128]{2,1,0:T(8,128)(2,1)S(1)}, bf16[2,256,128]{2,1,0:T(8,128)(2,1)S(1)}, u32[]{:S(2)}, u32[]{:S(2)}) collective-permute-start(bf16[2,256,128]{2,1,0:T(8,128)(2,1)S(1)} %get-tuple-element.68.own), channel_id=1, source_target_pairs={{8,16},{9,17},{10,18},{11,19},{12,20},{13,21},{14,22},{15,23},{16,... | collective-permute-start | bytes 393224 | tf_op jit(solution)/shard_map/ppermute | solution.py:57
  51.2 7.8 %collective-permute-start.19 = (bf16[2,256,128]{2,1,0:T(8,128)(2,1)S(1)}, bf16[2,256,128]{2,1,0:T(8,128)(2,1)S(1)}, u32[]{:S(2)}, u32[]{:S(2)}) collective-permute-start(bf16[2,256,128]{2,1,0:T(8,128)(2,1)S(1)} %get-tuple-element.67.own), channel_id=1, source_target_pairs={{0,8},{1,9},{2,10},{3,11},{4,12},{5,13},{6,14},{7,15},{8,0},{9,1},... | collective-permute-start | bytes 393224 | tf_op jit(solution)/shard_map/ppermute | solution.py:57
  52.5 6.8 %collective-permute-start.20 = (bf16[2,256,128]{2,1,0:T(8,128)(2,1)S(1)}, bf16[2,256,128]{2,1,0:T(8,128)(2,1)S(1)}, u32[]{:S(2)}, u32[]{:S(2)}) collective-permute-start(bf16[2,256,128]{2,1,0:T(8,128)(2,1)S(1)} %get-tuple-element.67.own), channel_id=1, source_target_pairs={{8,16},{9,17},{10,18},{11,19},{12,20},{13,21},{14,22},{15,23},{16,... | collective-permute-start | bytes 393224 | tf_op jit(solution)/shard_map/ppermute | solution.py:57
  57.3 5.4 %collective-permute-start.25 = (bf16[256,128]{1,0:T(8,128)(2,1)S(1)}, bf16[256,128]{1,0:T(8,128)(2,1)S(1)}, u32[]{:S(2)}, u32[]{:S(2)}) collective-permute-start(bf16[256,128]{1,0:T(8,128)(2,1)S(1)} %shard_map.79), channel_id=1, source_target_pairs={{0,3},{1,2},{2,1},{3,0},{4,7},{5,6},{6,5},{7,4},{8,11},{9,10},{10,... | collective-permute-start | bytes 196616 | tf_op jit(solution)/shard_map/ppermute | solution.py:57
  60.6 4.4 %collective-permute-start.23 = (bf16[256,128]{1,0:T(8,128)(2,1)S(1)}, bf16[256,128]{1,0:T(8,128)(2,1)S(1)}, u32[]{:S(2)}, u32[]{:S(2)}) collective-permute-start(bf16[256,128]{1,0:T(8,128)(2,1)S(1)} %shard_map.77), channel_id=1, source_target_pairs={{0,1},{1,0},{2,3},{3,2},{4,5},{5,4},{6,7},{7,6},{8,9},{9,8},{10,11... | collective-permute-start | bytes 196616 | tf_op jit(solution)/shard_map/ppermute | solution.py:57
  65.0 3.3 %collective-permute-start.26 = (bf16[4,128,128]{2,1,0:T(8,128)(2,1)S(1)}, bf16[4,128,128]{2,1,0:T(8,128)(2,1)S(1)}, u32[]{:S(2)}, u32[]{:S(2)}) collective-permute-start(bf16[4,128,128]{2,1,0:T(8,128)(2,1)S(1)} %get-tuple-element.70), channel_id=1, source_target_pairs={{0,4},{1,5},{2,6},{3,7},{4,0},{5,1},{6,2},{7,3},{8,12},{9,13},{10,... | collective-permute-start | bytes 393224 | tf_op jit(solution)/shard_map/ppermute | solution.py:57
  (7 other events, 74.3 us)

commit v25 on v24

--- a/solution.py
+++ b/solution.py
@@ -353,13 +353,13 @@
 
     tied = after(stream, to[0])
     beside, above = swap_depth(tied, 1), swap_depth(tied, 2)
-    (normed,) = embed((0,), stream)
 
     even = (lax.axis_index("depth") & 1) == 0
     low, to_x, high = (far_raw[:, k * PAIR : (k + 1) * PAIR] for k in range(3))
     kept, to_y = jnp.where(even, low, high), jnp.where(even, high, low)
     from_x, from_y = swap_depth(to_x, 1), swap_depth(to_y, 2)
     beside, above = after(beside, to_x), after(above, to_y)
+    (normed,) = embed((0,), after(stream, to_x))
     stack, *diagonal = embed((1, 2), beside, above, finished=(normed,))
     from_x, from_y, stack, near = lax.optimization_barrier((from_x, from_y, stack, near))
     keep, send, flags = call(

time: 69.7 us -> 69.7 us (level)
  no operation moved by 1% of the time
where the time goes in v25:
time: 69.7 us; the launch traced here: 69 us
  starting transfers between devices  29.9 us (43%)
  waiting for transfers between devices  25.4 us (36%)
  Pallas kernels  9.98 us (14%)
  other arithmetic  2.48 us (4%)
  local copies, waits for them, and re-layouts  1.07 us (2%)
    ppermute x27, starting transfers between devices, hop(): return lax.ppermute(value, ('tm', 'depth'), pairs)  29.9 us
    ppermute x27, waiting for transfers between devices, hop(): return lax.ppermute(value, ('tm', 'depth'), pairs)  25.4 us
    pallas_call x3, Pallas kernels, embed(): call(functools.partial(embed_kernel, rs, len(finished)), out, 'v' * (6 +...  3.56 us
  transfers between devices with their start and end apart: 27, of which 16 were waited for; matrix products, arithmetic and copies ran while one was open for 4% of the time, Pallas kernels for 13%

profile of v25, /device:TPU:9, one launch (start us, length us, event | category | flops | bytes accessed | tf_op | source)
XLA Modules:
  0.0 69.0 jit_solution(6626168439112595566)
XLA Ops:
  0.0 2.3 %collective-permute-start = (bf16[256,768]{1,0:T(8,128)(2,1)}, bf16[256,768]{1,0:T(8,128)(2,1)}, u32[]{:S(2)}, u32[]{:S(2)}) collective-permute-start(bf16[256,768]{1,0:T(8,128)(2,1)} %w.1), channel_id=1, source_target_pairs={{0,16},{1,17},{2,18},{3,19},{4,20},{5,21},{6,22},{7,23},{8,24},{9,... | collective-permute-start | bytes 1179656 | tf_op jit(solution)/shard_map/ppermute | solution.py:57
  4.8 1.3 %collective-permute-start.1 = (bf16[336,256]{1,0:T(8,128)(2,1)S(1)}, bf16[336,256]{1,0:T(8,128)(2,1)S(1)}, u32[]{:S(2)}, u32[]{:S(2)}) collective-permute-start(bf16[336,256]{1,0:T(8,128)(2,1)S(1)} %get-tuple-element.40), channel_id=1, source_target_pairs={{0,1},{1,0},{2,3},{3,2},{4,5},{5,4},{6,7},{7,6},{8,9},{9,8},{10,11... | collective-permute-start | bytes 516104 | tf_op jit(solution)/shard_map/ppermute | solution.py:57
  6.1 1.2 %collective-permute-start.2 = (bf16[336,256]{1,0:T(8,128)(2,1)S(1)}, bf16[336,256]{1,0:T(8,128)(2,1)S(1)}, u32[]{:S(2)}, u32[]{:S(2)}) collective-permute-start(bf16[336,256]{1,0:T(8,128)(2,1)S(1)} %get-tuple-element.41), channel_id=1, source_target_pairs={{0,2},{1,3},{2,0},{3,1},{4,6},{5,7},{6,4},{7,5},{8,10},{9,11},{10,... | collective-permute-start | bytes 516104 | tf_op jit(solution)/shard_map/ppermute | solution.py:57
  7.8 2.1 %collective-permute-done.1.from_x.plane_x = bf16[336,256]{1,0:T(8,128)(2,1)S(1)} collective-permute-done((bf16[336,256]{1,0:T(8,128)(2,1)S(1)}, bf16[336,256]{1,0:T(8,128)(2,1)S(1)}, u32[]{:S(2)}, u32[]{:S(2)}) %collective-permute-start.1) | collective-permute-done | bytes 172064 | tf_op jit(solution)/shard_map/ppermute | solution.py:57
  11.2 1.2 %collective-permute-start.5 = (bf16[80,256]{1,0:T(8,128)(2,1)S(1)}, bf16[80,256]{1,0:T(8,128)(2,1)S(1)}, u32[]{:S(2)}, u32[]{:S(2)}) collective-permute-start(bf16[80,256]{1,0:T(8,128)(2,1)S(1)} %get-tuple-element.43), channel_id=1, source_target_pairs={{0,3},{1,2},{2,1},{3,0},{4,7},{5,6},{6,5},{7,4},{8,11},{9,10},{10,... | collective-permute-start | bytes 122888 | tf_op jit(solution)/shard_map/ppermute | solution.py:57
  12.3 7.5 %collective-permute-done = bf16[256,768]{1,0:T(8,128)(2,1)} collective-permute-done((bf16[256,768]{1,0:T(8,128)(2,1)}, bf16[256,768]{1,0:T(8,128)(2,1)}, u32[]{:S(2)}, u32[]{:S(2)}) %collective-permute-start) | collective-permute-done | bytes 393248 | tf_op jit(solution)/shard_map/ppermute | solution.py:57
  20.9 1.3 %collective-permute-start.3 = (bf16[256,256]{1,0:T(8,128)(2,1)S(1)}, bf16[256,256]{1,0:T(8,128)(2,1)S(1)}, u32[]{:S(2)}, u32[]{:S(2)}) collective-permute-start(bf16[256,256]{1,0:T(8,128)(2,1)S(1)} %get-tuple-element.74), channel_id=1, source_target_pairs={{0,1},{1,0},{2,3},{3,2},{4,5},{5,4},{6,7},{7,6},{8,9},{9,8},{10,11... | collective-permute-start | bytes 393224 | tf_op jit(solution)/shard_map/ppermute | solution.py:57
  24.1 2.3 %shard_map.67 = (bf16[384,2048]{1,0:T(8,128)(2,1)S(1)}, bf16[128,1024]{1,0:T(8,128)(2,1)S(1)}, bf16[128,1024]{1,0:T(8,128)(2,1)S(1)}) custom-call(bf16[144,128]{1,0:T(8,128)(2,1)S(1)} %pad_maximum_fusion.raw, bf16[336,256]{1,0:T(8,128)(2,1)S(1)} %collective-permute-done.1.from_x.plane_x, bf16[336,256]{1,0:T(8,128)(2,1)S(1)} %collective-permute-done.2.from_y.plane_y, ...), custom_call_target="tpu_custom_call" | custom-call | flops 402653184 | tf_op jit(solution)/shard_map/pallas_call | solution.py:346
  27.0 2.9 %collective-permute-start.9 = (bf16[256,384]{1,0:T(8,128)(2,1)S(1)}, bf16[256,384]{1,0:T(8,128)(2,1)S(1)}, u32[]{:S(2)}, u32[]{:S(2)}) collective-permute-start(bf16[256,384]{1,0:T(8,128)(2,1)S(1)} %get-tuple-element.52), channel_id=1, source_target_pairs={{0,4},{1,5},{2,6},{3,7},{4,0},{5,1},{6,2},{7,3},{8,12},{9,13},{10,... | collective-permute-start | bytes 589832 | tf_op jit(solution)/shard_map/ppermute | solution.py:57
  33.4 1.7 %collective-permute-done.12.refs_4_.refs_2_.received = bf16[528,384]{1,0:T(8,128)(2,1)S(1)} collective-permute-done((bf16[528,384]{1,0:T(8,128)(2,1)S(1)}, bf16[528,384]{1,0:T(8,128)(2,1)S(1)}, u32[]{:S(2)}, u32[]{:S(2)}) %collective-permute-start.12) | collective-permute-done | bytes 405536 | tf_op jit(solution)/shard_map/ppermute | solution.py:57
  35.1 1.4 %shard_map.70.refs_4_ = f32[768,384]{1,0:T(8,128)S(1)} custom-call(bf16[384,2048]{1,0:T(8,128)(2,1)S(1)} %get-tuple-element.55.refs_0_, bf16[384,2048]{1,0:T(8,128)(2,1)S(1)} %collective-permute-done.10.refs_1_, bf16[256,768]{1,0:T(8,128)(2,1)S(1)} %shard_map.65.own.refs_2_.refs_0_, bf16[256,768]{1,0:T(8,128)(2,1)S(1)} %collective-permute-done.8.near.refs_3_.refs_1_, ...), custom_call_target="tpu_custom_call" | custom-call | flops 905969664 | tf_op jit(solution)/shard_map/pallas_call | solution.py:379
  36.5 2.8 %collective-permute-done.13.refs_1_ = bf16[128,1024]{1,0:T(8,128)(2,1)S(1)} collective-permute-done((bf16[128,1024]{1,0:T(8,128)(2,1)S(1)}, bf16[128,1024]{1,0:T(8,128)(2,1)S(1)}, u32[]{:S(2)}, u32[]{:S(2)}) %collective-permute-start.13) | collective-permute-done | bytes 262176 | tf_op jit(solution)/shard_map/ppermute | solution.py:57
  40.7 1.6 %collective-permute-start.14 = (bf16[80,2048]{1,0:T(8,128)(2,1)S(1)}, bf16[80,2048]{1,0:T(8,128)(2,1)S(1)}, u32[]{:S(2)}, u32[]{:S(2)}) collective-permute-start(bf16[80,2048]{1,0:T(8,128)(2,1)S(1)} %get-tuple-element.64), channel_id=1, source_target_pairs={{0,4},{1,5},{2,6},{3,7},{4,0},{5,1},{6,2},{7,3},{8,12},{9,13},{10,... | collective-permute-start | bytes 983048 | tf_op jit(solution)/shard_map/ppermute | solution.py:57
  42.4 1.5 %collective-permute-done.15.bottom = bf16[48,2048]{1,0:T(8,128)(2,1)S(1)} collective-permute-done((bf16[48,2048]{1,0:T(8,128)(2,1)S(1)}, bf16[48,2048]{1,0:T(8,128)(2,1)S(1)}, u32[]{:S(2)}, u32[]{:S(2)}) %collective-permute-start.15) | collective-permute-done | bytes 196640 | tf_op jit(solution)/shard_map/ppermute | solution.py:57
  45.2 2.6 %collective-permute-start.18 = (bf16[4,256,128]{2,1,0:T(8,128)(2,1)S(1)}, bf16[4,256,128]{2,1,0:T(8,128)(2,1)S(1)}, u32[]{:S(2)}, u32[]{:S(2)}) collective-permute-start(bf16[4,256,128]{2,1,0:T(8,128)(2,1)S(1)} %shard_map.74.own), channel_id=1, source_target_pairs={{8,16},{9,17},{10,18},{11,19},{12,20},{13,21},{14,22},{15,23},{16,... | collective-permute-start | bytes 786440 | tf_op jit(solution)/shard_map/ppermute | solution.py:57
  48.5 2.7 %collective-permute-start.22 = (bf16[2,256,128]{2,1,0:T(8,128)(2,1)S(1)}, bf16[2,256,128]{2,1,0:T(8,128)(2,1)S(1)}, u32[]{:S(2)}, u32[]{:S(2)}) collective-permute-start(bf16[2,256,128]{2,1,0:T(8,128)(2,1)S(1)} %get-tuple-element.70.own), channel_id=1, source_target_pairs={{8,16},{9,17},{10,18},{11,19},{12,20},{13,21},{14,22},{15,23},{16,... | collective-permute-start | bytes 393224 | tf_op jit(solution)/shard_map/ppermute | solution.py:57
  51.3 1.2 %collective-permute-done.17.outer = bf16[4,256,128]{2,1,0:T(8,128)(2,1)S(1)} collective-permute-done((bf16[4,256,128]{2,1,0:T(8,128)(2,1)S(1)}, bf16[4,256,128]{2,1,0:T(8,128)(2,1)S(1)}, u32[]{:S(2)}, u32[]{:S(2)}) %collective-permute-start.17) | collective-permute-done | bytes 262176 | tf_op jit(solution)/shard_map/ppermute | solution.py:57
  52.5 1.9 %collective-permute-start.20 = (bf16[2,256,128]{2,1,0:T(8,128)(2,1)S(1)}, bf16[2,256,128]{2,1,0:T(8,128)(2,1)S(1)}, u32[]{:S(2)}, u32[]{:S(2)}) collective-permute-start(bf16[2,256,128]{2,1,0:T(8,128)(2,1)S(1)} %get-tuple-element.69.own), channel_id=1, source_target_pairs={{8,16},{9,17},{10,18},{11,19},{12,20},{13,21},{14,22},{15,23},{16,... | collective-permute-start | bytes 393224 | tf_op jit(solution)/shard_map/ppermute | solution.py:57
  54.4 1.2 %shard_map.75.weights = bf16[4,256,640]{2,1,0:T(8,128)(2,1)S(1)} custom-call(bf16[4,256,128]{2,1,0:T(8,128)(2,1)S(1)} %get-tuple-element.68.q_ref, bf16[4,256,128]{2,1,0:T(8,128)(2,1)S(1)} %collective-permute-done.17.outer, bf16[4,256,128]{2,1,0:T(8,128)(2,1)S(1)} %shard_map.74.own, bf16[4,256,128]{2,1,0:T(8,128)(2,1)S(1)} %collective-permute-done.18.middle, ...), custom_call_target="tpu_custom_call" | custom-call | flops 167772160 | tf_op jit(solution)/shard_map/pallas_call | solution.py:396
  55.6 1.4 %collective-permute-done.22.middle = bf16[2,256,128]{2,1,0:T(8,128)(2,1)S(1)} collective-permute-done((bf16[2,256,128]{2,1,0:T(8,128)(2,1)S(1)}, bf16[2,256,128]{2,1,0:T(8,128)(2,1)S(1)}, u32[]{:S(2)}, u32[]{:S(2)}) %collective-permute-start.22) | collective-permute-done | bytes 131104 | tf_op jit(solution)/shard_map/ppermute | solution.py:57
  57.3 1.7 %collective-permute-start.25 = (bf16[256,128]{1,0:T(8,128)(2,1)S(1)}, bf16[256,128]{1,0:T(8,128)(2,1)S(1)}, u32[]{:S(2)}, u32[]{:S(2)}) collective-permute-start(bf16[256,128]{1,0:T(8,128)(2,1)S(1)} %shard_map.79), channel_id=1, source_target_pairs={{0,3},{1,2},{2,1},{3,0},{4,7},{5,6},{6,5},{7,4},{8,11},{9,10},{10,... | collective-permute-start | bytes 196616 | tf_op jit(solution)/shard_map/ppermute | solution.py:57
  60.6 1.9 %collective-permute-start.23 = (bf16[256,128]{1,0:T(8,128)(2,1)S(1)}, bf16[256,128]{1,0:T(8,128)(2,1)S(1)}, u32[]{:S(2)}, u32[]{:S(2)}) collective-permute-start(bf16[256,128]{1,0:T(8,128)(2,1)S(1)} %shard_map.77), channel_id=1, source_target_pairs={{0,1},{1,0},{2,3},{3,2},{4,5},{5,4},{6,7},{7,6},{8,9},{9,8},{10,11... | collective-permute-start | bytes 196616 | tf_op jit(solution)/shard_map/ppermute | solution.py:57
  62.7 2.3 %collective-permute-done.23.refs_1_ = bf16[256,128]{1,0:T(8,128)(2,1)S(1)} collective-permute-done((bf16[256,128]{1,0:T(8,128)(2,1)S(1)}, bf16[256,128]{1,0:T(8,128)(2,1)S(1)}, u32[]{:S(2)}, u32[]{:S(2)}) %collective-permute-start.23) | collective-permute-done | bytes 65568 | tf_op jit(solution)/shard_map/ppermute | solution.py:57
  65.0 2.3 %collective-permute-start.26 = (bf16[4,128,128]{2,1,0:T(8,128)(2,1)S(1)}, bf16[4,128,128]{2,1,0:T(8,128)(2,1)S(1)}, u32[]{:S(2)}, u32[]{:S(2)}) collective-permute-start(bf16[4,128,128]{2,1,0:T(8,128)(2,1)S(1)} %get-tuple-element.72), channel_id=1, source_target_pairs={{0,4},{1,5},{2,6},{3,7},{4,0},{5,1},{6,2},{7,3},{8,12},{9,13},{10,... | collective-permute-start | bytes 393224 | tf_op jit(solution)/shard_map/ppermute | solution.py:57
  (63 shorter events, 18.7 us)
Async XLA Ops:
  0.0 19.8 %collective-permute-start = (bf16[256,768]{1,0:T(8,128)(2,1)}, bf16[256,768]{1,0:T(8,128)(2,1)}, u32[]{:S(2)}, u32[]{:S(2)}) collective-permute-start(bf16[256,768]{1,0:T(8,128)(2,1)} %w.1), channel_id=1, source_target_pairs={{0,16},{1,17},{2,18},{3,19},{4,20},{5,21},{6,22},{7,23},{8,24},{9,... | collective-permute-start | bytes 1179656 | tf_op jit(solution)/shard_map/ppermute | solution.py:57
  4.8 5.1 %collective-permute-start.1 = (bf16[336,256]{1,0:T(8,128)(2,1)S(1)}, bf16[336,256]{1,0:T(8,128)(2,1)S(1)}, u32[]{:S(2)}, u32[]{:S(2)}) collective-permute-start(bf16[336,256]{1,0:T(8,128)(2,1)S(1)} %get-tuple-element.40), channel_id=1, source_target_pairs={{0,1},{1,0},{2,3},{3,2},{4,5},{5,4},{6,7},{7,6},{8,9},{9,8},{10,11... | collective-permute-start | bytes 516104 | tf_op jit(solution)/shard_map/ppermute | solution.py:57
  6.1 4.7 %collective-permute-start.2 = (bf16[336,256]{1,0:T(8,128)(2,1)S(1)}, bf16[336,256]{1,0:T(8,128)(2,1)S(1)}, u32[]{:S(2)}, u32[]{:S(2)}) collective-permute-start(bf16[336,256]{1,0:T(8,128)(2,1)S(1)} %get-tuple-element.41), channel_id=1, source_target_pairs={{0,2},{1,3},{2,0},{3,1},{4,6},{5,7},{6,4},{7,5},{8,10},{9,11},{10,... | collective-permute-start | bytes 516104 | tf_op jit(solution)/shard_map/ppermute | solution.py:57
  7.3 16.7 %collective-permute-start.6 = (bf16[128,2048]{1,0:T(8,128)(2,1)}, bf16[128,2048]{1,0:T(8,128)(2,1)}, u32[]{:S(2)}, u32[]{:S(2)}) collective-permute-start(bf16[128,2048]{1,0:T(8,128)(2,1)} %bitcast.12), channel_id=1, source_target_pairs={{0,1},{1,0},{2,3},{3,2},{4,5},{5,4},{6,7},{7,6},{8,9},{9,8},{10,11... | collective-permute-start | bytes 1572872 | tf_op jit(solution)/shard_map/ppermute | solution.py:57
  7.6 16.5 %collective-permute-start.7 = (bf16[128,2048]{1,0:T(8,128)(2,1)}, bf16[128,2048]{1,0:T(8,128)(2,1)}, u32[]{:S(2)}, u32[]{:S(2)}) collective-permute-start(bf16[128,2048]{1,0:T(8,128)(2,1)} %bitcast.13), channel_id=1, source_target_pairs={{0,2},{1,3},{2,0},{3,1},{4,6},{5,7},{6,4},{7,5},{8,10},{9,11},{10,... | collective-permute-start | bytes 1572872 | tf_op jit(solution)/shard_map/ppermute | solution.py:57
  10.9 16.0 %collective-permute-start.8 = (bf16[256,768]{1,0:T(8,128)(2,1)S(1)}, bf16[256,768]{1,0:T(8,128)(2,1)S(1)}, u32[]{:S(2)}, u32[]{:S(2)}) collective-permute-start(bf16[256,768]{1,0:T(8,128)(2,1)S(1)} %shard_map.65.own.refs_2_.refs_0_), channel_id=1, source_target_pairs={{0,8},{1,9},{2,10},{3,11},{4,12},{5,13},{6,14},{7,15},{8,0},{9,1},... | collective-permute-start | bytes 1179656 | tf_op jit(solution)/shard_map/ppermute | solution.py:57
  11.2 11.4 %collective-permute-start.5 = (bf16[80,256]{1,0:T(8,128)(2,1)S(1)}, bf16[80,256]{1,0:T(8,128)(2,1)S(1)}, u32[]{:S(2)}, u32[]{:S(2)}) collective-permute-start(bf16[80,256]{1,0:T(8,128)(2,1)S(1)} %get-tuple-element.43), channel_id=1, source_target_pairs={{0,3},{1,2},{2,1},{3,0},{4,7},{5,6},{6,5},{7,4},{8,11},{9,10},{10,... | collective-permute-start | bytes 122888 | tf_op jit(solution)/shard_map/ppermute | solution.py:57
  20.9 5.5 %collective-permute-start.3 = (bf16[256,256]{1,0:T(8,128)(2,1)S(1)}, bf16[256,256]{1,0:T(8,128)(2,1)S(1)}, u32[]{:S(2)}, u32[]{:S(2)}) collective-permute-start(bf16[256,256]{1,0:T(8,128)(2,1)S(1)} %get-tuple-element.74), channel_id=1, source_target_pairs={{0,1},{1,0},{2,3},{3,2},{4,5},{5,4},{6,7},{7,6},{8,9},{9,8},{10,11... | collective-permute-start | bytes 393224 | tf_op jit(solution)/shard_map/ppermute | solution.py:57
  22.6 3.9 %collective-permute-start.4 = (bf16[256,256]{1,0:T(8,128)(2,1)S(1)}, bf16[256,256]{1,0:T(8,128)(2,1)S(1)}, u32[]{:S(2)}, u32[]{:S(2)}) collective-permute-start(bf16[256,256]{1,0:T(8,128)(2,1)S(1)} %get-tuple-element.73), channel_id=1, source_target_pairs={{0,2},{1,3},{2,0},{3,1},{4,6},{5,7},{6,4},{7,5},{8,10},{9,11},{10,... | collective-permute-start | bytes 393224 | tf_op jit(solution)/shard_map/ppermute | solution.py:57
  27.0 4.0 %collective-permute-start.9 = (bf16[256,384]{1,0:T(8,128)(2,1)S(1)}, bf16[256,384]{1,0:T(8,128)(2,1)S(1)}, u32[]{:S(2)}, u32[]{:S(2)}) collective-permute-start(bf16[256,384]{1,0:T(8,128)(2,1)S(1)} %get-tuple-element.52), channel_id=1, source_target_pairs={{0,4},{1,5},{2,6},{3,7},{4,0},{5,1},{6,2},{7,3},{8,12},{9,13},{10,... | collective-permute-start | bytes 589832 | tf_op jit(solution)/shard_map/ppermute | solution.py:57
  31.1 4.1 %collective-permute-start.10 = (bf16[384,2048]{1,0:T(8,128)(2,1)S(1)}, bf16[384,2048]{1,0:T(8,128)(2,1)S(1)}, u32[]{:S(2)}, u32[]{:S(2)}) collective-permute-start(bf16[384,2048]{1,0:T(8,128)(2,1)S(1)} %get-tuple-element.55.refs_0_), channel_id=1, source_target_pairs={{0,4},{1,5},{2,6},{3,7},{4,0},{5,1},{6,2},{7,3},{8,12},{9,13},{10,... | collective-permute-start | bytes 4718600 | tf_op jit(solution)/shard_map/ppermute | solution.py:57
  31.6 3.6 %collective-permute-start.12 = (bf16[528,384]{1,0:T(8,128)(2,1)S(1)}, bf16[528,384]{1,0:T(8,128)(2,1)S(1)}, u32[]{:S(2)}, u32[]{:S(2)}) collective-permute-start(bf16[528,384]{1,0:T(8,128)(2,1)S(1)} %shard_map.69), channel_id=1, source_target_pairs={{0,4},{1,5},{2,6},{3,7},{4,0},{5,1},{6,2},{7,3},{8,12},{9,13},{10,... | collective-permute-start | bytes 1216520 | tf_op jit(solution)/shard_map/ppermute | solution.py:57
  31.8 7.5 %collective-permute-start.13 = (bf16[128,1024]{1,0:T(8,128)(2,1)S(1)}, bf16[128,1024]{1,0:T(8,128)(2,1)S(1)}, u32[]{:S(2)}, u32[]{:S(2)}) collective-permute-start(bf16[128,1024]{1,0:T(8,128)(2,1)S(1)} %get-tuple-element.61), channel_id=1, source_target_pairs={{0,1},{1,0},{2,3},{3,2},{4,5},{5,4},{6,7},{7,6},{8,9},{9,8},{10,11... | collective-permute-start | bytes 786440 | tf_op jit(solution)/shard_map/ppermute | solution.py:57
  32.9 7.2 %collective-permute-start.11 = (bf16[128,1024]{1,0:T(8,128)(2,1)S(1)}, bf16[128,1024]{1,0:T(8,128)(2,1)S(1)}, u32[]{:S(2)}, u32[]{:S(2)}) collective-permute-start(bf16[128,1024]{1,0:T(8,128)(2,1)S(1)} %get-tuple-element.56), channel_id=1, source_target_pairs={{0,2},{1,3},{2,0},{3,1},{4,6},{5,7},{6,4},{7,5},{8,10},{9,11},{10,... | collective-permute-start | bytes 786440 | tf_op jit(solution)/shard_map/ppermute | solution.py:57
  33.2 11.3 %collective-permute-start.16 = (bf16[512,384]{1,0:T(8,128)(2,1)S(1)}, bf16[512,384]{1,0:T(8,128)(2,1)S(1)}, u32[]{:S(2)}, u32[]{:S(2)}) collective-permute-start(bf16[512,384]{1,0:T(8,128)(2,1)S(1)} %constant_dynamic-update-slice_fusion.refs_5_.refs_3_), channel_id=1, source_target_pairs={{0,8},{1,9},{2,10},{3,11},{4,12},{5,13},{6,14},{7,15},{8,0},{9,1},... | collective-permute-start | bytes 1179656 | tf_op jit(solution)/shard_map/ppermute | solution.py:57
  44.9 7.6 %collective-permute-start.17 = (bf16[4,256,128]{2,1,0:T(8,128)(2,1)S(1)}, bf16[4,256,128]{2,1,0:T(8,128)(2,1)S(1)}, u32[]{:S(2)}, u32[]{:S(2)}) collective-permute-start(bf16[4,256,128]{2,1,0:T(8,128)(2,1)S(1)} %shard_map.74.own), channel_id=1, source_target_pairs={{0,8},{1,9},{2,10},{3,11},{4,12},{5,13},{6,14},{7,15},{8,0},{9,1},... | collective-permute-start | bytes 786440 | tf_op jit(solution)/shard_map/ppermute | solution.py:57
  45.2 9.3 %collective-permute-start.18 = (bf16[4,256,128]{2,1,0:T(8,128)(2,1)S(1)}, bf16[4,256,128]{2,1,0:T(8,128)(2,1)S(1)}, u32[]{:S(2)}, u32[]{:S(2)}) collective-permute-start(bf16[4,256,128]{2,1,0:T(8,128)(2,1)S(1)} %shard_map.74.own), channel_id=1, source_target_pairs={{8,16},{9,17},{10,18},{11,19},{12,20},{13,21},{14,22},{15,23},{16,... | collective-permute-start | bytes 786440 | tf_op jit(solution)/shard_map/ppermute | solution.py:57
  48.4 7.2 %collective-permute-start.21 = (bf16[2,256,128]{2,1,0:T(8,128)(2,1)S(1)}, bf16[2,256,128]{2,1,0:T(8,128)(2,1)S(1)}, u32[]{:S(2)}, u32[]{:S(2)}) collective-permute-start(bf16[2,256,128]{2,1,0:T(8,128)(2,1)S(1)} %get-tuple-element.70.own), channel_id=1, source_target_pairs={{0,8},{1,9},{2,10},{3,11},{4,12},{5,13},{6,14},{7,15},{8,0},{9,1},... | collective-permute-start | bytes 393224 | tf_op jit(solution)/shard_map/ppermute | solution.py:57
  48.5 8.5 %collective-permute-start.22 = (bf16[2,256,128]{2,1,0:T(8,128)(2,1)S(1)}, bf16[2,256,128]{2,1,0:T(8,128)(2,1)S(1)}, u32[]{:S(2)}, u32[]{:S(2)}) collective-permute-start(bf16[2,256,128]{2,1,0:T(8,128)(2,1)S(1)} %get-tuple-element.70.own), channel_id=1, source_target_pairs={{8,16},{9,17},{10,18},{11,19},{12,20},{13,21},{14,22},{15,23},{16,... | collective-permute-start | bytes 393224 | tf_op jit(solution)/shard_map/ppermute | solution.py:57
  51.2 7.8 %collective-permute-start.19 = (bf16[2,256,128]{2,1,0:T(8,128)(2,1)S(1)}, bf16[2,256,128]{2,1,0:T(8,128)(2,1)S(1)}, u32[]{:S(2)}, u32[]{:S(2)}) collective-permute-start(bf16[2,256,128]{2,1,0:T(8,128)(2,1)S(1)} %get-tuple-element.69.own), channel_id=1, source_target_pairs={{0,8},{1,9},{2,10},{3,11},{4,12},{5,13},{6,14},{7,15},{8,0},{9,1},... | collective-permute-start | bytes 393224 | tf_op jit(solution)/shard_map/ppermute | solution.py:57
  52.5 6.8 %collective-permute-start.20 = (bf16[2,256,128]{2,1,0:T(8,128)(2,1)S(1)}, bf16[2,256,128]{2,1,0:T(8,128)(2,1)S(1)}, u32[]{:S(2)}, u32[]{:S(2)}) collective-permute-start(bf16[2,256,128]{2,1,0:T(8,128)(2,1)S(1)} %get-tuple-element.69.own), channel_id=1, source_target_pairs={{8,16},{9,17},{10,18},{11,19},{12,20},{13,21},{14,22},{15,23},{16,... | collective-permute-start | bytes 393224 | tf_op jit(solution)/shard_map/ppermute | solution.py:57
  57.3 5.4 %collective-permute-start.25 = (bf16[256,128]{1,0:T(8,128)(2,1)S(1)}, bf16[256,128]{1,0:T(8,128)(2,1)S(1)}, u32[]{:S(2)}, u32[]{:S(2)}) collective-permute-start(bf16[256,128]{1,0:T(8,128)(2,1)S(1)} %shard_map.79), channel_id=1, source_target_pairs={{0,3},{1,2},{2,1},{3,0},{4,7},{5,6},{6,5},{7,4},{8,11},{9,10},{10,... | collective-permute-start | bytes 196616 | tf_op jit(solution)/shard_map/ppermute | solution.py:57
  60.6 4.4 %collective-permute-start.23 = (bf16[256,128]{1,0:T(8,128)(2,1)S(1)}, bf16[256,128]{1,0:T(8,128)(2,1)S(1)}, u32[]{:S(2)}, u32[]{:S(2)}) collective-permute-start(bf16[256,128]{1,0:T(8,128)(2,1)S(1)} %shard_map.77), channel_id=1, source_target_pairs={{0,1},{1,0},{2,3},{3,2},{4,5},{5,4},{6,7},{7,6},{8,9},{9,8},{10,11... | collective-permute-start | bytes 196616 | tf_op jit(solution)/shard_map/ppermute | solution.py:57
  65.0 3.3 %collective-permute-start.26 = (bf16[4,128,128]{2,1,0:T(8,128)(2,1)S(1)}, bf16[4,128,128]{2,1,0:T(8,128)(2,1)S(1)}, u32[]{:S(2)}, u32[]{:S(2)}) collective-permute-start(bf16[4,128,128]{2,1,0:T(8,128)(2,1)S(1)} %get-tuple-element.72), channel_id=1, source_target_pairs={{0,4},{1,5},{2,6},{3,7},{4,0},{5,1},{6,2},{7,3},{8,12},{9,13},{10,... | collective-permute-start | bytes 393224 | tf_op jit(solution)/shard_map/ppermute | solution.py:57
  (7 other events, 74.3 us)

commit v26 on v24

--- a/solution.py
+++ b/solution.py
@@ -333,7 +333,7 @@
         "vv",
     )(w_qkv, raw)
     plane = [swap_depth(t, r) for t, r in zip(to, (1, 2, 3))]
-    own = call(sort_kernel, array(size, 6 * HD), "vvv")(kept, *plane[:2])
+    own = call(sort_kernel, array(size, 6 * HD), "vvv")(after(kept, plane[2]), *plane[:2])
     near = swap_z(own, 1)
     far_raw = after(far_raw, own)
 

time: 69.7 us -> 70.8 us (1.016)
  starting transfers between devices: 30 us -> 33.7 us
  waiting for transfers between devices: 25.3 us -> 22.9 us
    ppermute x27, starting transfers between devices: 30 us -> 33.7 us  [hop(): return lax.ppermute(value, ('tm', 'depth'), pairs)]
    ppermute x27, waiting for transfers between devices: 25.3 us -> 22.9 us  [hop(): return lax.ppermute(value, ('tm', 'depth'), pairs)]
  transfers between devices with their start and end apart: 27 -> 27, of which waited for: 16 -> 16; matrix products, arithmetic and copies ran while one was open for 4% -> 4% of each run, Pallas kernels for 13% -> 12%
where the time goes in v26:
time: 70.8 us; the launch traced here: 70.3 us
  starting transfers between devices  33.7 us (48%)
  waiting for transfers between devices  22.9 us (32%)
  Pallas kernels  9.97 us (14%)
  other arithmetic  2.48 us (4%)
  local copies, waits for them, and re-layouts  1.07 us (2%)
    ppermute x27, starting transfers between devices, hop(): return lax.ppermute(value, ('tm', 'depth'), pairs)  33.7 us
    ppermute x27, waiting for transfers between devices, hop(): return lax.ppermute(value, ('tm', 'depth'), pairs)  22.9 us
    pallas_call x3, Pallas kernels, embed(): call(functools.partial(embed_kernel, rs, len(finished)), out, 'v' * (6 +...  3.55 us
  transfers between devices with their start and end apart: 27, of which 16 were waited for; matrix products, arithmetic and copies ran while one was open for 4% of the time, Pallas kernels for 12%

profile of v26, /device:TPU:9, one launch (start us, length us, event | category | flops | bytes accessed | tf_op | source)
XLA Modules:
  0.0 70.3 jit_solution(13420957419300738144)
XLA Ops:
  0.0 2.3 %collective-permute-start = (bf16[256,768]{1,0:T(8,128)(2,1)}, bf16[256,768]{1,0:T(8,128)(2,1)}, u32[]{:S(2)}, u32[]{:S(2)}) collective-permute-start(bf16[256,768]{1,0:T(8,128)(2,1)} %w.1), channel_id=1, source_target_pairs={{0,16},{1,17},{2,18},{3,19},{4,20},{5,21},{6,22},{7,23},{8,24},{9,... | collective-permute-start | bytes 1179656 | tf_op jit(solution)/shard_map/ppermute | solution.py:57
  4.8 2.2 %collective-permute-start.1 = (bf16[80,256]{1,0:T(8,128)(2,1)S(1)}, bf16[80,256]{1,0:T(8,128)(2,1)S(1)}, u32[]{:S(2)}, u32[]{:S(2)}) collective-permute-start(bf16[80,256]{1,0:T(8,128)(2,1)S(1)} %get-tuple-element.40), channel_id=1, source_target_pairs={{0,3},{1,2},{2,1},{3,0},{4,7},{5,6},{6,5},{7,4},{8,11},{9,10},{10,... | collective-permute-start | bytes 122888 | tf_op jit(solution)/shard_map/ppermute | solution.py:57
  7.5 1.2 %collective-permute-start.7 = (bf16[128,2048]{1,0:T(8,128)(2,1)}, bf16[128,2048]{1,0:T(8,128)(2,1)}, u32[]{:S(2)}, u32[]{:S(2)}) collective-permute-start(bf16[128,2048]{1,0:T(8,128)(2,1)} %bitcast.12), channel_id=1, source_target_pairs={{0,2},{1,3},{2,0},{3,1},{4,6},{5,7},{6,4},{7,5},{8,10},{9,11},{10,... | collective-permute-start | bytes 1572872 | tf_op jit(solution)/shard_map/ppermute | solution.py:57
  9.0 1.2 %collective-permute-start.6 = (bf16[128,2048]{1,0:T(8,128)(2,1)}, bf16[128,2048]{1,0:T(8,128)(2,1)}, u32[]{:S(2)}, u32[]{:S(2)}) collective-permute-start(bf16[128,2048]{1,0:T(8,128)(2,1)} %bitcast.13), channel_id=1, source_target_pairs={{0,1},{1,0},{2,3},{3,2},{4,5},{5,4},{6,7},{7,6},{8,9},{9,8},{10,11... | collective-permute-start | bytes 1572872 | tf_op jit(solution)/shard_map/ppermute | solution.py:57
  10.2 2.3 %collective-permute-done.2.from_x.plane_x = bf16[336,256]{1,0:T(8,128)(2,1)S(1)} collective-permute-done((bf16[336,256]{1,0:T(8,128)(2,1)S(1)}, bf16[336,256]{1,0:T(8,128)(2,1)S(1)}, u32[]{:S(2)}, u32[]{:S(2)}) %collective-permute-start.2) | collective-permute-done | bytes 172064 | tf_op jit(solution)/shard_map/ppermute | solution.py:57
  13.0 6.8 %collective-permute-done = bf16[256,768]{1,0:T(8,128)(2,1)} collective-permute-done((bf16[256,768]{1,0:T(8,128)(2,1)}, bf16[256,768]{1,0:T(8,128)(2,1)}, u32[]{:S(2)}, u32[]{:S(2)}) %collective-permute-start) | collective-permute-done | bytes 393248 | tf_op jit(solution)/shard_map/ppermute | solution.py:57
  20.9 1.3 %collective-permute-start.4 = (bf16[256,256]{1,0:T(8,128)(2,1)S(1)}, bf16[256,256]{1,0:T(8,128)(2,1)S(1)}, u32[]{:S(2)}, u32[]{:S(2)}) collective-permute-start(bf16[256,256]{1,0:T(8,128)(2,1)S(1)} %get-tuple-element.74), channel_id=1, source_target_pairs={{0,1},{1,0},{2,3},{3,2},{4,5},{5,4},{6,7},{7,6},{8,9},{9,8},{10,11... | collective-permute-start | bytes 393224 | tf_op jit(solution)/shard_map/ppermute | solution.py:57
  22.2 1.2 %collective-permute-start.5 = (bf16[256,256]{1,0:T(8,128)(2,1)S(1)}, bf16[256,256]{1,0:T(8,128)(2,1)S(1)}, u32[]{:S(2)}, u32[]{:S(2)}) collective-permute-start(bf16[256,256]{1,0:T(8,128)(2,1)S(1)} %get-tuple-element.73), channel_id=1, source_target_pairs={{0,2},{1,3},{2,0},{3,1},{4,6},{5,7},{6,4},{7,5},{8,10},{9,11},{10,... | collective-permute-start | bytes 393224 | tf_op jit(solution)/shard_map/ppermute | solution.py:57
  24.1 2.3 %shard_map.67 = (bf16[384,2048]{1,0:T(8,128)(2,1)S(1)}, bf16[128,1024]{1,0:T(8,128)(2,1)S(1)}, bf16[128,1024]{1,0:T(8,128)(2,1)S(1)}) custom-call(bf16[144,128]{1,0:T(8,128)(2,1)S(1)} %pad_maximum_fusion.raw, bf16[336,256]{1,0:T(8,128)(2,1)S(1)} %collective-permute-done.2.from_x.plane_x, bf16[336,256]{1,0:T(8,128)(2,1)S(1)} %collective-permute-done.3.from_y.plane_y, ...), custom_call_target="tpu_custom_call" | custom-call | flops 402653184 | tf_op jit(solution)/shard_map/pallas_call | solution.py:346
  27.4 2.1 %collective-permute-start.9 = (bf16[256,384]{1,0:T(8,128)(2,1)S(1)}, bf16[256,384]{1,0:T(8,128)(2,1)S(1)}, u32[]{:S(2)}, u32[]{:S(2)}) collective-permute-start(bf16[256,384]{1,0:T(8,128)(2,1)S(1)} %get-tuple-element.52), channel_id=1, source_target_pairs={{0,4},{1,5},{2,6},{3,7},{4,0},{5,1},{6,2},{7,3},{8,12},{9,13},{10,... | collective-permute-start | bytes 589832 | tf_op jit(solution)/shard_map/ppermute | solution.py:57
  31.2 1.5 %collective-permute-start.13 = (bf16[128,1024]{1,0:T(8,128)(2,1)S(1)}, bf16[128,1024]{1,0:T(8,128)(2,1)S(1)}, u32[]{:S(2)}, u32[]{:S(2)}) collective-permute-start(bf16[128,1024]{1,0:T(8,128)(2,1)S(1)} %get-tuple-element.61), channel_id=1, source_target_pairs={{0,1},{1,0},{2,3},{3,2},{4,5},{5,4},{6,7},{7,6},{8,9},{9,8},{10,11... | collective-permute-start | bytes 786440 | tf_op jit(solution)/shard_map/ppermute | solution.py:57
  32.7 1.4 %collective-permute-start.16 = (bf16[512,384]{1,0:T(8,128)(2,1)S(1)}, bf16[512,384]{1,0:T(8,128)(2,1)S(1)}, u32[]{:S(2)}, u32[]{:S(2)}) collective-permute-start(bf16[512,384]{1,0:T(8,128)(2,1)S(1)} %constant_dynamic-update-slice_fusion.refs_5_.refs_3_), channel_id=1, source_target_pairs={{0,8},{1,9},{2,10},{3,11},{4,12},{5,13},{6,14},{7,15},{8,0},{9,1},... | collective-permute-start | bytes 1179656 | tf_op jit(solution)/shard_map/ppermute | solution.py:57
  34.6 1.4 %shard_map.70.refs_4_ = f32[768,384]{1,0:T(8,128)S(1)} custom-call(bf16[384,2048]{1,0:T(8,128)(2,1)S(1)} %get-tuple-element.55.refs_0_, bf16[384,2048]{1,0:T(8,128)(2,1)S(1)} %collective-permute-done.10.refs_1_, bf16[256,768]{1,0:T(8,128)(2,1)S(1)} %shard_map.65.own.refs_2_.refs_0_, bf16[256,768]{1,0:T(8,128)(2,1)S(1)} %collective-permute-done.8.near.refs_3_.refs_1_, ...), custom_call_target="tpu_custom_call" | custom-call | flops 905969664 | tf_op jit(solution)/shard_map/pallas_call | solution.py:379
  36.0 2.8 %collective-permute-done.13.refs_1_ = bf16[128,1024]{1,0:T(8,128)(2,1)S(1)} collective-permute-done((bf16[128,1024]{1,0:T(8,128)(2,1)S(1)}, bf16[128,1024]{1,0:T(8,128)(2,1)S(1)}, u32[]{:S(2)}, u32[]{:S(2)}) %collective-permute-start.13) | collective-permute-done | bytes 262176 | tf_op jit(solution)/shard_map/ppermute | solution.py:57
  40.5 1.6 %collective-permute-start.14 = (bf16[80,2048]{1,0:T(8,128)(2,1)S(1)}, bf16[80,2048]{1,0:T(8,128)(2,1)S(1)}, u32[]{:S(2)}, u32[]{:S(2)}) collective-permute-start(bf16[80,2048]{1,0:T(8,128)(2,1)S(1)} %get-tuple-element.64), channel_id=1, source_target_pairs={{0,4},{1,5},{2,6},{3,7},{4,0},{5,1},{6,2},{7,3},{8,12},{9,13},{10,... | collective-permute-start | bytes 983048 | tf_op jit(solution)/shard_map/ppermute | solution.py:57
  42.2 1.5 %collective-permute-done.15.bottom = bf16[48,2048]{1,0:T(8,128)(2,1)S(1)} collective-permute-done((bf16[48,2048]{1,0:T(8,128)(2,1)S(1)}, bf16[48,2048]{1,0:T(8,128)(2,1)S(1)}, u32[]{:S(2)}, u32[]{:S(2)}) %collective-permute-start.15) | collective-permute-done | bytes 196640 | tf_op jit(solution)/shard_map/ppermute | solution.py:57
  45.0 4.2 %collective-permute-start.18 = (bf16[4,256,128]{2,1,0:T(8,128)(2,1)S(1)}, bf16[4,256,128]{2,1,0:T(8,128)(2,1)S(1)}, u32[]{:S(2)}, u32[]{:S(2)}) collective-permute-start(bf16[4,256,128]{2,1,0:T(8,128)(2,1)S(1)} %shard_map.74.own), channel_id=1, source_target_pairs={{8,16},{9,17},{10,18},{11,19},{12,20},{13,21},{14,22},{15,23},{16,... | collective-permute-start | bytes 786440 | tf_op jit(solution)/shard_map/ppermute | solution.py:57
  50.0 1.9 %collective-permute-start.22 = (bf16[2,256,128]{2,1,0:T(8,128)(2,1)S(1)}, bf16[2,256,128]{2,1,0:T(8,128)(2,1)S(1)}, u32[]{:S(2)}, u32[]{:S(2)}) collective-permute-start(bf16[2,256,128]{2,1,0:T(8,128)(2,1)S(1)} %get-tuple-element.70.own), channel_id=1, source_target_pairs={{8,16},{9,17},{10,18},{11,19},{12,20},{13,21},{14,22},{15,23},{16,... | collective-permute-start | bytes 393224 | tf_op jit(solution)/shard_map/ppermute | solution.py:57
  52.3 3.0 %collective-permute-start.20 = (bf16[2,256,128]{2,1,0:T(8,128)(2,1)S(1)}, bf16[2,256,128]{2,1,0:T(8,128)(2,1)S(1)}, u32[]{:S(2)}, u32[]{:S(2)}) collective-permute-start(bf16[2,256,128]{2,1,0:T(8,128)(2,1)S(1)} %get-tuple-element.69.own), channel_id=1, source_target_pairs={{8,16},{9,17},{10,18},{11,19},{12,20},{13,21},{14,22},{15,23},{16,... | collective-permute-start | bytes 393224 | tf_op jit(solution)/shard_map/ppermute | solution.py:57
  55.4 1.2 %shard_map.75.weights = bf16[4,256,640]{2,1,0:T(8,128)(2,1)S(1)} custom-call(bf16[4,256,128]{2,1,0:T(8,128)(2,1)S(1)} %get-tuple-element.68.q_ref, bf16[4,256,128]{2,1,0:T(8,128)(2,1)S(1)} %collective-permute-done.17.outer, bf16[4,256,128]{2,1,0:T(8,128)(2,1)S(1)} %shard_map.74.own, bf16[4,256,128]{2,1,0:T(8,128)(2,1)S(1)} %collective-permute-done.18.middle, ...), custom_call_target="tpu_custom_call" | custom-call | flops 167772160 | tf_op jit(solution)/shard_map/pallas_call | solution.py:396
  57.7 1.8 %collective-permute-start.25 = (bf16[256,128]{1,0:T(8,128)(2,1)S(1)}, bf16[256,128]{1,0:T(8,128)(2,1)S(1)}, u32[]{:S(2)}, u32[]{:S(2)}) collective-permute-start(bf16[256,128]{1,0:T(8,128)(2,1)S(1)} %shard_map.79), channel_id=1, source_target_pairs={{0,3},{1,2},{2,1},{3,0},{4,7},{5,6},{6,5},{7,4},{8,11},{9,10},{10,... | collective-permute-start | bytes 196616 | tf_op jit(solution)/shard_map/ppermute | solution.py:57
  60.5 1.9 %collective-permute-start.24 = (bf16[256,128]{1,0:T(8,128)(2,1)S(1)}, bf16[256,128]{1,0:T(8,128)(2,1)S(1)}, u32[]{:S(2)}, u32[]{:S(2)}) collective-permute-start(bf16[256,128]{1,0:T(8,128)(2,1)S(1)} %shard_map.78), channel_id=1, source_target_pairs={{0,2},{1,3},{2,0},{3,1},{4,6},{5,7},{6,4},{7,5},{8,10},{9,11},{10,... | collective-permute-start | bytes 196616 | tf_op jit(solution)/shard_map/ppermute | solution.py:57
  64.0 2.1 %collective-permute-done.23.refs_1_ = bf16[256,128]{1,0:T(8,128)(2,1)S(1)} collective-permute-done((bf16[256,128]{1,0:T(8,128)(2,1)S(1)}, bf16[256,128]{1,0:T(8,128)(2,1)S(1)}, u32[]{:S(2)}, u32[]{:S(2)}) %collective-permute-start.23) | collective-permute-done | bytes 65568 | tf_op jit(solution)/shard_map/ppermute | solution.py:57
  66.1 2.4 %collective-permute-start.26 = (bf16[4,128,128]{2,1,0:T(8,128)(2,1)S(1)}, bf16[4,128,128]{2,1,0:T(8,128)(2,1)S(1)}, u32[]{:S(2)}, u32[]{:S(2)}) collective-permute-start(bf16[4,128,128]{2,1,0:T(8,128)(2,1)S(1)} %get-tuple-element.72), channel_id=1, source_target_pairs={{0,4},{1,5},{2,6},{3,7},{4,0},{5,1},{6,2},{7,3},{8,12},{9,13},{10,... | collective-permute-start | bytes 393224 | tf_op jit(solution)/shard_map/ppermute | solution.py:57
  (63 shorter events, 18.5 us)
Async XLA Ops:
  0.0 19.8 %collective-permute-start = (bf16[256,768]{1,0:T(8,128)(2,1)}, bf16[256,768]{1,0:T(8,128)(2,1)}, u32[]{:S(2)}, u32[]{:S(2)}) collective-permute-start(bf16[256,768]{1,0:T(8,128)(2,1)} %w.1), channel_id=1, source_target_pairs={{0,16},{1,17},{2,18},{3,19},{4,20},{5,21},{6,22},{7,23},{8,24},{9,... | collective-permute-start | bytes 1179656 | tf_op jit(solution)/shard_map/ppermute | solution.py:57
  4.8 4.2 %collective-permute-start.1 = (bf16[80,256]{1,0:T(8,128)(2,1)S(1)}, bf16[80,256]{1,0:T(8,128)(2,1)S(1)}, u32[]{:S(2)}, u32[]{:S(2)}) collective-permute-start(bf16[80,256]{1,0:T(8,128)(2,1)S(1)} %get-tuple-element.40), channel_id=1, source_target_pairs={{0,3},{1,2},{2,1},{3,0},{4,7},{5,6},{6,5},{7,4},{8,11},{9,10},{10,... | collective-permute-start | bytes 122888 | tf_op jit(solution)/shard_map/ppermute | solution.py:57
  7.0 5.5 %collective-permute-start.2 = (bf16[336,256]{1,0:T(8,128)(2,1)S(1)}, bf16[336,256]{1,0:T(8,128)(2,1)S(1)}, u32[]{:S(2)}, u32[]{:S(2)}) collective-permute-start(bf16[336,256]{1,0:T(8,128)(2,1)S(1)} %get-tuple-element.42), channel_id=1, source_target_pairs={{0,1},{1,0},{2,3},{3,2},{4,5},{5,4},{6,7},{7,6},{8,9},{9,8},{10,11... | collective-permute-start | bytes 516104 | tf_op jit(solution)/shard_map/ppermute | solution.py:57
  7.3 5.3 %collective-permute-start.3 = (bf16[336,256]{1,0:T(8,128)(2,1)S(1)}, bf16[336,256]{1,0:T(8,128)(2,1)S(1)}, u32[]{:S(2)}, u32[]{:S(2)}) collective-permute-start(bf16[336,256]{1,0:T(8,128)(2,1)S(1)} %get-tuple-element.43), channel_id=1, source_target_pairs={{0,2},{1,3},{2,0},{3,1},{4,6},{5,7},{6,4},{7,5},{8,10},{9,11},{10,... | collective-permute-start | bytes 516104 | tf_op jit(solution)/shard_map/ppermute | solution.py:57
  7.5 16.5 %collective-permute-start.7 = (bf16[128,2048]{1,0:T(8,128)(2,1)}, bf16[128,2048]{1,0:T(8,128)(2,1)}, u32[]{:S(2)}, u32[]{:S(2)}) collective-permute-start(bf16[128,2048]{1,0:T(8,128)(2,1)} %bitcast.12), channel_id=1, source_target_pairs={{0,2},{1,3},{2,0},{3,1},{4,6},{5,7},{6,4},{7,5},{8,10},{9,11},{10,... | collective-permute-start | bytes 1572872 | tf_op jit(solution)/shard_map/ppermute | solution.py:57
  9.0 15.0 %collective-permute-start.6 = (bf16[128,2048]{1,0:T(8,128)(2,1)}, bf16[128,2048]{1,0:T(8,128)(2,1)}, u32[]{:S(2)}, u32[]{:S(2)}) collective-permute-start(bf16[128,2048]{1,0:T(8,128)(2,1)} %bitcast.13), channel_id=1, source_target_pairs={{0,1},{1,0},{2,3},{3,2},{4,5},{5,4},{6,7},{7,6},{8,9},{9,8},{10,11... | collective-permute-start | bytes 1572872 | tf_op jit(solution)/shard_map/ppermute | solution.py:57
  12.7 14.6 %collective-permute-start.8 = (bf16[256,768]{1,0:T(8,128)(2,1)S(1)}, bf16[256,768]{1,0:T(8,128)(2,1)S(1)}, u32[]{:S(2)}, u32[]{:S(2)}) collective-permute-start(bf16[256,768]{1,0:T(8,128)(2,1)S(1)} %shard_map.65.own.refs_2_.refs_0_), channel_id=1, source_target_pairs={{0,8},{1,9},{2,10},{3,11},{4,12},{5,13},{6,14},{7,15},{8,0},{9,1},... | collective-permute-start | bytes 1179656 | tf_op jit(solution)/shard_map/ppermute | solution.py:57
  20.9 5.7 %collective-permute-start.4 = (bf16[256,256]{1,0:T(8,128)(2,1)S(1)}, bf16[256,256]{1,0:T(8,128)(2,1)S(1)}, u32[]{:S(2)}, u32[]{:S(2)}) collective-permute-start(bf16[256,256]{1,0:T(8,128)(2,1)S(1)} %get-tuple-element.74), channel_id=1, source_target_pairs={{0,1},{1,0},{2,3},{3,2},{4,5},{5,4},{6,7},{7,6},{8,9},{9,8},{10,11... | collective-permute-start | bytes 393224 | tf_op jit(solution)/shard_map/ppermute | solution.py:57
  22.2 5.1 %collective-permute-start.5 = (bf16[256,256]{1,0:T(8,128)(2,1)S(1)}, bf16[256,256]{1,0:T(8,128)(2,1)S(1)}, u32[]{:S(2)}, u32[]{:S(2)}) collective-permute-start(bf16[256,256]{1,0:T(8,128)(2,1)S(1)} %get-tuple-element.73), channel_id=1, source_target_pairs={{0,2},{1,3},{2,0},{3,1},{4,6},{5,7},{6,4},{7,5},{8,10},{9,11},{10,... | collective-permute-start | bytes 393224 | tf_op jit(solution)/shard_map/ppermute | solution.py:57
  30.6 4.1 %collective-permute-start.10 = (bf16[384,2048]{1,0:T(8,128)(2,1)S(1)}, bf16[384,2048]{1,0:T(8,128)(2,1)S(1)}, u32[]{:S(2)}, u32[]{:S(2)}) collective-permute-start(bf16[384,2048]{1,0:T(8,128)(2,1)S(1)} %get-tuple-element.55.refs_0_), channel_id=1, source_target_pairs={{0,4},{1,5},{2,6},{3,7},{4,0},{5,1},{6,2},{7,3},{8,12},{9,13},{10,... | collective-permute-start | bytes 4718600 | tf_op jit(solution)/shard_map/ppermute | solution.py:57
  31.0 3.6 %collective-permute-start.12 = (bf16[528,384]{1,0:T(8,128)(2,1)S(1)}, bf16[528,384]{1,0:T(8,128)(2,1)S(1)}, u32[]{:S(2)}, u32[]{:S(2)}) collective-permute-start(bf16[528,384]{1,0:T(8,128)(2,1)S(1)} %shard_map.69), channel_id=1, source_target_pairs={{0,4},{1,5},{2,6},{3,7},{4,0},{5,1},{6,2},{7,3},{8,12},{9,13},{10,... | collective-permute-start | bytes 1216520 | tf_op jit(solution)/shard_map/ppermute | solution.py:57
  31.2 7.5 %collective-permute-start.13 = (bf16[128,1024]{1,0:T(8,128)(2,1)S(1)}, bf16[128,1024]{1,0:T(8,128)(2,1)S(1)}, u32[]{:S(2)}, u32[]{:S(2)}) collective-permute-start(bf16[128,1024]{1,0:T(8,128)(2,1)S(1)} %get-tuple-element.61), channel_id=1, source_target_pairs={{0,1},{1,0},{2,3},{3,2},{4,5},{5,4},{6,7},{7,6},{8,9},{9,8},{10,11... | collective-permute-start | bytes 786440 | tf_op jit(solution)/shard_map/ppermute | solution.py:57
  32.7 7.2 %collective-permute-start.11 = (bf16[128,1024]{1,0:T(8,128)(2,1)S(1)}, bf16[128,1024]{1,0:T(8,128)(2,1)S(1)}, u32[]{:S(2)}, u32[]{:S(2)}) collective-permute-start(bf16[128,1024]{1,0:T(8,128)(2,1)S(1)} %get-tuple-element.56), channel_id=1, source_target_pairs={{0,2},{1,3},{2,0},{3,1},{4,6},{5,7},{6,4},{7,5},{8,10},{9,11},{10,... | collective-permute-start | bytes 786440 | tf_op jit(solution)/shard_map/ppermute | solution.py:57
  32.7 11.6 %collective-permute-start.16 = (bf16[512,384]{1,0:T(8,128)(2,1)S(1)}, bf16[512,384]{1,0:T(8,128)(2,1)S(1)}, u32[]{:S(2)}, u32[]{:S(2)}) collective-permute-start(bf16[512,384]{1,0:T(8,128)(2,1)S(1)} %constant_dynamic-update-slice_fusion.refs_5_.refs_3_), channel_id=1, source_target_pairs={{0,8},{1,9},{2,10},{3,11},{4,12},{5,13},{6,14},{7,15},{8,0},{9,1},... | collective-permute-start | bytes 1179656 | tf_op jit(solution)/shard_map/ppermute | solution.py:57
  44.8 7.6 %collective-permute-start.17 = (bf16[4,256,128]{2,1,0:T(8,128)(2,1)S(1)}, bf16[4,256,128]{2,1,0:T(8,128)(2,1)S(1)}, u32[]{:S(2)}, u32[]{:S(2)}) collective-permute-start(bf16[4,256,128]{2,1,0:T(8,128)(2,1)S(1)} %shard_map.74.own), channel_id=1, source_target_pairs={{0,8},{1,9},{2,10},{3,11},{4,12},{5,13},{6,14},{7,15},{8,0},{9,1},... | collective-permute-start | bytes 786440 | tf_op jit(solution)/shard_map/ppermute | solution.py:57
  45.0 10.4 %collective-permute-start.18 = (bf16[4,256,128]{2,1,0:T(8,128)(2,1)S(1)}, bf16[4,256,128]{2,1,0:T(8,128)(2,1)S(1)}, u32[]{:S(2)}, u32[]{:S(2)}) collective-permute-start(bf16[4,256,128]{2,1,0:T(8,128)(2,1)S(1)} %shard_map.74.own), channel_id=1, source_target_pairs={{8,16},{9,17},{10,18},{11,19},{12,20},{13,21},{14,22},{15,23},{16,... | collective-permute-start | bytes 786440 | tf_op jit(solution)/shard_map/ppermute | solution.py:57
  49.9 6.7 %collective-permute-start.21 = (bf16[2,256,128]{2,1,0:T(8,128)(2,1)S(1)}, bf16[2,256,128]{2,1,0:T(8,128)(2,1)S(1)}, u32[]{:S(2)}, u32[]{:S(2)}) collective-permute-start(bf16[2,256,128]{2,1,0:T(8,128)(2,1)S(1)} %get-tuple-element.70.own), channel_id=1, source_target_pairs={{0,8},{1,9},{2,10},{3,11},{4,12},{5,13},{6,14},{7,15},{8,0},{9,1},... | collective-permute-start | bytes 393224 | tf_op jit(solution)/shard_map/ppermute | solution.py:57
  50.0 7.5 %collective-permute-start.22 = (bf16[2,256,128]{2,1,0:T(8,128)(2,1)S(1)}, bf16[2,256,128]{2,1,0:T(8,128)(2,1)S(1)}, u32[]{:S(2)}, u32[]{:S(2)}) collective-permute-start(bf16[2,256,128]{2,1,0:T(8,128)(2,1)S(1)} %get-tuple-element.70.own), channel_id=1, source_target_pairs={{8,16},{9,17},{10,18},{11,19},{12,20},{13,21},{14,22},{15,23},{16,... | collective-permute-start | bytes 393224 | tf_op jit(solution)/shard_map/ppermute | solution.py:57
  51.9 7.6 %collective-permute-start.19 = (bf16[2,256,128]{2,1,0:T(8,128)(2,1)S(1)}, bf16[2,256,128]{2,1,0:T(8,128)(2,1)S(1)}, u32[]{:S(2)}, u32[]{:S(2)}) collective-permute-start(bf16[2,256,128]{2,1,0:T(8,128)(2,1)S(1)} %get-tuple-element.69.own), channel_id=1, source_target_pairs={{0,8},{1,9},{2,10},{3,11},{4,12},{5,13},{6,14},{7,15},{8,0},{9,1},... | collective-permute-start | bytes 393224 | tf_op jit(solution)/shard_map/ppermute | solution.py:57
  52.3 7.9 %collective-permute-start.20 = (bf16[2,256,128]{2,1,0:T(8,128)(2,1)S(1)}, bf16[2,256,128]{2,1,0:T(8,128)(2,1)S(1)}, u32[]{:S(2)}, u32[]{:S(2)}) collective-permute-start(bf16[2,256,128]{2,1,0:T(8,128)(2,1)S(1)} %get-tuple-element.69.own), channel_id=1, source_target_pairs={{8,16},{9,17},{10,18},{11,19},{12,20},{13,21},{14,22},{15,23},{16,... | collective-permute-start | bytes 393224 | tf_op jit(solution)/shard_map/ppermute | solution.py:57
  57.7 5.5 %collective-permute-start.25 = (bf16[256,128]{1,0:T(8,128)(2,1)S(1)}, bf16[256,128]{1,0:T(8,128)(2,1)S(1)}, u32[]{:S(2)}, u32[]{:S(2)}) collective-permute-start(bf16[256,128]{1,0:T(8,128)(2,1)S(1)} %shard_map.79), channel_id=1, source_target_pairs={{0,3},{1,2},{2,1},{3,0},{4,7},{5,6},{6,5},{7,4},{8,11},{9,10},{10,... | collective-permute-start | bytes 196616 | tf_op jit(solution)/shard_map/ppermute | solution.py:57
  60.5 3.5 %collective-permute-start.24 = (bf16[256,128]{1,0:T(8,128)(2,1)S(1)}, bf16[256,128]{1,0:T(8,128)(2,1)S(1)}, u32[]{:S(2)}, u32[]{:S(2)}) collective-permute-start(bf16[256,128]{1,0:T(8,128)(2,1)S(1)} %shard_map.78), channel_id=1, source_target_pairs={{0,2},{1,3},{2,0},{3,1},{4,6},{5,7},{6,4},{7,5},{8,10},{9,11},{10,... | collective-permute-start | bytes 196616 | tf_op jit(solution)/shard_map/ppermute | solution.py:57
  62.6 3.5 %collective-permute-start.23 = (bf16[256,128]{1,0:T(8,128)(2,1)S(1)}, bf16[256,128]{1,0:T(8,128)(2,1)S(1)}, u32[]{:S(2)}, u32[]{:S(2)}) collective-permute-start(bf16[256,128]{1,0:T(8,128)(2,1)S(1)} %shard_map.77), channel_id=1, source_target_pairs={{0,1},{1,0},{2,3},{3,2},{4,5},{5,4},{6,7},{7,6},{8,9},{9,8},{10,11... | collective-permute-start | bytes 196616 | tf_op jit(solution)/shard_map/ppermute | solution.py:57
  66.1 3.4 %collective-permute-start.26 = (bf16[4,128,128]{2,1,0:T(8,128)(2,1)S(1)}, bf16[4,128,128]{2,1,0:T(8,128)(2,1)S(1)}, u32[]{:S(2)}, u32[]{:S(2)}) collective-permute-start(bf16[4,128,128]{2,1,0:T(8,128)(2,1)S(1)} %get-tuple-element.72), channel_id=1, source_target_pairs={{0,4},{1,5},{2,6},{3,7},{4,0},{5,1},{6,2},{7,3},{8,12},{9,13},{10,... | collective-permute-start | bytes 393224 | tf_op jit(solution)/shard_map/ppermute | solution.py:57
  (7 other events, 74.3 us)

commit v27 on v24

--- a/solution.py
+++ b/solution.py
@@ -138,15 +138,24 @@
 
 def embed_kernel(rs, more, raw, plane_x, plane_y, across, conv_w, gain, *refs):
     count = len(rs)
+    streamed = count > 1
+    if streamed:
+        refs, (tokens, sems) = refs[:-2], refs[-2:]
     halves = 2 if rs == (3,) else 1
     count *= halves
     streams, finished, (out_ref, *onward, acc) = refs[:count], refs[count : count + more], refs[count + more :]
     for ref in finished:
         out_ref[: ref.shape[0]] = ref[...]
-    if len(rs) > 1:
-        for i, ref in enumerate(onward):
-            half = ref.shape[1]
-            ref[...] = streams[i][:, i * half : (i + 1) * half]
+    copies = {}
+    if streamed:
+        part = conv_w.shape[1] // 4
+        for i in range(count):
+            for at in range(0, conv_w.shape[1], part):
+                here = pl.ds(at, part)
+                copies[i, at] = pltpu.make_async_copy(
+                    streams[i].at[:, here], tokens.at[i, :, here], sems.at[4 * i + at // part]
+                )
+                copies[i, at].start()
     _, _, depth = where_am_i()
     rows, width = raw.shape[0] - EXTRA, conv_w.shape[1]
     raws = [raw[:rows]]
@@ -168,13 +177,20 @@
         for at in range(0, width, step):
             here = slice(at, at + step)
             part = jnp.dot(windows, conv_w[:, here], preferred_element_type=jnp.float32)
-            each = width // halves
-            part += streams[i + at // each][:, at % each : at % each + step].astype(jnp.float32)
+            if streamed:
+                copies[i, at].wait()
+                part += tokens[i, :, here].astype(jnp.float32)
+            else:
+                each = width // halves
+                part += streams[i + at // each][:, at % each : at % each + step].astype(jnp.float32)
             acc[:, here] = part
             total += jnp.sum(part * part, axis=1, keepdims=True)
         scale = lax.rsqrt(total / width + 1e-05)
         normed = (acc[...] * scale * gain[...]).astype(jnp.bfloat16)
         out_ref[done + i * rows : done + (i + 1) * rows] = normed
+        if streamed:
+            half = onward[i].shape[1]
+            onward[i][...] = tokens[i, :, i * half : (i + 1) * half]
         if halves > 1:
             cut = onward[0].shape[0]
             onward[0][...], onward[1][...] = normed[:cut], normed[cut:]
@@ -299,7 +315,7 @@
 
 
 def call(kernel, outs, places, scratch=(), macs=0, limit=32):
-    spaces = {"v": VMEM}
+    spaces = {"v": VMEM, "a": pl.ANY}
     return pl.pallas_call(
         kernel,
         out_shape=outs,
@@ -346,8 +362,9 @@
         return call(
             functools.partial(embed_kernel, rs, len(finished)),
             out,
-            "v" * (6 + len(streams) + len(finished)),
-            scratch=[VMEM((block, width), f32)],
+            "v" * 6 + ("a" if len(rs) > 1 else "v") * len(streams) + "v" * len(finished),
+            scratch=[VMEM((block, width), f32)]
+            + [VMEM((2, block, width), bf16), pltpu.SemaphoreType.DMA((8,))] * (len(rs) > 1),
             macs=len(rs) * block * 3 * feat_len * width,
         )(raw, *plane, conv_w, gain, *streams, *finished)
 

time: 69.7 us -> 70.3 us (level)
  Pallas kernels: 9.98 us -> 11.4 us
  waiting for transfers between devices: 25.3 us -> 24 us
    pallas_call x3, Pallas kernels: 3.56 us -> 4.97 us  [embed(): call(functools.partial(embed_kernel, rs, len(finished)), out, 'v' * 6 + (...]
    ppermute x27, waiting for transfers between devices: 25.3 us -> 24 us  [hop(): return lax.ppermute(value, ('tm', 'depth'), pairs)]
  transfers between devices with their start and end apart: 27 -> 27, of which waited for: 16 -> 15; matrix products, arithmetic and copies ran while one was open for 4% -> 4% of each run, Pallas kernels for 13% -> 14%
where the time goes in v27:
time: 70.3 us; the launch traced here: 69.6 us
  starting transfers between devices  30.4 us (43%)
  waiting for transfers between devices  24 us (34%)
  Pallas kernels  11.4 us (16%)
  other arithmetic  2.48 us (4%)
  local copies, waits for them, and re-layouts  1.07 us (2%)
    ppermute x27, starting transfers between devices, hop(): return lax.ppermute(value, ('tm', 'depth'), pairs)  30.4 us
    ppermute x27, waiting for transfers between devices, hop(): return lax.ppermute(value, ('tm', 'depth'), pairs)  24 us
    pallas_call x3, Pallas kernels, embed(): call(functools.partial(embed_kernel, rs, len(finished)), out, 'v' * 6 + (...  4.97 us
  transfers between devices with their start and end apart: 27, of which 15 were waited for; matrix products, arithmetic and copies ran while one was open for 4% of the time, Pallas kernels for 14%

profile of v27, /device:TPU:9, one launch (start us, length us, event | category | flops | bytes accessed | tf_op | source)
XLA Modules:
  0.0 69.6 jit_solution(10016643713056915059)
XLA Ops:
  0.0 2.3 %collective-permute-start = (bf16[256,768]{1,0:T(8,128)(2,1)}, bf16[256,768]{1,0:T(8,128)(2,1)}, u32[]{:S(2)}, u32[]{:S(2)}) collective-permute-start(bf16[256,768]{1,0:T(8,128)(2,1)} %w.1), channel_id=1, source_target_pairs={{0,16},{1,17},{2,18},{3,19},{4,20},{5,21},{6,22},{7,23},{8,24},{9,... | collective-permute-start | bytes 1179656 | tf_op jit(solution)/shard_map/ppermute | solution.py:57
  4.8 1.3 %collective-permute-start.1 = (bf16[336,256]{1,0:T(8,128)(2,1)S(1)}, bf16[336,256]{1,0:T(8,128)(2,1)S(1)}, u32[]{:S(2)}, u32[]{:S(2)}) collective-permute-start(bf16[336,256]{1,0:T(8,128)(2,1)S(1)} %get-tuple-element.39), channel_id=1, source_target_pairs={{0,1},{1,0},{2,3},{3,2},{4,5},{5,4},{6,7},{7,6},{8,9},{9,8},{10,11... | collective-permute-start | bytes 516104 | tf_op jit(solution)/shard_map/ppermute | solution.py:57
  6.1 1.2 %collective-permute-start.2 = (bf16[336,256]{1,0:T(8,128)(2,1)S(1)}, bf16[336,256]{1,0:T(8,128)(2,1)S(1)}, u32[]{:S(2)}, u32[]{:S(2)}) collective-permute-start(bf16[336,256]{1,0:T(8,128)(2,1)S(1)} %get-tuple-element.40), channel_id=1, source_target_pairs={{0,2},{1,3},{2,0},{3,1},{4,6},{5,7},{6,4},{7,5},{8,10},{9,11},{10,... | collective-permute-start | bytes 516104 | tf_op jit(solution)/shard_map/ppermute | solution.py:57
  7.8 2.1 %collective-permute-done.1.from_x.plane_x = bf16[336,256]{1,0:T(8,128)(2,1)S(1)} collective-permute-done((bf16[336,256]{1,0:T(8,128)(2,1)S(1)}, bf16[336,256]{1,0:T(8,128)(2,1)S(1)}, u32[]{:S(2)}, u32[]{:S(2)}) %collective-permute-start.1) | collective-permute-done | bytes 172064 | tf_op jit(solution)/shard_map/ppermute | solution.py:57
  11.2 1.2 %collective-permute-start.5 = (bf16[80,256]{1,0:T(8,128)(2,1)S(1)}, bf16[80,256]{1,0:T(8,128)(2,1)S(1)}, u32[]{:S(2)}, u32[]{:S(2)}) collective-permute-start(bf16[80,256]{1,0:T(8,128)(2,1)S(1)} %get-tuple-element.42), channel_id=1, source_target_pairs={{0,3},{1,2},{2,1},{3,0},{4,7},{5,6},{6,5},{7,4},{8,11},{9,10},{10,... | collective-permute-start | bytes 122888 | tf_op jit(solution)/shard_map/ppermute | solution.py:57
  12.3 7.5 %collective-permute-done = bf16[256,768]{1,0:T(8,128)(2,1)} collective-permute-done((bf16[256,768]{1,0:T(8,128)(2,1)}, bf16[256,768]{1,0:T(8,128)(2,1)}, u32[]{:S(2)}, u32[]{:S(2)}) %collective-permute-start) | collective-permute-done | bytes 393248 | tf_op jit(solution)/shard_map/ppermute | solution.py:57
  19.8 1.1 %broadcast_select_fusion = (bf16[256,256]{1,0:T(8,128)(2,1)S(1)}, bf16[256,256]{1,0:T(8,128)(2,1)S(1)}, bf16[256,256]{1,0:T(8,128)(2,1)S(1)}) fusion(pred[]{:T(512)S(6)} %eq.3, bf16[256,768]{1,0:T(8,128)(2,1)} %collective-permute-done), kind=kLoop, calls=%fused_computation | loop fusion | flops 131072 | bytes 786433 | tf_op jit(solution)/shard_map/jit(_where)/select_n | solution.py:377
  20.9 1.3 %collective-permute-start.3 = (bf16[256,256]{1,0:T(8,128)(2,1)S(1)}, bf16[256,256]{1,0:T(8,128)(2,1)S(1)}, u32[]{:S(2)}, u32[]{:S(2)}) collective-permute-start(bf16[256,256]{1,0:T(8,128)(2,1)S(1)} %get-tuple-element.72), channel_id=1, source_target_pairs={{0,1},{1,0},{2,3},{3,2},{4,5},{5,4},{6,7},{7,6},{8,9},{9,8},{10,11... | collective-permute-start | bytes 393224 | tf_op jit(solution)/shard_map/ppermute | solution.py:57
  24.1 3.7 %shard_map.67 = (bf16[384,2048]{1,0:T(8,128)(2,1)S(1)}, bf16[128,1024]{1,0:T(8,128)(2,1)S(1)}, bf16[128,1024]{1,0:T(8,128)(2,1)S(1)}) custom-call(bf16[144,128]{1,0:T(8,128)(2,1)S(1)} %pad_maximum_fusion.raw, bf16[336,256]{1,0:T(8,128)(2,1)S(1)} %collective-permute-done.1.from_x.plane_x, bf16[336,256]{1,0:T(8,128)(2,1)S(1)} %collective-permute-done.2.from_y.plane_y, ...), custom_call_target="tpu_custom_call" | custom-call | flops 402653184 | tf_op jit(solution)/shard_map/pallas_call | solution.py:362
  28.0 2.0 %collective-permute-start.9 = (bf16[256,384]{1,0:T(8,128)(2,1)S(1)}, bf16[256,384]{1,0:T(8,128)(2,1)S(1)}, u32[]{:S(2)}, u32[]{:S(2)}) collective-permute-start(bf16[256,384]{1,0:T(8,128)(2,1)S(1)} %get-tuple-element.50), channel_id=1, source_target_pairs={{0,4},{1,5},{2,6},{3,7},{4,0},{5,1},{6,2},{7,3},{8,12},{9,13},{10,... | collective-permute-start | bytes 589832 | tf_op jit(solution)/shard_map/ppermute | solution.py:57
  31.8 1.2 %collective-permute-start.13 = (bf16[128,1024]{1,0:T(8,128)(2,1)S(1)}, bf16[128,1024]{1,0:T(8,128)(2,1)S(1)}, u32[]{:S(2)}, u32[]{:S(2)}) collective-permute-start(bf16[128,1024]{1,0:T(8,128)(2,1)S(1)} %get-tuple-element.59), channel_id=1, source_target_pairs={{0,1},{1,0},{2,3},{3,2},{4,5},{5,4},{6,7},{7,6},{8,9},{9,8},{10,11... | collective-permute-start | bytes 786440 | tf_op jit(solution)/shard_map/ppermute | solution.py:57
  33.0 1.1 %collective-permute-start.11 = (bf16[128,1024]{1,0:T(8,128)(2,1)S(1)}, bf16[128,1024]{1,0:T(8,128)(2,1)S(1)}, u32[]{:S(2)}, u32[]{:S(2)}) collective-permute-start(bf16[128,1024]{1,0:T(8,128)(2,1)S(1)} %get-tuple-element.54), channel_id=1, source_target_pairs={{0,2},{1,3},{2,0},{3,1},{4,6},{5,7},{6,4},{7,5},{8,10},{9,11},{10,... | collective-permute-start | bytes 786440 | tf_op jit(solution)/shard_map/ppermute | solution.py:57
  35.1 1.4 %shard_map.70.refs_4_ = f32[768,384]{1,0:T(8,128)S(1)} custom-call(bf16[384,2048]{1,0:T(8,128)(2,1)S(1)} %get-tuple-element.53.refs_0_, bf16[384,2048]{1,0:T(8,128)(2,1)S(1)} %collective-permute-done.10.refs_1_, bf16[256,768]{1,0:T(8,128)(2,1)S(1)} %shard_map.65.own.refs_2_.refs_0_, bf16[256,768]{1,0:T(8,128)(2,1)S(1)} %collective-permute-done.8.near.refs_3_.refs_1_, ...), custom_call_target="tpu_custom_call" | custom-call | flops 905969664 | tf_op jit(solution)/shard_map/pallas_call | solution.py:396
  36.5 2.8 %collective-permute-done.13.refs_1_ = bf16[128,1024]{1,0:T(8,128)(2,1)S(1)} collective-permute-done((bf16[128,1024]{1,0:T(8,128)(2,1)S(1)}, bf16[128,1024]{1,0:T(8,128)(2,1)S(1)}, u32[]{:S(2)}, u32[]{:S(2)}) %collective-permute-start.13) | collective-permute-done | bytes 262176 | tf_op jit(solution)/shard_map/ppermute | solution.py:57
  40.8 1.6 %collective-permute-start.14 = (bf16[80,2048]{1,0:T(8,128)(2,1)S(1)}, bf16[80,2048]{1,0:T(8,128)(2,1)S(1)}, u32[]{:S(2)}, u32[]{:S(2)}) collective-permute-start(bf16[80,2048]{1,0:T(8,128)(2,1)S(1)} %get-tuple-element.62), channel_id=1, source_target_pairs={{0,4},{1,5},{2,6},{3,7},{4,0},{5,1},{6,2},{7,3},{8,12},{9,13},{10,... | collective-permute-start | bytes 983048 | tf_op jit(solution)/shard_map/ppermute | solution.py:57
  42.4 1.5 %collective-permute-done.15.bottom = bf16[48,2048]{1,0:T(8,128)(2,1)S(1)} collective-permute-done((bf16[48,2048]{1,0:T(8,128)(2,1)S(1)}, bf16[48,2048]{1,0:T(8,128)(2,1)S(1)}, u32[]{:S(2)}, u32[]{:S(2)}) %collective-permute-start.15) | collective-permute-done | bytes 196640 | tf_op jit(solution)/shard_map/ppermute | solution.py:57
  45.2 3.3 %collective-permute-start.18 = (bf16[4,256,128]{2,1,0:T(8,128)(2,1)S(1)}, bf16[4,256,128]{2,1,0:T(8,128)(2,1)S(1)}, u32[]{:S(2)}, u32[]{:S(2)}) collective-permute-start(bf16[4,256,128]{2,1,0:T(8,128)(2,1)S(1)} %shard_map.74.own), channel_id=1, source_target_pairs={{8,16},{9,17},{10,18},{11,19},{12,20},{13,21},{14,22},{15,23},{16,... | collective-permute-start | bytes 786440 | tf_op jit(solution)/shard_map/ppermute | solution.py:57
  49.4 1.9 %collective-permute-start.22 = (bf16[2,256,128]{2,1,0:T(8,128)(2,1)S(1)}, bf16[2,256,128]{2,1,0:T(8,128)(2,1)S(1)}, u32[]{:S(2)}, u32[]{:S(2)}) collective-permute-start(bf16[2,256,128]{2,1,0:T(8,128)(2,1)S(1)} %get-tuple-element.68.own), channel_id=1, source_target_pairs={{8,16},{9,17},{10,18},{11,19},{12,20},{13,21},{14,22},{15,23},{16,... | collective-permute-start | bytes 393224 | tf_op jit(solution)/shard_map/ppermute | solution.py:57
  51.8 3.0 %collective-permute-start.20 = (bf16[2,256,128]{2,1,0:T(8,128)(2,1)S(1)}, bf16[2,256,128]{2,1,0:T(8,128)(2,1)S(1)}, u32[]{:S(2)}, u32[]{:S(2)}) collective-permute-start(bf16[2,256,128]{2,1,0:T(8,128)(2,1)S(1)} %get-tuple-element.67.own), channel_id=1, source_target_pairs={{8,16},{9,17},{10,18},{11,19},{12,20},{13,21},{14,22},{15,23},{16,... | collective-permute-start | bytes 393224 | tf_op jit(solution)/shard_map/ppermute | solution.py:57
  54.8 1.2 %shard_map.75.weights = bf16[4,256,640]{2,1,0:T(8,128)(2,1)S(1)} custom-call(bf16[4,256,128]{2,1,0:T(8,128)(2,1)S(1)} %get-tuple-element.66.q_ref, bf16[4,256,128]{2,1,0:T(8,128)(2,1)S(1)} %collective-permute-done.17.outer, bf16[4,256,128]{2,1,0:T(8,128)(2,1)S(1)} %shard_map.74.own, bf16[4,256,128]{2,1,0:T(8,128)(2,1)S(1)} %collective-permute-done.18.middle, ...), custom_call_target="tpu_custom_call" | custom-call | flops 167772160 | tf_op jit(solution)/shard_map/pallas_call | solution.py:413
  57.1 1.4 %collective-permute-start.25 = (bf16[256,128]{1,0:T(8,128)(2,1)S(1)}, bf16[256,128]{1,0:T(8,128)(2,1)S(1)}, u32[]{:S(2)}, u32[]{:S(2)}) collective-permute-start(bf16[256,128]{1,0:T(8,128)(2,1)S(1)} %shard_map.79), channel_id=1, source_target_pairs={{0,3},{1,2},{2,1},{3,0},{4,7},{5,6},{6,5},{7,4},{8,11},{9,10},{10,... | collective-permute-start | bytes 196616 | tf_op jit(solution)/shard_map/ppermute | solution.py:57
  58.5 1.2 %collective-permute-done.20.middle = bf16[2,256,128]{2,1,0:T(8,128)(2,1)S(1)} collective-permute-done((bf16[2,256,128]{2,1,0:T(8,128)(2,1)S(1)}, bf16[2,256,128]{2,1,0:T(8,128)(2,1)S(1)}, u32[]{:S(2)}, u32[]{:S(2)}) %collective-permute-start.20) | collective-permute-done | bytes 131104 | tf_op jit(solution)/shard_map/ppermute | solution.py:57
  63.1 2.0 %collective-permute-done.23.refs_1_ = bf16[256,128]{1,0:T(8,128)(2,1)S(1)} collective-permute-done((bf16[256,128]{1,0:T(8,128)(2,1)S(1)}, bf16[256,128]{1,0:T(8,128)(2,1)S(1)}, u32[]{:S(2)}, u32[]{:S(2)}) %collective-permute-start.23) | collective-permute-done | bytes 65568 | tf_op jit(solution)/shard_map/ppermute | solution.py:57
  65.1 2.8 %collective-permute-start.26 = (bf16[4,128,128]{2,1,0:T(8,128)(2,1)S(1)}, bf16[4,128,128]{2,1,0:T(8,128)(2,1)S(1)}, u32[]{:S(2)}, u32[]{:S(2)}) collective-permute-start(bf16[4,128,128]{2,1,0:T(8,128)(2,1)S(1)} %get-tuple-element.70), channel_id=1, source_target_pairs={{0,4},{1,5},{2,6},{3,7},{4,0},{5,1},{6,2},{7,3},{8,12},{9,13},{10,... | collective-permute-start | bytes 393224 | tf_op jit(solution)/shard_map/ppermute | solution.py:57
  (63 shorter events, 19.5 us)
Async XLA Ops:
  0.0 19.8 %collective-permute-start = (bf16[256,768]{1,0:T(8,128)(2,1)}, bf16[256,768]{1,0:T(8,128)(2,1)}, u32[]{:S(2)}, u32[]{:S(2)}) collective-permute-start(bf16[256,768]{1,0:T(8,128)(2,1)} %w.1), channel_id=1, source_target_pairs={{0,16},{1,17},{2,18},{3,19},{4,20},{5,21},{6,22},{7,23},{8,24},{9,... | collective-permute-start | bytes 1179656 | tf_op jit(solution)/shard_map/ppermute | solution.py:57
  4.8 5.1 %collective-permute-start.1 = (bf16[336,256]{1,0:T(8,128)(2,1)S(1)}, bf16[336,256]{1,0:T(8,128)(2,1)S(1)}, u32[]{:S(2)}, u32[]{:S(2)}) collective-permute-start(bf16[336,256]{1,0:T(8,128)(2,1)S(1)} %get-tuple-element.39), channel_id=1, source_target_pairs={{0,1},{1,0},{2,3},{3,2},{4,5},{5,4},{6,7},{7,6},{8,9},{9,8},{10,11... | collective-permute-start | bytes 516104 | tf_op jit(solution)/shard_map/ppermute | solution.py:57
  6.1 4.7 %collective-permute-start.2 = (bf16[336,256]{1,0:T(8,128)(2,1)S(1)}, bf16[336,256]{1,0:T(8,128)(2,1)S(1)}, u32[]{:S(2)}, u32[]{:S(2)}) collective-permute-start(bf16[336,256]{1,0:T(8,128)(2,1)S(1)} %get-tuple-element.40), channel_id=1, source_target_pairs={{0,2},{1,3},{2,0},{3,1},{4,6},{5,7},{6,4},{7,5},{8,10},{9,11},{10,... | collective-permute-start | bytes 516104 | tf_op jit(solution)/shard_map/ppermute | solution.py:57
  7.3 16.7 %collective-permute-start.7 = (bf16[128,2048]{1,0:T(8,128)(2,1)}, bf16[128,2048]{1,0:T(8,128)(2,1)}, u32[]{:S(2)}, u32[]{:S(2)}) collective-permute-start(bf16[128,2048]{1,0:T(8,128)(2,1)} %bitcast.12), channel_id=1, source_target_pairs={{0,2},{1,3},{2,0},{3,1},{4,6},{5,7},{6,4},{7,5},{8,10},{9,11},{10,... | collective-permute-start | bytes 1572872 | tf_op jit(solution)/shard_map/ppermute | solution.py:57
  7.5 16.5 %collective-permute-start.6 = (bf16[128,2048]{1,0:T(8,128)(2,1)}, bf16[128,2048]{1,0:T(8,128)(2,1)}, u32[]{:S(2)}, u32[]{:S(2)}) collective-permute-start(bf16[128,2048]{1,0:T(8,128)(2,1)} %bitcast.13), channel_id=1, source_target_pairs={{0,1},{1,0},{2,3},{3,2},{4,5},{5,4},{6,7},{7,6},{8,9},{9,8},{10,11... | collective-permute-start | bytes 1572872 | tf_op jit(solution)/shard_map/ppermute | solution.py:57
  10.9 16.9 %collective-permute-start.8 = (bf16[256,768]{1,0:T(8,128)(2,1)S(1)}, bf16[256,768]{1,0:T(8,128)(2,1)S(1)}, u32[]{:S(2)}, u32[]{:S(2)}) collective-permute-start(bf16[256,768]{1,0:T(8,128)(2,1)S(1)} %shard_map.65.own.refs_2_.refs_0_), channel_id=1, source_target_pairs={{0,8},{1,9},{2,10},{3,11},{4,12},{5,13},{6,14},{7,15},{8,0},{9,1},... | collective-permute-start | bytes 1179656 | tf_op jit(solution)/shard_map/ppermute | solution.py:57
  11.2 11.4 %collective-permute-start.5 = (bf16[80,256]{1,0:T(8,128)(2,1)S(1)}, bf16[80,256]{1,0:T(8,128)(2,1)S(1)}, u32[]{:S(2)}, u32[]{:S(2)}) collective-permute-start(bf16[80,256]{1,0:T(8,128)(2,1)S(1)} %get-tuple-element.42), channel_id=1, source_target_pairs={{0,3},{1,2},{2,1},{3,0},{4,7},{5,6},{6,5},{7,4},{8,11},{9,10},{10,... | collective-permute-start | bytes 122888 | tf_op jit(solution)/shard_map/ppermute | solution.py:57
  20.9 6.9 %collective-permute-start.3 = (bf16[256,256]{1,0:T(8,128)(2,1)S(1)}, bf16[256,256]{1,0:T(8,128)(2,1)S(1)}, u32[]{:S(2)}, u32[]{:S(2)}) collective-permute-start(bf16[256,256]{1,0:T(8,128)(2,1)S(1)} %get-tuple-element.72), channel_id=1, source_target_pairs={{0,1},{1,0},{2,3},{3,2},{4,5},{5,4},{6,7},{7,6},{8,9},{9,8},{10,11... | collective-permute-start | bytes 393224 | tf_op jit(solution)/shard_map/ppermute | solution.py:57
  22.5 5.3 %collective-permute-start.4 = (bf16[256,256]{1,0:T(8,128)(2,1)S(1)}, bf16[256,256]{1,0:T(8,128)(2,1)S(1)}, u32[]{:S(2)}, u32[]{:S(2)}) collective-permute-start(bf16[256,256]{1,0:T(8,128)(2,1)S(1)} %get-tuple-element.71), channel_id=1, source_target_pairs={{0,2},{1,3},{2,0},{3,1},{4,6},{5,7},{6,4},{7,5},{8,10},{9,11},{10,... | collective-permute-start | bytes 393224 | tf_op jit(solution)/shard_map/ppermute | solution.py:57
  31.1 4.1 %collective-permute-start.10 = (bf16[384,2048]{1,0:T(8,128)(2,1)S(1)}, bf16[384,2048]{1,0:T(8,128)(2,1)S(1)}, u32[]{:S(2)}, u32[]{:S(2)}) collective-permute-start(bf16[384,2048]{1,0:T(8,128)(2,1)S(1)} %get-tuple-element.53.refs_0_), channel_id=1, source_target_pairs={{0,4},{1,5},{2,6},{3,7},{4,0},{5,1},{6,2},{7,3},{8,12},{9,13},{10,... | collective-permute-start | bytes 4718600 | tf_op jit(solution)/shard_map/ppermute | solution.py:57
  31.6 3.6 %collective-permute-start.12 = (bf16[528,384]{1,0:T(8,128)(2,1)S(1)}, bf16[528,384]{1,0:T(8,128)(2,1)S(1)}, u32[]{:S(2)}, u32[]{:S(2)}) collective-permute-start(bf16[528,384]{1,0:T(8,128)(2,1)S(1)} %shard_map.69), channel_id=1, source_target_pairs={{0,4},{1,5},{2,6},{3,7},{4,0},{5,1},{6,2},{7,3},{8,12},{9,13},{10,... | collective-permute-start | bytes 1216520 | tf_op jit(solution)/shard_map/ppermute | solution.py:57
  31.8 7.5 %collective-permute-start.13 = (bf16[128,1024]{1,0:T(8,128)(2,1)S(1)}, bf16[128,1024]{1,0:T(8,128)(2,1)S(1)}, u32[]{:S(2)}, u32[]{:S(2)}) collective-permute-start(bf16[128,1024]{1,0:T(8,128)(2,1)S(1)} %get-tuple-element.59), channel_id=1, source_target_pairs={{0,1},{1,0},{2,3},{3,2},{4,5},{5,4},{6,7},{7,6},{8,9},{9,8},{10,11... | collective-permute-start | bytes 786440 | tf_op jit(solution)/shard_map/ppermute | solution.py:57
  33.0 7.2 %collective-permute-start.11 = (bf16[128,1024]{1,0:T(8,128)(2,1)S(1)}, bf16[128,1024]{1,0:T(8,128)(2,1)S(1)}, u32[]{:S(2)}, u32[]{:S(2)}) collective-permute-start(bf16[128,1024]{1,0:T(8,128)(2,1)S(1)} %get-tuple-element.54), channel_id=1, source_target_pairs={{0,2},{1,3},{2,0},{3,1},{4,6},{5,7},{6,4},{7,5},{8,10},{9,11},{10,... | collective-permute-start | bytes 786440 | tf_op jit(solution)/shard_map/ppermute | solution.py:57
  34.1 10.5 %collective-permute-start.16 = (bf16[512,384]{1,0:T(8,128)(2,1)S(1)}, bf16[512,384]{1,0:T(8,128)(2,1)S(1)}, u32[]{:S(2)}, u32[]{:S(2)}) collective-permute-start(bf16[512,384]{1,0:T(8,128)(2,1)S(1)} %constant_dynamic-update-slice_fusion.refs_5_.refs_3_), channel_id=1, source_target_pairs={{0,8},{1,9},{2,10},{3,11},{4,12},{5,13},{6,14},{7,15},{8,0},{9,1},... | collective-permute-start | bytes 1179656 | tf_op jit(solution)/shard_map/ppermute | solution.py:57
  45.0 6.8 %collective-permute-start.17 = (bf16[4,256,128]{2,1,0:T(8,128)(2,1)S(1)}, bf16[4,256,128]{2,1,0:T(8,128)(2,1)S(1)}, u32[]{:S(2)}, u32[]{:S(2)}) collective-permute-start(bf16[4,256,128]{2,1,0:T(8,128)(2,1)S(1)} %shard_map.74.own), channel_id=1, source_target_pairs={{0,8},{1,9},{2,10},{3,11},{4,12},{5,13},{6,14},{7,15},{8,0},{9,1},... | collective-permute-start | bytes 786440 | tf_op jit(solution)/shard_map/ppermute | solution.py:57
  45.2 9.5 %collective-permute-start.18 = (bf16[4,256,128]{2,1,0:T(8,128)(2,1)S(1)}, bf16[4,256,128]{2,1,0:T(8,128)(2,1)S(1)}, u32[]{:S(2)}, u32[]{:S(2)}) collective-permute-start(bf16[4,256,128]{2,1,0:T(8,128)(2,1)S(1)} %shard_map.74.own), channel_id=1, source_target_pairs={{8,16},{9,17},{10,18},{11,19},{12,20},{13,21},{14,22},{15,23},{16,... | collective-permute-start | bytes 786440 | tf_op jit(solution)/shard_map/ppermute | solution.py:57
  49.3 6.7 %collective-permute-start.21 = (bf16[2,256,128]{2,1,0:T(8,128)(2,1)S(1)}, bf16[2,256,128]{2,1,0:T(8,128)(2,1)S(1)}, u32[]{:S(2)}, u32[]{:S(2)}) collective-permute-start(bf16[2,256,128]{2,1,0:T(8,128)(2,1)S(1)} %get-tuple-element.68.own), channel_id=1, source_target_pairs={{0,8},{1,9},{2,10},{3,11},{4,12},{5,13},{6,14},{7,15},{8,0},{9,1},... | collective-permute-start | bytes 393224 | tf_op jit(solution)/shard_map/ppermute | solution.py:57
  49.4 7.5 %collective-permute-start.22 = (bf16[2,256,128]{2,1,0:T(8,128)(2,1)S(1)}, bf16[2,256,128]{2,1,0:T(8,128)(2,1)S(1)}, u32[]{:S(2)}, u32[]{:S(2)}) collective-permute-start(bf16[2,256,128]{2,1,0:T(8,128)(2,1)S(1)} %get-tuple-element.68.own), channel_id=1, source_target_pairs={{8,16},{9,17},{10,18},{11,19},{12,20},{13,21},{14,22},{15,23},{16,... | collective-permute-start | bytes 393224 | tf_op jit(solution)/shard_map/ppermute | solution.py:57
  51.3 7.1 %collective-permute-start.19 = (bf16[2,256,128]{2,1,0:T(8,128)(2,1)S(1)}, bf16[2,256,128]{2,1,0:T(8,128)(2,1)S(1)}, u32[]{:S(2)}, u32[]{:S(2)}) collective-permute-start(bf16[2,256,128]{2,1,0:T(8,128)(2,1)S(1)} %get-tuple-element.67.own), channel_id=1, source_target_pairs={{0,8},{1,9},{2,10},{3,11},{4,12},{5,13},{6,14},{7,15},{8,0},{9,1},... | collective-permute-start | bytes 393224 | tf_op jit(solution)/shard_map/ppermute | solution.py:57
  51.8 7.8 %collective-permute-start.20 = (bf16[2,256,128]{2,1,0:T(8,128)(2,1)S(1)}, bf16[2,256,128]{2,1,0:T(8,128)(2,1)S(1)}, u32[]{:S(2)}, u32[]{:S(2)}) collective-permute-start(bf16[2,256,128]{2,1,0:T(8,128)(2,1)S(1)} %get-tuple-element.67.own), channel_id=1, source_target_pairs={{8,16},{9,17},{10,18},{11,19},{12,20},{13,21},{14,22},{15,23},{16,... | collective-permute-start | bytes 393224 | tf_op jit(solution)/shard_map/ppermute | solution.py:57
  57.1 5.1 %collective-permute-start.25 = (bf16[256,128]{1,0:T(8,128)(2,1)S(1)}, bf16[256,128]{1,0:T(8,128)(2,1)S(1)}, u32[]{:S(2)}, u32[]{:S(2)}) collective-permute-start(bf16[256,128]{1,0:T(8,128)(2,1)S(1)} %shard_map.79), channel_id=1, source_target_pairs={{0,3},{1,2},{2,1},{3,0},{4,7},{5,6},{6,5},{7,4},{8,11},{9,10},{10,... | collective-permute-start | bytes 196616 | tf_op jit(solution)/shard_map/ppermute | solution.py:57
  59.9 3.2 %collective-permute-start.24 = (bf16[256,128]{1,0:T(8,128)(2,1)S(1)}, bf16[256,128]{1,0:T(8,128)(2,1)S(1)}, u32[]{:S(2)}, u32[]{:S(2)}) collective-permute-start(bf16[256,128]{1,0:T(8,128)(2,1)S(1)} %shard_map.78), channel_id=1, source_target_pairs={{0,2},{1,3},{2,0},{3,1},{4,6},{5,7},{6,4},{7,5},{8,10},{9,11},{10,... | collective-permute-start | bytes 196616 | tf_op jit(solution)/shard_map/ppermute | solution.py:57
  61.1 4.0 %collective-permute-start.23 = (bf16[256,128]{1,0:T(8,128)(2,1)S(1)}, bf16[256,128]{1,0:T(8,128)(2,1)S(1)}, u32[]{:S(2)}, u32[]{:S(2)}) collective-permute-start(bf16[256,128]{1,0:T(8,128)(2,1)S(1)} %shard_map.77), channel_id=1, source_target_pairs={{0,1},{1,0},{2,3},{3,2},{4,5},{5,4},{6,7},{7,6},{8,9},{9,8},{10,11... | collective-permute-start | bytes 196616 | tf_op jit(solution)/shard_map/ppermute | solution.py:57
  65.1 3.7 %collective-permute-start.26 = (bf16[4,128,128]{2,1,0:T(8,128)(2,1)S(1)}, bf16[4,128,128]{2,1,0:T(8,128)(2,1)S(1)}, u32[]{:S(2)}, u32[]{:S(2)}) collective-permute-start(bf16[4,128,128]{2,1,0:T(8,128)(2,1)S(1)} %get-tuple-element.70), channel_id=1, source_target_pairs={{0,4},{1,5},{2,6},{3,7},{4,0},{5,1},{6,2},{7,3},{8,12},{9,13},{10,... | collective-permute-start | bytes 393224 | tf_op jit(solution)/shard_map/ppermute | solution.py:57
  (7 other events, 74.3 us)

commit v28 on v24

--- a/solution.py
+++ b/solution.py
@@ -337,7 +337,7 @@
     near = swap_z(own, 1)
     far_raw = after(far_raw, own)
 
-    piece = 5 * block // 8
+    piece = block // 2
     def embed(rs, *streams, finished=()):
         onward = {1: (), 2: (array(block, half),) * 2}[len(rs)]
         if rs == (3,):

time: 69.7 us -> 69.7 us (level)
  transfers between devices with their start and end apart: 27 -> 27, of which waited for: 16 -> 17; matrix products, arithmetic and copies ran while one was open for 4% -> 4% of each run, Pallas kernels for 13% -> 13%
where the time goes in v28:
time: 69.7 us; the launch traced here: 69.1 us
  starting transfers between devices  30 us (43%)
  waiting for transfers between devices  25.3 us (36%)
  Pallas kernels  9.98 us (14%)
  other arithmetic  2.48 us (4%)
  local copies, waits for them, and re-layouts  1.07 us (2%)
    ppermute x27, starting transfers between devices, hop(): return lax.ppermute(value, ('tm', 'depth'), pairs)  30 us
    ppermute x27, waiting for transfers between devices, hop(): return lax.ppermute(value, ('tm', 'depth'), pairs)  25.3 us
    pallas_call x3, Pallas kernels, embed(): call(functools.partial(embed_kernel, rs, len(finished)), out, 'v' * (6 +...  3.56 us
  transfers between devices with their start and end apart: 27, of which 17 were waited for; matrix products, arithmetic and copies ran while one was open for 4% of the time, Pallas kernels for 13%

profile of v28, /device:TPU:9, one launch (start us, length us, event | category | flops | bytes accessed | tf_op | source)
XLA Modules:
  0.0 69.1 jit_solution(3854598904352321779)
XLA Ops:
  0.0 2.3 %collective-permute-start = (bf16[256,768]{1,0:T(8,128)(2,1)}, bf16[256,768]{1,0:T(8,128)(2,1)}, u32[]{:S(2)}, u32[]{:S(2)}) collective-permute-start(bf16[256,768]{1,0:T(8,128)(2,1)} %w.1), channel_id=1, source_target_pairs={{0,16},{1,17},{2,18},{3,19},{4,20},{5,21},{6,22},{7,23},{8,24},{9,... | collective-permute-start | bytes 1179656 | tf_op jit(solution)/shard_map/ppermute | solution.py:57
  4.8 1.3 %collective-permute-start.1 = (bf16[336,256]{1,0:T(8,128)(2,1)S(1)}, bf16[336,256]{1,0:T(8,128)(2,1)S(1)}, u32[]{:S(2)}, u32[]{:S(2)}) collective-permute-start(bf16[336,256]{1,0:T(8,128)(2,1)S(1)} %get-tuple-element.39), channel_id=1, source_target_pairs={{0,1},{1,0},{2,3},{3,2},{4,5},{5,4},{6,7},{7,6},{8,9},{9,8},{10,11... | collective-permute-start | bytes 516104 | tf_op jit(solution)/shard_map/ppermute | solution.py:57
  6.1 1.2 %collective-permute-start.2 = (bf16[336,256]{1,0:T(8,128)(2,1)S(1)}, bf16[336,256]{1,0:T(8,128)(2,1)S(1)}, u32[]{:S(2)}, u32[]{:S(2)}) collective-permute-start(bf16[336,256]{1,0:T(8,128)(2,1)S(1)} %get-tuple-element.40), channel_id=1, source_target_pairs={{0,2},{1,3},{2,0},{3,1},{4,6},{5,7},{6,4},{7,5},{8,10},{9,11},{10,... | collective-permute-start | bytes 516104 | tf_op jit(solution)/shard_map/ppermute | solution.py:57
  7.8 2.1 %collective-permute-done.1.from_x.plane_x = bf16[336,256]{1,0:T(8,128)(2,1)S(1)} collective-permute-done((bf16[336,256]{1,0:T(8,128)(2,1)S(1)}, bf16[336,256]{1,0:T(8,128)(2,1)S(1)}, u32[]{:S(2)}, u32[]{:S(2)}) %collective-permute-start.1) | collective-permute-done | bytes 172064 | tf_op jit(solution)/shard_map/ppermute | solution.py:57
  11.2 1.2 %collective-permute-start.5 = (bf16[80,256]{1,0:T(8,128)(2,1)S(1)}, bf16[80,256]{1,0:T(8,128)(2,1)S(1)}, u32[]{:S(2)}, u32[]{:S(2)}) collective-permute-start(bf16[80,256]{1,0:T(8,128)(2,1)S(1)} %get-tuple-element.42), channel_id=1, source_target_pairs={{0,3},{1,2},{2,1},{3,0},{4,7},{5,6},{6,5},{7,4},{8,11},{9,10},{10,... | collective-permute-start | bytes 122888 | tf_op jit(solution)/shard_map/ppermute | solution.py:57
  12.3 7.5 %collective-permute-done = bf16[256,768]{1,0:T(8,128)(2,1)} collective-permute-done((bf16[256,768]{1,0:T(8,128)(2,1)}, bf16[256,768]{1,0:T(8,128)(2,1)}, u32[]{:S(2)}, u32[]{:S(2)}) %collective-permute-start) | collective-permute-done | bytes 393248 | tf_op jit(solution)/shard_map/ppermute | solution.py:57
  20.9 1.3 %collective-permute-start.3 = (bf16[256,256]{1,0:T(8,128)(2,1)S(1)}, bf16[256,256]{1,0:T(8,128)(2,1)S(1)}, u32[]{:S(2)}, u32[]{:S(2)}) collective-permute-start(bf16[256,256]{1,0:T(8,128)(2,1)S(1)} %get-tuple-element.72), channel_id=1, source_target_pairs={{0,1},{1,0},{2,3},{3,2},{4,5},{5,4},{6,7},{7,6},{8,9},{9,8},{10,11... | collective-permute-start | bytes 393224 | tf_op jit(solution)/shard_map/ppermute | solution.py:57
  24.1 2.3 %shard_map.67 = (bf16[384,2048]{1,0:T(8,128)(2,1)S(1)}, bf16[128,1024]{1,0:T(8,128)(2,1)S(1)}, bf16[128,1024]{1,0:T(8,128)(2,1)S(1)}) custom-call(bf16[144,128]{1,0:T(8,128)(2,1)S(1)} %pad_maximum_fusion.raw, bf16[336,256]{1,0:T(8,128)(2,1)S(1)} %collective-permute-done.1.from_x.plane_x, bf16[336,256]{1,0:T(8,128)(2,1)S(1)} %collective-permute-done.2.from_y.plane_y, ...), custom_call_target="tpu_custom_call" | custom-call | flops 402653184 | tf_op jit(solution)/shard_map/pallas_call | solution.py:346
  27.0 2.9 %collective-permute-start.9 = (bf16[256,384]{1,0:T(8,128)(2,1)S(1)}, bf16[256,384]{1,0:T(8,128)(2,1)S(1)}, u32[]{:S(2)}, u32[]{:S(2)}) collective-permute-start(bf16[256,384]{1,0:T(8,128)(2,1)S(1)} %get-tuple-element.50), channel_id=1, source_target_pairs={{0,4},{1,5},{2,6},{3,7},{4,0},{5,1},{6,2},{7,3},{8,12},{9,13},{10,... | collective-permute-start | bytes 589832 | tf_op jit(solution)/shard_map/ppermute | solution.py:57
  31.8 1.1 %collective-permute-start.13 = (bf16[128,1024]{1,0:T(8,128)(2,1)S(1)}, bf16[128,1024]{1,0:T(8,128)(2,1)S(1)}, u32[]{:S(2)}, u32[]{:S(2)}) collective-permute-start(bf16[128,1024]{1,0:T(8,128)(2,1)S(1)} %get-tuple-element.59), channel_id=1, source_target_pairs={{0,1},{1,0},{2,3},{3,2},{4,5},{5,4},{6,7},{7,6},{8,9},{9,8},{10,11... | collective-permute-start | bytes 786440 | tf_op jit(solution)/shard_map/ppermute | solution.py:57
  33.4 1.7 %collective-permute-done.12.refs_4_.refs_2_.received = bf16[528,384]{1,0:T(8,128)(2,1)S(1)} collective-permute-done((bf16[528,384]{1,0:T(8,128)(2,1)S(1)}, bf16[528,384]{1,0:T(8,128)(2,1)S(1)}, u32[]{:S(2)}, u32[]{:S(2)}) %collective-permute-start.12) | collective-permute-done | bytes 405536 | tf_op jit(solution)/shard_map/ppermute | solution.py:57
  35.1 1.4 %shard_map.70.refs_4_ = f32[768,384]{1,0:T(8,128)S(1)} custom-call(bf16[384,2048]{1,0:T(8,128)(2,1)S(1)} %get-tuple-element.53.refs_0_, bf16[384,2048]{1,0:T(8,128)(2,1)S(1)} %collective-permute-done.10.refs_1_, bf16[256,768]{1,0:T(8,128)(2,1)S(1)} %shard_map.65.own.refs_2_.refs_0_, bf16[256,768]{1,0:T(8,128)(2,1)S(1)} %collective-permute-done.8.near.refs_3_.refs_1_, ...), custom_call_target="tpu_custom_call" | custom-call | flops 905969664 | tf_op jit(solution)/shard_map/pallas_call | solution.py:379
  36.5 2.8 %collective-permute-done.13.refs_1_ = bf16[128,1024]{1,0:T(8,128)(2,1)S(1)} collective-permute-done((bf16[128,1024]{1,0:T(8,128)(2,1)S(1)}, bf16[128,1024]{1,0:T(8,128)(2,1)S(1)}, u32[]{:S(2)}, u32[]{:S(2)}) %collective-permute-start.13) | collective-permute-done | bytes 262176 | tf_op jit(solution)/shard_map/ppermute | solution.py:57
  40.7 1.6 %collective-permute-start.14 = (bf16[64,2048]{1,0:T(8,128)(2,1)S(1)}, bf16[64,2048]{1,0:T(8,128)(2,1)S(1)}, u32[]{:S(2)}, u32[]{:S(2)}) collective-permute-start(bf16[64,2048]{1,0:T(8,128)(2,1)S(1)} %get-tuple-element.62), channel_id=1, source_target_pairs={{0,4},{1,5},{2,6},{3,7},{4,0},{5,1},{6,2},{7,3},{8,12},{9,13},{10,... | collective-permute-start | bytes 786440 | tf_op jit(solution)/shard_map/ppermute | solution.py:57
  45.2 2.5 %collective-permute-start.18 = (bf16[4,256,128]{2,1,0:T(8,128)(2,1)S(1)}, bf16[4,256,128]{2,1,0:T(8,128)(2,1)S(1)}, u32[]{:S(2)}, u32[]{:S(2)}) collective-permute-start(bf16[4,256,128]{2,1,0:T(8,128)(2,1)S(1)} %shard_map.74.own), channel_id=1, source_target_pairs={{8,16},{9,17},{10,18},{11,19},{12,20},{13,21},{14,22},{15,23},{16,... | collective-permute-start | bytes 786440 | tf_op jit(solution)/shard_map/ppermute | solution.py:57
  48.5 2.7 %collective-permute-start.22 = (bf16[2,256,128]{2,1,0:T(8,128)(2,1)S(1)}, bf16[2,256,128]{2,1,0:T(8,128)(2,1)S(1)}, u32[]{:S(2)}, u32[]{:S(2)}) collective-permute-start(bf16[2,256,128]{2,1,0:T(8,128)(2,1)S(1)} %get-tuple-element.68.own), channel_id=1, source_target_pairs={{8,16},{9,17},{10,18},{11,19},{12,20},{13,21},{14,22},{15,23},{16,... | collective-permute-start | bytes 393224 | tf_op jit(solution)/shard_map/ppermute | solution.py:57
  51.3 1.2 %collective-permute-done.17.outer = bf16[4,256,128]{2,1,0:T(8,128)(2,1)S(1)} collective-permute-done((bf16[4,256,128]{2,1,0:T(8,128)(2,1)S(1)}, bf16[4,256,128]{2,1,0:T(8,128)(2,1)S(1)}, u32[]{:S(2)}, u32[]{:S(2)}) %collective-permute-start.17) | collective-permute-done | bytes 262176 | tf_op jit(solution)/shard_map/ppermute | solution.py:57
  52.5 1.9 %collective-permute-start.20 = (bf16[2,256,128]{2,1,0:T(8,128)(2,1)S(1)}, bf16[2,256,128]{2,1,0:T(8,128)(2,1)S(1)}, u32[]{:S(2)}, u32[]{:S(2)}) collective-permute-start(bf16[2,256,128]{2,1,0:T(8,128)(2,1)S(1)} %get-tuple-element.67.own), channel_id=1, source_target_pairs={{8,16},{9,17},{10,18},{11,19},{12,20},{13,21},{14,22},{15,23},{16,... | collective-permute-start | bytes 393224 | tf_op jit(solution)/shard_map/ppermute | solution.py:57
  54.4 1.2 %shard_map.75.weights = bf16[4,256,640]{2,1,0:T(8,128)(2,1)S(1)} custom-call(bf16[4,256,128]{2,1,0:T(8,128)(2,1)S(1)} %get-tuple-element.66.q_ref, bf16[4,256,128]{2,1,0:T(8,128)(2,1)S(1)} %collective-permute-done.17.outer, bf16[4,256,128]{2,1,0:T(8,128)(2,1)S(1)} %shard_map.74.own, bf16[4,256,128]{2,1,0:T(8,128)(2,1)S(1)} %collective-permute-done.18.middle, ...), custom_call_target="tpu_custom_call" | custom-call | flops 167772160 | tf_op jit(solution)/shard_map/pallas_call | solution.py:396
  55.6 1.4 %collective-permute-done.22.middle = bf16[2,256,128]{2,1,0:T(8,128)(2,1)S(1)} collective-permute-done((bf16[2,256,128]{2,1,0:T(8,128)(2,1)S(1)}, bf16[2,256,128]{2,1,0:T(8,128)(2,1)S(1)}, u32[]{:S(2)}, u32[]{:S(2)}) %collective-permute-start.22) | collective-permute-done | bytes 131104 | tf_op jit(solution)/shard_map/ppermute | solution.py:57
  57.3 1.7 %collective-permute-start.25 = (bf16[256,128]{1,0:T(8,128)(2,1)S(1)}, bf16[256,128]{1,0:T(8,128)(2,1)S(1)}, u32[]{:S(2)}, u32[]{:S(2)}) collective-permute-start(bf16[256,128]{1,0:T(8,128)(2,1)S(1)} %shard_map.79), channel_id=1, source_target_pairs={{0,3},{1,2},{2,1},{3,0},{4,7},{5,6},{6,5},{7,4},{8,11},{9,10},{10,... | collective-permute-start | bytes 196616 | tf_op jit(solution)/shard_map/ppermute | solution.py:57
  60.6 1.9 %collective-permute-start.23 = (bf16[256,128]{1,0:T(8,128)(2,1)S(1)}, bf16[256,128]{1,0:T(8,128)(2,1)S(1)}, u32[]{:S(2)}, u32[]{:S(2)}) collective-permute-start(bf16[256,128]{1,0:T(8,128)(2,1)S(1)} %shard_map.77), channel_id=1, source_target_pairs={{0,1},{1,0},{2,3},{3,2},{4,5},{5,4},{6,7},{7,6},{8,9},{9,8},{10,11... | collective-permute-start | bytes 196616 | tf_op jit(solution)/shard_map/ppermute | solution.py:57
  62.7 2.3 %collective-permute-done.23.refs_1_ = bf16[256,128]{1,0:T(8,128)(2,1)S(1)} collective-permute-done((bf16[256,128]{1,0:T(8,128)(2,1)S(1)}, bf16[256,128]{1,0:T(8,128)(2,1)S(1)}, u32[]{:S(2)}, u32[]{:S(2)}) %collective-permute-start.23) | collective-permute-done | bytes 65568 | tf_op jit(solution)/shard_map/ppermute | solution.py:57
  65.0 2.3 %collective-permute-start.26 = (bf16[4,128,128]{2,1,0:T(8,128)(2,1)S(1)}, bf16[4,128,128]{2,1,0:T(8,128)(2,1)S(1)}, u32[]{:S(2)}, u32[]{:S(2)}) collective-permute-start(bf16[4,128,128]{2,1,0:T(8,128)(2,1)S(1)} %get-tuple-element.70), channel_id=1, source_target_pairs={{0,4},{1,5},{2,6},{3,7},{4,0},{5,1},{6,2},{7,3},{8,12},{9,13},{10,... | collective-permute-start | bytes 393224 | tf_op jit(solution)/shard_map/ppermute | solution.py:57
  (63 shorter events, 19.0 us)
Async XLA Ops:
  0.0 19.8 %collective-permute-start = (bf16[256,768]{1,0:T(8,128)(2,1)}, bf16[256,768]{1,0:T(8,128)(2,1)}, u32[]{:S(2)}, u32[]{:S(2)}) collective-permute-start(bf16[256,768]{1,0:T(8,128)(2,1)} %w.1), channel_id=1, source_target_pairs={{0,16},{1,17},{2,18},{3,19},{4,20},{5,21},{6,22},{7,23},{8,24},{9,... | collective-permute-start | bytes 1179656 | tf_op jit(solution)/shard_map/ppermute | solution.py:57
  4.8 5.1 %collective-permute-start.1 = (bf16[336,256]{1,0:T(8,128)(2,1)S(1)}, bf16[336,256]{1,0:T(8,128)(2,1)S(1)}, u32[]{:S(2)}, u32[]{:S(2)}) collective-permute-start(bf16[336,256]{1,0:T(8,128)(2,1)S(1)} %get-tuple-element.39), channel_id=1, source_target_pairs={{0,1},{1,0},{2,3},{3,2},{4,5},{5,4},{6,7},{7,6},{8,9},{9,8},{10,11... | collective-permute-start | bytes 516104 | tf_op jit(solution)/shard_map/ppermute | solution.py:57
  6.1 4.7 %collective-permute-start.2 = (bf16[336,256]{1,0:T(8,128)(2,1)S(1)}, bf16[336,256]{1,0:T(8,128)(2,1)S(1)}, u32[]{:S(2)}, u32[]{:S(2)}) collective-permute-start(bf16[336,256]{1,0:T(8,128)(2,1)S(1)} %get-tuple-element.40), channel_id=1, source_target_pairs={{0,2},{1,3},{2,0},{3,1},{4,6},{5,7},{6,4},{7,5},{8,10},{9,11},{10,... | collective-permute-start | bytes 516104 | tf_op jit(solution)/shard_map/ppermute | solution.py:57
  7.3 16.7 %collective-permute-start.7 = (bf16[128,2048]{1,0:T(8,128)(2,1)}, bf16[128,2048]{1,0:T(8,128)(2,1)}, u32[]{:S(2)}, u32[]{:S(2)}) collective-permute-start(bf16[128,2048]{1,0:T(8,128)(2,1)} %bitcast.12), channel_id=1, source_target_pairs={{0,2},{1,3},{2,0},{3,1},{4,6},{5,7},{6,4},{7,5},{8,10},{9,11},{10,... | collective-permute-start | bytes 1572872 | tf_op jit(solution)/shard_map/ppermute | solution.py:57
  7.5 16.5 %collective-permute-start.6 = (bf16[128,2048]{1,0:T(8,128)(2,1)}, bf16[128,2048]{1,0:T(8,128)(2,1)}, u32[]{:S(2)}, u32[]{:S(2)}) collective-permute-start(bf16[128,2048]{1,0:T(8,128)(2,1)} %bitcast.13), channel_id=1, source_target_pairs={{0,1},{1,0},{2,3},{3,2},{4,5},{5,4},{6,7},{7,6},{8,9},{9,8},{10,11... | collective-permute-start | bytes 1572872 | tf_op jit(solution)/shard_map/ppermute | solution.py:57
  10.9 16.0 %collective-permute-start.8 = (bf16[256,768]{1,0:T(8,128)(2,1)S(1)}, bf16[256,768]{1,0:T(8,128)(2,1)S(1)}, u32[]{:S(2)}, u32[]{:S(2)}) collective-permute-start(bf16[256,768]{1,0:T(8,128)(2,1)S(1)} %shard_map.65.own.refs_2_.refs_0_), channel_id=1, source_target_pairs={{0,8},{1,9},{2,10},{3,11},{4,12},{5,13},{6,14},{7,15},{8,0},{9,1},... | collective-permute-start | bytes 1179656 | tf_op jit(solution)/shard_map/ppermute | solution.py:57
  11.2 11.4 %collective-permute-start.5 = (bf16[80,256]{1,0:T(8,128)(2,1)S(1)}, bf16[80,256]{1,0:T(8,128)(2,1)S(1)}, u32[]{:S(2)}, u32[]{:S(2)}) collective-permute-start(bf16[80,256]{1,0:T(8,128)(2,1)S(1)} %get-tuple-element.42), channel_id=1, source_target_pairs={{0,3},{1,2},{2,1},{3,0},{4,7},{5,6},{6,5},{7,4},{8,11},{9,10},{10,... | collective-permute-start | bytes 122888 | tf_op jit(solution)/shard_map/ppermute | solution.py:57
  20.9 5.5 %collective-permute-start.3 = (bf16[256,256]{1,0:T(8,128)(2,1)S(1)}, bf16[256,256]{1,0:T(8,128)(2,1)S(1)}, u32[]{:S(2)}, u32[]{:S(2)}) collective-permute-start(bf16[256,256]{1,0:T(8,128)(2,1)S(1)} %get-tuple-element.72), channel_id=1, source_target_pairs={{0,1},{1,0},{2,3},{3,2},{4,5},{5,4},{6,7},{7,6},{8,9},{9,8},{10,11... | collective-permute-start | bytes 393224 | tf_op jit(solution)/shard_map/ppermute | solution.py:57
  22.5 4.0 %collective-permute-start.4 = (bf16[256,256]{1,0:T(8,128)(2,1)S(1)}, bf16[256,256]{1,0:T(8,128)(2,1)S(1)}, u32[]{:S(2)}, u32[]{:S(2)}) collective-permute-start(bf16[256,256]{1,0:T(8,128)(2,1)S(1)} %get-tuple-element.71), channel_id=1, source_target_pairs={{0,2},{1,3},{2,0},{3,1},{4,6},{5,7},{6,4},{7,5},{8,10},{9,11},{10,... | collective-permute-start | bytes 393224 | tf_op jit(solution)/shard_map/ppermute | solution.py:57
  27.0 4.0 %collective-permute-start.9 = (bf16[256,384]{1,0:T(8,128)(2,1)S(1)}, bf16[256,384]{1,0:T(8,128)(2,1)S(1)}, u32[]{:S(2)}, u32[]{:S(2)}) collective-permute-start(bf16[256,384]{1,0:T(8,128)(2,1)S(1)} %get-tuple-element.50), channel_id=1, source_target_pairs={{0,4},{1,5},{2,6},{3,7},{4,0},{5,1},{6,2},{7,3},{8,12},{9,13},{10,... | collective-permute-start | bytes 589832 | tf_op jit(solution)/shard_map/ppermute | solution.py:57
  31.1 4.1 %collective-permute-start.10 = (bf16[384,2048]{1,0:T(8,128)(2,1)S(1)}, bf16[384,2048]{1,0:T(8,128)(2,1)S(1)}, u32[]{:S(2)}, u32[]{:S(2)}) collective-permute-start(bf16[384,2048]{1,0:T(8,128)(2,1)S(1)} %get-tuple-element.53.refs_0_), channel_id=1, source_target_pairs={{0,4},{1,5},{2,6},{3,7},{4,0},{5,1},{6,2},{7,3},{8,12},{9,13},{10,... | collective-permute-start | bytes 4718600 | tf_op jit(solution)/shard_map/ppermute | solution.py:57
  31.6 3.6 %collective-permute-start.12 = (bf16[528,384]{1,0:T(8,128)(2,1)S(1)}, bf16[528,384]{1,0:T(8,128)(2,1)S(1)}, u32[]{:S(2)}, u32[]{:S(2)}) collective-permute-start(bf16[528,384]{1,0:T(8,128)(2,1)S(1)} %shard_map.69), channel_id=1, source_target_pairs={{0,4},{1,5},{2,6},{3,7},{4,0},{5,1},{6,2},{7,3},{8,12},{9,13},{10,... | collective-permute-start | bytes 1216520 | tf_op jit(solution)/shard_map/ppermute | solution.py:57
  31.8 7.5 %collective-permute-start.13 = (bf16[128,1024]{1,0:T(8,128)(2,1)S(1)}, bf16[128,1024]{1,0:T(8,128)(2,1)S(1)}, u32[]{:S(2)}, u32[]{:S(2)}) collective-permute-start(bf16[128,1024]{1,0:T(8,128)(2,1)S(1)} %get-tuple-element.59), channel_id=1, source_target_pairs={{0,1},{1,0},{2,3},{3,2},{4,5},{5,4},{6,7},{7,6},{8,9},{9,8},{10,11... | collective-permute-start | bytes 786440 | tf_op jit(solution)/shard_map/ppermute | solution.py:57
  32.9 7.2 %collective-permute-start.11 = (bf16[128,1024]{1,0:T(8,128)(2,1)S(1)}, bf16[128,1024]{1,0:T(8,128)(2,1)S(1)}, u32[]{:S(2)}, u32[]{:S(2)}) collective-permute-start(bf16[128,1024]{1,0:T(8,128)(2,1)S(1)} %get-tuple-element.54), channel_id=1, source_target_pairs={{0,2},{1,3},{2,0},{3,1},{4,6},{5,7},{6,4},{7,5},{8,10},{9,11},{10,... | collective-permute-start | bytes 786440 | tf_op jit(solution)/shard_map/ppermute | solution.py:57
  33.2 11.3 %collective-permute-start.16 = (bf16[512,384]{1,0:T(8,128)(2,1)S(1)}, bf16[512,384]{1,0:T(8,128)(2,1)S(1)}, u32[]{:S(2)}, u32[]{:S(2)}) collective-permute-start(bf16[512,384]{1,0:T(8,128)(2,1)S(1)} %constant_dynamic-update-slice_fusion.refs_5_.refs_3_), channel_id=1, source_target_pairs={{0,8},{1,9},{2,10},{3,11},{4,12},{5,13},{6,14},{7,15},{8,0},{9,1},... | collective-permute-start | bytes 1179656 | tf_op jit(solution)/shard_map/ppermute | solution.py:57
  44.9 7.6 %collective-permute-start.17 = (bf16[4,256,128]{2,1,0:T(8,128)(2,1)S(1)}, bf16[4,256,128]{2,1,0:T(8,128)(2,1)S(1)}, u32[]{:S(2)}, u32[]{:S(2)}) collective-permute-start(bf16[4,256,128]{2,1,0:T(8,128)(2,1)S(1)} %shard_map.74.own), channel_id=1, source_target_pairs={{0,8},{1,9},{2,10},{3,11},{4,12},{5,13},{6,14},{7,15},{8,0},{9,1},... | collective-permute-start | bytes 786440 | tf_op jit(solution)/shard_map/ppermute | solution.py:57
  45.2 9.3 %collective-permute-start.18 = (bf16[4,256,128]{2,1,0:T(8,128)(2,1)S(1)}, bf16[4,256,128]{2,1,0:T(8,128)(2,1)S(1)}, u32[]{:S(2)}, u32[]{:S(2)}) collective-permute-start(bf16[4,256,128]{2,1,0:T(8,128)(2,1)S(1)} %shard_map.74.own), channel_id=1, source_target_pairs={{8,16},{9,17},{10,18},{11,19},{12,20},{13,21},{14,22},{15,23},{16,... | collective-permute-start | bytes 786440 | tf_op jit(solution)/shard_map/ppermute | solution.py:57
  48.4 7.2 %collective-permute-start.21 = (bf16[2,256,128]{2,1,0:T(8,128)(2,1)S(1)}, bf16[2,256,128]{2,1,0:T(8,128)(2,1)S(1)}, u32[]{:S(2)}, u32[]{:S(2)}) collective-permute-start(bf16[2,256,128]{2,1,0:T(8,128)(2,1)S(1)} %get-tuple-element.68.own), channel_id=1, source_target_pairs={{0,8},{1,9},{2,10},{3,11},{4,12},{5,13},{6,14},{7,15},{8,0},{9,1},... | collective-permute-start | bytes 393224 | tf_op jit(solution)/shard_map/ppermute | solution.py:57
  48.5 8.5 %collective-permute-start.22 = (bf16[2,256,128]{2,1,0:T(8,128)(2,1)S(1)}, bf16[2,256,128]{2,1,0:T(8,128)(2,1)S(1)}, u32[]{:S(2)}, u32[]{:S(2)}) collective-permute-start(bf16[2,256,128]{2,1,0:T(8,128)(2,1)S(1)} %get-tuple-element.68.own), channel_id=1, source_target_pairs={{8,16},{9,17},{10,18},{11,19},{12,20},{13,21},{14,22},{15,23},{16,... | collective-permute-start | bytes 393224 | tf_op jit(solution)/shard_map/ppermute | solution.py:57
  51.2 7.8 %collective-permute-start.19 = (bf16[2,256,128]{2,1,0:T(8,128)(2,1)S(1)}, bf16[2,256,128]{2,1,0:T(8,128)(2,1)S(1)}, u32[]{:S(2)}, u32[]{:S(2)}) collective-permute-start(bf16[2,256,128]{2,1,0:T(8,128)(2,1)S(1)} %get-tuple-element.67.own), channel_id=1, source_target_pairs={{0,8},{1,9},{2,10},{3,11},{4,12},{5,13},{6,14},{7,15},{8,0},{9,1},... | collective-permute-start | bytes 393224 | tf_op jit(solution)/shard_map/ppermute | solution.py:57
  52.5 6.8 %collective-permute-start.20 = (bf16[2,256,128]{2,1,0:T(8,128)(2,1)S(1)}, bf16[2,256,128]{2,1,0:T(8,128)(2,1)S(1)}, u32[]{:S(2)}, u32[]{:S(2)}) collective-permute-start(bf16[2,256,128]{2,1,0:T(8,128)(2,1)S(1)} %get-tuple-element.67.own), channel_id=1, source_target_pairs={{8,16},{9,17},{10,18},{11,19},{12,20},{13,21},{14,22},{15,23},{16,... | collective-permute-start | bytes 393224 | tf_op jit(solution)/shard_map/ppermute | solution.py:57
  57.3 5.4 %collective-permute-start.25 = (bf16[256,128]{1,0:T(8,128)(2,1)S(1)}, bf16[256,128]{1,0:T(8,128)(2,1)S(1)}, u32[]{:S(2)}, u32[]{:S(2)}) collective-permute-start(bf16[256,128]{1,0:T(8,128)(2,1)S(1)} %shard_map.79), channel_id=1, source_target_pairs={{0,3},{1,2},{2,1},{3,0},{4,7},{5,6},{6,5},{7,4},{8,11},{9,10},{10,... | collective-permute-start | bytes 196616 | tf_op jit(solution)/shard_map/ppermute | solution.py:57
  60.6 4.4 %collective-permute-start.23 = (bf16[256,128]{1,0:T(8,128)(2,1)S(1)}, bf16[256,128]{1,0:T(8,128)(2,1)S(1)}, u32[]{:S(2)}, u32[]{:S(2)}) collective-permute-start(bf16[256,128]{1,0:T(8,128)(2,1)S(1)} %shard_map.77), channel_id=1, source_target_pairs={{0,1},{1,0},{2,3},{3,2},{4,5},{5,4},{6,7},{7,6},{8,9},{9,8},{10,11... | collective-permute-start | bytes 196616 | tf_op jit(solution)/shard_map/ppermute | solution.py:57
  65.0 3.3 %collective-permute-start.26 = (bf16[4,128,128]{2,1,0:T(8,128)(2,1)S(1)}, bf16[4,128,128]{2,1,0:T(8,128)(2,1)S(1)}, u32[]{:S(2)}, u32[]{:S(2)}) collective-permute-start(bf16[4,128,128]{2,1,0:T(8,128)(2,1)S(1)} %get-tuple-element.70), channel_id=1, source_target_pairs={{0,4},{1,5},{2,6},{3,7},{4,0},{5,1},{6,2},{7,3},{8,12},{9,13},{10,... | collective-permute-start | bytes 393224 | tf_op jit(solution)/shard_map/ppermute | solution.py:57
  (7 other events, 74.0 us)

commit v29 on v24

--- a/solution.py
+++ b/solution.py
@@ -42,7 +42,7 @@
 
 
 PAIR = 2 * HD
-V_ORDER = (3, 1, 2, 0)
+V_ORDER = (3, 2, 1, 0)
 EXTRA = 16
 
 

time: 69.7 us -> 69.7 us (level)
  transfers between devices with their start and end apart: 27 -> 27, of which waited for: 16 -> 17; matrix products, arithmetic and copies ran while one was open for 4% -> 4% of each run, Pallas kernels for 13% -> 13%
where the time goes in v29:
time: 69.7 us; the launch traced here: 68.8 us
  starting transfers between devices  30.4 us (44%)
  waiting for transfers between devices  24.7 us (35%)
  Pallas kernels  9.98 us (14%)
  other arithmetic  2.48 us (4%)
  local copies, waits for them, and re-layouts  1.07 us (2%)
    ppermute x27, starting transfers between devices, hop(): return lax.ppermute(value, ('tm', 'depth'), pairs)  30.4 us
    ppermute x27, waiting for transfers between devices, hop(): return lax.ppermute(value, ('tm', 'depth'), pairs)  24.7 us
    pallas_call x3, Pallas kernels, embed(): call(functools.partial(embed_kernel, rs, len(finished)), out, 'v' * (6 +...  3.56 us
  transfers between devices with their start and end apart: 27, of which 17 were waited for; matrix products, arithmetic and copies ran while one was open for 4% of the time, Pallas kernels for 13%

profile of v29, /device:TPU:9, one launch (start us, length us, event | category | flops | bytes accessed | tf_op | source)
XLA Modules:
  0.0 68.8 jit_solution(15051303856261174492)
XLA Ops:
  0.0 2.3 %collective-permute-start = (bf16[256,768]{1,0:T(8,128)(2,1)}, bf16[256,768]{1,0:T(8,128)(2,1)}, u32[]{:S(2)}, u32[]{:S(2)}) collective-permute-start(bf16[256,768]{1,0:T(8,128)(2,1)} %w.1), channel_id=1, source_target_pairs={{0,16},{1,17},{2,18},{3,19},{4,20},{5,21},{6,22},{7,23},{8,24},{9,... | collective-permute-start | bytes 1179656 | tf_op jit(solution)/shard_map/ppermute | solution.py:57
  4.8 1.3 %collective-permute-start.1 = (bf16[336,256]{1,0:T(8,128)(2,1)S(1)}, bf16[336,256]{1,0:T(8,128)(2,1)S(1)}, u32[]{:S(2)}, u32[]{:S(2)}) collective-permute-start(bf16[336,256]{1,0:T(8,128)(2,1)S(1)} %get-tuple-element.39), channel_id=1, source_target_pairs={{0,1},{1,0},{2,3},{3,2},{4,5},{5,4},{6,7},{7,6},{8,9},{9,8},{10,11... | collective-permute-start | bytes 516104 | tf_op jit(solution)/shard_map/ppermute | solution.py:57
  6.1 1.2 %collective-permute-start.2 = (bf16[336,256]{1,0:T(8,128)(2,1)S(1)}, bf16[336,256]{1,0:T(8,128)(2,1)S(1)}, u32[]{:S(2)}, u32[]{:S(2)}) collective-permute-start(bf16[336,256]{1,0:T(8,128)(2,1)S(1)} %get-tuple-element.40), channel_id=1, source_target_pairs={{0,2},{1,3},{2,0},{3,1},{4,6},{5,7},{6,4},{7,5},{8,10},{9,11},{10,... | collective-permute-start | bytes 516104 | tf_op jit(solution)/shard_map/ppermute | solution.py:57
  7.8 2.1 %collective-permute-done.1.from_x.plane_x = bf16[336,256]{1,0:T(8,128)(2,1)S(1)} collective-permute-done((bf16[336,256]{1,0:T(8,128)(2,1)S(1)}, bf16[336,256]{1,0:T(8,128)(2,1)S(1)}, u32[]{:S(2)}, u32[]{:S(2)}) %collective-permute-start.1) | collective-permute-done | bytes 172064 | tf_op jit(solution)/shard_map/ppermute | solution.py:57
  11.2 1.2 %collective-permute-start.5 = (bf16[80,256]{1,0:T(8,128)(2,1)S(1)}, bf16[80,256]{1,0:T(8,128)(2,1)S(1)}, u32[]{:S(2)}, u32[]{:S(2)}) collective-permute-start(bf16[80,256]{1,0:T(8,128)(2,1)S(1)} %get-tuple-element.42), channel_id=1, source_target_pairs={{0,3},{1,2},{2,1},{3,0},{4,7},{5,6},{6,5},{7,4},{8,11},{9,10},{10,... | collective-permute-start | bytes 122888 | tf_op jit(solution)/shard_map/ppermute | solution.py:57
  12.3 7.5 %collective-permute-done = bf16[256,768]{1,0:T(8,128)(2,1)} collective-permute-done((bf16[256,768]{1,0:T(8,128)(2,1)}, bf16[256,768]{1,0:T(8,128)(2,1)}, u32[]{:S(2)}, u32[]{:S(2)}) %collective-permute-start) | collective-permute-done | bytes 393248 | tf_op jit(solution)/shard_map/ppermute | solution.py:57
  20.9 1.3 %collective-permute-start.3 = (bf16[256,256]{1,0:T(8,128)(2,1)S(1)}, bf16[256,256]{1,0:T(8,128)(2,1)S(1)}, u32[]{:S(2)}, u32[]{:S(2)}) collective-permute-start(bf16[256,256]{1,0:T(8,128)(2,1)S(1)} %get-tuple-element.72), channel_id=1, source_target_pairs={{0,1},{1,0},{2,3},{3,2},{4,5},{5,4},{6,7},{7,6},{8,9},{9,8},{10,11... | collective-permute-start | bytes 393224 | tf_op jit(solution)/shard_map/ppermute | solution.py:57
  24.1 2.3 %shard_map.67 = (bf16[384,2048]{1,0:T(8,128)(2,1)S(1)}, bf16[128,1024]{1,0:T(8,128)(2,1)S(1)}, bf16[128,1024]{1,0:T(8,128)(2,1)S(1)}) custom-call(bf16[144,128]{1,0:T(8,128)(2,1)S(1)} %pad_maximum_fusion.raw, bf16[336,256]{1,0:T(8,128)(2,1)S(1)} %collective-permute-done.1.from_x.plane_x, bf16[336,256]{1,0:T(8,128)(2,1)S(1)} %collective-permute-done.2.from_y.plane_y, ...), custom_call_target="tpu_custom_call" | custom-call | flops 402653184 | tf_op jit(solution)/shard_map/pallas_call | solution.py:346
  27.0 2.9 %collective-permute-start.9 = (bf16[256,384]{1,0:T(8,128)(2,1)S(1)}, bf16[256,384]{1,0:T(8,128)(2,1)S(1)}, u32[]{:S(2)}, u32[]{:S(2)}) collective-permute-start(bf16[256,384]{1,0:T(8,128)(2,1)S(1)} %get-tuple-element.50), channel_id=1, source_target_pairs={{0,4},{1,5},{2,6},{3,7},{4,0},{5,1},{6,2},{7,3},{8,12},{9,13},{10,... | collective-permute-start | bytes 589832 | tf_op jit(solution)/shard_map/ppermute | solution.py:57
  31.8 1.1 %collective-permute-start.13 = (bf16[128,1024]{1,0:T(8,128)(2,1)S(1)}, bf16[128,1024]{1,0:T(8,128)(2,1)S(1)}, u32[]{:S(2)}, u32[]{:S(2)}) collective-permute-start(bf16[128,1024]{1,0:T(8,128)(2,1)S(1)} %get-tuple-element.59), channel_id=1, source_target_pairs={{0,1},{1,0},{2,3},{3,2},{4,5},{5,4},{6,7},{7,6},{8,9},{9,8},{10,11... | collective-permute-start | bytes 786440 | tf_op jit(solution)/shard_map/ppermute | solution.py:57
  33.4 1.7 %collective-permute-done.12.refs_4_.refs_2_.received = bf16[528,384]{1,0:T(8,128)(2,1)S(1)} collective-permute-done((bf16[528,384]{1,0:T(8,128)(2,1)S(1)}, bf16[528,384]{1,0:T(8,128)(2,1)S(1)}, u32[]{:S(2)}, u32[]{:S(2)}) %collective-permute-start.12) | collective-permute-done | bytes 405536 | tf_op jit(solution)/shard_map/ppermute | solution.py:57
  35.1 1.4 %shard_map.70.refs_4_ = f32[768,384]{1,0:T(8,128)S(1)} custom-call(bf16[384,2048]{1,0:T(8,128)(2,1)S(1)} %get-tuple-element.53.refs_0_, bf16[384,2048]{1,0:T(8,128)(2,1)S(1)} %collective-permute-done.10.refs_1_, bf16[256,768]{1,0:T(8,128)(2,1)S(1)} %shard_map.65.own.refs_2_.refs_0_, bf16[256,768]{1,0:T(8,128)(2,1)S(1)} %collective-permute-done.8.near.refs_3_.refs_1_, ...), custom_call_target="tpu_custom_call" | custom-call | flops 905969664 | tf_op jit(solution)/shard_map/pallas_call | solution.py:379
  36.5 2.8 %collective-permute-done.13.refs_1_ = bf16[128,1024]{1,0:T(8,128)(2,1)S(1)} collective-permute-done((bf16[128,1024]{1,0:T(8,128)(2,1)S(1)}, bf16[128,1024]{1,0:T(8,128)(2,1)S(1)}, u32[]{:S(2)}, u32[]{:S(2)}) %collective-permute-start.13) | collective-permute-done | bytes 262176 | tf_op jit(solution)/shard_map/ppermute | solution.py:57
  40.7 1.6 %collective-permute-start.14 = (bf16[80,2048]{1,0:T(8,128)(2,1)S(1)}, bf16[80,2048]{1,0:T(8,128)(2,1)S(1)}, u32[]{:S(2)}, u32[]{:S(2)}) collective-permute-start(bf16[80,2048]{1,0:T(8,128)(2,1)S(1)} %get-tuple-element.62), channel_id=1, source_target_pairs={{0,4},{1,5},{2,6},{3,7},{4,0},{5,1},{6,2},{7,3},{8,12},{9,13},{10,... | collective-permute-start | bytes 983048 | tf_op jit(solution)/shard_map/ppermute | solution.py:57
  42.4 1.5 %collective-permute-done.15.bottom = bf16[48,2048]{1,0:T(8,128)(2,1)S(1)} collective-permute-done((bf16[48,2048]{1,0:T(8,128)(2,1)S(1)}, bf16[48,2048]{1,0:T(8,128)(2,1)S(1)}, u32[]{:S(2)}, u32[]{:S(2)}) %collective-permute-start.15) | collective-permute-done | bytes 196640 | tf_op jit(solution)/shard_map/ppermute | solution.py:57
  45.2 2.6 %collective-permute-start.18 = (bf16[4,256,128]{2,1,0:T(8,128)(2,1)S(1)}, bf16[4,256,128]{2,1,0:T(8,128)(2,1)S(1)}, u32[]{:S(2)}, u32[]{:S(2)}) collective-permute-start(bf16[4,256,128]{2,1,0:T(8,128)(2,1)S(1)} %shard_map.74.own), channel_id=1, source_target_pairs={{8,16},{9,17},{10,18},{11,19},{12,20},{13,21},{14,22},{15,23},{16,... | collective-permute-start | bytes 786440 | tf_op jit(solution)/shard_map/ppermute | solution.py:57
  48.5 2.7 %collective-permute-start.23 = (bf16[2,256,128]{2,1,0:T(8,128)(2,1)S(1)}, bf16[2,256,128]{2,1,0:T(8,128)(2,1)S(1)}, u32[]{:S(2)}, u32[]{:S(2)}) collective-permute-start(bf16[2,256,128]{2,1,0:T(8,128)(2,1)S(1)} %get-tuple-element.68.own), channel_id=1, source_target_pairs={{8,16},{9,17},{10,18},{11,19},{12,20},{13,21},{14,22},{15,23},{16,... | collective-permute-start | bytes 393224 | tf_op jit(solution)/shard_map/ppermute | solution.py:57
  51.3 1.2 %collective-permute-done.17.outer = bf16[4,256,128]{2,1,0:T(8,128)(2,1)S(1)} collective-permute-done((bf16[4,256,128]{2,1,0:T(8,128)(2,1)S(1)}, bf16[4,256,128]{2,1,0:T(8,128)(2,1)S(1)}, u32[]{:S(2)}, u32[]{:S(2)}) %collective-permute-start.17) | collective-permute-done | bytes 262176 | tf_op jit(solution)/shard_map/ppermute | solution.py:57
  52.5 1.9 %collective-permute-start.20 = (bf16[2,256,128]{2,1,0:T(8,128)(2,1)S(1)}, bf16[2,256,128]{2,1,0:T(8,128)(2,1)S(1)}, u32[]{:S(2)}, u32[]{:S(2)}) collective-permute-start(bf16[2,256,128]{2,1,0:T(8,128)(2,1)S(1)} %get-tuple-element.67.own), channel_id=1, source_target_pairs={{8,16},{9,17},{10,18},{11,19},{12,20},{13,21},{14,22},{15,23},{16,... | collective-permute-start | bytes 393224 | tf_op jit(solution)/shard_map/ppermute | solution.py:57
  54.4 1.2 %shard_map.75.weights = bf16[4,256,640]{2,1,0:T(8,128)(2,1)S(1)} custom-call(bf16[4,256,128]{2,1,0:T(8,128)(2,1)S(1)} %get-tuple-element.66.q_ref, bf16[4,256,128]{2,1,0:T(8,128)(2,1)S(1)} %collective-permute-done.17.outer, bf16[4,256,128]{2,1,0:T(8,128)(2,1)S(1)} %shard_map.74.own, bf16[4,256,128]{2,1,0:T(8,128)(2,1)S(1)} %collective-permute-done.18.middle, ...), custom_call_target="tpu_custom_call" | custom-call | flops 167772160 | tf_op jit(solution)/shard_map/pallas_call | solution.py:396
  55.6 1.4 %collective-permute-done.23.middle = bf16[2,256,128]{2,1,0:T(8,128)(2,1)S(1)} collective-permute-done((bf16[2,256,128]{2,1,0:T(8,128)(2,1)S(1)}, bf16[2,256,128]{2,1,0:T(8,128)(2,1)S(1)}, u32[]{:S(2)}, u32[]{:S(2)}) %collective-permute-start.23) | collective-permute-done | bytes 131104 | tf_op jit(solution)/shard_map/ppermute | solution.py:57
  57.3 1.7 %collective-permute-start.25 = (bf16[256,128]{1,0:T(8,128)(2,1)S(1)}, bf16[256,128]{1,0:T(8,128)(2,1)S(1)}, u32[]{:S(2)}, u32[]{:S(2)}) collective-permute-start(bf16[256,128]{1,0:T(8,128)(2,1)S(1)} %shard_map.79), channel_id=1, source_target_pairs={{0,3},{1,2},{2,1},{3,0},{4,7},{5,6},{6,5},{7,4},{8,11},{9,10},{10,... | collective-permute-start | bytes 196616 | tf_op jit(solution)/shard_map/ppermute | solution.py:57
  61.4 1.1 %collective-permute-done.24.refs_2_ = bf16[256,128]{1,0:T(8,128)(2,1)S(1)} collective-permute-done((bf16[256,128]{1,0:T(8,128)(2,1)S(1)}, bf16[256,128]{1,0:T(8,128)(2,1)S(1)}, u32[]{:S(2)}, u32[]{:S(2)}) %collective-permute-start.24) | collective-permute-done | bytes 65568 | tf_op jit(solution)/shard_map/ppermute | solution.py:57
  62.8 4.2 %collective-permute-start.26 = (bf16[4,128,128]{2,1,0:T(8,128)(2,1)S(1)}, bf16[4,128,128]{2,1,0:T(8,128)(2,1)S(1)}, u32[]{:S(2)}, u32[]{:S(2)}) collective-permute-start(bf16[4,128,128]{2,1,0:T(8,128)(2,1)S(1)} %get-tuple-element.70), channel_id=1, source_target_pairs={{0,4},{1,5},{2,6},{3,7},{4,0},{5,1},{6,2},{7,3},{8,12},{9,13},{10,... | collective-permute-start | bytes 393224 | tf_op jit(solution)/shard_map/ppermute | solution.py:57
  (63 shorter events, 18.4 us)
Async XLA Ops:
  0.0 19.8 %collective-permute-start = (bf16[256,768]{1,0:T(8,128)(2,1)}, bf16[256,768]{1,0:T(8,128)(2,1)}, u32[]{:S(2)}, u32[]{:S(2)}) collective-permute-start(bf16[256,768]{1,0:T(8,128)(2,1)} %w.1), channel_id=1, source_target_pairs={{0,16},{1,17},{2,18},{3,19},{4,20},{5,21},{6,22},{7,23},{8,24},{9,... | collective-permute-start | bytes 1179656 | tf_op jit(solution)/shard_map/ppermute | solution.py:57
  4.8 5.1 %collective-permute-start.1 = (bf16[336,256]{1,0:T(8,128)(2,1)S(1)}, bf16[336,256]{1,0:T(8,128)(2,1)S(1)}, u32[]{:S(2)}, u32[]{:S(2)}) collective-permute-start(bf16[336,256]{1,0:T(8,128)(2,1)S(1)} %get-tuple-element.39), channel_id=1, source_target_pairs={{0,1},{1,0},{2,3},{3,2},{4,5},{5,4},{6,7},{7,6},{8,9},{9,8},{10,11... | collective-permute-start | bytes 516104 | tf_op jit(solution)/shard_map/ppermute | solution.py:57
  6.1 4.7 %collective-permute-start.2 = (bf16[336,256]{1,0:T(8,128)(2,1)S(1)}, bf16[336,256]{1,0:T(8,128)(2,1)S(1)}, u32[]{:S(2)}, u32[]{:S(2)}) collective-permute-start(bf16[336,256]{1,0:T(8,128)(2,1)S(1)} %get-tuple-element.40), channel_id=1, source_target_pairs={{0,2},{1,3},{2,0},{3,1},{4,6},{5,7},{6,4},{7,5},{8,10},{9,11},{10,... | collective-permute-start | bytes 516104 | tf_op jit(solution)/shard_map/ppermute | solution.py:57
  7.3 16.7 %collective-permute-start.7 = (bf16[128,2048]{1,0:T(8,128)(2,1)}, bf16[128,2048]{1,0:T(8,128)(2,1)}, u32[]{:S(2)}, u32[]{:S(2)}) collective-permute-start(bf16[128,2048]{1,0:T(8,128)(2,1)} %bitcast.12), channel_id=1, source_target_pairs={{0,2},{1,3},{2,0},{3,1},{4,6},{5,7},{6,4},{7,5},{8,10},{9,11},{10,... | collective-permute-start | bytes 1572872 | tf_op jit(solution)/shard_map/ppermute | solution.py:57
  7.5 16.5 %collective-permute-start.6 = (bf16[128,2048]{1,0:T(8,128)(2,1)}, bf16[128,2048]{1,0:T(8,128)(2,1)}, u32[]{:S(2)}, u32[]{:S(2)}) collective-permute-start(bf16[128,2048]{1,0:T(8,128)(2,1)} %bitcast.13), channel_id=1, source_target_pairs={{0,1},{1,0},{2,3},{3,2},{4,5},{5,4},{6,7},{7,6},{8,9},{9,8},{10,11... | collective-permute-start | bytes 1572872 | tf_op jit(solution)/shard_map/ppermute | solution.py:57
  10.9 16.0 %collective-permute-start.8 = (bf16[256,768]{1,0:T(8,128)(2,1)S(1)}, bf16[256,768]{1,0:T(8,128)(2,1)S(1)}, u32[]{:S(2)}, u32[]{:S(2)}) collective-permute-start(bf16[256,768]{1,0:T(8,128)(2,1)S(1)} %shard_map.65.own.refs_2_.refs_0_), channel_id=1, source_target_pairs={{0,8},{1,9},{2,10},{3,11},{4,12},{5,13},{6,14},{7,15},{8,0},{9,1},... | collective-permute-start | bytes 1179656 | tf_op jit(solution)/shard_map/ppermute | solution.py:57
  11.2 11.4 %collective-permute-start.5 = (bf16[80,256]{1,0:T(8,128)(2,1)S(1)}, bf16[80,256]{1,0:T(8,128)(2,1)S(1)}, u32[]{:S(2)}, u32[]{:S(2)}) collective-permute-start(bf16[80,256]{1,0:T(8,128)(2,1)S(1)} %get-tuple-element.42), channel_id=1, source_target_pairs={{0,3},{1,2},{2,1},{3,0},{4,7},{5,6},{6,5},{7,4},{8,11},{9,10},{10,... | collective-permute-start | bytes 122888 | tf_op jit(solution)/shard_map/ppermute | solution.py:57
  20.9 5.5 %collective-permute-start.3 = (bf16[256,256]{1,0:T(8,128)(2,1)S(1)}, bf16[256,256]{1,0:T(8,128)(2,1)S(1)}, u32[]{:S(2)}, u32[]{:S(2)}) collective-permute-start(bf16[256,256]{1,0:T(8,128)(2,1)S(1)} %get-tuple-element.72), channel_id=1, source_target_pairs={{0,1},{1,0},{2,3},{3,2},{4,5},{5,4},{6,7},{7,6},{8,9},{9,8},{10,11... | collective-permute-start | bytes 393224 | tf_op jit(solution)/shard_map/ppermute | solution.py:57
  22.5 4.0 %collective-permute-start.4 = (bf16[256,256]{1,0:T(8,128)(2,1)S(1)}, bf16[256,256]{1,0:T(8,128)(2,1)S(1)}, u32[]{:S(2)}, u32[]{:S(2)}) collective-permute-start(bf16[256,256]{1,0:T(8,128)(2,1)S(1)} %get-tuple-element.71), channel_id=1, source_target_pairs={{0,2},{1,3},{2,0},{3,1},{4,6},{5,7},{6,4},{7,5},{8,10},{9,11},{10,... | collective-permute-start | bytes 393224 | tf_op jit(solution)/shard_map/ppermute | solution.py:57
  27.0 4.0 %collective-permute-start.9 = (bf16[256,384]{1,0:T(8,128)(2,1)S(1)}, bf16[256,384]{1,0:T(8,128)(2,1)S(1)}, u32[]{:S(2)}, u32[]{:S(2)}) collective-permute-start(bf16[256,384]{1,0:T(8,128)(2,1)S(1)} %get-tuple-element.50), channel_id=1, source_target_pairs={{0,4},{1,5},{2,6},{3,7},{4,0},{5,1},{6,2},{7,3},{8,12},{9,13},{10,... | collective-permute-start | bytes 589832 | tf_op jit(solution)/shard_map/ppermute | solution.py:57
  31.1 4.1 %collective-permute-start.10 = (bf16[384,2048]{1,0:T(8,128)(2,1)S(1)}, bf16[384,2048]{1,0:T(8,128)(2,1)S(1)}, u32[]{:S(2)}, u32[]{:S(2)}) collective-permute-start(bf16[384,2048]{1,0:T(8,128)(2,1)S(1)} %get-tuple-element.53.refs_0_), channel_id=1, source_target_pairs={{0,4},{1,5},{2,6},{3,7},{4,0},{5,1},{6,2},{7,3},{8,12},{9,13},{10,... | collective-permute-start | bytes 4718600 | tf_op jit(solution)/shard_map/ppermute | solution.py:57
  31.6 3.6 %collective-permute-start.12 = (bf16[528,384]{1,0:T(8,128)(2,1)S(1)}, bf16[528,384]{1,0:T(8,128)(2,1)S(1)}, u32[]{:S(2)}, u32[]{:S(2)}) collective-permute-start(bf16[528,384]{1,0:T(8,128)(2,1)S(1)} %shard_map.69), channel_id=1, source_target_pairs={{0,4},{1,5},{2,6},{3,7},{4,0},{5,1},{6,2},{7,3},{8,12},{9,13},{10,... | collective-permute-start | bytes 1216520 | tf_op jit(solution)/shard_map/ppermute | solution.py:57
  31.8 7.5 %collective-permute-start.13 = (bf16[128,1024]{1,0:T(8,128)(2,1)S(1)}, bf16[128,1024]{1,0:T(8,128)(2,1)S(1)}, u32[]{:S(2)}, u32[]{:S(2)}) collective-permute-start(bf16[128,1024]{1,0:T(8,128)(2,1)S(1)} %get-tuple-element.59), channel_id=1, source_target_pairs={{0,1},{1,0},{2,3},{3,2},{4,5},{5,4},{6,7},{7,6},{8,9},{9,8},{10,11... | collective-permute-start | bytes 786440 | tf_op jit(solution)/shard_map/ppermute | solution.py:57
  32.9 7.2 %collective-permute-start.11 = (bf16[128,1024]{1,0:T(8,128)(2,1)S(1)}, bf16[128,1024]{1,0:T(8,128)(2,1)S(1)}, u32[]{:S(2)}, u32[]{:S(2)}) collective-permute-start(bf16[128,1024]{1,0:T(8,128)(2,1)S(1)} %get-tuple-element.54), channel_id=1, source_target_pairs={{0,2},{1,3},{2,0},{3,1},{4,6},{5,7},{6,4},{7,5},{8,10},{9,11},{10,... | collective-permute-start | bytes 786440 | tf_op jit(solution)/shard_map/ppermute | solution.py:57
  33.2 11.3 %collective-permute-start.16 = (bf16[512,384]{1,0:T(8,128)(2,1)S(1)}, bf16[512,384]{1,0:T(8,128)(2,1)S(1)}, u32[]{:S(2)}, u32[]{:S(2)}) collective-permute-start(bf16[512,384]{1,0:T(8,128)(2,1)S(1)} %constant_dynamic-update-slice_fusion.refs_5_.refs_3_), channel_id=1, source_target_pairs={{0,8},{1,9},{2,10},{3,11},{4,12},{5,13},{6,14},{7,15},{8,0},{9,1},... | collective-permute-start | bytes 1179656 | tf_op jit(solution)/shard_map/ppermute | solution.py:57
  44.9 7.6 %collective-permute-start.17 = (bf16[4,256,128]{2,1,0:T(8,128)(2,1)S(1)}, bf16[4,256,128]{2,1,0:T(8,128)(2,1)S(1)}, u32[]{:S(2)}, u32[]{:S(2)}) collective-permute-start(bf16[4,256,128]{2,1,0:T(8,128)(2,1)S(1)} %shard_map.74.own), channel_id=1, source_target_pairs={{0,8},{1,9},{2,10},{3,11},{4,12},{5,13},{6,14},{7,15},{8,0},{9,1},... | collective-permute-start | bytes 786440 | tf_op jit(solution)/shard_map/ppermute | solution.py:57
  45.2 9.3 %collective-permute-start.18 = (bf16[4,256,128]{2,1,0:T(8,128)(2,1)S(1)}, bf16[4,256,128]{2,1,0:T(8,128)(2,1)S(1)}, u32[]{:S(2)}, u32[]{:S(2)}) collective-permute-start(bf16[4,256,128]{2,1,0:T(8,128)(2,1)S(1)} %shard_map.74.own), channel_id=1, source_target_pairs={{8,16},{9,17},{10,18},{11,19},{12,20},{13,21},{14,22},{15,23},{16,... | collective-permute-start | bytes 786440 | tf_op jit(solution)/shard_map/ppermute | solution.py:57
  48.4 7.2 %collective-permute-start.22 = (bf16[2,256,128]{2,1,0:T(8,128)(2,1)S(1)}, bf16[2,256,128]{2,1,0:T(8,128)(2,1)S(1)}, u32[]{:S(2)}, u32[]{:S(2)}) collective-permute-start(bf16[2,256,128]{2,1,0:T(8,128)(2,1)S(1)} %get-tuple-element.68.own), channel_id=1, source_target_pairs={{0,8},{1,9},{2,10},{3,11},{4,12},{5,13},{6,14},{7,15},{8,0},{9,1},... | collective-permute-start | bytes 393224 | tf_op jit(solution)/shard_map/ppermute | solution.py:57
  48.5 8.5 %collective-permute-start.23 = (bf16[2,256,128]{2,1,0:T(8,128)(2,1)S(1)}, bf16[2,256,128]{2,1,0:T(8,128)(2,1)S(1)}, u32[]{:S(2)}, u32[]{:S(2)}) collective-permute-start(bf16[2,256,128]{2,1,0:T(8,128)(2,1)S(1)} %get-tuple-element.68.own), channel_id=1, source_target_pairs={{8,16},{9,17},{10,18},{11,19},{12,20},{13,21},{14,22},{15,23},{16,... | collective-permute-start | bytes 393224 | tf_op jit(solution)/shard_map/ppermute | solution.py:57
  51.2 8.1 %collective-permute-start.19 = (bf16[2,256,128]{2,1,0:T(8,128)(2,1)S(1)}, bf16[2,256,128]{2,1,0:T(8,128)(2,1)S(1)}, u32[]{:S(2)}, u32[]{:S(2)}) collective-permute-start(bf16[2,256,128]{2,1,0:T(8,128)(2,1)S(1)} %get-tuple-element.67.own), channel_id=1, source_target_pairs={{0,8},{1,9},{2,10},{3,11},{4,12},{5,13},{6,14},{7,15},{8,0},{9,1},... | collective-permute-start | bytes 393224 | tf_op jit(solution)/shard_map/ppermute | solution.py:57
  52.5 6.9 %collective-permute-start.20 = (bf16[2,256,128]{2,1,0:T(8,128)(2,1)S(1)}, bf16[2,256,128]{2,1,0:T(8,128)(2,1)S(1)}, u32[]{:S(2)}, u32[]{:S(2)}) collective-permute-start(bf16[2,256,128]{2,1,0:T(8,128)(2,1)S(1)} %get-tuple-element.67.own), channel_id=1, source_target_pairs={{8,16},{9,17},{10,18},{11,19},{12,20},{13,21},{14,22},{15,23},{16,... | collective-permute-start | bytes 393224 | tf_op jit(solution)/shard_map/ppermute | solution.py:57
  57.3 4.1 %collective-permute-start.25 = (bf16[256,128]{1,0:T(8,128)(2,1)S(1)}, bf16[256,128]{1,0:T(8,128)(2,1)S(1)}, u32[]{:S(2)}, u32[]{:S(2)}) collective-permute-start(bf16[256,128]{1,0:T(8,128)(2,1)S(1)} %shard_map.79), channel_id=1, source_target_pairs={{0,3},{1,2},{2,1},{3,0},{4,7},{5,6},{6,5},{7,4},{8,11},{9,10},{10,... | collective-permute-start | bytes 196616 | tf_op jit(solution)/shard_map/ppermute | solution.py:57
  59.3 3.2 %collective-permute-start.24 = (bf16[256,128]{1,0:T(8,128)(2,1)S(1)}, bf16[256,128]{1,0:T(8,128)(2,1)S(1)}, u32[]{:S(2)}, u32[]{:S(2)}) collective-permute-start(bf16[256,128]{1,0:T(8,128)(2,1)S(1)} %shard_map.78), channel_id=1, source_target_pairs={{0,2},{1,3},{2,0},{3,1},{4,6},{5,7},{6,4},{7,5},{8,10},{9,11},{10,... | collective-permute-start | bytes 196616 | tf_op jit(solution)/shard_map/ppermute | solution.py:57
  62.8 5.2 %collective-permute-start.26 = (bf16[4,128,128]{2,1,0:T(8,128)(2,1)S(1)}, bf16[4,128,128]{2,1,0:T(8,128)(2,1)S(1)}, u32[]{:S(2)}, u32[]{:S(2)}) collective-permute-start(bf16[4,128,128]{2,1,0:T(8,128)(2,1)S(1)} %get-tuple-element.70), channel_id=1, source_target_pairs={{0,4},{1,5},{2,6},{3,7},{4,0},{5,1},{6,2},{7,3},{8,12},{9,13},{10,... | collective-permute-start | bytes 393224 | tf_op jit(solution)/shard_map/ppermute | solution.py:57
  (7 other events, 74.3 us)
